TPU v7x, 32 devices: a whole 2x2x4 slice. The times are simulated.
32 devices in a mesh: dp: 8 (over y, x, core), tensor: 4 (over z).
Axes of the slice: x: 2, y: 2, z: 4, core: 2. Of those that a mesh axis runs over, the one named last changes fastest.
Arguments:
- query: bfloat16 [8192, 2048], P('dp', 'tensor'), may hold values from -26.25 to 26.25
- key: bfloat16 [8192, 512], P('dp'), may hold values from -26.25 to 26.25
- value: bfloat16 [8192, 512], P('dp'), may hold values from -6 to 6
- grad_out: bfloat16 [8192, 3584], P('dp'), may hold values from -12 to 12
- out_weight: bfloat16 [3584, 2048], P(None, 'tensor'), may hold values from -0.125 to 0.125
- plan: int32 [64], replicated, may hold values from 0 to 63, as said below
- segments: int32 [8192], P('dp'), may hold values from 0 to 1023, as said below
Outputs:
- grad_query: bfloat16 [8192, 2048], P('dp', 'tensor')
- grad_key: bfloat16 [8192, 512], P('dp')
- grad_value: bfloat16 [8192, 512], P('dp')
- grad_out_weight: float32 [3584, 2048], P('dp', 'tensor')
Inputs may be any that keep to these rules, and one draw needn't show every extreme that they name: plan is a permutation of the blocks; the 8 blocks that one index of dp holds go to 8 different indices of dp, at most one to each. `segments`: within each aligned block of 1024 rows of one index of dp the ids start at 0 and never fall; ids may skip values.
All inputs are finite; a program needn't handle non-finite values.
Results may differ from a plain program's by a relative error of at most 0.034.
The roundings to bfloat16 on the way count: a program that leaves them out, or rounds other values in their place, can miss the bound.
Values may be sent and summed in bfloat16 or wider, within the bound.
No kernel may reach another device: no remote copies, remote signals or barrier semaphores. Data moves between devices by JAX's collectives and lax.ppermute only.
A program may use at most 128 MiB of HBM per device.

v0:
```python
from functools import partial
import math

import jax
import jax.numpy as jnp
from jax import lax
from jax.sharding import PartitionSpec as P

KV = 4
HD = 128
HEADS = 16
ROWBLK = 128


rope_base = 1000000.0
yarn_factor = 4.0
yarn_context = 32768.0
beta_fast = 32.0
beta_slow = 1.0
masked_score = -1e30


def yarn_frequencies(head_size):
    half_size = head_size // 2

    def correction(rotations):
        return (
            head_size
            * math.log(yarn_context / (rotations * 2.0 * math.pi))
            / (2.0 * math.log(rope_base))
        )

    lower_bound = max(math.floor(correction(beta_fast)), 0)
    upper_bound = min(math.ceil(correction(beta_slow)), head_size - 1)
    ramp_span = max(upper_bound - lower_bound, 0.001)
    row_index = jnp.arange(half_size).astype(jnp.float32)
    extrap_freq = rope_base ** (-2.0 * row_index / head_size)
    interp_freq = extrap_freq / yarn_factor
    ramp_weight = jnp.clip((row_index - lower_bound) / ramp_span, 0.0, 1.0)
    return interp_freq * ramp_weight + extrap_freq * (1.0 - ramp_weight)


def positions_of(segments):
    row_count = segments.shape[-1]
    row_index = jnp.arange(row_count, dtype=jnp.int32)
    is_start = jnp.concatenate(
        [
            jnp.ones(segments.shape[:-1] + (1,), dtype=jnp.bool_),
            segments[..., 1:] != segments[..., :-1],
        ],
        axis=-1,
    )
    seg_start = lax.cummax(jnp.where(is_start, row_index, 0), axis=segments.ndim - 1)
    return row_index - seg_start


def rotate(values, cosine, sine):
    half_size = values.shape[-1] // 2
    first_half = values[..., :half_size]
    second_half = values[..., half_size:]
    return jnp.concatenate(
        [first_half * cosine - second_half * sine, second_half * cosine + first_half * sine],
        axis=-1,
    )


def unrotate(grads, cosine, sine):
    half_size = grads.shape[-1] // 2
    first_half = grads[..., :half_size]
    second_half = grads[..., half_size:]
    return jnp.concatenate(
        [first_half * cosine + second_half * sine, second_half * cosine - first_half * sine],
        axis=-1,
    )


def rope_tables(segments, head_size):
    places = positions_of(segments)
    angles = places.astype(jnp.float32)[:, None] * yarn_frequencies(head_size)[None, :]
    factor = 0.1 * math.log(yarn_factor) + 1.0
    return (jnp.cos(angles) * factor, jnp.sin(angles) * factor)


def pack_blocks(blocks, slots, present):
    taken = jnp.take(blocks, slots, axis=0)
    return jnp.where(present[:, None, None], taken, jnp.zeros_like(taken))


def score_tile(stacked, key_tile, key_seg, key_pos, query_seg, query_pos, inv_scale):
    raw_scores = jnp.dot(stacked, key_tile.T, preferred_element_type=jnp.float32) * inv_scale
    allowed = (query_seg[:, None] == key_seg[None, :]) & (key_pos[None, :] <= query_pos[:, None])
    return jnp.where(allowed, raw_scores, masked_score)


def attend(queries, key_rows, value_rows, upstream, segments):
    head_count, row_count, head_size = queries.shape
    tile_rows = min(512, row_count)
    tile_count = row_count // tile_rows
    inv_scale = 1.0 / math.sqrt(head_size)
    row_index = jnp.arange(row_count, dtype=jnp.int32)
    stacked_rows = head_count * tile_rows
    key_grads = [jnp.zeros((tile_rows, head_size), jnp.float32) for unused in range(tile_count)]
    value_grads = [jnp.zeros((tile_rows, head_size), jnp.float32) for unused in range(tile_count)]
    query_grads = []
    outputs = []
    for query_block in range(tile_count):
        row_start = query_block * tile_rows
        stacked = queries[:, row_start : row_start + tile_rows].reshape(stacked_rows, head_size)
        incoming = upstream[:, row_start : row_start + tile_rows].reshape(stacked_rows, head_size)
        query_seg = jnp.tile(segments[row_start : row_start + tile_rows], head_count)
        query_pos = jnp.tile(row_index[row_start : row_start + tile_rows], head_count)
        tile_list = list(range(tile_count))
        tile_flags = []
        for key_block in tile_list:
            tile_flags.append(None)
        score_tiles = []
        for key_block, tile_flag in zip(tile_list, tile_flags):
            key_start = key_block * tile_rows
            compute = partial(
                score_tile,
                stacked,
                key_rows[key_start : key_start + tile_rows],
                segments[key_start : key_start + tile_rows],
                row_index[key_start : key_start + tile_rows],
                query_seg,
                query_pos,
                inv_scale,
            )
            score_tiles.append(compute())
        scores = jnp.concatenate(score_tiles, axis=1)
        row_peak = jnp.max(scores, axis=1, keepdims=True)
        exp_scores = jnp.exp(scores - row_peak)
        prob_full = exp_scores / jnp.sum(exp_scores, axis=1, keepdims=True)
        prob_bf = prob_full.astype(jnp.bfloat16)
        head_out = jnp.zeros((stacked_rows, head_size), jnp.float32)
        for key_block, tile_flag in zip(tile_list, tile_flags):
            key_start = key_block * tile_rows
            compute = partial(
                jnp.dot,
                prob_bf[:, key_start : key_start + tile_rows],
                value_rows[key_start : key_start + tile_rows],
                preferred_element_type=jnp.float32,
            )
            head_out = head_out + compute()
        out_bf = head_out.astype(jnp.bfloat16)
        row_delta = jnp.sum(
            incoming.astype(jnp.float32) * out_bf.astype(jnp.float32), axis=1, keepdims=True
        )
        grad_tiles = []
        for key_block, tile_flag in zip(tile_list, tile_flags):
            key_start = key_block * tile_rows
            compute = partial(
                jnp.dot,
                incoming,
                value_rows[key_start : key_start + tile_rows].T,
                preferred_element_type=jnp.float32,
            )
            grad_tiles.append(compute())
        grad_prob = jnp.concatenate(grad_tiles, axis=1)
        grad_score = (prob_full * (grad_prob - row_delta)).astype(jnp.bfloat16)
        query_grad = jnp.zeros((stacked_rows, head_size), jnp.float32)
        for key_block, tile_flag in zip(tile_list, tile_flags):
            key_start = key_block * tile_rows
            score_piece = grad_score[:, key_start : key_start + tile_rows]
            prob_piece = prob_bf[:, key_start : key_start + tile_rows]
            query_grad = (
                query_grad
                + partial(
                    jnp.dot,
                    score_piece,
                    key_rows[key_start : key_start + tile_rows],
                    preferred_element_type=jnp.float32,
                )()
            )
            key_grads[key_block] = (
                key_grads[key_block]
                + partial(jnp.dot, score_piece.T, stacked, preferred_element_type=jnp.float32)()
            )
            value_grads[key_block] = (
                value_grads[key_block]
                + partial(jnp.dot, prob_piece.T, incoming, preferred_element_type=jnp.float32)()
            )
        query_grads.append((query_grad * inv_scale).reshape(head_count, tile_rows, head_size))
        outputs.append(out_bf.reshape(head_count, tile_rows, head_size))
    key_total = jnp.concatenate(key_grads, axis=0) * inv_scale
    value_total = jnp.concatenate(value_grads, axis=0)
    return (
        jnp.concatenate(query_grads, axis=1),
        jnp.concatenate(outputs, axis=1),
        key_total,
        value_total,
    )


def weight_term(grad_rows, attn_rows):
    return lax.psum_scatter(
        jnp.dot(grad_rows.T, attn_rows, preferred_element_type=jnp.float32),
        "dp",
        scatter_dimension=0,
        tiled=True,
    )


def local(query, key, value, grad_out, out_weight, plan, segments):
    rank_count = lax.axis_size("dp")
    lane_count = lax.axis_size("tensor")
    my_rank = lax.axis_index("dp")
    my_lane = lax.axis_index("tensor")
    row_count = query.shape[0]
    block_count = row_count // ROWBLK
    head_size = HD
    local_heads = query.shape[1] // head_size
    group = HEADS // KV
    kv_head = my_lane * local_heads // group
    own_key = lax.dynamic_slice_in_dim(key, kv_head * head_size, head_size, 1)
    own_value = lax.dynamic_slice_in_dim(value, kv_head * head_size, head_size, 1)
    plan_table = plan.reshape(rank_count, block_count)
    source_rank = plan_table // block_count
    source_slot = plan_table % block_count
    from_mine = source_rank == my_rank
    send_present = jnp.any(from_mine, axis=1)
    send_slot = jnp.sum(jnp.where(from_mine, source_slot, 0), axis=1)
    arrive_from = lax.dynamic_index_in_dim(source_rank, my_rank, 0, keepdims=False)
    senders = jnp.arange(rank_count, dtype=jnp.int32)
    slot_match = arrive_from[None, :] == senders[:, None]
    back_present = jnp.any(slot_match, axis=1)
    back_slot = jnp.sum(
        jnp.where(slot_match, jnp.arange(block_count, dtype=jnp.int32)[None, :], 0), axis=1
    )
    landing = from_mine[:, :, None] & (
        source_slot[:, :, None] == jnp.arange(block_count, dtype=jnp.int32)[None, None, :]
    )
    return_rank = jnp.sum(jnp.where(landing, senders[:, None, None], 0), axis=(0, 1))

    def outbound(array):
        return pack_blocks(
            array.reshape((block_count, ROWBLK, array.shape[1])), send_slot, send_present
        )

    def inbound(received):
        return jnp.take(received, arrive_from, axis=0).reshape(row_count, received.shape[2])

    def homeward(array):
        return pack_blocks(
            array.reshape((block_count, ROWBLK, array.shape[1])), back_slot, back_present
        )

    def landed(received):
        return jnp.take(received, return_rank, axis=0).reshape(row_count, received.shape[2])

    lane_rows = ROWBLK // lane_count
    grad_blocks = grad_out.reshape(block_count, ROWBLK, grad_out.shape[1])
    grad_piece = lax.dynamic_slice_in_dim(grad_blocks, my_lane * lane_rows, lane_rows, 1)
    moved = (
        lax.all_to_all(outbound(query), "dp", split_axis=0, concat_axis=0, tiled=True),
        lax.all_to_all(outbound(own_key), "dp", split_axis=0, concat_axis=0, tiled=True),
        lax.all_to_all(outbound(own_value), "dp", split_axis=0, concat_axis=0, tiled=True),
        lax.all_to_all(
            pack_blocks(grad_piece, send_slot, send_present),
            "dp",
            split_axis=0,
            concat_axis=0,
            tiled=True,
        ),
    )
    query_dest = inbound(moved[0])
    key_dest = inbound(moved[1])
    value_dest = inbound(moved[2])
    piece_dest = jnp.take(moved[3], arrive_from, axis=0)
    grad_dest = lax.all_gather(piece_dest, "tensor", axis=1, tiled=True).reshape(
        row_count, grad_out.shape[1]
    )
    attn_grad = jnp.dot(grad_dest, out_weight, preferred_element_type=jnp.float32).astype(
        jnp.bfloat16
    )
    cosine, sine = rope_tables(segments, head_size)
    rot_query = rotate(
        query_dest.reshape(row_count, local_heads, head_size).astype(jnp.float32),
        cosine[:, None, :],
        sine[:, None, :],
    ).astype(jnp.bfloat16)
    rot_key = rotate(key_dest.astype(jnp.float32), cosine, sine).astype(jnp.bfloat16)
    query_heads = jnp.transpose(rot_query, (1, 0, 2))
    upstream_heads = jnp.transpose(attn_grad.reshape(row_count, local_heads, head_size), (1, 0, 2))
    query_grad, outputs, key_grad, value_grad = attend(
        query_heads, rot_key, value_dest, upstream_heads, segments
    )
    grad_rows_query = (
        unrotate(jnp.transpose(query_grad, (1, 0, 2)), cosine[:, None, :], sine[:, None, :])
        .astype(jnp.bfloat16)
        .reshape(row_count, local_heads * head_size)
    )
    key_partial = unrotate(key_grad, cosine, sine).astype(jnp.bfloat16)
    value_partial = value_grad.astype(jnp.bfloat16)
    attn_out = jnp.transpose(outputs, (1, 0, 2)).reshape(row_count, local_heads * head_size)
    returned = (
        lax.all_to_all(homeward(grad_rows_query), "dp", split_axis=0, concat_axis=0, tiled=True),
        lax.all_to_all(homeward(key_partial), "dp", split_axis=0, concat_axis=0, tiled=True),
        lax.all_to_all(homeward(value_partial), "dp", split_axis=0, concat_axis=0, tiled=True),
    )
    grad_query = landed(returned[0])
    key_source = landed(returned[1])
    value_source = landed(returned[2])
    weight_grad = weight_term(grad_dest, attn_out)
    key_all, value_all = (
        lax.all_gather(key_source, "tensor", axis=1, tiled=True),
        lax.all_gather(value_source, "tensor", axis=1, tiled=True),
    )
    lanes_per_key = group // local_heads

    def combine(gathered):
        merged = (
            gathered.astype(jnp.float32)
            .reshape(row_count, KV, lanes_per_key, head_size)
            .sum(axis=2)
        )
        return merged.astype(jnp.bfloat16).reshape(row_count, KV * head_size)

    return (grad_query, combine(key_all), combine(value_all), weight_grad * (1.0 / rank_count))


def solution(mesh):
    in_specs = (
        P("dp", "tensor"),
        P("dp", None),
        P("dp", None),
        P("dp", None),
        P(None, "tensor"),
        P(),
        P("dp"),
    )
    out_specs = (P("dp", "tensor"), P("dp", None), P("dp", None), P("dp", "tensor"))
    return jax.shard_map(local, mesh=mesh, in_specs=in_specs, out_specs=out_specs, check_vma=False)
```

profile of v0, /device:TPU:0, one launch (start us, length us, event | category | flops | bytes accessed | tf_op | source)
XLA Modules:
  0.0 388.5 jit_solution(12765565718014872817)
XLA Ops:
  9.0 2.9 constant_dynamic-slice_fusion.1
  15.6 5.2 %all-to-all-start.2 = ((bf16[8,32,3584]{2,1,0:T(8,128)(2,1)}), bf16[8,32,3584]{2,1,0:T(8,128)(2,1)S(1)}, u32[]{:S(2)}, u32[]{:S(2)}) async-start(bf16[8,32,3584]{2,1,0:T(8,128)(2,1)} %select_select_fusion), calls=%async_computation.2 | async-start | bytes 3670016 | tf_op jit(solution)/shard_map/all_to_all | solution.py:258
  20.9 23.8 %all-to-all-done.2 = bf16[8,32,3584]{2,1,0:T(8,128)(2,1)S(1)} async-done(((bf16[8,32,3584]{2,1,0:T(8,128)(2,1)}), bf16[8,32,3584]{2,1,0:T(8,128)(2,1)S(1)}, u32[]{:S(2)}, u32[]{:S(2)}) %all-to-all-start.2) | async-done | bytes 1835040 | tf_op jit(solution)/shard_map/all_to_all | solution.py:258
  46.6 3.0 broadcast_select_fusion
  52.8 3.4 all-to-all-start.3
  60.1 3.0 all-to-all-done.3
  63.1 3.4 all-to-all-start.1
  69.6 3.8 all-to-all-done.1
  73.4 4.1 %all-to-all-start = ((bf16[8,128,512]{2,1,0:T(8,128)(2,1)}), bf16[8,128,512]{2,1,0:T(8,128)(2,1)S(1)}, u32[]{:S(2)}, u32[]{:S(2)}) async-start(bf16[8,128,512]{2,1,0:T(8,128)(2,1)} %select_select_fusion.2), calls=%async_computation | async-start | bytes 2097152 | tf_op jit(solution)/shard_map/all_to_all | solution.py:255
  79.0 2.3 fusion.62
  84.9 7.9 %all-to-all-done = bf16[8,128,512]{2,1,0:T(8,128)(2,1)S(1)} async-done(((bf16[8,128,512]{2,1,0:T(8,128)(2,1)}), bf16[8,128,512]{2,1,0:T(8,128)(2,1)S(1)}, u32[]{:S(2)}, u32[]{:S(2)}) %all-to-all-start) | async-done | bytes 1048608 | tf_op jit(solution)/shard_map/all_to_all | solution.py:255
  97.6 3.2 fusion.89
  123.5 58.2 %all-gather.4.cloned.1.call-done = bf16[8,128,3584]{2,1,0:T(8,128)(2,1)} async-done(((bf16[8,32,3584]{2,1,0:T(8,128)(2,1)}), bf16[8,128,3584]{2,1,0:T(8,128)(2,1)}) %all-gather.4.cloned.1.call-update) | async-done | bytes 7340048 | tf_op jit(solution)/shard_map/all_gather | solution.py:270
  181.6 8.1 %convolution_convert_fusion = bf16[1024,512]{0,1:T(8,128)(2,1)S(1)} fusion(bf16[1024,3584]{1,0:T(8,128)(2,1)} %bitcast.150, bf16[3584,512]{1,0:T(8,128)(2,1)} %param.17), kind=kOutput, calls=%fused_computation.71 | convolution fusion | flops 3758620672 | bytes 12058624 | tf_op jit(solution)/shard_map/dot_general | solution.py:273
  191.1 2.7 fusion.101
  201.2 5.6 %fusion.5 = bf16[2048,1024]{0,1:T(8,128)(2,1)} fusion(f32[2048,512]{0,1:T(8,128)} %fusion.101, f32[2048,512]{0,1:T(8,128)S(1)} %fusion.100, f32[2048]{0:T(1024)} %get-tuple-element.54, f32[2048]{0:T(1024)S(1)} %fusion.7, f32[2048]{0:T(1024)S(1)} %reduce_max.45, f32[2048,512]{0,1:T(8,128)S(1)} %copy-done.7, f32[2048,512]{0,1:T(8,128)S(1)} %copy-done.9), kind=kLoop, calls=%fused_computation.23 | loop fusion | flops 14680064 | bytes 20996096 | tf_op jit(solution)/shard_map/convert_element_type | solution.py:160
  206.8 3.2 fusion.17
  209.9 3.0 fusion.14
  217.4 2.4 fusion.2
  222.7 2.5 fusion.72
  227.9 3.7 all-to-all-start.6
  231.7 6.8 %all-to-all-done.6 = bf16[8,128,128]{2,1,0:T(8,128)(2,1)S(1)} async-done(((bf16[8,128,128]{2,1,0:T(8,128)(2,1)}), bf16[8,128,128]{2,1,0:T(8,128)(2,1)S(1)}, u32[]{:S(2)}, u32[]{:S(2)}) %all-to-all-start.6) | async-done | bytes 262176 | tf_op jit(solution)/shard_map/all_to_all | solution.py:299
  238.5 3.4 all-to-all-start.5
  242.6 6.2 %all-to-all-done.5 = bf16[8,128,128]{2,1,0:T(8,128)(2,1)S(1)} async-done(((bf16[8,128,128]{2,1,0:T(8,128)(2,1)}), bf16[8,128,128]{2,1,0:T(8,128)(2,1)S(1)}, u32[]{:S(2)}, u32[]{:S(2)}) %all-to-all-start.5) | async-done | bytes 262176 | tf_op jit(solution)/shard_map/all_to_all | solution.py:298
  251.7 9.6 %fusion.102 = f32[3584,512]{1,0:T(8,128)} fusion(bf16[1024,3584]{1,0:T(8,128)(2,1)} %bitcast.151, bf16[1024,512]{0,1:T(8,128)(2,1)S(1)} %bitcast.123), kind=kOutput, calls=%fused_computation.188 | convolution fusion | flops 3758096384 | bytes 15728640 | tf_op jit(solution)/shard_map/dot_general | solution.py:197
  262.3 2.3 fusion.19
  264.6 2.4 fusion.10
  267.3 2.3 fusion.33
  269.6 2.3 fusion.11
  275.6 17.8 %all_to_all.35 = bf16[8,128,512]{2,1,0:T(8,128)(2,1)S(1)} all-to-all(bf16[8,128,512]{2,1,0:T(8,128)(2,1)S(1)} %select_select_fusion.1), channel_id=1, replica_groups=mesh['dp'=8,'tensor'=4] {'dp'}, dimensions={0} | all-to-all | bytes 2097152 | tf_op jit(solution)/shard_map/all_to_all | solution.py:297
  295.2 12.6 %all-gather.8.cloned.1.call-done = bf16[1024,512]{1,0:T(8,128)(2,1)} async-done(((bf16[1024,128]{1,0:T(8,128)(2,1)}), bf16[1024,512]{1,0:T(8,128)(2,1)}) %all-gather.8.cloned.1.call-update) | async-done | bytes 1048592 | tf_op jit(solution)/shard_map/all_gather | solution.py:307
  307.7 68.5 %reduce-scatter.2.cloned.1.call-done = f32[448,512]{1,0:T(8,128)} async-done(((f32[3584,512]{1,0:T(8,128)}), f32[448,512]{1,0:T(8,128)}) %reduce-scatter.2.cloned.1.call-update) | async-done | bytes 917520 | tf_op jit(solution)/shard_map/reduce_scatter | solution.py:196
  (232 shorter events, 83.6 us)
Async XLA Ops:
  7.2 49.7 %copy-start = (bf16[1024,512]{1,0:T(8,128)(2,1)S(1)}, bf16[1024,512]{1,0:T(8,128)(2,1)}, u32[]{:S(2)}) copy-start(bf16[1024,512]{1,0:T(8,128)(2,1)} %param.13) | copy-start | bytes 3145732
  8.2 70.0 %copy-start.43 = (pred[8]{0:T(512)(128)(4,1)}, pred[8]{0:T(512)(128)(4,1)S(1)}, u32[]{:S(2)}) copy-start(pred[8]{0:T(512)(128)(4,1)S(1)} %get-tuple-element.11) | copy-start | bytes 28
  15.6 29.0 %all-to-all-start.2 = ((bf16[8,32,3584]{2,1,0:T(8,128)(2,1)}), bf16[8,32,3584]{2,1,0:T(8,128)(2,1)S(1)}, u32[]{:S(2)}, u32[]{:S(2)}) async-start(bf16[8,32,3584]{2,1,0:T(8,128)(2,1)} %select_select_fusion), calls=%async_computation.2 | async-start | bytes 3670016 | tf_op jit(solution)/shard_map/all_to_all | solution.py:258
  20.8 160.8 %all-gather.4.cloned.1.call-start = ((), (), s32[]{:S(2)}) async-start(), calls=%async_computation.8 | async-start | bytes 9175040 | tf_op jit(solution)/shard_map/all_gather | solution.py:270
  46.6 9.7 %copy-start.30 = (s32[1024]{0:T(1024)S(1)}, s32[1024]{0:T(1024)}, u32[]{:S(2)}) copy-start(s32[1024]{0:T(1024)} %param.19) | copy-start | bytes 12292
  52.8 10.3 %all-to-all-start.3 = ((bf16[8,128,128]{2,1,0:T(8,128)(2,1)}), bf16[8,128,128]{2,1,0:T(8,128)(2,1)S(1)}, u32[]{:S(2)}, u32[]{:S(2)}) async-start(bf16[8,128,128]{2,1,0:T(8,128)(2,1)} %get-tuple-element.44), calls=%async_computation.3 | async-start | bytes 524288 | tf_op jit(solution)/shard_map/all_to_all | solution.py:257
  56.8 22.1 %copy-start.31 = (s32[512]{0:T(512)}, s32[512]{0:T(512)S(1)}, u32[]{:S(2)}) copy-start(s32[512]{0:T(512)S(1)} %slice.148) | copy-start | bytes 6148
  56.9 22.1 %copy-start.33 = (s32[512]{0:T(512)}, s32[512]{0:T(512)S(1)}, u32[]{:S(2)}) copy-start(s32[512]{0:T(512)S(1)} %slice.136) | copy-start | bytes 6148
  58.2 20.7 %copy-start.39 = (s32[512]{0:T(512)}, s32[512]{0:T(512)S(1)}, u32[]{:S(2)}) copy-start(s32[512]{0:T(512)S(1)} %get-tuple-element.41) | copy-start | bytes 6148
  58.2 20.7 %copy-start.41 = (s32[512]{0:T(512)}, s32[512]{0:T(512)S(1)}, u32[]{:S(2)}) copy-start(s32[512]{0:T(512)S(1)} %get-tuple-element.40) | copy-start | bytes 6148
  63.1 10.3 %all-to-all-start.1 = ((bf16[8,128,128]{2,1,0:T(8,128)(2,1)}), bf16[8,128,128]{2,1,0:T(8,128)(2,1)S(1)}, u32[]{:S(2)}, u32[]{:S(2)}) async-start(bf16[8,128,128]{2,1,0:T(8,128)(2,1)} %get-tuple-element.45), calls=%async_computation.1 | async-start | bytes 524288 | tf_op jit(solution)/shard_map/all_to_all | solution.py:256
  66.6 14.8 %copy-start.47 = (f32[64]{0:T(128)}, f32[64]{0:T(128)S(1)}, u32[]{:S(2)}) copy-start(f32[64]{0:T(128)S(1)} %multiply_add_fusion) | copy-start | bytes 772
  73.4 19.4 %all-to-all-start = ((bf16[8,128,512]{2,1,0:T(8,128)(2,1)}), bf16[8,128,512]{2,1,0:T(8,128)(2,1)S(1)}, u32[]{:S(2)}, u32[]{:S(2)}) async-start(bf16[8,128,512]{2,1,0:T(8,128)(2,1)} %select_select_fusion.2), calls=%async_computation | async-start | bytes 2097152 | tf_op jit(solution)/shard_map/all_to_all | solution.py:255
  110.6 7.6 %copy-start.2 = (f32[2048,512]{0,1:T(8,128)}, f32[2048,512]{0,1:T(8,128)S(1)}, u32[]{:S(2)}) copy-start(f32[2048,512]{0,1:T(8,128)S(1)} %get-tuple-element.57) | copy-start | bytes 12582916
  111.7 6.5 %copy-start.4 = (f32[2048,512]{0,1:T(8,128)}, f32[2048,512]{0,1:T(8,128)S(1)}, u32[]{:S(2)}) copy-start(f32[2048,512]{0,1:T(8,128)S(1)} %get-tuple-element.59) | copy-start | bytes 12582916
  196.1 5.1 %copy-start.9 = (f32[2048,512]{0,1:T(8,128)S(1)}, f32[2048,512]{0,1:T(8,128)}, u32[]{:S(2)}) copy-start(f32[2048,512]{0,1:T(8,128)} %copy-done.8) | copy-start | bytes 12582916
  201.2 5.6 %copy-start.25 = (bf16[4,512,128]{2,1,0:T(8,128)(2,1)S(1)}, bf16[4,512,128]{2,1,0:T(8,128)(2,1)}, u32[]{:S(2)}) copy-start(bf16[4,512,128]{2,1,0:T(8,128)(2,1)} %copy-done.24) | copy-start | bytes 1572868
  206.7 6.2 %copy-start.13 = (bf16[2048,1024]{0,1:T(8,128)(2,1)S(1)}, bf16[2048,1024]{0,1:T(8,128)(2,1)}, u32[]{:S(2)}) copy-start(bf16[2048,1024]{0,1:T(8,128)(2,1)} %copy-done.12) | copy-start | bytes 12582916
  206.7 6.2 %copy-start.53 = (f32[512,128]{1,0:T(8,128)S(1)}, f32[512,128]{1,0:T(8,128)}, u32[]{:S(2)}) copy-start(f32[512,128]{1,0:T(8,128)} %fusion.24) | copy-start | bytes 786436
  219.9 5.3 %copy-start.28 = (bf16[512,128]{1,0:T(8,128)(2,1)S(1)}, bf16[512,128]{1,0:T(8,128)(2,1)}, u32[]{:S(2)}) copy-start(bf16[512,128]{1,0:T(8,128)(2,1)} %fusion.57) | copy-start | bytes 393220
  219.9 5.3 %copy-start.29 = (bf16[512,128]{1,0:T(8,128)(2,1)S(1)}, bf16[512,128]{1,0:T(8,128)(2,1)}, u32[]{:S(2)}) copy-start(bf16[512,128]{1,0:T(8,128)(2,1)} %fusion.54) | copy-start | bytes 393220
  220.7 6.3 %copy-start.44 = (pred[8]{0:T(512)(128)(4,1)S(1)}, pred[8]{0:T(512)(128)(4,1)}, u32[]{:S(2)}) copy-start(pred[8]{0:T(512)(128)(4,1)} %get-tuple-element.64) | copy-start | bytes 28
  220.7 6.3 %copy-start.45 = (pred[8]{0:T(512)(128)(4,1)S(1)}, pred[8]{0:T(512)(128)(4,1)}, u32[]{:S(2)}) copy-start(pred[8]{0:T(512)(128)(4,1)} %fusion.83) | copy-start | bytes 28
  222.7 28.5 %copy-start.20 = (bf16[2048,128]{1,0:T(8,128)(2,1)S(1)}, bf16[2048,128]{1,0:T(8,128)(2,1)}, u32[]{:S(2)}) copy-start(bf16[2048,128]{1,0:T(8,128)(2,1)} %get-tuple-element.55) | copy-start | bytes 1572868
  225.2 26.2 %copy-start.21 = (bf16[2048,128]{1,0:T(8,128)(2,1)S(1)}, bf16[2048,128]{1,0:T(8,128)(2,1)}, u32[]{:S(2)}) copy-start(bf16[2048,128]{1,0:T(8,128)(2,1)} %get-tuple-element.61) | copy-start | bytes 1572868
  227.9 10.6 %all-to-all-start.6 = ((bf16[8,128,128]{2,1,0:T(8,128)(2,1)}), bf16[8,128,128]{2,1,0:T(8,128)(2,1)S(1)}, u32[]{:S(2)}, u32[]{:S(2)}) async-start(bf16[8,128,128]{2,1,0:T(8,128)(2,1)} %get-tuple-element.42), calls=%async_computation.6 | async-start | bytes 524288 | tf_op jit(solution)/shard_map/all_to_all | solution.py:299
  238.5 10.3 %all-to-all-start.5 = ((bf16[8,128,128]{2,1,0:T(8,128)(2,1)}), bf16[8,128,128]{2,1,0:T(8,128)(2,1)S(1)}, u32[]{:S(2)}, u32[]{:S(2)}) async-start(bf16[8,128,128]{2,1,0:T(8,128)(2,1)} %get-tuple-element.43), calls=%async_computation.5 | async-start | bytes 524288 | tf_op jit(solution)/shard_map/all_to_all | solution.py:298
  241.9 53.2 %all-gather.6.cloned.1.call-start = ((), (), s32[]{:S(2)}) async-start(), calls=%async_computation.9 | async-start | bytes 1310720 | tf_op jit(solution)/shard_map/all_gather | solution.py:306
  250.3 57.4 %all-gather.8.cloned.1.call-start = ((), (), s32[]{:S(2)}) async-start(), calls=%async_computation.10 | async-start | bytes 1310720 | tf_op jit(solution)/shard_map/all_gather | solution.py:307
  251.1 125.2 %reduce-scatter.2.cloned.1.call-start = ((), (), s32[]{:S(2)}) async-start(), calls=%async_computation.11 | async-start | bytes 8257536 | tf_op jit(solution)/shard_map/reduce_scatter | solution.py:196
  293.4 88.3 %copy-start.1 = (bf16[1024,512]{1,0:T(8,128)(2,1)S(1)}, bf16[1024,512]{1,0:T(8,128)(2,1)}, u32[]{:S(2)}) copy-start(bf16[1024,512]{1,0:T(8,128)(2,1)} %param.13) | copy-start | bytes 3145732
  307.7 72.9 %copy-start.19 = (bf16[1024,512]{1,0:T(8,128)(2,1)S(1)}, bf16[1024,512]{1,0:T(8,128)(2,1)}, u32[]{:S(2)}) copy-start(bf16[1024,512]{1,0:T(8,128)(2,1)} %all-gather.8.cloned.1.call-done) | copy-start | bytes 3145732
  (32 other events, 79.6 us)
Sparse Core Ops, SparseCore 0:
  49.7 131.8 all-gather.3
  250.5 26.5 all-gather.5
  279.2 28.4 all-gather.7
  311.0 65.2 reduce-scatter.1
where the time goes:
time: 392 us; the launch traced here: 388 us
  waiting for transfers between devices  191 us (49%)
  matrix products  58.6 us (15%)
  local copies, waits for them, and re-layouts  42.1 us (11%)
  other arithmetic  39.9 us (10%)
  starting transfers between devices  23.3 us (6%)
  blocking collectives  17.8 us (5%)
  between operations  15.2 us (4%)
    reduce_scatter x1, waiting for transfers between devices, weight_term(): lax.psum_scatter(jnp.dot(grad_rows.T, attn_rows, preferred_element_type=j...  68.5 us
    all_gather x1, waiting for transfers between devices, local(): lax.all_gather(piece_dest, 'tensor', axis=1, tiled=True)  58.2 us
    all_to_all x1, waiting for transfers between devices, local(): lax.all_to_all(pack_blocks(grad_piece, send_slot, send_present), 'dp', sp...  23.8 us
    all_to_all x1, blocking collectives, local(): lax.all_to_all(homeward(grad_rows_query), 'dp', split_axis=0, concat_axis...  17.8 us
    unnamed x120, local copies, waits for them, and re-layouts  14.4 us
    all_gather x1, waiting for transfers between devices, local(): lax.all_gather(value_source, 'tensor', axis=1, tiled=True)  12.6 us
    dot_general x1, matrix products, weight_term(): jnp.dot(grad_rows.T, attn_rows, preferred_element_type=jnp.float32)  9.65 us
    dot_general x4, matrix products, attend(): partial(jnp.dot, score_piece, key_rows[key_start:key_start + tile_rows],...  9.35 us
  transfers between devices with their start and end apart: 10, of which 9 were waited for; matrix products, arithmetic and copies ran while one was open for 18% of the time, Pallas kernels for 0%

commit v1 on v0

v1 whole, which is shorter than its diff:
```python
from functools import partial
import math

import jax
import jax.numpy as jnp
from jax import lax
from jax.experimental import pallas as pl
from jax.experimental.pallas import tpu as pltpu
from jax.sharding import PartitionSpec as P

KV = 4
HD = 128
HEADS = 16
ROWBLK = 128
RUN_BLOCKS = 8


rope_base = 1000000.0
yarn_factor = 4.0
yarn_context = 32768.0
beta_fast = 32.0
beta_slow = 1.0
masked_score = -1e30


def yarn_frequencies(head_size):
    half_size = head_size // 2

    def correction(rotations):
        return (
            head_size
            * math.log(yarn_context / (rotations * 2.0 * math.pi))
            / (2.0 * math.log(rope_base))
        )

    lower_bound = max(math.floor(correction(beta_fast)), 0)
    upper_bound = min(math.ceil(correction(beta_slow)), head_size - 1)
    ramp_span = max(upper_bound - lower_bound, 0.001)
    row_index = jnp.arange(half_size).astype(jnp.float32)
    extrap_freq = rope_base ** (-2.0 * row_index / head_size)
    interp_freq = extrap_freq / yarn_factor
    ramp_weight = jnp.clip((row_index - lower_bound) / ramp_span, 0.0, 1.0)
    return interp_freq * ramp_weight + extrap_freq * (1.0 - ramp_weight)


def positions_of(segments):
    row_count = segments.shape[-1]
    row_index = jnp.arange(row_count, dtype=jnp.int32)
    is_start = jnp.concatenate(
        [
            jnp.ones(segments.shape[:-1] + (1,), dtype=jnp.bool_),
            segments[..., 1:] != segments[..., :-1],
        ],
        axis=-1,
    )
    seg_start = lax.cummax(jnp.where(is_start, row_index, 0), axis=segments.ndim - 1)
    return row_index - seg_start


def rope_tables(places, head_size):
    angles = places.astype(jnp.float32)[:, None] * yarn_frequencies(head_size)[None, :]
    factor = 0.1 * math.log(yarn_factor) + 1.0
    cosine = jnp.cos(angles) * factor
    sine = jnp.sin(angles) * factor
    return (
        jnp.concatenate([cosine, cosine], axis=1),
        jnp.concatenate([-sine, sine], axis=1),
    )


def swap_halves(values):
    half = values.shape[-1] // 2
    return jnp.concatenate([values[..., half:], values[..., :half]], axis=-1)


NT = (((1,), (1,)), ((), ()))
TN = (((0,), (0,)), ((), ()))


def attend_kernel(
    heads,
    plan_ref,
    run_ref,
    slot_ref,
    need_ref,
    query_ref,
    up_ref,
    cos_ref,
    sin_ref,
    key_ref,
    value_ref,
    place_ref,
    gquery_ref,
    out_ref,
    gkv_ref,
    key_win,
    value_win,
):
    scale = 1.0 / math.sqrt(HD)
    to_exp2 = scale * math.log2(math.e)
    wide = min(2, heads)
    cols = wide * ROWBLK
    gkv_ref[...] = jnp.zeros_like(gkv_ref)

    def window(count, block):
        slot = slot_ref[block]
        run = run_ref[block]
        first = jnp.maximum(slot + 1 - count, 0)
        rows = count * ROWBLK
        for step in range(count):
            source = plan_ref[run * RUN_BLOCKS + first + step]
            start = pl.multiple_of(source * ROWBLK, ROWBLK)
            key_win[pl.ds(step * ROWBLK, ROWBLK), :] = key_ref[pl.ds(start, ROWBLK), :]
            value_win[pl.ds(step * ROWBLK, ROWBLK), :] = value_ref[pl.ds(start, ROWBLK), :]
        base = pl.multiple_of(block * ROWBLK, ROWBLK)
        cosine = cos_ref[pl.ds(base, ROWBLK), :]
        sine = sin_ref[pl.ds(base, ROWBLK), :]
        place = place_ref[pl.ds(block, 1), :]
        lane = lax.broadcasted_iota(jnp.int32, (1, ROWBLK), 1)
        last = (slot - first) * ROWBLK + lane
        last_all = jnp.concatenate([last] * wide, axis=1)
        start_all = jnp.concatenate([last - place] * wide, axis=1)
        key_index = lax.broadcasted_iota(jnp.int32, (rows, cols), 0)
        allowed = (key_index >= start_all) & (key_index <= last_all)
        keys = key_win[pl.ds(0, rows), :]
        values = value_win[pl.ds(0, rows), :]
        gkey = jnp.zeros((rows, HD), jnp.float32)
        gvalue = jnp.zeros((rows, HD), jnp.float32)
        for group in range(heads // wide):
            queries = []
            ups = []
            for item in range(wide):
                at = (group * wide + item) * HD
                raw = query_ref[pl.ds(base, ROWBLK), pl.ds(at, HD)].astype(jnp.float32)
                turned = raw * cosine + pltpu.roll(raw, HD // 2, 1) * sine
                queries.append(turned.astype(jnp.bfloat16))
                ups.append(up_ref[pl.ds(base, ROWBLK), pl.ds(at, HD)])
            query = jnp.concatenate(queries, axis=0)
            up = jnp.concatenate(ups, axis=0)
            up_t = jnp.concatenate([u.astype(jnp.float32).T for u in ups], axis=1)
            score = lax.dot_general(keys, query, NT, preferred_element_type=jnp.float32)
            score = jnp.where(allowed, score, masked_score)
            peak = jnp.max(score, axis=0, keepdims=True)
            raised = jnp.exp2((score - peak) * to_exp2)
            total = jnp.sum(raised, axis=0, keepdims=True)
            prob = raised * (1.0 / total)
            prob_b = prob.astype(jnp.bfloat16)
            out_t = lax.dot_general(values, prob_b, TN, preferred_element_type=jnp.float32)
            out_r = out_t.astype(jnp.bfloat16).astype(jnp.float32)
            delta = jnp.sum(up_t * out_r, axis=0, keepdims=True)
            gprob = lax.dot_general(values, up, NT, preferred_element_type=jnp.float32)
            gscore = (prob * (gprob - delta)).astype(jnp.bfloat16)
            gquery_t = lax.dot_general(keys, gscore, TN, preferred_element_type=jnp.float32)
            gkey = gkey + jnp.dot(gscore, query, preferred_element_type=jnp.float32)
            gvalue = gvalue + jnp.dot(prob_b, up, preferred_element_type=jnp.float32)
            for item in range(wide):
                at = (group * wide + item) * HD
                part = slice(item * ROWBLK, (item + 1) * ROWBLK)
                out_ref[pl.ds(base, ROWBLK), pl.ds(at, HD)] = out_r[:, part].T.astype(jnp.bfloat16)
                grad = gquery_t[:, part].T * scale
                back = grad * cosine - pltpu.roll(grad, HD // 2, 1) * sine
                gquery_ref[pl.ds(base, ROWBLK), pl.ds(at, HD)] = back.astype(jnp.bfloat16)
        gkey = (gkey * scale).astype(jnp.bfloat16)
        gvalue = gvalue.astype(jnp.bfloat16)
        for step in range(count):
            source = plan_ref[run * RUN_BLOCKS + first + step]
            start = pl.multiple_of(source * ROWBLK, ROWBLK)
            part = slice(step * ROWBLK, (step + 1) * ROWBLK)
            gkv_ref[pl.ds(start, ROWBLK), pl.ds(0, HD)] = gkey[part]
            gkv_ref[pl.ds(start, ROWBLK), pl.ds(HD, HD)] = gvalue[part]

    def body(block, carry):
        need = need_ref[block]
        sizes = (1, 2, 4, 8)
        floor = 0
        for size in sizes:
            pl.when((need > floor) & (need <= size))(partial(window, size, block))
            floor = size
        return carry

    lax.fori_loop(0, query_ref.shape[0] // ROWBLK, body, 0)


def attend(plan, run, slot, need, query, up, cosine, sine, keys, values, places):
    rows, width = query.shape
    heads = width // HD
    every = keys.shape[0]
    smem = pl.BlockSpec(memory_space=pltpu.SMEM)
    vmem = pl.BlockSpec(memory_space=pltpu.VMEM)
    pairs = rows * RUN_BLOCKS * ROWBLK * heads
    return pl.pallas_call(
        partial(attend_kernel, heads),
        out_shape=(
            jax.ShapeDtypeStruct((rows, width), jnp.bfloat16),
            jax.ShapeDtypeStruct((rows, width), jnp.bfloat16),
            jax.ShapeDtypeStruct((every, 2 * HD), jnp.bfloat16),
        ),
        in_specs=[smem] * 4 + [vmem] * 7,
        out_specs=(vmem, vmem, vmem),
        scratch_shapes=[
            pltpu.VMEM((RUN_BLOCKS * ROWBLK, HD), jnp.bfloat16),
            pltpu.VMEM((RUN_BLOCKS * ROWBLK, HD), jnp.bfloat16),
        ],
        compiler_params=pltpu.CompilerParams(vmem_limit_bytes=48 * 1024 * 1024),
        cost_estimate=pl.CostEstimate(
            flops=10 * pairs * HD, bytes_accessed=16 * 1024 * 1024, transcendentals=pairs
        ),
    )(plan, run, slot, need, query, up, cosine, sine, keys, values, places)


def local(query, key, value, grad_out, out_weight, plan, segments):
    rank_count = lax.axis_size("dp")
    my_rank = lax.axis_index("dp")
    my_lane = lax.axis_index("tensor")
    row_count = query.shape[0]
    block_count = row_count // ROWBLK
    local_heads = query.shape[1] // HD
    group = HEADS // KV
    kv_head = my_lane * local_heads // group
    own_key = lax.dynamic_slice_in_dim(key, kv_head * HD, HD, 1)
    own_value = lax.dynamic_slice_in_dim(value, kv_head * HD, HD, 1)

    places_all = lax.all_gather(positions_of(segments), "dp", axis=0, tiled=True)
    values = lax.all_gather(own_value, "dp", axis=0, tiled=True)
    up = jnp.dot(grad_out, out_weight, preferred_element_type=jnp.float32).astype(jnp.bfloat16)

    mine = my_rank * block_count + jnp.arange(block_count, dtype=jnp.int32)
    hit = plan[None, :] == mine[:, None]
    dest = jnp.sum(
        jnp.where(hit, jnp.arange(plan.shape[0], dtype=jnp.int32)[None, :], 0), axis=1
    )
    run = dest // RUN_BLOCKS
    slot = dest % RUN_BLOCKS
    places = jnp.take(places_all.reshape(-1, ROWBLK), dest, axis=0)
    need = slot - (slot * ROWBLK - places[:, 0]) // ROWBLK + 1
    cosine, sine = rope_tables(places.reshape(row_count), HD)
    key_f = own_key.astype(jnp.float32)
    rot_key = (key_f * cosine + swap_halves(key_f) * sine).astype(jnp.bfloat16)
    keys = lax.all_gather(rot_key, "dp", axis=0, tiled=True)

    grad_query, attn_out, gkv = attend(
        plan, run, slot, need, query, up, cosine, sine, keys, values, places
    )
    gkv_sum = lax.psum_scatter(gkv, "dp", scatter_dimension=0, tiled=True)
    gkey = gkv_sum[:, :HD].astype(jnp.float32)
    key_partial = (gkey * cosine - swap_halves(gkey) * sine).astype(jnp.bfloat16)
    value_partial = gkv_sum[:, HD:]
    key_all = lax.all_gather(key_partial, "tensor", axis=1, tiled=True)
    value_all = lax.all_gather(value_partial, "tensor", axis=1, tiled=True)

    weight_term = jnp.dot(
        grad_out.T, attn_out, preferred_element_type=jnp.float32
    ).astype(jnp.bfloat16)
    weight_grad = lax.psum_scatter(
        weight_term, "dp", scatter_dimension=0, tiled=True
    ).astype(jnp.float32)

    lanes_per_key = group // local_heads

    def combine(gathered):
        if lanes_per_key == 1:
            return gathered
        merged = (
            gathered.astype(jnp.float32).reshape(row_count, KV, lanes_per_key, HD).sum(axis=2)
        )
        return merged.astype(jnp.bfloat16).reshape(row_count, KV * HD)

    return (grad_query, combine(key_all), combine(value_all), weight_grad * (1.0 / rank_count))


def solution(mesh):
    in_specs = (
        P("dp", "tensor"),
        P("dp", None),
        P("dp", None),
        P("dp", None),
        P(None, "tensor"),
        P(),
        P("dp"),
    )
    out_specs = (P("dp", "tensor"), P("dp", None), P("dp", None), P("dp", "tensor"))
    return jax.shard_map(local, mesh=mesh, in_specs=in_specs, out_specs=out_specs, check_vma=False)
```

time: 392 us -> 274 us (0.70)
  matrix products: 58.6 us -> 18 us
  other arithmetic: 39.9 us -> 10.4 us
  starting transfers between devices: 23.3 us -> 0.43 us
  local copies, waits for them, and re-layouts: 42.1 us -> 20.4 us
  Pallas kernels: 0 us -> 20.5 us
  waiting for transfers between devices: 191 us -> 179 us
  blocking collectives: 17.8 us -> 10.5 us
    all_to_all x6 -> x0, waiting for transfers between devices: 51.5 us -> none  [the longest x1 23.8 us: local(): lax.all_to_all(pack_blocks(grad_piece, send_slot, send_present), 'dp', sp...]
    unnamed x4 -> x7, waiting for transfers between devices: 0.73 us -> 49.3 us
    dot_general x26 -> x2, matrix products: 58.6 us -> 18 us  [the longest x1 9.46 us: local(): jnp.dot(grad_out, out_weight, preferred_element_type=jnp.float32)]
    reduce_scatter x1, waiting for transfers between devices: 68.5 us -> 36.3 us  [local(): gkv_sum = lax.psum_scatter(gkv, 'dp', scatter_dimension=0, tiled=True)]
    all_to_all x6 -> x0, starting transfers between devices: 23.2 us -> none  [the longest x1 5.17 us: local(): lax.all_to_all(pack_blocks(grad_piece, send_slot, send_present), 'dp', sp...]
    all_gather x3 -> x4, waiting for transfers between devices: 70.8 us -> 92.9 us  [the longest x1 30.5 us: local(): key_all = lax.all_gather(key_partial, 'tensor', axis=1, tiled=True)]
    pallas_call x0 -> x1, Pallas kernels: none -> 20.5 us  [attend(): pl.pallas_call(partial(attend_kernel, heads), out_shape=(jax.ShapeDtypeSt...]
    all_to_all x1 -> x0, blocking collectives: 17.8 us -> none  [local(): lax.all_to_all(homeward(grad_rows_query), 'dp', split_axis=0, concat_axis...]
  transfers between devices with their start and end apart: 10 -> 6, of which waited for: 9 -> 6; matrix products, arithmetic and copies ran while one was open for 18% -> 14% of each run, Pallas kernels for 0% -> 0%
where the time goes in v1:
time: 274 us; the launch traced here: 273 us
  waiting for transfers between devices  179 us (65%)
  Pallas kernels  20.5 us (7%)
  local copies, waits for them, and re-layouts  20.4 us (7%)
  matrix products  18 us (7%)
  between operations  14.2 us (5%)
  blocking collectives  10.5 us (4%)
  other arithmetic  10.4 us (4%)
    unnamed x7, waiting for transfers between devices  49.3 us
    reduce_scatter x1, waiting for transfers between devices, local(): gkv_sum = lax.psum_scatter(gkv, 'dp', scatter_dimension=0, tiled=True)  36.3 us
    all_gather x1, waiting for transfers between devices, local(): key_all = lax.all_gather(key_partial, 'tensor', axis=1, tiled=True)  30.5 us
    all_gather x1, waiting for transfers between devices, local(): keys = lax.all_gather(rot_key, 'dp', axis=0, tiled=True)  30.4 us
    all_gather x1, waiting for transfers between devices, local(): value_all = lax.all_gather(value_partial, 'tensor', axis=1, tiled=True)  29.6 us
    pallas_call x1, Pallas kernels, attend(): pl.pallas_call(partial(attend_kernel, heads), out_shape=(jax.ShapeDtypeSt...  20.5 us
    unnamed x23, local copies, waits for them, and re-layouts  18.4 us
    all_gather x1, blocking collectives, local(): lax.all_gather(positions_of(segments), 'dp', axis=0, tiled=True)  10.5 us
  transfers between devices with their start and end apart: 6, of which 6 were waited for; matrix products, arithmetic and copies ran while one was open for 14% of the time, Pallas kernels for 0%

profile of v1, /device:TPU:0, one launch (start us, length us, event | category | flops | bytes accessed | tf_op | source)
XLA Modules:
  0.0 273.0 jit_solution(16120040501030265618)
XLA Ops:
  7.2 1.1 copy-done
  8.4 0.7 constant_dynamic-slice_fusion
  9.2 0.8 slice_compare_fusion
  10.1 0.3 reduce-window.9
  10.7 10.5 %all_gather.15 = s32[8192]{0:T(1024)S(1)} all-gather(s32[1024]{0:T(1024)S(1)} %bitcast_subtract_fusion), channel_id=1, replica_groups=mesh['dp'=8,'tensor'=4] {'dp'}, dimensions={0}, use_global_device_ids=true | all-gather | bytes 36864 | tf_op jit(solution)/shard_map/all_gather | solution.py:223
  21.2 0.8 select_reduce_fusion
  22.1 0.6 gather_fusion
  22.7 1.0 dynamic-slice_convert_fusion
  23.9 1.9 fusion.7
  25.9 0.8 copy-done.6
  26.7 2.1 fusion.4
  28.8 0.2 reduce-scatter.5.cloned.1.call-start
  29.2 9.5 %convolution_convert_fusion.1.up_ref = bf16[1024,512]{1,0:T(8,128)(2,1)} fusion(bf16[1024,3584]{1,0:T(8,128)(2,1)} %param.10, bf16[3584,512]{1,0:T(8,128)(2,1)} %param.11), kind=kOutput, calls=%fused_computation.3 | convolution fusion | flops 3758620672 | bytes 12058624 | tf_op jit(solution)/shard_map/dot_general | solution.py:225
  38.7 2.4 all-gather.7.cloned.1.call-done.value_ref
  41.1 30.4 %all-gather.5.cloned.1.call-done.key_ref = bf16[8192,128]{1,0:T(8,128)(2,1)} async-done(((bf16[1024,128]{1,0:T(8,128)(2,1)}), bf16[8192,128]{1,0:T(8,128)(2,1)}) %all-gather.5.cloned.1.call-update) | async-done | bytes 2097168 | tf_op jit(solution)/shard_map/all_gather | solution.py:239
  71.5 1.2 copy-done.5
  72.7 20.5 %shard_map.102 = (bf16[1024,512]{1,0:T(8,128)(2,1)}, bf16[1024,512]{1,0:T(8,128)(2,1)S(1)}, bf16[8192,256]{1,0:T(8,128)(2,1)}) custom-call(s32[64]{0:T(128)S(1)} %copy-done.2, s32[8]{0:T(128)S(1)} %get-tuple-element.42.run_ref, s32[8]{0:T(128)S(1)} %get-tuple-element.31.slot_ref, s32[8]{0:T(128)S(1)} %get-tuple-element.30.need_ref, ...), custom_call_target="tpu_custom_call" | custom-call | flops 5368709120 | bytes 16777216 | tf_op jit(solution)/shard_map/pallas_call | solution.py:191
  93.2 1.0 copy-done.3
  94.3 1.1 copy-done.4
  95.4 8.5 %fusion = bf16[3584,512]{0,1:T(8,128)(2,1)} fusion(bf16[1024,512]{1,0:T(8,128)(2,1)S(1)} %copy-done.4, bf16[1024,3584]{1,0:T(8,128)(2,1)} %param.10), kind=kOutput, calls=%fused_computation.2 | convolution fusion | flops 3759931392 | bytes 12058624 | tf_op jit(solution)/shard_map/dot_general | solution.py:251
  104.0 6.1 %copy.15 = bf16[3584,512]{1,0:T(8,128)(2,1)} copy(bf16[3584,512]{0,1:T(8,128)(2,1)} %fusion) | data formatting | bytes 7340032
  110.2 36.3 %reduce-scatter.5.cloned.1.call-done = bf16[1024,256]{1,0:T(8,128)(2,1)} async-done(((bf16[8192,256]{1,0:T(8,128)(2,1)}), bf16[1024,256]{1,0:T(8,128)(2,1)}) %reduce-scatter.5.cloned.1.call-update) | async-done | bytes 524304 | tf_op jit(solution)/shard_map/reduce_scatter | solution.py:244
  146.5 1.8 fusion.9
  148.4 0.2 fusion.10
  148.6 1.1 fusion.6
  149.7 49.2 %reduce-scatter.7.cloned.1.call-done = bf16[448,512]{1,0:T(8,128)(2,1)} async-done(((bf16[3584,512]{1,0:T(8,128)(2,1)}), bf16[448,512]{1,0:T(8,128)(2,1)}) %reduce-scatter.7.cloned.1.call-update) | async-done | bytes 458768
  198.9 1.2 copy.16
  200.3 1.2 copy.14
  201.5 29.6 %all-gather.11.cloned.1.call-done = bf16[1024,512]{1,0:T(8,128)(2,1)} async-done(((bf16[1024,128]{1,0:T(8,128)(2,1)}), bf16[1024,512]{1,0:T(8,128)(2,1)}) %all-gather.11.cloned.1.call-update) | async-done | bytes 1048592 | tf_op jit(solution)/shard_map/all_gather | solution.py:249
  231.1 30.5 %all-gather.9.cloned.1.call-done = bf16[1024,512]{1,0:T(8,128)(2,1)} async-done(((bf16[1024,128]{1,0:T(8,128)(2,1)}), bf16[1024,512]{1,0:T(8,128)(2,1)}) %all-gather.9.cloned.1.call-update) | async-done | bytes 1048592 | tf_op jit(solution)/shard_map/all_gather | solution.py:248
  261.6 2.3 copy.19
  263.9 2.3 copy.20
  (39 shorter events, 1.3 us)
Async XLA Ops:
  7.2 1.2 copy-start
  7.2 33.9 %all-gather.7.cloned.1.call-start = ((), (), s32[]{:S(2)}) async-start(), calls=%async_computation.3 | async-start | bytes 2359296 | tf_op jit(solution)/shard_map/all_gather | solution.py:224
  9.2 62.3 %all-gather.5.cloned.1.call-start = ((), (), s32[]{:S(2)}) async-start(), calls=%async_computation.2 | async-start | bytes 2359296 | tf_op jit(solution)/shard_map/all_gather | solution.py:239
  25.9 0.8 copy-start.6
  28.8 117.6 %reduce-scatter.5.cloned.1.call-start = ((), (), s32[]{:S(2)}) async-start(), calls=%async_computation.4 | async-start | bytes 4718592 | tf_op jit(solution)/shard_map/reduce_scatter | solution.py:244
  29.2 42.3 %copy-start.1 = (bf16[1024,512]{1,0:T(8,128)(2,1)S(1)}, bf16[1024,512]{1,0:T(8,128)(2,1)}, u32[]{:S(2)}) copy-start(bf16[1024,512]{1,0:T(8,128)(2,1)} %query_ref.1) | copy-start | bytes 3145732
  29.2 42.3 %copy-start.2 = (s32[64]{0:T(128)S(1)}, s32[64]{0:T(128)}, u32[]{:S(2)}) copy-start(s32[64]{0:T(128)} %plan_ref.1) | copy-start | bytes 772
  71.5 1.2 copy-start.5
  93.2 1.0 copy-start.3
  94.2 1.2 copy-start.4
  94.2 104.7 %reduce-scatter.7.cloned.1.call-start = ((), (), s32[]{:S(2)}) async-start(), calls=%async_computation.7 | async-start | bytes 4128768
  110.1 38.5 %copy-start.7 = (f32[1024,64]{1,0:T(8,128)S(1)}, f32[1024,64]{1,0:T(8,128)}, u32[]{:S(2)}) copy-start(f32[1024,64]{1,0:T(8,128)} %copy-done.6) | copy-start | bytes 786436
  110.1 121.0 %all-gather.11.cloned.1.call-start = ((), (), s32[]{:S(2)}) async-start(), calls=%async_computation.6 | async-start | bytes 1310720 | tf_op jit(solution)/shard_map/all_gather | solution.py:249
  146.5 2.1 copy-start.8
  148.3 113.3 %all-gather.9.cloned.1.call-start = ((), (), s32[]{:S(2)}) async-start(), calls=%async_computation.5 | async-start | bytes 1310720 | tf_op jit(solution)/shard_map/all_gather | solution.py:248
Sparse Core Ops, SparseCore 0:
  10.5 30.5 all-gather.6
  43.6 27.8 all-gather.4
  94.3 52.0 reduce-scatter.4
  150.2 48.7 reduce-scatter.6
  200.9 30.1 all-gather.10
  233.1 28.4 all-gather.8

commit v2 on v1

--- a/solution.py
+++ b/solution.py
@@ -79,7 +79,10 @@
 
 def attend_kernel(
     heads,
-    plan_ref,
+    ranks,
+    key_at_ref,
+    value_at_ref,
+    source_ref,
     run_ref,
     slot_ref,
     need_ref,
@@ -87,20 +90,31 @@
     up_ref,
     cos_ref,
     sin_ref,
-    key_ref,
-    value_ref,
     place_ref,
-    gquery_ref,
-    out_ref,
-    gkv_ref,
-    key_win,
-    value_win,
+    *refs,
 ):
+    key_parts, refs = refs[:ranks], refs[ranks:]
+    value_parts, refs = refs[:ranks], refs[ranks:]
+    gquery_ref, out_ref, gkey_keep, gkey_send, gvalue_keep, gvalue_send = refs[:6]
+    key_ref, value_ref, gkey_ref, gvalue_ref, key_win, value_win, sems = refs[6:]
+    rows_each = query_ref.shape[0]
     scale = 1.0 / math.sqrt(HD)
     to_exp2 = scale * math.log2(math.e)
     wide = min(2, heads)
     cols = wide * ROWBLK
-    gkv_ref[...] = jnp.zeros_like(gkv_ref)
+
+    loads = []
+    for item, (parts, whole) in enumerate(((key_parts, key_ref), (value_parts, value_ref))):
+        for rank in range(ranks):
+            copy = pltpu.make_async_copy(
+                parts[rank], whole.at[pl.ds(rank * rows_each, rows_each)], sems.at[item, rank]
+            )
+            copy.start()
+            loads.append(copy)
+    gkey_ref[...] = jnp.zeros_like(gkey_ref)
+    gvalue_ref[...] = jnp.zeros_like(gvalue_ref)
+    for copy in loads:
+        copy.wait()
 
     def window(count, block):
         slot = slot_ref[block]
@@ -108,7 +122,7 @@
         first = jnp.maximum(slot + 1 - count, 0)
         rows = count * ROWBLK
         for step in range(count):
-            source = plan_ref[run * RUN_BLOCKS + first + step]
+            source = source_ref[run * RUN_BLOCKS + first + step]
             start = pl.multiple_of(source * ROWBLK, ROWBLK)
             key_win[pl.ds(step * ROWBLK, ROWBLK), :] = key_ref[pl.ds(start, ROWBLK), :]
             value_win[pl.ds(step * ROWBLK, ROWBLK), :] = value_ref[pl.ds(start, ROWBLK), :]
@@ -146,8 +160,8 @@
             prob = raised * (1.0 / total)
             prob_b = prob.astype(jnp.bfloat16)
             out_t = lax.dot_general(values, prob_b, TN, preferred_element_type=jnp.float32)
-            out_r = out_t.astype(jnp.bfloat16).astype(jnp.float32)
-            delta = jnp.sum(up_t * out_r, axis=0, keepdims=True)
+            out_b = out_t.astype(jnp.bfloat16)
+            delta = jnp.sum(up_t * out_b.astype(jnp.float32), axis=0, keepdims=True)
             gprob = lax.dot_general(values, up, NT, preferred_element_type=jnp.float32)
             gscore = (prob * (gprob - delta)).astype(jnp.bfloat16)
             gquery_t = lax.dot_general(keys, gscore, TN, preferred_element_type=jnp.float32)
@@ -156,72 +170,197 @@
             for item in range(wide):
                 at = (group * wide + item) * HD
                 part = slice(item * ROWBLK, (item + 1) * ROWBLK)
-                out_ref[pl.ds(base, ROWBLK), pl.ds(at, HD)] = out_r[:, part].T.astype(jnp.bfloat16)
+                out_ref[pl.ds(at, HD), pl.ds(base, ROWBLK)] = out_b[:, part]
                 grad = gquery_t[:, part].T * scale
                 back = grad * cosine - pltpu.roll(grad, HD // 2, 1) * sine
                 gquery_ref[pl.ds(base, ROWBLK), pl.ds(at, HD)] = back.astype(jnp.bfloat16)
         gkey = (gkey * scale).astype(jnp.bfloat16)
         gvalue = gvalue.astype(jnp.bfloat16)
         for step in range(count):
-            source = plan_ref[run * RUN_BLOCKS + first + step]
-            start = pl.multiple_of(source * ROWBLK, ROWBLK)
+            block_id = run * RUN_BLOCKS + first + step
             part = slice(step * ROWBLK, (step + 1) * ROWBLK)
-            gkv_ref[pl.ds(start, ROWBLK), pl.ds(0, HD)] = gkey[part]
-            gkv_ref[pl.ds(start, ROWBLK), pl.ds(HD, HD)] = gvalue[part]
+            key_start = pl.multiple_of(key_at_ref[block_id] * ROWBLK, ROWBLK)
+            value_start = pl.multiple_of(value_at_ref[block_id] * ROWBLK, ROWBLK)
+            gkey_ref[pl.ds(key_start, ROWBLK), :] = gkey[part]
+            gvalue_ref[pl.ds(value_start, ROWBLK), :] = gvalue[part]
 
     def body(block, carry):
         need = need_ref[block]
-        sizes = (1, 2, 4, 8)
         floor = 0
-        for size in sizes:
+        for size in (1, 2, 4, 8):
             pl.when((need > floor) & (need <= size))(partial(window, size, block))
             floor = size
         return carry
 
-    lax.fori_loop(0, query_ref.shape[0] // ROWBLK, body, 0)
-
-
-def attend(plan, run, slot, need, query, up, cosine, sine, keys, values, places):
+    lax.fori_loop(0, rows_each // ROWBLK, body, 0)
+    half = ranks * rows_each // 2
+    stores = []
+    for item, (whole, keep, send) in enumerate(
+        ((gkey_ref, gkey_keep, gkey_send), (gvalue_ref, gvalue_keep, gvalue_send))
+    ):
+        for place, target in enumerate((keep, send)):
+            copy = pltpu.make_async_copy(
+                whole.at[pl.ds(place * half, half)], target, sems.at[item, place]
+            )
+            copy.start()
+            stores.append(copy)
+    for copy in stores:
+        copy.wait()
+
+
+def attend(tables, query, up, cosine, sine, places, keys, values):
     rows, width = query.shape
     heads = width // HD
-    every = keys.shape[0]
+    ranks = len(keys)
+    every = rows * ranks
     smem = pl.BlockSpec(memory_space=pltpu.SMEM)
     vmem = pl.BlockSpec(memory_space=pltpu.VMEM)
+    hbm = pl.BlockSpec(memory_space=pl.ANY)
     pairs = rows * RUN_BLOCKS * ROWBLK * heads
+    half = jax.ShapeDtypeStruct((every // 2, HD), jnp.bfloat16)
     return pl.pallas_call(
-        partial(attend_kernel, heads),
+        partial(attend_kernel, heads, ranks),
         out_shape=(
             jax.ShapeDtypeStruct((rows, width), jnp.bfloat16),
-            jax.ShapeDtypeStruct((rows, width), jnp.bfloat16),
-            jax.ShapeDtypeStruct((every, 2 * HD), jnp.bfloat16),
+            jax.ShapeDtypeStruct((width, rows), jnp.bfloat16),
+            half,
+            half,
+            half,
+            half,
         ),
-        in_specs=[smem] * 4 + [vmem] * 7,
-        out_specs=(vmem, vmem, vmem),
-        scratch_shapes=[
-            pltpu.VMEM((RUN_BLOCKS * ROWBLK, HD), jnp.bfloat16),
-            pltpu.VMEM((RUN_BLOCKS * ROWBLK, HD), jnp.bfloat16),
-        ],
+        in_specs=[smem] * 6 + [vmem] * 5 + [hbm] * (2 * ranks),
+        out_specs=(vmem, vmem, hbm, hbm, hbm, hbm),
+        scratch_shapes=[pltpu.VMEM((every, HD), jnp.bfloat16)] * 4
+        + [pltpu.VMEM((RUN_BLOCKS * ROWBLK, HD), jnp.bfloat16)] * 2
+        + [pltpu.SemaphoreType.DMA((2, ranks))],
         compiler_params=pltpu.CompilerParams(vmem_limit_bytes=48 * 1024 * 1024),
         cost_estimate=pl.CostEstimate(
             flops=10 * pairs * HD, bytes_accessed=16 * 1024 * 1024, transcendentals=pairs
         ),
-    )(plan, run, slot, need, query, up, cosine, sine, keys, values, places)
+    )(*tables, query, up, cosine, sine, places, *keys, *values)
+
+
+def assemble_kernel(lanes, order_ref, *refs):
+    sources, outs, sems = refs[: 2 * lanes], refs[2 * lanes : 2 * lanes + 2], refs[-1]
+    copies = []
+    for index, source in enumerate(sources):
+        column = pl.multiple_of(order_ref[index] * HD, HD)
+        target = outs[index // lanes].at[:, pl.ds(column, HD)]
+        copy = pltpu.make_async_copy(source, target, sems.at[index])
+        copy.start()
+        copies.append(copy)
+    for copy in copies:
+        copy.wait()
+
+
+def assemble(order, pieces):
+    lanes = len(pieces) // 2
+    hbm = pl.BlockSpec(memory_space=pl.ANY)
+    whole = jax.ShapeDtypeStruct((pieces[0].shape[0], lanes * HD), pieces[0].dtype)
+    return pl.pallas_call(
+        partial(assemble_kernel, lanes),
+        out_shape=(whole, whole),
+        in_specs=[pl.BlockSpec(memory_space=pltpu.SMEM)] + [hbm] * len(pieces),
+        out_specs=(hbm, hbm),
+        scratch_shapes=[pltpu.SemaphoreType.DMA((len(pieces),))],
+    )(order, *pieces)
+
+
+def swap(array, bit):
+    ranks = lax.axis_size("dp")
+    return lax.ppermute(array, "dp", [(rank, rank ^ bit) for rank in range(ranks)])
+
+
+def spread(array, bits):
+    found = {0: array}
+    for bit in bits:
+        found.update({place | bit: swap(item, bit) for place, item in list(found.items())})
+    return [found[place] for place in range(len(found))]
+
+
+def added(left, right):
+    return left.astype(jnp.float32) + right.astype(jnp.float32)
+
+
+def halve(keep, send, bits):
+    received = swap(send, bits[0])
+    for bit in bits[1:]:
+        half = keep.shape[0] // 2
+        send = added(keep[half:], received[half:]).astype(keep.dtype)
+        keep = added(keep[:half], received[:half]).astype(keep.dtype)
+        received = swap(send, bit)
+    return added(keep, received)
+
+
+def place_of(distance, bits):
+    place = jnp.zeros_like(distance)
+    for bit in bits:
+        place = place * 2 + (distance & bit) // bit
+    return place
+
+
+def weight_sum(attn_t, grad_out, my_rank, bits):
+    width = attn_t.shape[0]
+    odd = my_rank & 1
+    halves = attn_t.reshape(2, width // 2, attn_t.shape[1])
+
+    def product(which):
+        picked = lax.dynamic_index_in_dim(halves, which, 0, keepdims=False)
+        return jnp.dot(picked, grad_out, preferred_element_type=jnp.float32)
+
+    received = swap(product(1 - odd).astype(jnp.bfloat16), 1)
+    total = product(odd) + received.astype(jnp.float32)
+    pair_count = lax.axis_size("dp") // 2
+    pair_rows = grad_out.shape[1] // pair_count
+    sums = []
+    for part, order in enumerate((bits[1:], bits[1:][::-1])):
+        rows = total[part * width // 4 : (part + 1) * width // 4]
+        pieces = {
+            2 * pair: rows[:, pair * pair_rows : (pair + 1) * pair_rows]
+            for pair in range(pair_count)
+        }
+        for bit in order:
+            high = (my_rank & bit) > 0
+            lows = [rank for rank in sorted(pieces) if not rank & bit]
+            send = jnp.concatenate(
+                [jnp.where(high, pieces[rank], pieces[rank | bit]) for rank in lows], axis=1
+            )
+            back = swap(send.astype(jnp.bfloat16), bit).astype(jnp.float32)
+            pieces = {
+                rank: jnp.where(high, pieces[rank | bit], pieces[rank])
+                + back[:, at * pair_rows : (at + 1) * pair_rows]
+                for at, rank in enumerate(lows)
+            }
+        sums.append(pieces[0])
+    total = jnp.concatenate(sums, axis=0)
+    first, second = total[:, : pair_rows // 2], total[:, pair_rows // 2 :]
+    is_odd = odd > 0
+    other = swap(jnp.where(is_odd, first, second).astype(jnp.bfloat16), 1).astype(jnp.float32)
+    mine = jnp.where(is_odd, second, first)
+    return jnp.concatenate(
+        [jnp.where(is_odd, other, mine), jnp.where(is_odd, mine, other)], axis=0
+    )
 
 
 def local(query, key, value, grad_out, out_weight, plan, segments):
     rank_count = lax.axis_size("dp")
+    lane_count = lax.axis_size("tensor")
     my_rank = lax.axis_index("dp")
     my_lane = lax.axis_index("tensor")
     row_count = query.shape[0]
     block_count = row_count // ROWBLK
     local_heads = query.shape[1] // HD
     group = HEADS // KV
+    bits = [1 << at for at in range(rank_count.bit_length() - 1)]
     kv_head = my_lane * local_heads // group
     own_key = lax.dynamic_slice_in_dim(key, kv_head * HD, HD, 1)
     own_value = lax.dynamic_slice_in_dim(value, kv_head * HD, HD, 1)
 
-    places_all = lax.all_gather(positions_of(segments), "dp", axis=0, tiled=True)
-    values = lax.all_gather(own_value, "dp", axis=0, tiled=True)
+    own_places = positions_of(segments).reshape(block_count, ROWBLK)
+    places_all = jnp.concatenate(
+        [own_places] + [swap(own_places, step) for step in range(1, rank_count)], axis=0
+    )
+    values = spread(own_value, bits[1:] + bits[:1])
     up = jnp.dot(grad_out, out_weight, preferred_element_type=jnp.float32).astype(jnp.bfloat16)
 
     mine = my_rank * block_count + jnp.arange(block_count, dtype=jnp.int32)
@@ -231,30 +370,43 @@
     )
     run = dest // RUN_BLOCKS
     slot = dest % RUN_BLOCKS
-    places = jnp.take(places_all.reshape(-1, ROWBLK), dest, axis=0)
+    places = jnp.take(places_all, (run ^ my_rank) * RUN_BLOCKS + slot, axis=0)
     need = slot - (slot * ROWBLK - places[:, 0]) // ROWBLK + 1
     cosine, sine = rope_tables(places.reshape(row_count), HD)
     key_f = own_key.astype(jnp.float32)
     rot_key = (key_f * cosine + swap_halves(key_f) * sine).astype(jnp.bfloat16)
-    keys = lax.all_gather(rot_key, "dp", axis=0, tiled=True)
-
-    grad_query, attn_out, gkv = attend(
-        plan, run, slot, need, query, up, cosine, sine, keys, values, places
-    )
-    gkv_sum = lax.psum_scatter(gkv, "dp", scatter_dimension=0, tiled=True)
-    gkey = gkv_sum[:, :HD].astype(jnp.float32)
+    keys = spread(rot_key, bits[:0:-1] + bits[:1])
+
+    distance = (plan // block_count) ^ my_rank
+    within = plan % block_count
+    key_bits = bits[:1] + bits[:0:-1]
+    tables = (
+        place_of(distance, key_bits) * block_count + within,
+        place_of(distance, bits) * block_count + within,
+        distance * block_count + within,
+        run,
+        slot,
+        need,
+    )
+    grad_query, attn_t, gkey_keep, gkey_send, gvalue_keep, gvalue_send = attend(
+        tables, query, up, cosine, sine, places, keys, values
+    )
+    value_partial = halve(gvalue_keep, gvalue_send, bits).astype(jnp.bfloat16)
+    gkey = halve(gkey_keep, gkey_send, key_bits)
     key_partial = (gkey * cosine - swap_halves(gkey) * sine).astype(jnp.bfloat16)
-    value_partial = gkv_sum[:, HD:]
-    key_all = lax.all_gather(key_partial, "tensor", axis=1, tiled=True)
-    value_all = lax.all_gather(value_partial, "tensor", axis=1, tiled=True)
-
-    weight_term = jnp.dot(
-        grad_out.T, attn_out, preferred_element_type=jnp.float32
-    ).astype(jnp.bfloat16)
-    weight_grad = lax.psum_scatter(
-        weight_term, "dp", scatter_dimension=0, tiled=True
-    ).astype(jnp.float32)
-
+
+    key_ring = [key_partial]
+    value_ring = [value_partial]
+    down = [(lane, (lane - 1) % lane_count) for lane in range(lane_count)]
+    above = [(lane, (lane + 1) % lane_count) for lane in range(lane_count)]
+    for unused in range(lane_count - 1):
+        value_ring.append(lax.ppermute(value_ring[-1], "tensor", above))
+        key_ring.append(lax.ppermute(key_ring[-1], "tensor", down))
+    step = jnp.arange(lane_count, dtype=jnp.int32)
+    order = jnp.concatenate([(my_lane + step) % lane_count, (my_lane - step) % lane_count])
+    key_all, value_all = assemble(order, key_ring + value_ring)
+
+    weight_grad = weight_sum(attn_t, grad_out, my_rank, bits).T
     lanes_per_key = group // local_heads
 
     def combine(gathered):

time: 274 us -> 215 us (0.78)
  waiting for transfers between devices: 179 us -> 45.7 us
  Pallas kernels: 20.5 us -> 87.1 us
  starting transfers between devices: 0.43 us -> 37.7 us
  local copies, waits for them, and re-layouts: 20.4 us -> 5.27 us
  between operations: 14.2 us -> 1.09 us
  blocking collectives: 10.5 us -> 0 us
  other arithmetic: 10.4 us -> 17.6 us
    all_gather x4 -> x0, waiting for transfers between devices: 92.9 us -> none  [the longest x1 30.5 us: local(): key_all = lax.all_gather(key_partial, 'tensor', axis=1, tiled=True)]
    pallas_call x1 -> x2, Pallas kernels: 20.5 us -> 87.1 us  [the longest x1 65.4 us: assemble(): pl.pallas_call(partial(assemble_kernel, lanes), out_shape=(whole, whole),...]
    unnamed x7 -> x0, waiting for transfers between devices: 49.3 us -> none
    ppermute x0 -> x39, waiting for transfers between devices: none -> 45.7 us  [the longest x33 25.6 us: swap(): lax.ppermute(array, 'dp', [(rank, rank ^ bit) for rank in range(ranks)])]
    ppermute x0 -> x39, starting transfers between devices: none -> 37.7 us  [the longest x33 27.3 us: swap(): lax.ppermute(array, 'dp', [(rank, rank ^ bit) for rank in range(ranks)])]
    reduce_scatter x1 -> x0, waiting for transfers between devices: 36.3 us -> none  [local(): gkv_sum = lax.psum_scatter(gkv, 'dp', scatter_dimension=0, tiled=True)]
    unnamed x23 -> x29, local copies, waits for them, and re-layouts: 18.4 us -> 3.06 us
    all_gather x1 -> x0, blocking collectives: 10.5 us -> none  [local(): lax.all_gather(positions_of(segments), 'dp', axis=0, tiled=True)]
  transfers between devices with their start and end apart: 6 -> 39, of which waited for: 6 -> 11; matrix products, arithmetic and copies ran while one was open for 14% -> 18% of each run, Pallas kernels for 0% -> 31%
where the time goes in v2:
time: 215 us; the launch traced here: 214 us
  Pallas kernels  87.1 us (41%)
  waiting for transfers between devices  45.7 us (21%)
  starting transfers between devices  37.7 us (18%)
  matrix products  19.7 us (9%)
  other arithmetic  17.6 us (8%)
  local copies, waits for them, and re-layouts  5.27 us (2%)
    pallas_call x1, Pallas kernels, assemble(): pl.pallas_call(partial(assemble_kernel, lanes), out_shape=(whole, whole),...  65.4 us
    ppermute x33, starting transfers between devices, swap(): lax.ppermute(array, 'dp', [(rank, rank ^ bit) for rank in range(ranks)])  27.3 us
    ppermute x33, waiting for transfers between devices, swap(): lax.ppermute(array, 'dp', [(rank, rank ^ bit) for rank in range(ranks)])  25.6 us
    pallas_call x1, Pallas kernels, attend(): pl.pallas_call(partial(attend_kernel, heads, ranks), out_shape=(jax.Shape...  21.8 us
    ppermute x3, waiting for transfers between devices, local(): value_ring.append(lax.ppermute(value_ring[-1], 'tensor', above))  18.6 us
    dot_general x2, matrix products, product(): return jnp.dot(picked, grad_out, preferred_element_type=jnp.float32)  12.3 us
    ppermute x3, starting transfers between devices, local(): key_ring.append(lax.ppermute(key_ring[-1], 'tensor', down))  10.3 us
    dot_general x1, matrix products, local(): jnp.dot(grad_out, out_weight, preferred_element_type=jnp.float32)  7.32 us
  transfers between devices with their start and end apart: 39, of which 11 were waited for; matrix products, arithmetic and copies ran while one was open for 18% of the time, Pallas kernels for 31%

profile of v2, /device:TPU:0, one launch (start us, length us, event | category | flops | bytes accessed | tf_op | source)
XLA Modules:
  0.0 214.2 jit_solution(5452222221901201214)
XLA Ops:
  2.6 2.6 %collective-permute-start.1 = (s32[8,128]{1,0:T(8,128)S(1)}, s32[8,128]{1,0:T(8,128)S(1)}, u32[]{:S(2)}, u32[]{:S(2)}) collective-permute-start(s32[8,128]{1,0:T(8,128)S(1)} %get-tuple-element.48), channel_id=1, source_target_pairs={{0,8},{4,12},{8,0},{12,4},{16,24},{20,28},{24,16},{28,20},{1,9},{5... | collective-permute-start | bytes 12296 | tf_op jit(solution)/shard_map/ppermute | solution.py:271
  5.3 1.8 collective-permute-start.3
  10.1 2.7 %collective-permute-start.5 = (s32[8,128]{1,0:T(8,128)S(1)}, s32[8,128]{1,0:T(8,128)S(1)}, u32[]{:S(2)}, u32[]{:S(2)}) collective-permute-start(s32[8,128]{1,0:T(8,128)S(1)} %get-tuple-element.48), channel_id=1, source_target_pairs={{0,24},{4,28},{8,16},{12,20},{16,8},{20,12},{24,0},{28,4},{1,25},{... | collective-permute-start | bytes 12296 | tf_op jit(solution)/shard_map/ppermute | solution.py:271
  13.3 1.6 collective-permute-start.15
  14.9 1.5 collective-permute-start.17
  17.4 1.9 fusion.15
  19.3 1.8 fusion.5
  21.7 7.3 %convolution_convert_fusion.1.up_ref = bf16[1024,512]{1,0:T(8,128)(2,1)} fusion(bf16[1024,3584]{1,0:T(8,128)(2,1)} %param.10, bf16[3584,512]{1,0:T(8,128)(2,1)S(1)} %copy-done.10), kind=kOutput, calls=%fused_computation.3 | convolution fusion | flops 3758620672 | bytes 12058624 | tf_op jit(solution)/shard_map/dot_general | solution.py:364
  30.0 1.4 collective-permute-start.19
  31.4 1.5 collective-permute-start.12
  33.0 5.3 %collective-permute-done.8.refs_2_ = bf16[1024,128]{1,0:T(8,128)(2,1)S(1)} collective-permute-done((bf16[1024,128]{1,0:T(8,128)(2,1)S(1)}, bf16[1024,128]{1,0:T(8,128)(2,1)S(1)}, u32[]{:S(2)}, u32[]{:S(2)}) %collective-permute-start.8) | collective-permute-done | bytes 262176 | tf_op jit(solution)/shard_map/ppermute | solution.py:271
  38.9 4.6 %collective-permute-done.12.refs_6_ = bf16[1024,128]{1,0:T(8,128)(2,1)S(1)} collective-permute-done((bf16[1024,128]{1,0:T(8,128)(2,1)S(1)}, bf16[1024,128]{1,0:T(8,128)(2,1)S(1)}, u32[]{:S(2)}, u32[]{:S(2)}) %collective-permute-start.12) | collective-permute-done | bytes 262176 | tf_op jit(solution)/shard_map/ppermute | solution.py:271
  43.6 1.4 collective-permute-done.13.refs_7_
  45.0 21.8 %shard_map.102 = (bf16[1024,512]{1,0:T(8,128)(2,1)}, bf16[512,1024]{1,0:T(8,128)(2,1)}, bf16[4096,128]{1,0:T(8,128)(2,1)}, bf16[4096,128]{1,0:T(8,128)(2,1)}, bf...) custom-call(s32[64]{0:T(128)S(1)} %multiply_add_fusion.4.key_at_ref, s32[64]{0:T(128)S(1)} %get-tuple-element.52.value_at_ref, ...), custom_call_target="tpu_custom_call" | custom-call | flops 5368709120 | bytes 16777216 | tf_op jit(solution)/shard_map/pallas_call | solution.py:221
  67.3 6.7 %convolution_convert_fusion = bf16[256,3584]{1,0:T(8,128)(2,1)} fusion(bf16[1024,3584]{1,0:T(8,128)(2,1)} %param.10, bf16[2,256,1024]{2,1,0:T(8,128)(2,1)} %bitcast.38, s32[]{:T(128)S(6)} %select_n.189), kind=kOutput, calls=%fused_computation.1 | convolution fusion | flops 1879965696 | bytes 9699332 | tf_op jit(solution)/shard_map/dot_general | solution.py:309
  75.0 1.5 add_convert_fusion.3
  77.7 3.0 %collective-permute-start.28 = (bf16[2048,128]{1,0:T(8,128)(2,1)}, bf16[2048,128]{1,0:T(8,128)(2,1)}, u32[]{:S(2)}, u32[]{:S(2)}) collective-permute-start(bf16[2048,128]{1,0:T(8,128)(2,1)} %get-tuple-element.63), channel_id=1, source_target_pairs={{0,8},{4,12},{8,0},{12,4},{16,24},{20,28},{24,16},{28,20},{1,9},{5... | collective-permute-start | bytes 1572872 | tf_op jit(solution)/shard_map/ppermute | solution.py:271
  80.7 10.1 %collective-permute-done.22 = bf16[2048,128]{1,0:T(8,128)(2,1)S(1)} collective-permute-done((bf16[2048,128]{1,0:T(8,128)(2,1)S(1)}, bf16[2048,128]{1,0:T(8,128)(2,1)S(1)}, u32[]{:S(2)}, u32[]{:S(2)}) %collective-permute-start.22) | collective-permute-done | bytes 524320 | tf_op jit(solution)/shard_map/ppermute | solution.py:271
  92.5 1.3 collective-permute-start.23
  94.9 1.8 collective-permute-start.29
  96.7 3.9 %collective-permute-done.23 = bf16[1024,128]{1,0:T(8,128)(2,1)S(1)} collective-permute-done((bf16[1024,128]{1,0:T(8,128)(2,1)}, bf16[1024,128]{1,0:T(8,128)(2,1)S(1)}, u32[]{:S(2)}, u32[]{:S(2)}) %collective-permute-start.23) | collective-permute-done | bytes 262176 | tf_op jit(solution)/shard_map/ppermute | solution.py:271
  102.3 3.6 %collective-permute-start.24 = (bf16[1024,128]{1,0:T(8,128)(2,1)S(1)}, bf16[1024,128]{1,0:T(8,128)(2,1)}, u32[]{:S(2)}, u32[]{:S(2)}) collective-permute-start(bf16[1024,128]{1,0:T(8,128)(2,1)S(1)} %fusion.7.refs_0_), channel_id=1, source_target_pairs={{0,3},{1,0},{2,1},{3,2},{4,7},{5,4},{6,5},{7,6},{8,11},{9,8},{10,9... | collective-permute-start | bytes 786440 | tf_op jit(solution)/shard_map/ppermute | solution.py:404
  106.0 5.7 %convert_add_fusion = f32[256,3584]{1,0:T(8,128)S(1)} fusion(bf16[256,3584]{1,0:T(8,128)(2,1)} %collective-permute-done.33, bf16[1024,3584]{1,0:T(8,128)(2,1)} %param.10, bf16[2,256,1024]{2,1,0:T(8,128)(2,1)S(1)} %bitcast.39, s32[]{:T(128)S(6)} %select_n.188), kind=kOutput, calls=%fused_computation.2 | convolution fusion | flops 1880883200 | bytes 13369348 | tf_op jit(solution)/shard_map/dot_general | solution.py:309
  111.9 1.6 collective-permute-start.34
  113.5 1.6 collective-permute-start.36
  116.3 3.8 %collective-permute-start.25 = (bf16[1024,128]{1,0:T(8,128)(2,1)}, bf16[1024,128]{1,0:T(8,128)(2,1)}, u32[]{:S(2)}, u32[]{:S(2)}) collective-permute-start(bf16[1024,128]{1,0:T(8,128)(2,1)} %collective-permute-done.24.refs_1_), channel_id=1, source_target_pairs={{0,3},{1,0},{2,1},{3,2},{4,7},{5,4},{6,5},{7,6},{8,11},{9,8},{10,9... | collective-permute-start | bytes 786440 | tf_op jit(solution)/shard_map/ppermute | solution.py:404
  120.1 7.2 %collective-permute-done.30.refs_5_ = bf16[1024,128]{1,0:T(8,128)(2,1)S(1)} collective-permute-done((bf16[1024,128]{1,0:T(8,128)(2,1)S(1)}, bf16[1024,128]{1,0:T(8,128)(2,1)S(1)}, u32[]{:S(2)}, u32[]{:S(2)}) %collective-permute-start.30) | collective-permute-done | bytes 262176 | tf_op jit(solution)/shard_map/ppermute | solution.py:403
  130.5 2.9 %collective-permute-start.26 = (bf16[1024,128]{1,0:T(8,128)(2,1)}, bf16[1024,128]{1,0:T(8,128)(2,1)}, u32[]{:S(2)}, u32[]{:S(2)}) collective-permute-start(bf16[1024,128]{1,0:T(8,128)(2,1)} %collective-permute-done.25.refs_2_), channel_id=1, source_target_pairs={{0,3},{1,0},{2,1},{3,2},{4,7},{5,4},{6,5},{7,6},{8,11},{9,8},{10,9... | collective-permute-start | bytes 786440 | tf_op jit(solution)/shard_map/ppermute | solution.py:404
  133.3 5.3 %collective-permute-done.31.refs_6_ = bf16[1024,128]{1,0:T(8,128)(2,1)} collective-permute-done((bf16[1024,128]{1,0:T(8,128)(2,1)S(1)}, bf16[1024,128]{1,0:T(8,128)(2,1)}, u32[]{:S(2)}, u32[]{:S(2)}) %collective-permute-start.31) | collective-permute-done | bytes 262176 | tf_op jit(solution)/shard_map/ppermute | solution.py:403
  141.1 6.0 %collective-permute-done.32.refs_7_ = bf16[1024,128]{1,0:T(8,128)(2,1)} collective-permute-done((bf16[1024,128]{1,0:T(8,128)(2,1)}, bf16[1024,128]{1,0:T(8,128)(2,1)}, u32[]{:S(2)}, u32[]{:S(2)}) %collective-permute-start.32) | collective-permute-done | bytes 262176 | tf_op jit(solution)/shard_map/ppermute | solution.py:403
  147.1 65.4 %shard_map.103 = (bf16[1024,512]{1,0:T(8,128)(2,1)}, bf16[1024,512]{1,0:T(8,128)(2,1)}) custom-call(s32[8]{0:T(128)} %pad_add_fusion.order_ref, bf16[1024,128]{1,0:T(8,128)(2,1)} %copy-done.5, bf16[1024,128]{1,0:T(8,128)(2,1)} %collective-permute-done.24.refs_1_, bf16[1024,128]{1,0:T(8,128)(2,1)} %collective-permute-done.25.refs_2_, ...), custom_call_target="tpu_custom_call" | custom-call | tf_op jit(solution)/shard_map/pallas_call | solution.py:260
  212.9 1.2 copy.13
  (128 shorter events, 23.3 us)
Async XLA Ops:
  2.2 7.9 %collective-permute-start = (s32[8,128]{1,0:T(8,128)S(1)}, s32[8,128]{1,0:T(8,128)S(1)}, u32[]{:S(2)}, u32[]{:S(2)}) collective-permute-start(s32[8,128]{1,0:T(8,128)S(1)} %get-tuple-element.48), channel_id=1, source_target_pairs={{0,4},{4,0},{8,12},{12,8},{16,20},{20,16},{24,28},{28,24},{1,5},{5... | collective-permute-start | bytes 12296 | tf_op jit(solution)/shard_map/ppermute | solution.py:271
  2.6 10.2 %collective-permute-start.1 = (s32[8,128]{1,0:T(8,128)S(1)}, s32[8,128]{1,0:T(8,128)S(1)}, u32[]{:S(2)}, u32[]{:S(2)}) collective-permute-start(s32[8,128]{1,0:T(8,128)S(1)} %get-tuple-element.48), channel_id=1, source_target_pairs={{0,8},{4,12},{8,0},{12,4},{16,24},{20,28},{24,16},{28,20},{1,9},{5... | collective-permute-start | bytes 12296 | tf_op jit(solution)/shard_map/ppermute | solution.py:271
  5.2 7.8 %collective-permute-start.2 = (s32[8,128]{1,0:T(8,128)S(1)}, s32[8,128]{1,0:T(8,128)S(1)}, u32[]{:S(2)}, u32[]{:S(2)}) collective-permute-start(s32[8,128]{1,0:T(8,128)S(1)} %get-tuple-element.48), channel_id=1, source_target_pairs={{0,12},{4,8},{8,4},{12,0},{16,28},{20,24},{24,20},{28,16},{1,13},{... | collective-permute-start | bytes 12296 | tf_op jit(solution)/shard_map/ppermute | solution.py:271
  5.3 8.0 %collective-permute-start.3 = (s32[8,128]{1,0:T(8,128)S(1)}, s32[8,128]{1,0:T(8,128)S(1)}, u32[]{:S(2)}, u32[]{:S(2)}) collective-permute-start(s32[8,128]{1,0:T(8,128)S(1)} %get-tuple-element.48), channel_id=1, source_target_pairs={{0,16},{4,20},{8,24},{12,28},{16,0},{20,4},{24,8},{28,12},{1,17},{... | collective-permute-start | bytes 12296 | tf_op jit(solution)/shard_map/ppermute | solution.py:271
  7.0 7.9 %collective-permute-start.4 = (s32[8,128]{1,0:T(8,128)S(1)}, s32[8,128]{1,0:T(8,128)S(1)}, u32[]{:S(2)}, u32[]{:S(2)}) collective-permute-start(s32[8,128]{1,0:T(8,128)S(1)} %get-tuple-element.48), channel_id=1, source_target_pairs={{0,20},{4,16},{8,28},{12,24},{16,4},{20,0},{24,12},{28,8},{1,21},{... | collective-permute-start | bytes 12296 | tf_op jit(solution)/shard_map/ppermute | solution.py:271
  12.9 16.1 %collective-permute-start.14 = (bf16[1024,128]{1,0:T(8,128)(2,1)S(1)}, bf16[1024,128]{1,0:T(8,128)(2,1)S(1)}, u32[]{:S(2)}, u32[]{:S(2)}) collective-permute-start(bf16[1024,128]{1,0:T(8,128)(2,1)S(1)} %constant_dynamic-slice_fusion.refs_8_), channel_id=1, source_target_pairs={{0,4},{4,0},{8,12},{12,8},{16,20},{20,16},{24,28},{28,24},{1,5},{5... | collective-permute-start | bytes 786440 | tf_op jit(solution)/shard_map/ppermute | solution.py:271
  13.3 16.5 %collective-permute-start.15 = (bf16[1024,128]{1,0:T(8,128)(2,1)S(1)}, bf16[1024,128]{1,0:T(8,128)(2,1)S(1)}, u32[]{:S(2)}, u32[]{:S(2)}) collective-permute-start(bf16[1024,128]{1,0:T(8,128)(2,1)S(1)} %constant_dynamic-slice_fusion.refs_8_), channel_id=1, source_target_pairs={{0,8},{4,12},{8,0},{12,4},{16,24},{20,28},{24,16},{28,20},{1,9},{5... | collective-permute-start | bytes 786440 | tf_op jit(solution)/shard_map/ppermute | solution.py:271
  14.9 15.1 %collective-permute-start.17 = (bf16[1024,128]{1,0:T(8,128)(2,1)S(1)}, bf16[1024,128]{1,0:T(8,128)(2,1)S(1)}, u32[]{:S(2)}, u32[]{:S(2)}) collective-permute-start(bf16[1024,128]{1,0:T(8,128)(2,1)S(1)} %constant_dynamic-slice_fusion.refs_8_), channel_id=1, source_target_pairs={{0,16},{4,20},{8,24},{12,28},{16,0},{20,4},{24,8},{28,12},{1,17},{... | collective-permute-start | bytes 786440 | tf_op jit(solution)/shard_map/ppermute | solution.py:271
  21.1 10.3 %collective-permute-start.10 = (bf16[1024,128]{1,0:T(8,128)(2,1)S(1)}, bf16[1024,128]{1,0:T(8,128)(2,1)S(1)}, u32[]{:S(2)}, u32[]{:S(2)}) collective-permute-start(bf16[1024,128]{1,0:T(8,128)(2,1)S(1)} %get-tuple-element.40.refs_0_), channel_id=1, source_target_pairs={{0,16},{4,20},{8,24},{12,28},{16,0},{20,4},{24,8},{28,12},{1,17},{... | collective-permute-start | bytes 786440 | tf_op jit(solution)/shard_map/ppermute | solution.py:271
  29.1 9.2 %collective-permute-start.8 = (bf16[1024,128]{1,0:T(8,128)(2,1)S(1)}, bf16[1024,128]{1,0:T(8,128)(2,1)S(1)}, u32[]{:S(2)}, u32[]{:S(2)}) collective-permute-start(bf16[1024,128]{1,0:T(8,128)(2,1)S(1)} %get-tuple-element.40.refs_0_), channel_id=1, source_target_pairs={{0,8},{4,12},{8,0},{12,4},{16,24},{20,28},{24,16},{28,20},{1,9},{5... | collective-permute-start | bytes 786440 | tf_op jit(solution)/shard_map/ppermute | solution.py:271
  29.8 8.5 %collective-permute-start.16 = (bf16[1024,128]{1,0:T(8,128)(2,1)S(1)}, bf16[1024,128]{1,0:T(8,128)(2,1)S(1)}, u32[]{:S(2)}, u32[]{:S(2)}) collective-permute-start(bf16[1024,128]{1,0:T(8,128)(2,1)S(1)} %collective-permute-done.15.refs_10_), channel_id=1, source_target_pairs={{0,4},{4,0},{8,12},{12,8},{16,20},{20,16},{24,28},{28,24},{1,5},{5... | collective-permute-start | bytes 786440 | tf_op jit(solution)/shard_map/ppermute | solution.py:271
  30.0 8.8 %collective-permute-start.19 = (bf16[1024,128]{1,0:T(8,128)(2,1)S(1)}, bf16[1024,128]{1,0:T(8,128)(2,1)S(1)}, u32[]{:S(2)}, u32[]{:S(2)}) collective-permute-start(bf16[1024,128]{1,0:T(8,128)(2,1)S(1)} %collective-permute-done.15.refs_10_), channel_id=1, source_target_pairs={{0,16},{4,20},{8,24},{12,28},{16,0},{20,4},{24,8},{28,12},{1,17},{... | collective-permute-start | bytes 786440 | tf_op jit(solution)/shard_map/ppermute | solution.py:271
  31.4 12.0 %collective-permute-start.12 = (bf16[1024,128]{1,0:T(8,128)(2,1)S(1)}, bf16[1024,128]{1,0:T(8,128)(2,1)S(1)}, u32[]{:S(2)}, u32[]{:S(2)}) collective-permute-start(bf16[1024,128]{1,0:T(8,128)(2,1)S(1)} %collective-permute-done.10.refs_4_), channel_id=1, source_target_pairs={{0,8},{4,12},{8,0},{12,4},{16,24},{20,28},{24,16},{28,20},{1,9},{5... | collective-permute-start | bytes 786440 | tf_op jit(solution)/shard_map/ppermute | solution.py:271
  32.9 10.6 %collective-permute-start.18 = (bf16[1024,128]{1,0:T(8,128)(2,1)S(1)}, bf16[1024,128]{1,0:T(8,128)(2,1)S(1)}, u32[]{:S(2)}, u32[]{:S(2)}) collective-permute-start(bf16[1024,128]{1,0:T(8,128)(2,1)S(1)} %collective-permute-done.17.refs_12_), channel_id=1, source_target_pairs={{0,4},{4,0},{8,12},{12,8},{16,20},{20,16},{24,28},{28,24},{1,5},{5... | collective-permute-start | bytes 786440 | tf_op jit(solution)/shard_map/ppermute | solution.py:271
  66.7 7.3 %collective-permute-start.21 = (bf16[4096,128]{1,0:T(8,128)(2,1)}, bf16[4096,128]{1,0:T(8,128)(2,1)S(1)}, u32[]{:S(2)}, u32[]{:S(2)}) collective-permute-start(bf16[4096,128]{1,0:T(8,128)(2,1)} %get-tuple-element.14), channel_id=1, source_target_pairs={{0,4},{4,0},{8,12},{12,8},{16,20},{20,16},{24,28},{28,24},{1,5},{5... | collective-permute-start | bytes 3145736 | tf_op jit(solution)/shard_map/ppermute | solution.py:271
  66.8 9.8 %collective-permute-start.27 = (bf16[4096,128]{1,0:T(8,128)(2,1)}, bf16[4096,128]{1,0:T(8,128)(2,1)S(1)}, u32[]{:S(2)}, u32[]{:S(2)}) collective-permute-start(bf16[4096,128]{1,0:T(8,128)(2,1)} %get-tuple-element.16), channel_id=1, source_target_pairs={{0,4},{4,0},{8,12},{12,8},{16,20},{20,16},{24,28},{28,24},{1,5},{5... | collective-permute-start | bytes 3145736 | tf_op jit(solution)/shard_map/ppermute | solution.py:271
  74.0 32.0 %collective-permute-start.33 = (bf16[256,3584]{1,0:T(8,128)(2,1)}, bf16[256,3584]{1,0:T(8,128)(2,1)}, u32[]{:S(2)}, u32[]{:S(2)}) collective-permute-start(bf16[256,3584]{1,0:T(8,128)(2,1)} %convolution_convert_fusion), channel_id=1, source_target_pairs={{0,4},{4,0},{8,12},{12,8},{16,20},{20,16},{24,28},{28,24},{1,5},{5... | collective-permute-start | bytes 5505032 | tf_op jit(solution)/shard_map/ppermute | solution.py:271
  76.5 14.3 %collective-permute-start.22 = (bf16[2048,128]{1,0:T(8,128)(2,1)S(1)}, bf16[2048,128]{1,0:T(8,128)(2,1)S(1)}, u32[]{:S(2)}, u32[]{:S(2)}) collective-permute-start(bf16[2048,128]{1,0:T(8,128)(2,1)S(1)} %get-tuple-element.65), channel_id=1, source_target_pairs={{0,16},{4,20},{8,24},{12,28},{16,0},{20,4},{24,8},{28,12},{1,17},{... | collective-permute-start | bytes 1572872 | tf_op jit(solution)/shard_map/ppermute | solution.py:271
  77.7 16.1 %collective-permute-start.28 = (bf16[2048,128]{1,0:T(8,128)(2,1)}, bf16[2048,128]{1,0:T(8,128)(2,1)}, u32[]{:S(2)}, u32[]{:S(2)}) collective-permute-start(bf16[2048,128]{1,0:T(8,128)(2,1)} %get-tuple-element.63), channel_id=1, source_target_pairs={{0,8},{4,12},{8,0},{12,4},{16,24},{20,28},{24,16},{28,20},{1,9},{5... | collective-permute-start | bytes 1572872 | tf_op jit(solution)/shard_map/ppermute | solution.py:271
  92.5 8.2 %collective-permute-start.23 = (bf16[1024,128]{1,0:T(8,128)(2,1)}, bf16[1024,128]{1,0:T(8,128)(2,1)S(1)}, u32[]{:S(2)}, u32[]{:S(2)}) collective-permute-start(bf16[1024,128]{1,0:T(8,128)(2,1)} %add_convert_fusion.7), channel_id=1, source_target_pairs={{0,8},{4,12},{8,0},{12,4},{16,24},{20,28},{24,16},{28,20},{1,9},{5... | collective-permute-start | bytes 786440 | tf_op jit(solution)/shard_map/ppermute | solution.py:271
  94.9 20.2 %collective-permute-start.29 = (bf16[1024,128]{1,0:T(8,128)(2,1)S(1)}, bf16[1024,128]{1,0:T(8,128)(2,1)S(1)}, u32[]{:S(2)}, u32[]{:S(2)}) collective-permute-start(bf16[1024,128]{1,0:T(8,128)(2,1)S(1)} %add_convert_fusion.5), channel_id=1, source_target_pairs={{0,16},{4,20},{8,24},{12,28},{16,0},{20,4},{24,8},{28,12},{1,17},{... | collective-permute-start | bytes 786440 | tf_op jit(solution)/shard_map/ppermute | solution.py:271
  102.3 13.9 %collective-permute-start.24 = (bf16[1024,128]{1,0:T(8,128)(2,1)S(1)}, bf16[1024,128]{1,0:T(8,128)(2,1)}, u32[]{:S(2)}, u32[]{:S(2)}) collective-permute-start(bf16[1024,128]{1,0:T(8,128)(2,1)S(1)} %fusion.7.refs_0_), channel_id=1, source_target_pairs={{0,3},{1,0},{2,1},{3,2},{4,7},{5,4},{6,5},{7,6},{8,11},{9,8},{10,9... | collective-permute-start | bytes 786440 | tf_op jit(solution)/shard_map/ppermute | solution.py:404
  111.9 15.4 %collective-permute-start.34 = (bf16[128,1792]{1,0:T(8,128)(2,1)S(1)}, bf16[128,1792]{1,0:T(8,128)(2,1)S(1)}, u32[]{:S(2)}, u32[]{:S(2)}) collective-permute-start(bf16[128,1792]{1,0:T(8,128)(2,1)S(1)} %pad_maximum_fusion.3), channel_id=1, source_target_pairs={{0,8},{4,12},{8,0},{12,4},{16,24},{20,28},{24,16},{28,20},{1,9},{5... | collective-permute-start | bytes 1376264 | tf_op jit(solution)/shard_map/ppermute | solution.py:271
  113.5 13.9 %collective-permute-start.36 = (bf16[128,1792]{1,0:T(8,128)(2,1)S(1)}, bf16[128,1792]{1,0:T(8,128)(2,1)S(1)}, u32[]{:S(2)}, u32[]{:S(2)}) collective-permute-start(bf16[128,1792]{1,0:T(8,128)(2,1)S(1)} %pad_maximum_fusion.4), channel_id=1, source_target_pairs={{0,16},{4,20},{8,24},{12,28},{16,0},{20,4},{24,8},{28,12},{1,17},{... | collective-permute-start | bytes 1376264 | tf_op jit(solution)/shard_map/ppermute | solution.py:271
  116.2 11.1 %collective-permute-start.30 = (bf16[1024,128]{1,0:T(8,128)(2,1)S(1)}, bf16[1024,128]{1,0:T(8,128)(2,1)S(1)}, u32[]{:S(2)}, u32[]{:S(2)}) collective-permute-start(bf16[1024,128]{1,0:T(8,128)(2,1)S(1)} %add_convert_fusion.4.refs_4_), channel_id=1, source_target_pairs={{0,1},{1,2},{2,3},{3,0},{4,5},{5,6},{6,7},{7,4},{8,9},{9,10},{10,1... | collective-permute-start | bytes 786440 | tf_op jit(solution)/shard_map/ppermute | solution.py:403
  116.3 14.2 %collective-permute-start.25 = (bf16[1024,128]{1,0:T(8,128)(2,1)}, bf16[1024,128]{1,0:T(8,128)(2,1)}, u32[]{:S(2)}, u32[]{:S(2)}) collective-permute-start(bf16[1024,128]{1,0:T(8,128)(2,1)} %collective-permute-done.24.refs_1_), channel_id=1, source_target_pairs={{0,3},{1,0},{2,1},{3,2},{4,7},{5,4},{6,5},{7,6},{8,11},{9,8},{10,9... | collective-permute-start | bytes 786440 | tf_op jit(solution)/shard_map/ppermute | solution.py:404
  127.3 11.3 %collective-permute-start.31 = (bf16[1024,128]{1,0:T(8,128)(2,1)S(1)}, bf16[1024,128]{1,0:T(8,128)(2,1)}, u32[]{:S(2)}, u32[]{:S(2)}) collective-permute-start(bf16[1024,128]{1,0:T(8,128)(2,1)S(1)} %collective-permute-done.30.refs_5_), channel_id=1, source_target_pairs={{0,1},{1,2},{2,3},{3,0},{4,5},{5,6},{6,7},{7,4},{8,9},{9,10},{10,1... | collective-permute-start | bytes 786440 | tf_op jit(solution)/shard_map/ppermute | solution.py:403
  128.5 10.1 %collective-permute-start.37 = (bf16[128,896]{1,0:T(8,128)(2,1)}, bf16[128,896]{1,0:T(8,128)(2,1)}, u32[]{:S(2)}, u32[]{:S(2)}) collective-permute-start(bf16[128,896]{1,0:T(8,128)(2,1)} %get-tuple-element.55), channel_id=1, source_target_pairs={{0,8},{4,12},{8,0},{12,4},{16,24},{20,28},{24,16},{28,20},{1,9},{5... | collective-permute-start | bytes 688136 | tf_op jit(solution)/shard_map/ppermute | solution.py:271
  128.8 10.9 %collective-permute-start.35 = (bf16[128,896]{1,0:T(8,128)(2,1)}, bf16[128,896]{1,0:T(8,128)(2,1)S(1)}, u32[]{:S(2)}, u32[]{:S(2)}) collective-permute-start(bf16[128,896]{1,0:T(8,128)(2,1)} %get-tuple-element.34), channel_id=1, source_target_pairs={{0,16},{4,20},{8,24},{12,28},{16,0},{20,4},{24,8},{28,12},{1,17},{... | collective-permute-start | bytes 688136 | tf_op jit(solution)/shard_map/ppermute | solution.py:271
  130.5 10.6 %collective-permute-start.26 = (bf16[1024,128]{1,0:T(8,128)(2,1)}, bf16[1024,128]{1,0:T(8,128)(2,1)}, u32[]{:S(2)}, u32[]{:S(2)}) collective-permute-start(bf16[1024,128]{1,0:T(8,128)(2,1)} %collective-permute-done.25.refs_2_), channel_id=1, source_target_pairs={{0,3},{1,0},{2,1},{3,2},{4,7},{5,4},{6,5},{7,6},{8,11},{9,8},{10,9... | collective-permute-start | bytes 786440 | tf_op jit(solution)/shard_map/ppermute | solution.py:404
  138.7 8.5 %collective-permute-start.32 = (bf16[1024,128]{1,0:T(8,128)(2,1)}, bf16[1024,128]{1,0:T(8,128)(2,1)}, u32[]{:S(2)}, u32[]{:S(2)}) collective-permute-start(bf16[1024,128]{1,0:T(8,128)(2,1)} %collective-permute-done.31.refs_6_), channel_id=1, source_target_pairs={{0,1},{1,2},{2,3},{3,0},{4,5},{5,6},{6,7},{7,4},{8,9},{9,10},{10,1... | collective-permute-start | bytes 786440 | tf_op jit(solution)/shard_map/ppermute | solution.py:403
  139.9 72.6 %collective-permute-start.38 = (bf16[256,448]{1,0:T(8,128)(2,1)S(1)}, bf16[256,448]{1,0:T(8,128)(2,1)S(1)}, u32[]{:S(2)}, u32[]{:S(2)}) collective-permute-start(bf16[256,448]{1,0:T(8,128)(2,1)S(1)} %select_convert_fusion), channel_id=1, source_target_pairs={{0,4},{4,0},{8,12},{12,8},{16,20},{20,16},{24,28},{28,24},{1,5},{5... | collective-permute-start | bytes 688136 | tf_op jit(solution)/shard_map/ppermute | solution.py:271
  (18 other events, 98.9 us)

commit v3 on v2

--- a/solution.py
+++ b/solution.py
@@ -187,7 +187,7 @@
     def body(block, carry):
         need = need_ref[block]
         floor = 0
-        for size in (1, 2, 4, 8):
+        for size in (1, 2, 3, 4, 6, 8):
             pl.when((need > floor) & (need <= size))(partial(window, size, block))
             floor = size
         return carry
@@ -240,30 +240,57 @@
     )(*tables, query, up, cosine, sine, places, *keys, *values)
 
 
-def assemble_kernel(lanes, order_ref, *refs):
-    sources, outs, sems = refs[: 2 * lanes], refs[2 * lanes : 2 * lanes + 2], refs[-1]
-    copies = []
-    for index, source in enumerate(sources):
-        column = pl.multiple_of(order_ref[index] * HD, HD)
-        target = outs[index // lanes].at[:, pl.ds(column, HD)]
-        copy = pltpu.make_async_copy(source, target, sems.at[index])
-        copy.start()
-        copies.append(copy)
-    for copy in copies:
-        copy.wait()
-
-
-def assemble(order, pieces):
-    lanes = len(pieces) // 2
-    hbm = pl.BlockSpec(memory_space=pl.ANY)
-    whole = jax.ShapeDtypeStruct((pieces[0].shape[0], lanes * HD), pieces[0].dtype)
+def assemble_kernel(count, column_ref, active_ref, *refs):
+    out_ref = refs[count]
+    for index in range(count):
+
+        @pl.when(active_ref[index] > 0)
+        def store():
+            column = pl.multiple_of(column_ref[index] * HD, HD)
+            out_ref[:, pl.ds(column, HD)] = refs[index][...]
+
+
+def assemble(columns, active, pieces, lanes):
+    rows = pieces[0].shape[0]
+    steps = 4
+    smem = pl.BlockSpec(memory_space=pltpu.SMEM)
     return pl.pallas_call(
-        partial(assemble_kernel, lanes),
-        out_shape=(whole, whole),
-        in_specs=[pl.BlockSpec(memory_space=pltpu.SMEM)] + [hbm] * len(pieces),
-        out_specs=(hbm, hbm),
-        scratch_shapes=[pltpu.SemaphoreType.DMA((len(pieces),))],
-    )(order, *pieces)
+        partial(assemble_kernel, len(pieces)),
+        grid=(steps,),
+        out_shape=jax.ShapeDtypeStruct((rows, lanes * HD), pieces[0].dtype),
+        in_specs=[smem, smem]
+        + [pl.BlockSpec((rows // steps, HD), lambda step: (step, 0))] * len(pieces),
+        out_specs=pl.BlockSpec((rows // steps, lanes * HD), lambda step: (step, 0)),
+        cost_estimate=pl.CostEstimate(
+            flops=0, bytes_accessed=4 * rows * lanes * HD, transcendentals=0
+        ),
+    )(columns, active, *pieces)
+
+
+def lane_gather(array, my_lane):
+    lanes = lax.axis_size("tensor")
+
+    def send(item, pairs):
+        return lax.ppermute(item, "tensor", pairs)
+
+    if lanes == 4:
+        second = send(array, [(0, 2), (2, 0), (1, 3), (3, 1)])
+        first = send(array, [(0, 1), (1, 0), (2, 3), (3, 2)])
+        inner = send(array, [(1, 2), (2, 1)])
+        outer = send(second, [(1, 0), (2, 3)])
+        middle = (my_lane == 1) | (my_lane == 2)
+        pieces = [array, first, second, inner, outer]
+        columns = my_lane ^ jnp.array([0, 1, 2, 3, 3], jnp.int32)
+        always = jnp.array([True, True, True, False, False])
+        at_inner = jnp.array([False, False, False, True, False])
+        active = always | (at_inner & middle) | (~always & ~at_inner & ~middle)
+    else:
+        pieces = [array]
+        for unused in range(lanes - 1):
+            pieces.append(send(pieces[-1], [(lane, (lane + 1) % lanes) for lane in range(lanes)]))
+        columns = (my_lane - jnp.arange(lanes, dtype=jnp.int32)) % lanes
+        active = jnp.ones((lanes,), jnp.bool_)
+    return assemble(columns, active.astype(jnp.int32), pieces, lanes)
 
 
 def swap(array, bit):
@@ -344,7 +371,6 @@
 
 def local(query, key, value, grad_out, out_weight, plan, segments):
     rank_count = lax.axis_size("dp")
-    lane_count = lax.axis_size("tensor")
     my_rank = lax.axis_index("dp")
     my_lane = lax.axis_index("tensor")
     row_count = query.shape[0]
@@ -357,9 +383,9 @@
     own_value = lax.dynamic_slice_in_dim(value, kv_head * HD, HD, 1)
 
     own_places = positions_of(segments).reshape(block_count, ROWBLK)
-    places_all = jnp.concatenate(
-        [own_places] + [swap(own_places, step) for step in range(1, rank_count)], axis=0
-    )
+    places_all = own_places
+    for bit in bits:
+        places_all = jnp.concatenate([places_all, swap(places_all, bit)], axis=0)
     values = spread(own_value, bits[1:] + bits[:1])
     up = jnp.dot(grad_out, out_weight, preferred_element_type=jnp.float32).astype(jnp.bfloat16)
 
@@ -395,17 +421,10 @@
     gkey = halve(gkey_keep, gkey_send, key_bits)
     key_partial = (gkey * cosine - swap_halves(gkey) * sine).astype(jnp.bfloat16)
 
-    key_ring = [key_partial]
-    value_ring = [value_partial]
-    down = [(lane, (lane - 1) % lane_count) for lane in range(lane_count)]
-    above = [(lane, (lane + 1) % lane_count) for lane in range(lane_count)]
-    for unused in range(lane_count - 1):
-        value_ring.append(lax.ppermute(value_ring[-1], "tensor", above))
-        key_ring.append(lax.ppermute(key_ring[-1], "tensor", down))
-    step = jnp.arange(lane_count, dtype=jnp.int32)
-    order = jnp.concatenate([(my_lane + step) % lane_count, (my_lane - step) % lane_count])
-    key_all, value_all = assemble(order, key_ring + value_ring)
-
+    value_all = lane_gather(value_partial, my_lane)
+    key_all = lane_gather(key_partial, my_lane)
+
+    attn_t = lax.optimization_barrier((attn_t, key_partial, value_partial))[0]
     weight_grad = weight_sum(attn_t, grad_out, my_rank, bits).T
     lanes_per_key = group // local_heads
 

time: 215 us -> 176 us (0.82)
  Pallas kernels: 87.1 us -> 27.6 us
  waiting for transfers between devices: 45.7 us -> 66.9 us
  starting transfers between devices: 37.7 us -> 33.8 us
  local copies, waits for them, and re-layouts: 5.27 us -> 7.57 us
    pallas_call x1 -> x2, Pallas kernels: 65.4 us -> 7.08 us  [assemble(): pl.pallas_call(partial(assemble_kernel, len(pieces)), grid=(steps,), out_...]
    ppermute x33 -> x29, waiting for transfers between devices: 25.6 us -> 51.1 us  [swap(): lax.ppermute(array, 'dp', [(rank, rank ^ bit) for rank in range(ranks)])]
    ppermute x33 -> x29, starting transfers between devices: 27.3 us -> 22.3 us  [swap(): lax.ppermute(array, 'dp', [(rank, rank ^ bit) for rank in range(ranks)])]
    ppermute x6 -> x8, waiting for transfers between devices: 20.1 us -> 15.8 us  [send(): return lax.ppermute(item, 'tensor', pairs)]
    unnamed x29 -> x35, local copies, waits for them, and re-layouts: 3.06 us -> 5.37 us
    ppermute x6 -> x8, starting transfers between devices: 10.4 us -> 11.4 us  [send(): return lax.ppermute(item, 'tensor', pairs)]
  transfers between devices with their start and end apart: 39 -> 37, of which waited for: 11 -> 17; matrix products, arithmetic and copies ran while one was open for 18% -> 15% of each run, Pallas kernels for 31% -> 4%
where the time goes in v3:
time: 176 us
  waiting for transfers between devices  66.9 us (38%)
  starting transfers between devices  33.8 us (19%)
  Pallas kernels  27.6 us (16%)
  other arithmetic  19.6 us (11%)
  matrix products  19.1 us (11%)
  local copies, waits for them, and re-layouts  7.57 us (4%)
    ppermute x29, waiting for transfers between devices, swap(): lax.ppermute(array, 'dp', [(rank, rank ^ bit) for rank in range(ranks)])  51.1 us
    ppermute x29, starting transfers between devices, swap(): lax.ppermute(array, 'dp', [(rank, rank ^ bit) for rank in range(ranks)])  22.3 us
    pallas_call x1, Pallas kernels, attend(): pl.pallas_call(partial(attend_kernel, heads, ranks), out_shape=(jax.Shape...  20.5 us
    ppermute x8, waiting for transfers between devices, send(): return lax.ppermute(item, 'tensor', pairs)  15.8 us
    dot_general x2, matrix products, product(): return jnp.dot(picked, grad_out, preferred_element_type=jnp.float32)  11.8 us
    ppermute x8, starting transfers between devices, send(): return lax.ppermute(item, 'tensor', pairs)  11.4 us
    dot_general x1, matrix products, local(): jnp.dot(grad_out, out_weight, preferred_element_type=jnp.float32)  7.31 us
    pallas_call x2, Pallas kernels, assemble(): pl.pallas_call(partial(assemble_kernel, len(pieces)), grid=(steps,), out_...  7.08 us
  transfers between devices with their start and end apart: 37, of which 17 were waited for; matrix products, arithmetic and copies ran while one was open for 15% of the time, Pallas kernels for 4%

profile of v3, /device:TPU:0, one launch (start us, length us, event | category | flops | bytes accessed | tf_op | source)
XLA Modules:
  0.0 175.5 jit_solution(551519192681015304)
XLA Ops:
  1.9 3.0 %collective-permute-start.11 = (bf16[1024,128]{1,0:T(8,128)(2,1)S(1)}, bf16[1024,128]{1,0:T(8,128)(2,1)S(1)}, u32[]{:S(2)}, u32[]{:S(2)}) collective-permute-start(bf16[1024,128]{1,0:T(8,128)(2,1)S(1)} %constant_dynamic-slice_fusion.refs_8_), channel_id=1, source_target_pairs={{0,8},{4,12},{8,0},{12,4},{16,24},{20,28},{24,16},{28,20},{1,9},{5... | collective-permute-start | bytes 786440 | tf_op jit(solution)/shard_map/ppermute | solution.py:298
  4.9 1.5 collective-permute-start.13
  12.0 3.1 %collective-permute-done.1 = s32[16,128]{1,0:T(8,128)S(1)} collective-permute-done((s32[16,128]{1,0:T(8,128)S(1)}, s32[16,128]{1,0:T(8,128)S(1)}, u32[]{:S(2)}, u32[]{:S(2)}) %collective-permute-start.1) | collective-permute-done | bytes 8224 | tf_op jit(solution)/shard_map/ppermute | solution.py:298
  15.7 3.2 %collective-permute-done.2 = s32[32,128]{1,0:T(8,128)S(1)} collective-permute-done((s32[32,128]{1,0:T(8,128)S(1)}, s32[32,128]{1,0:T(8,128)S(1)}, u32[]{:S(2)}, u32[]{:S(2)}) %collective-permute-start.2) | collective-permute-done | bytes 16416 | tf_op jit(solution)/shard_map/ppermute | solution.py:298
  19.5 1.9 %fusion.15 = (f32[1024,64]{1,0:T(8,128)S(1)}, f32[1024,64]{1,0:T(8,128)S(1)}, f32[1024,64]{1,0:T(8,128)S(1)}) fusion(f32[64]{0:T(128)S(1)} %multiply_add_fusion.1, f32[1024]{0:T(1024)S(1)} %get-tuple-element.40), kind=kLoop, calls=%fused_computation.56 | loop fusion | flops 262144 | bytes 790784 | tf_op jit(solution)/shard_map/neg | solution.py:67
  21.5 1.8 %fusion.5 = (bf16[1024,128]{1,0:T(8,128)(2,1)S(1)}, f32[1024,128]{1,0:T(8,128)S(1)}, f32[1024,128]{1,0:T(8,128)S(1)}) fusion(f32[1024,64]{1,0:T(8,128)} %get-tuple-element.66, f32[1024,64]{1,0:T(8,128)} %get-tuple-element.65, bf16[1024,512]{1,0:T(8,128)(2,1)} %param.14, s32[]{:T(128)S(6)} %select_n.172, f32[1024,64]{1,0:T(8,128)S(1)} %get-tuple-element.69, ...), kind=kLoop, calls=%fused_computation.24 | loop fusion | flops 1048576 | bytes 2883588 | tf_op jit(solution)/shard_map/convert_element_type | solution.py:403
  23.9 7.3 %convolution_convert_fusion.1.up_ref = bf16[1024,512]{1,0:T(8,128)(2,1)} fusion(bf16[1024,3584]{1,0:T(8,128)(2,1)} %param.16, bf16[3584,512]{1,0:T(8,128)(2,1)S(1)} %copy-done.15), kind=kOutput, calls=%fused_computation.3 | convolution fusion | flops 3758620672 | bytes 12058624 | tf_op jit(solution)/shard_map/dot_general | solution.py:390
  31.4 2.0 %collective-permute-start.15 = (bf16[1024,128]{1,0:T(8,128)(2,1)S(1)}, bf16[1024,128]{1,0:T(8,128)(2,1)S(1)}, u32[]{:S(2)}, u32[]{:S(2)}) collective-permute-start(bf16[1024,128]{1,0:T(8,128)(2,1)S(1)} %collective-permute-done.11.refs_10_), channel_id=1, source_target_pairs={{0,16},{4,20},{8,24},{12,28},{16,0},{20,4},{24,8},{28,12},{1,17},{... | collective-permute-start | bytes 786440 | tf_op jit(solution)/shard_map/ppermute | solution.py:298
  33.6 1.5 collective-permute-start.8
  35.1 3.6 %collective-permute-done.4.refs_2_ = bf16[1024,128]{1,0:T(8,128)(2,1)S(1)} collective-permute-done((bf16[1024,128]{1,0:T(8,128)(2,1)S(1)}, bf16[1024,128]{1,0:T(8,128)(2,1)S(1)}, u32[]{:S(2)}, u32[]{:S(2)}) %collective-permute-start.4) | collective-permute-done | bytes 262176 | tf_op jit(solution)/shard_map/ppermute | solution.py:298
  40.8 2.4 %collective-permute-done.8.refs_6_ = bf16[1024,128]{1,0:T(8,128)(2,1)S(1)} collective-permute-done((bf16[1024,128]{1,0:T(8,128)(2,1)S(1)}, bf16[1024,128]{1,0:T(8,128)(2,1)S(1)}, u32[]{:S(2)}, u32[]{:S(2)}) %collective-permute-start.8) | collective-permute-done | bytes 262176 | tf_op jit(solution)/shard_map/ppermute | solution.py:298
  44.8 20.5 %shard_map.156 = (bf16[1024,512]{1,0:T(8,128)(2,1)}, bf16[512,1024]{1,0:T(8,128)(2,1)}, bf16[4096,128]{1,0:T(8,128)(2,1)}, bf16[4096,128]{1,0:T(8,128)(2,1)}, bf...) custom-call(s32[64]{0:T(128)S(1)} %multiply_add_fusion.4.key_at_ref, s32[64]{0:T(128)S(1)} %get-tuple-element.48.value_at_ref, ...), custom_call_target="tpu_custom_call" | custom-call | flops 5368709120 | bytes 16777216 | tf_op jit(solution)/shard_map/pallas_call | solution.py:221
  65.9 2.4 %collective-permute-done.17 = bf16[4096,128]{1,0:T(8,128)(2,1)S(1)} collective-permute-done((bf16[4096,128]{1,0:T(8,128)(2,1)}, bf16[4096,128]{1,0:T(8,128)(2,1)S(1)}, u32[]{:S(2)}, u32[]{:S(2)}) %collective-permute-start.17) | collective-permute-done | bytes 1048608 | tf_op jit(solution)/shard_map/ppermute | solution.py:298
  68.3 1.5 add_convert_fusion.3
  73.1 10.7 %collective-permute-done.18 = bf16[2048,128]{1,0:T(8,128)(2,1)S(1)} collective-permute-done((bf16[2048,128]{1,0:T(8,128)(2,1)S(1)}, bf16[2048,128]{1,0:T(8,128)(2,1)S(1)}, u32[]{:S(2)}, u32[]{:S(2)}) %collective-permute-start.18) | collective-permute-done | bytes 524320 | tf_op jit(solution)/shard_map/ppermute | solution.py:298
  84.6 2.3 %collective-permute-start.19 = (bf16[1024,128]{1,0:T(8,128)(2,1)S(1)}, bf16[1024,128]{1,0:T(8,128)(2,1)S(1)}, u32[]{:S(2)}, u32[]{:S(2)}) collective-permute-start(bf16[1024,128]{1,0:T(8,128)(2,1)S(1)} %add_convert_fusion.7), channel_id=1, source_target_pairs={{0,8},{4,12},{8,0},{12,4},{16,24},{20,28},{24,16},{28,20},{1,9},{5... | collective-permute-start | bytes 786440 | tf_op jit(solution)/shard_map/ppermute | solution.py:298
  88.8 4.3 %collective-permute-done.19 = bf16[1024,128]{1,0:T(8,128)(2,1)S(1)} collective-permute-done((bf16[1024,128]{1,0:T(8,128)(2,1)S(1)}, bf16[1024,128]{1,0:T(8,128)(2,1)S(1)}, u32[]{:S(2)}, u32[]{:S(2)}) %collective-permute-start.19) | collective-permute-done | bytes 262176 | tf_op jit(solution)/shard_map/ppermute | solution.py:298
  95.7 1.8 %add_convert_fusion.4.refs_0_ = bf16[1024,128]{1,0:T(8,128)(2,1)} fusion(bf16[1024,128]{1,0:T(8,128)(2,1)S(1)} %collective-permute-done.26, bf16[2048,128]{1,0:T(8,128)(2,1)} %collective-permute-done.25, bf16[2048,128]{1,0:T(8,128)(2,1)} %get-tuple-element.58), kind=kLoop, calls=%fused_computation.34 | loop fusion | flops 1048576 | bytes 1048576 | tf_op jit(solution)/shard_map/convert_element_type | solution.py:420
  97.6 6.4 %convolution_convert_fusion = bf16[256,3584]{1,0:T(8,128)(2,1)} fusion(bf16[1024,3584]{1,0:T(8,128)(2,1)} %param.16, bf16[2,256,1024]{2,1,0:T(8,128)(2,1)S(1)} %bitcast.39, s32[]{:T(128)S(6)} %select_n.177), kind=kOutput, calls=%fused_computation.1 | convolution fusion | flops 1879965696 | bytes 9699332 | tf_op jit(solution)/shard_map/dot_general | solution.py:336
  104.0 4.0 %collective-permute-done.31 = bf16[256,3584]{1,0:T(8,128)(2,1)S(1)} collective-permute-done((bf16[256,3584]{1,0:T(8,128)(2,1)}, bf16[256,3584]{1,0:T(8,128)(2,1)S(1)}, u32[]{:S(2)}, u32[]{:S(2)}) %collective-permute-start.31) | collective-permute-done | bytes 1835040 | tf_op jit(solution)/shard_map/ppermute | solution.py:298
  108.0 5.3 %convert_add_fusion = f32[256,3584]{1,0:T(8,128)S(1)} fusion(bf16[256,3584]{1,0:T(8,128)(2,1)S(1)} %collective-permute-done.31, bf16[1024,3584]{1,0:T(8,128)(2,1)} %param.16, bf16[2,256,1024]{2,1,0:T(8,128)(2,1)} %bitcast.38, s32[]{:T(128)S(6)} %select_n.176), kind=kOutput, calls=%fused_computation.2 | convolution fusion | flops 1880883200 | bytes 13369348 | tf_op jit(solution)/shard_map/dot_general | solution.py:336
  114.4 1.5 collective-permute-start.32
  116.0 10.2 %collective-permute-done.34 = bf16[128,1792]{1,0:T(8,128)(2,1)S(1)} collective-permute-done((bf16[128,1792]{1,0:T(8,128)(2,1)S(1)}, bf16[128,1792]{1,0:T(8,128)(2,1)S(1)}, u32[]{:S(2)}, u32[]{:S(2)}) %collective-permute-start.34) | collective-permute-done | bytes 458784 | tf_op jit(solution)/shard_map/ppermute | solution.py:298
  129.1 2.8 %collective-permute-start.28 = (bf16[1024,128]{1,0:T(8,128)(2,1)}, bf16[1024,128]{1,0:T(8,128)(2,1)}, u32[]{:S(2)}, u32[]{:S(2)}) collective-permute-start(bf16[1024,128]{1,0:T(8,128)(2,1)} %add_convert_fusion.4.refs_0_), channel_id=1, source_target_pairs={{0,2},{2,0},{1,3},{3,1},{4,6},{6,4},{5,7},{7,5},{8,10},{10,8},{9,1... | collective-permute-start | bytes 786440 | tf_op jit(solution)/shard_map/ppermute | solution.py:274
  131.9 1.6 collective-permute-start.27
  134.1 3.2 %collective-permute-start.21 = (bf16[1024,128]{1,0:T(8,128)(2,1)}, bf16[1024,128]{1,0:T(8,128)(2,1)}, u32[]{:S(2)}, u32[]{:S(2)}) collective-permute-start(bf16[1024,128]{1,0:T(8,128)(2,1)} %fusion.7.refs_0_), channel_id=1, source_target_pairs={{0,2},{2,0},{1,3},{3,1},{4,6},{6,4},{5,7},{7,5},{8,10},{10,8},{9,1... | collective-permute-start | bytes 786440 | tf_op jit(solution)/shard_map/ppermute | solution.py:274
  137.4 1.4 collective-permute-start.35
  139.8 3.8 %collective-permute-done.35 = bf16[128,896]{1,0:T(8,128)(2,1)S(1)} collective-permute-done((bf16[128,896]{1,0:T(8,128)(2,1)}, bf16[128,896]{1,0:T(8,128)(2,1)S(1)}, u32[]{:S(2)}, u32[]{:S(2)}) %collective-permute-start.35) | collective-permute-done | bytes 229408 | tf_op jit(solution)/shard_map/ppermute | solution.py:298
  144.5 3.2 %collective-permute-done.28.refs_2_ = bf16[1024,128]{1,0:T(8,128)(2,1)} collective-permute-done((bf16[1024,128]{1,0:T(8,128)(2,1)}, bf16[1024,128]{1,0:T(8,128)(2,1)}, u32[]{:S(2)}, u32[]{:S(2)}) %collective-permute-start.28) | collective-permute-done | bytes 262176 | tf_op jit(solution)/shard_map/ppermute | solution.py:274
  149.7 11.4 %collective-permute-done.21.refs_2_ = bf16[1024,128]{1,0:T(8,128)(2,1)} collective-permute-done((bf16[1024,128]{1,0:T(8,128)(2,1)}, bf16[1024,128]{1,0:T(8,128)(2,1)}, u32[]{:S(2)}, u32[]{:S(2)}) %collective-permute-start.21) | collective-permute-done | bytes 262176 | tf_op jit(solution)/shard_map/ppermute | solution.py:274
  165.0 3.5 %shard_map.158 = bf16[1024,512]{1,0:T(8,128)(2,1)} custom-call(s32[5]{0:T(128)} %broadcast_xor_fusion.column_ref, s32[5]{0:T(128)} %or_convert_fusion.active_ref, bf16[1024,128]{1,0:T(8,128)(2,1)} %add_convert_fusion.4.refs_0_, bf16[1024,128]{1,0:T(8,128)(2,1)} %copy-done.3, bf16[1024,128]{1,0:T(8,128)(2,1)} %collective-permute-done.28.refs_2_, ...), custom_call_target="tpu_custom_call" | custom-call | bytes 2097152 | tf_op jit(solution)/shard_map/pallas_call | solution.py:257
  170.3 3.5 %shard_map.157 = bf16[1024,512]{1,0:T(8,128)(2,1)} custom-call(s32[5]{0:T(128)} %broadcast_xor_fusion.column_ref, s32[5]{0:T(128)} %or_convert_fusion.active_ref, bf16[1024,128]{1,0:T(8,128)(2,1)} %fusion.7.refs_0_, bf16[1024,128]{1,0:T(8,128)(2,1)} %copy-done.5, bf16[1024,128]{1,0:T(8,128)(2,1)} %collective-permute-done.21.refs_2_, ...), custom_call_target="tpu_custom_call" | custom-call | bytes 2097152 | tf_op jit(solution)/shard_map/pallas_call | solution.py:257
  (133 shorter events, 37.5 us)
Async XLA Ops:
  1.9 29.4 %collective-permute-start.11 = (bf16[1024,128]{1,0:T(8,128)(2,1)S(1)}, bf16[1024,128]{1,0:T(8,128)(2,1)S(1)}, u32[]{:S(2)}, u32[]{:S(2)}) collective-permute-start(bf16[1024,128]{1,0:T(8,128)(2,1)S(1)} %constant_dynamic-slice_fusion.refs_8_), channel_id=1, source_target_pairs={{0,8},{4,12},{8,0},{12,4},{16,24},{20,28},{24,16},{28,20},{1,9},{5... | collective-permute-start | bytes 786440 | tf_op jit(solution)/shard_map/ppermute | solution.py:298
  4.9 26.5 %collective-permute-start.13 = (bf16[1024,128]{1,0:T(8,128)(2,1)S(1)}, bf16[1024,128]{1,0:T(8,128)(2,1)S(1)}, u32[]{:S(2)}, u32[]{:S(2)}) collective-permute-start(bf16[1024,128]{1,0:T(8,128)(2,1)S(1)} %constant_dynamic-slice_fusion.refs_8_), channel_id=1, source_target_pairs={{0,16},{4,20},{8,24},{12,28},{16,0},{20,4},{24,8},{28,12},{1,17},{... | collective-permute-start | bytes 786440 | tf_op jit(solution)/shard_map/ppermute | solution.py:298
  6.4 27.0 %collective-permute-start.10 = (bf16[1024,128]{1,0:T(8,128)(2,1)S(1)}, bf16[1024,128]{1,0:T(8,128)(2,1)S(1)}, u32[]{:S(2)}, u32[]{:S(2)}) collective-permute-start(bf16[1024,128]{1,0:T(8,128)(2,1)S(1)} %constant_dynamic-slice_fusion.refs_8_), channel_id=1, source_target_pairs={{0,4},{4,0},{8,12},{12,8},{16,20},{20,16},{24,28},{28,24},{1,5},{5... | collective-permute-start | bytes 786440 | tf_op jit(solution)/shard_map/ppermute | solution.py:298
  11.4 3.7 %collective-permute-start.1 = (s32[16,128]{1,0:T(8,128)S(1)}, s32[16,128]{1,0:T(8,128)S(1)}, u32[]{:S(2)}, u32[]{:S(2)}) collective-permute-start(s32[16,128]{1,0:T(8,128)S(1)} %pad_add_fusion.2), channel_id=1, source_target_pairs={{0,8},{4,12},{8,0},{12,4},{16,24},{20,28},{24,16},{28,20},{1,9},{5... | collective-permute-start | bytes 24584 | tf_op jit(solution)/shard_map/ppermute | solution.py:298
  15.1 3.7 %collective-permute-start.2 = (s32[32,128]{1,0:T(8,128)S(1)}, s32[32,128]{1,0:T(8,128)S(1)}, u32[]{:S(2)}, u32[]{:S(2)}) collective-permute-start(s32[32,128]{1,0:T(8,128)S(1)} %pad_add_fusion.1), channel_id=1, source_target_pairs={{0,16},{4,20},{8,24},{12,28},{16,0},{20,4},{24,8},{28,12},{1,17},{... | collective-permute-start | bytes 49160 | tf_op jit(solution)/shard_map/ppermute | solution.py:298
  23.3 10.3 %collective-permute-start.6 = (bf16[1024,128]{1,0:T(8,128)(2,1)S(1)}, bf16[1024,128]{1,0:T(8,128)(2,1)S(1)}, u32[]{:S(2)}, u32[]{:S(2)}) collective-permute-start(bf16[1024,128]{1,0:T(8,128)(2,1)S(1)} %get-tuple-element.38.refs_0_), channel_id=1, source_target_pairs={{0,16},{4,20},{8,24},{12,28},{16,0},{20,4},{24,8},{28,12},{1,17},{... | collective-permute-start | bytes 786440 | tf_op jit(solution)/shard_map/ppermute | solution.py:298
  31.2 7.5 %collective-permute-start.4 = (bf16[1024,128]{1,0:T(8,128)(2,1)S(1)}, bf16[1024,128]{1,0:T(8,128)(2,1)S(1)}, u32[]{:S(2)}, u32[]{:S(2)}) collective-permute-start(bf16[1024,128]{1,0:T(8,128)(2,1)S(1)} %get-tuple-element.38.refs_0_), channel_id=1, source_target_pairs={{0,8},{4,12},{8,0},{12,4},{16,24},{20,28},{24,16},{28,20},{1,9},{5... | collective-permute-start | bytes 786440 | tf_op jit(solution)/shard_map/ppermute | solution.py:298
  31.3 7.4 %collective-permute-start.3 = (bf16[1024,128]{1,0:T(8,128)(2,1)S(1)}, bf16[1024,128]{1,0:T(8,128)(2,1)S(1)}, u32[]{:S(2)}, u32[]{:S(2)}) collective-permute-start(bf16[1024,128]{1,0:T(8,128)(2,1)S(1)} %get-tuple-element.38.refs_0_), channel_id=1, source_target_pairs={{0,4},{4,0},{8,12},{12,8},{16,20},{20,16},{24,28},{28,24},{1,5},{5... | collective-permute-start | bytes 786440 | tf_op jit(solution)/shard_map/ppermute | solution.py:298
  31.4 8.9 %collective-permute-start.15 = (bf16[1024,128]{1,0:T(8,128)(2,1)S(1)}, bf16[1024,128]{1,0:T(8,128)(2,1)S(1)}, u32[]{:S(2)}, u32[]{:S(2)}) collective-permute-start(bf16[1024,128]{1,0:T(8,128)(2,1)S(1)} %collective-permute-done.11.refs_10_), channel_id=1, source_target_pairs={{0,16},{4,20},{8,24},{12,28},{16,0},{20,4},{24,8},{28,12},{1,17},{... | collective-permute-start | bytes 786440 | tf_op jit(solution)/shard_map/ppermute | solution.py:298
  33.4 6.9 %collective-permute-start.12 = (bf16[1024,128]{1,0:T(8,128)(2,1)S(1)}, bf16[1024,128]{1,0:T(8,128)(2,1)S(1)}, u32[]{:S(2)}, u32[]{:S(2)}) collective-permute-start(bf16[1024,128]{1,0:T(8,128)(2,1)S(1)} %collective-permute-done.11.refs_10_), channel_id=1, source_target_pairs={{0,4},{4,0},{8,12},{12,8},{16,20},{20,16},{24,28},{28,24},{1,5},{5... | collective-permute-start | bytes 786440 | tf_op jit(solution)/shard_map/ppermute | solution.py:298
  33.6 9.7 %collective-permute-start.8 = (bf16[1024,128]{1,0:T(8,128)(2,1)S(1)}, bf16[1024,128]{1,0:T(8,128)(2,1)S(1)}, u32[]{:S(2)}, u32[]{:S(2)}) collective-permute-start(bf16[1024,128]{1,0:T(8,128)(2,1)S(1)} %collective-permute-done.6.refs_4_), channel_id=1, source_target_pairs={{0,8},{4,12},{8,0},{12,4},{16,24},{20,28},{24,16},{28,20},{1,9},{5... | collective-permute-start | bytes 786440 | tf_op jit(solution)/shard_map/ppermute | solution.py:298
  38.7 4.7 %collective-permute-start.14 = (bf16[1024,128]{1,0:T(8,128)(2,1)S(1)}, bf16[1024,128]{1,0:T(8,128)(2,1)S(1)}, u32[]{:S(2)}, u32[]{:S(2)}) collective-permute-start(bf16[1024,128]{1,0:T(8,128)(2,1)S(1)} %collective-permute-done.13.refs_12_), channel_id=1, source_target_pairs={{0,4},{4,0},{8,12},{12,8},{16,20},{20,16},{24,28},{28,24},{1,5},{5... | collective-permute-start | bytes 786440 | tf_op jit(solution)/shard_map/ppermute | solution.py:298
  38.7 4.7 %collective-permute-start.7 = (bf16[1024,128]{1,0:T(8,128)(2,1)S(1)}, bf16[1024,128]{1,0:T(8,128)(2,1)S(1)}, u32[]{:S(2)}, u32[]{:S(2)}) collective-permute-start(bf16[1024,128]{1,0:T(8,128)(2,1)S(1)} %collective-permute-done.6.refs_4_), channel_id=1, source_target_pairs={{0,4},{4,0},{8,12},{12,8},{16,20},{20,16},{24,28},{28,24},{1,5},{5... | collective-permute-start | bytes 786440 | tf_op jit(solution)/shard_map/ppermute | solution.py:298
  65.4 5.3 %collective-permute-start.24 = (bf16[4096,128]{1,0:T(8,128)(2,1)}, bf16[4096,128]{1,0:T(8,128)(2,1)S(1)}, u32[]{:S(2)}, u32[]{:S(2)}) collective-permute-start(bf16[4096,128]{1,0:T(8,128)(2,1)} %get-tuple-element.15), channel_id=1, source_target_pairs={{0,4},{4,0},{8,12},{12,8},{16,20},{20,16},{24,28},{28,24},{1,5},{5... | collective-permute-start | bytes 3145736 | tf_op jit(solution)/shard_map/ppermute | solution.py:298
  69.7 14.0 %collective-permute-start.18 = (bf16[2048,128]{1,0:T(8,128)(2,1)S(1)}, bf16[2048,128]{1,0:T(8,128)(2,1)S(1)}, u32[]{:S(2)}, u32[]{:S(2)}) collective-permute-start(bf16[2048,128]{1,0:T(8,128)(2,1)S(1)} %get-tuple-element.61), channel_id=1, source_target_pairs={{0,16},{4,20},{8,24},{12,28},{16,0},{20,4},{24,8},{28,12},{1,17},{... | collective-permute-start | bytes 1572872 | tf_op jit(solution)/shard_map/ppermute | solution.py:298
  72.0 15.0 %collective-permute-start.25 = (bf16[2048,128]{1,0:T(8,128)(2,1)}, bf16[2048,128]{1,0:T(8,128)(2,1)}, u32[]{:S(2)}, u32[]{:S(2)}) collective-permute-start(bf16[2048,128]{1,0:T(8,128)(2,1)} %get-tuple-element.59), channel_id=1, source_target_pairs={{0,8},{4,12},{8,0},{12,4},{16,24},{20,28},{24,16},{28,20},{1,9},{5... | collective-permute-start | bytes 1572872 | tf_op jit(solution)/shard_map/ppermute | solution.py:298
  84.6 8.4 %collective-permute-start.19 = (bf16[1024,128]{1,0:T(8,128)(2,1)S(1)}, bf16[1024,128]{1,0:T(8,128)(2,1)S(1)}, u32[]{:S(2)}, u32[]{:S(2)}) collective-permute-start(bf16[1024,128]{1,0:T(8,128)(2,1)S(1)} %add_convert_fusion.7), channel_id=1, source_target_pairs={{0,8},{4,12},{8,0},{12,4},{16,24},{20,28},{24,16},{28,20},{1,9},{5... | collective-permute-start | bytes 786440 | tf_op jit(solution)/shard_map/ppermute | solution.py:298
  88.1 7.7 %collective-permute-start.26 = (bf16[1024,128]{1,0:T(8,128)(2,1)S(1)}, bf16[1024,128]{1,0:T(8,128)(2,1)S(1)}, u32[]{:S(2)}, u32[]{:S(2)}) collective-permute-start(bf16[1024,128]{1,0:T(8,128)(2,1)S(1)} %add_convert_fusion.5), channel_id=1, source_target_pairs={{0,16},{4,20},{8,24},{12,28},{16,0},{20,4},{24,8},{28,12},{1,17},{... | collective-permute-start | bytes 786440 | tf_op jit(solution)/shard_map/ppermute | solution.py:298
  104.0 4.0 %collective-permute-start.31 = (bf16[256,3584]{1,0:T(8,128)(2,1)}, bf16[256,3584]{1,0:T(8,128)(2,1)S(1)}, u32[]{:S(2)}, u32[]{:S(2)}) collective-permute-start(bf16[256,3584]{1,0:T(8,128)(2,1)} %convolution_convert_fusion), channel_id=1, source_target_pairs={{0,4},{4,0},{8,12},{12,8},{16,20},{20,16},{24,28},{28,24},{1,5},{5... | collective-permute-start | bytes 5505032 | tf_op jit(solution)/shard_map/ppermute | solution.py:298
  113.6 12.6 %collective-permute-start.34 = (bf16[128,1792]{1,0:T(8,128)(2,1)S(1)}, bf16[128,1792]{1,0:T(8,128)(2,1)S(1)}, u32[]{:S(2)}, u32[]{:S(2)}) collective-permute-start(bf16[128,1792]{1,0:T(8,128)(2,1)S(1)} %pad_maximum_fusion.4), channel_id=1, source_target_pairs={{0,16},{4,20},{8,24},{12,28},{16,0},{20,4},{24,8},{28,12},{1,17},{... | collective-permute-start | bytes 1376264 | tf_op jit(solution)/shard_map/ppermute | solution.py:298
  114.4 12.3 %collective-permute-start.32 = (bf16[128,1792]{1,0:T(8,128)(2,1)S(1)}, bf16[128,1792]{1,0:T(8,128)(2,1)S(1)}, u32[]{:S(2)}, u32[]{:S(2)}) collective-permute-start(bf16[128,1792]{1,0:T(8,128)(2,1)S(1)} %pad_maximum_fusion.3), channel_id=1, source_target_pairs={{0,8},{4,12},{8,0},{12,4},{16,24},{20,28},{24,16},{28,20},{1,9},{5... | collective-permute-start | bytes 1376264 | tf_op jit(solution)/shard_map/ppermute | solution.py:298
  127.8 9.5 %collective-permute-start.33 = (bf16[128,896]{1,0:T(8,128)(2,1)S(1)}, bf16[128,896]{1,0:T(8,128)(2,1)S(1)}, u32[]{:S(2)}, u32[]{:S(2)}) collective-permute-start(bf16[128,896]{1,0:T(8,128)(2,1)S(1)} %get-tuple-element.32), channel_id=1, source_target_pairs={{0,16},{4,20},{8,24},{12,28},{16,0},{20,4},{24,8},{28,12},{1,17},{... | collective-permute-start | bytes 688136 | tf_op jit(solution)/shard_map/ppermute | solution.py:298
  129.1 18.6 %collective-permute-start.28 = (bf16[1024,128]{1,0:T(8,128)(2,1)}, bf16[1024,128]{1,0:T(8,128)(2,1)}, u32[]{:S(2)}, u32[]{:S(2)}) collective-permute-start(bf16[1024,128]{1,0:T(8,128)(2,1)} %add_convert_fusion.4.refs_0_), channel_id=1, source_target_pairs={{0,2},{2,0},{1,3},{3,1},{4,6},{6,4},{5,7},{7,5},{8,10},{10,8},{9,1... | collective-permute-start | bytes 786440 | tf_op jit(solution)/shard_map/ppermute | solution.py:274
  131.9 16.5 %collective-permute-start.27 = (bf16[1024,128]{1,0:T(8,128)(2,1)}, bf16[1024,128]{1,0:T(8,128)(2,1)S(1)}, u32[]{:S(2)}, u32[]{:S(2)}) collective-permute-start(bf16[1024,128]{1,0:T(8,128)(2,1)} %add_convert_fusion.4.refs_0_), channel_id=1, source_target_pairs={{0,1},{1,0},{2,3},{3,2},{4,5},{5,4},{6,7},{7,6},{8,9},{9,8},{10,11... | collective-permute-start | bytes 786440 | tf_op jit(solution)/shard_map/ppermute | solution.py:274
  133.5 29.0 %collective-permute-start.29 = (bf16[1024,128]{1,0:T(8,128)(2,1)}, bf16[1024,128]{1,0:T(8,128)(2,1)S(1)}, u32[]{:S(2)}, u32[]{:S(2)}) collective-permute-start(bf16[1024,128]{1,0:T(8,128)(2,1)} %add_convert_fusion.4.refs_0_), channel_id=1, source_target_pairs={{1,2},{2,1},{5,6},{6,5},{9,10},{10,9},{13,14},{14,13},{17,18},{18,... | collective-permute-start | bytes 786440 | tf_op jit(solution)/shard_map/ppermute | solution.py:274
  134.1 27.0 %collective-permute-start.21 = (bf16[1024,128]{1,0:T(8,128)(2,1)}, bf16[1024,128]{1,0:T(8,128)(2,1)}, u32[]{:S(2)}, u32[]{:S(2)}) collective-permute-start(bf16[1024,128]{1,0:T(8,128)(2,1)} %fusion.7.refs_0_), channel_id=1, source_target_pairs={{0,2},{2,0},{1,3},{3,1},{4,6},{6,4},{5,7},{7,5},{8,10},{10,8},{9,1... | collective-permute-start | bytes 786440 | tf_op jit(solution)/shard_map/ppermute | solution.py:274
  137.4 6.2 %collective-permute-start.35 = (bf16[128,896]{1,0:T(8,128)(2,1)}, bf16[128,896]{1,0:T(8,128)(2,1)S(1)}, u32[]{:S(2)}, u32[]{:S(2)}) collective-permute-start(bf16[128,896]{1,0:T(8,128)(2,1)} %get-tuple-element.51), channel_id=1, source_target_pairs={{0,8},{4,12},{8,0},{12,4},{16,24},{20,28},{24,16},{28,20},{1,9},{5... | collective-permute-start | bytes 688136 | tf_op jit(solution)/shard_map/ppermute | solution.py:298
  143.6 24.9 %collective-permute-start.20 = (bf16[1024,128]{1,0:T(8,128)(2,1)}, bf16[1024,128]{1,0:T(8,128)(2,1)S(1)}, u32[]{:S(2)}, u32[]{:S(2)}) collective-permute-start(bf16[1024,128]{1,0:T(8,128)(2,1)} %fusion.7.refs_0_), channel_id=1, source_target_pairs={{0,1},{1,0},{2,3},{3,2},{4,5},{5,4},{6,7},{7,6},{8,9},{9,8},{10,11... | collective-permute-start | bytes 786440 | tf_op jit(solution)/shard_map/ppermute | solution.py:274
  147.7 20.8 %collective-permute-start.22 = (bf16[1024,128]{1,0:T(8,128)(2,1)}, bf16[1024,128]{1,0:T(8,128)(2,1)S(1)}, u32[]{:S(2)}, u32[]{:S(2)}) collective-permute-start(bf16[1024,128]{1,0:T(8,128)(2,1)} %fusion.7.refs_0_), channel_id=1, source_target_pairs={{1,2},{2,1},{5,6},{6,5},{9,10},{10,9},{13,14},{14,13},{17,18},{18,... | collective-permute-start | bytes 786440 | tf_op jit(solution)/shard_map/ppermute | solution.py:274
  148.4 15.9 %collective-permute-start.30 = (bf16[1024,128]{1,0:T(8,128)(2,1)}, bf16[1024,128]{1,0:T(8,128)(2,1)S(1)}, u32[]{:S(2)}, u32[]{:S(2)}) collective-permute-start(bf16[1024,128]{1,0:T(8,128)(2,1)} %collective-permute-done.28.refs_2_), channel_id=1, source_target_pairs={{1,0},{2,3},{5,4},{6,7},{9,8},{10,11},{13,12},{14,15},{17,16},{18,... | collective-permute-start | bytes 786440 | tf_op jit(solution)/shard_map/ppermute | solution.py:274
  161.2 8.5 %collective-permute-start.23 = (bf16[1024,128]{1,0:T(8,128)(2,1)}, bf16[1024,128]{1,0:T(8,128)(2,1)S(1)}, u32[]{:S(2)}, u32[]{:S(2)}) collective-permute-start(bf16[1024,128]{1,0:T(8,128)(2,1)} %collective-permute-done.21.refs_2_), channel_id=1, source_target_pairs={{1,0},{2,3},{5,4},{6,7},{9,8},{10,11},{13,12},{14,15},{17,16},{18,... | collective-permute-start | bytes 786440 | tf_op jit(solution)/shard_map/ppermute | solution.py:274
  163.2 10.7 %collective-permute-start.36 = (bf16[256,448]{1,0:T(8,128)(2,1)}, bf16[256,448]{1,0:T(8,128)(2,1)S(1)}, u32[]{:S(2)}, u32[]{:S(2)}) collective-permute-start(bf16[256,448]{1,0:T(8,128)(2,1)} %select_convert_fusion), channel_id=1, source_target_pairs={{0,4},{4,0},{8,12},{12,8},{16,20},{20,16},{24,28},{28,24},{1,5},{5... | collective-permute-start | bytes 688136 | tf_op jit(solution)/shard_map/ppermute | solution.py:298
  (22 other events, 206.2 us)

commit v4 on v3

--- a/solution.py
+++ b/solution.py
@@ -80,8 +80,7 @@
 def attend_kernel(
     heads,
     ranks,
-    key_at_ref,
-    value_at_ref,
+    target_ref,
     source_ref,
     run_ref,
     slot_ref,
@@ -179,10 +178,9 @@
         for step in range(count):
             block_id = run * RUN_BLOCKS + first + step
             part = slice(step * ROWBLK, (step + 1) * ROWBLK)
-            key_start = pl.multiple_of(key_at_ref[block_id] * ROWBLK, ROWBLK)
-            value_start = pl.multiple_of(value_at_ref[block_id] * ROWBLK, ROWBLK)
-            gkey_ref[pl.ds(key_start, ROWBLK), :] = gkey[part]
-            gvalue_ref[pl.ds(value_start, ROWBLK), :] = gvalue[part]
+            start = pl.multiple_of(target_ref[block_id] * ROWBLK, ROWBLK)
+            gkey_ref[pl.ds(start, ROWBLK), :] = gkey[part]
+            gvalue_ref[pl.ds(start, ROWBLK), :] = gvalue[part]
 
     def body(block, carry):
         need = need_ref[block]
@@ -228,7 +226,7 @@
             half,
             half,
         ),
-        in_specs=[smem] * 6 + [vmem] * 5 + [hbm] * (2 * ranks),
+        in_specs=[smem] * 5 + [vmem] * 5 + [hbm] * (2 * ranks),
         out_specs=(vmem, vmem, hbm, hbm, hbm, hbm),
         scratch_shapes=[pltpu.VMEM((every, HD), jnp.bfloat16)] * 4
         + [pltpu.VMEM((RUN_BLOCKS * ROWBLK, HD), jnp.bfloat16)] * 2
@@ -241,26 +239,30 @@
 
 
 def assemble_kernel(count, column_ref, active_ref, *refs):
-    out_ref = refs[count]
+    out_ref, sems = refs[count:]
+
+    def copy_of(index):
+        column = pl.multiple_of(column_ref[index] * HD, HD)
+        return pltpu.make_async_copy(
+            refs[index], out_ref.at[:, pl.ds(column, HD)], sems.at[index]
+        )
+
     for index in range(count):
-
-        @pl.when(active_ref[index] > 0)
-        def store():
-            column = pl.multiple_of(column_ref[index] * HD, HD)
-            out_ref[:, pl.ds(column, HD)] = refs[index][...]
+        pl.when(active_ref[index] > 0)(lambda index=index: copy_of(index).start())
+    for index in range(count):
+        pl.when(active_ref[index] > 0)(lambda index=index: copy_of(index).wait())
 
 
 def assemble(columns, active, pieces, lanes):
     rows = pieces[0].shape[0]
-    steps = 4
     smem = pl.BlockSpec(memory_space=pltpu.SMEM)
+    vmem = pl.BlockSpec(memory_space=pltpu.VMEM)
     return pl.pallas_call(
         partial(assemble_kernel, len(pieces)),
-        grid=(steps,),
         out_shape=jax.ShapeDtypeStruct((rows, lanes * HD), pieces[0].dtype),
-        in_specs=[smem, smem]
-        + [pl.BlockSpec((rows // steps, HD), lambda step: (step, 0))] * len(pieces),
-        out_specs=pl.BlockSpec((rows // steps, lanes * HD), lambda step: (step, 0)),
+        in_specs=[smem, smem] + [vmem] * len(pieces),
+        out_specs=pl.BlockSpec(memory_space=pl.ANY),
+        scratch_shapes=[pltpu.SemaphoreType.DMA((len(pieces),))],
         cost_estimate=pl.CostEstimate(
             flops=0, bytes_accessed=4 * rows * lanes * HD, transcendentals=0
         ),
@@ -290,7 +292,7 @@
             pieces.append(send(pieces[-1], [(lane, (lane + 1) % lanes) for lane in range(lanes)]))
         columns = (my_lane - jnp.arange(lanes, dtype=jnp.int32)) % lanes
         active = jnp.ones((lanes,), jnp.bool_)
-    return assemble(columns, active.astype(jnp.int32), pieces, lanes)
+    return assemble(columns, active.astype(jnp.int32), pieces, lanes), pieces[1:]
 
 
 def swap(array, bit):
@@ -298,75 +300,118 @@
     return lax.ppermute(array, "dp", [(rank, rank ^ bit) for rank in range(ranks)])
 
 
-def spread(array, bits):
-    found = {0: array}
-    for bit in bits:
-        found.update({place | bit: swap(item, bit) for place, item in list(found.items())})
-    return [found[place] for place in range(len(found))]
+def spread(array):
+    found = [array, swap(array, 1)]
+    others = [swap(array, step) for step in range(2, lax.axis_size("dp"), 2)]
+    for other in others:
+        found += [other, swap(other, 1)]
+    return found
 
 
 def added(left, right):
     return left.astype(jnp.float32) + right.astype(jnp.float32)
 
 
-def halve(keep, send, bits):
-    received = swap(send, bits[0])
-    for bit in bits[1:]:
-        half = keep.shape[0] // 2
-        send = added(keep[half:], received[half:]).astype(keep.dtype)
-        keep = added(keep[:half], received[:half]).astype(keep.dtype)
-        received = swap(send, bit)
-    return added(keep, received)
-
-
-def place_of(distance, bits):
-    place = jnp.zeros_like(distance)
-    for bit in bits:
-        place = place * 2 + (distance & bit) // bit
-    return place
-
-
-def weight_sum(attn_t, grad_out, my_rank, bits):
-    width = attn_t.shape[0]
-    odd = my_rank & 1
-    halves = attn_t.reshape(2, width // 2, attn_t.shape[1])
-
-    def product(which):
-        picked = lax.dynamic_index_in_dim(halves, which, 0, keepdims=False)
-        return jnp.dot(picked, grad_out, preferred_element_type=jnp.float32)
-
-    received = swap(product(1 - odd).astype(jnp.bfloat16), 1)
-    total = product(odd) + received.astype(jnp.float32)
-    pair_count = lax.axis_size("dp") // 2
-    pair_rows = grad_out.shape[1] // pair_count
-    sums = []
-    for part, order in enumerate((bits[1:], bits[1:][::-1])):
-        rows = total[part * width // 4 : (part + 1) * width // 4]
-        pieces = {
-            2 * pair: rows[:, pair * pair_rows : (pair + 1) * pair_rows]
-            for pair in range(pair_count)
-        }
-        for bit in order:
-            high = (my_rank & bit) > 0
-            lows = [rank for rank in sorted(pieces) if not rank & bit]
-            send = jnp.concatenate(
-                [jnp.where(high, pieces[rank], pieces[rank | bit]) for rank in lows], axis=1
-            )
-            back = swap(send.astype(jnp.bfloat16), bit).astype(jnp.float32)
-            pieces = {
-                rank: jnp.where(high, pieces[rank | bit], pieces[rank])
-                + back[:, at * pair_rows : (at + 1) * pair_rows]
-                for at, rank in enumerate(lows)
-            }
-        sums.append(pieces[0])
-    total = jnp.concatenate(sums, axis=0)
-    first, second = total[:, : pair_rows // 2], total[:, pair_rows // 2 :]
-    is_odd = odd > 0
-    other = swap(jnp.where(is_odd, first, second).astype(jnp.bfloat16), 1).astype(jnp.float32)
-    mine = jnp.where(is_odd, second, first)
-    return jnp.concatenate(
-        [jnp.where(is_odd, other, mine), jnp.where(is_odd, mine, other)], axis=0
-    )
+def chip_sum(keep, send):
+    received = swap(send, 1)
+    count = lax.axis_size("dp") // 2
+    rows = keep.shape[0] // count
+    total = [
+        added(keep[at * rows : (at + 1) * rows], received[at * rows : (at + 1) * rows])
+        for at in range(count)
+    ]
+    return total[0], [item.astype(keep.dtype) for item in total[1:]]
+
+
+def exchange(sends):
+    return [swap(item, 2 * at + 2) for at, item in enumerate(sends)]
+
+
+def final_kernel(count, rotary, *refs):
+    total = refs[0][...].astype(jnp.float32)
+    for ref in refs[1 : 1 + count]:
+        total = total + ref[...].astype(jnp.float32)
+    if rotary:
+        total = total * refs[1 + count][...] - pltpu.roll(total, HD // 2, 1) * refs[2 + count][...]
+    out_ref = refs[-1]
+    out_ref[...] = total.astype(out_ref.dtype)
+
+
+def final_sum(keep, received, tables, after):
+    vmem = pl.BlockSpec(memory_space=pltpu.VMEM)
+    hbm = pl.BlockSpec(memory_space=pl.ANY)
+    parts = [keep, *received, *tables]
+    return pl.pallas_call(
+        partial(final_kernel, len(received), len(tables) > 0),
+        out_shape=jax.ShapeDtypeStruct(keep.shape, jnp.bfloat16),
+        in_specs=[vmem] * len(parts) + [hbm] * len(after),
+        out_specs=vmem,
+        cost_estimate=pl.CostEstimate(
+            flops=8 * keep.size, bytes_accessed=12 * keep.size, transcendentals=0
+        ),
+    )(*parts, *after)
+
+
+def product_kernel(my_ref, left_ref, right_ref, *refs):
+    total = jnp.dot(left_ref[...], right_ref[...], preferred_element_type=jnp.float32)
+    refs[-1][0] = total.astype(refs[-1].dtype)
+
+
+def product_sum_kernel(count, my_ref, left_ref, right_ref, base_ref, *refs):
+    total = jnp.dot(left_ref[...], right_ref[...], preferred_element_type=jnp.float32)
+    total = total + base_ref[0].astype(jnp.float32)
+    for at, out_ref in enumerate(refs[-count:]):
+
+        @pl.when(pl.program_id(0) == at)
+        def store():
+            out_ref[...] = total.astype(out_ref.dtype)
+
+
+def product(mine, left, right, base, after):
+    count = lax.axis_size("dp") // 2
+    rows = left.shape[0]
+    cols = right.shape[1] // count
+    if cols % 128:
+        total = jnp.dot(left, right, preferred_element_type=jnp.float32)
+        pieces = jnp.moveaxis(total.reshape(rows, count, cols), 1, 0)
+        pieces = jnp.take(pieces, jnp.arange(count, dtype=jnp.int32) ^ mine, axis=0)
+        if base is None:
+            return pieces.astype(jnp.bfloat16)
+        pieces = pieces + base.astype(jnp.float32)
+        return [pieces[0]] + [pieces[at].astype(jnp.bfloat16) for at in range(1, count)]
+    stacked = pl.BlockSpec((1, rows, cols), lambda step, my_ref: (step, 0, 0))
+    if base is None:
+        body = product_kernel
+        bases = []
+        out_specs = stacked
+        out_shape = jax.ShapeDtypeStruct((count, rows, cols), jnp.bfloat16)
+    else:
+        body = partial(product_sum_kernel, count)
+        bases = [base]
+        out_specs = [pl.BlockSpec((rows, cols), lambda step, my_ref: (0, 0))] * count
+        out_shape = [
+            jax.ShapeDtypeStruct((rows, cols), jnp.bfloat16 if at else jnp.float32)
+            for at in range(count)
+        ]
+    return pl.pallas_call(
+        body,
+        grid_spec=pltpu.PrefetchScalarGridSpec(
+            num_scalar_prefetch=1,
+            grid=(count,),
+            in_specs=[
+                pl.BlockSpec(left.shape, lambda step, my_ref: (0, 0)),
+                pl.BlockSpec((right.shape[0], cols), lambda step, my_ref: (0, step ^ my_ref[0])),
+            ]
+            + [stacked] * len(bases)
+            + [pl.BlockSpec(memory_space=pl.ANY)] * len(after),
+            out_specs=out_specs,
+        ),
+        out_shape=out_shape,
+        compiler_params=pltpu.CompilerParams(vmem_limit_bytes=32 * 1024 * 1024),
+        cost_estimate=pl.CostEstimate(
+            flops=2 * rows * right.size, bytes_accessed=2 * right.size, transcendentals=0
+        ),
+    )(mine.reshape(1), left, right, *bases, *after)
 
 
 def local(query, key, value, grad_out, out_weight, plan, segments):
@@ -382,11 +427,12 @@
     own_key = lax.dynamic_slice_in_dim(key, kv_head * HD, HD, 1)
     own_value = lax.dynamic_slice_in_dim(value, kv_head * HD, HD, 1)
 
-    own_places = positions_of(segments).reshape(block_count, ROWBLK)
-    places_all = own_places
-    for bit in bits:
-        places_all = jnp.concatenate([places_all, swap(places_all, bit)], axis=0)
-    values = spread(own_value, bits[1:] + bits[:1])
+    own_places = positions_of(segments).reshape(1, block_count, ROWBLK)
+    pair_places = jnp.concatenate([own_places, swap(own_places, 1)], axis=0)
+    places_all = jnp.concatenate(
+        [pair_places] + [swap(pair_places, step) for step in range(2, rank_count, 2)], axis=0
+    ).reshape(-1, ROWBLK)
+    values = spread(own_value)
     up = jnp.dot(grad_out, out_weight, preferred_element_type=jnp.float32).astype(jnp.bfloat16)
 
     mine = my_rank * block_count + jnp.arange(block_count, dtype=jnp.int32)
@@ -401,14 +447,13 @@
     cosine, sine = rope_tables(places.reshape(row_count), HD)
     key_f = own_key.astype(jnp.float32)
     rot_key = (key_f * cosine + swap_halves(key_f) * sine).astype(jnp.bfloat16)
-    keys = spread(rot_key, bits[:0:-1] + bits[:1])
+    keys = spread(rot_key)
 
     distance = (plan // block_count) ^ my_rank
     within = plan % block_count
-    key_bits = bits[:1] + bits[:0:-1]
+    half_place = (distance & 1) * (rank_count // 2) + distance // 2
     tables = (
-        place_of(distance, key_bits) * block_count + within,
-        place_of(distance, bits) * block_count + within,
+        half_place * block_count + within,
         distance * block_count + within,
         run,
         slot,
@@ -417,15 +462,35 @@
     grad_query, attn_t, gkey_keep, gkey_send, gvalue_keep, gvalue_send = attend(
         tables, query, up, cosine, sine, places, keys, values
     )
-    value_partial = halve(gvalue_keep, gvalue_send, bits).astype(jnp.bfloat16)
-    gkey = halve(gkey_keep, gkey_send, key_bits)
-    key_partial = (gkey * cosine - swap_halves(gkey) * sine).astype(jnp.bfloat16)
-
-    value_all = lane_gather(value_partial, my_lane)
-    key_all = lane_gather(key_partial, my_lane)
-
-    attn_t = lax.optimization_barrier((attn_t, key_partial, value_partial))[0]
-    weight_grad = weight_sum(attn_t, grad_out, my_rank, bits).T
+    value_keep, value_sends = chip_sum(gvalue_keep, gvalue_send)
+    value_received = exchange(value_sends)
+    key_keep, key_sends = chip_sum(gkey_keep, gkey_send)
+    key_received = exchange(key_sends)
+
+    width = attn_t.shape[0]
+    odd = my_rank & 1
+    halves = attn_t.reshape(2, width // 2, row_count)
+    pair_rows = grad_out.shape[1] // (rank_count // 2)
+
+    def half_of(which):
+        return lax.dynamic_index_in_dim(halves, which, 0, keepdims=False)
+
+    first = swap(product(my_rank // 2, half_of(1 - odd), grad_out, None, key_sends), 1)
+    value_partial = final_sum(value_keep, value_received, (), ())
+    value_all, value_pieces = lane_gather(value_partial, my_lane)
+    kept, *sends = product(my_rank // 2, half_of(odd), grad_out, first, [value_partial])
+    key_partial = final_sum(key_keep, key_received, (cosine, sine), [sends[0], value_pieces[0]])
+    key_all, key_pieces = lane_gather(key_partial, my_lane)
+    total = kept
+    for item in exchange(sends):
+        total = total + item.astype(jnp.float32)
+    low, high = total[:, : pair_rows // 2], total[:, pair_rows // 2 :]
+    is_odd = odd > 0
+    other = swap(jnp.where(is_odd, low, high).astype(jnp.bfloat16), 1).astype(jnp.float32)
+    mine_half = jnp.where(is_odd, high, low)
+    weight_grad = jnp.concatenate(
+        [jnp.where(is_odd, other, mine_half), jnp.where(is_odd, mine_half, other)], axis=0
+    ).T
     lanes_per_key = group // local_heads
 
     def combine(gathered):

time: 176 us -> 173 us (0.983)
  starting transfers between devices: 33.8 us -> 44.1 us
  waiting for transfers between devices: 66.9 us -> 56.7 us
  matrix products: 19.1 us -> 9.04 us
  Pallas kernels: 27.6 us -> 37 us
  other arithmetic: 19.6 us -> 13 us
  local copies, waits for them, and re-layouts: 7.57 us -> 11.9 us
    ppermute x29 -> x31, waiting for transfers between devices: 51.1 us -> 31.7 us  [swap(): lax.ppermute(array, 'dp', [(rank, rank ^ bit) for rank in range(ranks)])]
    dot_general x2 -> x0, matrix products: 11.8 us -> none  [product(): return jnp.dot(picked, grad_out, preferred_element_type=jnp.float32)]
    pallas_call x2 -> x6, Pallas kernels: 7.08 us -> 18.3 us  [the longest x2 9.1 us: product(): pl.pallas_call(body, grid_spec=pltpu.PrefetchScalarGridSpec(num_scalar_pr...]
    ppermute x8, waiting for transfers between devices: 15.8 us -> 25 us  [send(): return lax.ppermute(item, 'tensor', pairs)]
    ppermute x29 -> x31, starting transfers between devices: 22.3 us -> 31 us  [swap(): lax.ppermute(array, 'dp', [(rank, rank ^ bit) for rank in range(ranks)])]
    convert_element_type x11 -> x4, other arithmetic: 9.32 us -> 4.11 us  [the longest x2 3.46 us: chip_sum(): return (total[0], [item.astype(keep.dtype) for item in total[1:]])]
    unnamed x35 -> x36, local copies, waits for them, and re-layouts: 5.37 us -> 9.58 us
    pallas_call x1, Pallas kernels: 20.5 us -> 18.7 us  [attend(): pl.pallas_call(partial(attend_kernel, heads, ranks), out_shape=(jax.Shape...]
  transfers between devices with their start and end apart: 37 -> 39, of which waited for: 17 -> 18; matrix products, arithmetic and copies ran while one was open for 15% -> 13% of each run, Pallas kernels for 4% -> 8%
where the time goes in v4:
time: 173 us
  waiting for transfers between devices  56.7 us (33%)
  starting transfers between devices  44.1 us (25%)
  Pallas kernels  37 us (21%)
  other arithmetic  13 us (8%)
  local copies, waits for them, and re-layouts  11.9 us (7%)
  matrix products  9.04 us (5%)
    ppermute x31, waiting for transfers between devices, swap(): lax.ppermute(array, 'dp', [(rank, rank ^ bit) for rank in range(ranks)])  31.7 us
    ppermute x31, starting transfers between devices, swap(): lax.ppermute(array, 'dp', [(rank, rank ^ bit) for rank in range(ranks)])  31 us
    ppermute x8, waiting for transfers between devices, send(): return lax.ppermute(item, 'tensor', pairs)  25 us
    pallas_call x1, Pallas kernels, attend(): pl.pallas_call(partial(attend_kernel, heads, ranks), out_shape=(jax.Shape...  18.7 us
    ppermute x8, starting transfers between devices, send(): return lax.ppermute(item, 'tensor', pairs)  13.1 us
    unnamed x36, local copies, waits for them, and re-layouts  9.58 us
    pallas_call x2, Pallas kernels, product(): pl.pallas_call(body, grid_spec=pltpu.PrefetchScalarGridSpec(num_scalar_pr...  9.1 us
    dot_general x1, matrix products, local(): jnp.dot(grad_out, out_weight, preferred_element_type=jnp.float32)  9.04 us
  transfers between devices with their start and end apart: 39, of which 18 were waited for; matrix products, arithmetic and copies ran while one was open for 13% of the time, Pallas kernels for 8%

profile of v4, /device:TPU:0, one launch (start us, length us, event | category | flops | bytes accessed | tf_op | source)
XLA Modules:
  0.0 172.7 jit_solution(14296052174345698405)
XLA Ops:
  1.9 3.0 %collective-permute-start.12 = (bf16[1024,128]{1,0:T(8,128)(2,1)S(1)}, bf16[1024,128]{1,0:T(8,128)(2,1)S(1)}, u32[]{:S(2)}, u32[]{:S(2)}) collective-permute-start(bf16[1024,128]{1,0:T(8,128)(2,1)S(1)} %constant_dynamic-slice_fusion.refs_8_), channel_id=1, source_target_pairs={{0,8},{4,12},{8,0},{12,4},{16,24},{20,28},{24,16},{28,20},{1,9},{5... | collective-permute-start | bytes 786440 | tf_op jit(solution)/shard_map/ppermute | solution.py:300
  10.5 9.0 %convolution_convert_fusion.up_ref = bf16[1024,512]{1,0:T(8,128)(2,1)} fusion(bf16[1024,3584]{1,0:T(8,128)(2,1)} %right_ref.3, bf16[3584,512]{1,0:T(8,128)(2,1)} %param.17), kind=kOutput, calls=%fused_computation.1 | convolution fusion | flops 3758620672 | bytes 12058624 | tf_op jit(solution)/shard_map/dot_general | solution.py:436
  19.6 2.0 %collective-permute-start.1 = (s32[2,8,128]{2,1,0:T(8,128)S(1)}, s32[2,8,128]{2,1,0:T(8,128)S(1)}, u32[]{:S(2)}, u32[]{:S(2)}) collective-permute-start(s32[2,8,128]{2,1,0:T(8,128)S(1)} %pad_add_fusion), channel_id=1, source_target_pairs={{0,8},{4,12},{8,0},{12,4},{16,24},{20,28},{24,16},{28,20},{1,9},{5... | collective-permute-start | bytes 24584 | tf_op jit(solution)/shard_map/ppermute | solution.py:300
  21.6 1.7 collective-permute-done.1
  23.3 2.0 %collective-permute-start.2 = (s32[2,8,128]{2,1,0:T(8,128)S(1)}, s32[2,8,128]{2,1,0:T(8,128)S(1)}, u32[]{:S(2)}, u32[]{:S(2)}) collective-permute-start(s32[2,8,128]{2,1,0:T(8,128)S(1)} %pad_add_fusion), channel_id=1, source_target_pairs={{0,16},{4,20},{8,24},{12,28},{16,0},{20,4},{24,8},{28,12},{1,17},{... | collective-permute-start | bytes 24584 | tf_op jit(solution)/shard_map/ppermute | solution.py:300
  25.3 1.7 collective-permute-done.2
  27.0 2.9 %collective-permute-start.3 = (s32[2,8,128]{2,1,0:T(8,128)S(1)}, s32[2,8,128]{2,1,0:T(8,128)S(1)}, u32[]{:S(2)}, u32[]{:S(2)}) collective-permute-start(s32[2,8,128]{2,1,0:T(8,128)S(1)} %pad_add_fusion), channel_id=1, source_target_pairs={{0,24},{4,28},{8,16},{12,20},{16,8},{20,12},{24,0},{28,4},{1,25},{... | collective-permute-start | bytes 24584 | tf_op jit(solution)/shard_map/ppermute | solution.py:300
  32.2 1.9 %fusion.5 = (f32[1024,64]{1,0:T(8,128)S(1)}, f32[1024,64]{1,0:T(8,128)S(1)}, f32[1024,64]{1,0:T(8,128)S(1)}) fusion(f32[64]{0:T(128)S(1)} %multiply_add_fusion, f32[1024]{0:T(1024)S(1)} %get-tuple-element.38), kind=kLoop, calls=%fused_computation.29 | loop fusion | flops 262144 | bytes 790784 | tf_op jit(solution)/shard_map/neg | solution.py:67
  35.6 3.0 %collective-permute-start.9 = (bf16[1024,128]{1,0:T(8,128)(2,1)S(1)}, bf16[1024,128]{1,0:T(8,128)(2,1)S(1)}, u32[]{:S(2)}, u32[]{:S(2)}) collective-permute-start(bf16[1024,128]{1,0:T(8,128)(2,1)S(1)} %get-tuple-element.36.refs_0_), channel_id=1, source_target_pairs={{0,24},{4,28},{8,16},{12,20},{16,8},{20,12},{24,0},{28,4},{1,25},{... | collective-permute-start | bytes 786440 | tf_op jit(solution)/shard_map/ppermute | solution.py:300
  39.8 4.7 %collective-permute-done.9.refs_6_ = bf16[1024,128]{1,0:T(8,128)(2,1)S(1)} collective-permute-done((bf16[1024,128]{1,0:T(8,128)(2,1)S(1)}, bf16[1024,128]{1,0:T(8,128)(2,1)S(1)}, u32[]{:S(2)}, u32[]{:S(2)}) %collective-permute-start.9) | collective-permute-done | bytes 262176 | tf_op jit(solution)/shard_map/ppermute | solution.py:300
  44.5 3.0 %collective-permute-done.5.refs_2_ = bf16[1024,128]{1,0:T(8,128)(2,1)S(1)} collective-permute-done((bf16[1024,128]{1,0:T(8,128)(2,1)S(1)}, bf16[1024,128]{1,0:T(8,128)(2,1)S(1)}, u32[]{:S(2)}, u32[]{:S(2)}) %collective-permute-start.5) | collective-permute-done | bytes 262176 | tf_op jit(solution)/shard_map/ppermute | solution.py:300
  50.2 18.7 %shard_map.156 = (bf16[1024,512]{1,0:T(8,128)(2,1)}, bf16[512,1024]{1,0:T(8,128)(2,1)}, bf16[4096,128]{1,0:T(8,128)(2,1)}, bf16[4096,128]{1,0:T(8,128)(2,1)}, bf...) custom-call(s32[64]{0:T(128)S(1)} %multiply_add_fusion.2.target_ref, s32[64]{0:T(128)S(1)} %get-tuple-element.45.source_ref, ...), custom_call_target="tpu_custom_call" | custom-call | flops 5368709120 | bytes 16777216 | tf_op jit(solution)/shard_map/pallas_call | solution.py:219
  69.0 4.7 %collective-permute-start.18 = (bf16[4096,128]{1,0:T(8,128)(2,1)}, bf16[4096,128]{1,0:T(8,128)(2,1)S(1)}, u32[]{:S(2)}, u32[]{:S(2)}) collective-permute-start(bf16[4096,128]{1,0:T(8,128)(2,1)} %get-tuple-element.16), channel_id=1, source_target_pairs={{0,4},{4,0},{8,12},{12,8},{16,20},{20,16},{24,28},{28,24},{1,5},{5... | collective-permute-start | bytes 3145736 | tf_op jit(solution)/shard_map/ppermute | solution.py:300
  76.2 2.4 %add_convert_fusion.3 = (bf16[1024,128]{1,0:T(8,128)(2,1)}, bf16[1024,128]{1,0:T(8,128)(2,1)}, bf16[1024,128]{1,0:T(8,128)(2,1)}, f32[1024,128]{1,0:T(8,128)}) fusion(bf16[4096,128]{1,0:T(8,128)(2,1)S(1)} %collective-permute-done.18, bf16[4096,128]{1,0:T(8,128)(2,1)} %get-tuple-element.15), kind=kLoop, calls=%fused_computation.23 | loop fusion | flops 1966080 | bytes 3407872 | tf_op jit(solution)/shard_map/convert_element_type | solution.py:323
  78.6 3.1 %copy-done.1 = bf16[1024,3584]{1,0:T(8,128)(2,1)S(1)} copy-done((bf16[1024,3584]{1,0:T(8,128)(2,1)S(1)}, bf16[1024,3584]{1,0:T(8,128)(2,1)}, u32[]{:S(2)}) %copy-start.1) | copy-done | bytes 7340056
  81.7 4.3 %shard_map.157 = bf16[4,256,896]{2,1,0:T(8,128)(2,1)} custom-call(s32[1]{0:T(128)} %bitcast.6.my_ref, bf16[256,1024]{1,0:T(8,128)(2,1)S(1)} %get-tuple-element.58.left_ref, bf16[1024,3584]{1,0:T(8,128)(2,1)S(1)} %copy-done.1, bf16[1024,128]{1,0:T(8,128)(2,1)} %get-tuple-element.54.refs_0_, bf16[1024,128]{1,0:T(8,128)(2,1)} %get-tuple-element.53.refs_1_, ...), custom_call_target="tpu_custom_call" | custom-call | flops 1879048192 | bytes 7340032 | tf_op jit(solution)/shard_map/pallas_call | solution.py:396
  86.5 4.8 %collective-permute-done.23 = bf16[4096,128]{1,0:T(8,128)(2,1)S(1)} collective-permute-done((bf16[4096,128]{1,0:T(8,128)(2,1)S(1)}, bf16[4096,128]{1,0:T(8,128)(2,1)S(1)}, u32[]{:S(2)}, u32[]{:S(2)}) %collective-permute-start.23) | collective-permute-done | bytes 1048608 | tf_op jit(solution)/shard_map/ppermute | solution.py:300
  92.3 3.5 %collective-permute-start.26 = (bf16[1024,128]{1,0:T(8,128)(2,1)S(1)}, bf16[1024,128]{1,0:T(8,128)(2,1)}, u32[]{:S(2)}, u32[]{:S(2)}) collective-permute-start(bf16[1024,128]{1,0:T(8,128)(2,1)S(1)} %get-tuple-element.48), channel_id=1, source_target_pairs={{0,24},{4,28},{8,16},{12,20},{16,8},{20,12},{24,0},{28,4},{1,25},{... | collective-permute-start | bytes 786440 | tf_op jit(solution)/shard_map/ppermute | solution.py:300
  95.8 5.7 %collective-permute-done.24.refs_1_ = bf16[1024,128]{1,0:T(8,128)(2,1)} collective-permute-done((bf16[1024,128]{1,0:T(8,128)(2,1)S(1)}, bf16[1024,128]{1,0:T(8,128)(2,1)}, u32[]{:S(2)}, u32[]{:S(2)}) %collective-permute-start.24) | collective-permute-done | bytes 262176 | tf_op jit(solution)/shard_map/ppermute | solution.py:300
  101.6 5.6 %collective-permute-done.25.refs_2_ = bf16[1024,128]{1,0:T(8,128)(2,1)} collective-permute-done((bf16[1024,128]{1,0:T(8,128)(2,1)S(1)}, bf16[1024,128]{1,0:T(8,128)(2,1)}, u32[]{:S(2)}, u32[]{:S(2)}) %collective-permute-start.25) | collective-permute-done | bytes 262176 | tf_op jit(solution)/shard_map/ppermute | solution.py:300
  108.2 2.1 %shard_map.158.refs_0_ = bf16[1024,128]{1,0:T(8,128)(2,1)} custom-call(f32[1024,128]{1,0:T(8,128)} %get-tuple-element.51.refs_0_, bf16[1024,128]{1,0:T(8,128)(2,1)} %collective-permute-done.24.refs_1_, bf16[1024,128]{1,0:T(8,128)(2,1)} %collective-permute-done.25.refs_2_, bf16[1024,128]{1,0:T(8,128)(2,1)} %collective-permute-done.26.refs_3_), custom_call_target="tpu_custom_call" | custom-call | flops 1048576 | bytes 1572864 | tf_op jit(solution)/shard_map/pallas_call | solution.py:344
  111.9 3.1 %copy-done.2 = bf16[1024,3584]{1,0:T(8,128)(2,1)S(1)} copy-done((bf16[1024,3584]{1,0:T(8,128)(2,1)S(1)}, bf16[1024,3584]{1,0:T(8,128)(2,1)}, u32[]{:S(2)}) %copy-start.2) | copy-done | bytes 7340056
  115.0 4.8 %shard_map.159 = (f32[256,896]{1,0:T(8,128)S(1)}, bf16[256,896]{1,0:T(8,128)(2,1)}, bf16[256,896]{1,0:T(8,128)(2,1)}, bf16[256,896]{1,0:T(8,128)(2,1)}) custom-call(s32[1]{0:T(128)} %bitcast.6.my_ref, bf16[256,1024]{1,0:T(8,128)(2,1)S(1)} %get-tuple-element.59.left_ref, bf16[1024,3584]{1,0:T(8,128)(2,1)S(1)} %copy-done.2, ...), custom_call_target="tpu_custom_call" | custom-call | flops 1879048192 | bytes 7340032 | tf_op jit(solution)/shard_map/pallas_call | solution.py:396
  124.7 2.6 %collective-permute-start.32 = (bf16[1024,128]{1,0:T(8,128)(2,1)}, bf16[1024,128]{1,0:T(8,128)(2,1)}, u32[]{:S(2)}, u32[]{:S(2)}) collective-permute-start(bf16[1024,128]{1,0:T(8,128)(2,1)} %shard_map.158.refs_0_), channel_id=1, source_target_pairs={{0,2},{2,0},{1,3},{3,1},{4,6},{6,4},{5,7},{7,5},{8,10},{10,8},{9,1... | collective-permute-start | bytes 786440 | tf_op jit(solution)/shard_map/ppermute | solution.py:276
  127.4 2.5 %shard_map.160.refs_0_ = bf16[1024,128]{1,0:T(8,128)(2,1)} custom-call(f32[1024,128]{1,0:T(8,128)} %get-tuple-element.55.refs_0_, bf16[1024,128]{1,0:T(8,128)(2,1)} %collective-permute-done.19.refs_1_, bf16[1024,128]{1,0:T(8,128)(2,1)} %collective-permute-done.20.refs_2_, bf16[1024,128]{1,0:T(8,128)(2,1)} %collective-permute-done.21.refs_3_, ...), custom_call_target="tpu_custom_call" | custom-call | flops 1048576 | bytes 1572864 | tf_op jit(solution)/shard_map/pallas_call | solution.py:344
  130.2 13.4 %collective-permute-done.32.refs_2_ = bf16[1024,128]{1,0:T(8,128)(2,1)} collective-permute-done((bf16[1024,128]{1,0:T(8,128)(2,1)}, bf16[1024,128]{1,0:T(8,128)(2,1)}, u32[]{:S(2)}, u32[]{:S(2)}) %collective-permute-start.32) | collective-permute-done | bytes 262176 | tf_op jit(solution)/shard_map/ppermute | solution.py:276
  145.0 4.3 %collective-permute-done.29.refs_2_ = bf16[1024,128]{1,0:T(8,128)(2,1)} collective-permute-done((bf16[1024,128]{1,0:T(8,128)(2,1)}, bf16[1024,128]{1,0:T(8,128)(2,1)}, u32[]{:S(2)}, u32[]{:S(2)}) %collective-permute-start.29) | collective-permute-done | bytes 262176 | tf_op jit(solution)/shard_map/ppermute | solution.py:276
  150.5 3.3 %collective-permute-start.28 = (bf16[1024,128]{1,0:T(8,128)(2,1)}, bf16[1024,128]{1,0:T(8,128)(2,1)}, u32[]{:S(2)}, u32[]{:S(2)}) collective-permute-start(bf16[1024,128]{1,0:T(8,128)(2,1)} %shard_map.160.refs_0_), channel_id=1, source_target_pairs={{0,1},{1,0},{2,3},{3,2},{4,5},{5,4},{6,7},{7,6},{8,9},{9,8},{10,11... | collective-permute-start | bytes 786440 | tf_op jit(solution)/shard_map/ppermute | solution.py:276
  160.7 2.3 %shard_map.162 = bf16[1024,512]{1,0:T(8,128)(2,1)} custom-call(s32[5]{0:T(128)} %broadcast_xor_fusion.column_ref, s32[5]{0:T(128)} %or_convert_fusion.active_ref, bf16[1024,128]{1,0:T(8,128)(2,1)} %shard_map.158.refs_0_, bf16[1024,128]{1,0:T(8,128)(2,1)} %collective-permute-done.27.refs_7_.refs_1_, bf16[1024,128]{1,0:T(8,128)(2,1)} %collective-permute-done.32.refs_2_, ...), custom_call_target="tpu_custom_call" | custom-call | bytes 2097152 | tf_op jit(solution)/shard_map/pallas_call | solution.py:260
  163.0 3.1 %collective-permute-done.28.refs_1_ = bf16[1024,128]{1,0:T(8,128)(2,1)} collective-permute-done((bf16[1024,128]{1,0:T(8,128)(2,1)}, bf16[1024,128]{1,0:T(8,128)(2,1)}, u32[]{:S(2)}, u32[]{:S(2)}) %collective-permute-start.28) | collective-permute-done | bytes 262176 | tf_op jit(solution)/shard_map/ppermute | solution.py:276
  166.0 2.8 %collective-permute-done.31.refs_4_ = bf16[1024,128]{1,0:T(8,128)(2,1)} collective-permute-done((bf16[1024,128]{1,0:T(8,128)(2,1)}, bf16[1024,128]{1,0:T(8,128)(2,1)}, u32[]{:S(2)}, u32[]{:S(2)}) %collective-permute-start.31) | collective-permute-done | bytes 262176 | tf_op jit(solution)/shard_map/ppermute | solution.py:276
  168.8 2.3 %shard_map.161 = bf16[1024,512]{1,0:T(8,128)(2,1)} custom-call(s32[5]{0:T(128)} %broadcast_xor_fusion.column_ref, s32[5]{0:T(128)} %or_convert_fusion.active_ref, bf16[1024,128]{1,0:T(8,128)(2,1)} %shard_map.160.refs_0_, bf16[1024,128]{1,0:T(8,128)(2,1)} %collective-permute-done.28.refs_1_, bf16[1024,128]{1,0:T(8,128)(2,1)} %collective-permute-done.29.refs_2_, ...), custom_call_target="tpu_custom_call" | custom-call | bytes 2097152 | tf_op jit(solution)/shard_map/pallas_call | solution.py:260
  (125 shorter events, 37.4 us)
Async XLA Ops:
  1.9 36.7 %collective-permute-start.12 = (bf16[1024,128]{1,0:T(8,128)(2,1)S(1)}, bf16[1024,128]{1,0:T(8,128)(2,1)S(1)}, u32[]{:S(2)}, u32[]{:S(2)}) collective-permute-start(bf16[1024,128]{1,0:T(8,128)(2,1)S(1)} %constant_dynamic-slice_fusion.refs_8_), channel_id=1, source_target_pairs={{0,8},{4,12},{8,0},{12,4},{16,24},{20,28},{24,16},{28,20},{1,9},{5... | collective-permute-start | bytes 786440 | tf_op jit(solution)/shard_map/ppermute | solution.py:300
  4.9 34.2 %collective-permute-start.14 = (bf16[1024,128]{1,0:T(8,128)(2,1)S(1)}, bf16[1024,128]{1,0:T(8,128)(2,1)S(1)}, u32[]{:S(2)}, u32[]{:S(2)}) collective-permute-start(bf16[1024,128]{1,0:T(8,128)(2,1)S(1)} %constant_dynamic-slice_fusion.refs_8_), channel_id=1, source_target_pairs={{0,16},{4,20},{8,24},{12,28},{16,0},{20,4},{24,8},{28,12},{1,17},{... | collective-permute-start | bytes 786440 | tf_op jit(solution)/shard_map/ppermute | solution.py:300
  6.4 32.8 %collective-permute-start.16 = (bf16[1024,128]{1,0:T(8,128)(2,1)S(1)}, bf16[1024,128]{1,0:T(8,128)(2,1)S(1)}, u32[]{:S(2)}, u32[]{:S(2)}) collective-permute-start(bf16[1024,128]{1,0:T(8,128)(2,1)S(1)} %constant_dynamic-slice_fusion.refs_8_), channel_id=1, source_target_pairs={{0,24},{4,28},{8,16},{12,20},{16,8},{20,12},{24,0},{28,4},{1,25},{... | collective-permute-start | bytes 786440 | tf_op jit(solution)/shard_map/ppermute | solution.py:300
  6.4 32.8 %collective-permute-start.11 = (bf16[1024,128]{1,0:T(8,128)(2,1)S(1)}, bf16[1024,128]{1,0:T(8,128)(2,1)S(1)}, u32[]{:S(2)}, u32[]{:S(2)}) collective-permute-start(bf16[1024,128]{1,0:T(8,128)(2,1)S(1)} %constant_dynamic-slice_fusion.refs_8_), channel_id=1, source_target_pairs={{0,4},{4,0},{8,12},{12,8},{16,20},{20,16},{24,28},{28,24},{1,5},{5... | collective-permute-start | bytes 786440 | tf_op jit(solution)/shard_map/ppermute | solution.py:300
  7.9 11.7 %collective-permute-start = (s32[1,8,128]{2,1,0:T(8,128)S(1)}, s32[1,8,128]{2,1,0:T(8,128)S(1)}, u32[]{:S(2)}, u32[]{:S(2)}) collective-permute-start(s32[1,8,128]{2,1,0:T(8,128)S(1)} %get-tuple-element.44), channel_id=1, source_target_pairs={{0,4},{4,0},{8,12},{12,8},{16,20},{20,16},{24,28},{28,24},{1,5},{5... | collective-permute-start | bytes 12296 | tf_op jit(solution)/shard_map/ppermute | solution.py:300
  27.0 4.5 %collective-permute-start.3 = (s32[2,8,128]{2,1,0:T(8,128)S(1)}, s32[2,8,128]{2,1,0:T(8,128)S(1)}, u32[]{:S(2)}, u32[]{:S(2)}) collective-permute-start(s32[2,8,128]{2,1,0:T(8,128)S(1)} %pad_add_fusion), channel_id=1, source_target_pairs={{0,24},{4,28},{8,16},{12,20},{16,8},{20,12},{24,0},{28,4},{1,25},{... | collective-permute-start | bytes 24584 | tf_op jit(solution)/shard_map/ppermute | solution.py:300
  35.6 8.9 %collective-permute-start.9 = (bf16[1024,128]{1,0:T(8,128)(2,1)S(1)}, bf16[1024,128]{1,0:T(8,128)(2,1)S(1)}, u32[]{:S(2)}, u32[]{:S(2)}) collective-permute-start(bf16[1024,128]{1,0:T(8,128)(2,1)S(1)} %get-tuple-element.36.refs_0_), channel_id=1, source_target_pairs={{0,24},{4,28},{8,16},{12,20},{16,8},{20,12},{24,0},{28,4},{1,25},{... | collective-permute-start | bytes 786440 | tf_op jit(solution)/shard_map/ppermute | solution.py:300
  38.6 9.0 %collective-permute-start.5 = (bf16[1024,128]{1,0:T(8,128)(2,1)S(1)}, bf16[1024,128]{1,0:T(8,128)(2,1)S(1)}, u32[]{:S(2)}, u32[]{:S(2)}) collective-permute-start(bf16[1024,128]{1,0:T(8,128)(2,1)S(1)} %get-tuple-element.36.refs_0_), channel_id=1, source_target_pairs={{0,8},{4,12},{8,0},{12,4},{16,24},{20,28},{24,16},{28,20},{1,9},{5... | collective-permute-start | bytes 786440 | tf_op jit(solution)/shard_map/ppermute | solution.py:300
  39.1 8.5 %collective-permute-start.7 = (bf16[1024,128]{1,0:T(8,128)(2,1)S(1)}, bf16[1024,128]{1,0:T(8,128)(2,1)S(1)}, u32[]{:S(2)}, u32[]{:S(2)}) collective-permute-start(bf16[1024,128]{1,0:T(8,128)(2,1)S(1)} %get-tuple-element.36.refs_0_), channel_id=1, source_target_pairs={{0,16},{4,20},{8,24},{12,28},{16,0},{20,4},{24,8},{28,12},{1,17},{... | collective-permute-start | bytes 786440 | tf_op jit(solution)/shard_map/ppermute | solution.py:300
  39.2 8.9 %collective-permute-start.4 = (bf16[1024,128]{1,0:T(8,128)(2,1)S(1)}, bf16[1024,128]{1,0:T(8,128)(2,1)S(1)}, u32[]{:S(2)}, u32[]{:S(2)}) collective-permute-start(bf16[1024,128]{1,0:T(8,128)(2,1)S(1)} %get-tuple-element.36.refs_0_), channel_id=1, source_target_pairs={{0,4},{4,0},{8,12},{12,8},{16,20},{20,16},{24,28},{28,24},{1,5},{5... | collective-permute-start | bytes 786440 | tf_op jit(solution)/shard_map/ppermute | solution.py:300
  39.2 8.9 %collective-permute-start.13 = (bf16[1024,128]{1,0:T(8,128)(2,1)S(1)}, bf16[1024,128]{1,0:T(8,128)(2,1)S(1)}, u32[]{:S(2)}, u32[]{:S(2)}) collective-permute-start(bf16[1024,128]{1,0:T(8,128)(2,1)S(1)} %collective-permute-done.12.refs_10_), channel_id=1, source_target_pairs={{0,4},{4,0},{8,12},{12,8},{16,20},{20,16},{24,28},{28,24},{1,5},{5... | collective-permute-start | bytes 786440 | tf_op jit(solution)/shard_map/ppermute | solution.py:300
  69.0 7.2 %collective-permute-start.18 = (bf16[4096,128]{1,0:T(8,128)(2,1)}, bf16[4096,128]{1,0:T(8,128)(2,1)S(1)}, u32[]{:S(2)}, u32[]{:S(2)}) collective-permute-start(bf16[4096,128]{1,0:T(8,128)(2,1)} %get-tuple-element.16), channel_id=1, source_target_pairs={{0,4},{4,0},{8,12},{12,8},{16,20},{20,16},{24,28},{28,24},{1,5},{5... | collective-permute-start | bytes 3145736 | tf_op jit(solution)/shard_map/ppermute | solution.py:300
  86.0 25.9 %collective-permute-start.22 = (bf16[4,256,896]{2,1,0:T(8,128)(2,1)}, bf16[4,256,896]{2,1,0:T(8,128)(2,1)S(1)}, u32[]{:S(2)}, u32[]{:S(2)}) collective-permute-start(bf16[4,256,896]{2,1,0:T(8,128)(2,1)} %shard_map.157), channel_id=1, source_target_pairs={{0,4},{4,0},{8,12},{12,8},{16,20},{20,16},{24,28},{28,24},{1,5},{5... | collective-permute-start | bytes 5505032 | tf_op jit(solution)/shard_map/ppermute | solution.py:300
  86.4 4.9 %collective-permute-start.23 = (bf16[4096,128]{1,0:T(8,128)(2,1)S(1)}, bf16[4096,128]{1,0:T(8,128)(2,1)S(1)}, u32[]{:S(2)}, u32[]{:S(2)}) collective-permute-start(bf16[4096,128]{1,0:T(8,128)(2,1)S(1)} %copy-done.14), channel_id=1, source_target_pairs={{0,4},{4,0},{8,12},{12,8},{16,20},{20,16},{24,28},{28,24},{1,5},{5... | collective-permute-start | bytes 3145736 | tf_op jit(solution)/shard_map/ppermute | solution.py:300
  92.3 9.2 %collective-permute-start.24 = (bf16[1024,128]{1,0:T(8,128)(2,1)S(1)}, bf16[1024,128]{1,0:T(8,128)(2,1)}, u32[]{:S(2)}, u32[]{:S(2)}) collective-permute-start(bf16[1024,128]{1,0:T(8,128)(2,1)S(1)} %get-tuple-element.50), channel_id=1, source_target_pairs={{0,8},{4,12},{8,0},{12,4},{16,24},{20,28},{24,16},{28,20},{1,9},{5... | collective-permute-start | bytes 786440 | tf_op jit(solution)/shard_map/ppermute | solution.py:300
  92.3 14.9 %collective-permute-start.25 = (bf16[1024,128]{1,0:T(8,128)(2,1)S(1)}, bf16[1024,128]{1,0:T(8,128)(2,1)}, u32[]{:S(2)}, u32[]{:S(2)}) collective-permute-start(bf16[1024,128]{1,0:T(8,128)(2,1)S(1)} %get-tuple-element.49), channel_id=1, source_target_pairs={{0,16},{4,20},{8,24},{12,28},{16,0},{20,4},{24,8},{28,12},{1,17},{... | collective-permute-start | bytes 786440 | tf_op jit(solution)/shard_map/ppermute | solution.py:300
  92.3 15.9 %collective-permute-start.26 = (bf16[1024,128]{1,0:T(8,128)(2,1)S(1)}, bf16[1024,128]{1,0:T(8,128)(2,1)}, u32[]{:S(2)}, u32[]{:S(2)}) collective-permute-start(bf16[1024,128]{1,0:T(8,128)(2,1)S(1)} %get-tuple-element.48), channel_id=1, source_target_pairs={{0,24},{4,28},{8,16},{12,20},{16,8},{20,12},{24,0},{28,4},{1,25},{... | collective-permute-start | bytes 786440 | tf_op jit(solution)/shard_map/ppermute | solution.py:300
  95.8 25.9 %collective-permute-start.19 = (bf16[1024,128]{1,0:T(8,128)(2,1)}, bf16[1024,128]{1,0:T(8,128)(2,1)}, u32[]{:S(2)}, u32[]{:S(2)}) collective-permute-start(bf16[1024,128]{1,0:T(8,128)(2,1)} %get-tuple-element.54.refs_0_), channel_id=1, source_target_pairs={{0,8},{4,12},{8,0},{12,4},{16,24},{20,28},{24,16},{28,20},{1,9},{5... | collective-permute-start | bytes 786440 | tf_op jit(solution)/shard_map/ppermute | solution.py:300
  101.6 21.7 %collective-permute-start.20 = (bf16[1024,128]{1,0:T(8,128)(2,1)}, bf16[1024,128]{1,0:T(8,128)(2,1)}, u32[]{:S(2)}, u32[]{:S(2)}) collective-permute-start(bf16[1024,128]{1,0:T(8,128)(2,1)} %get-tuple-element.53.refs_1_), channel_id=1, source_target_pairs={{0,16},{4,20},{8,24},{12,28},{16,0},{20,4},{24,8},{28,12},{1,17},{... | collective-permute-start | bytes 786440 | tf_op jit(solution)/shard_map/ppermute | solution.py:300
  107.2 17.6 %collective-permute-start.21 = (bf16[1024,128]{1,0:T(8,128)(2,1)}, bf16[1024,128]{1,0:T(8,128)(2,1)}, u32[]{:S(2)}, u32[]{:S(2)}) collective-permute-start(bf16[1024,128]{1,0:T(8,128)(2,1)} %get-tuple-element.52.refs_2_), channel_id=1, source_target_pairs={{0,24},{4,28},{8,16},{12,20},{16,8},{20,12},{24,0},{28,4},{1,25},{... | collective-permute-start | bytes 786440 | tf_op jit(solution)/shard_map/ppermute | solution.py:300
  110.3 17.0 %collective-permute-start.27 = (bf16[1024,128]{1,0:T(8,128)(2,1)}, bf16[1024,128]{1,0:T(8,128)(2,1)}, u32[]{:S(2)}, u32[]{:S(2)}) collective-permute-start(bf16[1024,128]{1,0:T(8,128)(2,1)} %shard_map.158.refs_0_), channel_id=1, source_target_pairs={{0,1},{1,0},{2,3},{3,2},{4,5},{5,4},{6,7},{7,6},{8,9},{9,8},{10,11... | collective-permute-start | bytes 786440 | tf_op jit(solution)/shard_map/ppermute | solution.py:276
  120.7 29.8 %collective-permute-start.35 = (bf16[256,896]{1,0:T(8,128)(2,1)}, bf16[256,896]{1,0:T(8,128)(2,1)S(1)}, u32[]{:S(2)}, u32[]{:S(2)}) collective-permute-start(bf16[256,896]{1,0:T(8,128)(2,1)} %get-tuple-element.20.refs_6_), channel_id=1, source_target_pairs={{0,8},{4,12},{8,0},{12,4},{16,24},{20,28},{24,16},{28,20},{1,9},{5... | collective-permute-start | bytes 1376264 | tf_op jit(solution)/shard_map/ppermute | solution.py:300
  121.8 32.1 %collective-permute-start.36 = (bf16[256,896]{1,0:T(8,128)(2,1)}, bf16[256,896]{1,0:T(8,128)(2,1)S(1)}, u32[]{:S(2)}, u32[]{:S(2)}) collective-permute-start(bf16[256,896]{1,0:T(8,128)(2,1)} %get-tuple-element.22), channel_id=1, source_target_pairs={{0,16},{4,20},{8,24},{12,28},{16,0},{20,4},{24,8},{28,12},{1,17},{... | collective-permute-start | bytes 1376264 | tf_op jit(solution)/shard_map/ppermute | solution.py:300
  123.3 32.0 %collective-permute-start.37 = (bf16[256,896]{1,0:T(8,128)(2,1)}, bf16[256,896]{1,0:T(8,128)(2,1)S(1)}, u32[]{:S(2)}, u32[]{:S(2)}) collective-permute-start(bf16[256,896]{1,0:T(8,128)(2,1)} %get-tuple-element.23), channel_id=1, source_target_pairs={{0,24},{4,28},{8,16},{12,20},{16,8},{20,12},{24,0},{28,4},{1,25},{... | collective-permute-start | bytes 1376264 | tf_op jit(solution)/shard_map/ppermute | solution.py:300
  124.7 18.9 %collective-permute-start.32 = (bf16[1024,128]{1,0:T(8,128)(2,1)}, bf16[1024,128]{1,0:T(8,128)(2,1)}, u32[]{:S(2)}, u32[]{:S(2)}) collective-permute-start(bf16[1024,128]{1,0:T(8,128)(2,1)} %shard_map.158.refs_0_), channel_id=1, source_target_pairs={{0,2},{2,0},{1,3},{3,1},{4,6},{6,4},{5,7},{7,5},{8,10},{10,8},{9,1... | collective-permute-start | bytes 786440 | tf_op jit(solution)/shard_map/ppermute | solution.py:276
  129.9 19.3 %collective-permute-start.29 = (bf16[1024,128]{1,0:T(8,128)(2,1)}, bf16[1024,128]{1,0:T(8,128)(2,1)}, u32[]{:S(2)}, u32[]{:S(2)}) collective-permute-start(bf16[1024,128]{1,0:T(8,128)(2,1)} %shard_map.160.refs_0_), channel_id=1, source_target_pairs={{0,2},{2,0},{1,3},{3,1},{4,6},{6,4},{5,7},{7,5},{8,10},{10,8},{9,1... | collective-permute-start | bytes 786440 | tf_op jit(solution)/shard_map/ppermute | solution.py:276
  143.6 14.4 %collective-permute-start.33 = (bf16[1024,128]{1,0:T(8,128)(2,1)}, bf16[1024,128]{1,0:T(8,128)(2,1)}, u32[]{:S(2)}, u32[]{:S(2)}) collective-permute-start(bf16[1024,128]{1,0:T(8,128)(2,1)} %shard_map.158.refs_0_), channel_id=1, source_target_pairs={{1,2},{2,1},{5,6},{6,5},{9,10},{10,9},{13,14},{14,13},{17,18},{18,... | collective-permute-start | bytes 786440 | tf_op jit(solution)/shard_map/ppermute | solution.py:276
  149.2 11.4 %collective-permute-start.34 = (bf16[1024,128]{1,0:T(8,128)(2,1)}, bf16[1024,128]{1,0:T(8,128)(2,1)}, u32[]{:S(2)}, u32[]{:S(2)}) collective-permute-start(bf16[1024,128]{1,0:T(8,128)(2,1)} %collective-permute-done.32.refs_2_), channel_id=1, source_target_pairs={{1,0},{2,3},{5,4},{6,7},{9,8},{10,11},{13,12},{14,15},{17,16},{18,... | collective-permute-start | bytes 786440 | tf_op jit(solution)/shard_map/ppermute | solution.py:276
  150.5 15.5 %collective-permute-start.28 = (bf16[1024,128]{1,0:T(8,128)(2,1)}, bf16[1024,128]{1,0:T(8,128)(2,1)}, u32[]{:S(2)}, u32[]{:S(2)}) collective-permute-start(bf16[1024,128]{1,0:T(8,128)(2,1)} %shard_map.160.refs_0_), channel_id=1, source_target_pairs={{0,1},{1,0},{2,3},{3,2},{4,5},{5,4},{6,7},{7,6},{8,9},{9,8},{10,11... | collective-permute-start | bytes 786440 | tf_op jit(solution)/shard_map/ppermute | solution.py:276
  153.9 12.2 %collective-permute-start.30 = (bf16[1024,128]{1,0:T(8,128)(2,1)}, bf16[1024,128]{1,0:T(8,128)(2,1)}, u32[]{:S(2)}, u32[]{:S(2)}) collective-permute-start(bf16[1024,128]{1,0:T(8,128)(2,1)} %shard_map.160.refs_0_), channel_id=1, source_target_pairs={{1,2},{2,1},{5,6},{6,5},{9,10},{10,9},{13,14},{14,13},{17,18},{18,... | collective-permute-start | bytes 786440 | tf_op jit(solution)/shard_map/ppermute | solution.py:276
  155.3 13.6 %collective-permute-start.31 = (bf16[1024,128]{1,0:T(8,128)(2,1)}, bf16[1024,128]{1,0:T(8,128)(2,1)}, u32[]{:S(2)}, u32[]{:S(2)}) collective-permute-start(bf16[1024,128]{1,0:T(8,128)(2,1)} %collective-permute-done.29.refs_2_), channel_id=1, source_target_pairs={{1,0},{2,3},{5,4},{6,7},{9,8},{10,11},{13,12},{14,15},{17,16},{18,... | collective-permute-start | bytes 786440 | tf_op jit(solution)/shard_map/ppermute | solution.py:276
  158.1 13.1 %collective-permute-start.38 = (bf16[256,448]{1,0:T(8,128)(2,1)S(1)}, bf16[256,448]{1,0:T(8,128)(2,1)S(1)}, u32[]{:S(2)}, u32[]{:S(2)}) collective-permute-start(bf16[256,448]{1,0:T(8,128)(2,1)S(1)} %select_convert_fusion), channel_id=1, source_target_pairs={{0,4},{4,0},{8,12},{12,8},{16,20},{20,16},{24,28},{28,24},{1,5},{5... | collective-permute-start | bytes 688136 | tf_op jit(solution)/shard_map/ppermute | solution.py:300
  (23 other events, 293.0 us)

commit v5 on v4

--- a/solution.py
+++ b/solution.py
@@ -13,6 +13,8 @@
 HEADS = 16
 ROWBLK = 128
 RUN_BLOCKS = 8
+VMEM_BYTES = 58 * 1024 * 1024
+NO_COST = pl.CostEstimate(flops=0, bytes_accessed=0, transcendentals=0)
 
 
 rope_base = 1000000.0
@@ -85,6 +87,7 @@
     run_ref,
     slot_ref,
     need_ref,
+    odd_ref,
     query_ref,
     up_ref,
     cos_ref,
@@ -169,7 +172,9 @@
             for item in range(wide):
                 at = (group * wide + item) * HD
                 part = slice(item * ROWBLK, (item + 1) * ROWBLK)
-                out_ref[pl.ds(at, HD), pl.ds(base, ROWBLK)] = out_b[:, part]
+                head = group * wide + item
+                half, row = head * 2 // heads, head % (heads // 2) * HD
+                out_ref[half ^ odd_ref[0], pl.ds(row, HD), pl.ds(base, ROWBLK)] = out_b[:, part]
                 grad = gquery_t[:, part].T * scale
                 back = grad * cosine - pltpu.roll(grad, HD // 2, 1) * sine
                 gquery_ref[pl.ds(base, ROWBLK), pl.ds(at, HD)] = back.astype(jnp.bfloat16)
@@ -214,27 +219,24 @@
     smem = pl.BlockSpec(memory_space=pltpu.SMEM)
     vmem = pl.BlockSpec(memory_space=pltpu.VMEM)
     hbm = pl.BlockSpec(memory_space=pl.ANY)
-    pairs = rows * RUN_BLOCKS * ROWBLK * heads
     half = jax.ShapeDtypeStruct((every // 2, HD), jnp.bfloat16)
     return pl.pallas_call(
         partial(attend_kernel, heads, ranks),
         out_shape=(
             jax.ShapeDtypeStruct((rows, width), jnp.bfloat16),
-            jax.ShapeDtypeStruct((width, rows), jnp.bfloat16),
+            jax.ShapeDtypeStruct((2, width // 2, rows), jnp.bfloat16),
             half,
             half,
             half,
             half,
         ),
-        in_specs=[smem] * 5 + [vmem] * 5 + [hbm] * (2 * ranks),
+        in_specs=[smem] * 6 + [vmem] * 5 + [hbm] * (2 * ranks),
         out_specs=(vmem, vmem, hbm, hbm, hbm, hbm),
         scratch_shapes=[pltpu.VMEM((every, HD), jnp.bfloat16)] * 4
         + [pltpu.VMEM((RUN_BLOCKS * ROWBLK, HD), jnp.bfloat16)] * 2
         + [pltpu.SemaphoreType.DMA((2, ranks))],
-        compiler_params=pltpu.CompilerParams(vmem_limit_bytes=48 * 1024 * 1024),
-        cost_estimate=pl.CostEstimate(
-            flops=10 * pairs * HD, bytes_accessed=16 * 1024 * 1024, transcendentals=pairs
-        ),
+        compiler_params=pltpu.CompilerParams(vmem_limit_bytes=VMEM_BYTES),
+        cost_estimate=NO_COST,
     )(*tables, query, up, cosine, sine, places, *keys, *values)
 
 
@@ -263,9 +265,8 @@
         in_specs=[smem, smem] + [vmem] * len(pieces),
         out_specs=pl.BlockSpec(memory_space=pl.ANY),
         scratch_shapes=[pltpu.SemaphoreType.DMA((len(pieces),))],
-        cost_estimate=pl.CostEstimate(
-            flops=0, bytes_accessed=4 * rows * lanes * HD, transcendentals=0
-        ),
+        compiler_params=pltpu.CompilerParams(vmem_limit_bytes=VMEM_BYTES),
+        cost_estimate=NO_COST,
     )(columns, active, *pieces)
 
 
@@ -337,28 +338,50 @@
     out_ref[...] = total.astype(out_ref.dtype)
 
 
-def final_sum(keep, received, tables, after):
+def final_sum(keep, received, tables, after, kind=jnp.bfloat16):
     vmem = pl.BlockSpec(memory_space=pltpu.VMEM)
     hbm = pl.BlockSpec(memory_space=pl.ANY)
     parts = [keep, *received, *tables]
     return pl.pallas_call(
         partial(final_kernel, len(received), len(tables) > 0),
-        out_shape=jax.ShapeDtypeStruct(keep.shape, jnp.bfloat16),
+        out_shape=jax.ShapeDtypeStruct(keep.shape, kind),
         in_specs=[vmem] * len(parts) + [hbm] * len(after),
         out_specs=vmem,
-        cost_estimate=pl.CostEstimate(
-            flops=8 * keep.size, bytes_accessed=12 * keep.size, transcendentals=0
-        ),
+        compiler_params=pltpu.CompilerParams(vmem_limit_bytes=VMEM_BYTES),
+        cost_estimate=NO_COST,
     )(*parts, *after)
 
 
-def product_kernel(my_ref, left_ref, right_ref, *refs):
-    total = jnp.dot(left_ref[...], right_ref[...], preferred_element_type=jnp.float32)
-    refs[-1][0] = total.astype(refs[-1].dtype)
+def up_kernel(rows_ref, weight_ref, *refs):
+    total = jnp.dot(rows_ref[...], weight_ref[...], preferred_element_type=jnp.float32)
+    refs[-1][...] = total.astype(refs[-1].dtype)
+
+
+def up_product(rows, weight, after):
+    height, depth = rows.shape
+    steps = 4
+    return pl.pallas_call(
+        up_kernel,
+        grid=(steps,),
+        out_shape=jax.ShapeDtypeStruct((height, weight.shape[1]), jnp.bfloat16),
+        in_specs=[
+            pl.BlockSpec((height // steps, depth), lambda step: (step, 0)),
+            pl.BlockSpec(weight.shape, lambda step: (0, 0)),
+        ]
+        + [pl.BlockSpec(memory_space=pl.ANY)] * len(after),
+        out_specs=pl.BlockSpec((height // steps, weight.shape[1]), lambda step: (step, 0)),
+        compiler_params=pltpu.CompilerParams(vmem_limit_bytes=VMEM_BYTES),
+        cost_estimate=NO_COST,
+    )(rows, weight, *after)
+
+
+def product_kernel(my_ref, left_ref, right_ref, thru_ref, out_ref, unused):
+    total = jnp.dot(left_ref[0], right_ref[...], preferred_element_type=jnp.float32)
+    out_ref[0] = total.astype(out_ref.dtype)
 
 
 def product_sum_kernel(count, my_ref, left_ref, right_ref, base_ref, *refs):
-    total = jnp.dot(left_ref[...], right_ref[...], preferred_element_type=jnp.float32)
+    total = jnp.dot(left_ref[0], right_ref[...], preferred_element_type=jnp.float32)
     total = total + base_ref[0].astype(jnp.float32)
     for at, out_ref in enumerate(refs[-count:]):
 
@@ -367,51 +390,64 @@
             out_ref[...] = total.astype(out_ref.dtype)
 
 
-def product(mine, left, right, base, after):
+def product_specs(left, which, right):
     count = lax.axis_size("dp") // 2
-    rows = left.shape[0]
-    cols = right.shape[1] // count
+    rows, cols = left.shape[1], right.shape[1] // count
+    stacked = pl.BlockSpec((1, rows, cols), lambda step, my_ref: (step, 0, 0))
+    ins = [
+        pl.BlockSpec((1,) + left.shape[1:], lambda step, my_ref: (which, 0, 0)),
+        pl.BlockSpec((right.shape[0], cols), lambda step, my_ref: (0, step ^ my_ref[0])),
+    ]
+    return count, rows, cols, stacked, ins
+
+
+def plain_pieces(mine, left, right):
+    count = lax.axis_size("dp") // 2
+    total = jnp.dot(left, right, preferred_element_type=jnp.float32)
+    pieces = jnp.moveaxis(total.reshape(left.shape[0], count, -1), 1, 0)
+    return jnp.take(pieces, jnp.arange(count, dtype=jnp.int32) ^ mine, axis=0)
+
+
+def product(mine, left, right, thru):
+    count, rows, cols, stacked, ins = product_specs(left, 1, right)
     if cols % 128:
-        total = jnp.dot(left, right, preferred_element_type=jnp.float32)
-        pieces = jnp.moveaxis(total.reshape(rows, count, cols), 1, 0)
-        pieces = jnp.take(pieces, jnp.arange(count, dtype=jnp.int32) ^ mine, axis=0)
-        if base is None:
-            return pieces.astype(jnp.bfloat16)
-        pieces = pieces + base.astype(jnp.float32)
+        return plain_pieces(mine, left[1], right).astype(jnp.bfloat16), thru
+    hbm = pl.BlockSpec(memory_space=pl.ANY)
+    return pl.pallas_call(
+        product_kernel,
+        grid_spec=pltpu.PrefetchScalarGridSpec(
+            num_scalar_prefetch=1, grid=(count,), in_specs=ins + [hbm], out_specs=[stacked, hbm]
+        ),
+        out_shape=[
+            jax.ShapeDtypeStruct((count, rows, cols), jnp.bfloat16),
+            jax.ShapeDtypeStruct(thru.shape, thru.dtype),
+        ],
+        input_output_aliases={3: 1},
+        compiler_params=pltpu.CompilerParams(vmem_limit_bytes=VMEM_BYTES),
+        cost_estimate=NO_COST,
+    )(mine.reshape(1), left, right, thru)
+
+
+def product_sum(mine, left, right, base, after):
+    count, rows, cols, stacked, ins = product_specs(left, 0, right)
+    if cols % 128:
+        pieces = plain_pieces(mine, left[0], right) + base.astype(jnp.float32)
         return [pieces[0]] + [pieces[at].astype(jnp.bfloat16) for at in range(1, count)]
-    stacked = pl.BlockSpec((1, rows, cols), lambda step, my_ref: (step, 0, 0))
-    if base is None:
-        body = product_kernel
-        bases = []
-        out_specs = stacked
-        out_shape = jax.ShapeDtypeStruct((count, rows, cols), jnp.bfloat16)
-    else:
-        body = partial(product_sum_kernel, count)
-        bases = [base]
-        out_specs = [pl.BlockSpec((rows, cols), lambda step, my_ref: (0, 0))] * count
-        out_shape = [
-            jax.ShapeDtypeStruct((rows, cols), jnp.bfloat16 if at else jnp.float32)
-            for at in range(count)
-        ]
     return pl.pallas_call(
-        body,
+        partial(product_sum_kernel, count),
         grid_spec=pltpu.PrefetchScalarGridSpec(
             num_scalar_prefetch=1,
             grid=(count,),
-            in_specs=[
-                pl.BlockSpec(left.shape, lambda step, my_ref: (0, 0)),
-                pl.BlockSpec((right.shape[0], cols), lambda step, my_ref: (0, step ^ my_ref[0])),
-            ]
-            + [stacked] * len(bases)
-            + [pl.BlockSpec(memory_space=pl.ANY)] * len(after),
-            out_specs=out_specs,
+            in_specs=ins + [stacked] + [pl.BlockSpec(memory_space=pl.ANY)] * len(after),
+            out_specs=[pl.BlockSpec((rows, cols), lambda step, my_ref: (0, 0))] * count,
         ),
-        out_shape=out_shape,
-        compiler_params=pltpu.CompilerParams(vmem_limit_bytes=32 * 1024 * 1024),
-        cost_estimate=pl.CostEstimate(
-            flops=2 * rows * right.size, bytes_accessed=2 * right.size, transcendentals=0
-        ),
-    )(mine.reshape(1), left, right, *bases, *after)
+        out_shape=[
+            jax.ShapeDtypeStruct((rows, cols), jnp.bfloat16 if at else jnp.float32)
+            for at in range(count)
+        ],
+        compiler_params=pltpu.CompilerParams(vmem_limit_bytes=VMEM_BYTES),
+        cost_estimate=NO_COST,
+    )(mine.reshape(1), left, right, base, *after)
 
 
 def local(query, key, value, grad_out, out_weight, plan, segments):
@@ -428,12 +464,14 @@
     own_value = lax.dynamic_slice_in_dim(value, kv_head * HD, HD, 1)
 
     own_places = positions_of(segments).reshape(1, block_count, ROWBLK)
-    pair_places = jnp.concatenate([own_places, swap(own_places, 1)], axis=0)
-    places_all = jnp.concatenate(
-        [pair_places] + [swap(pair_places, step) for step in range(2, rank_count, 2)], axis=0
+    places_all = lax.all_to_all(
+        jnp.broadcast_to(own_places, (rank_count, block_count, ROWBLK)),
+        "dp",
+        split_axis=0,
+        concat_axis=0,
+        tiled=True,
     ).reshape(-1, ROWBLK)
     values = spread(own_value)
-    up = jnp.dot(grad_out, out_weight, preferred_element_type=jnp.float32).astype(jnp.bfloat16)
 
     mine = my_rank * block_count + jnp.arange(block_count, dtype=jnp.int32)
     hit = plan[None, :] == mine[:, None]
@@ -442,12 +480,13 @@
     )
     run = dest // RUN_BLOCKS
     slot = dest % RUN_BLOCKS
-    places = jnp.take(places_all, (run ^ my_rank) * RUN_BLOCKS + slot, axis=0)
+    places = jnp.take(places_all, dest, axis=0)
     need = slot - (slot * ROWBLK - places[:, 0]) // ROWBLK + 1
     cosine, sine = rope_tables(places.reshape(row_count), HD)
     key_f = own_key.astype(jnp.float32)
     rot_key = (key_f * cosine + swap_halves(key_f) * sine).astype(jnp.bfloat16)
     keys = spread(rot_key)
+    up = up_product(grad_out, out_weight, [rot_key])
 
     distance = (plan // block_count) ^ my_rank
     within = plan % block_count
@@ -458,32 +497,29 @@
         run,
         slot,
         need,
+        (my_rank & 1).reshape(1),
     )
     grad_query, attn_t, gkey_keep, gkey_send, gvalue_keep, gvalue_send = attend(
         tables, query, up, cosine, sine, places, keys, values
     )
+    mine_pair = my_rank // 2
     value_keep, value_sends = chip_sum(gvalue_keep, gvalue_send)
     value_received = exchange(value_sends)
+    first, gkey_keep = product(mine_pair, attn_t, grad_out, gkey_keep)
+    first = swap(first, 1)
     key_keep, key_sends = chip_sum(gkey_keep, gkey_send)
     key_received = exchange(key_sends)
-
-    width = attn_t.shape[0]
+    value_partial = final_sum(value_keep, value_received, (), key_sends)
+    value_all, value_pieces = lane_gather(value_partial, my_lane)
+    kept, *sends = product_sum(mine_pair, attn_t, grad_out, first, [value_partial])
+    received = exchange(sends)
+    key_partial = final_sum(
+        key_keep, key_received, (cosine, sine), [sends[0], value_pieces[0], value_pieces[2]]
+    )
+    key_all, key_pieces = lane_gather(key_partial, my_lane)
+    total = final_sum(kept, received, (), key_pieces[:3] + value_pieces[3:], jnp.float32)
     odd = my_rank & 1
-    halves = attn_t.reshape(2, width // 2, row_count)
     pair_rows = grad_out.shape[1] // (rank_count // 2)
-
-    def half_of(which):
-        return lax.dynamic_index_in_dim(halves, which, 0, keepdims=False)
-
-    first = swap(product(my_rank // 2, half_of(1 - odd), grad_out, None, key_sends), 1)
-    value_partial = final_sum(value_keep, value_received, (), ())
-    value_all, value_pieces = lane_gather(value_partial, my_lane)
-    kept, *sends = product(my_rank // 2, half_of(odd), grad_out, first, [value_partial])
-    key_partial = final_sum(key_keep, key_received, (cosine, sine), [sends[0], value_pieces[0]])
-    key_all, key_pieces = lane_gather(key_partial, my_lane)
-    total = kept
-    for item in exchange(sends):
-        total = total + item.astype(jnp.float32)
     low, high = total[:, : pair_rows // 2], total[:, pair_rows // 2 :]
     is_odd = odd > 0
     other = swap(jnp.where(is_odd, low, high).astype(jnp.bfloat16), 1).astype(jnp.float32)

time: 173 us -> 159 us (0.919)
  Pallas kernels: 37 us -> 58.5 us
  waiting for transfers between devices: 56.7 us -> 41.8 us
  matrix products: 9.04 us -> 0 us
  starting transfers between devices: 44.1 us -> 36.1 us
  local copies, waits for them, and re-layouts: 11.9 us -> 7.6 us
    pallas_call x2 -> x3, Pallas kernels: 9.1 us -> 22.2 us  [the longest x1 8.38 us: up_product(): pl.pallas_call(up_kernel, grid=(steps,), out_shape=jax.ShapeDtypeStruct((...]
    ppermute x31 -> x27, starting transfers between devices: 31 us -> 18.3 us  [swap(): lax.ppermute(array, 'dp', [(rank, rank ^ bit) for rank in range(ranks)])]
    ppermute x8, waiting for transfers between devices: 25 us -> 14.8 us  [send(): return lax.ppermute(item, 'tensor', pairs)]
    ppermute x31 -> x27, waiting for transfers between devices: 31.7 us -> 22.3 us  [swap(): lax.ppermute(array, 'dp', [(rank, rank ^ bit) for rank in range(ranks)])]
    dot_general x1 -> x0, matrix products: 9.04 us -> none  [local(): jnp.dot(grad_out, out_weight, preferred_element_type=jnp.float32)]
    pallas_call x1, Pallas kernels: 18.7 us -> 24.4 us  [attend(): pl.pallas_call(partial(attend_kernel, heads, ranks), out_shape=(jax.Shape...]
    all_to_all x0 -> x1, waiting for transfers between devices: none -> 4.66 us  [local(): lax.all_to_all(jnp.broadcast_to(own_places, (rank_count, block_count, ROW...]
    all_to_all x0 -> x1, starting transfers between devices: none -> 4.26 us  [local(): lax.all_to_all(jnp.broadcast_to(own_places, (rank_count, block_count, ROW...]
  transfers between devices with their start and end apart: 39 -> 36, of which waited for: 18 -> 10; matrix products, arithmetic and copies ran while one was open for 13% -> 10% of each run, Pallas kernels for 8% -> 21%
where the time goes in v5:
time: 159 us
  Pallas kernels  58.5 us (37%)
  waiting for transfers between devices  41.8 us (26%)
  starting transfers between devices  36.1 us (23%)
  other arithmetic  14.3 us (9%)
  local copies, waits for them, and re-layouts  7.6 us (5%)
    pallas_call x1, Pallas kernels, attend(): pl.pallas_call(partial(attend_kernel, heads, ranks), out_shape=(jax.Shape...  24.4 us
    ppermute x27, waiting for transfers between devices, swap(): lax.ppermute(array, 'dp', [(rank, rank ^ bit) for rank in range(ranks)])  22.3 us
    ppermute x27, starting transfers between devices, swap(): lax.ppermute(array, 'dp', [(rank, rank ^ bit) for rank in range(ranks)])  18.3 us
    ppermute x8, waiting for transfers between devices, send(): return lax.ppermute(item, 'tensor', pairs)  14.8 us
    ppermute x8, starting transfers between devices, send(): return lax.ppermute(item, 'tensor', pairs)  13.5 us
    pallas_call x1, Pallas kernels, up_product(): pl.pallas_call(up_kernel, grid=(steps,), out_shape=jax.ShapeDtypeStruct((...  8.38 us
    pallas_call x3, Pallas kernels, final_sum(): pl.pallas_call(partial(final_kernel, len(received), len(tables) > 0), out...  7.37 us
    pallas_call x1, Pallas kernels, product_sum(): pl.pallas_call(partial(product_sum_kernel, count), grid_spec=pltpu.Prefet...  7.24 us
  transfers between devices with their start and end apart: 36, of which 10 were waited for; matrix products, arithmetic and copies ran while one was open for 10% of the time, Pallas kernels for 21%

profile of v5, /device:TPU:0, one launch (start us, length us, event | category | flops | bytes accessed | tf_op | source)
XLA Modules:
  0.0 159.5 jit_solution(16996927825376616457)
XLA Ops:
  1.9 3.0 %collective-permute-start.10 = (bf16[1024,128]{1,0:T(8,128)(2,1)S(1)}, bf16[1024,128]{1,0:T(8,128)(2,1)S(1)}, u32[]{:S(2)}, u32[]{:S(2)}) collective-permute-start(bf16[1024,128]{1,0:T(8,128)(2,1)S(1)} %constant_dynamic-slice_fusion.refs_8_), channel_id=1, source_target_pairs={{0,16},{4,20},{8,24},{12,28},{16,0},{20,4},{24,8},{28,12},{1,17},{... | collective-permute-start | bytes 786440 | tf_op jit(solution)/shard_map/ppermute | solution.py:301
  4.9 1.4 collective-permute-start.12
  8.6 4.3 %all-to-all-start = ((s32[8,8,128]{2,1,0:T(8,128)}), s32[8,8,128]{2,1,0:T(8,128)S(1)}, u32[]{:S(2)}, u32[]{:S(2)}) async-start(s32[8,8,128]{2,1,0:T(8,128)} %broadcast_in_dim.40), calls=%async_computation | async-start | bytes 65536 | tf_op jit(solution)/shard_map/all_to_all | solution.py:467
  15.0 4.7 %all-to-all-done = s32[8,8,128]{2,1,0:T(8,128)S(1)} async-done(((s32[8,8,128]{2,1,0:T(8,128)}), s32[8,8,128]{2,1,0:T(8,128)S(1)}, u32[]{:S(2)}, u32[]{:S(2)}) %all-to-all-start) | async-done | bytes 32800 | tf_op jit(solution)/shard_map/all_to_all | solution.py:467
  20.3 1.9 %fusion.5 = (f32[1024,64]{1,0:T(8,128)S(1)}, f32[1024,64]{1,0:T(8,128)S(1)}, f32[1024,64]{1,0:T(8,128)S(1)}) fusion(f32[64]{0:T(128)S(1)} %multiply_add_fusion.1, f32[1024]{0:T(1024)S(1)} %get-tuple-element.42), kind=kLoop, calls=%fused_computation.25 | loop fusion | flops 262144 | bytes 790784 | tf_op jit(solution)/shard_map/neg | solution.py:69
  22.2 2.4 %fusion.4 = (bf16[1024,128]{1,0:T(8,128)(2,1)S(1)}, f32[1024,128]{1,0:T(8,128)}, f32[1024,128]{1,0:T(8,128)}) fusion(f32[1024,64]{1,0:T(8,128)S(1)} %get-tuple-element.61, f32[1024,64]{1,0:T(8,128)S(1)} %get-tuple-element.60, bf16[1024,512]{1,0:T(8,128)(2,1)} %param.14, s32[]{:T(128)S(6)} %select_n.100, f32[1024,64]{1,0:T(8,128)S(1)} %get-tuple-element.64, ...), kind=kLoop, calls=%fused_computation.12 | loop fusion | flops 1048576 | bytes 2883588 | tf_op jit(solution)/shard_map/convert_element_type | solution.py:487
  24.6 1.4 collective-permute-start.1
  26.7 1.4 collective-permute-start.5
  29.7 4.1 %collective-permute-done.1.refs_2_ = bf16[1024,128]{1,0:T(8,128)(2,1)S(1)} collective-permute-done((bf16[1024,128]{1,0:T(8,128)(2,1)S(1)}, bf16[1024,128]{1,0:T(8,128)(2,1)S(1)}, u32[]{:S(2)}, u32[]{:S(2)}) %collective-permute-start.1) | collective-permute-done | bytes 262176 | tf_op jit(solution)/shard_map/ppermute | solution.py:301
  33.8 5.5 %collective-permute-done.3.refs_4_ = bf16[1024,128]{1,0:T(8,128)(2,1)S(1)} collective-permute-done((bf16[1024,128]{1,0:T(8,128)(2,1)S(1)}, bf16[1024,128]{1,0:T(8,128)(2,1)S(1)}, u32[]{:S(2)}, u32[]{:S(2)}) %collective-permute-start.3) | collective-permute-done | bytes 262176 | tf_op jit(solution)/shard_map/ppermute | solution.py:301
  40.5 8.4 %shard_map.156.up_ref = bf16[1024,512]{1,0:T(8,128)(2,1)} custom-call(bf16[1024,3584]{1,0:T(8,128)(2,1)} %right_ref.3, bf16[3584,512]{1,0:T(8,128)(2,1)} %weight_ref.1, bf16[1024,128]{1,0:T(8,128)(2,1)} %copy-done.3), custom_call_target="tpu_custom_call" | custom-call | tf_op jit(solution)/shard_map/pallas_call | solution.py:363
  50.7 24.4 %shard_map.157 = (bf16[1024,512]{1,0:T(8,128)(2,1)}, bf16[2,256,1024]{2,1,0:T(8,128)(2,1)}, bf16[4096,128]{1,0:T(8,128)(2,1)}, bf16[4096,128]{1,0:T(8,128)(2,1)}...) custom-call(s32[64]{0:T(128)} %multiply_add_fusion.3.target_ref, s32[64]{0:T(128)} %get-tuple-element.46.source_ref, ...), custom_call_target="tpu_custom_call" | custom-call | tf_op jit(solution)/shard_map/pallas_call | solution.py:223
  75.2 6.5 %shard_map.158 = (bf16[4,256,896]{2,1,0:T(8,128)(2,1)}, bf16[4096,128]{1,0:T(8,128)(2,1)}) custom-call(s32[1]{0:T(128)} %bitcast.6.my_ref, bf16[2,256,1024]{2,1,0:T(8,128)(2,1)} %get-tuple-element.17.left_ref, bf16[1024,3584]{1,0:T(8,128)(2,1)} %right_ref.3, bf16[4096,128]{1,0:T(8,128)(2,1)} %get-tuple-element.18.thru_ref), custom_call_target="tpu_custom_call", output_to_operand_aliasing={{1}: (3, {})} | custom-call | tf_op jit(solution)/shard_map/pallas_call | solution.py:416
  83.3 1.6 %collective-permute-start.21 = (bf16[1024,128]{1,0:T(8,128)(2,1)S(1)}, bf16[1024,128]{1,0:T(8,128)(2,1)S(1)}, u32[]{:S(2)}, u32[]{:S(2)}) collective-permute-start(bf16[1024,128]{1,0:T(8,128)(2,1)S(1)} %get-tuple-element.50), channel_id=1, source_target_pairs={{0,16},{4,20},{8,24},{12,28},{16,0},{20,4},{24,8},{28,12},{1,17},{... | collective-permute-start | bytes 786440 | tf_op jit(solution)/shard_map/ppermute | solution.py:301
  84.9 1.9 %collective-permute-start.22 = (bf16[1024,128]{1,0:T(8,128)(2,1)S(1)}, bf16[1024,128]{1,0:T(8,128)(2,1)S(1)}, u32[]{:S(2)}, u32[]{:S(2)}) collective-permute-start(bf16[1024,128]{1,0:T(8,128)(2,1)S(1)} %get-tuple-element.49), channel_id=1, source_target_pairs={{0,24},{4,28},{8,16},{12,20},{16,8},{20,12},{24,0},{28,4},{1,25},{... | collective-permute-start | bytes 786440 | tf_op jit(solution)/shard_map/ppermute | solution.py:301
  88.1 4.3 %collective-permute-done.20.refs_1_ = bf16[1024,128]{1,0:T(8,128)(2,1)S(1)} collective-permute-done((bf16[1024,128]{1,0:T(8,128)(2,1)S(1)}, bf16[1024,128]{1,0:T(8,128)(2,1)S(1)}, u32[]{:S(2)}, u32[]{:S(2)}) %collective-permute-start.20) | collective-permute-done | bytes 262176 | tf_op jit(solution)/shard_map/ppermute | solution.py:301
  92.4 5.6 %collective-permute-done.21.refs_2_ = bf16[1024,128]{1,0:T(8,128)(2,1)S(1)} collective-permute-done((bf16[1024,128]{1,0:T(8,128)(2,1)S(1)}, bf16[1024,128]{1,0:T(8,128)(2,1)S(1)}, u32[]{:S(2)}, u32[]{:S(2)}) %collective-permute-start.21) | collective-permute-done | bytes 262176 | tf_op jit(solution)/shard_map/ppermute | solution.py:301
  98.8 2.1 %shard_map.159.refs_0_ = bf16[1024,128]{1,0:T(8,128)(2,1)} custom-call(f32[1024,128]{1,0:T(8,128)} %get-tuple-element.52.refs_0_, bf16[1024,128]{1,0:T(8,128)(2,1)} %copy-done.34, bf16[1024,128]{1,0:T(8,128)(2,1)} %copy-done.35, bf16[1024,128]{1,0:T(8,128)(2,1)} %copy-done.36, bf16[1024,128]{1,0:T(8,128)(2,1)} %copy-done.14, bf16[1024,128]{1,0:T(8,128)(2,1)} %copy-done.13, ...), custom_call_target="tpu_custom_call" | custom-call | tf_op jit(solution)/shard_map/pallas_call | solution.py:345
  100.9 2.6 %collective-permute-start.29 = (bf16[1024,128]{1,0:T(8,128)(2,1)}, bf16[1024,128]{1,0:T(8,128)(2,1)S(1)}, u32[]{:S(2)}, u32[]{:S(2)}) collective-permute-start(bf16[1024,128]{1,0:T(8,128)(2,1)} %shard_map.159.refs_0_), channel_id=1, source_target_pairs={{0,2},{2,0},{1,3},{3,1},{4,6},{6,4},{5,7},{7,5},{8,10},{10,8},{9,1... | collective-permute-start | bytes 786440 | tf_op jit(solution)/shard_map/ppermute | solution.py:277
  104.6 1.6 collective-permute-start.23
  107.5 7.2 %shard_map.160 = (f32[256,896]{1,0:T(8,128)}, bf16[256,896]{1,0:T(8,128)(2,1)}, bf16[256,896]{1,0:T(8,128)(2,1)}, bf16[256,896]{1,0:T(8,128)(2,1)}) custom-call(s32[1]{0:T(128)} %bitcast.6.my_ref, bf16[2,256,1024]{2,1,0:T(8,128)(2,1)} %get-tuple-element.17.left_ref, bf16[1024,3584]{1,0:T(8,128)(2,1)} %right_ref.3, bf16[4,256,896]{2,1,0:T(8,128)(2,1)} %copy-done.4, ...), custom_call_target="tpu_custom_call" | custom-call | tf_op jit(solution)/shard_map/pallas_call | solution.py:436
  114.7 1.5 collective-permute-done.29.refs_2_
  118.5 2.5 %shard_map.161.refs_0_ = bf16[1024,128]{1,0:T(8,128)(2,1)} custom-call(f32[1024,128]{1,0:T(8,128)} %get-tuple-element.56.refs_0_, bf16[1024,128]{1,0:T(8,128)(2,1)} %copy-done.26, bf16[1024,128]{1,0:T(8,128)(2,1)} %copy-done.28, bf16[1024,128]{1,0:T(8,128)(2,1)} %copy-done.33, f32[1024,128]{1,0:T(8,128)} %get-tuple-element.59.cos_ref.refs_4_, ...), custom_call_target="tpu_custom_call" | custom-call | tf_op jit(solution)/shard_map/pallas_call | solution.py:345
  121.0 3.7 %collective-permute-start.25 = (bf16[1024,128]{1,0:T(8,128)(2,1)}, bf16[1024,128]{1,0:T(8,128)(2,1)S(1)}, u32[]{:S(2)}, u32[]{:S(2)}) collective-permute-start(bf16[1024,128]{1,0:T(8,128)(2,1)} %shard_map.161.refs_0_), channel_id=1, source_target_pairs={{0,1},{1,0},{2,3},{3,2},{4,5},{5,4},{6,7},{7,6},{8,9},{9,8},{10,11... | collective-permute-start | bytes 786440 | tf_op jit(solution)/shard_map/ppermute | solution.py:277
  126.6 1.5 collective-permute-start.33
  128.2 1.8 %collective-permute-start.26 = (bf16[1024,128]{1,0:T(8,128)(2,1)}, bf16[1024,128]{1,0:T(8,128)(2,1)S(1)}, u32[]{:S(2)}, u32[]{:S(2)}) collective-permute-start(bf16[1024,128]{1,0:T(8,128)(2,1)} %shard_map.161.refs_0_), channel_id=1, source_target_pairs={{0,2},{2,0},{1,3},{3,1},{4,6},{6,4},{5,7},{7,5},{8,10},{10,8},{9,1... | collective-permute-start | bytes 786440 | tf_op jit(solution)/shard_map/ppermute | solution.py:277
  130.0 4.5 %collective-permute-done.25.refs_1_.refs_4_ = bf16[1024,128]{1,0:T(8,128)(2,1)S(1)} collective-permute-done((bf16[1024,128]{1,0:T(8,128)(2,1)}, bf16[1024,128]{1,0:T(8,128)(2,1)S(1)}, u32[]{:S(2)}, u32[]{:S(2)}) %collective-permute-start.25) | collective-permute-done | bytes 262176 | tf_op jit(solution)/shard_map/ppermute | solution.py:277
  135.2 8.7 %collective-permute-done.26.refs_2_.refs_5_ = bf16[1024,128]{1,0:T(8,128)(2,1)S(1)} collective-permute-done((bf16[1024,128]{1,0:T(8,128)(2,1)}, bf16[1024,128]{1,0:T(8,128)(2,1)S(1)}, u32[]{:S(2)}, u32[]{:S(2)}) %collective-permute-start.26) | collective-permute-done | bytes 262176 | tf_op jit(solution)/shard_map/ppermute | solution.py:277
  145.3 2.6 %collective-permute-done.33.refs_3_ = bf16[256,896]{1,0:T(8,128)(2,1)} collective-permute-done((bf16[256,896]{1,0:T(8,128)(2,1)}, bf16[256,896]{1,0:T(8,128)(2,1)}, u32[]{:S(2)}, u32[]{:S(2)}) %collective-permute-start.33) | collective-permute-done | bytes 458784 | tf_op jit(solution)/shard_map/ppermute | solution.py:301
  147.9 2.7 %shard_map.164 = f32[256,896]{1,0:T(8,128)} custom-call(f32[256,896]{1,0:T(8,128)} %get-tuple-element.25.refs_0_, bf16[256,896]{1,0:T(8,128)(2,1)} %copy-done.15, bf16[256,896]{1,0:T(8,128)(2,1)} %copy-done.16, bf16[256,896]{1,0:T(8,128)(2,1)} %collective-permute-done.33.refs_3_, bf16[1024,128]{1,0:T(8,128)(2,1)} %copy-done.8, bf16[1024,128]{1,0:T(8,128)(2,1)} %copy-done.9, ...), custom_call_target="tpu_custom_call" | custom-call | tf_op jit(solution)/shard_map/pallas_call | solution.py:345
  153.3 2.3 %shard_map.163 = bf16[1024,512]{1,0:T(8,128)(2,1)} custom-call(s32[5]{0:T(128)} %broadcast_xor_fusion.column_ref, s32[5]{0:T(128)} %or_convert_fusion.active_ref, bf16[1024,128]{1,0:T(8,128)(2,1)} %shard_map.159.refs_0_, bf16[1024,128]{1,0:T(8,128)(2,1)} %copy-done.5, bf16[1024,128]{1,0:T(8,128)(2,1)} %copy-done.20, bf16[1024,128]{1,0:T(8,128)(2,1)} %copy-done.6, ...), custom_call_target="tpu_custom_call" | custom-call | tf_op jit(solution)/shard_map/pallas_call | solution.py:262
  155.6 2.3 %shard_map.162 = bf16[1024,512]{1,0:T(8,128)(2,1)} custom-call(s32[5]{0:T(128)} %broadcast_xor_fusion.column_ref, s32[5]{0:T(128)} %or_convert_fusion.active_ref, bf16[1024,128]{1,0:T(8,128)(2,1)} %shard_map.161.refs_0_, bf16[1024,128]{1,0:T(8,128)(2,1)} %copy-done.8, bf16[1024,128]{1,0:T(8,128)(2,1)} %copy-done.9, bf16[1024,128]{1,0:T(8,128)(2,1)} %copy-done.10, ...), custom_call_target="tpu_custom_call" | custom-call | tf_op jit(solution)/shard_map/pallas_call | solution.py:262
  (170 shorter events, 27.7 us)
Async XLA Ops:
  1.9 24.2 %collective-permute-start.10 = (bf16[1024,128]{1,0:T(8,128)(2,1)S(1)}, bf16[1024,128]{1,0:T(8,128)(2,1)S(1)}, u32[]{:S(2)}, u32[]{:S(2)}) collective-permute-start(bf16[1024,128]{1,0:T(8,128)(2,1)S(1)} %constant_dynamic-slice_fusion.refs_8_), channel_id=1, source_target_pairs={{0,16},{4,20},{8,24},{12,28},{16,0},{20,4},{24,8},{28,12},{1,17},{... | collective-permute-start | bytes 786440 | tf_op jit(solution)/shard_map/ppermute | solution.py:301
  4.9 21.7 %collective-permute-start.12 = (bf16[1024,128]{1,0:T(8,128)(2,1)S(1)}, bf16[1024,128]{1,0:T(8,128)(2,1)S(1)}, u32[]{:S(2)}, u32[]{:S(2)}) collective-permute-start(bf16[1024,128]{1,0:T(8,128)(2,1)S(1)} %constant_dynamic-slice_fusion.refs_8_), channel_id=1, source_target_pairs={{0,24},{4,28},{8,16},{12,20},{16,8},{20,12},{24,0},{28,4},{1,25},{... | collective-permute-start | bytes 786440 | tf_op jit(solution)/shard_map/ppermute | solution.py:301
  6.4 21.8 %collective-permute-start.8 = (bf16[1024,128]{1,0:T(8,128)(2,1)S(1)}, bf16[1024,128]{1,0:T(8,128)(2,1)S(1)}, u32[]{:S(2)}, u32[]{:S(2)}) collective-permute-start(bf16[1024,128]{1,0:T(8,128)(2,1)S(1)} %constant_dynamic-slice_fusion.refs_8_), channel_id=1, source_target_pairs={{0,8},{4,12},{8,0},{12,4},{16,24},{20,28},{24,16},{28,20},{1,9},{5... | collective-permute-start | bytes 786440 | tf_op jit(solution)/shard_map/ppermute | solution.py:301
  6.5 21.7 %collective-permute-start.7 = (bf16[1024,128]{1,0:T(8,128)(2,1)S(1)}, bf16[1024,128]{1,0:T(8,128)(2,1)}, u32[]{:S(2)}, u32[]{:S(2)}) collective-permute-start(bf16[1024,128]{1,0:T(8,128)(2,1)S(1)} %constant_dynamic-slice_fusion.refs_8_), channel_id=1, source_target_pairs={{0,4},{4,0},{8,12},{12,8},{16,20},{20,16},{24,28},{28,24},{1,5},{5... | collective-permute-start | bytes 786440 | tf_op jit(solution)/shard_map/ppermute | solution.py:301
  8.6 11.0 %all-to-all-start = ((s32[8,8,128]{2,1,0:T(8,128)}), s32[8,8,128]{2,1,0:T(8,128)S(1)}, u32[]{:S(2)}, u32[]{:S(2)}) async-start(s32[8,8,128]{2,1,0:T(8,128)} %broadcast_in_dim.40), calls=%async_computation | async-start | bytes 65536 | tf_op jit(solution)/shard_map/all_to_all | solution.py:467
  24.6 9.2 %collective-permute-start.1 = (bf16[1024,128]{1,0:T(8,128)(2,1)S(1)}, bf16[1024,128]{1,0:T(8,128)(2,1)S(1)}, u32[]{:S(2)}, u32[]{:S(2)}) collective-permute-start(bf16[1024,128]{1,0:T(8,128)(2,1)S(1)} %get-tuple-element.40.refs_0_), channel_id=1, source_target_pairs={{0,8},{4,12},{8,0},{12,4},{16,24},{20,28},{24,16},{28,20},{1,9},{5... | collective-permute-start | bytes 786440 | tf_op jit(solution)/shard_map/ppermute | solution.py:301
  26.1 13.3 %collective-permute-start.3 = (bf16[1024,128]{1,0:T(8,128)(2,1)S(1)}, bf16[1024,128]{1,0:T(8,128)(2,1)S(1)}, u32[]{:S(2)}, u32[]{:S(2)}) collective-permute-start(bf16[1024,128]{1,0:T(8,128)(2,1)S(1)} %get-tuple-element.40.refs_0_), channel_id=1, source_target_pairs={{0,16},{4,20},{8,24},{12,28},{16,0},{20,4},{24,8},{28,12},{1,17},{... | collective-permute-start | bytes 786440 | tf_op jit(solution)/shard_map/ppermute | solution.py:301
  26.7 12.7 %collective-permute-start.5 = (bf16[1024,128]{1,0:T(8,128)(2,1)S(1)}, bf16[1024,128]{1,0:T(8,128)(2,1)S(1)}, u32[]{:S(2)}, u32[]{:S(2)}) collective-permute-start(bf16[1024,128]{1,0:T(8,128)(2,1)S(1)} %get-tuple-element.40.refs_0_), channel_id=1, source_target_pairs={{0,24},{4,28},{8,16},{12,20},{16,8},{20,12},{24,0},{28,4},{1,25},{... | collective-permute-start | bytes 786440 | tf_op jit(solution)/shard_map/ppermute | solution.py:301
  28.1 11.7 %collective-permute-start = (bf16[1024,128]{1,0:T(8,128)(2,1)S(1)}, bf16[1024,128]{1,0:T(8,128)(2,1)S(1)}, u32[]{:S(2)}, u32[]{:S(2)}) collective-permute-start(bf16[1024,128]{1,0:T(8,128)(2,1)S(1)} %get-tuple-element.40.refs_0_), channel_id=1, source_target_pairs={{0,4},{4,0},{8,12},{12,8},{16,20},{20,16},{24,28},{28,24},{1,5},{5... | collective-permute-start | bytes 786440 | tf_op jit(solution)/shard_map/ppermute | solution.py:301
  28.2 11.8 %collective-permute-start.11 = (bf16[1024,128]{1,0:T(8,128)(2,1)S(1)}, bf16[1024,128]{1,0:T(8,128)(2,1)S(1)}, u32[]{:S(2)}, u32[]{:S(2)}) collective-permute-start(bf16[1024,128]{1,0:T(8,128)(2,1)S(1)} %collective-permute-done.10.refs_12_), channel_id=1, source_target_pairs={{0,4},{4,0},{8,12},{12,8},{16,20},{20,16},{24,28},{28,24},{1,5},{5... | collective-permute-start | bytes 786440 | tf_op jit(solution)/shard_map/ppermute | solution.py:301
  33.8 15.7 %collective-permute-start.13 = (bf16[1024,128]{1,0:T(8,128)(2,1)S(1)}, bf16[1024,128]{1,0:T(8,128)(2,1)S(1)}, u32[]{:S(2)}, u32[]{:S(2)}) collective-permute-start(bf16[1024,128]{1,0:T(8,128)(2,1)S(1)} %collective-permute-done.12.refs_14_), channel_id=1, source_target_pairs={{0,4},{4,0},{8,12},{12,8},{16,20},{20,16},{24,28},{28,24},{1,5},{5... | collective-permute-start | bytes 786440 | tf_op jit(solution)/shard_map/ppermute | solution.py:301
  39.4 10.2 %collective-permute-start.9 = (bf16[1024,128]{1,0:T(8,128)(2,1)S(1)}, bf16[1024,128]{1,0:T(8,128)(2,1)S(1)}, u32[]{:S(2)}, u32[]{:S(2)}) collective-permute-start(bf16[1024,128]{1,0:T(8,128)(2,1)S(1)} %collective-permute-done.8.refs_10_), channel_id=1, source_target_pairs={{0,4},{4,0},{8,12},{12,8},{16,20},{20,16},{24,28},{28,24},{1,5},{5... | collective-permute-start | bytes 786440 | tf_op jit(solution)/shard_map/ppermute | solution.py:301
  39.4 10.2 %collective-permute-start.2 = (bf16[1024,128]{1,0:T(8,128)(2,1)S(1)}, bf16[1024,128]{1,0:T(8,128)(2,1)S(1)}, u32[]{:S(2)}, u32[]{:S(2)}) collective-permute-start(bf16[1024,128]{1,0:T(8,128)(2,1)S(1)} %collective-permute-done.1.refs_2_), channel_id=1, source_target_pairs={{0,4},{4,0},{8,12},{12,8},{16,20},{20,16},{24,28},{28,24},{1,5},{5... | collective-permute-start | bytes 786440 | tf_op jit(solution)/shard_map/ppermute | solution.py:301
  39.9 9.7 %collective-permute-start.4 = (bf16[1024,128]{1,0:T(8,128)(2,1)S(1)}, bf16[1024,128]{1,0:T(8,128)(2,1)S(1)}, u32[]{:S(2)}, u32[]{:S(2)}) collective-permute-start(bf16[1024,128]{1,0:T(8,128)(2,1)S(1)} %collective-permute-done.3.refs_4_), channel_id=1, source_target_pairs={{0,4},{4,0},{8,12},{12,8},{16,20},{20,16},{24,28},{28,24},{1,5},{5... | collective-permute-start | bytes 786440 | tf_op jit(solution)/shard_map/ppermute | solution.py:301
  40.0 9.6 %collective-permute-start.6 = (bf16[1024,128]{1,0:T(8,128)(2,1)S(1)}, bf16[1024,128]{1,0:T(8,128)(2,1)S(1)}, u32[]{:S(2)}, u32[]{:S(2)}) collective-permute-start(bf16[1024,128]{1,0:T(8,128)(2,1)S(1)} %collective-permute-done.5.refs_6_), channel_id=1, source_target_pairs={{0,4},{4,0},{8,12},{12,8},{16,20},{20,16},{24,28},{28,24},{1,5},{5... | collective-permute-start | bytes 786440 | tf_op jit(solution)/shard_map/ppermute | solution.py:301
  81.7 24.5 %collective-permute-start.18 = (bf16[4,256,896]{2,1,0:T(8,128)(2,1)}, bf16[4,256,896]{2,1,0:T(8,128)(2,1)S(1)}, u32[]{:S(2)}, u32[]{:S(2)}) collective-permute-start(bf16[4,256,896]{2,1,0:T(8,128)(2,1)} %get-tuple-element.21), channel_id=1, source_target_pairs={{0,4},{4,0},{8,12},{12,8},{16,20},{20,16},{24,28},{28,24},{1,5},{5... | collective-permute-start | bytes 5505032 | tf_op jit(solution)/shard_map/ppermute | solution.py:301
  83.3 14.7 %collective-permute-start.21 = (bf16[1024,128]{1,0:T(8,128)(2,1)S(1)}, bf16[1024,128]{1,0:T(8,128)(2,1)S(1)}, u32[]{:S(2)}, u32[]{:S(2)}) collective-permute-start(bf16[1024,128]{1,0:T(8,128)(2,1)S(1)} %get-tuple-element.50), channel_id=1, source_target_pairs={{0,16},{4,20},{8,24},{12,28},{16,0},{20,4},{24,8},{28,12},{1,17},{... | collective-permute-start | bytes 786440 | tf_op jit(solution)/shard_map/ppermute | solution.py:301
  84.9 13.1 %collective-permute-start.22 = (bf16[1024,128]{1,0:T(8,128)(2,1)S(1)}, bf16[1024,128]{1,0:T(8,128)(2,1)S(1)}, u32[]{:S(2)}, u32[]{:S(2)}) collective-permute-start(bf16[1024,128]{1,0:T(8,128)(2,1)S(1)} %get-tuple-element.49), channel_id=1, source_target_pairs={{0,24},{4,28},{8,16},{12,20},{16,8},{20,12},{24,0},{28,4},{1,25},{... | collective-permute-start | bytes 786440 | tf_op jit(solution)/shard_map/ppermute | solution.py:301
  88.1 16.5 %collective-permute-start.15 = (bf16[1024,128]{1,0:T(8,128)(2,1)S(1)}, bf16[1024,128]{1,0:T(8,128)(2,1)S(1)}, u32[]{:S(2)}, u32[]{:S(2)}) collective-permute-start(bf16[1024,128]{1,0:T(8,128)(2,1)S(1)} %get-tuple-element.55.refs_4_), channel_id=1, source_target_pairs={{0,8},{4,12},{8,0},{12,4},{16,24},{20,28},{24,16},{28,20},{1,9},{5... | collective-permute-start | bytes 786440 | tf_op jit(solution)/shard_map/ppermute | solution.py:301
  92.4 25.1 %collective-permute-start.16 = (bf16[1024,128]{1,0:T(8,128)(2,1)S(1)}, bf16[1024,128]{1,0:T(8,128)(2,1)S(1)}, u32[]{:S(2)}, u32[]{:S(2)}) collective-permute-start(bf16[1024,128]{1,0:T(8,128)(2,1)S(1)} %get-tuple-element.54.refs_5_), channel_id=1, source_target_pairs={{0,16},{4,20},{8,24},{12,28},{16,0},{20,4},{24,8},{28,12},{1,17},{... | collective-permute-start | bytes 786440 | tf_op jit(solution)/shard_map/ppermute | solution.py:301
  100.9 15.3 %collective-permute-start.29 = (bf16[1024,128]{1,0:T(8,128)(2,1)}, bf16[1024,128]{1,0:T(8,128)(2,1)S(1)}, u32[]{:S(2)}, u32[]{:S(2)}) collective-permute-start(bf16[1024,128]{1,0:T(8,128)(2,1)} %shard_map.159.refs_0_), channel_id=1, source_target_pairs={{0,2},{2,0},{1,3},{3,1},{4,6},{6,4},{5,7},{7,5},{8,10},{10,8},{9,1... | collective-permute-start | bytes 786440 | tf_op jit(solution)/shard_map/ppermute | solution.py:277
  103.5 14.0 %collective-permute-start.17 = (bf16[1024,128]{1,0:T(8,128)(2,1)}, bf16[1024,128]{1,0:T(8,128)(2,1)S(1)}, u32[]{:S(2)}, u32[]{:S(2)}) collective-permute-start(bf16[1024,128]{1,0:T(8,128)(2,1)} %get-tuple-element.53.refs_6_), channel_id=1, source_target_pairs={{0,24},{4,28},{8,16},{12,20},{16,8},{20,12},{24,0},{28,4},{1,25},{... | collective-permute-start | bytes 786440 | tf_op jit(solution)/shard_map/ppermute | solution.py:301
  104.6 12.9 %collective-permute-start.23 = (bf16[1024,128]{1,0:T(8,128)(2,1)}, bf16[1024,128]{1,0:T(8,128)(2,1)S(1)}, u32[]{:S(2)}, u32[]{:S(2)}) collective-permute-start(bf16[1024,128]{1,0:T(8,128)(2,1)} %shard_map.159.refs_0_), channel_id=1, source_target_pairs={{0,1},{1,0},{2,3},{3,2},{4,5},{5,4},{6,7},{7,6},{8,9},{9,8},{10,11... | collective-permute-start | bytes 786440 | tf_op jit(solution)/shard_map/ppermute | solution.py:277
  106.2 11.3 %collective-permute-start.24 = (bf16[1024,128]{1,0:T(8,128)(2,1)}, bf16[1024,128]{1,0:T(8,128)(2,1)S(1)}, u32[]{:S(2)}, u32[]{:S(2)}) collective-permute-start(bf16[1024,128]{1,0:T(8,128)(2,1)} %shard_map.159.refs_0_), channel_id=1, source_target_pairs={{1,2},{2,1},{5,6},{6,5},{9,10},{10,9},{13,14},{14,13},{17,18},{18,... | collective-permute-start | bytes 786440 | tf_op jit(solution)/shard_map/ppermute | solution.py:277
  116.2 12.0 %collective-permute-start.30 = (bf16[1024,128]{1,0:T(8,128)(2,1)S(1)}, bf16[1024,128]{1,0:T(8,128)(2,1)S(1)}, u32[]{:S(2)}, u32[]{:S(2)}) collective-permute-start(bf16[1024,128]{1,0:T(8,128)(2,1)S(1)} %collective-permute-done.29.refs_2_), channel_id=1, source_target_pairs={{1,0},{2,3},{5,4},{6,7},{9,8},{10,11},{13,12},{14,15},{17,16},{18,... | collective-permute-start | bytes 786440 | tf_op jit(solution)/shard_map/ppermute | solution.py:277
  121.0 13.5 %collective-permute-start.25 = (bf16[1024,128]{1,0:T(8,128)(2,1)}, bf16[1024,128]{1,0:T(8,128)(2,1)S(1)}, u32[]{:S(2)}, u32[]{:S(2)}) collective-permute-start(bf16[1024,128]{1,0:T(8,128)(2,1)} %shard_map.161.refs_0_), channel_id=1, source_target_pairs={{0,1},{1,0},{2,3},{3,2},{4,5},{5,4},{6,7},{7,6},{8,9},{9,8},{10,11... | collective-permute-start | bytes 786440 | tf_op jit(solution)/shard_map/ppermute | solution.py:277
  124.7 20.6 %collective-permute-start.31 = (bf16[256,896]{1,0:T(8,128)(2,1)}, bf16[256,896]{1,0:T(8,128)(2,1)S(1)}, u32[]{:S(2)}, u32[]{:S(2)}) collective-permute-start(bf16[256,896]{1,0:T(8,128)(2,1)} %get-tuple-element.24.refs_6_), channel_id=1, source_target_pairs={{0,8},{4,12},{8,0},{12,4},{16,24},{20,28},{24,16},{28,20},{1,9},{5... | collective-permute-start | bytes 1376264 | tf_op jit(solution)/shard_map/ppermute | solution.py:301
  125.7 19.6 %collective-permute-start.32 = (bf16[256,896]{1,0:T(8,128)(2,1)}, bf16[256,896]{1,0:T(8,128)(2,1)S(1)}, u32[]{:S(2)}, u32[]{:S(2)}) collective-permute-start(bf16[256,896]{1,0:T(8,128)(2,1)} %get-tuple-element.26), channel_id=1, source_target_pairs={{0,16},{4,20},{8,24},{12,28},{16,0},{20,4},{24,8},{28,12},{1,17},{... | collective-permute-start | bytes 1376264 | tf_op jit(solution)/shard_map/ppermute | solution.py:301
  126.6 21.2 %collective-permute-start.33 = (bf16[256,896]{1,0:T(8,128)(2,1)}, bf16[256,896]{1,0:T(8,128)(2,1)}, u32[]{:S(2)}, u32[]{:S(2)}) collective-permute-start(bf16[256,896]{1,0:T(8,128)(2,1)} %get-tuple-element.27), channel_id=1, source_target_pairs={{0,24},{4,28},{8,16},{12,20},{16,8},{20,12},{24,0},{28,4},{1,25},{... | collective-permute-start | bytes 1376264 | tf_op jit(solution)/shard_map/ppermute | solution.py:301
  128.2 15.8 %collective-permute-start.26 = (bf16[1024,128]{1,0:T(8,128)(2,1)}, bf16[1024,128]{1,0:T(8,128)(2,1)S(1)}, u32[]{:S(2)}, u32[]{:S(2)}) collective-permute-start(bf16[1024,128]{1,0:T(8,128)(2,1)} %shard_map.161.refs_0_), channel_id=1, source_target_pairs={{0,2},{2,0},{1,3},{3,1},{4,6},{6,4},{5,7},{7,5},{8,10},{10,8},{9,1... | collective-permute-start | bytes 786440 | tf_op jit(solution)/shard_map/ppermute | solution.py:277
  134.5 10.7 %collective-permute-start.27 = (bf16[1024,128]{1,0:T(8,128)(2,1)}, bf16[1024,128]{1,0:T(8,128)(2,1)S(1)}, u32[]{:S(2)}, u32[]{:S(2)}) collective-permute-start(bf16[1024,128]{1,0:T(8,128)(2,1)} %shard_map.161.refs_0_), channel_id=1, source_target_pairs={{1,2},{2,1},{5,6},{6,5},{9,10},{10,9},{13,14},{14,13},{17,18},{18,... | collective-permute-start | bytes 786440 | tf_op jit(solution)/shard_map/ppermute | solution.py:277
  144.0 11.6 %collective-permute-start.28 = (bf16[1024,128]{1,0:T(8,128)(2,1)S(1)}, bf16[1024,128]{1,0:T(8,128)(2,1)}, u32[]{:S(2)}, u32[]{:S(2)}) collective-permute-start(bf16[1024,128]{1,0:T(8,128)(2,1)S(1)} %collective-permute-done.26.refs_2_.refs_5_), channel_id=1, source_target_pairs={{1,0},{2,3},{5,4},{6,7},{9,8},{10,11},{13,12},{14,15},{17,16},{18,... | collective-permute-start | bytes 786440 | tf_op jit(solution)/shard_map/ppermute | solution.py:277
  (48 other events, 521.2 us)

commit v6 on v5

--- a/solution.py
+++ b/solution.py
@@ -313,38 +313,44 @@
     return left.astype(jnp.float32) + right.astype(jnp.float32)
 
 
-def chip_sum(keep, send):
-    received = swap(send, 1)
-    count = lax.axis_size("dp") // 2
-    rows = keep.shape[0] // count
-    total = [
-        added(keep[at * rows : (at + 1) * rows], received[at * rows : (at + 1) * rows])
-        for at in range(count)
-    ]
-    return total[0], [item.astype(keep.dtype) for item in total[1:]]
-
-
-def exchange(sends):
-    return [swap(item, 2 * at + 2) for at, item in enumerate(sends)]
-
-
-def final_kernel(count, rotary, *refs):
-    total = refs[0][...].astype(jnp.float32)
-    for ref in refs[1 : 1 + count]:
-        total = total + ref[...].astype(jnp.float32)
-    if rotary:
-        total = total * refs[1 + count][...] - pltpu.roll(total, HD // 2, 1) * refs[2 + count][...]
+def halved(keep, received, last):
+    half = keep.shape[0] // 2
+    send = added(keep[half:], received[half:]).astype(jnp.bfloat16)
+    kept = added(keep[:half], received[:half])
+    return (kept if last else kept.astype(jnp.bfloat16)), send
+
+
+def sum_stages(keeps, receives, bits, between=None):
+    orders = (bits[1:], bits[:0:-1])
+    for stage in range(len(bits) - 1):
+        last = stage == len(bits) - 2
+        pairs = [halved(keep, received, last) for keep, received in zip(keeps, receives)]
+        keeps = [pair[0] for pair in pairs]
+        receives = [swap(pair[1], orders[part][stage]) for part, pair in enumerate(pairs)]
+        if stage == 0 and between is not None:
+            keeps[0] = between(keeps[0], pairs[0][1])
+    return keeps, receives
+
+
+def final_kernel(rotary, *refs):
     out_ref = refs[-1]
-    out_ref[...] = total.astype(out_ref.dtype)
-
-
-def final_sum(keep, received, tables, after, kind=jnp.bfloat16):
+    half = refs[0].shape[0]
+    for part in range(2):
+        rows = pl.ds(part * half, half)
+        total = refs[part][...].astype(jnp.float32) + refs[2 + part][...].astype(jnp.float32)
+        if rotary:
+            total = total * refs[4][rows, :] - pltpu.roll(total, HD // 2, 1) * refs[5][rows, :]
+        out_ref[rows, :] = total.astype(out_ref.dtype)
+
+
+def final_sum(keeps, received, tables, after, kind=jnp.bfloat16):
     vmem = pl.BlockSpec(memory_space=pltpu.VMEM)
     hbm = pl.BlockSpec(memory_space=pl.ANY)
-    parts = [keep, *received, *tables]
+    parts = [*keeps, *received, *tables]
+    rows, cols = keeps[0].shape
     return pl.pallas_call(
-        partial(final_kernel, len(received), len(tables) > 0),
-        out_shape=jax.ShapeDtypeStruct(keep.shape, kind),
+        partial(final_kernel, len(tables) > 0),
+        out_shape=jax.ShapeDtypeStruct((2 * rows, cols), kind),
         in_specs=[vmem] * len(parts) + [hbm] * len(after),
         out_specs=vmem,
         compiler_params=pltpu.CompilerParams(vmem_limit_bytes=VMEM_BYTES),
@@ -353,101 +359,128 @@
 
 
 def up_kernel(rows_ref, weight_ref, *refs):
-    total = jnp.dot(rows_ref[...], weight_ref[...], preferred_element_type=jnp.float32)
-    refs[-1][...] = total.astype(refs[-1].dtype)
+    out_ref, total_ref = refs[-2:]
+    part = jnp.dot(rows_ref[...], weight_ref[...], preferred_element_type=jnp.float32)
+    step = pl.program_id(0)
+
+    @pl.when(step == 0)
+    def first():
+        total_ref[...] = part
+
+    @pl.when(step > 0)
+    def later():
+        total_ref[...] += part
+
+    @pl.when(step == pl.num_programs(0) - 1)
+    def last():
+        out_ref[...] = total_ref[...].astype(out_ref.dtype)
 
 
 def up_product(rows, weight, after):
     height, depth = rows.shape
-    steps = 4
+    width = weight.shape[1]
+    piece = 512
     return pl.pallas_call(
         up_kernel,
-        grid=(steps,),
-        out_shape=jax.ShapeDtypeStruct((height, weight.shape[1]), jnp.bfloat16),
+        grid=(depth // piece,),
+        out_shape=jax.ShapeDtypeStruct((height, width), jnp.bfloat16),
         in_specs=[
-            pl.BlockSpec((height // steps, depth), lambda step: (step, 0)),
-            pl.BlockSpec(weight.shape, lambda step: (0, 0)),
+            pl.BlockSpec((height, piece), lambda step: (0, step)),
+            pl.BlockSpec((piece, width), lambda step: (step, 0)),
         ]
         + [pl.BlockSpec(memory_space=pl.ANY)] * len(after),
-        out_specs=pl.BlockSpec((height // steps, weight.shape[1]), lambda step: (step, 0)),
+        out_specs=pl.BlockSpec((height, width), lambda step: (0, 0)),
+        scratch_shapes=[pltpu.VMEM((height, width), jnp.float32)],
         compiler_params=pltpu.CompilerParams(vmem_limit_bytes=VMEM_BYTES),
+        cost_estimate=pl.CostEstimate(
+            flops=2 * height * weight.size, bytes_accessed=2 * rows.size, transcendentals=0
+        ),
+    )(rows, weight, *after)
+
+
+def take_heads_kernel(at_ref, key_ref, value_ref, after_ref, own_key_ref, own_value_ref):
+    own_key_ref[...] = key_ref[...]
+    own_value_ref[...] = value_ref[...]
+
+
+def take_heads(key, value, kv_head, after):
+    rows = key.shape[0]
+    steps = 2
+    picked = pl.BlockSpec((rows // steps, HD), lambda step, at_ref: (step, at_ref[0]))
+    own = pl.BlockSpec((rows // steps, HD), lambda step, at_ref: (step, 0))
+    shape = jax.ShapeDtypeStruct((rows, HD), key.dtype)
+    return pl.pallas_call(
+        take_heads_kernel,
+        grid_spec=pltpu.PrefetchScalarGridSpec(
+            num_scalar_prefetch=1,
+            grid=(steps,),
+            in_specs=[picked, picked, pl.BlockSpec(memory_space=pl.ANY)],
+            out_specs=[own, own],
+        ),
+        out_shape=[shape, shape],
         cost_estimate=NO_COST,
-    )(rows, weight, *after)
-
-
-def product_kernel(my_ref, left_ref, right_ref, thru_ref, out_ref, unused):
-    total = jnp.dot(left_ref[0], right_ref[...], preferred_element_type=jnp.float32)
-    out_ref[0] = total.astype(out_ref.dtype)
-
-
-def product_sum_kernel(count, my_ref, left_ref, right_ref, base_ref, *refs):
-    total = jnp.dot(left_ref[0], right_ref[...], preferred_element_type=jnp.float32)
-    total = total + base_ref[0].astype(jnp.float32)
-    for at, out_ref in enumerate(refs[-count:]):
-
-        @pl.when(pl.program_id(0) == at)
-        def store():
-            out_ref[...] = total.astype(out_ref.dtype)
-
-
-def product_specs(left, which, right):
+    )(kv_head.reshape(1), key, value, after)
+
+
+def place_of(distance, bits):
+    place = distance * 0
+    for bit in bits:
+        place = place * 2 + (distance & bit) // bit
+    return place
+
+
+def product_kernel(orders, my_ref, left_ref, right_ref, *refs):
+    outs = refs[-6:-2]
+    width = left_ref.shape[0] * left_ref.shape[1]
+    left = left_ref[...].reshape(width, left_ref.shape[2])
+    total = jnp.dot(left, right_ref[...], preferred_element_type=jnp.float32)
+    for at, out_ref in enumerate(outs):
+        out_ref[0] = total[at * width // 4 : (at + 1) * width // 4].astype(out_ref.dtype)
+
+
+def product(mine, left, right, thru, after, bits):
     count = lax.axis_size("dp") // 2
-    rows, cols = left.shape[1], right.shape[1] // count
-    stacked = pl.BlockSpec((1, rows, cols), lambda step, my_ref: (step, 0, 0))
-    ins = [
-        pl.BlockSpec((1,) + left.shape[1:], lambda step, my_ref: (which, 0, 0)),
-        pl.BlockSpec((right.shape[0], cols), lambda step, my_ref: (0, step ^ my_ref[0])),
+    width, depth = left.shape[0] * left.shape[1], left.shape[2]
+    rows, cols = width // 4, right.shape[1] // count
+    orders = ([bit // 2 for bit in bits[1:]], [bit // 2 for bit in bits[:0:-1]])
+    if cols % 128:
+        total = jnp.dot(left.reshape(width, depth), right, preferred_element_type=jnp.float32)
+        pieces = jnp.moveaxis(total.astype(jnp.bfloat16).reshape(width, count, cols), 1, 0)
+        stacks = []
+        for at in range(4):
+            order = sorted(range(count), key=lambda step: place_of(step, orders[at % 2]))
+            picked = jnp.take(pieces, jnp.array(order, jnp.int32) ^ mine, axis=0)
+            stacks.append(picked[:, at * rows : (at + 1) * rows])
+        return stacks, thru
+    hbm = pl.BlockSpec(memory_space=pl.ANY)
+    outs = [
+        pl.BlockSpec(
+            (1, rows, cols), lambda step, my_ref, at=at: (place_of(step, orders[at % 2]), 0, 0)
+        )
+        for at in range(4)
     ]
-    return count, rows, cols, stacked, ins
-
-
-def plain_pieces(mine, left, right):
-    count = lax.axis_size("dp") // 2
-    total = jnp.dot(left, right, preferred_element_type=jnp.float32)
-    pieces = jnp.moveaxis(total.reshape(left.shape[0], count, -1), 1, 0)
-    return jnp.take(pieces, jnp.arange(count, dtype=jnp.int32) ^ mine, axis=0)
-
-
-def product(mine, left, right, thru):
-    count, rows, cols, stacked, ins = product_specs(left, 1, right)
-    if cols % 128:
-        return plain_pieces(mine, left[1], right).astype(jnp.bfloat16), thru
-    hbm = pl.BlockSpec(memory_space=pl.ANY)
-    return pl.pallas_call(
-        product_kernel,
-        grid_spec=pltpu.PrefetchScalarGridSpec(
-            num_scalar_prefetch=1, grid=(count,), in_specs=ins + [hbm], out_specs=[stacked, hbm]
-        ),
-        out_shape=[
-            jax.ShapeDtypeStruct((count, rows, cols), jnp.bfloat16),
-            jax.ShapeDtypeStruct(thru.shape, thru.dtype),
-        ],
-        input_output_aliases={3: 1},
-        compiler_params=pltpu.CompilerParams(vmem_limit_bytes=VMEM_BYTES),
-        cost_estimate=NO_COST,
-    )(mine.reshape(1), left, right, thru)
-
-
-def product_sum(mine, left, right, base, after):
-    count, rows, cols, stacked, ins = product_specs(left, 0, right)
-    if cols % 128:
-        pieces = plain_pieces(mine, left[0], right) + base.astype(jnp.float32)
-        return [pieces[0]] + [pieces[at].astype(jnp.bfloat16) for at in range(1, count)]
-    return pl.pallas_call(
-        partial(product_sum_kernel, count),
+    inputs = [mine.reshape(1), left, right, *after, *thru]
+    results = pl.pallas_call(
+        partial(product_kernel, orders),
         grid_spec=pltpu.PrefetchScalarGridSpec(
             num_scalar_prefetch=1,
             grid=(count,),
-            in_specs=ins + [stacked] + [pl.BlockSpec(memory_space=pl.ANY)] * len(after),
-            out_specs=[pl.BlockSpec((rows, cols), lambda step, my_ref: (0, 0))] * count,
+            in_specs=[
+                pl.BlockSpec(left.shape, lambda step, my_ref: (0, 0, 0)),
+                pl.BlockSpec((depth, cols), lambda step, my_ref: (0, step ^ my_ref[0])),
+            ]
+            + [hbm] * (len(after) + 2),
+            out_specs=outs + [hbm] * 2,
         ),
-        out_shape=[
-            jax.ShapeDtypeStruct((rows, cols), jnp.bfloat16 if at else jnp.float32)
-            for at in range(count)
-        ],
+        out_shape=[jax.ShapeDtypeStruct((count, rows, cols), jnp.bfloat16)] * 4
+        + [jax.ShapeDtypeStruct(item.shape, item.dtype) for item in thru],
+        input_output_aliases={len(inputs) - 2: 4, len(inputs) - 1: 5},
         compiler_params=pltpu.CompilerParams(vmem_limit_bytes=VMEM_BYTES),
-        cost_estimate=NO_COST,
-    )(mine.reshape(1), left, right, base, *after)
+        cost_estimate=pl.CostEstimate(
+            flops=2 * width * right.size, bytes_accessed=2 * right.size, transcendentals=0
+        ),
+    )(*inputs)
+    return results[:4], results[4:]
 
 
 def local(query, key, value, grad_out, out_weight, plan, segments):
@@ -460,9 +493,6 @@
     group = HEADS // KV
     bits = [1 << at for at in range(rank_count.bit_length() - 1)]
     kv_head = my_lane * local_heads // group
-    own_key = lax.dynamic_slice_in_dim(key, kv_head * HD, HD, 1)
-    own_value = lax.dynamic_slice_in_dim(value, kv_head * HD, HD, 1)
-
     own_places = positions_of(segments).reshape(1, block_count, ROWBLK)
     places_all = lax.all_to_all(
         jnp.broadcast_to(own_places, (rank_count, block_count, ROWBLK)),
@@ -471,6 +501,7 @@
         concat_axis=0,
         tiled=True,
     ).reshape(-1, ROWBLK)
+    own_key, own_value = take_heads(key, value, kv_head, places_all)
     values = spread(own_value)
 
     mine = my_rank * block_count + jnp.arange(block_count, dtype=jnp.int32)
@@ -490,9 +521,14 @@
 
     distance = (plan // block_count) ^ my_rank
     within = plan % block_count
-    half_place = (distance & 1) * (rank_count // 2) + distance // 2
+    part_blocks = block_count // 2
+    stage_place = jnp.where(
+        within < part_blocks, place_of(distance, bits[1:]), place_of(distance, bits[:0:-1])
+    )
+    quarter = (distance & 1) * 2 + within // part_blocks
+    target = (quarter * (rank_count // 2) + stage_place) * part_blocks + within % part_blocks
     tables = (
-        half_place * block_count + within,
+        target,
         distance * block_count + within,
         run,
         slot,
@@ -502,22 +538,40 @@
     grad_query, attn_t, gkey_keep, gkey_send, gvalue_keep, gvalue_send = attend(
         tables, query, up, cosine, sine, places, keys, values
     )
-    mine_pair = my_rank // 2
-    value_keep, value_sends = chip_sum(gvalue_keep, gvalue_send)
-    value_received = exchange(value_sends)
-    first, gkey_keep = product(mine_pair, attn_t, grad_out, gkey_keep)
-    first = swap(first, 1)
-    key_keep, key_sends = chip_sum(gkey_keep, gkey_send)
-    key_received = exchange(key_sends)
-    value_partial = final_sum(value_keep, value_received, (), key_sends)
+    def parts_of(array):
+        return [array[: array.shape[0] // 2], array[array.shape[0] // 2 :]]
+
+    held = {}
+
+    def weight_product(keep, send):
+        stacks, (held["send"], keep) = product(
+            my_rank // 2, attn_t, grad_out, (gkey_send, keep), [send], bits
+        )
+        held["stacks"] = stacks
+        return keep
+
+    value_keeps, value_received = sum_stages(
+        parts_of(gvalue_keep), parts_of(swap(gvalue_send, 1)), bits, weight_product
+    )
+    stacks = held["stacks"]
+    weight_received = [swap(item, 1) for item in stacks[2:]]
+    value_partial = final_sum(value_keeps, value_received, (), ())
     value_all, value_pieces = lane_gather(value_partial, my_lane)
-    kept, *sends = product_sum(mine_pair, attn_t, grad_out, first, [value_partial])
-    received = exchange(sends)
-    key_partial = final_sum(
-        key_keep, key_received, (cosine, sine), [sends[0], value_pieces[0], value_pieces[2]]
-    )
+
+    key_keeps, key_received = sum_stages(
+        parts_of(gkey_keep), parts_of(swap(held["send"], 1)), bits
+    )
+    key_partial = final_sum(key_keeps, key_received, (cosine, sine), value_pieces[:1])
     key_all, key_pieces = lane_gather(key_partial, my_lane)
-    total = final_sum(kept, received, (), key_pieces[:3] + value_pieces[3:], jnp.float32)
+
+    weight_keeps, weight_received = sum_stages(stacks[:2], weight_received, bits)
+    total = final_sum(
+        [item[0] for item in weight_keeps],
+        [item[0] for item in weight_received],
+        (),
+        [*key_pieces[:3], value_all],
+        jnp.float32,
+    )
     odd = my_rank & 1
     pair_rows = grad_out.shape[1] // (rank_count // 2)
     low, high = total[:, : pair_rows // 2], total[:, pair_rows // 2 :]

time: 159 us -> 201 us (1.26); the launches traced: 159 us -> 199 us
  waiting for transfers between devices: 41.8 us -> 71.7 us
  other arithmetic: 14.3 us -> 22.1 us
  starting transfers between devices: 36.1 us -> 39.9 us
  Pallas kernels: 58.5 us -> 55.4 us
    ppermute x27 -> x31, waiting for transfers between devices: 22.3 us -> 45.5 us  [swap(): lax.ppermute(array, 'dp', [(rank, rank ^ bit) for rank in range(ranks)])]
    ppermute x8, waiting for transfers between devices: 14.8 us -> 22.3 us  [send(): return lax.ppermute(item, 'tensor', pairs)]
    convert_element_type x3 -> x10, other arithmetic: 3.18 us -> 9.96 us  [the longest x6 5.82 us: halved(): send = added(keep[half:], received[half:]).astype(jnp.bfloat16)]
    pallas_call x6, Pallas kernels: 29.5 us -> 26.9 us  [the longest x1 10.2 us: up_product(): pl.pallas_call(up_kernel, grid=(depth // piece,), out_shape=jax.ShapeDtyp...]
    ppermute x27 -> x31, starting transfers between devices: 18.3 us -> 19.8 us  [swap(): lax.ppermute(array, 'dp', [(rank, rank ^ bit) for rank in range(ranks)])]
    unnamed x89 -> x81, local copies, waits for them, and re-layouts: 5.88 us -> 5.38 us
  transfers between devices with their start and end apart: 36 -> 40, of which waited for: 10 -> 19; matrix products, arithmetic and copies ran while one was open for 10% -> 7% of each run, Pallas kernels for 21% -> 13%
where the time goes in v6:
time: 201 us; the launch traced here: 199 us
  waiting for transfers between devices  71.7 us (36%)
  Pallas kernels  55.4 us (28%)
  starting transfers between devices  39.9 us (20%)
  other arithmetic  22.1 us (11%)
  local copies, waits for them, and re-layouts  8.84 us (4%)
    ppermute x31, waiting for transfers between devices, swap(): lax.ppermute(array, 'dp', [(rank, rank ^ bit) for rank in range(ranks)])  45.5 us
    pallas_call x1, Pallas kernels, attend(): pl.pallas_call(partial(attend_kernel, heads, ranks), out_shape=(jax.Shape...  23.9 us
    ppermute x8, waiting for transfers between devices, send(): return lax.ppermute(item, 'tensor', pairs)  22.3 us
    ppermute x31, starting transfers between devices, swap(): lax.ppermute(array, 'dp', [(rank, rank ^ bit) for rank in range(ranks)])  19.8 us
    ppermute x8, starting transfers between devices, send(): return lax.ppermute(item, 'tensor', pairs)  15 us
    pallas_call x1, Pallas kernels, up_product(): pl.pallas_call(up_kernel, grid=(depth // piece,), out_shape=jax.ShapeDtyp...  10.2 us
    pallas_call x1, Pallas kernels, product(): pl.pallas_call(partial(product_kernel, orders), grid_spec=pltpu.PrefetchS...  8.38 us
    pallas_call x3, Pallas kernels, final_sum(): pl.pallas_call(partial(final_kernel, len(tables) > 0), out_shape=jax.Shap...  6.5 us
  transfers between devices with their start and end apart: 40, of which 19 were waited for; matrix products, arithmetic and copies ran while one was open for 7% of the time, Pallas kernels for 13%

profile of v6, /device:TPU:0, one launch (start us, length us, event | category | flops | bytes accessed | tf_op | source)
XLA Modules:
  0.0 199.2 jit_solution(15010884034021325159)
XLA Ops:
  2.8 5.2 %all-to-all-start = ((s32[8,8,128]{2,1,0:T(8,128)}), s32[8,8,128]{2,1,0:T(8,128)S(1)}, u32[]{:S(2)}, u32[]{:S(2)}) async-start(s32[8,8,128]{2,1,0:T(8,128)} %broadcast_in_dim.40), calls=%async_computation | async-start | bytes 65536 | tf_op jit(solution)/shard_map/all_to_all | solution.py:497
  8.8 3.9 %all-to-all-done = s32[8,8,128]{2,1,0:T(8,128)S(1)} async-done(((s32[8,8,128]{2,1,0:T(8,128)}), s32[8,8,128]{2,1,0:T(8,128)S(1)}, u32[]{:S(2)}, u32[]{:S(2)}) %all-to-all-start) | async-done | bytes 32800 | tf_op jit(solution)/shard_map/all_to_all | solution.py:497
  13.4 1.8 shard_map.156
  17.8 1.9 fusion.5
  19.8 2.4 %fusion.4 = (bf16[1024,128]{1,0:T(8,128)(2,1)S(1)}, f32[1024,128]{1,0:T(8,128)}, f32[1024,128]{1,0:T(8,128)}) fusion(f32[1024,64]{1,0:T(8,128)S(1)} %get-tuple-element.81, f32[1024,64]{1,0:T(8,128)S(1)} %get-tuple-element.80, bf16[1024,128]{1,0:T(8,128)(2,1)} %get-tuple-element.18, f32[1024,64]{1,0:T(8,128)S(1)} %get-tuple-element.84, ...), kind=kLoop, calls=%fused_computation.16 | loop fusion | flops 1048576 | bytes 2883584 | tf_op jit(solution)/shard_map/convert_element_type | solution.py:518
  23.3 2.4 %collective-permute-start.5 = (bf16[1024,128]{1,0:T(8,128)(2,1)S(1)}, bf16[1024,128]{1,0:T(8,128)(2,1)S(1)}, u32[]{:S(2)}, u32[]{:S(2)}) collective-permute-start(bf16[1024,128]{1,0:T(8,128)(2,1)S(1)} %get-tuple-element.44.refs_0_), channel_id=1, source_target_pairs={{0,24},{4,28},{8,16},{12,20},{16,8},{20,12},{24,0},{28,4},{1,25},{... | collective-permute-start | bytes 786440 | tf_op jit(solution)/shard_map/ppermute | solution.py:301
  27.3 4.1 %collective-permute-done.1.refs_2_ = bf16[1024,128]{1,0:T(8,128)(2,1)S(1)} collective-permute-done((bf16[1024,128]{1,0:T(8,128)(2,1)S(1)}, bf16[1024,128]{1,0:T(8,128)(2,1)S(1)}, u32[]{:S(2)}, u32[]{:S(2)}) %collective-permute-start.1) | collective-permute-done | bytes 262176 | tf_op jit(solution)/shard_map/ppermute | solution.py:301
  31.9 11.1 %collective-permute-done.3.refs_4_ = bf16[1024,128]{1,0:T(8,128)(2,1)S(1)} collective-permute-done((bf16[1024,128]{1,0:T(8,128)(2,1)S(1)}, bf16[1024,128]{1,0:T(8,128)(2,1)S(1)}, u32[]{:S(2)}, u32[]{:S(2)}) %collective-permute-start.3) | collective-permute-done | bytes 262176 | tf_op jit(solution)/shard_map/ppermute | solution.py:301
  45.2 10.2 %shard_map.157.up_ref = bf16[1024,512]{1,0:T(8,128)(2,1)} custom-call(bf16[1024,3584]{1,0:T(8,128)(2,1)} %right_ref.1, bf16[3584,512]{1,0:T(8,128)(2,1)} %weight_ref.1, bf16[1024,128]{1,0:T(8,128)(2,1)} %copy-done.2), custom_call_target="tpu_custom_call" | custom-call | flops 3758096384 | bytes 7340032 | tf_op jit(solution)/shard_map/pallas_call | solution.py:383
  59.2 23.9 %shard_map.158 = (bf16[1024,512]{1,0:T(8,128)(2,1)}, bf16[2,256,1024]{2,1,0:T(8,128)(2,1)}, bf16[4096,128]{1,0:T(8,128)(2,1)}, bf16[4096,128]{1,0:T(8,128)(2,1)}...) custom-call(s32[64]{0:T(128)} %fusion.7.target_ref, s32[64]{0:T(128)} %get-tuple-element.50.source_ref, ...), custom_call_target="tpu_custom_call" | custom-call | tf_op jit(solution)/shard_map/pallas_call | solution.py:223
  84.4 2.5 %collective-permute-done.14 = bf16[4096,128]{1,0:T(8,128)(2,1)S(1)} collective-permute-done((bf16[4096,128]{1,0:T(8,128)(2,1)}, bf16[4096,128]{1,0:T(8,128)(2,1)S(1)}, u32[]{:S(2)}, u32[]{:S(2)}) %collective-permute-start.14) | collective-permute-done | bytes 1048608 | tf_op jit(solution)/shard_map/ppermute | solution.py:301
  86.9 2.3 %add_convert_fusion.5 = (bf16[1024,128]{1,0:T(8,128)(2,1)S(1)}, bf16[1024,128]{1,0:T(8,128)(2,1)S(1)}, bf16[1024,128]{1,0:T(8,128)(2,1)}, bf16[1024,128]{1,0:T(8,128)(2,1)}) fusion(bf16[4096,128]{1,0:T(8,128)(2,1)S(1)} %collective-permute-done.14, bf16[4096,128]{1,0:T(8,128)(2,1)} %get-tuple-element.23), kind=kLoop, calls=%fused_computation.20 | loop fusion | flops 2097152 | bytes 3145728 | tf_op jit(solution)/shard_map/convert_element_type | solution.py:320
  89.2 8.4 %shard_map.159 = (bf16[4,128,896]{2,1,0:T(8,128)(2,1)}, bf16[4,128,896]{2,1,0:T(8,128)(2,1)}, bf16[4,128,896]{2,1,0:T(8,128)(2,1)}, bf16[4,128,896]{2,1,0:T(8,12...) custom-call(s32[1]{0:T(128)} %bitcast.7.my_ref, ...), custom_call_target="tpu_custom_call", output_to_operand_aliasing={{4}: (4, {}), {5}: (5, {})} | custom-call | flops 3758096384 | bytes 7340032 | tf_op jit(solution)/shard_map/pallas_call | solution.py:463
  98.9 1.9 collective-permute-start.23
  100.8 6.3 %collective-permute-done.20 = bf16[1024,128]{1,0:T(8,128)(2,1)S(1)} collective-permute-done((bf16[1024,128]{1,0:T(8,128)(2,1)S(1)}, bf16[1024,128]{1,0:T(8,128)(2,1)S(1)}, u32[]{:S(2)}, u32[]{:S(2)}) %collective-permute-start.20) | collective-permute-done | bytes 262176 | tf_op jit(solution)/shard_map/ppermute | solution.py:301
  110.5 3.3 %collective-permute-done.22.refs_2_ = bf16[512,128]{1,0:T(8,128)(2,1)S(1)} collective-permute-done((bf16[512,128]{1,0:T(8,128)(2,1)S(1)}, bf16[512,128]{1,0:T(8,128)(2,1)S(1)}, u32[]{:S(2)}, u32[]{:S(2)}) %collective-permute-start.22) | collective-permute-done | bytes 131104 | tf_op jit(solution)/shard_map/ppermute | solution.py:301
  114.5 1.9 shard_map.160.refs_0_
  116.3 2.6 %collective-permute-start.29 = (bf16[1024,128]{1,0:T(8,128)(2,1)}, bf16[1024,128]{1,0:T(8,128)(2,1)S(1)}, u32[]{:S(2)}, u32[]{:S(2)}) collective-permute-start(bf16[1024,128]{1,0:T(8,128)(2,1)} %shard_map.160.refs_0_), channel_id=1, source_target_pairs={{0,2},{2,0},{1,3},{3,1},{4,6},{6,4},{5,7},{7,5},{8,10},{10,8},{9,1... | collective-permute-start | bytes 786440 | tf_op jit(solution)/shard_map/ppermute | solution.py:277
  120.5 8.8 %collective-permute-done.29.refs_2_ = bf16[1024,128]{1,0:T(8,128)(2,1)S(1)} collective-permute-done((bf16[1024,128]{1,0:T(8,128)(2,1)}, bf16[1024,128]{1,0:T(8,128)(2,1)S(1)}, u32[]{:S(2)}, u32[]{:S(2)}) %collective-permute-start.29) | collective-permute-done | bytes 262176 | tf_op jit(solution)/shard_map/ppermute | solution.py:277
  133.0 1.8 collective-permute-start.17
  135.6 4.6 %collective-permute-done.17 = bf16[1024,128]{1,0:T(8,128)(2,1)S(1)} collective-permute-done((bf16[1024,128]{1,0:T(8,128)(2,1)S(1)}, bf16[1024,128]{1,0:T(8,128)(2,1)S(1)}, u32[]{:S(2)}, u32[]{:S(2)}) %collective-permute-start.17) | collective-permute-done | bytes 262176 | tf_op jit(solution)/shard_map/ppermute | solution.py:301
  140.2 1.7 collective-permute-start.35
  143.9 6.6 %collective-permute-done.35 = bf16[2,128,896]{2,1,0:T(8,128)(2,1)S(1)} collective-permute-done((bf16[2,128,896]{2,1,0:T(8,128)(2,1)S(1)}, bf16[2,128,896]{2,1,0:T(8,128)(2,1)S(1)}, u32[]{:S(2)}, u32[]{:S(2)}) %collective-permute-start.35) | collective-permute-done | bytes 458784 | tf_op jit(solution)/shard_map/ppermute | solution.py:301
  151.9 2.9 %collective-permute-done.33 = bf16[2,128,896]{2,1,0:T(8,128)(2,1)S(1)} collective-permute-done((bf16[2,128,896]{2,1,0:T(8,128)(2,1)S(1)}, bf16[2,128,896]{2,1,0:T(8,128)(2,1)S(1)}, u32[]{:S(2)}, u32[]{:S(2)}) %collective-permute-start.33) | collective-permute-done | bytes 458784 | tf_op jit(solution)/shard_map/ppermute | solution.py:301
  160.4 2.4 %shard_map.161.refs_0_ = bf16[1024,128]{1,0:T(8,128)(2,1)} custom-call(f32[512,128]{1,0:T(8,128)} %get-tuple-element.78.refs_0_, f32[512,128]{1,0:T(8,128)} %get-tuple-element.76.refs_1_, bf16[512,128]{1,0:T(8,128)(2,1)} %copy-done.31, bf16[512,128]{1,0:T(8,128)(2,1)} %copy-done.30, f32[1024,128]{1,0:T(8,128)} %get-tuple-element.79.cos_ref.refs_4_, ...), custom_call_target="tpu_custom_call" | custom-call | tf_op jit(solution)/shard_map/pallas_call | solution.py:351
  162.8 3.6 %collective-permute-start.25 = (bf16[1024,128]{1,0:T(8,128)(2,1)}, bf16[1024,128]{1,0:T(8,128)(2,1)S(1)}, u32[]{:S(2)}, u32[]{:S(2)}) collective-permute-start(bf16[1024,128]{1,0:T(8,128)(2,1)} %shard_map.161.refs_0_), channel_id=1, source_target_pairs={{0,1},{1,0},{2,3},{3,2},{4,5},{5,4},{6,7},{7,6},{8,9},{9,8},{10,11... | collective-permute-start | bytes 786440 | tf_op jit(solution)/shard_map/ppermute | solution.py:277
  166.3 3.3 %collective-permute-start.26 = (bf16[1024,128]{1,0:T(8,128)(2,1)}, bf16[1024,128]{1,0:T(8,128)(2,1)S(1)}, u32[]{:S(2)}, u32[]{:S(2)}) collective-permute-start(bf16[1024,128]{1,0:T(8,128)(2,1)} %shard_map.161.refs_0_), channel_id=1, source_target_pairs={{0,2},{2,0},{1,3},{3,1},{4,6},{6,4},{5,7},{7,5},{8,10},{10,8},{9,1... | collective-permute-start | bytes 786440 | tf_op jit(solution)/shard_map/ppermute | solution.py:277
  171.5 2.3 %shard_map.163.refs_7_ = bf16[1024,512]{1,0:T(8,128)(2,1)} custom-call(s32[5]{0:T(128)} %broadcast_xor_fusion.column_ref, s32[5]{0:T(128)} %or_convert_fusion.active_ref, bf16[1024,128]{1,0:T(8,128)(2,1)} %shard_map.160.refs_0_, bf16[1024,128]{1,0:T(8,128)(2,1)} %copy-done.1, bf16[1024,128]{1,0:T(8,128)(2,1)} %copy-done.8, bf16[1024,128]{1,0:T(8,128)(2,1)} %copy-done.9, ...), custom_call_target="tpu_custom_call" | custom-call | tf_op jit(solution)/shard_map/pallas_call | solution.py:262
  173.8 6.0 %collective-permute-done.26.refs_2_.refs_5_ = bf16[1024,128]{1,0:T(8,128)(2,1)S(1)} collective-permute-done((bf16[1024,128]{1,0:T(8,128)(2,1)}, bf16[1024,128]{1,0:T(8,128)(2,1)S(1)}, u32[]{:S(2)}, u32[]{:S(2)}) %collective-permute-start.26) | collective-permute-done | bytes 262176 | tf_op jit(solution)/shard_map/ppermute | solution.py:277
  180.7 2.3 %shard_map.164 = f32[256,896]{1,0:T(8,128)} custom-call(f32[128,896]{1,0:T(8,128)} %get-tuple-element.70.refs_0_, f32[128,896]{1,0:T(8,128)} %get-tuple-element.68.refs_1_, bf16[128,896]{1,0:T(8,128)(2,1)} %bitcast.25, bf16[128,896]{1,0:T(8,128)(2,1)} %bitcast.24, bf16[1024,128]{1,0:T(8,128)(2,1)} %copy-done.3, bf16[1024,128]{1,0:T(8,128)(2,1)} %copy-done.4, ...), custom_call_target="tpu_custom_call" | custom-call | tf_op jit(solution)/shard_map/pallas_call | solution.py:351
  188.7 7.4 %collective-permute-done.28.refs_4_ = bf16[1024,128]{1,0:T(8,128)(2,1)S(1)} collective-permute-done((bf16[1024,128]{1,0:T(8,128)(2,1)}, bf16[1024,128]{1,0:T(8,128)(2,1)S(1)}, u32[]{:S(2)}, u32[]{:S(2)}) %collective-permute-start.28) | collective-permute-done | bytes 262176 | tf_op jit(solution)/shard_map/ppermute | solution.py:277
  196.8 2.3 %shard_map.162 = bf16[1024,512]{1,0:T(8,128)(2,1)} custom-call(s32[5]{0:T(128)} %broadcast_xor_fusion.column_ref, s32[5]{0:T(128)} %or_convert_fusion.active_ref, bf16[1024,128]{1,0:T(8,128)(2,1)} %shard_map.161.refs_0_, bf16[1024,128]{1,0:T(8,128)(2,1)} %copy-done.3, bf16[1024,128]{1,0:T(8,128)(2,1)} %copy-done.4, bf16[1024,128]{1,0:T(8,128)(2,1)} %copy-done.5, ...), custom_call_target="tpu_custom_call" | custom-call | tf_op jit(solution)/shard_map/pallas_call | solution.py:262
  (176 shorter events, 45.9 us)
Async XLA Ops:
  2.8 10.0 %all-to-all-start = ((s32[8,8,128]{2,1,0:T(8,128)}), s32[8,8,128]{2,1,0:T(8,128)S(1)}, u32[]{:S(2)}, u32[]{:S(2)}) async-start(s32[8,8,128]{2,1,0:T(8,128)} %broadcast_in_dim.40), calls=%async_computation | async-start | bytes 65536 | tf_op jit(solution)/shard_map/all_to_all | solution.py:497
  22.2 9.2 %collective-permute-start.1 = (bf16[1024,128]{1,0:T(8,128)(2,1)S(1)}, bf16[1024,128]{1,0:T(8,128)(2,1)S(1)}, u32[]{:S(2)}, u32[]{:S(2)}) collective-permute-start(bf16[1024,128]{1,0:T(8,128)(2,1)S(1)} %get-tuple-element.44.refs_0_), channel_id=1, source_target_pairs={{0,8},{4,12},{8,0},{12,4},{16,24},{20,28},{24,16},{28,20},{1,9},{5... | collective-permute-start | bytes 786440 | tf_op jit(solution)/shard_map/ppermute | solution.py:301
  22.8 20.2 %collective-permute-start.3 = (bf16[1024,128]{1,0:T(8,128)(2,1)S(1)}, bf16[1024,128]{1,0:T(8,128)(2,1)S(1)}, u32[]{:S(2)}, u32[]{:S(2)}) collective-permute-start(bf16[1024,128]{1,0:T(8,128)(2,1)S(1)} %get-tuple-element.44.refs_0_), channel_id=1, source_target_pairs={{0,16},{4,20},{8,24},{12,28},{16,0},{20,4},{24,8},{28,12},{1,17},{... | collective-permute-start | bytes 786440 | tf_op jit(solution)/shard_map/ppermute | solution.py:301
  23.3 21.4 %collective-permute-start.5 = (bf16[1024,128]{1,0:T(8,128)(2,1)S(1)}, bf16[1024,128]{1,0:T(8,128)(2,1)S(1)}, u32[]{:S(2)}, u32[]{:S(2)}) collective-permute-start(bf16[1024,128]{1,0:T(8,128)(2,1)S(1)} %get-tuple-element.44.refs_0_), channel_id=1, source_target_pairs={{0,24},{4,28},{8,16},{12,20},{16,8},{20,12},{24,0},{28,4},{1,25},{... | collective-permute-start | bytes 786440 | tf_op jit(solution)/shard_map/ppermute | solution.py:301
  25.7 19.0 %collective-permute-start = (bf16[1024,128]{1,0:T(8,128)(2,1)S(1)}, bf16[1024,128]{1,0:T(8,128)(2,1)S(1)}, u32[]{:S(2)}, u32[]{:S(2)}) collective-permute-start(bf16[1024,128]{1,0:T(8,128)(2,1)S(1)} %get-tuple-element.44.refs_0_), channel_id=1, source_target_pairs={{0,4},{4,0},{8,12},{12,8},{16,20},{20,16},{24,28},{28,24},{1,5},{5... | collective-permute-start | bytes 786440 | tf_op jit(solution)/shard_map/ppermute | solution.py:301
  26.7 28.7 %collective-permute-start.10 = (bf16[1024,128]{1,0:T(8,128)(2,1)S(1)}, bf16[1024,128]{1,0:T(8,128)(2,1)S(1)}, u32[]{:S(2)}, u32[]{:S(2)}) collective-permute-start(bf16[1024,128]{1,0:T(8,128)(2,1)S(1)} %copy-done.11), channel_id=1, source_target_pairs={{0,16},{4,20},{8,24},{12,28},{16,0},{20,4},{24,8},{28,12},{1,17},{... | collective-permute-start | bytes 786440 | tf_op jit(solution)/shard_map/ppermute | solution.py:301
  31.4 24.1 %collective-permute-start.12 = (bf16[1024,128]{1,0:T(8,128)(2,1)S(1)}, bf16[1024,128]{1,0:T(8,128)(2,1)S(1)}, u32[]{:S(2)}, u32[]{:S(2)}) collective-permute-start(bf16[1024,128]{1,0:T(8,128)(2,1)S(1)} %copy-done.11), channel_id=1, source_target_pairs={{0,24},{4,28},{8,16},{12,20},{16,8},{20,12},{24,0},{28,4},{1,25},{... | collective-permute-start | bytes 786440 | tf_op jit(solution)/shard_map/ppermute | solution.py:301
  43.0 12.9 %collective-permute-start.8 = (bf16[1024,128]{1,0:T(8,128)(2,1)S(1)}, bf16[1024,128]{1,0:T(8,128)(2,1)S(1)}, u32[]{:S(2)}, u32[]{:S(2)}) collective-permute-start(bf16[1024,128]{1,0:T(8,128)(2,1)S(1)} %copy-done.11), channel_id=1, source_target_pairs={{0,8},{4,12},{8,0},{12,4},{16,24},{20,28},{24,16},{28,20},{1,9},{5... | collective-permute-start | bytes 786440 | tf_op jit(solution)/shard_map/ppermute | solution.py:301
  44.7 11.3 %collective-permute-start.7 = (bf16[1024,128]{1,0:T(8,128)(2,1)S(1)}, bf16[1024,128]{1,0:T(8,128)(2,1)S(1)}, u32[]{:S(2)}, u32[]{:S(2)}) collective-permute-start(bf16[1024,128]{1,0:T(8,128)(2,1)S(1)} %copy-done.11), channel_id=1, source_target_pairs={{0,4},{4,0},{8,12},{12,8},{16,20},{20,16},{24,28},{28,24},{1,5},{5... | collective-permute-start | bytes 786440 | tf_op jit(solution)/shard_map/ppermute | solution.py:301
  44.8 11.7 %collective-permute-start.2 = (bf16[1024,128]{1,0:T(8,128)(2,1)S(1)}, bf16[1024,128]{1,0:T(8,128)(2,1)S(1)}, u32[]{:S(2)}, u32[]{:S(2)}) collective-permute-start(bf16[1024,128]{1,0:T(8,128)(2,1)S(1)} %collective-permute-done.1.refs_2_), channel_id=1, source_target_pairs={{0,4},{4,0},{8,12},{12,8},{16,20},{20,16},{24,28},{28,24},{1,5},{5... | collective-permute-start | bytes 786440 | tf_op jit(solution)/shard_map/ppermute | solution.py:301
  89.2 8.9 %collective-permute-start.21 = (bf16[1024,128]{1,0:T(8,128)(2,1)S(1)}, bf16[1024,128]{1,0:T(8,128)(2,1)S(1)}, u32[]{:S(2)}, u32[]{:S(2)}) collective-permute-start(bf16[1024,128]{1,0:T(8,128)(2,1)S(1)} %get-tuple-element.54), channel_id=1, source_target_pairs={{0,16},{4,20},{8,24},{12,28},{16,0},{20,4},{24,8},{28,12},{1,17},{... | collective-permute-start | bytes 786440 | tf_op jit(solution)/shard_map/ppermute | solution.py:301
  97.6 32.4 %collective-permute-start.34 = (bf16[4,128,896]{2,1,0:T(8,128)(2,1)}, bf16[4,128,896]{2,1,0:T(8,128)(2,1)S(1)}, u32[]{:S(2)}, u32[]{:S(2)}) collective-permute-start(bf16[4,128,896]{2,1,0:T(8,128)(2,1)} %get-tuple-element.31), channel_id=1, source_target_pairs={{0,4},{4,0},{8,12},{12,8},{16,20},{20,16},{24,28},{28,24},{1,5},{5... | collective-permute-start | bytes 2752520 | tf_op jit(solution)/shard_map/ppermute | solution.py:301
  98.0 9.1 %collective-permute-start.20 = (bf16[1024,128]{1,0:T(8,128)(2,1)S(1)}, bf16[1024,128]{1,0:T(8,128)(2,1)S(1)}, u32[]{:S(2)}, u32[]{:S(2)}) collective-permute-start(bf16[1024,128]{1,0:T(8,128)(2,1)S(1)} %copy-done.26), channel_id=1, source_target_pairs={{0,8},{4,12},{8,0},{12,4},{16,24},{20,28},{24,16},{28,20},{1,9},{5... | collective-permute-start | bytes 786440 | tf_op jit(solution)/shard_map/ppermute | solution.py:301
  98.0 34.7 %collective-permute-start.15 = (bf16[4096,128]{1,0:T(8,128)(2,1)}, bf16[4096,128]{1,0:T(8,128)(2,1)S(1)}, u32[]{:S(2)}, u32[]{:S(2)}) collective-permute-start(bf16[4096,128]{1,0:T(8,128)(2,1)} %get-tuple-element.26), channel_id=1, source_target_pairs={{0,4},{4,0},{8,12},{12,8},{16,20},{20,16},{24,28},{28,24},{1,5},{5... | collective-permute-start | bytes 3145736 | tf_op jit(solution)/shard_map/ppermute | solution.py:301
  98.9 11.6 %collective-permute-start.23 = (bf16[512,128]{1,0:T(8,128)(2,1)S(1)}, bf16[512,128]{1,0:T(8,128)(2,1)S(1)}, u32[]{:S(2)}, u32[]{:S(2)}) collective-permute-start(bf16[512,128]{1,0:T(8,128)(2,1)S(1)} %get-tuple-element.71), channel_id=1, source_target_pairs={{0,8},{4,12},{8,0},{12,4},{16,24},{20,28},{24,16},{28,20},{1,9},{5... | collective-permute-start | bytes 393224 | tf_op jit(solution)/shard_map/ppermute | solution.py:301
  108.9 5.0 %collective-permute-start.22 = (bf16[512,128]{1,0:T(8,128)(2,1)S(1)}, bf16[512,128]{1,0:T(8,128)(2,1)S(1)}, u32[]{:S(2)}, u32[]{:S(2)}) collective-permute-start(bf16[512,128]{1,0:T(8,128)(2,1)S(1)} %get-tuple-element.73), channel_id=1, source_target_pairs={{0,16},{4,20},{8,24},{12,28},{16,0},{20,4},{24,8},{28,12},{1,17},{... | collective-permute-start | bytes 393224 | tf_op jit(solution)/shard_map/ppermute | solution.py:301
  110.5 24.3 %collective-permute-start.32 = (bf16[4,128,896]{2,1,0:T(8,128)(2,1)}, bf16[4,128,896]{2,1,0:T(8,128)(2,1)S(1)}, u32[]{:S(2)}, u32[]{:S(2)}) collective-permute-start(bf16[4,128,896]{2,1,0:T(8,128)(2,1)} %get-tuple-element.29), channel_id=1, source_target_pairs={{0,4},{4,0},{8,12},{12,8},{16,20},{20,16},{24,28},{28,24},{1,5},{5... | collective-permute-start | bytes 2752520 | tf_op jit(solution)/shard_map/ppermute | solution.py:301
  116.3 13.0 %collective-permute-start.29 = (bf16[1024,128]{1,0:T(8,128)(2,1)}, bf16[1024,128]{1,0:T(8,128)(2,1)S(1)}, u32[]{:S(2)}, u32[]{:S(2)}) collective-permute-start(bf16[1024,128]{1,0:T(8,128)(2,1)} %shard_map.160.refs_0_), channel_id=1, source_target_pairs={{0,2},{2,0},{1,3},{3,1},{4,6},{6,4},{5,7},{7,5},{8,10},{10,8},{9,1... | collective-permute-start | bytes 786440 | tf_op jit(solution)/shard_map/ppermute | solution.py:277
  118.9 36.7 %collective-permute-start.24 = (bf16[1024,128]{1,0:T(8,128)(2,1)}, bf16[1024,128]{1,0:T(8,128)(2,1)S(1)}, u32[]{:S(2)}, u32[]{:S(2)}) collective-permute-start(bf16[1024,128]{1,0:T(8,128)(2,1)} %shard_map.160.refs_0_), channel_id=1, source_target_pairs={{0,1},{1,0},{2,3},{3,2},{4,5},{5,4},{6,7},{7,6},{8,9},{9,8},{10,11... | collective-permute-start | bytes 786440 | tf_op jit(solution)/shard_map/ppermute | solution.py:277
  129.3 37.0 %collective-permute-start.30 = (bf16[1024,128]{1,0:T(8,128)(2,1)}, bf16[1024,128]{1,0:T(8,128)(2,1)S(1)}, u32[]{:S(2)}, u32[]{:S(2)}) collective-permute-start(bf16[1024,128]{1,0:T(8,128)(2,1)} %shard_map.160.refs_0_), channel_id=1, source_target_pairs={{1,2},{2,1},{5,6},{6,5},{9,10},{10,9},{13,14},{14,13},{17,18},{18,... | collective-permute-start | bytes 786440 | tf_op jit(solution)/shard_map/ppermute | solution.py:277
  130.0 39.7 %collective-permute-start.31 = (bf16[1024,128]{1,0:T(8,128)(2,1)S(1)}, bf16[1024,128]{1,0:T(8,128)(2,1)S(1)}, u32[]{:S(2)}, u32[]{:S(2)}) collective-permute-start(bf16[1024,128]{1,0:T(8,128)(2,1)S(1)} %collective-permute-done.29.refs_2_), channel_id=1, source_target_pairs={{1,0},{2,3},{5,4},{6,7},{9,8},{10,11},{13,12},{14,15},{17,16},{18,... | collective-permute-start | bytes 786440 | tf_op jit(solution)/shard_map/ppermute | solution.py:277
  133.0 7.2 %collective-permute-start.17 = (bf16[1024,128]{1,0:T(8,128)(2,1)S(1)}, bf16[1024,128]{1,0:T(8,128)(2,1)S(1)}, u32[]{:S(2)}, u32[]{:S(2)}) collective-permute-start(bf16[1024,128]{1,0:T(8,128)(2,1)S(1)} %get-tuple-element.58), channel_id=1, source_target_pairs={{0,16},{4,20},{8,24},{12,28},{16,0},{20,4},{24,8},{28,12},{1,17},{... | collective-permute-start | bytes 786440 | tf_op jit(solution)/shard_map/ppermute | solution.py:301
  134.8 7.9 %collective-permute-start.16 = (bf16[1024,128]{1,0:T(8,128)(2,1)S(1)}, bf16[1024,128]{1,0:T(8,128)(2,1)S(1)}, u32[]{:S(2)}, u32[]{:S(2)}) collective-permute-start(bf16[1024,128]{1,0:T(8,128)(2,1)S(1)} %get-tuple-element.59), channel_id=1, source_target_pairs={{0,8},{4,12},{8,0},{12,4},{16,24},{20,28},{24,16},{28,20},{1,9},{5... | collective-permute-start | bytes 786440 | tf_op jit(solution)/shard_map/ppermute | solution.py:301
  140.2 10.4 %collective-permute-start.35 = (bf16[2,128,896]{2,1,0:T(8,128)(2,1)S(1)}, bf16[2,128,896]{2,1,0:T(8,128)(2,1)S(1)}, u32[]{:S(2)}, u32[]{:S(2)}) collective-permute-start(bf16[2,128,896]{2,1,0:T(8,128)(2,1)S(1)} %get-tuple-element.62), channel_id=1, source_target_pairs={{0,16},{4,20},{8,24},{12,28},{16,0},{20,4},{24,8},{28,12},{1,17},{... | collective-permute-start | bytes 1376264 | tf_op jit(solution)/shard_map/ppermute | solution.py:301
  142.7 12.1 %collective-permute-start.33 = (bf16[2,128,896]{2,1,0:T(8,128)(2,1)S(1)}, bf16[2,128,896]{2,1,0:T(8,128)(2,1)S(1)}, u32[]{:S(2)}, u32[]{:S(2)}) collective-permute-start(bf16[2,128,896]{2,1,0:T(8,128)(2,1)S(1)} %get-tuple-element.64), channel_id=1, source_target_pairs={{0,8},{4,12},{8,0},{12,4},{16,24},{20,28},{24,16},{28,20},{1,9},{5... | collective-permute-start | bytes 1376264 | tf_op jit(solution)/shard_map/ppermute | solution.py:301
  150.6 7.0 %collective-permute-start.19 = (bf16[512,128]{1,0:T(8,128)(2,1)S(1)}, bf16[512,128]{1,0:T(8,128)(2,1)S(1)}, u32[]{:S(2)}, u32[]{:S(2)}) collective-permute-start(bf16[512,128]{1,0:T(8,128)(2,1)S(1)} %get-tuple-element.75), channel_id=1, source_target_pairs={{0,8},{4,12},{8,0},{12,4},{16,24},{20,28},{24,16},{28,20},{1,9},{5... | collective-permute-start | bytes 393224 | tf_op jit(solution)/shard_map/ppermute | solution.py:301
  155.7 18.1 %collective-permute-start.37 = (bf16[1,128,896]{2,1,0:T(8,128)(2,1)S(1)}, bf16[1,128,896]{2,1,0:T(8,128)(2,1)S(1)}, u32[]{:S(2)}, u32[]{:S(2)}) collective-permute-start(bf16[1,128,896]{2,1,0:T(8,128)(2,1)S(1)} %get-tuple-element.67), channel_id=1, source_target_pairs={{0,8},{4,12},{8,0},{12,4},{16,24},{20,28},{24,16},{28,20},{1,9},{5... | collective-permute-start | bytes 688136 | tf_op jit(solution)/shard_map/ppermute | solution.py:301
  157.6 16.2 %collective-permute-start.36 = (bf16[1,128,896]{2,1,0:T(8,128)(2,1)S(1)}, bf16[1,128,896]{2,1,0:T(8,128)(2,1)S(1)}, u32[]{:S(2)}, u32[]{:S(2)}) collective-permute-start(bf16[1,128,896]{2,1,0:T(8,128)(2,1)S(1)} %get-tuple-element.69), channel_id=1, source_target_pairs={{0,16},{4,20},{8,24},{12,28},{16,0},{20,4},{24,8},{28,12},{1,17},{... | collective-permute-start | bytes 688136 | tf_op jit(solution)/shard_map/ppermute | solution.py:301
  162.8 11.0 %collective-permute-start.25 = (bf16[1024,128]{1,0:T(8,128)(2,1)}, bf16[1024,128]{1,0:T(8,128)(2,1)S(1)}, u32[]{:S(2)}, u32[]{:S(2)}) collective-permute-start(bf16[1024,128]{1,0:T(8,128)(2,1)} %shard_map.161.refs_0_), channel_id=1, source_target_pairs={{0,1},{1,0},{2,3},{3,2},{4,5},{5,4},{6,7},{7,6},{8,9},{9,8},{10,11... | collective-permute-start | bytes 786440 | tf_op jit(solution)/shard_map/ppermute | solution.py:277
  166.3 13.5 %collective-permute-start.26 = (bf16[1024,128]{1,0:T(8,128)(2,1)}, bf16[1024,128]{1,0:T(8,128)(2,1)S(1)}, u32[]{:S(2)}, u32[]{:S(2)}) collective-permute-start(bf16[1024,128]{1,0:T(8,128)(2,1)} %shard_map.161.refs_0_), channel_id=1, source_target_pairs={{0,2},{2,0},{1,3},{3,1},{4,6},{6,4},{5,7},{7,5},{8,10},{10,8},{9,1... | collective-permute-start | bytes 786440 | tf_op jit(solution)/shard_map/ppermute | solution.py:277
  169.7 10.2 %collective-permute-start.27 = (bf16[1024,128]{1,0:T(8,128)(2,1)}, bf16[1024,128]{1,0:T(8,128)(2,1)S(1)}, u32[]{:S(2)}, u32[]{:S(2)}) collective-permute-start(bf16[1024,128]{1,0:T(8,128)(2,1)} %shard_map.161.refs_0_), channel_id=1, source_target_pairs={{1,2},{2,1},{5,6},{6,5},{9,10},{10,9},{13,14},{14,13},{17,18},{18,... | collective-permute-start | bytes 786440 | tf_op jit(solution)/shard_map/ppermute | solution.py:277
  184.4 11.7 %collective-permute-start.28 = (bf16[1024,128]{1,0:T(8,128)(2,1)}, bf16[1024,128]{1,0:T(8,128)(2,1)S(1)}, u32[]{:S(2)}, u32[]{:S(2)}) collective-permute-start(bf16[1024,128]{1,0:T(8,128)(2,1)} %copy-done.4), channel_id=1, source_target_pairs={{1,0},{2,3},{5,4},{6,7},{9,8},{10,11},{13,12},{14,15},{17,16},{18,... | collective-permute-start | bytes 786440 | tf_op jit(solution)/shard_map/ppermute | solution.py:277
  (48 other events, 520.7 us)

commit v7 on v5

--- a/solution.py
+++ b/solution.py
@@ -313,8 +313,7 @@
     return left.astype(jnp.float32) + right.astype(jnp.float32)
 
 
-def chip_sum(keep, send):
-    received = swap(send, 1)
+def chip_sum(keep, received):
     count = lax.axis_size("dp") // 2
     rows = keep.shape[0] // count
     total = [
@@ -328,28 +327,31 @@
     return [swap(item, 2 * at + 2) for at, item in enumerate(sends)]
 
 
-def final_kernel(count, rotary, *refs):
+def final_kernel(count, rotary, out_at, *refs):
     total = refs[0][...].astype(jnp.float32)
     for ref in refs[1 : 1 + count]:
         total = total + ref[...].astype(jnp.float32)
     if rotary:
         total = total * refs[1 + count][...] - pltpu.roll(total, HD // 2, 1) * refs[2 + count][...]
-    out_ref = refs[-1]
-    out_ref[...] = total.astype(out_ref.dtype)
-
-
-def final_sum(keep, received, tables, after, kind=jnp.bfloat16):
+    refs[out_at][...] = total.astype(refs[out_at].dtype)
+
+
+def final_sum(keep, received, tables, after, kind=jnp.bfloat16, thru=()):
     vmem = pl.BlockSpec(memory_space=pltpu.VMEM)
     hbm = pl.BlockSpec(memory_space=pl.ANY)
     parts = [keep, *received, *tables]
-    return pl.pallas_call(
-        partial(final_kernel, len(received), len(tables) > 0),
-        out_shape=jax.ShapeDtypeStruct(keep.shape, kind),
-        in_specs=[vmem] * len(parts) + [hbm] * len(after),
-        out_specs=vmem,
+    inputs = len(parts) + len(after) + len(thru)
+    results = pl.pallas_call(
+        partial(final_kernel, len(received), len(tables) > 0, inputs),
+        out_shape=[jax.ShapeDtypeStruct(keep.shape, kind)]
+        + [jax.ShapeDtypeStruct(item.shape, item.dtype) for item in thru],
+        in_specs=[vmem] * len(parts) + [hbm] * (len(after) + len(thru)),
+        out_specs=[vmem] + [hbm] * len(thru),
+        input_output_aliases={inputs - len(thru) + at: 1 + at for at in range(len(thru))},
         compiler_params=pltpu.CompilerParams(vmem_limit_bytes=VMEM_BYTES),
         cost_estimate=NO_COST,
-    )(*parts, *after)
+    )(*parts, *after, *thru)
+    return results if thru else results[0]
 
 
 def up_kernel(rows_ref, weight_ref, *refs):
@@ -371,83 +373,51 @@
         + [pl.BlockSpec(memory_space=pl.ANY)] * len(after),
         out_specs=pl.BlockSpec((height // steps, weight.shape[1]), lambda step: (step, 0)),
         compiler_params=pltpu.CompilerParams(vmem_limit_bytes=VMEM_BYTES),
-        cost_estimate=NO_COST,
+        cost_estimate=pl.CostEstimate(
+            flops=2 * height * weight.size, bytes_accessed=2 * rows.size, transcendentals=0
+        ),
     )(rows, weight, *after)
 
 
-def product_kernel(my_ref, left_ref, right_ref, thru_ref, out_ref, unused):
-    total = jnp.dot(left_ref[0], right_ref[...], preferred_element_type=jnp.float32)
-    out_ref[0] = total.astype(out_ref.dtype)
-
-
-def product_sum_kernel(count, my_ref, left_ref, right_ref, base_ref, *refs):
-    total = jnp.dot(left_ref[0], right_ref[...], preferred_element_type=jnp.float32)
-    total = total + base_ref[0].astype(jnp.float32)
-    for at, out_ref in enumerate(refs[-count:]):
-
-        @pl.when(pl.program_id(0) == at)
-        def store():
-            out_ref[...] = total.astype(out_ref.dtype)
-
-
-def product_specs(left, which, right):
+def product_kernel(my_ref, left_ref, right_ref, *refs):
+    keep_ref, send_ref = refs[-3:-1]
+    half = left_ref.shape[1]
+    left = left_ref[...].reshape(2 * half, left_ref.shape[2])
+    total = jnp.dot(left, right_ref[...], preferred_element_type=jnp.float32)
+    keep_ref[0] = total[:half].astype(keep_ref.dtype)
+    send_ref[0] = total[half:].astype(send_ref.dtype)
+
+
+def product(mine, left, right, thru, after):
     count = lax.axis_size("dp") // 2
-    rows, cols = left.shape[1], right.shape[1] // count
-    stacked = pl.BlockSpec((1, rows, cols), lambda step, my_ref: (step, 0, 0))
-    ins = [
-        pl.BlockSpec((1,) + left.shape[1:], lambda step, my_ref: (which, 0, 0)),
-        pl.BlockSpec((right.shape[0], cols), lambda step, my_ref: (0, step ^ my_ref[0])),
-    ]
-    return count, rows, cols, stacked, ins
-
-
-def plain_pieces(mine, left, right):
-    count = lax.axis_size("dp") // 2
-    total = jnp.dot(left, right, preferred_element_type=jnp.float32)
-    pieces = jnp.moveaxis(total.reshape(left.shape[0], count, -1), 1, 0)
-    return jnp.take(pieces, jnp.arange(count, dtype=jnp.int32) ^ mine, axis=0)
-
-
-def product(mine, left, right, thru):
-    count, rows, cols, stacked, ins = product_specs(left, 1, right)
+    half, depth = left.shape[1:]
+    cols = right.shape[1] // count
     if cols % 128:
-        return plain_pieces(mine, left[1], right).astype(jnp.bfloat16), thru
+        total = jnp.dot(left.reshape(2 * half, depth), right, preferred_element_type=jnp.float32)
+        pieces = jnp.moveaxis(total.astype(jnp.bfloat16).reshape(2 * half, count, cols), 1, 0)
+        pieces = jnp.take(pieces, jnp.arange(count, dtype=jnp.int32) ^ mine, axis=0)
+        return pieces[:, :half], pieces[:, half:], thru
     hbm = pl.BlockSpec(memory_space=pl.ANY)
+    stacked = pl.BlockSpec((1, half, cols), lambda step, my_ref: (step, 0, 0))
+    stack = jax.ShapeDtypeStruct((count, half, cols), jnp.bfloat16)
+    inputs = [mine.reshape(1), left, right, *after, thru]
     return pl.pallas_call(
         product_kernel,
         grid_spec=pltpu.PrefetchScalarGridSpec(
-            num_scalar_prefetch=1, grid=(count,), in_specs=ins + [hbm], out_specs=[stacked, hbm]
+            num_scalar_prefetch=1,
+            grid=(count,),
+            in_specs=[
+                pl.BlockSpec(left.shape, lambda step, my_ref: (0, 0, 0)),
+                pl.BlockSpec((depth, cols), lambda step, my_ref: (0, step ^ my_ref[0])),
+            ]
+            + [hbm] * (len(after) + 1),
+            out_specs=[stacked, stacked, hbm],
         ),
-        out_shape=[
-            jax.ShapeDtypeStruct((count, rows, cols), jnp.bfloat16),
-            jax.ShapeDtypeStruct(thru.shape, thru.dtype),
-        ],
-        input_output_aliases={3: 1},
+        out_shape=[stack, stack, jax.ShapeDtypeStruct(thru.shape, thru.dtype)],
+        input_output_aliases={len(inputs) - 1: 2},
         compiler_params=pltpu.CompilerParams(vmem_limit_bytes=VMEM_BYTES),
         cost_estimate=NO_COST,
-    )(mine.reshape(1), left, right, thru)
-
-
-def product_sum(mine, left, right, base, after):
-    count, rows, cols, stacked, ins = product_specs(left, 0, right)
-    if cols % 128:
-        pieces = plain_pieces(mine, left[0], right) + base.astype(jnp.float32)
-        return [pieces[0]] + [pieces[at].astype(jnp.bfloat16) for at in range(1, count)]
-    return pl.pallas_call(
-        partial(product_sum_kernel, count),
-        grid_spec=pltpu.PrefetchScalarGridSpec(
-            num_scalar_prefetch=1,
-            grid=(count,),
-            in_specs=ins + [stacked] + [pl.BlockSpec(memory_space=pl.ANY)] * len(after),
-            out_specs=[pl.BlockSpec((rows, cols), lambda step, my_ref: (0, 0))] * count,
-        ),
-        out_shape=[
-            jax.ShapeDtypeStruct((rows, cols), jnp.bfloat16 if at else jnp.float32)
-            for at in range(count)
-        ],
-        compiler_params=pltpu.CompilerParams(vmem_limit_bytes=VMEM_BYTES),
-        cost_estimate=NO_COST,
-    )(mine.reshape(1), left, right, base, *after)
+    )(*inputs)
 
 
 def local(query, key, value, grad_out, out_weight, plan, segments):
@@ -502,22 +472,27 @@
     grad_query, attn_t, gkey_keep, gkey_send, gvalue_keep, gvalue_send = attend(
         tables, query, up, cosine, sine, places, keys, values
     )
-    mine_pair = my_rank // 2
-    value_keep, value_sends = chip_sum(gvalue_keep, gvalue_send)
+    value_keep, value_sends = chip_sum(gvalue_keep, swap(gvalue_send, 1))
     value_received = exchange(value_sends)
-    first, gkey_keep = product(mine_pair, attn_t, grad_out, gkey_keep)
-    first = swap(first, 1)
-    key_keep, key_sends = chip_sum(gkey_keep, gkey_send)
+    key_keep, key_sends = chip_sum(gkey_keep, swap(gkey_send, 1))
     key_received = exchange(key_sends)
-    value_partial = final_sum(value_keep, value_received, (), key_sends)
+    weight_keep, weight_send, value_keep = product(
+        my_rank // 2, attn_t, grad_out, value_keep, [value_sends[0], key_sends[0]]
+    )
+    value_partial, weight_send = final_sum(
+        value_keep, value_received, (), (), thru=[weight_send]
+    )
     value_all, value_pieces = lane_gather(value_partial, my_lane)
-    kept, *sends = product_sum(mine_pair, attn_t, grad_out, first, [value_partial])
-    received = exchange(sends)
-    key_partial = final_sum(
-        key_keep, key_received, (cosine, sine), [sends[0], value_pieces[0], value_pieces[2]]
+    weight_other = swap(weight_send, 1)
+    key_partial, weight_keep = final_sum(
+        key_keep, key_received, (cosine, sine), value_pieces[:1], thru=[weight_keep]
     )
     key_all, key_pieces = lane_gather(key_partial, my_lane)
-    total = final_sum(kept, received, (), key_pieces[:3] + value_pieces[3:], jnp.float32)
+    weight_keep, weight_sends = chip_sum(weight_keep, weight_other)
+    weight_received = exchange(weight_sends)
+    total = final_sum(
+        weight_keep, weight_received, (), [*key_pieces[:3], value_all], jnp.float32
+    )[0]
     odd = my_rank & 1
     pair_rows = grad_out.shape[1] // (rank_count // 2)
     low, high = total[:, : pair_rows // 2], total[:, pair_rows // 2 :]

time: 159 us -> 154 us (0.969)
  waiting for transfers between devices: 41.8 us -> 33 us
  Pallas kernels: 58.5 us -> 52.5 us
  other arithmetic: 14.3 us -> 19.5 us
  starting transfers between devices: 36.1 us -> 39.5 us
    pallas_call x4 -> x3, Pallas kernels: 14.6 us -> 7.36 us  [final_sum(): pl.pallas_call(partial(final_kernel, len(received), len(tables) > 0, inpu...]
    ppermute x27, waiting for transfers between devices: 22.3 us -> 15.4 us  [swap(): lax.ppermute(array, 'dp', [(rank, rank ^ bit) for rank in range(ranks)])]
    convert_element_type x2 -> x3, other arithmetic: 2.18 us -> 6.7 us  [chip_sum(): return (total[0], [item.astype(keep.dtype) for item in total[1:]])]
    ppermute x27, starting transfers between devices: 18.3 us -> 20.8 us  [swap(): lax.ppermute(array, 'dp', [(rank, rank ^ bit) for rank in range(ranks)])]
    pallas_call x1, Pallas kernels: 6.53 us -> 8.37 us  [product(): pl.pallas_call(product_kernel, grid_spec=pltpu.PrefetchScalarGridSpec(num...]
    all_to_all x1, waiting for transfers between devices: 4.66 us -> 2.94 us  [local(): lax.all_to_all(jnp.broadcast_to(own_places, (rank_count, block_count, ROW...]
    unnamed x89 -> x85, local copies, waits for them, and re-layouts: 5.88 us -> 6.19 us
  transfers between devices with their start and end apart: 36 -> 36, of which waited for: 10 -> 13; matrix products, arithmetic and copies ran while one was open for 10% -> 14% of each run, Pallas kernels for 21% -> 17%
where the time goes in v7:
time: 154 us
  Pallas kernels  52.5 us (34%)
  starting transfers between devices  39.5 us (26%)
  waiting for transfers between devices  33 us (21%)
  other arithmetic  19.5 us (13%)
  local copies, waits for them, and re-layouts  7.91 us (5%)
    pallas_call x1, Pallas kernels, attend(): pl.pallas_call(partial(attend_kernel, heads, ranks), out_shape=(jax.Shape...  23.8 us
    ppermute x27, starting transfers between devices, swap(): lax.ppermute(array, 'dp', [(rank, rank ^ bit) for rank in range(ranks)])  20.8 us
    ppermute x27, waiting for transfers between devices, swap(): lax.ppermute(array, 'dp', [(rank, rank ^ bit) for rank in range(ranks)])  15.4 us
    ppermute x8, waiting for transfers between devices, send(): return lax.ppermute(item, 'tensor', pairs)  14.6 us
    ppermute x8, starting transfers between devices, send(): return lax.ppermute(item, 'tensor', pairs)  14.4 us
    pallas_call x1, Pallas kernels, product(): pl.pallas_call(product_kernel, grid_spec=pltpu.PrefetchScalarGridSpec(num...  8.37 us
    pallas_call x1, Pallas kernels, up_product(): pl.pallas_call(up_kernel, grid=(steps,), out_shape=jax.ShapeDtypeStruct((...  8.36 us
    pallas_call x3, Pallas kernels, final_sum(): pl.pallas_call(partial(final_kernel, len(received), len(tables) > 0, inpu...  7.36 us
  transfers between devices with their start and end apart: 36, of which 13 were waited for; matrix products, arithmetic and copies ran while one was open for 14% of the time, Pallas kernels for 17%

profile of v7, /device:TPU:0, one launch (start us, length us, event | category | flops | bytes accessed | tf_op | source)
XLA Modules:
  0.0 153.6 jit_solution(4472816058560039570)
XLA Ops:
  1.9 3.0 %collective-permute-start.10 = (bf16[1024,128]{1,0:T(8,128)(2,1)S(1)}, bf16[1024,128]{1,0:T(8,128)(2,1)S(1)}, u32[]{:S(2)}, u32[]{:S(2)}) collective-permute-start(bf16[1024,128]{1,0:T(8,128)(2,1)S(1)} %constant_dynamic-slice_fusion.refs_8_), channel_id=1, source_target_pairs={{0,16},{4,20},{8,24},{12,28},{16,0},{20,4},{24,8},{28,12},{1,17},{... | collective-permute-start | bytes 786440 | tf_op jit(solution)/shard_map/ppermute | solution.py:301
  4.9 1.4 collective-permute-start.12
  8.6 4.3 %all-to-all-start = ((s32[8,8,128]{2,1,0:T(8,128)}), s32[8,8,128]{2,1,0:T(8,128)S(1)}, u32[]{:S(2)}, u32[]{:S(2)}) async-start(s32[8,8,128]{2,1,0:T(8,128)} %broadcast_in_dim.40), calls=%async_computation | async-start | bytes 65536 | tf_op jit(solution)/shard_map/all_to_all | solution.py:437
  16.7 2.9 %all-to-all-done = s32[8,8,128]{2,1,0:T(8,128)S(1)} async-done(((s32[8,8,128]{2,1,0:T(8,128)}), s32[8,8,128]{2,1,0:T(8,128)S(1)}, u32[]{:S(2)}, u32[]{:S(2)}) %all-to-all-start) | async-done | bytes 32800 | tf_op jit(solution)/shard_map/all_to_all | solution.py:437
  20.3 1.9 %fusion.5 = (f32[1024,64]{1,0:T(8,128)S(1)}, f32[1024,64]{1,0:T(8,128)S(1)}, f32[1024,64]{1,0:T(8,128)S(1)}) fusion(f32[64]{0:T(128)S(1)} %multiply_add_fusion.1, f32[1024]{0:T(1024)S(1)} %get-tuple-element.44), kind=kLoop, calls=%fused_computation.29 | loop fusion | flops 262144 | bytes 790784 | tf_op jit(solution)/shard_map/neg | solution.py:69
  22.2 2.4 %fusion.4 = (bf16[1024,128]{1,0:T(8,128)(2,1)S(1)}, f32[1024,128]{1,0:T(8,128)}, f32[1024,128]{1,0:T(8,128)}) fusion(f32[1024,64]{1,0:T(8,128)S(1)} %get-tuple-element.67, f32[1024,64]{1,0:T(8,128)S(1)} %get-tuple-element.66, bf16[1024,512]{1,0:T(8,128)(2,1)} %param.14, s32[]{:T(128)S(6)} %select_n.100, f32[1024,64]{1,0:T(8,128)S(1)} %get-tuple-element.70, ...), kind=kLoop, calls=%fused_computation.16 | loop fusion | flops 1048576 | bytes 2883588 | tf_op jit(solution)/shard_map/convert_element_type | solution.py:457
  24.7 1.4 collective-permute-start.1
  26.7 1.4 collective-permute-start.5
  28.7 8.4 %shard_map.156.up_ref = bf16[1024,512]{1,0:T(8,128)(2,1)} custom-call(bf16[1024,3584]{1,0:T(8,128)(2,1)} %right_ref.1, bf16[3584,512]{1,0:T(8,128)(2,1)} %weight_ref.1, bf16[1024,128]{1,0:T(8,128)(2,1)} %copy-done.2), custom_call_target="tpu_custom_call" | custom-call | flops 3758096384 | bytes 7340032 | tf_op jit(solution)/shard_map/pallas_call | solution.py:365
  37.2 2.1 %collective-permute-done.3.refs_4_ = bf16[1024,128]{1,0:T(8,128)(2,1)S(1)} collective-permute-done((bf16[1024,128]{1,0:T(8,128)(2,1)S(1)}, bf16[1024,128]{1,0:T(8,128)(2,1)S(1)}, u32[]{:S(2)}, u32[]{:S(2)}) %collective-permute-start.3) | collective-permute-done | bytes 262176 | tf_op jit(solution)/shard_map/ppermute | solution.py:301
  42.8 23.8 %shard_map.157 = (bf16[1024,512]{1,0:T(8,128)(2,1)}, bf16[2,256,1024]{2,1,0:T(8,128)(2,1)}, bf16[4096,128]{1,0:T(8,128)(2,1)}, bf16[4096,128]{1,0:T(8,128)(2,1)}...) custom-call(s32[64]{0:T(128)} %multiply_add_fusion.3.target_ref, s32[64]{0:T(128)} %get-tuple-element.48.source_ref, ...), custom_call_target="tpu_custom_call" | custom-call | tf_op jit(solution)/shard_map/pallas_call | solution.py:223
  67.2 3.2 %collective-permute-done.18 = bf16[4096,128]{1,0:T(8,128)(2,1)} collective-permute-done((bf16[4096,128]{1,0:T(8,128)(2,1)}, bf16[4096,128]{1,0:T(8,128)(2,1)}, u32[]{:S(2)}, u32[]{:S(2)}) %collective-permute-start.18) | collective-permute-done | bytes 1048608 | tf_op jit(solution)/shard_map/ppermute | solution.py:301
  70.4 2.6 %add_convert_fusion.3 = (bf16[1024,128]{1,0:T(8,128)(2,1)S(1)}, bf16[1024,128]{1,0:T(8,128)(2,1)S(1)}, f32[1024,128]{1,0:T(8,128)}, bf16[1024,128]{1,0:T(8,128)(2,1)S(1)}) fusion(bf16[4096,128]{1,0:T(8,128)(2,1)} %collective-permute-done.18, bf16[4096,128]{1,0:T(8,128)(2,1)} %get-tuple-element.21), kind=kLoop, calls=%fused_computation.19 | loop fusion | flops 1966080 | bytes 3407872 | tf_op jit(solution)/shard_map/convert_element_type | solution.py:323
  74.1 2.3 %collective-permute-start.21 = (bf16[1024,128]{1,0:T(8,128)(2,1)S(1)}, bf16[1024,128]{1,0:T(8,128)(2,1)S(1)}, u32[]{:S(2)}, u32[]{:S(2)}) collective-permute-start(bf16[1024,128]{1,0:T(8,128)(2,1)S(1)} %get-tuple-element.55), channel_id=1, source_target_pairs={{0,24},{4,28},{8,16},{12,20},{16,8},{20,12},{24,0},{28,4},{1,25},{... | collective-permute-start | bytes 786440 | tf_op jit(solution)/shard_map/ppermute | solution.py:301
  77.6 8.4 %shard_map.158 = (bf16[4,256,896]{2,1,0:T(8,128)(2,1)}, bf16[4,256,896]{2,1,0:T(8,128)(2,1)}, f32[1024,128]{1,0:T(8,128)}) custom-call(s32[1]{0:T(128)} %bitcast.6.my_ref, bf16[2,256,1024]{2,1,0:T(8,128)(2,1)} %get-tuple-element.20.left_ref, bf16[1024,3584]{1,0:T(8,128)(2,1)} %right_ref.1, ...), custom_call_target="tpu_custom_call", output_to_operand_aliasing={{2}: (5, {})} | custom-call | tf_op jit(solution)/shard_map/pallas_call | solution.py:404
  86.0 1.4 collective-permute-done.21.refs_3_
  88.1 2.1 %shard_map.159 = (bf16[1024,128]{1,0:T(8,128)(2,1)}, bf16[4,256,896]{2,1,0:T(8,128)(2,1)}) custom-call(f32[1024,128]{1,0:T(8,128)} %get-tuple-element.23.refs_0_, bf16[1024,128]{1,0:T(8,128)(2,1)} %copy-done.30, bf16[1024,128]{1,0:T(8,128)(2,1)} %copy-done.32, bf16[1024,128]{1,0:T(8,128)(2,1)} %copy-done.34, ...), custom_call_target="tpu_custom_call", output_to_operand_aliasing={{1}: (4, {})} | custom-call | tf_op jit(solution)/shard_map/pallas_call | solution.py:344
  93.7 1.6 %collective-permute-start.22 = (bf16[1024,128]{1,0:T(8,128)(2,1)}, bf16[1024,128]{1,0:T(8,128)(2,1)S(1)}, u32[]{:S(2)}, u32[]{:S(2)}) collective-permute-start(bf16[1024,128]{1,0:T(8,128)(2,1)} %get-tuple-element.25.refs_0_), channel_id=1, source_target_pairs={{0,1},{1,0},{2,3},{3,2},{4,5},{5,4},{6,7},{7,6},{8,9},{9,8},{10,11... | collective-permute-start | bytes 786440 | tf_op jit(solution)/shard_map/ppermute | solution.py:277
  95.3 4.0 %collective-permute-done.15.refs_1_ = bf16[1024,128]{1,0:T(8,128)(2,1)S(1)} collective-permute-done((bf16[1024,128]{1,0:T(8,128)(2,1)S(1)}, bf16[1024,128]{1,0:T(8,128)(2,1)S(1)}, u32[]{:S(2)}, u32[]{:S(2)}) %collective-permute-start.15) | collective-permute-done | bytes 262176 | tf_op jit(solution)/shard_map/ppermute | solution.py:301
  99.3 2.6 %collective-permute-start.27 = (bf16[1024,128]{1,0:T(8,128)(2,1)}, bf16[1024,128]{1,0:T(8,128)(2,1)S(1)}, u32[]{:S(2)}, u32[]{:S(2)}) collective-permute-start(bf16[1024,128]{1,0:T(8,128)(2,1)} %get-tuple-element.25.refs_0_), channel_id=1, source_target_pairs={{0,2},{2,0},{1,3},{3,1},{4,6},{6,4},{5,7},{7,5},{8,10},{10,8},{9,1... | collective-permute-start | bytes 786440 | tf_op jit(solution)/shard_map/ppermute | solution.py:277
  101.9 3.7 %collective-permute-done.16.refs_2_ = bf16[1024,128]{1,0:T(8,128)(2,1)S(1)} collective-permute-done((bf16[1024,128]{1,0:T(8,128)(2,1)S(1)}, bf16[1024,128]{1,0:T(8,128)(2,1)S(1)}, u32[]{:S(2)}, u32[]{:S(2)}) %collective-permute-start.16) | collective-permute-done | bytes 262176 | tf_op jit(solution)/shard_map/ppermute | solution.py:301
  107.1 2.5 %shard_map.160 = (bf16[1024,128]{1,0:T(8,128)(2,1)}, bf16[4,256,896]{2,1,0:T(8,128)(2,1)}) custom-call(f32[1024,128]{1,0:T(8,128)} %get-tuple-element.62.refs_0_, bf16[1024,128]{1,0:T(8,128)(2,1)} %copy-done.29, bf16[1024,128]{1,0:T(8,128)(2,1)} %copy-done.31, bf16[1024,128]{1,0:T(8,128)(2,1)} %copy-done.33, ...), custom_call_target="tpu_custom_call", output_to_operand_aliasing={{1}: (7, {})} | custom-call | tf_op jit(solution)/shard_map/pallas_call | solution.py:344
  109.6 4.4 %collective-permute-start.23 = (bf16[1024,128]{1,0:T(8,128)(2,1)}, bf16[1024,128]{1,0:T(8,128)(2,1)S(1)}, u32[]{:S(2)}, u32[]{:S(2)}) collective-permute-start(bf16[1024,128]{1,0:T(8,128)(2,1)} %get-tuple-element.27.refs_0_), channel_id=1, source_target_pairs={{0,1},{1,0},{2,3},{3,2},{4,5},{5,4},{6,7},{7,6},{8,9},{9,8},{10,11... | collective-permute-start | bytes 786440 | tf_op jit(solution)/shard_map/ppermute | solution.py:277
  116.4 3.0 %add_convert_fusion = (bf16[1,256,896]{2,1,0:T(8,128)(2,1)S(1)}, bf16[1,256,896]{2,1,0:T(8,128)(2,1)S(1)}, bf16[1,256,896]{2,1,0:T(8,128)(2,1)}, f32[1,256,896]{2,1,0:T(8,128)}) fusion(bf16[4,256,896]{2,1,0:T(8,128)(2,1)S(1)} %collective-permute-done.30, bf16[4,256,896]{2,1,0:T(8,128)(2,1)} %get-tuple-element.28), kind=kLoop, calls=%fused_computation.3 | loop fusion | flops 3440640 | bytes 5963776 | tf_op jit(solution)/shard_map/convert_element_type | solution.py:323
  122.9 2.1 %collective-permute-done.29.refs_4_ = bf16[1024,128]{1,0:T(8,128)(2,1)} collective-permute-done((bf16[1024,128]{1,0:T(8,128)(2,1)S(1)}, bf16[1024,128]{1,0:T(8,128)(2,1)}, u32[]{:S(2)}, u32[]{:S(2)}) %collective-permute-start.29) | collective-permute-done | bytes 262176 | tf_op jit(solution)/shard_map/ppermute | solution.py:277
  125.0 2.0 %collective-permute-start.24 = (bf16[1024,128]{1,0:T(8,128)(2,1)S(1)}, bf16[1024,128]{1,0:T(8,128)(2,1)S(1)}, u32[]{:S(2)}, u32[]{:S(2)}) collective-permute-start(bf16[1024,128]{1,0:T(8,128)(2,1)S(1)} %copy-done.16), channel_id=1, source_target_pairs={{0,2},{2,0},{1,3},{3,1},{4,6},{6,4},{5,7},{7,5},{8,10},{10,8},{9,1... | collective-permute-start | bytes 786440 | tf_op jit(solution)/shard_map/ppermute | solution.py:277
  128.7 2.3 %shard_map.162.refs_7_ = bf16[1024,512]{1,0:T(8,128)(2,1)} custom-call(s32[5]{0:T(128)} %broadcast_xor_fusion.column_ref, s32[5]{0:T(128)} %or_convert_fusion.active_ref, bf16[1024,128]{1,0:T(8,128)(2,1)} %get-tuple-element.25.refs_0_, bf16[1024,128]{1,0:T(8,128)(2,1)} %copy-done.4, bf16[1024,128]{1,0:T(8,128)(2,1)} %copy-done.18, ...), custom_call_target="tpu_custom_call" | custom-call | tf_op jit(solution)/shard_map/pallas_call | solution.py:262
  131.0 9.7 %collective-permute-done.24.refs_2_.refs_5_ = bf16[1024,128]{1,0:T(8,128)(2,1)S(1)} collective-permute-done((bf16[1024,128]{1,0:T(8,128)(2,1)S(1)}, bf16[1024,128]{1,0:T(8,128)(2,1)S(1)}, u32[]{:S(2)}, u32[]{:S(2)}) %collective-permute-start.24) | collective-permute-done | bytes 262176 | tf_op jit(solution)/shard_map/ppermute | solution.py:277
  142.9 2.7 %shard_map.163 = f32[1,256,896]{2,1,0:T(8,128)} custom-call(f32[1,256,896]{2,1,0:T(8,128)} %get-tuple-element.54.refs_0_, bf16[1,256,896]{2,1,0:T(8,128)(2,1)} %copy-done.11, bf16[1,256,896]{2,1,0:T(8,128)(2,1)} %collective-permute-done.32.refs_2_, bf16[1,256,896]{2,1,0:T(8,128)(2,1)} %collective-permute-done.33.refs_3_, bf16[1024,128]{1,0:T(8,128)(2,1)} %copy-done.3, ...), custom_call_target="tpu_custom_call" | custom-call | tf_op jit(solution)/shard_map/pallas_call | solution.py:344
  145.6 1.4 select_convert_fusion
  147.1 1.9 %collective-permute-done.26.refs_4_ = bf16[1024,128]{1,0:T(8,128)(2,1)S(1)} collective-permute-done((bf16[1024,128]{1,0:T(8,128)(2,1)S(1)}, bf16[1024,128]{1,0:T(8,128)(2,1)S(1)}, u32[]{:S(2)}, u32[]{:S(2)}) %collective-permute-start.26) | collective-permute-done | bytes 262176 | tf_op jit(solution)/shard_map/ppermute | solution.py:277
  149.7 2.3 %shard_map.161 = bf16[1024,512]{1,0:T(8,128)(2,1)} custom-call(s32[5]{0:T(128)} %broadcast_xor_fusion.column_ref, s32[5]{0:T(128)} %or_convert_fusion.active_ref, bf16[1024,128]{1,0:T(8,128)(2,1)} %get-tuple-element.27.refs_0_, bf16[1024,128]{1,0:T(8,128)(2,1)} %copy-done.3, bf16[1024,128]{1,0:T(8,128)(2,1)} %copy-done.5, bf16[1024,128]{1,0:T(8,128)(2,1)} %copy-done.6, ...), custom_call_target="tpu_custom_call" | custom-call | tf_op jit(solution)/shard_map/pallas_call | solution.py:262
  (166 shorter events, 33.0 us)
Async XLA Ops:
  1.9 24.2 %collective-permute-start.10 = (bf16[1024,128]{1,0:T(8,128)(2,1)S(1)}, bf16[1024,128]{1,0:T(8,128)(2,1)S(1)}, u32[]{:S(2)}, u32[]{:S(2)}) collective-permute-start(bf16[1024,128]{1,0:T(8,128)(2,1)S(1)} %constant_dynamic-slice_fusion.refs_8_), channel_id=1, source_target_pairs={{0,16},{4,20},{8,24},{12,28},{16,0},{20,4},{24,8},{28,12},{1,17},{... | collective-permute-start | bytes 786440 | tf_op jit(solution)/shard_map/ppermute | solution.py:301
  4.9 21.8 %collective-permute-start.12 = (bf16[1024,128]{1,0:T(8,128)(2,1)S(1)}, bf16[1024,128]{1,0:T(8,128)(2,1)S(1)}, u32[]{:S(2)}, u32[]{:S(2)}) collective-permute-start(bf16[1024,128]{1,0:T(8,128)(2,1)S(1)} %constant_dynamic-slice_fusion.refs_8_), channel_id=1, source_target_pairs={{0,24},{4,28},{8,16},{12,20},{16,8},{20,12},{24,0},{28,4},{1,25},{... | collective-permute-start | bytes 786440 | tf_op jit(solution)/shard_map/ppermute | solution.py:301
  6.4 21.8 %collective-permute-start.8 = (bf16[1024,128]{1,0:T(8,128)(2,1)S(1)}, bf16[1024,128]{1,0:T(8,128)(2,1)S(1)}, u32[]{:S(2)}, u32[]{:S(2)}) collective-permute-start(bf16[1024,128]{1,0:T(8,128)(2,1)S(1)} %constant_dynamic-slice_fusion.refs_8_), channel_id=1, source_target_pairs={{0,8},{4,12},{8,0},{12,4},{16,24},{20,28},{24,16},{28,20},{1,9},{5... | collective-permute-start | bytes 786440 | tf_op jit(solution)/shard_map/ppermute | solution.py:301
  6.5 21.7 %collective-permute-start.7 = (bf16[1024,128]{1,0:T(8,128)(2,1)S(1)}, bf16[1024,128]{1,0:T(8,128)(2,1)S(1)}, u32[]{:S(2)}, u32[]{:S(2)}) collective-permute-start(bf16[1024,128]{1,0:T(8,128)(2,1)S(1)} %constant_dynamic-slice_fusion.refs_8_), channel_id=1, source_target_pairs={{0,4},{4,0},{8,12},{12,8},{16,20},{20,16},{24,28},{28,24},{1,5},{5... | collective-permute-start | bytes 786440 | tf_op jit(solution)/shard_map/ppermute | solution.py:301
  8.6 11.0 %all-to-all-start = ((s32[8,8,128]{2,1,0:T(8,128)}), s32[8,8,128]{2,1,0:T(8,128)S(1)}, u32[]{:S(2)}, u32[]{:S(2)}) async-start(s32[8,8,128]{2,1,0:T(8,128)} %broadcast_in_dim.40), calls=%async_computation | async-start | bytes 65536 | tf_op jit(solution)/shard_map/all_to_all | solution.py:437
  24.7 12.4 %collective-permute-start.1 = (bf16[1024,128]{1,0:T(8,128)(2,1)S(1)}, bf16[1024,128]{1,0:T(8,128)(2,1)S(1)}, u32[]{:S(2)}, u32[]{:S(2)}) collective-permute-start(bf16[1024,128]{1,0:T(8,128)(2,1)S(1)} %get-tuple-element.42.refs_0_), channel_id=1, source_target_pairs={{0,8},{4,12},{8,0},{12,4},{16,24},{20,28},{24,16},{28,20},{1,9},{5... | collective-permute-start | bytes 786440 | tf_op jit(solution)/shard_map/ppermute | solution.py:301
  26.1 13.3 %collective-permute-start.3 = (bf16[1024,128]{1,0:T(8,128)(2,1)S(1)}, bf16[1024,128]{1,0:T(8,128)(2,1)S(1)}, u32[]{:S(2)}, u32[]{:S(2)}) collective-permute-start(bf16[1024,128]{1,0:T(8,128)(2,1)S(1)} %get-tuple-element.42.refs_0_), channel_id=1, source_target_pairs={{0,16},{4,20},{8,24},{12,28},{16,0},{20,4},{24,8},{28,12},{1,17},{... | collective-permute-start | bytes 786440 | tf_op jit(solution)/shard_map/ppermute | solution.py:301
  26.7 12.7 %collective-permute-start.5 = (bf16[1024,128]{1,0:T(8,128)(2,1)S(1)}, bf16[1024,128]{1,0:T(8,128)(2,1)S(1)}, u32[]{:S(2)}, u32[]{:S(2)}) collective-permute-start(bf16[1024,128]{1,0:T(8,128)(2,1)S(1)} %get-tuple-element.42.refs_0_), channel_id=1, source_target_pairs={{0,24},{4,28},{8,16},{12,20},{16,8},{20,12},{24,0},{28,4},{1,25},{... | collective-permute-start | bytes 786440 | tf_op jit(solution)/shard_map/ppermute | solution.py:301
  28.2 11.8 %collective-permute-start = (bf16[1024,128]{1,0:T(8,128)(2,1)S(1)}, bf16[1024,128]{1,0:T(8,128)(2,1)S(1)}, u32[]{:S(2)}, u32[]{:S(2)}) collective-permute-start(bf16[1024,128]{1,0:T(8,128)(2,1)S(1)} %get-tuple-element.42.refs_0_), channel_id=1, source_target_pairs={{0,4},{4,0},{8,12},{12,8},{16,20},{20,16},{24,28},{28,24},{1,5},{5... | collective-permute-start | bytes 786440 | tf_op jit(solution)/shard_map/ppermute | solution.py:301
  28.2 11.8 %collective-permute-start.11 = (bf16[1024,128]{1,0:T(8,128)(2,1)S(1)}, bf16[1024,128]{1,0:T(8,128)(2,1)S(1)}, u32[]{:S(2)}, u32[]{:S(2)}) collective-permute-start(bf16[1024,128]{1,0:T(8,128)(2,1)S(1)} %collective-permute-done.10.refs_12_), channel_id=1, source_target_pairs={{0,4},{4,0},{8,12},{12,8},{16,20},{20,16},{24,28},{28,24},{1,5},{5... | collective-permute-start | bytes 786440 | tf_op jit(solution)/shard_map/ppermute | solution.py:301
  37.1 4.1 %collective-permute-start.13 = (bf16[1024,128]{1,0:T(8,128)(2,1)S(1)}, bf16[1024,128]{1,0:T(8,128)(2,1)S(1)}, u32[]{:S(2)}, u32[]{:S(2)}) collective-permute-start(bf16[1024,128]{1,0:T(8,128)(2,1)S(1)} %collective-permute-done.12.refs_14_), channel_id=1, source_target_pairs={{0,4},{4,0},{8,12},{12,8},{16,20},{20,16},{24,28},{28,24},{1,5},{5... | collective-permute-start | bytes 786440 | tf_op jit(solution)/shard_map/ppermute | solution.py:301
  66.6 3.8 %collective-permute-start.18 = (bf16[4096,128]{1,0:T(8,128)(2,1)}, bf16[4096,128]{1,0:T(8,128)(2,1)}, u32[]{:S(2)}, u32[]{:S(2)}) collective-permute-start(bf16[4096,128]{1,0:T(8,128)(2,1)} %get-tuple-element.22), channel_id=1, source_target_pairs={{0,4},{4,0},{8,12},{12,8},{16,20},{20,16},{24,28},{28,24},{1,5},{5... | collective-permute-start | bytes 3145736 | tf_op jit(solution)/shard_map/ppermute | solution.py:301
  66.7 9.7 %collective-permute-start.14 = (bf16[4096,128]{1,0:T(8,128)(2,1)}, bf16[4096,128]{1,0:T(8,128)(2,1)S(1)}, u32[]{:S(2)}, u32[]{:S(2)}) collective-permute-start(bf16[4096,128]{1,0:T(8,128)(2,1)} %get-tuple-element.19), channel_id=1, source_target_pairs={{0,4},{4,0},{8,12},{12,8},{16,20},{20,16},{24,28},{28,24},{1,5},{5... | collective-permute-start | bytes 3145736 | tf_op jit(solution)/shard_map/ppermute | solution.py:301
  72.9 13.0 %collective-permute-start.19 = (bf16[1024,128]{1,0:T(8,128)(2,1)S(1)}, bf16[1024,128]{1,0:T(8,128)(2,1)S(1)}, u32[]{:S(2)}, u32[]{:S(2)}) collective-permute-start(bf16[1024,128]{1,0:T(8,128)(2,1)S(1)} %get-tuple-element.58.refs_0_), channel_id=1, source_target_pairs={{0,8},{4,12},{8,0},{12,4},{16,24},{20,28},{24,16},{28,20},{1,9},{5... | collective-permute-start | bytes 786440 | tf_op jit(solution)/shard_map/ppermute | solution.py:301
  73.7 12.3 %collective-permute-start.20 = (bf16[1024,128]{1,0:T(8,128)(2,1)S(1)}, bf16[1024,128]{1,0:T(8,128)(2,1)S(1)}, u32[]{:S(2)}, u32[]{:S(2)}) collective-permute-start(bf16[1024,128]{1,0:T(8,128)(2,1)S(1)} %get-tuple-element.56), channel_id=1, source_target_pairs={{0,16},{4,20},{8,24},{12,28},{16,0},{20,4},{24,8},{28,12},{1,17},{... | collective-permute-start | bytes 786440 | tf_op jit(solution)/shard_map/ppermute | solution.py:301
  74.1 13.3 %collective-permute-start.21 = (bf16[1024,128]{1,0:T(8,128)(2,1)S(1)}, bf16[1024,128]{1,0:T(8,128)(2,1)S(1)}, u32[]{:S(2)}, u32[]{:S(2)}) collective-permute-start(bf16[1024,128]{1,0:T(8,128)(2,1)S(1)} %get-tuple-element.55), channel_id=1, source_target_pairs={{0,24},{4,28},{8,16},{12,20},{16,8},{20,12},{24,0},{28,4},{1,25},{... | collective-permute-start | bytes 786440 | tf_op jit(solution)/shard_map/ppermute | solution.py:301
  90.2 26.1 %collective-permute-start.30 = (bf16[4,256,896]{2,1,0:T(8,128)(2,1)}, bf16[4,256,896]{2,1,0:T(8,128)(2,1)S(1)}, u32[]{:S(2)}, u32[]{:S(2)}) collective-permute-start(bf16[4,256,896]{2,1,0:T(8,128)(2,1)} %get-tuple-element.29), channel_id=1, source_target_pairs={{0,4},{4,0},{8,12},{12,8},{16,20},{20,16},{24,28},{28,24},{1,5},{5... | collective-permute-start | bytes 5505032 | tf_op jit(solution)/shard_map/ppermute | solution.py:301
  90.2 9.1 %collective-permute-start.15 = (bf16[1024,128]{1,0:T(8,128)(2,1)S(1)}, bf16[1024,128]{1,0:T(8,128)(2,1)S(1)}, u32[]{:S(2)}, u32[]{:S(2)}) collective-permute-start(bf16[1024,128]{1,0:T(8,128)(2,1)S(1)} %copy-done.9), channel_id=1, source_target_pairs={{0,8},{4,12},{8,0},{12,4},{16,24},{20,28},{24,16},{28,20},{1,9},{5... | collective-permute-start | bytes 786440 | tf_op jit(solution)/shard_map/ppermute | solution.py:301
  91.6 14.1 %collective-permute-start.16 = (bf16[1024,128]{1,0:T(8,128)(2,1)S(1)}, bf16[1024,128]{1,0:T(8,128)(2,1)S(1)}, u32[]{:S(2)}, u32[]{:S(2)}) collective-permute-start(bf16[1024,128]{1,0:T(8,128)(2,1)S(1)} %copy-done.36), channel_id=1, source_target_pairs={{0,16},{4,20},{8,24},{12,28},{16,0},{20,4},{24,8},{28,12},{1,17},{... | collective-permute-start | bytes 786440 | tf_op jit(solution)/shard_map/ppermute | solution.py:301
  92.6 13.7 %collective-permute-start.17 = (bf16[1024,128]{1,0:T(8,128)(2,1)S(1)}, bf16[1024,128]{1,0:T(8,128)(2,1)S(1)}, u32[]{:S(2)}, u32[]{:S(2)}) collective-permute-start(bf16[1024,128]{1,0:T(8,128)(2,1)S(1)} %get-tuple-element.59), channel_id=1, source_target_pairs={{0,24},{4,28},{8,16},{12,20},{16,8},{20,12},{24,0},{28,4},{1,25},{... | collective-permute-start | bytes 786440 | tf_op jit(solution)/shard_map/ppermute | solution.py:301
  93.7 12.6 %collective-permute-start.22 = (bf16[1024,128]{1,0:T(8,128)(2,1)}, bf16[1024,128]{1,0:T(8,128)(2,1)S(1)}, u32[]{:S(2)}, u32[]{:S(2)}) collective-permute-start(bf16[1024,128]{1,0:T(8,128)(2,1)} %get-tuple-element.25.refs_0_), channel_id=1, source_target_pairs={{0,1},{1,0},{2,3},{3,2},{4,5},{5,4},{6,7},{7,6},{8,9},{9,8},{10,11... | collective-permute-start | bytes 786440 | tf_op jit(solution)/shard_map/ppermute | solution.py:277
  99.3 15.7 %collective-permute-start.27 = (bf16[1024,128]{1,0:T(8,128)(2,1)}, bf16[1024,128]{1,0:T(8,128)(2,1)S(1)}, u32[]{:S(2)}, u32[]{:S(2)}) collective-permute-start(bf16[1024,128]{1,0:T(8,128)(2,1)} %get-tuple-element.25.refs_0_), channel_id=1, source_target_pairs={{0,2},{2,0},{1,3},{3,1},{4,6},{6,4},{5,7},{7,5},{8,10},{10,8},{9,1... | collective-permute-start | bytes 786440 | tf_op jit(solution)/shard_map/ppermute | solution.py:277
  105.6 16.2 %collective-permute-start.28 = (bf16[1024,128]{1,0:T(8,128)(2,1)}, bf16[1024,128]{1,0:T(8,128)(2,1)S(1)}, u32[]{:S(2)}, u32[]{:S(2)}) collective-permute-start(bf16[1024,128]{1,0:T(8,128)(2,1)} %get-tuple-element.25.refs_0_), channel_id=1, source_target_pairs={{1,2},{2,1},{5,6},{6,5},{9,10},{10,9},{13,14},{14,13},{17,18},{18,... | collective-permute-start | bytes 786440 | tf_op jit(solution)/shard_map/ppermute | solution.py:277
  109.6 17.3 %collective-permute-start.23 = (bf16[1024,128]{1,0:T(8,128)(2,1)}, bf16[1024,128]{1,0:T(8,128)(2,1)S(1)}, u32[]{:S(2)}, u32[]{:S(2)}) collective-permute-start(bf16[1024,128]{1,0:T(8,128)(2,1)} %get-tuple-element.27.refs_0_), channel_id=1, source_target_pairs={{0,1},{1,0},{2,3},{3,2},{4,5},{5,4},{6,7},{7,6},{8,9},{9,8},{10,11... | collective-permute-start | bytes 786440 | tf_op jit(solution)/shard_map/ppermute | solution.py:277
  115.0 9.9 %collective-permute-start.29 = (bf16[1024,128]{1,0:T(8,128)(2,1)S(1)}, bf16[1024,128]{1,0:T(8,128)(2,1)}, u32[]{:S(2)}, u32[]{:S(2)}) collective-permute-start(bf16[1024,128]{1,0:T(8,128)(2,1)S(1)} %collective-permute-done.27.refs_2_), channel_id=1, source_target_pairs={{1,0},{2,3},{5,4},{6,7},{9,8},{10,11},{13,12},{14,15},{17,16},{18,... | collective-permute-start | bytes 786440 | tf_op jit(solution)/shard_map/ppermute | solution.py:277
  119.4 22.6 %collective-permute-start.31 = (bf16[1,256,896]{2,1,0:T(8,128)(2,1)}, bf16[1,256,896]{2,1,0:T(8,128)(2,1)S(1)}, u32[]{:S(2)}, u32[]{:S(2)}) collective-permute-start(bf16[1,256,896]{2,1,0:T(8,128)(2,1)} %get-tuple-element.53), channel_id=1, source_target_pairs={{0,8},{4,12},{8,0},{12,4},{16,24},{20,28},{24,16},{28,20},{1,9},{5... | collective-permute-start | bytes 1376264 | tf_op jit(solution)/shard_map/ppermute | solution.py:301
  120.7 21.3 %collective-permute-start.32 = (bf16[1,256,896]{2,1,0:T(8,128)(2,1)S(1)}, bf16[1,256,896]{2,1,0:T(8,128)(2,1)}, u32[]{:S(2)}, u32[]{:S(2)}) collective-permute-start(bf16[1,256,896]{2,1,0:T(8,128)(2,1)S(1)} %get-tuple-element.52), channel_id=1, source_target_pairs={{0,16},{4,20},{8,24},{12,28},{16,0},{20,4},{24,8},{28,12},{1,17},{... | collective-permute-start | bytes 1376264 | tf_op jit(solution)/shard_map/ppermute | solution.py:301
  121.8 20.2 %collective-permute-start.33 = (bf16[1,256,896]{2,1,0:T(8,128)(2,1)S(1)}, bf16[1,256,896]{2,1,0:T(8,128)(2,1)}, u32[]{:S(2)}, u32[]{:S(2)}) collective-permute-start(bf16[1,256,896]{2,1,0:T(8,128)(2,1)S(1)} %get-tuple-element.51), channel_id=1, source_target_pairs={{0,24},{4,28},{8,16},{12,20},{16,8},{20,12},{24,0},{28,4},{1,25},{... | collective-permute-start | bytes 1376264 | tf_op jit(solution)/shard_map/ppermute | solution.py:301
  125.0 15.7 %collective-permute-start.24 = (bf16[1024,128]{1,0:T(8,128)(2,1)S(1)}, bf16[1024,128]{1,0:T(8,128)(2,1)S(1)}, u32[]{:S(2)}, u32[]{:S(2)}) collective-permute-start(bf16[1024,128]{1,0:T(8,128)(2,1)S(1)} %copy-done.16), channel_id=1, source_target_pairs={{0,2},{2,0},{1,3},{3,1},{4,6},{6,4},{5,7},{7,5},{8,10},{10,8},{9,1... | collective-permute-start | bytes 786440 | tf_op jit(solution)/shard_map/ppermute | solution.py:277
  126.9 15.1 %collective-permute-start.25 = (bf16[1024,128]{1,0:T(8,128)(2,1)S(1)}, bf16[1024,128]{1,0:T(8,128)(2,1)S(1)}, u32[]{:S(2)}, u32[]{:S(2)}) collective-permute-start(bf16[1024,128]{1,0:T(8,128)(2,1)S(1)} %copy-done.16), channel_id=1, source_target_pairs={{1,2},{2,1},{5,6},{6,5},{9,10},{10,9},{13,14},{14,13},{17,18},{18,... | collective-permute-start | bytes 786440 | tf_op jit(solution)/shard_map/ppermute | solution.py:277
  140.7 8.3 %collective-permute-start.26 = (bf16[1024,128]{1,0:T(8,128)(2,1)S(1)}, bf16[1024,128]{1,0:T(8,128)(2,1)S(1)}, u32[]{:S(2)}, u32[]{:S(2)}) collective-permute-start(bf16[1024,128]{1,0:T(8,128)(2,1)S(1)} %collective-permute-done.24.refs_2_.refs_5_), channel_id=1, source_target_pairs={{1,0},{2,3},{5,4},{6,7},{9,8},{10,11},{13,12},{14,15},{17,16},{18,... | collective-permute-start | bytes 786440 | tf_op jit(solution)/shard_map/ppermute | solution.py:277
  147.0 4.9 %collective-permute-start.34 = (bf16[256,448]{1,0:T(8,128)(2,1)S(1)}, bf16[256,448]{1,0:T(8,128)(2,1)S(1)}, u32[]{:S(2)}, u32[]{:S(2)}) collective-permute-start(bf16[256,448]{1,0:T(8,128)(2,1)S(1)} %select_convert_fusion), channel_id=1, source_target_pairs={{0,4},{4,0},{8,12},{12,8},{16,20},{20,16},{24,28},{28,24},{1,5},{5... | collective-permute-start | bytes 688136 | tf_op jit(solution)/shard_map/ppermute | solution.py:301
  (46 other events, 241.2 us)

commit v8 on v7

--- a/solution.py
+++ b/solution.py
@@ -97,26 +97,41 @@
 ):
     key_parts, refs = refs[:ranks], refs[ranks:]
     value_parts, refs = refs[:ranks], refs[ranks:]
-    gquery_ref, out_ref, gkey_keep, gkey_send, gvalue_keep, gvalue_send = refs[:6]
-    key_ref, value_ref, gkey_ref, gvalue_ref, key_win, value_win, sems = refs[6:]
+    gquery_ref, out_ref, *halves = refs[:6]
+    key_ref, value_ref, gkey_ref, gvalue_ref, key_win, value_win, load_sems, sems = refs[6:]
     rows_each = query_ref.shape[0]
+    half_blocks = ranks * RUN_BLOCKS // 2
     scale = 1.0 / math.sqrt(HD)
     to_exp2 = scale * math.log2(math.e)
-    wide = min(2, heads)
-    cols = wide * ROWBLK
 
     loads = []
     for item, (parts, whole) in enumerate(((key_parts, key_ref), (value_parts, value_ref))):
         for rank in range(ranks):
             copy = pltpu.make_async_copy(
-                parts[rank], whole.at[pl.ds(rank * rows_each, rows_each)], sems.at[item, rank]
+                parts[rank], whole.at[pl.ds(rank * rows_each, rows_each)], load_sems.at[item, rank]
             )
             copy.start()
             loads.append(copy)
-    gkey_ref[...] = jnp.zeros_like(gkey_ref)
-    gvalue_ref[...] = jnp.zeros_like(gvalue_ref)
     for copy in loads:
         copy.wait()
+
+    def stores(block, act):
+        side = block % 2
+        for step in range(RUN_BLOCKS):
+            target = target_ref[run_ref[block] * RUN_BLOCKS + step]
+            for place in range(2):
+
+                @pl.when(target // half_blocks == place)
+                def one_half():
+                    start = pl.multiple_of(target % half_blocks * ROWBLK, ROWBLK)
+                    for item, source in enumerate((gkey_ref, gvalue_ref)):
+                        act(
+                            pltpu.make_async_copy(
+                                source.at[side, pl.ds(step * ROWBLK, ROWBLK)],
+                                halves[2 * item + place].at[pl.ds(start, ROWBLK)],
+                                sems.at[side, item, step],
+                            )
+                        )
 
     def window(count, block):
         slot = slot_ref[block]
@@ -128,6 +143,8 @@
             start = pl.multiple_of(source * ROWBLK, ROWBLK)
             key_win[pl.ds(step * ROWBLK, ROWBLK), :] = key_ref[pl.ds(start, ROWBLK), :]
             value_win[pl.ds(step * ROWBLK, ROWBLK), :] = value_ref[pl.ds(start, ROWBLK), :]
+        wide = heads if count <= 4 else min(2, heads)
+        cols = wide * ROWBLK
         base = pl.multiple_of(block * ROWBLK, ROWBLK)
         cosine = cos_ref[pl.ds(base, ROWBLK), :]
         sine = sin_ref[pl.ds(base, ROWBLK), :]
@@ -180,35 +197,27 @@
                 gquery_ref[pl.ds(base, ROWBLK), pl.ds(at, HD)] = back.astype(jnp.bfloat16)
         gkey = (gkey * scale).astype(jnp.bfloat16)
         gvalue = gvalue.astype(jnp.bfloat16)
-        for step in range(count):
-            block_id = run * RUN_BLOCKS + first + step
-            part = slice(step * ROWBLK, (step + 1) * ROWBLK)
-            start = pl.multiple_of(target_ref[block_id] * ROWBLK, ROWBLK)
-            gkey_ref[pl.ds(start, ROWBLK), :] = gkey[part]
-            gvalue_ref[pl.ds(start, ROWBLK), :] = gvalue[part]
+        place_at = pl.ds(pl.multiple_of(first * ROWBLK, ROWBLK), rows)
+        gkey_ref[block % 2, place_at, :] = gkey
+        gvalue_ref[block % 2, place_at, :] = gvalue
 
     def body(block, carry):
+        pl.when(block >= 2)(lambda: stores(block - 2, lambda copy: copy.wait()))
+        blank = jnp.zeros(gkey_ref.shape[1:], jnp.bfloat16)
+        gkey_ref[block % 2] = blank
+        gvalue_ref[block % 2] = blank
         need = need_ref[block]
         floor = 0
         for size in (1, 2, 3, 4, 6, 8):
             pl.when((need > floor) & (need <= size))(partial(window, size, block))
             floor = size
+        stores(block, lambda copy: copy.start())
         return carry
 
-    lax.fori_loop(0, rows_each // ROWBLK, body, 0)
-    half = ranks * rows_each // 2
-    stores = []
-    for item, (whole, keep, send) in enumerate(
-        ((gkey_ref, gkey_keep, gkey_send), (gvalue_ref, gvalue_keep, gvalue_send))
-    ):
-        for place, target in enumerate((keep, send)):
-            copy = pltpu.make_async_copy(
-                whole.at[pl.ds(place * half, half)], target, sems.at[item, place]
-            )
-            copy.start()
-            stores.append(copy)
-    for copy in stores:
-        copy.wait()
+    blocks = rows_each // ROWBLK
+    lax.fori_loop(0, blocks, body, 0)
+    for block in range(max(blocks - 2, 0), blocks):
+        stores(block, lambda copy: copy.wait())
 
 
 def attend(tables, query, up, cosine, sine, places, keys, values):
@@ -232,68 +241,56 @@
         ),
         in_specs=[smem] * 6 + [vmem] * 5 + [hbm] * (2 * ranks),
         out_specs=(vmem, vmem, hbm, hbm, hbm, hbm),
-        scratch_shapes=[pltpu.VMEM((every, HD), jnp.bfloat16)] * 4
+        scratch_shapes=[pltpu.VMEM((every, HD), jnp.bfloat16)] * 2
+        + [pltpu.VMEM((2, RUN_BLOCKS * ROWBLK, HD), jnp.bfloat16)] * 2
         + [pltpu.VMEM((RUN_BLOCKS * ROWBLK, HD), jnp.bfloat16)] * 2
-        + [pltpu.SemaphoreType.DMA((2, ranks))],
+        + [pltpu.SemaphoreType.DMA((2, ranks)), pltpu.SemaphoreType.DMA((2, 2, RUN_BLOCKS))],
         compiler_params=pltpu.CompilerParams(vmem_limit_bytes=VMEM_BYTES),
         cost_estimate=NO_COST,
     )(*tables, query, up, cosine, sine, places, *keys, *values)
 
 
-def assemble_kernel(count, column_ref, active_ref, *refs):
-    out_ref, sems = refs[count:]
-
-    def copy_of(index):
-        column = pl.multiple_of(column_ref[index] * HD, HD)
-        return pltpu.make_async_copy(
+def assemble_kernel(lanes, my_ref, *refs):
+    out_ref, sems = refs[lanes:]
+    copies = []
+    for index in range(lanes):
+        column = pl.multiple_of((my_ref[0] ^ index) * HD, HD)
+        copy = pltpu.make_async_copy(
             refs[index], out_ref.at[:, pl.ds(column, HD)], sems.at[index]
         )
-
-    for index in range(count):
-        pl.when(active_ref[index] > 0)(lambda index=index: copy_of(index).start())
-    for index in range(count):
-        pl.when(active_ref[index] > 0)(lambda index=index: copy_of(index).wait())
-
-
-def assemble(columns, active, pieces, lanes):
+        copy.start()
+        copies.append(copy)
+    for copy in copies:
+        copy.wait()
+
+
+def assemble(my_lane, pieces):
     rows = pieces[0].shape[0]
-    smem = pl.BlockSpec(memory_space=pltpu.SMEM)
+    lanes = len(pieces)
     vmem = pl.BlockSpec(memory_space=pltpu.VMEM)
     return pl.pallas_call(
-        partial(assemble_kernel, len(pieces)),
+        partial(assemble_kernel, lanes),
         out_shape=jax.ShapeDtypeStruct((rows, lanes * HD), pieces[0].dtype),
-        in_specs=[smem, smem] + [vmem] * len(pieces),
+        in_specs=[pl.BlockSpec(memory_space=pltpu.SMEM)] + [vmem] * lanes,
         out_specs=pl.BlockSpec(memory_space=pl.ANY),
-        scratch_shapes=[pltpu.SemaphoreType.DMA((len(pieces),))],
+        scratch_shapes=[pltpu.SemaphoreType.DMA((lanes,))],
         compiler_params=pltpu.CompilerParams(vmem_limit_bytes=VMEM_BYTES),
         cost_estimate=NO_COST,
-    )(columns, active, *pieces)
+    )(my_lane.reshape(1), *pieces)
 
 
 def lane_gather(array, my_lane):
     lanes = lax.axis_size("tensor")
-
-    def send(item, pairs):
-        return lax.ppermute(item, "tensor", pairs)
-
-    if lanes == 4:
-        second = send(array, [(0, 2), (2, 0), (1, 3), (3, 1)])
-        first = send(array, [(0, 1), (1, 0), (2, 3), (3, 2)])
-        inner = send(array, [(1, 2), (2, 1)])
-        outer = send(second, [(1, 0), (2, 3)])
-        middle = (my_lane == 1) | (my_lane == 2)
-        pieces = [array, first, second, inner, outer]
-        columns = my_lane ^ jnp.array([0, 1, 2, 3, 3], jnp.int32)
-        always = jnp.array([True, True, True, False, False])
-        at_inner = jnp.array([False, False, False, True, False])
-        active = always | (at_inner & middle) | (~always & ~at_inner & ~middle)
-    else:
-        pieces = [array]
-        for unused in range(lanes - 1):
-            pieces.append(send(pieces[-1], [(lane, (lane + 1) % lanes) for lane in range(lanes)]))
-        columns = (my_lane - jnp.arange(lanes, dtype=jnp.int32)) % lanes
-        active = jnp.ones((lanes,), jnp.bool_)
-    return assemble(columns, active.astype(jnp.int32), pieces, lanes), pieces[1:]
+    pieces = {0: array}
+    bit = lanes // 2
+    while bit:
+        pairs = [(lane, lane ^ bit) for lane in range(lanes)]
+        pieces.update(
+            {at | bit: lax.ppermute(item, "tensor", pairs) for at, item in list(pieces.items())}
+        )
+        bit //= 2
+    pieces = [pieces[at] for at in range(lanes)]
+    return assemble(my_lane, pieces), pieces[1:]
 
 
 def swap(array, bit):
@@ -491,7 +488,7 @@
     weight_keep, weight_sends = chip_sum(weight_keep, weight_other)
     weight_received = exchange(weight_sends)
     total = final_sum(
-        weight_keep, weight_received, (), [*key_pieces[:3], value_all], jnp.float32
+        weight_keep, weight_received, (), [*key_pieces[:2], value_all], jnp.float32
     )[0]
     odd = my_rank & 1
     pair_rows = grad_out.shape[1] // (rank_count // 2)

time: 154 us -> 151 us (0.981)
  starting transfers between devices: 39.5 us -> 36 us
  waiting for transfers between devices: 33 us -> 35.5 us
  Pallas kernels: 52.5 us -> 50.9 us
    ppermute x8 -> x6, starting transfers between devices: 14.4 us -> 9.66 us  [lane_gather(): lax.ppermute(item, 'tensor', pairs)]
    ppermute x8 -> x6, waiting for transfers between devices: 14.6 us -> 19.1 us  [lane_gather(): lax.ppermute(item, 'tensor', pairs)]
    ppermute x27, waiting for transfers between devices: 15.4 us -> 13.5 us  [swap(): lax.ppermute(array, 'dp', [(rank, rank ^ bit) for rank in range(ranks)])]
    unnamed x85 -> x75, local copies, waits for them, and re-layouts: 6.19 us -> 5.98 us
  transfers between devices with their start and end apart: 36 -> 34, of which waited for: 13 -> 14; matrix products, arithmetic and copies ran while one was open for 14% -> 13% of each run, Pallas kernels for 17% -> 18%
where the time goes in v8:
time: 151 us; the launch traced here: 150 us
  Pallas kernels  50.9 us (34%)
  starting transfers between devices  36 us (24%)
  waiting for transfers between devices  35.5 us (24%)
  other arithmetic  18.3 us (12%)
  local copies, waits for them, and re-layouts  7.7 us (5%)
    pallas_call x1, Pallas kernels, attend(): pl.pallas_call(partial(attend_kernel, heads, ranks), out_shape=(jax.Shape...  22.4 us
    ppermute x27, starting transfers between devices, swap(): lax.ppermute(array, 'dp', [(rank, rank ^ bit) for rank in range(ranks)])  22.1 us
    ppermute x6, waiting for transfers between devices, lane_gather(): lax.ppermute(item, 'tensor', pairs)  19.1 us
    ppermute x27, waiting for transfers between devices, swap(): lax.ppermute(array, 'dp', [(rank, rank ^ bit) for rank in range(ranks)])  13.5 us
    ppermute x6, starting transfers between devices, lane_gather(): lax.ppermute(item, 'tensor', pairs)  9.66 us
    pallas_call x1, Pallas kernels, product(): pl.pallas_call(product_kernel, grid_spec=pltpu.PrefetchScalarGridSpec(num...  8.37 us
    pallas_call x1, Pallas kernels, up_product(): pl.pallas_call(up_kernel, grid=(steps,), out_shape=jax.ShapeDtypeStruct((...  8.36 us
    pallas_call x3, Pallas kernels, final_sum(): pl.pallas_call(partial(final_kernel, len(received), len(tables) > 0, inpu...  7.36 us
  transfers between devices with their start and end apart: 34, of which 14 were waited for; matrix products, arithmetic and copies ran while one was open for 13% of the time, Pallas kernels for 18%

profile of v8, /device:TPU:0, one launch (start us, length us, event | category | flops | bytes accessed | tf_op | source)
XLA Modules:
  0.0 149.5 jit_solution(701592084854846220)
XLA Ops:
  1.9 3.0 %collective-permute-start.10 = (bf16[1024,128]{1,0:T(8,128)(2,1)S(1)}, bf16[1024,128]{1,0:T(8,128)(2,1)S(1)}, u32[]{:S(2)}, u32[]{:S(2)}) collective-permute-start(bf16[1024,128]{1,0:T(8,128)(2,1)S(1)} %constant_dynamic-slice_fusion.refs_8_), channel_id=1, source_target_pairs={{0,16},{4,20},{8,24},{12,28},{16,0},{20,4},{24,8},{28,12},{1,17},{... | collective-permute-start | bytes 786440 | tf_op jit(solution)/shard_map/ppermute | solution.py:298
  4.9 1.4 collective-permute-start.12
  8.6 4.3 %all-to-all-start = ((s32[8,8,128]{2,1,0:T(8,128)}), s32[8,8,128]{2,1,0:T(8,128)S(1)}, u32[]{:S(2)}, u32[]{:S(2)}) async-start(s32[8,8,128]{2,1,0:T(8,128)} %broadcast_in_dim.40), calls=%async_computation | async-start | bytes 65536 | tf_op jit(solution)/shard_map/all_to_all | solution.py:434
  16.7 2.9 %all-to-all-done = s32[8,8,128]{2,1,0:T(8,128)S(1)} async-done(((s32[8,8,128]{2,1,0:T(8,128)}), s32[8,8,128]{2,1,0:T(8,128)S(1)}, u32[]{:S(2)}, u32[]{:S(2)}) %all-to-all-start) | async-done | bytes 32800 | tf_op jit(solution)/shard_map/all_to_all | solution.py:434
  20.3 1.9 %fusion.5 = (f32[1024,64]{1,0:T(8,128)S(1)}, f32[1024,64]{1,0:T(8,128)S(1)}, f32[1024,64]{1,0:T(8,128)S(1)}) fusion(f32[64]{0:T(128)S(1)} %multiply_add_fusion.1, f32[1024]{0:T(1024)S(1)} %get-tuple-element.44), kind=kLoop, calls=%fused_computation.29 | loop fusion | flops 262144 | bytes 790784 | tf_op jit(solution)/shard_map/neg | solution.py:69
  22.2 2.4 %fusion.4 = (bf16[1024,128]{1,0:T(8,128)(2,1)S(1)}, f32[1024,128]{1,0:T(8,128)}, f32[1024,128]{1,0:T(8,128)}) fusion(f32[1024,64]{1,0:T(8,128)S(1)} %get-tuple-element.67, f32[1024,64]{1,0:T(8,128)S(1)} %get-tuple-element.66, bf16[1024,512]{1,0:T(8,128)(2,1)} %param.8, s32[]{:T(128)S(6)} %select_n.100, f32[1024,64]{1,0:T(8,128)S(1)} %get-tuple-element.70, ...), kind=kLoop, calls=%fused_computation.16 | loop fusion | flops 1048576 | bytes 2883588 | tf_op jit(solution)/shard_map/convert_element_type | solution.py:454
  24.7 1.4 collective-permute-start.1
  26.7 1.4 collective-permute-start.5
  28.7 8.4 %shard_map.102.up_ref = bf16[1024,512]{1,0:T(8,128)(2,1)} custom-call(bf16[1024,3584]{1,0:T(8,128)(2,1)} %right_ref.1, bf16[3584,512]{1,0:T(8,128)(2,1)} %weight_ref.1, bf16[1024,128]{1,0:T(8,128)(2,1)} %copy-done.2), custom_call_target="tpu_custom_call" | custom-call | flops 3758096384 | bytes 7340032 | tf_op jit(solution)/shard_map/pallas_call | solution.py:362
  37.2 2.1 %collective-permute-done.3.refs_4_ = bf16[1024,128]{1,0:T(8,128)(2,1)S(1)} collective-permute-done((bf16[1024,128]{1,0:T(8,128)(2,1)S(1)}, bf16[1024,128]{1,0:T(8,128)(2,1)S(1)}, u32[]{:S(2)}, u32[]{:S(2)}) %collective-permute-start.3) | collective-permute-done | bytes 262176 | tf_op jit(solution)/shard_map/ppermute | solution.py:298
  42.7 22.4 %shard_map.103 = (bf16[1024,512]{1,0:T(8,128)(2,1)}, bf16[2,256,1024]{2,1,0:T(8,128)(2,1)}, bf16[4096,128]{1,0:T(8,128)(2,1)}, bf16[4096,128]{1,0:T(8,128)(2,1)}...) custom-call(s32[64]{0:T(128)} %multiply_add_fusion.3.target_ref, s32[64]{0:T(128)} %get-tuple-element.48.source_ref, ...), custom_call_target="tpu_custom_call" | custom-call | tf_op jit(solution)/shard_map/pallas_call | solution.py:232
  65.8 3.2 %collective-permute-done.18 = bf16[4096,128]{1,0:T(8,128)(2,1)} collective-permute-done((bf16[4096,128]{1,0:T(8,128)(2,1)}, bf16[4096,128]{1,0:T(8,128)(2,1)}, u32[]{:S(2)}, u32[]{:S(2)}) %collective-permute-start.18) | collective-permute-done | bytes 1048608 | tf_op jit(solution)/shard_map/ppermute | solution.py:298
  69.0 2.6 %add_convert_fusion.3 = (bf16[1024,128]{1,0:T(8,128)(2,1)S(1)}, bf16[1024,128]{1,0:T(8,128)(2,1)S(1)}, f32[1024,128]{1,0:T(8,128)}, bf16[1024,128]{1,0:T(8,128)(2,1)S(1)}) fusion(bf16[4096,128]{1,0:T(8,128)(2,1)} %collective-permute-done.18, bf16[4096,128]{1,0:T(8,128)(2,1)} %get-tuple-element.21), kind=kLoop, calls=%fused_computation.19 | loop fusion | flops 1966080 | bytes 3407872 | tf_op jit(solution)/shard_map/convert_element_type | solution.py:320
  71.5 3.9 %collective-permute-start.20 = (bf16[1024,128]{1,0:T(8,128)(2,1)S(1)}, bf16[1024,128]{1,0:T(8,128)(2,1)S(1)}, u32[]{:S(2)}, u32[]{:S(2)}) collective-permute-start(bf16[1024,128]{1,0:T(8,128)(2,1)S(1)} %get-tuple-element.56), channel_id=1, source_target_pairs={{0,16},{4,20},{8,24},{12,28},{16,0},{20,4},{24,8},{28,12},{1,17},{... | collective-permute-start | bytes 786440 | tf_op jit(solution)/shard_map/ppermute | solution.py:298
  77.4 8.4 %shard_map.104 = (bf16[4,256,896]{2,1,0:T(8,128)(2,1)}, bf16[4,256,896]{2,1,0:T(8,128)(2,1)}, f32[1024,128]{1,0:T(8,128)}) custom-call(s32[1]{0:T(128)} %bitcast.7.my_ref, bf16[2,256,1024]{2,1,0:T(8,128)(2,1)} %get-tuple-element.20.left_ref, bf16[1024,3584]{1,0:T(8,128)(2,1)} %right_ref.1, ...), custom_call_target="tpu_custom_call", output_to_operand_aliasing={{2}: (5, {})} | custom-call | tf_op jit(solution)/shard_map/pallas_call | solution.py:401
  86.7 1.5 %collective-permute-done.21.refs_3_ = bf16[1024,128]{1,0:T(8,128)(2,1)S(1)} collective-permute-done((bf16[1024,128]{1,0:T(8,128)(2,1)S(1)}, bf16[1024,128]{1,0:T(8,128)(2,1)S(1)}, u32[]{:S(2)}, u32[]{:S(2)}) %collective-permute-start.21) | collective-permute-done | bytes 262176 | tf_op jit(solution)/shard_map/ppermute | solution.py:298
  88.9 2.1 %shard_map.105 = (bf16[1024,128]{1,0:T(8,128)(2,1)}, bf16[4,256,896]{2,1,0:T(8,128)(2,1)}) custom-call(f32[1024,128]{1,0:T(8,128)} %get-tuple-element.23.refs_0_, bf16[1024,128]{1,0:T(8,128)(2,1)} %copy-done.30, bf16[1024,128]{1,0:T(8,128)(2,1)} %copy-done.31, bf16[1024,128]{1,0:T(8,128)(2,1)} %copy-done.34, ...), custom_call_target="tpu_custom_call", output_to_operand_aliasing={{1}: (4, {})} | custom-call | tf_op jit(solution)/shard_map/pallas_call | solution.py:341
  91.7 1.7 %collective-permute-start.16 = (bf16[1024,128]{1,0:T(8,128)(2,1)S(1)}, bf16[1024,128]{1,0:T(8,128)(2,1)S(1)}, u32[]{:S(2)}, u32[]{:S(2)}) collective-permute-start(bf16[1024,128]{1,0:T(8,128)(2,1)S(1)} %copy-done.35), channel_id=1, source_target_pairs={{0,16},{4,20},{8,24},{12,28},{16,0},{20,4},{24,8},{28,12},{1,17},{... | collective-permute-start | bytes 786440 | tf_op jit(solution)/shard_map/ppermute | solution.py:298
  93.4 2.6 %collective-permute-start.26 = (bf16[1024,128]{1,0:T(8,128)(2,1)}, bf16[1024,128]{1,0:T(8,128)(2,1)S(1)}, u32[]{:S(2)}, u32[]{:S(2)}) collective-permute-start(bf16[1024,128]{1,0:T(8,128)(2,1)} %get-tuple-element.25.refs_0_), channel_id=1, source_target_pairs={{0,2},{1,3},{2,0},{3,1},{4,6},{5,7},{6,4},{7,5},{8,10},{9,11},{10,... | collective-permute-start | bytes 786440 | tf_op jit(solution)/shard_map/ppermute | solution.py:289
  97.1 3.0 %collective-permute-done.15.refs_1_ = bf16[1024,128]{1,0:T(8,128)(2,1)S(1)} collective-permute-done((bf16[1024,128]{1,0:T(8,128)(2,1)S(1)}, bf16[1024,128]{1,0:T(8,128)(2,1)S(1)}, u32[]{:S(2)}, u32[]{:S(2)}) %collective-permute-start.15) | collective-permute-done | bytes 262176 | tf_op jit(solution)/shard_map/ppermute | solution.py:298
  100.1 1.6 %collective-permute-start.22 = (bf16[1024,128]{1,0:T(8,128)(2,1)}, bf16[1024,128]{1,0:T(8,128)(2,1)S(1)}, u32[]{:S(2)}, u32[]{:S(2)}) collective-permute-start(bf16[1024,128]{1,0:T(8,128)(2,1)} %get-tuple-element.25.refs_0_), channel_id=1, source_target_pairs={{0,1},{1,0},{2,3},{3,2},{4,5},{5,4},{6,7},{7,6},{8,9},{9,8},{10,11... | collective-permute-start | bytes 786440 | tf_op jit(solution)/shard_map/ppermute | solution.py:289
  101.7 6.7 %collective-permute-done.26.refs_2_ = bf16[1024,128]{1,0:T(8,128)(2,1)S(1)} collective-permute-done((bf16[1024,128]{1,0:T(8,128)(2,1)}, bf16[1024,128]{1,0:T(8,128)(2,1)S(1)}, u32[]{:S(2)}, u32[]{:S(2)}) %collective-permute-start.26) | collective-permute-done | bytes 262176 | tf_op jit(solution)/shard_map/ppermute | solution.py:289
  109.1 4.9 %collective-permute-done.22.refs_6_.refs_1_ = bf16[1024,128]{1,0:T(8,128)(2,1)S(1)} collective-permute-done((bf16[1024,128]{1,0:T(8,128)(2,1)}, bf16[1024,128]{1,0:T(8,128)(2,1)S(1)}, u32[]{:S(2)}, u32[]{:S(2)}) %collective-permute-start.22) | collective-permute-done | bytes 262176 | tf_op jit(solution)/shard_map/ppermute | solution.py:289
  114.8 2.5 %shard_map.106 = (bf16[1024,128]{1,0:T(8,128)(2,1)}, bf16[4,256,896]{2,1,0:T(8,128)(2,1)}) custom-call(f32[1024,128]{1,0:T(8,128)} %get-tuple-element.62.refs_0_, bf16[1024,128]{1,0:T(8,128)(2,1)} %copy-done.28, bf16[1024,128]{1,0:T(8,128)(2,1)} %copy-done.29, bf16[1024,128]{1,0:T(8,128)(2,1)} %copy-done.33, ...), custom_call_target="tpu_custom_call", output_to_operand_aliasing={{1}: (7, {})} | custom-call | tf_op jit(solution)/shard_map/pallas_call | solution.py:341
  117.3 2.9 %add_convert_fusion = (bf16[1,256,896]{2,1,0:T(8,128)(2,1)S(1)}, bf16[1,256,896]{2,1,0:T(8,128)(2,1)S(1)}, bf16[1,256,896]{2,1,0:T(8,128)(2,1)}, f32[1,256,896]{2,1,0:T(8,128)}) fusion(bf16[4,256,896]{2,1,0:T(8,128)(2,1)S(1)} %collective-permute-done.28, bf16[4,256,896]{2,1,0:T(8,128)(2,1)} %get-tuple-element.28), kind=kLoop, calls=%fused_computation.3 | loop fusion | flops 3440640 | bytes 5963776 | tf_op jit(solution)/shard_map/convert_element_type | solution.py:320
  121.9 1.8 %collective-permute-start.31 = (bf16[1,256,896]{2,1,0:T(8,128)(2,1)S(1)}, bf16[1,256,896]{2,1,0:T(8,128)(2,1)}, u32[]{:S(2)}, u32[]{:S(2)}) collective-permute-start(bf16[1,256,896]{2,1,0:T(8,128)(2,1)S(1)} %get-tuple-element.51), channel_id=1, source_target_pairs={{0,24},{4,28},{8,16},{12,20},{16,8},{20,12},{24,0},{28,4},{1,25},{... | collective-permute-start | bytes 1376264 | tf_op jit(solution)/shard_map/ppermute | solution.py:298
  123.7 1.7 %collective-permute-start.24 = (bf16[1024,128]{1,0:T(8,128)(2,1)}, bf16[1024,128]{1,0:T(8,128)(2,1)S(1)}, u32[]{:S(2)}, u32[]{:S(2)}) collective-permute-start(bf16[1024,128]{1,0:T(8,128)(2,1)} %get-tuple-element.27.refs_0_), channel_id=1, source_target_pairs={{0,2},{1,3},{2,0},{3,1},{4,6},{5,7},{6,4},{7,5},{8,10},{9,11},{10,... | collective-permute-start | bytes 786440 | tf_op jit(solution)/shard_map/ppermute | solution.py:289
  126.1 2.4 %collective-permute-start.23 = (bf16[1024,128]{1,0:T(8,128)(2,1)}, bf16[1024,128]{1,0:T(8,128)(2,1)S(1)}, u32[]{:S(2)}, u32[]{:S(2)}) collective-permute-start(bf16[1024,128]{1,0:T(8,128)(2,1)} %get-tuple-element.27.refs_0_), channel_id=1, source_target_pairs={{0,1},{1,0},{2,3},{3,2},{4,5},{5,4},{6,7},{7,6},{8,9},{9,8},{10,11... | collective-permute-start | bytes 786440 | tf_op jit(solution)/shard_map/ppermute | solution.py:289
  128.5 7.4 %collective-permute-done.24.refs_2_.refs_5_ = bf16[1024,128]{1,0:T(8,128)(2,1)S(1)} collective-permute-done((bf16[1024,128]{1,0:T(8,128)(2,1)}, bf16[1024,128]{1,0:T(8,128)(2,1)S(1)}, u32[]{:S(2)}, u32[]{:S(2)}) %collective-permute-start.24) | collective-permute-done | bytes 262176 | tf_op jit(solution)/shard_map/ppermute | solution.py:289
  136.6 2.2 %shard_map.108.refs_6_ = bf16[1024,512]{1,0:T(8,128)(2,1)} custom-call(s32[1]{0:T(128)} %bitcast.6.my_ref, bf16[1024,128]{1,0:T(8,128)(2,1)} %get-tuple-element.25.refs_0_, bf16[1024,128]{1,0:T(8,128)(2,1)} %copy-done.3, bf16[1024,128]{1,0:T(8,128)(2,1)} %copy-done.19, bf16[1024,128]{1,0:T(8,128)(2,1)} %copy-done.23), custom_call_target="tpu_custom_call" | custom-call | tf_op jit(solution)/shard_map/pallas_call | solution.py:271
  140.8 2.8 %shard_map.109 = f32[1,256,896]{2,1,0:T(8,128)} custom-call(f32[1,256,896]{2,1,0:T(8,128)} %get-tuple-element.54.refs_0_, bf16[1,256,896]{2,1,0:T(8,128)(2,1)} %copy-done.10, bf16[1,256,896]{2,1,0:T(8,128)(2,1)} %copy-done.11, bf16[1,256,896]{2,1,0:T(8,128)(2,1)} %collective-permute-done.31.refs_3_, bf16[1024,128]{1,0:T(8,128)(2,1)} %copy-done.5, ...), custom_call_target="tpu_custom_call" | custom-call | tf_op jit(solution)/shard_map/pallas_call | solution.py:341
  145.7 2.2 %shard_map.107 = bf16[1024,512]{1,0:T(8,128)(2,1)} custom-call(s32[1]{0:T(128)} %bitcast.6.my_ref, bf16[1024,128]{1,0:T(8,128)(2,1)} %get-tuple-element.27.refs_0_, bf16[1024,128]{1,0:T(8,128)(2,1)} %copy-done.5, bf16[1024,128]{1,0:T(8,128)(2,1)} %copy-done.4, bf16[1024,128]{1,0:T(8,128)(2,1)} %copy-done.32), custom_call_target="tpu_custom_call" | custom-call | tf_op jit(solution)/shard_map/pallas_call | solution.py:271
  (150 shorter events, 28.5 us)
Async XLA Ops:
  1.9 24.2 %collective-permute-start.10 = (bf16[1024,128]{1,0:T(8,128)(2,1)S(1)}, bf16[1024,128]{1,0:T(8,128)(2,1)S(1)}, u32[]{:S(2)}, u32[]{:S(2)}) collective-permute-start(bf16[1024,128]{1,0:T(8,128)(2,1)S(1)} %constant_dynamic-slice_fusion.refs_8_), channel_id=1, source_target_pairs={{0,16},{4,20},{8,24},{12,28},{16,0},{20,4},{24,8},{28,12},{1,17},{... | collective-permute-start | bytes 786440 | tf_op jit(solution)/shard_map/ppermute | solution.py:298
  4.9 21.8 %collective-permute-start.12 = (bf16[1024,128]{1,0:T(8,128)(2,1)S(1)}, bf16[1024,128]{1,0:T(8,128)(2,1)S(1)}, u32[]{:S(2)}, u32[]{:S(2)}) collective-permute-start(bf16[1024,128]{1,0:T(8,128)(2,1)S(1)} %constant_dynamic-slice_fusion.refs_8_), channel_id=1, source_target_pairs={{0,24},{4,28},{8,16},{12,20},{16,8},{20,12},{24,0},{28,4},{1,25},{... | collective-permute-start | bytes 786440 | tf_op jit(solution)/shard_map/ppermute | solution.py:298
  6.4 21.8 %collective-permute-start.8 = (bf16[1024,128]{1,0:T(8,128)(2,1)S(1)}, bf16[1024,128]{1,0:T(8,128)(2,1)S(1)}, u32[]{:S(2)}, u32[]{:S(2)}) collective-permute-start(bf16[1024,128]{1,0:T(8,128)(2,1)S(1)} %constant_dynamic-slice_fusion.refs_8_), channel_id=1, source_target_pairs={{0,8},{4,12},{8,0},{12,4},{16,24},{20,28},{24,16},{28,20},{1,9},{5... | collective-permute-start | bytes 786440 | tf_op jit(solution)/shard_map/ppermute | solution.py:298
  6.5 21.7 %collective-permute-start.7 = (bf16[1024,128]{1,0:T(8,128)(2,1)S(1)}, bf16[1024,128]{1,0:T(8,128)(2,1)S(1)}, u32[]{:S(2)}, u32[]{:S(2)}) collective-permute-start(bf16[1024,128]{1,0:T(8,128)(2,1)S(1)} %constant_dynamic-slice_fusion.refs_8_), channel_id=1, source_target_pairs={{0,4},{4,0},{8,12},{12,8},{16,20},{20,16},{24,28},{28,24},{1,5},{5... | collective-permute-start | bytes 786440 | tf_op jit(solution)/shard_map/ppermute | solution.py:298
  8.6 11.0 %all-to-all-start = ((s32[8,8,128]{2,1,0:T(8,128)}), s32[8,8,128]{2,1,0:T(8,128)S(1)}, u32[]{:S(2)}, u32[]{:S(2)}) async-start(s32[8,8,128]{2,1,0:T(8,128)} %broadcast_in_dim.40), calls=%async_computation | async-start | bytes 65536 | tf_op jit(solution)/shard_map/all_to_all | solution.py:434
  24.7 12.4 %collective-permute-start.1 = (bf16[1024,128]{1,0:T(8,128)(2,1)S(1)}, bf16[1024,128]{1,0:T(8,128)(2,1)S(1)}, u32[]{:S(2)}, u32[]{:S(2)}) collective-permute-start(bf16[1024,128]{1,0:T(8,128)(2,1)S(1)} %get-tuple-element.42.refs_0_), channel_id=1, source_target_pairs={{0,8},{4,12},{8,0},{12,4},{16,24},{20,28},{24,16},{28,20},{1,9},{5... | collective-permute-start | bytes 786440 | tf_op jit(solution)/shard_map/ppermute | solution.py:298
  26.1 13.3 %collective-permute-start.3 = (bf16[1024,128]{1,0:T(8,128)(2,1)S(1)}, bf16[1024,128]{1,0:T(8,128)(2,1)S(1)}, u32[]{:S(2)}, u32[]{:S(2)}) collective-permute-start(bf16[1024,128]{1,0:T(8,128)(2,1)S(1)} %get-tuple-element.42.refs_0_), channel_id=1, source_target_pairs={{0,16},{4,20},{8,24},{12,28},{16,0},{20,4},{24,8},{28,12},{1,17},{... | collective-permute-start | bytes 786440 | tf_op jit(solution)/shard_map/ppermute | solution.py:298
  26.7 12.7 %collective-permute-start.5 = (bf16[1024,128]{1,0:T(8,128)(2,1)S(1)}, bf16[1024,128]{1,0:T(8,128)(2,1)S(1)}, u32[]{:S(2)}, u32[]{:S(2)}) collective-permute-start(bf16[1024,128]{1,0:T(8,128)(2,1)S(1)} %get-tuple-element.42.refs_0_), channel_id=1, source_target_pairs={{0,24},{4,28},{8,16},{12,20},{16,8},{20,12},{24,0},{28,4},{1,25},{... | collective-permute-start | bytes 786440 | tf_op jit(solution)/shard_map/ppermute | solution.py:298
  28.2 11.8 %collective-permute-start = (bf16[1024,128]{1,0:T(8,128)(2,1)S(1)}, bf16[1024,128]{1,0:T(8,128)(2,1)S(1)}, u32[]{:S(2)}, u32[]{:S(2)}) collective-permute-start(bf16[1024,128]{1,0:T(8,128)(2,1)S(1)} %get-tuple-element.42.refs_0_), channel_id=1, source_target_pairs={{0,4},{4,0},{8,12},{12,8},{16,20},{20,16},{24,28},{28,24},{1,5},{5... | collective-permute-start | bytes 786440 | tf_op jit(solution)/shard_map/ppermute | solution.py:298
  28.2 11.8 %collective-permute-start.11 = (bf16[1024,128]{1,0:T(8,128)(2,1)S(1)}, bf16[1024,128]{1,0:T(8,128)(2,1)S(1)}, u32[]{:S(2)}, u32[]{:S(2)}) collective-permute-start(bf16[1024,128]{1,0:T(8,128)(2,1)S(1)} %collective-permute-done.10.refs_12_), channel_id=1, source_target_pairs={{0,4},{4,0},{8,12},{12,8},{16,20},{20,16},{24,28},{28,24},{1,5},{5... | collective-permute-start | bytes 786440 | tf_op jit(solution)/shard_map/ppermute | solution.py:298
  37.1 4.1 %collective-permute-start.13 = (bf16[1024,128]{1,0:T(8,128)(2,1)S(1)}, bf16[1024,128]{1,0:T(8,128)(2,1)S(1)}, u32[]{:S(2)}, u32[]{:S(2)}) collective-permute-start(bf16[1024,128]{1,0:T(8,128)(2,1)S(1)} %collective-permute-done.12.refs_14_), channel_id=1, source_target_pairs={{0,4},{4,0},{8,12},{12,8},{16,20},{20,16},{24,28},{28,24},{1,5},{5... | collective-permute-start | bytes 786440 | tf_op jit(solution)/shard_map/ppermute | solution.py:298
  39.4 1.9 %collective-permute-start.2 = (bf16[1024,128]{1,0:T(8,128)(2,1)S(1)}, bf16[1024,128]{1,0:T(8,128)(2,1)S(1)}, u32[]{:S(2)}, u32[]{:S(2)}) collective-permute-start(bf16[1024,128]{1,0:T(8,128)(2,1)S(1)} %collective-permute-done.1.refs_2_), channel_id=1, source_target_pairs={{0,4},{4,0},{8,12},{12,8},{16,20},{20,16},{24,28},{28,24},{1,5},{5... | collective-permute-start | bytes 786440 | tf_op jit(solution)/shard_map/ppermute | solution.py:298
  40.0 2.0 %collective-permute-start.6 = (bf16[1024,128]{1,0:T(8,128)(2,1)S(1)}, bf16[1024,128]{1,0:T(8,128)(2,1)S(1)}, u32[]{:S(2)}, u32[]{:S(2)}) collective-permute-start(bf16[1024,128]{1,0:T(8,128)(2,1)S(1)} %collective-permute-done.5.refs_6_), channel_id=1, source_target_pairs={{0,4},{4,0},{8,12},{12,8},{16,20},{20,16},{24,28},{28,24},{1,5},{5... | collective-permute-start | bytes 786440 | tf_op jit(solution)/shard_map/ppermute | solution.py:298
  65.2 3.8 %collective-permute-start.18 = (bf16[4096,128]{1,0:T(8,128)(2,1)}, bf16[4096,128]{1,0:T(8,128)(2,1)}, u32[]{:S(2)}, u32[]{:S(2)}) collective-permute-start(bf16[4096,128]{1,0:T(8,128)(2,1)} %get-tuple-element.22), channel_id=1, source_target_pairs={{0,4},{4,0},{8,12},{12,8},{16,20},{20,16},{24,28},{28,24},{1,5},{5... | collective-permute-start | bytes 3145736 | tf_op jit(solution)/shard_map/ppermute | solution.py:298
  65.3 11.0 %collective-permute-start.14 = (bf16[4096,128]{1,0:T(8,128)(2,1)}, bf16[4096,128]{1,0:T(8,128)(2,1)S(1)}, u32[]{:S(2)}, u32[]{:S(2)}) collective-permute-start(bf16[4096,128]{1,0:T(8,128)(2,1)} %get-tuple-element.19), channel_id=1, source_target_pairs={{0,4},{4,0},{8,12},{12,8},{16,20},{20,16},{24,28},{28,24},{1,5},{5... | collective-permute-start | bytes 3145736 | tf_op jit(solution)/shard_map/ppermute | solution.py:298
  71.5 14.3 %collective-permute-start.19 = (bf16[1024,128]{1,0:T(8,128)(2,1)S(1)}, bf16[1024,128]{1,0:T(8,128)(2,1)S(1)}, u32[]{:S(2)}, u32[]{:S(2)}) collective-permute-start(bf16[1024,128]{1,0:T(8,128)(2,1)S(1)} %get-tuple-element.58.refs_0_), channel_id=1, source_target_pairs={{0,8},{4,12},{8,0},{12,4},{16,24},{20,28},{24,16},{28,20},{1,9},{5... | collective-permute-start | bytes 786440 | tf_op jit(solution)/shard_map/ppermute | solution.py:298
  71.5 15.1 %collective-permute-start.20 = (bf16[1024,128]{1,0:T(8,128)(2,1)S(1)}, bf16[1024,128]{1,0:T(8,128)(2,1)S(1)}, u32[]{:S(2)}, u32[]{:S(2)}) collective-permute-start(bf16[1024,128]{1,0:T(8,128)(2,1)S(1)} %get-tuple-element.56), channel_id=1, source_target_pairs={{0,16},{4,20},{8,24},{12,28},{16,0},{20,4},{24,8},{28,12},{1,17},{... | collective-permute-start | bytes 786440 | tf_op jit(solution)/shard_map/ppermute | solution.py:298
  75.5 12.7 %collective-permute-start.21 = (bf16[1024,128]{1,0:T(8,128)(2,1)S(1)}, bf16[1024,128]{1,0:T(8,128)(2,1)S(1)}, u32[]{:S(2)}, u32[]{:S(2)}) collective-permute-start(bf16[1024,128]{1,0:T(8,128)(2,1)S(1)} %get-tuple-element.55), channel_id=1, source_target_pairs={{0,24},{4,28},{8,16},{12,20},{16,8},{20,12},{24,0},{28,4},{1,25},{... | collective-permute-start | bytes 786440 | tf_op jit(solution)/shard_map/ppermute | solution.py:298
  91.0 26.3 %collective-permute-start.28 = (bf16[4,256,896]{2,1,0:T(8,128)(2,1)}, bf16[4,256,896]{2,1,0:T(8,128)(2,1)S(1)}, u32[]{:S(2)}, u32[]{:S(2)}) collective-permute-start(bf16[4,256,896]{2,1,0:T(8,128)(2,1)} %get-tuple-element.29), channel_id=1, source_target_pairs={{0,4},{4,0},{8,12},{12,8},{16,20},{20,16},{24,28},{28,24},{1,5},{5... | collective-permute-start | bytes 5505032 | tf_op jit(solution)/shard_map/ppermute | solution.py:298
  91.0 9.1 %collective-permute-start.15 = (bf16[1024,128]{1,0:T(8,128)(2,1)S(1)}, bf16[1024,128]{1,0:T(8,128)(2,1)S(1)}, u32[]{:S(2)}, u32[]{:S(2)}) collective-permute-start(bf16[1024,128]{1,0:T(8,128)(2,1)S(1)} %copy-done.8), channel_id=1, source_target_pairs={{0,8},{4,12},{8,0},{12,4},{16,24},{20,28},{24,16},{28,20},{1,9},{5... | collective-permute-start | bytes 786440 | tf_op jit(solution)/shard_map/ppermute | solution.py:298
  91.7 17.4 %collective-permute-start.16 = (bf16[1024,128]{1,0:T(8,128)(2,1)S(1)}, bf16[1024,128]{1,0:T(8,128)(2,1)S(1)}, u32[]{:S(2)}, u32[]{:S(2)}) collective-permute-start(bf16[1024,128]{1,0:T(8,128)(2,1)S(1)} %copy-done.35), channel_id=1, source_target_pairs={{0,16},{4,20},{8,24},{12,28},{16,0},{20,4},{24,8},{28,12},{1,17},{... | collective-permute-start | bytes 786440 | tf_op jit(solution)/shard_map/ppermute | solution.py:298
  93.4 15.0 %collective-permute-start.26 = (bf16[1024,128]{1,0:T(8,128)(2,1)}, bf16[1024,128]{1,0:T(8,128)(2,1)S(1)}, u32[]{:S(2)}, u32[]{:S(2)}) collective-permute-start(bf16[1024,128]{1,0:T(8,128)(2,1)} %get-tuple-element.25.refs_0_), channel_id=1, source_target_pairs={{0,2},{1,3},{2,0},{3,1},{4,6},{5,7},{6,4},{7,5},{8,10},{9,11},{10,... | collective-permute-start | bytes 786440 | tf_op jit(solution)/shard_map/ppermute | solution.py:289
  96.0 13.1 %collective-permute-start.17 = (bf16[1024,128]{1,0:T(8,128)(2,1)S(1)}, bf16[1024,128]{1,0:T(8,128)(2,1)S(1)}, u32[]{:S(2)}, u32[]{:S(2)}) collective-permute-start(bf16[1024,128]{1,0:T(8,128)(2,1)S(1)} %get-tuple-element.59), channel_id=1, source_target_pairs={{0,24},{4,28},{8,16},{12,20},{16,8},{20,12},{24,0},{28,4},{1,25},{... | collective-permute-start | bytes 786440 | tf_op jit(solution)/shard_map/ppermute | solution.py:298
  100.1 13.9 %collective-permute-start.22 = (bf16[1024,128]{1,0:T(8,128)(2,1)}, bf16[1024,128]{1,0:T(8,128)(2,1)S(1)}, u32[]{:S(2)}, u32[]{:S(2)}) collective-permute-start(bf16[1024,128]{1,0:T(8,128)(2,1)} %get-tuple-element.25.refs_0_), channel_id=1, source_target_pairs={{0,1},{1,0},{2,3},{3,2},{4,5},{5,4},{6,7},{7,6},{8,9},{9,8},{10,11... | collective-permute-start | bytes 786440 | tf_op jit(solution)/shard_map/ppermute | solution.py:289
  108.4 17.0 %collective-permute-start.27 = (bf16[1024,128]{1,0:T(8,128)(2,1)S(1)}, bf16[1024,128]{1,0:T(8,128)(2,1)S(1)}, u32[]{:S(2)}, u32[]{:S(2)}) collective-permute-start(bf16[1024,128]{1,0:T(8,128)(2,1)S(1)} %collective-permute-done.26.refs_2_), channel_id=1, source_target_pairs={{0,1},{1,0},{2,3},{3,2},{4,5},{5,4},{6,7},{7,6},{8,9},{9,8},{10,11... | collective-permute-start | bytes 786440 | tf_op jit(solution)/shard_map/ppermute | solution.py:289
  120.2 18.6 %collective-permute-start.29 = (bf16[1,256,896]{2,1,0:T(8,128)(2,1)}, bf16[1,256,896]{2,1,0:T(8,128)(2,1)S(1)}, u32[]{:S(2)}, u32[]{:S(2)}) collective-permute-start(bf16[1,256,896]{2,1,0:T(8,128)(2,1)} %get-tuple-element.53), channel_id=1, source_target_pairs={{0,8},{4,12},{8,0},{12,4},{16,24},{20,28},{24,16},{28,20},{1,9},{5... | collective-permute-start | bytes 1376264 | tf_op jit(solution)/shard_map/ppermute | solution.py:298
  120.9 18.7 %collective-permute-start.30 = (bf16[1,256,896]{2,1,0:T(8,128)(2,1)S(1)}, bf16[1,256,896]{2,1,0:T(8,128)(2,1)S(1)}, u32[]{:S(2)}, u32[]{:S(2)}) collective-permute-start(bf16[1,256,896]{2,1,0:T(8,128)(2,1)S(1)} %get-tuple-element.52), channel_id=1, source_target_pairs={{0,16},{4,20},{8,24},{12,28},{16,0},{20,4},{24,8},{28,12},{1,17},{... | collective-permute-start | bytes 1376264 | tf_op jit(solution)/shard_map/ppermute | solution.py:298
  121.9 18.9 %collective-permute-start.31 = (bf16[1,256,896]{2,1,0:T(8,128)(2,1)S(1)}, bf16[1,256,896]{2,1,0:T(8,128)(2,1)}, u32[]{:S(2)}, u32[]{:S(2)}) collective-permute-start(bf16[1,256,896]{2,1,0:T(8,128)(2,1)S(1)} %get-tuple-element.51), channel_id=1, source_target_pairs={{0,24},{4,28},{8,16},{12,20},{16,8},{20,12},{24,0},{28,4},{1,25},{... | collective-permute-start | bytes 1376264 | tf_op jit(solution)/shard_map/ppermute | solution.py:298
  123.7 12.2 %collective-permute-start.24 = (bf16[1024,128]{1,0:T(8,128)(2,1)}, bf16[1024,128]{1,0:T(8,128)(2,1)S(1)}, u32[]{:S(2)}, u32[]{:S(2)}) collective-permute-start(bf16[1024,128]{1,0:T(8,128)(2,1)} %get-tuple-element.27.refs_0_), channel_id=1, source_target_pairs={{0,2},{1,3},{2,0},{3,1},{4,6},{5,7},{6,4},{7,5},{8,10},{9,11},{10,... | collective-permute-start | bytes 786440 | tf_op jit(solution)/shard_map/ppermute | solution.py:289
  126.1 12.7 %collective-permute-start.23 = (bf16[1024,128]{1,0:T(8,128)(2,1)}, bf16[1024,128]{1,0:T(8,128)(2,1)S(1)}, u32[]{:S(2)}, u32[]{:S(2)}) collective-permute-start(bf16[1024,128]{1,0:T(8,128)(2,1)} %get-tuple-element.27.refs_0_), channel_id=1, source_target_pairs={{0,1},{1,0},{2,3},{3,2},{4,5},{5,4},{6,7},{7,6},{8,9},{9,8},{10,11... | collective-permute-start | bytes 786440 | tf_op jit(solution)/shard_map/ppermute | solution.py:289
  135.9 9.1 %collective-permute-start.25 = (bf16[1024,128]{1,0:T(8,128)(2,1)S(1)}, bf16[1024,128]{1,0:T(8,128)(2,1)S(1)}, u32[]{:S(2)}, u32[]{:S(2)}) collective-permute-start(bf16[1024,128]{1,0:T(8,128)(2,1)S(1)} %collective-permute-done.24.refs_2_.refs_5_), channel_id=1, source_target_pairs={{0,1},{1,0},{2,3},{3,2},{4,5},{5,4},{6,7},{7,6},{8,9},{9,8},{10,11... | collective-permute-start | bytes 786440 | tf_op jit(solution)/shard_map/ppermute | solution.py:289
  144.9 3.0 %collective-permute-start.32 = (bf16[256,448]{1,0:T(8,128)(2,1)S(1)}, bf16[256,448]{1,0:T(8,128)(2,1)S(1)}, u32[]{:S(2)}, u32[]{:S(2)}) collective-permute-start(bf16[256,448]{1,0:T(8,128)(2,1)S(1)} %select_convert_fusion), channel_id=1, source_target_pairs={{0,4},{4,0},{8,12},{12,8},{16,20},{20,16},{24,28},{28,24},{1,5},{5... | collective-permute-start | bytes 688136 | tf_op jit(solution)/shard_map/ppermute | solution.py:298
  (39 other events, 199.2 us)

commit v9 on v8

--- a/solution.py
+++ b/solution.py
@@ -90,8 +90,7 @@
     odd_ref,
     query_ref,
     up_ref,
-    cos_ref,
-    sin_ref,
+    up_t_ref,
     place_ref,
     *refs,
 ):
@@ -146,8 +145,6 @@
         wide = heads if count <= 4 else min(2, heads)
         cols = wide * ROWBLK
         base = pl.multiple_of(block * ROWBLK, ROWBLK)
-        cosine = cos_ref[pl.ds(base, ROWBLK), :]
-        sine = sin_ref[pl.ds(base, ROWBLK), :]
         place = place_ref[pl.ds(block, 1), :]
         lane = lax.broadcasted_iota(jnp.int32, (1, ROWBLK), 1)
         last = (slot - first) * ROWBLK + lane
@@ -160,17 +157,11 @@
         gkey = jnp.zeros((rows, HD), jnp.float32)
         gvalue = jnp.zeros((rows, HD), jnp.float32)
         for group in range(heads // wide):
-            queries = []
-            ups = []
-            for item in range(wide):
-                at = (group * wide + item) * HD
-                raw = query_ref[pl.ds(base, ROWBLK), pl.ds(at, HD)].astype(jnp.float32)
-                turned = raw * cosine + pltpu.roll(raw, HD // 2, 1) * sine
-                queries.append(turned.astype(jnp.bfloat16))
-                ups.append(up_ref[pl.ds(base, ROWBLK), pl.ds(at, HD)])
-            query = jnp.concatenate(queries, axis=0)
-            up = jnp.concatenate(ups, axis=0)
-            up_t = jnp.concatenate([u.astype(jnp.float32).T for u in ups], axis=1)
+            columns = [pl.ds((group * wide + item) * HD, HD) for item in range(wide)]
+            at_rows = pl.ds(base, ROWBLK)
+            query = jnp.concatenate([query_ref[at_rows, at] for at in columns], axis=0)
+            up = jnp.concatenate([up_ref[at_rows, at] for at in columns], axis=0)
+            up_t = jnp.concatenate([up_t_ref[at, at_rows] for at in columns], axis=1)
             score = lax.dot_general(keys, query, NT, preferred_element_type=jnp.float32)
             score = jnp.where(allowed, score, masked_score)
             peak = jnp.max(score, axis=0, keepdims=True)
@@ -180,21 +171,20 @@
             prob_b = prob.astype(jnp.bfloat16)
             out_t = lax.dot_general(values, prob_b, TN, preferred_element_type=jnp.float32)
             out_b = out_t.astype(jnp.bfloat16)
-            delta = jnp.sum(up_t * out_b.astype(jnp.float32), axis=0, keepdims=True)
+            delta = jnp.sum(
+                up_t.astype(jnp.float32) * out_b.astype(jnp.float32), axis=0, keepdims=True
+            )
             gprob = lax.dot_general(values, up, NT, preferred_element_type=jnp.float32)
             gscore = (prob * (gprob - delta)).astype(jnp.bfloat16)
             gquery_t = lax.dot_general(keys, gscore, TN, preferred_element_type=jnp.float32)
             gkey = gkey + jnp.dot(gscore, query, preferred_element_type=jnp.float32)
             gvalue = gvalue + jnp.dot(prob_b, up, preferred_element_type=jnp.float32)
             for item in range(wide):
-                at = (group * wide + item) * HD
                 part = slice(item * ROWBLK, (item + 1) * ROWBLK)
                 head = group * wide + item
                 half, row = head * 2 // heads, head % (heads // 2) * HD
-                out_ref[half ^ odd_ref[0], pl.ds(row, HD), pl.ds(base, ROWBLK)] = out_b[:, part]
-                grad = gquery_t[:, part].T * scale
-                back = grad * cosine - pltpu.roll(grad, HD // 2, 1) * sine
-                gquery_ref[pl.ds(base, ROWBLK), pl.ds(at, HD)] = back.astype(jnp.bfloat16)
+                out_ref[half ^ odd_ref[0], pl.ds(row, HD), at_rows] = out_b[:, part]
+                gquery_ref[columns[item], at_rows] = gquery_t[:, part]
         gkey = (gkey * scale).astype(jnp.bfloat16)
         gvalue = gvalue.astype(jnp.bfloat16)
         place_at = pl.ds(pl.multiple_of(first * ROWBLK, ROWBLK), rows)
@@ -220,7 +210,7 @@
         stores(block, lambda copy: copy.wait())
 
 
-def attend(tables, query, up, cosine, sine, places, keys, values):
+def attend(tables, query, up, up_t, places, keys, values):
     rows, width = query.shape
     heads = width // HD
     ranks = len(keys)
@@ -232,14 +222,14 @@
     return pl.pallas_call(
         partial(attend_kernel, heads, ranks),
         out_shape=(
-            jax.ShapeDtypeStruct((rows, width), jnp.bfloat16),
+            jax.ShapeDtypeStruct((width, rows), jnp.float32),
             jax.ShapeDtypeStruct((2, width // 2, rows), jnp.bfloat16),
             half,
             half,
             half,
             half,
         ),
-        in_specs=[smem] * 6 + [vmem] * 5 + [hbm] * (2 * ranks),
+        in_specs=[smem] * 6 + [vmem] * 4 + [hbm] * (2 * ranks),
         out_specs=(vmem, vmem, hbm, hbm, hbm, hbm),
         scratch_shapes=[pltpu.VMEM((every, HD), jnp.bfloat16)] * 2
         + [pltpu.VMEM((2, RUN_BLOCKS * ROWBLK, HD), jnp.bfloat16)] * 2
@@ -247,7 +237,7 @@
         + [pltpu.SemaphoreType.DMA((2, ranks)), pltpu.SemaphoreType.DMA((2, 2, RUN_BLOCKS))],
         compiler_params=pltpu.CompilerParams(vmem_limit_bytes=VMEM_BYTES),
         cost_estimate=NO_COST,
-    )(*tables, query, up, cosine, sine, places, *keys, *values)
+    )(*tables, query, up, up_t, places, *keys, *values)
 
 
 def assemble_kernel(lanes, my_ref, *refs):
@@ -351,29 +341,103 @@
     return results if thru else results[0]
 
 
-def up_kernel(rows_ref, weight_ref, *refs):
+def prepare_kernel(
+    rows_ref, weight_ref, query_ref, cos_ref, sin_ref, *refs
+):
+    up_ref, up_t_ref, turned_ref = refs[-3:]
     total = jnp.dot(rows_ref[...], weight_ref[...], preferred_element_type=jnp.float32)
-    refs[-1][...] = total.astype(refs[-1].dtype)
-
-
-def up_product(rows, weight, after):
+    up_ref[...] = total.astype(up_ref.dtype)
+    up_t_ref[...] = total.T.astype(up_t_ref.dtype)
+    for at in range(0, query_ref.shape[1], HD):
+        raw = query_ref[:, at : at + HD].astype(jnp.float32)
+        turned = raw * cos_ref[...] + pltpu.roll(raw, HD // 2, 1) * sin_ref[...]
+        turned_ref[:, at : at + HD] = turned.astype(turned_ref.dtype)
+
+
+def prepare(rows, weight, query, cosine, sine, after):
     height, depth = rows.shape
+    width = weight.shape[1]
     steps = 4
+    tall = height // steps
+    across = lambda columns: pl.BlockSpec((tall, columns), lambda step: (step, 0))
     return pl.pallas_call(
-        up_kernel,
+        prepare_kernel,
         grid=(steps,),
-        out_shape=jax.ShapeDtypeStruct((height, weight.shape[1]), jnp.bfloat16),
+        out_shape=[
+            jax.ShapeDtypeStruct((height, width), jnp.bfloat16),
+            jax.ShapeDtypeStruct((width, height), jnp.bfloat16),
+            jax.ShapeDtypeStruct(query.shape, jnp.bfloat16),
+        ],
         in_specs=[
-            pl.BlockSpec((height // steps, depth), lambda step: (step, 0)),
+            across(depth),
             pl.BlockSpec(weight.shape, lambda step: (0, 0)),
+            across(width),
+            across(HD),
+            across(HD),
         ]
         + [pl.BlockSpec(memory_space=pl.ANY)] * len(after),
-        out_specs=pl.BlockSpec((height // steps, weight.shape[1]), lambda step: (step, 0)),
+        out_specs=[
+            across(width),
+            pl.BlockSpec((width, tall), lambda step: (0, step)),
+            across(width),
+        ],
         compiler_params=pltpu.CompilerParams(vmem_limit_bytes=VMEM_BYTES),
         cost_estimate=pl.CostEstimate(
             flops=2 * height * weight.size, bytes_accessed=2 * rows.size, transcendentals=0
         ),
-    )(rows, weight, *after)
+    )(rows, weight, query, cosine, sine, *after)
+
+
+def turn_back_kernel(grad_ref, cos_ref, sin_ref, *refs):
+    out_ref = refs[-1]
+    scale = 1.0 / math.sqrt(HD)
+    for at in range(0, grad_ref.shape[0], HD):
+        grad = grad_ref[at : at + HD, :].T * scale
+        back = grad * cos_ref[...] - pltpu.roll(grad, HD // 2, 1) * sin_ref[...]
+        out_ref[:, at : at + HD] = back.astype(out_ref.dtype)
+
+
+def turn_back(grad_t, cosine, sine, after):
+    width, height = grad_t.shape
+    steps = 4
+    tall = height // steps
+    return pl.pallas_call(
+        turn_back_kernel,
+        grid=(steps,),
+        out_shape=jax.ShapeDtypeStruct((height, width), jnp.bfloat16),
+        in_specs=[
+            pl.BlockSpec((width, tall), lambda step: (0, step)),
+            pl.BlockSpec((tall, HD), lambda step: (step, 0)),
+            pl.BlockSpec((tall, HD), lambda step: (step, 0)),
+        ]
+        + [pl.BlockSpec(memory_space=pl.ANY)] * len(after),
+        out_specs=pl.BlockSpec((tall, width), lambda step: (step, 0)),
+        compiler_params=pltpu.CompilerParams(vmem_limit_bytes=VMEM_BYTES),
+        cost_estimate=NO_COST,
+    )(grad_t, cosine, sine, *after)
+
+
+def take_heads_kernel(at_ref, key_ref, value_ref, after_ref, own_key_ref, own_value_ref):
+    own_key_ref[...] = key_ref[...]
+    own_value_ref[...] = value_ref[...]
+
+
+def take_heads(key, value, kv_head, after):
+    rows = key.shape[0]
+    picked = pl.BlockSpec((rows, HD), lambda step, at_ref: (0, at_ref[0]))
+    own = pl.BlockSpec((rows, HD), lambda step, at_ref: (0, 0))
+    shape = jax.ShapeDtypeStruct((rows, HD), key.dtype)
+    return pl.pallas_call(
+        take_heads_kernel,
+        grid_spec=pltpu.PrefetchScalarGridSpec(
+            num_scalar_prefetch=1,
+            grid=(1,),
+            in_specs=[picked, picked, pl.BlockSpec(memory_space=pl.ANY)],
+            out_specs=[own, own],
+        ),
+        out_shape=[shape, shape],
+        cost_estimate=NO_COST,
+    )(kv_head.reshape(1), key, value, after)
 
 
 def product_kernel(my_ref, left_ref, right_ref, *refs):
@@ -427,17 +491,12 @@
     group = HEADS // KV
     bits = [1 << at for at in range(rank_count.bit_length() - 1)]
     kv_head = my_lane * local_heads // group
-    own_key = lax.dynamic_slice_in_dim(key, kv_head * HD, HD, 1)
-    own_value = lax.dynamic_slice_in_dim(value, kv_head * HD, HD, 1)
-
     own_places = positions_of(segments).reshape(1, block_count, ROWBLK)
-    places_all = lax.all_to_all(
-        jnp.broadcast_to(own_places, (rank_count, block_count, ROWBLK)),
-        "dp",
-        split_axis=0,
-        concat_axis=0,
-        tiled=True,
+    pair_places = jnp.concatenate([own_places, swap(own_places, 1)], axis=0)
+    places_all = jnp.concatenate(
+        [pair_places] + [swap(pair_places, step) for step in range(2, rank_count, 2)], axis=0
     ).reshape(-1, ROWBLK)
+    own_key, own_value = take_heads(key, value, kv_head, pair_places)
     values = spread(own_value)
 
     mine = my_rank * block_count + jnp.arange(block_count, dtype=jnp.int32)
@@ -447,13 +506,13 @@
     )
     run = dest // RUN_BLOCKS
     slot = dest % RUN_BLOCKS
-    places = jnp.take(places_all, dest, axis=0)
+    places = jnp.take(places_all, (run ^ my_rank) * RUN_BLOCKS + slot, axis=0)
     need = slot - (slot * ROWBLK - places[:, 0]) // ROWBLK + 1
     cosine, sine = rope_tables(places.reshape(row_count), HD)
     key_f = own_key.astype(jnp.float32)
     rot_key = (key_f * cosine + swap_halves(key_f) * sine).astype(jnp.bfloat16)
     keys = spread(rot_key)
-    up = up_product(grad_out, out_weight, [rot_key])
+    up, up_t, turned = prepare(grad_out, out_weight, query, cosine, sine, [rot_key])
 
     distance = (plan // block_count) ^ my_rank
     within = plan % block_count
@@ -466,8 +525,8 @@
         need,
         (my_rank & 1).reshape(1),
     )
-    grad_query, attn_t, gkey_keep, gkey_send, gvalue_keep, gvalue_send = attend(
-        tables, query, up, cosine, sine, places, keys, values
+    grad_query_t, attn_t, gkey_keep, gkey_send, gvalue_keep, gvalue_send = attend(
+        tables, turned, up, up_t, places, keys, values
     )
     value_keep, value_sends = chip_sum(gvalue_keep, swap(gvalue_send, 1))
     value_received = exchange(value_sends)
@@ -481,12 +540,13 @@
     )
     value_all, value_pieces = lane_gather(value_partial, my_lane)
     weight_other = swap(weight_send, 1)
-    key_partial, weight_keep = final_sum(
-        key_keep, key_received, (cosine, sine), value_pieces[:1], thru=[weight_keep]
-    )
-    key_all, key_pieces = lane_gather(key_partial, my_lane)
+    grad_query = turn_back(grad_query_t, cosine, sine, [weight_send])
     weight_keep, weight_sends = chip_sum(weight_keep, weight_other)
     weight_received = exchange(weight_sends)
+    key_partial = final_sum(
+        key_keep, key_received, (cosine, sine), [weight_sends[0], grad_query]
+    )
+    key_all, key_pieces = lane_gather(key_partial, my_lane)
     total = final_sum(
         weight_keep, weight_received, (), [*key_pieces[:2], value_all], jnp.float32
     )[0]

time: 151 us -> 150 us (level)
  starting transfers between devices: 36 us -> 40.9 us
  waiting for transfers between devices: 35.5 us -> 31.9 us
  Pallas kernels: 50.9 us -> 54.4 us
  other arithmetic: 18.3 us -> 14.9 us
    ppermute x27 -> x31, starting transfers between devices: 22.1 us -> 31.9 us  [swap(): lax.ppermute(array, 'dp', [(rank, rank ^ bit) for rank in range(ranks)])]
    pallas_call x1 -> x3, Pallas kernels: 8.36 us -> 15.7 us  [the longest x1 9.4 us: prepare(): pl.pallas_call(prepare_kernel, grid=(steps,), out_shape=[jax.ShapeDtypeSt...]
    all_to_all x1 -> x0, starting transfers between devices: 4.26 us -> none  [local(): lax.all_to_all(jnp.broadcast_to(own_places, (rank_count, block_count, ROW...]
    pallas_call x1, Pallas kernels: 22.4 us -> 18.6 us  [attend(): pl.pallas_call(partial(attend_kernel, heads, ranks), out_shape=(jax.Shape...]
    all_to_all x1 -> x0, waiting for transfers between devices: 2.92 us -> none  [local(): lax.all_to_all(jnp.broadcast_to(own_places, (rank_count, block_count, ROW...]
    convert_element_type x3, other arithmetic: 6.6 us -> 4.71 us  [chip_sum(): return (total[0], [item.astype(keep.dtype) for item in total[1:]])]
    unnamed x75 -> x82, local copies, waits for them, and re-layouts: 5.98 us -> 4.63 us
    ppermute x27 -> x31, waiting for transfers between devices: 13.5 us -> 14 us  [swap(): lax.ppermute(array, 'dp', [(rank, rank ^ bit) for rank in range(ranks)])]
  transfers between devices with their start and end apart: 34 -> 37, of which waited for: 14 -> 9; matrix products, arithmetic and copies ran while one was open for 13% -> 10% of each run, Pallas kernels for 18% -> 23%
where the time goes in v9:
time: 150 us
  Pallas kernels  54.4 us (36%)
  starting transfers between devices  40.9 us (27%)
  waiting for transfers between devices  31.9 us (21%)
  other arithmetic  14.9 us (10%)
  local copies, waits for them, and re-layouts  6.72 us (4%)
    ppermute x31, starting transfers between devices, swap(): lax.ppermute(array, 'dp', [(rank, rank ^ bit) for rank in range(ranks)])  31.9 us
    pallas_call x1, Pallas kernels, attend(): pl.pallas_call(partial(attend_kernel, heads, ranks), out_shape=(jax.Shape...  18.6 us
    ppermute x6, waiting for transfers between devices, lane_gather(): lax.ppermute(item, 'tensor', pairs)  17.9 us
    ppermute x31, waiting for transfers between devices, swap(): lax.ppermute(array, 'dp', [(rank, rank ^ bit) for rank in range(ranks)])  14 us
    pallas_call x1, Pallas kernels, prepare(): pl.pallas_call(prepare_kernel, grid=(steps,), out_shape=[jax.ShapeDtypeSt...  9.4 us
    ppermute x6, starting transfers between devices, lane_gather(): lax.ppermute(item, 'tensor', pairs)  9.02 us
    pallas_call x1, Pallas kernels, product(): pl.pallas_call(product_kernel, grid_spec=pltpu.PrefetchScalarGridSpec(num...  8.51 us
    pallas_call x3, Pallas kernels, final_sum(): pl.pallas_call(partial(final_kernel, len(received), len(tables) > 0, inpu...  7.33 us
  transfers between devices with their start and end apart: 37, of which 9 were waited for; matrix products, arithmetic and copies ran while one was open for 10% of the time, Pallas kernels for 23%

profile of v9, /device:TPU:0, one launch (start us, length us, event | category | flops | bytes accessed | tf_op | source)
XLA Modules:
  0.0 150.0 jit_solution(14411186489134796846)
XLA Ops:
  5.7 2.6 %collective-permute-start.1 = (s32[2,8,128]{2,1,0:T(8,128)S(1)}, s32[2,8,128]{2,1,0:T(8,128)S(1)}, u32[]{:S(2)}, u32[]{:S(2)}) collective-permute-start(s32[2,8,128]{2,1,0:T(8,128)S(1)} %pad_add_fusion.after_ref), channel_id=1, source_target_pairs={{0,8},{4,12},{8,0},{12,4},{16,24},{20,28},{24,16},{28,20},{1,9},{5... | collective-permute-start | bytes 24584 | tf_op jit(solution)/shard_map/ppermute | solution.py:288
  8.3 1.5 %collective-permute-start.2 = (s32[2,8,128]{2,1,0:T(8,128)S(1)}, s32[2,8,128]{2,1,0:T(8,128)S(1)}, u32[]{:S(2)}, u32[]{:S(2)}) collective-permute-start(s32[2,8,128]{2,1,0:T(8,128)S(1)} %pad_add_fusion.after_ref), channel_id=1, source_target_pairs={{0,16},{4,20},{8,24},{12,28},{16,0},{20,4},{24,8},{28,12},{1,17},{... | collective-permute-start | bytes 24584 | tf_op jit(solution)/shard_map/ppermute | solution.py:288
  9.8 1.8 %shard_map.102 = (bf16[1024,128]{1,0:T(8,128)(2,1)}, bf16[1024,128]{1,0:T(8,128)(2,1)}) custom-call(s32[1]{0:T(128)} %bitcast.7.at_ref, bf16[1024,512]{1,0:T(8,128)(2,1)} %key_ref.1, bf16[1024,512]{1,0:T(8,128)(2,1)} %value_ref.1, s32[2,8,128]{2,1,0:T(8,128)} %copy-done.37), custom_call_target="tpu_custom_call" | custom-call | tf_op jit(solution)/shard_map/pallas_call | solution.py:430
  11.7 1.9 %collective-permute-start.12 = (bf16[1024,128]{1,0:T(8,128)(2,1)}, bf16[1024,128]{1,0:T(8,128)(2,1)S(1)}, u32[]{:S(2)}, u32[]{:S(2)}) collective-permute-start(bf16[1024,128]{1,0:T(8,128)(2,1)} %get-tuple-element.24.refs_8_), channel_id=1, source_target_pairs={{0,8},{4,12},{8,0},{12,4},{16,24},{20,28},{24,16},{28,20},{1,9},{5... | collective-permute-start | bytes 786440 | tf_op jit(solution)/shard_map/ppermute | solution.py:288
  13.6 1.5 %collective-permute-start.14 = (bf16[1024,128]{1,0:T(8,128)(2,1)}, bf16[1024,128]{1,0:T(8,128)(2,1)S(1)}, u32[]{:S(2)}, u32[]{:S(2)}) collective-permute-start(bf16[1024,128]{1,0:T(8,128)(2,1)} %get-tuple-element.24.refs_8_), channel_id=1, source_target_pairs={{0,16},{4,20},{8,24},{12,28},{16,0},{20,4},{24,8},{28,12},{1,17},{... | collective-permute-start | bytes 786440 | tf_op jit(solution)/shard_map/ppermute | solution.py:288
  17.2 1.9 %fusion.5 = (f32[1024,64]{1,0:T(8,128)S(1)}, f32[1024,64]{1,0:T(8,128)S(1)}, f32[1024,64]{1,0:T(8,128)S(1)}) fusion(f32[64]{0:T(128)S(1)} %multiply_add_fusion, f32[1024]{0:T(1024)S(1)} %get-tuple-element.50), kind=kLoop, calls=%fused_computation.28 | loop fusion | flops 262144 | bytes 790784 | tf_op jit(solution)/shard_map/neg | solution.py:69
  19.2 1.5 %fusion.4 = (bf16[1024,128]{1,0:T(8,128)(2,1)S(1)}, f32[1024,128]{1,0:T(8,128)}, f32[1024,128]{1,0:T(8,128)}) fusion(f32[1024,64]{1,0:T(8,128)S(1)} %get-tuple-element.76, f32[1024,64]{1,0:T(8,128)S(1)} %get-tuple-element.75, bf16[1024,128]{1,0:T(8,128)(2,1)S(1)} %copy-done.1, f32[1024,64]{1,0:T(8,128)S(1)} %get-tuple-element.79, ...), kind=kLoop, calls=%fused_computation.17 | loop fusion | flops 1048576 | bytes 2883584 | tf_op jit(solution)/shard_map/convert_element_type | solution.py:513
  20.7 2.8 %collective-permute-start.9 = (bf16[1024,128]{1,0:T(8,128)(2,1)S(1)}, bf16[1024,128]{1,0:T(8,128)(2,1)S(1)}, u32[]{:S(2)}, u32[]{:S(2)}) collective-permute-start(bf16[1024,128]{1,0:T(8,128)(2,1)S(1)} %get-tuple-element.48.refs_0_), channel_id=1, source_target_pairs={{0,24},{4,28},{8,16},{12,20},{16,8},{20,12},{24,0},{28,4},{1,25},{... | collective-permute-start | bytes 786440 | tf_op jit(solution)/shard_map/ppermute | solution.py:288
  24.1 9.0 %collective-permute-done.14.refs_12_ = bf16[1024,128]{1,0:T(8,128)(2,1)S(1)} collective-permute-done((bf16[1024,128]{1,0:T(8,128)(2,1)}, bf16[1024,128]{1,0:T(8,128)(2,1)S(1)}, u32[]{:S(2)}, u32[]{:S(2)}) %collective-permute-start.14) | collective-permute-done | bytes 262176 | tf_op jit(solution)/shard_map/ppermute | solution.py:288
  33.1 2.4 %collective-permute-start.7 = (bf16[1024,128]{1,0:T(8,128)(2,1)S(1)}, bf16[1024,128]{1,0:T(8,128)(2,1)S(1)}, u32[]{:S(2)}, u32[]{:S(2)}) collective-permute-start(bf16[1024,128]{1,0:T(8,128)(2,1)S(1)} %get-tuple-element.48.refs_0_), channel_id=1, source_target_pairs={{0,16},{4,20},{8,24},{12,28},{16,0},{20,4},{24,8},{28,12},{1,17},{... | collective-permute-start | bytes 786440 | tf_op jit(solution)/shard_map/ppermute | solution.py:288
  36.0 9.4 %shard_map.103 = (bf16[1024,512]{1,0:T(8,128)(2,1)}, bf16[512,1024]{1,0:T(8,128)(2,1)}, bf16[1024,512]{1,0:T(8,128)(2,1)}) custom-call(bf16[1024,3584]{1,0:T(8,128)(2,1)} %right_ref.1, bf16[3584,512]{1,0:T(8,128)(2,1)} %weight_ref.1, bf16[1024,512]{1,0:T(8,128)(2,1)} %query_ref.1, f32[1024,128]{1,0:T(8,128)} %get-tuple-element.74.cos_ref.refs_4_, ...), custom_call_target="tpu_custom_call" | custom-call | flops 3758096384 | bytes 7340032 | tf_op jit(solution)/shard_map/pallas_call | solution.py:363
  49.2 18.6 %shard_map.104 = (f32[512,1024]{1,0:T(8,128)}, bf16[2,256,1024]{2,1,0:T(8,128)(2,1)}, bf16[4096,128]{1,0:T(8,128)(2,1)}, bf16[4096,128]{1,0:T(8,128)(2,1)}, bf16...) custom-call(s32[64]{0:T(128)} %multiply_add_fusion.2.target_ref, s32[64]{0:T(128)} %get-tuple-element.57.source_ref, ...), custom_call_target="tpu_custom_call" | custom-call | tf_op jit(solution)/shard_map/pallas_call | solution.py:222
  67.8 5.5 %collective-permute-start.18 = (bf16[4096,128]{1,0:T(8,128)(2,1)}, bf16[4096,128]{1,0:T(8,128)(2,1)S(1)}, u32[]{:S(2)}, u32[]{:S(2)}) collective-permute-start(bf16[4096,128]{1,0:T(8,128)(2,1)} %get-tuple-element.28), channel_id=1, source_target_pairs={{0,4},{4,0},{8,12},{12,8},{16,20},{20,16},{24,28},{28,24},{1,5},{5... | collective-permute-start | bytes 3145736 | tf_op jit(solution)/shard_map/ppermute | solution.py:288
  73.4 2.4 %collective-permute-done.18 = bf16[4096,128]{1,0:T(8,128)(2,1)S(1)} collective-permute-done((bf16[4096,128]{1,0:T(8,128)(2,1)}, bf16[4096,128]{1,0:T(8,128)(2,1)S(1)}, u32[]{:S(2)}, u32[]{:S(2)}) %collective-permute-start.18) | collective-permute-done | bytes 1048608 | tf_op jit(solution)/shard_map/ppermute | solution.py:288
  75.9 2.3 %add_convert_fusion.5 = (bf16[1024,128]{1,0:T(8,128)(2,1)S(1)}, bf16[1024,128]{1,0:T(8,128)(2,1)}, f32[1024,128]{1,0:T(8,128)}, bf16[1024,128]{1,0:T(8,128)(2,1)S(1)}) fusion(bf16[4096,128]{1,0:T(8,128)(2,1)S(1)} %collective-permute-done.18, bf16[4096,128]{1,0:T(8,128)(2,1)} %get-tuple-element.27), kind=kLoop, calls=%fused_computation.22 | loop fusion | flops 1966080 | bytes 3407872 | tf_op jit(solution)/shard_map/convert_element_type | solution.py:310
  78.3 3.4 %collective-permute-start.22 = (bf16[1024,128]{1,0:T(8,128)(2,1)S(1)}, bf16[1024,128]{1,0:T(8,128)(2,1)S(1)}, u32[]{:S(2)}, u32[]{:S(2)}) collective-permute-start(bf16[1024,128]{1,0:T(8,128)(2,1)S(1)} %get-tuple-element.68), channel_id=1, source_target_pairs={{0,24},{4,28},{8,16},{12,20},{16,8},{20,12},{24,0},{28,4},{1,25},{... | collective-permute-start | bytes 786440 | tf_op jit(solution)/shard_map/ppermute | solution.py:288
  82.7 8.5 %shard_map.105 = (bf16[4,256,896]{2,1,0:T(8,128)(2,1)}, bf16[4,256,896]{2,1,0:T(8,128)(2,1)}, f32[1024,128]{1,0:T(8,128)}) custom-call(s32[1]{0:T(128)} %bitcast.8.my_ref, bf16[2,256,1024]{2,1,0:T(8,128)(2,1)} %get-tuple-element.26.left_ref, bf16[1024,3584]{1,0:T(8,128)(2,1)} %right_ref.1, ...), custom_call_target="tpu_custom_call", output_to_operand_aliasing={{2}: (5, {})} | custom-call | tf_op jit(solution)/shard_map/pallas_call | solution.py:465
  93.5 2.1 %shard_map.106 = (bf16[1024,128]{1,0:T(8,128)(2,1)}, bf16[4,256,896]{2,1,0:T(8,128)(2,1)}) custom-call(f32[1024,128]{1,0:T(8,128)} %get-tuple-element.31.refs_0_, bf16[1024,128]{1,0:T(8,128)(2,1)} %copy-done.32, bf16[1024,128]{1,0:T(8,128)(2,1)} %copy-done.33, bf16[1024,128]{1,0:T(8,128)(2,1)} %copy-done.34, ...), custom_call_target="tpu_custom_call", output_to_operand_aliasing={{1}: (4, {})} | custom-call | tf_op jit(solution)/shard_map/pallas_call | solution.py:331
  95.6 2.4 %collective-permute-start.31 = (bf16[1024,128]{1,0:T(8,128)(2,1)}, bf16[1024,128]{1,0:T(8,128)(2,1)S(1)}, u32[]{:S(2)}, u32[]{:S(2)}) collective-permute-start(bf16[1024,128]{1,0:T(8,128)(2,1)} %get-tuple-element.35.refs_0_), channel_id=1, source_target_pairs={{0,2},{1,3},{2,0},{3,1},{4,6},{5,7},{6,4},{7,5},{8,10},{9,11},{10,... | collective-permute-start | bytes 786440 | tf_op jit(solution)/shard_map/ppermute | solution.py:279
  98.0 1.7 %collective-permute-start.23 = (bf16[1024,128]{1,0:T(8,128)(2,1)S(1)}, bf16[1024,128]{1,0:T(8,128)(2,1)S(1)}, u32[]{:S(2)}, u32[]{:S(2)}) collective-permute-start(bf16[1024,128]{1,0:T(8,128)(2,1)S(1)} %copy-done.8), channel_id=1, source_target_pairs={{0,8},{4,12},{8,0},{12,4},{16,24},{20,28},{24,16},{28,20},{1,9},{5... | collective-permute-start | bytes 786440 | tf_op jit(solution)/shard_map/ppermute | solution.py:288
  99.9 1.5 %collective-permute-start.25 = (bf16[1024,128]{1,0:T(8,128)(2,1)S(1)}, bf16[1024,128]{1,0:T(8,128)(2,1)S(1)}, u32[]{:S(2)}, u32[]{:S(2)}) collective-permute-start(bf16[1024,128]{1,0:T(8,128)(2,1)S(1)} %get-tuple-element.64), channel_id=1, source_target_pairs={{0,24},{4,28},{8,16},{12,20},{16,8},{20,12},{24,0},{28,4},{1,25},{... | collective-permute-start | bytes 786440 | tf_op jit(solution)/shard_map/ppermute | solution.py:288
  101.5 9.5 %collective-permute-done.31.refs_2_ = bf16[1024,128]{1,0:T(8,128)(2,1)S(1)} collective-permute-done((bf16[1024,128]{1,0:T(8,128)(2,1)}, bf16[1024,128]{1,0:T(8,128)(2,1)S(1)}, u32[]{:S(2)}, u32[]{:S(2)}) %collective-permute-start.31) | collective-permute-done | bytes 262176 | tf_op jit(solution)/shard_map/ppermute | solution.py:279
  114.4 1.7 %collective-permute-start.33 = (bf16[1,256,896]{2,1,0:T(8,128)(2,1)S(1)}, bf16[1,256,896]{2,1,0:T(8,128)(2,1)S(1)}, u32[]{:S(2)}, u32[]{:S(2)}) collective-permute-start(bf16[1,256,896]{2,1,0:T(8,128)(2,1)S(1)} %get-tuple-element.63.refs_6_), channel_id=1, source_target_pairs={{0,8},{4,12},{8,0},{12,4},{16,24},{20,28},{24,16},{28,20},{1,9},{5... | collective-permute-start | bytes 1376264 | tf_op jit(solution)/shard_map/ppermute | solution.py:288
  116.4 1.5 %collective-permute-start.35 = (bf16[1,256,896]{2,1,0:T(8,128)(2,1)S(1)}, bf16[1,256,896]{2,1,0:T(8,128)(2,1)S(1)}, u32[]{:S(2)}, u32[]{:S(2)}) collective-permute-start(bf16[1,256,896]{2,1,0:T(8,128)(2,1)S(1)} %get-tuple-element.60), channel_id=1, source_target_pairs={{0,24},{4,28},{8,16},{12,20},{16,8},{20,12},{24,0},{28,4},{1,25},{... | collective-permute-start | bytes 1376264 | tf_op jit(solution)/shard_map/ppermute | solution.py:288
  118.0 4.4 %shard_map.107.refs_7_ = bf16[1024,512]{1,0:T(8,128)(2,1)} custom-call(f32[512,1024]{1,0:T(8,128)} %get-tuple-element.25.grad_ref, f32[1024,128]{1,0:T(8,128)} %get-tuple-element.74.cos_ref.refs_4_, f32[1024,128]{1,0:T(8,128)} %get-tuple-element.49.sin_ref.refs_5_, bf16[4,256,896]{2,1,0:T(8,128)(2,1)} %get-tuple-element.33.refs_0_), custom_call_target="tpu_custom_call" | custom-call | tf_op jit(solution)/shard_map/pallas_call | solution.py:404
  122.4 2.5 %shard_map.108.refs_0_ = bf16[1024,128]{1,0:T(8,128)(2,1)} custom-call(f32[1024,128]{1,0:T(8,128)} %get-tuple-element.66.refs_0_, bf16[1024,128]{1,0:T(8,128)(2,1)} %copy-done.27, bf16[1024,128]{1,0:T(8,128)(2,1)} %copy-done.28, bf16[1024,128]{1,0:T(8,128)(2,1)} %copy-done.30, f32[1024,128]{1,0:T(8,128)} %get-tuple-element.74.cos_ref.refs_4_, ...), custom_call_target="tpu_custom_call" | custom-call | tf_op jit(solution)/shard_map/pallas_call | solution.py:331
  124.9 1.9 %collective-permute-start.28 = (bf16[1024,128]{1,0:T(8,128)(2,1)}, bf16[1024,128]{1,0:T(8,128)(2,1)S(1)}, u32[]{:S(2)}, u32[]{:S(2)}) collective-permute-start(bf16[1024,128]{1,0:T(8,128)(2,1)} %shard_map.108.refs_0_), channel_id=1, source_target_pairs={{0,2},{1,3},{2,0},{3,1},{4,6},{5,7},{6,4},{7,5},{8,10},{9,11},{10,... | collective-permute-start | bytes 786440 | tf_op jit(solution)/shard_map/ppermute | solution.py:279
  126.9 2.0 %collective-permute-start.27 = (bf16[1024,128]{1,0:T(8,128)(2,1)}, bf16[1024,128]{1,0:T(8,128)(2,1)S(1)}, u32[]{:S(2)}, u32[]{:S(2)}) collective-permute-start(bf16[1024,128]{1,0:T(8,128)(2,1)} %shard_map.108.refs_0_), channel_id=1, source_target_pairs={{0,1},{1,0},{2,3},{3,2},{4,5},{5,4},{6,7},{7,6},{8,9},{9,8},{10,11... | collective-permute-start | bytes 786440 | tf_op jit(solution)/shard_map/ppermute | solution.py:279
  128.8 2.2 %shard_map.110.refs_6_ = bf16[1024,512]{1,0:T(8,128)(2,1)} custom-call(s32[1]{0:T(128)} %bitcast.9.my_ref, bf16[1024,128]{1,0:T(8,128)(2,1)} %get-tuple-element.35.refs_0_, bf16[1024,128]{1,0:T(8,128)(2,1)} %collective-permute-done.30.refs_1_, bf16[1024,128]{1,0:T(8,128)(2,1)} %copy-done.22, bf16[1024,128]{1,0:T(8,128)(2,1)} %collective-permute-done.32.refs_3_), custom_call_target="tpu_custom_call" | custom-call | tf_op jit(solution)/shard_map/pallas_call | solution.py:261
  131.0 7.3 %collective-permute-done.28.refs_2_.refs_5_ = bf16[1024,128]{1,0:T(8,128)(2,1)S(1)} collective-permute-done((bf16[1024,128]{1,0:T(8,128)(2,1)}, bf16[1024,128]{1,0:T(8,128)(2,1)S(1)}, u32[]{:S(2)}, u32[]{:S(2)}) %collective-permute-start.28) | collective-permute-done | bytes 262176 | tf_op jit(solution)/shard_map/ppermute | solution.py:279
  140.2 2.7 %shard_map.111 = f32[1,256,896]{2,1,0:T(8,128)} custom-call(f32[1,256,896]{2,1,0:T(8,128)} %get-tuple-element.62.refs_0_, bf16[1,256,896]{2,1,0:T(8,128)(2,1)} %copy-done.10, bf16[1,256,896]{2,1,0:T(8,128)(2,1)} %copy-done.11, bf16[1,256,896]{2,1,0:T(8,128)(2,1)} %copy-done.12, bf16[1024,128]{1,0:T(8,128)(2,1)} %copy-done.6, bf16[1024,128]{1,0:T(8,128)(2,1)} %copy-done.5, ...), custom_call_target="tpu_custom_call" | custom-call | tf_op jit(solution)/shard_map/pallas_call | solution.py:331
  146.2 2.2 %shard_map.109 = bf16[1024,512]{1,0:T(8,128)(2,1)} custom-call(s32[1]{0:T(128)} %bitcast.9.my_ref, bf16[1024,128]{1,0:T(8,128)(2,1)} %shard_map.108.refs_0_, bf16[1024,128]{1,0:T(8,128)(2,1)} %copy-done.6, bf16[1024,128]{1,0:T(8,128)(2,1)} %copy-done.5, bf16[1024,128]{1,0:T(8,128)(2,1)} %copy-done.35), custom_call_target="tpu_custom_call" | custom-call | tf_op jit(solution)/shard_map/pallas_call | solution.py:261
  (164 shorter events, 26.0 us)
Async XLA Ops:
  2.1 3.6 %collective-permute-start = (s32[1,8,128]{2,1,0:T(8,128)S(1)}, s32[1,8,128]{2,1,0:T(8,128)S(1)}, u32[]{:S(2)}, u32[]{:S(2)}) collective-permute-start(s32[1,8,128]{2,1,0:T(8,128)S(1)} %get-tuple-element.56), channel_id=1, source_target_pairs={{0,4},{4,0},{8,12},{12,8},{16,20},{20,16},{24,28},{28,24},{1,5},{5... | collective-permute-start | bytes 12296 | tf_op jit(solution)/shard_map/ppermute | solution.py:288
  5.7 10.7 %collective-permute-start.1 = (s32[2,8,128]{2,1,0:T(8,128)S(1)}, s32[2,8,128]{2,1,0:T(8,128)S(1)}, u32[]{:S(2)}, u32[]{:S(2)}) collective-permute-start(s32[2,8,128]{2,1,0:T(8,128)S(1)} %pad_add_fusion.after_ref), channel_id=1, source_target_pairs={{0,8},{4,12},{8,0},{12,4},{16,24},{20,28},{24,16},{28,20},{1,9},{5... | collective-permute-start | bytes 24584 | tf_op jit(solution)/shard_map/ppermute | solution.py:288
  8.3 8.2 %collective-permute-start.2 = (s32[2,8,128]{2,1,0:T(8,128)S(1)}, s32[2,8,128]{2,1,0:T(8,128)S(1)}, u32[]{:S(2)}, u32[]{:S(2)}) collective-permute-start(s32[2,8,128]{2,1,0:T(8,128)S(1)} %pad_add_fusion.after_ref), channel_id=1, source_target_pairs={{0,16},{4,20},{8,24},{12,28},{16,0},{20,4},{24,8},{28,12},{1,17},{... | collective-permute-start | bytes 24584 | tf_op jit(solution)/shard_map/ppermute | solution.py:288
  9.8 6.8 %collective-permute-start.3 = (s32[2,8,128]{2,1,0:T(8,128)S(1)}, s32[2,8,128]{2,1,0:T(8,128)S(1)}, u32[]{:S(2)}, u32[]{:S(2)}) collective-permute-start(s32[2,8,128]{2,1,0:T(8,128)S(1)} %pad_add_fusion.after_ref), channel_id=1, source_target_pairs={{0,24},{4,28},{8,16},{12,20},{16,8},{20,12},{24,0},{28,4},{1,25},{... | collective-permute-start | bytes 24584 | tf_op jit(solution)/shard_map/ppermute | solution.py:288
  11.7 11.9 %collective-permute-start.12 = (bf16[1024,128]{1,0:T(8,128)(2,1)}, bf16[1024,128]{1,0:T(8,128)(2,1)S(1)}, u32[]{:S(2)}, u32[]{:S(2)}) collective-permute-start(bf16[1024,128]{1,0:T(8,128)(2,1)} %get-tuple-element.24.refs_8_), channel_id=1, source_target_pairs={{0,8},{4,12},{8,0},{12,4},{16,24},{20,28},{24,16},{28,20},{1,9},{5... | collective-permute-start | bytes 786440 | tf_op jit(solution)/shard_map/ppermute | solution.py:288
  13.6 19.4 %collective-permute-start.14 = (bf16[1024,128]{1,0:T(8,128)(2,1)}, bf16[1024,128]{1,0:T(8,128)(2,1)S(1)}, u32[]{:S(2)}, u32[]{:S(2)}) collective-permute-start(bf16[1024,128]{1,0:T(8,128)(2,1)} %get-tuple-element.24.refs_8_), channel_id=1, source_target_pairs={{0,16},{4,20},{8,24},{12,28},{16,0},{20,4},{24,8},{28,12},{1,17},{... | collective-permute-start | bytes 786440 | tf_op jit(solution)/shard_map/ppermute | solution.py:288
  16.4 19.0 %collective-permute-start.16 = (bf16[1024,128]{1,0:T(8,128)(2,1)S(1)}, bf16[1024,128]{1,0:T(8,128)(2,1)S(1)}, u32[]{:S(2)}, u32[]{:S(2)}) collective-permute-start(bf16[1024,128]{1,0:T(8,128)(2,1)S(1)} %copy-done.13), channel_id=1, source_target_pairs={{0,24},{4,28},{8,16},{12,20},{16,8},{20,12},{24,0},{28,4},{1,25},{... | collective-permute-start | bytes 786440 | tf_op jit(solution)/shard_map/ppermute | solution.py:288
  16.5 18.9 %collective-permute-start.11 = (bf16[1024,128]{1,0:T(8,128)(2,1)S(1)}, bf16[1024,128]{1,0:T(8,128)(2,1)S(1)}, u32[]{:S(2)}, u32[]{:S(2)}) collective-permute-start(bf16[1024,128]{1,0:T(8,128)(2,1)S(1)} %copy-done.13), channel_id=1, source_target_pairs={{0,4},{4,0},{8,12},{12,8},{16,20},{20,16},{24,28},{28,24},{1,5},{5... | collective-permute-start | bytes 786440 | tf_op jit(solution)/shard_map/ppermute | solution.py:288
  20.7 24.7 %collective-permute-start.9 = (bf16[1024,128]{1,0:T(8,128)(2,1)S(1)}, bf16[1024,128]{1,0:T(8,128)(2,1)S(1)}, u32[]{:S(2)}, u32[]{:S(2)}) collective-permute-start(bf16[1024,128]{1,0:T(8,128)(2,1)S(1)} %get-tuple-element.48.refs_0_), channel_id=1, source_target_pairs={{0,24},{4,28},{8,16},{12,20},{16,8},{20,12},{24,0},{28,4},{1,25},{... | collective-permute-start | bytes 786440 | tf_op jit(solution)/shard_map/ppermute | solution.py:288
  23.5 22.0 %collective-permute-start.5 = (bf16[1024,128]{1,0:T(8,128)(2,1)S(1)}, bf16[1024,128]{1,0:T(8,128)(2,1)S(1)}, u32[]{:S(2)}, u32[]{:S(2)}) collective-permute-start(bf16[1024,128]{1,0:T(8,128)(2,1)S(1)} %get-tuple-element.48.refs_0_), channel_id=1, source_target_pairs={{0,8},{4,12},{8,0},{12,4},{16,24},{20,28},{24,16},{28,20},{1,9},{5... | collective-permute-start | bytes 786440 | tf_op jit(solution)/shard_map/ppermute | solution.py:288
  33.1 13.0 %collective-permute-start.7 = (bf16[1024,128]{1,0:T(8,128)(2,1)S(1)}, bf16[1024,128]{1,0:T(8,128)(2,1)S(1)}, u32[]{:S(2)}, u32[]{:S(2)}) collective-permute-start(bf16[1024,128]{1,0:T(8,128)(2,1)S(1)} %get-tuple-element.48.refs_0_), channel_id=1, source_target_pairs={{0,16},{4,20},{8,24},{12,28},{16,0},{20,4},{24,8},{28,12},{1,17},{... | collective-permute-start | bytes 786440 | tf_op jit(solution)/shard_map/ppermute | solution.py:288
  35.4 10.7 %collective-permute-start.4 = (bf16[1024,128]{1,0:T(8,128)(2,1)S(1)}, bf16[1024,128]{1,0:T(8,128)(2,1)S(1)}, u32[]{:S(2)}, u32[]{:S(2)}) collective-permute-start(bf16[1024,128]{1,0:T(8,128)(2,1)S(1)} %get-tuple-element.48.refs_0_), channel_id=1, source_target_pairs={{0,4},{4,0},{8,12},{12,8},{16,20},{20,16},{24,28},{28,24},{1,5},{5... | collective-permute-start | bytes 786440 | tf_op jit(solution)/shard_map/ppermute | solution.py:288
  35.5 11.1 %collective-permute-start.13 = (bf16[1024,128]{1,0:T(8,128)(2,1)S(1)}, bf16[1024,128]{1,0:T(8,128)(2,1)S(1)}, u32[]{:S(2)}, u32[]{:S(2)}) collective-permute-start(bf16[1024,128]{1,0:T(8,128)(2,1)S(1)} %collective-permute-done.12.refs_10_), channel_id=1, source_target_pairs={{0,4},{4,0},{8,12},{12,8},{16,20},{20,16},{24,28},{28,24},{1,5},{5... | collective-permute-start | bytes 786440 | tf_op jit(solution)/shard_map/ppermute | solution.py:288
  67.8 8.0 %collective-permute-start.18 = (bf16[4096,128]{1,0:T(8,128)(2,1)}, bf16[4096,128]{1,0:T(8,128)(2,1)S(1)}, u32[]{:S(2)}, u32[]{:S(2)}) collective-permute-start(bf16[4096,128]{1,0:T(8,128)(2,1)} %get-tuple-element.28), channel_id=1, source_target_pairs={{0,4},{4,0},{8,12},{12,8},{16,20},{20,16},{24,28},{28,24},{1,5},{5... | collective-permute-start | bytes 3145736 | tf_op jit(solution)/shard_map/ppermute | solution.py:288
  73.4 8.3 %collective-permute-start.19 = (bf16[4096,128]{1,0:T(8,128)(2,1)}, bf16[4096,128]{1,0:T(8,128)(2,1)S(1)}, u32[]{:S(2)}, u32[]{:S(2)}) collective-permute-start(bf16[4096,128]{1,0:T(8,128)(2,1)} %get-tuple-element.30), channel_id=1, source_target_pairs={{0,4},{4,0},{8,12},{12,8},{16,20},{20,16},{24,28},{28,24},{1,5},{5... | collective-permute-start | bytes 3145736 | tf_op jit(solution)/shard_map/ppermute | solution.py:288
  78.2 13.1 %collective-permute-start.20 = (bf16[1024,128]{1,0:T(8,128)(2,1)S(1)}, bf16[1024,128]{1,0:T(8,128)(2,1)S(1)}, u32[]{:S(2)}, u32[]{:S(2)}) collective-permute-start(bf16[1024,128]{1,0:T(8,128)(2,1)S(1)} %get-tuple-element.71.refs_0_), channel_id=1, source_target_pairs={{0,8},{4,12},{8,0},{12,4},{16,24},{20,28},{24,16},{28,20},{1,9},{5... | collective-permute-start | bytes 786440 | tf_op jit(solution)/shard_map/ppermute | solution.py:288
  78.2 14.5 %collective-permute-start.21 = (bf16[1024,128]{1,0:T(8,128)(2,1)}, bf16[1024,128]{1,0:T(8,128)(2,1)S(1)}, u32[]{:S(2)}, u32[]{:S(2)}) collective-permute-start(bf16[1024,128]{1,0:T(8,128)(2,1)} %get-tuple-element.69), channel_id=1, source_target_pairs={{0,16},{4,20},{8,24},{12,28},{16,0},{20,4},{24,8},{28,12},{1,17},{... | collective-permute-start | bytes 786440 | tf_op jit(solution)/shard_map/ppermute | solution.py:288
  78.3 14.4 %collective-permute-start.22 = (bf16[1024,128]{1,0:T(8,128)(2,1)S(1)}, bf16[1024,128]{1,0:T(8,128)(2,1)S(1)}, u32[]{:S(2)}, u32[]{:S(2)}) collective-permute-start(bf16[1024,128]{1,0:T(8,128)(2,1)S(1)} %get-tuple-element.68), channel_id=1, source_target_pairs={{0,24},{4,28},{8,16},{12,20},{16,8},{20,12},{24,0},{28,4},{1,25},{... | collective-permute-start | bytes 786440 | tf_op jit(solution)/shard_map/ppermute | solution.py:288
  95.6 16.1 %collective-permute-start.26 = (bf16[4,256,896]{2,1,0:T(8,128)(2,1)}, bf16[4,256,896]{2,1,0:T(8,128)(2,1)S(1)}, u32[]{:S(2)}, u32[]{:S(2)}) collective-permute-start(bf16[4,256,896]{2,1,0:T(8,128)(2,1)} %get-tuple-element.33.refs_0_), channel_id=1, source_target_pairs={{0,4},{4,0},{8,12},{12,8},{16,20},{20,16},{24,28},{28,24},{1,5},{5... | collective-permute-start | bytes 5505032 | tf_op jit(solution)/shard_map/ppermute | solution.py:288
  95.6 15.4 %collective-permute-start.31 = (bf16[1024,128]{1,0:T(8,128)(2,1)}, bf16[1024,128]{1,0:T(8,128)(2,1)S(1)}, u32[]{:S(2)}, u32[]{:S(2)}) collective-permute-start(bf16[1024,128]{1,0:T(8,128)(2,1)} %get-tuple-element.35.refs_0_), channel_id=1, source_target_pairs={{0,2},{1,3},{2,0},{3,1},{4,6},{5,7},{6,4},{7,5},{8,10},{9,11},{10,... | collective-permute-start | bytes 786440 | tf_op jit(solution)/shard_map/ppermute | solution.py:279
  98.0 16.4 %collective-permute-start.23 = (bf16[1024,128]{1,0:T(8,128)(2,1)S(1)}, bf16[1024,128]{1,0:T(8,128)(2,1)S(1)}, u32[]{:S(2)}, u32[]{:S(2)}) collective-permute-start(bf16[1024,128]{1,0:T(8,128)(2,1)S(1)} %copy-done.8), channel_id=1, source_target_pairs={{0,8},{4,12},{8,0},{12,4},{16,24},{20,28},{24,16},{28,20},{1,9},{5... | collective-permute-start | bytes 786440 | tf_op jit(solution)/shard_map/ppermute | solution.py:288
  99.7 16.5 %collective-permute-start.24 = (bf16[1024,128]{1,0:T(8,128)(2,1)}, bf16[1024,128]{1,0:T(8,128)(2,1)S(1)}, u32[]{:S(2)}, u32[]{:S(2)}) collective-permute-start(bf16[1024,128]{1,0:T(8,128)(2,1)} %get-tuple-element.65), channel_id=1, source_target_pairs={{0,16},{4,20},{8,24},{12,28},{16,0},{20,4},{24,8},{28,12},{1,17},{... | collective-permute-start | bytes 786440 | tf_op jit(solution)/shard_map/ppermute | solution.py:288
  99.9 16.5 %collective-permute-start.25 = (bf16[1024,128]{1,0:T(8,128)(2,1)S(1)}, bf16[1024,128]{1,0:T(8,128)(2,1)S(1)}, u32[]{:S(2)}, u32[]{:S(2)}) collective-permute-start(bf16[1024,128]{1,0:T(8,128)(2,1)S(1)} %get-tuple-element.64), channel_id=1, source_target_pairs={{0,24},{4,28},{8,16},{12,20},{16,8},{20,12},{24,0},{28,4},{1,25},{... | collective-permute-start | bytes 786440 | tf_op jit(solution)/shard_map/ppermute | solution.py:288
  111.0 13.9 %collective-permute-start.30 = (bf16[1024,128]{1,0:T(8,128)(2,1)}, bf16[1024,128]{1,0:T(8,128)(2,1)}, u32[]{:S(2)}, u32[]{:S(2)}) collective-permute-start(bf16[1024,128]{1,0:T(8,128)(2,1)} %get-tuple-element.35.refs_0_), channel_id=1, source_target_pairs={{0,1},{1,0},{2,3},{3,2},{4,5},{5,4},{6,7},{7,6},{8,9},{9,8},{10,11... | collective-permute-start | bytes 786440 | tf_op jit(solution)/shard_map/ppermute | solution.py:279
  111.6 15.2 %collective-permute-start.32 = (bf16[1024,128]{1,0:T(8,128)(2,1)S(1)}, bf16[1024,128]{1,0:T(8,128)(2,1)}, u32[]{:S(2)}, u32[]{:S(2)}) collective-permute-start(bf16[1024,128]{1,0:T(8,128)(2,1)S(1)} %collective-permute-done.31.refs_2_), channel_id=1, source_target_pairs={{0,1},{1,0},{2,3},{3,2},{4,5},{5,4},{6,7},{7,6},{8,9},{9,8},{10,11... | collective-permute-start | bytes 786440 | tf_op jit(solution)/shard_map/ppermute | solution.py:279
  114.4 24.6 %collective-permute-start.33 = (bf16[1,256,896]{2,1,0:T(8,128)(2,1)S(1)}, bf16[1,256,896]{2,1,0:T(8,128)(2,1)S(1)}, u32[]{:S(2)}, u32[]{:S(2)}) collective-permute-start(bf16[1,256,896]{2,1,0:T(8,128)(2,1)S(1)} %get-tuple-element.63.refs_6_), channel_id=1, source_target_pairs={{0,8},{4,12},{8,0},{12,4},{16,24},{20,28},{24,16},{28,20},{1,9},{5... | collective-permute-start | bytes 1376264 | tf_op jit(solution)/shard_map/ppermute | solution.py:288
  116.1 22.9 %collective-permute-start.34 = (bf16[1,256,896]{2,1,0:T(8,128)(2,1)S(1)}, bf16[1,256,896]{2,1,0:T(8,128)(2,1)S(1)}, u32[]{:S(2)}, u32[]{:S(2)}) collective-permute-start(bf16[1,256,896]{2,1,0:T(8,128)(2,1)S(1)} %get-tuple-element.61), channel_id=1, source_target_pairs={{0,16},{4,20},{8,24},{12,28},{16,0},{20,4},{24,8},{28,12},{1,17},{... | collective-permute-start | bytes 1376264 | tf_op jit(solution)/shard_map/ppermute | solution.py:288
  116.4 22.6 %collective-permute-start.35 = (bf16[1,256,896]{2,1,0:T(8,128)(2,1)S(1)}, bf16[1,256,896]{2,1,0:T(8,128)(2,1)S(1)}, u32[]{:S(2)}, u32[]{:S(2)}) collective-permute-start(bf16[1,256,896]{2,1,0:T(8,128)(2,1)S(1)} %get-tuple-element.60), channel_id=1, source_target_pairs={{0,24},{4,28},{8,16},{12,20},{16,8},{20,12},{24,0},{28,4},{1,25},{... | collective-permute-start | bytes 1376264 | tf_op jit(solution)/shard_map/ppermute | solution.py:288
  124.9 13.4 %collective-permute-start.28 = (bf16[1024,128]{1,0:T(8,128)(2,1)}, bf16[1024,128]{1,0:T(8,128)(2,1)S(1)}, u32[]{:S(2)}, u32[]{:S(2)}) collective-permute-start(bf16[1024,128]{1,0:T(8,128)(2,1)} %shard_map.108.refs_0_), channel_id=1, source_target_pairs={{0,2},{1,3},{2,0},{3,1},{4,6},{5,7},{6,4},{7,5},{8,10},{9,11},{10,... | collective-permute-start | bytes 786440 | tf_op jit(solution)/shard_map/ppermute | solution.py:279
  126.9 12.1 %collective-permute-start.27 = (bf16[1024,128]{1,0:T(8,128)(2,1)}, bf16[1024,128]{1,0:T(8,128)(2,1)S(1)}, u32[]{:S(2)}, u32[]{:S(2)}) collective-permute-start(bf16[1024,128]{1,0:T(8,128)(2,1)} %shard_map.108.refs_0_), channel_id=1, source_target_pairs={{0,1},{1,0},{2,3},{3,2},{4,5},{5,4},{6,7},{7,6},{8,9},{9,8},{10,11... | collective-permute-start | bytes 786440 | tf_op jit(solution)/shard_map/ppermute | solution.py:279
  138.3 7.2 %collective-permute-start.29 = (bf16[1024,128]{1,0:T(8,128)(2,1)S(1)}, bf16[1024,128]{1,0:T(8,128)(2,1)S(1)}, u32[]{:S(2)}, u32[]{:S(2)}) collective-permute-start(bf16[1024,128]{1,0:T(8,128)(2,1)S(1)} %collective-permute-done.28.refs_2_.refs_5_), channel_id=1, source_target_pairs={{0,1},{1,0},{2,3},{3,2},{4,5},{5,4},{6,7},{7,6},{8,9},{9,8},{10,11... | collective-permute-start | bytes 786440 | tf_op jit(solution)/shard_map/ppermute | solution.py:279
  144.3 4.1 %collective-permute-start.36 = (bf16[256,448]{1,0:T(8,128)(2,1)S(1)}, bf16[256,448]{1,0:T(8,128)(2,1)S(1)}, u32[]{:S(2)}, u32[]{:S(2)}) collective-permute-start(bf16[256,448]{1,0:T(8,128)(2,1)S(1)} %select_convert_fusion), channel_id=1, source_target_pairs={{0,4},{4,0},{8,12},{12,8},{16,20},{20,16},{24,28},{28,24},{1,5},{5... | collective-permute-start | bytes 688136 | tf_op jit(solution)/shard_map/ppermute | solution.py:288
  (44 other events, 273.5 us)

commit v10 on v9

--- a/solution.py
+++ b/solution.py
@@ -87,7 +87,6 @@
     run_ref,
     slot_ref,
     need_ref,
-    odd_ref,
     query_ref,
     up_ref,
     up_t_ref,
@@ -97,7 +96,8 @@
     key_parts, refs = refs[:ranks], refs[ranks:]
     value_parts, refs = refs[:ranks], refs[ranks:]
     gquery_ref, out_ref, *halves = refs[:6]
-    key_ref, value_ref, gkey_ref, gvalue_ref, key_win, value_win, load_sems, sems = refs[6:]
+    key_ref, value_ref, gkey_ref, gvalue_ref, key_win, value_win = refs[6:12]
+    score_ref, prob_ref, gscore_ref, load_sems, sems = refs[12:]
     rows_each = query_ref.shape[0]
     half_blocks = ranks * RUN_BLOCKS // 2
     scale = 1.0 / math.sqrt(HD)
@@ -142,49 +142,75 @@
             start = pl.multiple_of(source * ROWBLK, ROWBLK)
             key_win[pl.ds(step * ROWBLK, ROWBLK), :] = key_ref[pl.ds(start, ROWBLK), :]
             value_win[pl.ds(step * ROWBLK, ROWBLK), :] = value_ref[pl.ds(start, ROWBLK), :]
-        wide = heads if count <= 4 else min(2, heads)
-        cols = wide * ROWBLK
+        wide = min(2, heads)
         base = pl.multiple_of(block * ROWBLK, ROWBLK)
+        at_rows = pl.ds(base, ROWBLK)
         place = place_ref[pl.ds(block, 1), :]
         lane = lax.broadcasted_iota(jnp.int32, (1, ROWBLK), 1)
         last = (slot - first) * ROWBLK + lane
         last_all = jnp.concatenate([last] * wide, axis=1)
         start_all = jnp.concatenate([last - place] * wide, axis=1)
-        key_index = lax.broadcasted_iota(jnp.int32, (rows, cols), 0)
-        allowed = (key_index >= start_all) & (key_index <= last_all)
+        key_index = lax.broadcasted_iota(jnp.int32, (ROWBLK, wide * ROWBLK), 0)
         keys = key_win[pl.ds(0, rows), :]
         values = value_win[pl.ds(0, rows), :]
-        gkey = jnp.zeros((rows, HD), jnp.float32)
-        gvalue = jnp.zeros((rows, HD), jnp.float32)
-        for group in range(heads // wide):
-            columns = [pl.ds((group * wide + item) * HD, HD) for item in range(wide)]
-            at_rows = pl.ds(base, ROWBLK)
-            query = jnp.concatenate([query_ref[at_rows, at] for at in columns], axis=0)
-            up = jnp.concatenate([up_ref[at_rows, at] for at in columns], axis=0)
-            up_t = jnp.concatenate([up_t_ref[at, at_rows] for at in columns], axis=1)
-            score = lax.dot_general(keys, query, NT, preferred_element_type=jnp.float32)
-            score = jnp.where(allowed, score, masked_score)
-            peak = jnp.max(score, axis=0, keepdims=True)
-            raised = jnp.exp2((score - peak) * to_exp2)
-            total = jnp.sum(raised, axis=0, keepdims=True)
-            prob = raised * (1.0 / total)
-            prob_b = prob.astype(jnp.bfloat16)
-            out_t = lax.dot_general(values, prob_b, TN, preferred_element_type=jnp.float32)
-            out_b = out_t.astype(jnp.bfloat16)
-            delta = jnp.sum(
-                up_t.astype(jnp.float32) * out_b.astype(jnp.float32), axis=0, keepdims=True
+        columns = [pl.ds(head * HD, HD) for head in range(heads)]
+        query = jnp.concatenate([query_ref[at_rows, at] for at in columns], axis=0)
+        up = jnp.concatenate([up_ref[at_rows, at] for at in columns], axis=0)
+        folded = lambda tile: tile.reshape(ROWBLK // 8, 8, tile.shape[1])
+        tiles = [pl.ds(step * ROWBLK, ROWBLK) for step in range(count)]
+        groups = heads // wide
+        spans = [slice(at * wide * ROWBLK, (at + 1) * wide * ROWBLK) for at in range(groups)]
+
+        score = lax.dot_general(keys, query, NT, preferred_element_type=jnp.float32)
+        gprob = lax.dot_general(values, up, NT, preferred_element_type=jnp.float32)
+        peaks = [None] * groups
+        for step, tile in enumerate(tiles):
+            seen = key_index >= start_all - step * ROWBLK
+            if step == count - 1:
+                seen = seen & (key_index <= last_all - step * ROWBLK)
+            for at, span in enumerate(spans):
+                part = jnp.where(
+                    seen, score[step * ROWBLK : (step + 1) * ROWBLK, span], masked_score
+                )
+                score_ref[tile, span] = part
+                most = jnp.max(folded(part), axis=0)
+                peaks[at] = most if peaks[at] is None else jnp.maximum(peaks[at], most)
+        peaks = [jnp.max(item, axis=0, keepdims=True) for item in peaks]
+        totals = [None] * groups
+        for tile in tiles:
+            for at, span in enumerate(spans):
+                part = jnp.exp2((score_ref[tile, span] - peaks[at]) * to_exp2)
+                score_ref[tile, span] = part
+                some = jnp.sum(folded(part), axis=0)
+                totals[at] = some if totals[at] is None else totals[at] + some
+        shares = [1.0 / jnp.sum(item, axis=0, keepdims=True) for item in totals]
+        for tile in tiles:
+            for at, span in enumerate(spans):
+                prob_ref[tile, span] = (score_ref[tile, span] * shares[at]).astype(jnp.bfloat16)
+        prob_b = prob_ref[pl.ds(0, rows), :]
+        out_t = lax.dot_general(values, prob_b, TN, preferred_element_type=jnp.float32)
+        out_b = out_t.astype(jnp.bfloat16)
+        deltas = []
+        for at in range(groups):
+            up_t = jnp.concatenate(
+                [up_t_ref[item, at_rows] for item in columns[at * wide : (at + 1) * wide]], axis=1
+            ).astype(jnp.float32)
+            deltas.append(
+                jnp.sum(up_t * out_b[:, spans[at]].astype(jnp.float32), axis=0, keepdims=True)
             )
-            gprob = lax.dot_general(values, up, NT, preferred_element_type=jnp.float32)
-            gscore = (prob * (gprob - delta)).astype(jnp.bfloat16)
-            gquery_t = lax.dot_general(keys, gscore, TN, preferred_element_type=jnp.float32)
-            gkey = gkey + jnp.dot(gscore, query, preferred_element_type=jnp.float32)
-            gvalue = gvalue + jnp.dot(prob_b, up, preferred_element_type=jnp.float32)
-            for item in range(wide):
-                part = slice(item * ROWBLK, (item + 1) * ROWBLK)
-                head = group * wide + item
-                half, row = head * 2 // heads, head % (heads // 2) * HD
-                out_ref[half ^ odd_ref[0], pl.ds(row, HD), at_rows] = out_b[:, part]
-                gquery_ref[columns[item], at_rows] = gquery_t[:, part]
+        for step, tile in enumerate(tiles):
+            for at, span in enumerate(spans):
+                prob = score_ref[tile, span] * shares[at]
+                part = gprob[step * ROWBLK : (step + 1) * ROWBLK, span] - deltas[at]
+                gscore_ref[tile, span] = (prob * part).astype(jnp.bfloat16)
+        gscore = gscore_ref[pl.ds(0, rows), :]
+        gquery_t = lax.dot_general(keys, gscore, TN, preferred_element_type=jnp.float32)
+        gkey = jnp.dot(gscore, query, preferred_element_type=jnp.float32)
+        gvalue = jnp.dot(prob_b, up, preferred_element_type=jnp.float32)
+        for head in range(heads):
+            part = slice(head * ROWBLK, (head + 1) * ROWBLK)
+            out_ref[columns[head], at_rows] = out_b[:, part]
+            gquery_ref[columns[head], at_rows] = gquery_t[:, part]
         gkey = (gkey * scale).astype(jnp.bfloat16)
         gvalue = gvalue.astype(jnp.bfloat16)
         place_at = pl.ds(pl.multiple_of(first * ROWBLK, ROWBLK), rows)
@@ -198,7 +224,7 @@
         gvalue_ref[block % 2] = blank
         need = need_ref[block]
         floor = 0
-        for size in (1, 2, 3, 4, 6, 8):
+        for size in range(1, RUN_BLOCKS + 1):
             pl.when((need > floor) & (need <= size))(partial(window, size, block))
             floor = size
         stores(block, lambda copy: copy.start())
@@ -223,17 +249,19 @@
         partial(attend_kernel, heads, ranks),
         out_shape=(
             jax.ShapeDtypeStruct((width, rows), jnp.float32),
-            jax.ShapeDtypeStruct((2, width // 2, rows), jnp.bfloat16),
+            jax.ShapeDtypeStruct((width, rows), jnp.bfloat16),
             half,
             half,
             half,
             half,
         ),
-        in_specs=[smem] * 6 + [vmem] * 4 + [hbm] * (2 * ranks),
+        in_specs=[smem] * 5 + [vmem] * 4 + [hbm] * (2 * ranks),
         out_specs=(vmem, vmem, hbm, hbm, hbm, hbm),
         scratch_shapes=[pltpu.VMEM((every, HD), jnp.bfloat16)] * 2
         + [pltpu.VMEM((2, RUN_BLOCKS * ROWBLK, HD), jnp.bfloat16)] * 2
         + [pltpu.VMEM((RUN_BLOCKS * ROWBLK, HD), jnp.bfloat16)] * 2
+        + [pltpu.VMEM((RUN_BLOCKS * ROWBLK, heads * ROWBLK), jnp.float32)]
+        + [pltpu.VMEM((RUN_BLOCKS * ROWBLK, heads * ROWBLK), jnp.bfloat16)] * 2
         + [pltpu.SemaphoreType.DMA((2, ranks)), pltpu.SemaphoreType.DMA((2, 2, RUN_BLOCKS))],
         compiler_params=pltpu.CompilerParams(vmem_limit_bytes=VMEM_BYTES),
         cost_estimate=NO_COST,
@@ -269,18 +297,17 @@
     )(my_lane.reshape(1), *pieces)
 
 
-def lane_gather(array, my_lane):
+def lane_swap(array, bit):
     lanes = lax.axis_size("tensor")
-    pieces = {0: array}
-    bit = lanes // 2
+    return lax.ppermute(array, "tensor", [(lane, lane ^ bit) for lane in range(lanes)])
+
+
+def lane_pieces(pieces, bit):
+    lanes = lax.axis_size("tensor")
     while bit:
-        pairs = [(lane, lane ^ bit) for lane in range(lanes)]
-        pieces.update(
-            {at | bit: lax.ppermute(item, "tensor", pairs) for at, item in list(pieces.items())}
-        )
+        pieces = {**pieces, **{at | bit: lane_swap(item, bit) for at, item in pieces.items()}}
         bit //= 2
-    pieces = [pieces[at] for at in range(lanes)]
-    return assemble(my_lane, pieces), pieces[1:]
+    return [pieces[at] for at in range(lanes)]
 
 
 def swap(array, bit):
@@ -314,31 +341,34 @@
     return [swap(item, 2 * at + 2) for at, item in enumerate(sends)]
 
 
-def final_kernel(count, rotary, out_at, *refs):
+def final_kernel(count, rotary, outs, *refs):
     total = refs[0][...].astype(jnp.float32)
     for ref in refs[1 : 1 + count]:
         total = total + ref[...].astype(jnp.float32)
     if rotary:
         total = total * refs[1 + count][...] - pltpu.roll(total, HD // 2, 1) * refs[2 + count][...]
-    refs[out_at][...] = total.astype(refs[out_at].dtype)
-
-
-def final_sum(keep, received, tables, after, kind=jnp.bfloat16, thru=()):
+    for at in outs:
+        refs[at][...] = total.astype(refs[at].dtype)
+
+
+def final_sum(keep, received, tables, after, thru=(), copies=1):
     vmem = pl.BlockSpec(memory_space=pltpu.VMEM)
     hbm = pl.BlockSpec(memory_space=pl.ANY)
     parts = [keep, *received, *tables]
     inputs = len(parts) + len(after) + len(thru)
     results = pl.pallas_call(
-        partial(final_kernel, len(received), len(tables) > 0, inputs),
-        out_shape=[jax.ShapeDtypeStruct(keep.shape, kind)]
+        partial(
+            final_kernel, len(received), len(tables) > 0, range(inputs, inputs + copies)
+        ),
+        out_shape=[jax.ShapeDtypeStruct(keep.shape, jnp.bfloat16)] * copies
         + [jax.ShapeDtypeStruct(item.shape, item.dtype) for item in thru],
         in_specs=[vmem] * len(parts) + [hbm] * (len(after) + len(thru)),
-        out_specs=[vmem] + [hbm] * len(thru),
-        input_output_aliases={inputs - len(thru) + at: 1 + at for at in range(len(thru))},
+        out_specs=[vmem] * copies + [hbm] * len(thru),
+        input_output_aliases={inputs - len(thru) + at: copies + at for at in range(len(thru))},
         compiler_params=pltpu.CompilerParams(vmem_limit_bytes=VMEM_BYTES),
         cost_estimate=NO_COST,
     )(*parts, *after, *thru)
-    return results if thru else results[0]
+    return results
 
 
 def prepare_kernel(
@@ -417,58 +447,62 @@
     )(grad_t, cosine, sine, *after)
 
 
-def take_heads_kernel(at_ref, key_ref, value_ref, after_ref, own_key_ref, own_value_ref):
-    own_key_ref[...] = key_ref[...]
-    own_value_ref[...] = value_ref[...]
-
-
-def take_heads(key, value, kv_head, after):
-    rows = key.shape[0]
-    picked = pl.BlockSpec((rows, HD), lambda step, at_ref: (0, at_ref[0]))
-    own = pl.BlockSpec((rows, HD), lambda step, at_ref: (0, 0))
-    shape = jax.ShapeDtypeStruct((rows, HD), key.dtype)
+def hold_kernel(*refs):
+    pass
+
+
+def hold(array, after):
+    hbm = pl.BlockSpec(memory_space=pl.ANY)
     return pl.pallas_call(
-        take_heads_kernel,
-        grid_spec=pltpu.PrefetchScalarGridSpec(
-            num_scalar_prefetch=1,
-            grid=(1,),
-            in_specs=[picked, picked, pl.BlockSpec(memory_space=pl.ANY)],
-            out_specs=[own, own],
-        ),
-        out_shape=[shape, shape],
+        hold_kernel,
+        out_shape=jax.ShapeDtypeStruct(array.shape, array.dtype),
+        in_specs=[hbm] * (1 + len(after)),
+        out_specs=hbm,
+        input_output_aliases={0: 0},
         cost_estimate=NO_COST,
-    )(kv_head.reshape(1), key, value, after)
+    )(array, *after)
 
 
 def product_kernel(my_ref, left_ref, right_ref, *refs):
     keep_ref, send_ref = refs[-3:-1]
-    half = left_ref.shape[1]
-    left = left_ref[...].reshape(2 * half, left_ref.shape[2])
-    total = jnp.dot(left, right_ref[...], preferred_element_type=jnp.float32)
-    keep_ref[0] = total[:half].astype(keep_ref.dtype)
-    send_ref[0] = total[half:].astype(send_ref.dtype)
-
-
-def product(mine, left, right, thru, after):
+    half = keep_ref.shape[1]
+    total = jnp.dot(left_ref[...], right_ref[...], preferred_element_type=jnp.float32)
+    total = total.astype(keep_ref.dtype).T
+    odd = my_ref[1]
+
+    @pl.when(odd == 0)
+    def even_core():
+        keep_ref[0] = total[:half]
+        send_ref[0] = total[half:]
+
+    @pl.when(odd == 1)
+    def odd_core():
+        keep_ref[0] = total[half:]
+        send_ref[0] = total[:half]
+
+
+def product(my_rank, left, right, thru, after):
     count = lax.axis_size("dp") // 2
-    half, depth = left.shape[1:]
+    width, depth = left.shape
     cols = right.shape[1] // count
+    mine, odd = my_rank // 2, my_rank & 1
     if cols % 128:
-        total = jnp.dot(left.reshape(2 * half, depth), right, preferred_element_type=jnp.float32)
-        pieces = jnp.moveaxis(total.astype(jnp.bfloat16).reshape(2 * half, count, cols), 1, 0)
+        total = jnp.dot(left, right, preferred_element_type=jnp.float32).astype(jnp.bfloat16)
+        pieces = total.T.reshape(count, 2, cols // 2, width)
         pieces = jnp.take(pieces, jnp.arange(count, dtype=jnp.int32) ^ mine, axis=0)
-        return pieces[:, :half], pieces[:, half:], thru
+        low, high = pieces[:, 0], pieces[:, 1]
+        return jnp.where(odd > 0, high, low), jnp.where(odd > 0, low, high), thru
     hbm = pl.BlockSpec(memory_space=pl.ANY)
-    stacked = pl.BlockSpec((1, half, cols), lambda step, my_ref: (step, 0, 0))
-    stack = jax.ShapeDtypeStruct((count, half, cols), jnp.bfloat16)
-    inputs = [mine.reshape(1), left, right, *after, thru]
+    stacked = pl.BlockSpec((1, cols // 2, width), lambda step, my_ref: (step, 0, 0))
+    stack = jax.ShapeDtypeStruct((count, cols // 2, width), jnp.bfloat16)
+    inputs = [jnp.stack([mine, odd]), left, right, *after, thru]
     return pl.pallas_call(
         product_kernel,
         grid_spec=pltpu.PrefetchScalarGridSpec(
             num_scalar_prefetch=1,
             grid=(count,),
             in_specs=[
-                pl.BlockSpec(left.shape, lambda step, my_ref: (0, 0, 0)),
+                pl.BlockSpec(left.shape, lambda step, my_ref: (0, 0)),
                 pl.BlockSpec((depth, cols), lambda step, my_ref: (0, step ^ my_ref[0])),
             ]
             + [hbm] * (len(after) + 1),
@@ -481,6 +515,26 @@
     )(*inputs)
 
 
+def weight_final_kernel(count, factor, *refs):
+    total = refs[0][0].astype(jnp.float32)
+    for ref in refs[1 : 1 + count]:
+        total = total + ref[0].astype(jnp.float32)
+    refs[-1][...] = total * factor
+
+
+def weight_final(keep, received, factor, after):
+    vmem = pl.BlockSpec(memory_space=pltpu.VMEM)
+    hbm = pl.BlockSpec(memory_space=pl.ANY)
+    return pl.pallas_call(
+        partial(weight_final_kernel, len(received), factor),
+        out_shape=jax.ShapeDtypeStruct(keep.shape[1:], jnp.float32),
+        in_specs=[vmem] * (1 + len(received)) + [hbm] * len(after),
+        out_specs=vmem,
+        compiler_params=pltpu.CompilerParams(vmem_limit_bytes=VMEM_BYTES),
+        cost_estimate=NO_COST,
+    )(keep, *received, *after)
+
+
 def local(query, key, value, grad_out, out_weight, plan, segments):
     rank_count = lax.axis_size("dp")
     my_rank = lax.axis_index("dp")
@@ -491,12 +545,16 @@
     group = HEADS // KV
     bits = [1 << at for at in range(rank_count.bit_length() - 1)]
     kv_head = my_lane * local_heads // group
+    own_key = lax.dynamic_slice_in_dim(key, kv_head * HD, HD, 1)
+    own_value = lax.dynamic_slice_in_dim(value, kv_head * HD, HD, 1)
     own_places = positions_of(segments).reshape(1, block_count, ROWBLK)
-    pair_places = jnp.concatenate([own_places, swap(own_places, 1)], axis=0)
-    places_all = jnp.concatenate(
-        [pair_places] + [swap(pair_places, step) for step in range(2, rank_count, 2)], axis=0
+    places_all = lax.all_to_all(
+        jnp.broadcast_to(own_places, (rank_count, block_count, ROWBLK)),
+        "dp",
+        split_axis=0,
+        concat_axis=0,
+        tiled=True,
     ).reshape(-1, ROWBLK)
-    own_key, own_value = take_heads(key, value, kv_head, pair_places)
     values = spread(own_value)
 
     mine = my_rank * block_count + jnp.arange(block_count, dtype=jnp.int32)
@@ -506,7 +564,7 @@
     )
     run = dest // RUN_BLOCKS
     slot = dest % RUN_BLOCKS
-    places = jnp.take(places_all, (run ^ my_rank) * RUN_BLOCKS + slot, axis=0)
+    places = jnp.take(places_all, dest, axis=0)
     need = slot - (slot * ROWBLK - places[:, 0]) // ROWBLK + 1
     cosine, sine = rope_tables(places.reshape(row_count), HD)
     key_f = own_key.astype(jnp.float32)
@@ -523,7 +581,6 @@
         run,
         slot,
         need,
-        (my_rank & 1).reshape(1),
     )
     grad_query_t, attn_t, gkey_keep, gkey_send, gvalue_keep, gvalue_send = attend(
         tables, turned, up, up_t, places, keys, values
@@ -533,32 +590,26 @@
     key_keep, key_sends = chip_sum(gkey_keep, swap(gkey_send, 1))
     key_received = exchange(key_sends)
     weight_keep, weight_send, value_keep = product(
-        my_rank // 2, attn_t, grad_out, value_keep, [value_sends[0], key_sends[0]]
-    )
-    value_partial, weight_send = final_sum(
-        value_keep, value_received, (), (), thru=[weight_send]
-    )
-    value_all, value_pieces = lane_gather(value_partial, my_lane)
-    weight_other = swap(weight_send, 1)
-    grad_query = turn_back(grad_query_t, cosine, sine, [weight_send])
-    weight_keep, weight_sends = chip_sum(weight_keep, weight_other)
+        my_rank, attn_t, grad_out, value_keep, [value_sends[0], key_sends[0]]
+    )
+    far = lax.axis_size("tensor") // 2
+    value_partial, value_near, weight_send = final_sum(
+        value_keep, value_received, (), (), thru=[weight_send], copies=2
+    )
+    value_far = lane_swap(value_partial, far)
+    weight_keep, weight_sends = chip_sum(weight_keep, swap(weight_send, 1))
     weight_received = exchange(weight_sends)
-    key_partial = final_sum(
-        key_keep, key_received, (cosine, sine), [weight_sends[0], grad_query]
-    )
-    key_all, key_pieces = lane_gather(key_partial, my_lane)
-    total = final_sum(
-        weight_keep, weight_received, (), [*key_pieces[:2], value_all], jnp.float32
-    )[0]
-    odd = my_rank & 1
-    pair_rows = grad_out.shape[1] // (rank_count // 2)
-    low, high = total[:, : pair_rows // 2], total[:, pair_rows // 2 :]
-    is_odd = odd > 0
-    other = swap(jnp.where(is_odd, low, high).astype(jnp.bfloat16), 1).astype(jnp.float32)
-    mine_half = jnp.where(is_odd, high, low)
-    weight_grad = jnp.concatenate(
-        [jnp.where(is_odd, other, mine_half), jnp.where(is_odd, mine_half, other)], axis=0
-    ).T
+    value_near = hold(value_near, weight_sends[:1])
+    grad_query = turn_back(grad_query_t, cosine, sine, weight_sends[:1])
+    key_partial, value_far = final_sum(
+        key_keep, key_received, (cosine, sine), [grad_query], thru=[value_far]
+    )
+    value_all = assemble(my_lane, lane_pieces({0: value_near, far: value_far}, far // 2))
+    key_pieces = lane_pieces({0: key_partial}, far)
+    key_all = assemble(my_lane, key_pieces)
+    weight_grad = weight_final(
+        weight_keep, weight_received, 1.0 / rank_count, [*key_pieces[1:3], value_all]
+    )
     lanes_per_key = group // local_heads
 
     def combine(gathered):
@@ -569,7 +620,7 @@
         )
         return merged.astype(jnp.bfloat16).reshape(row_count, KV * HD)
 
-    return (grad_query, combine(key_all), combine(value_all), weight_grad * (1.0 / rank_count))
+    return (grad_query, combine(key_all), combine(value_all), weight_grad)
 
 
 def solution(mesh):

time: 150 us -> 143 us (0.953); the launches traced: 150 us -> 141 us
  starting transfers between devices: 40.9 us -> 34.7 us
  waiting for transfers between devices: 31.9 us -> 28.4 us
    ppermute x31 -> x26, starting transfers between devices: 31.9 us -> 21.9 us  [swap(): lax.ppermute(array, 'dp', [(rank, rank ^ bit) for rank in range(ranks)])]
    all_to_all x0 -> x1, starting transfers between devices: none -> 4.23 us  [local(): lax.all_to_all(jnp.broadcast_to(own_places, (rank_count, block_count, ROW...]
    ppermute x6, waiting for transfers between devices: 17.9 us -> 14 us  [lane_swap(): lax.ppermute(array, 'tensor', [(lane, lane ^ bit) for lane in range(lanes)])]
    all_to_all x0 -> x1, waiting for transfers between devices: none -> 1.71 us  [local(): lax.all_to_all(jnp.broadcast_to(own_places, (rank_count, block_count, ROW...]
    pallas_call x4, Pallas kernels: 9.17 us -> 7.46 us  [the longest x2 4.76 us: final_sum(): pl.pallas_call(partial(final_kernel, len(received), len(tables) > 0, rang...]
    ppermute x31 -> x26, waiting for transfers between devices: 14 us -> 12.7 us  [swap(): lax.ppermute(array, 'dp', [(rank, rank ^ bit) for rank in range(ranks)])]
    unnamed x82 -> x76, local copies, waits for them, and re-layouts: 4.63 us -> 5.08 us
  transfers between devices with their start and end apart: 37 -> 33, of which waited for: 9 -> 14; matrix products, arithmetic and copies ran while one was open for 10% -> 13% of each run, Pallas kernels for 23% -> 22%
where the time goes in v10:
time: 143 us; the launch traced here: 141 us
  Pallas kernels  53.7 us (38%)
  starting transfers between devices  34.7 us (24%)
  waiting for transfers between devices  28.4 us (20%)
  other arithmetic  16.1 us (11%)
  local copies, waits for them, and re-layouts  6.79 us (5%)
    ppermute x26, starting transfers between devices, swap(): lax.ppermute(array, 'dp', [(rank, rank ^ bit) for rank in range(ranks)])  21.9 us
    pallas_call x1, Pallas kernels, attend(): pl.pallas_call(partial(attend_kernel, heads, ranks), out_shape=(jax.Shape...  18.7 us
    ppermute x6, waiting for transfers between devices, lane_swap(): lax.ppermute(array, 'tensor', [(lane, lane ^ bit) for lane in range(lanes)])  14 us
    ppermute x26, waiting for transfers between devices, swap(): lax.ppermute(array, 'dp', [(rank, rank ^ bit) for rank in range(ranks)])  12.7 us
    pallas_call x1, Pallas kernels, product(): pl.pallas_call(product_kernel, grid_spec=pltpu.PrefetchScalarGridSpec(num...  9.54 us
    pallas_call x1, Pallas kernels, prepare(): pl.pallas_call(prepare_kernel, grid=(steps,), out_shape=[jax.ShapeDtypeSt...  9.22 us
    ppermute x6, starting transfers between devices, lane_swap(): lax.ppermute(array, 'tensor', [(lane, lane ^ bit) for lane in range(lanes)])  8.54 us
    convert_element_type x3, other arithmetic, chip_sum(): return (total[0], [item.astype(keep.dtype) for item in total[1:]])  5.52 us
  transfers between devices with their start and end apart: 33, of which 14 were waited for; matrix products, arithmetic and copies ran while one was open for 13% of the time, Pallas kernels for 22%

profile of v10, /device:TPU:0, one launch (start us, length us, event | category | flops | bytes accessed | tf_op | source)
XLA Modules:
  0.0 140.9 jit_solution(5263205327307002730)
XLA Ops:
  1.9 4.0 %collective-permute-start.12 = (bf16[1024,128]{1,0:T(8,128)(2,1)S(1)}, bf16[1024,128]{1,0:T(8,128)(2,1)S(1)}, u32[]{:S(2)}, u32[]{:S(2)}) collective-permute-start(bf16[1024,128]{1,0:T(8,128)(2,1)S(1)} %constant_dynamic-slice_fusion.refs_8_), channel_id=1, source_target_pairs={{0,24},{4,28},{8,16},{12,20},{16,8},{20,12},{24,0},{28,4},{1,25},{... | collective-permute-start | bytes 786440 | tf_op jit(solution)/shard_map/ppermute | solution.py:315
  8.6 4.2 %all-to-all-start = ((s32[8,8,128]{2,1,0:T(8,128)}), s32[8,8,128]{2,1,0:T(8,128)S(1)}, u32[]{:S(2)}, u32[]{:S(2)}) async-start(s32[8,8,128]{2,1,0:T(8,128)} %broadcast_in_dim.40), calls=%async_computation | async-start | bytes 65536 | tf_op jit(solution)/shard_map/all_to_all | solution.py:551
  16.7 1.7 %all-to-all-done = s32[8,8,128]{2,1,0:T(8,128)S(1)} async-done(((s32[8,8,128]{2,1,0:T(8,128)}), s32[8,8,128]{2,1,0:T(8,128)S(1)}, u32[]{:S(2)}, u32[]{:S(2)}) %all-to-all-start) | async-done | bytes 32800 | tf_op jit(solution)/shard_map/all_to_all | solution.py:551
  19.0 1.9 %fusion.4 = (f32[1024,64]{1,0:T(8,128)S(1)}, f32[1024,64]{1,0:T(8,128)S(1)}, f32[1024,64]{1,0:T(8,128)S(1)}) fusion(f32[64]{0:T(128)S(1)} %multiply_add_fusion.1, f32[1024]{0:T(1024)S(1)} %get-tuple-element.40), kind=kLoop, calls=%fused_computation.23 | loop fusion | flops 262144 | bytes 790784 | tf_op jit(solution)/shard_map/neg | solution.py:69
  21.0 2.4 %fusion.3 = (bf16[1024,128]{1,0:T(8,128)(2,1)S(1)}, f32[1024,128]{1,0:T(8,128)}, f32[1024,128]{1,0:T(8,128)}) fusion(f32[1024,64]{1,0:T(8,128)S(1)} %get-tuple-element.61, f32[1024,64]{1,0:T(8,128)S(1)} %get-tuple-element.60, bf16[1024,512]{1,0:T(8,128)(2,1)} %param.8, s32[]{:T(128)S(6)} %select_n.80, f32[1024,64]{1,0:T(8,128)S(1)} %get-tuple-element.64, ...), kind=kLoop, calls=%fused_computation.13 | loop fusion | flops 1048576 | bytes 2883588 | tf_op jit(solution)/shard_map/convert_element_type | solution.py:571
  23.4 2.4 %collective-permute-start.5 = (bf16[1024,128]{1,0:T(8,128)(2,1)S(1)}, bf16[1024,128]{1,0:T(8,128)(2,1)S(1)}, u32[]{:S(2)}, u32[]{:S(2)}) collective-permute-start(bf16[1024,128]{1,0:T(8,128)(2,1)S(1)} %get-tuple-element.38.refs_0_), channel_id=1, source_target_pairs={{0,24},{4,28},{8,16},{12,20},{16,8},{20,12},{24,0},{28,4},{1,25},{... | collective-permute-start | bytes 786440 | tf_op jit(solution)/shard_map/ppermute | solution.py:315
  27.4 9.2 %shard_map.102 = (bf16[1024,512]{1,0:T(8,128)(2,1)}, bf16[512,1024]{1,0:T(8,128)(2,1)}, bf16[1024,512]{1,0:T(8,128)(2,1)}) custom-call(bf16[1024,3584]{1,0:T(8,128)(2,1)} %right_ref.1, bf16[3584,512]{1,0:T(8,128)(2,1)} %weight_ref.1, bf16[1024,512]{1,0:T(8,128)(2,1)} %query_ref.1, f32[1024,128]{1,0:T(8,128)} %get-tuple-element.59.cos_ref.refs_4_, ...), custom_call_target="tpu_custom_call" | custom-call | flops 3758096384 | bytes 7340032 | tf_op jit(solution)/shard_map/pallas_call | solution.py:393
  41.5 18.7 %shard_map.103 = (f32[512,1024]{1,0:T(8,128)}, bf16[512,1024]{1,0:T(8,128)(2,1)}, bf16[4096,128]{1,0:T(8,128)(2,1)}, bf16[4096,128]{1,0:T(8,128)(2,1)}, bf16[409...) custom-call(s32[64]{0:T(128)} %multiply_add_fusion.3.target_ref, s32[64]{0:T(128)} %get-tuple-element.44.source_ref, ...), custom_call_target="tpu_custom_call" | custom-call | tf_op jit(solution)/shard_map/pallas_call | solution.py:248
  61.9 2.6 %collective-permute-done.14 = bf16[4096,128]{1,0:T(8,128)(2,1)} collective-permute-done((bf16[4096,128]{1,0:T(8,128)(2,1)}, bf16[4096,128]{1,0:T(8,128)(2,1)}, u32[]{:S(2)}, u32[]{:S(2)}) %collective-permute-start.14) | collective-permute-done | bytes 1048608 | tf_op jit(solution)/shard_map/ppermute | solution.py:315
  64.5 2.6 %add_convert_fusion.5 = (bf16[1024,128]{1,0:T(8,128)(2,1)}, bf16[1024,128]{1,0:T(8,128)(2,1)}, f32[1024,128]{1,0:T(8,128)}, bf16[1024,128]{1,0:T(8,128)(2,1)S(1)}) fusion(bf16[4096,128]{1,0:T(8,128)(2,1)} %collective-permute-done.14, bf16[4096,128]{1,0:T(8,128)(2,1)} %get-tuple-element.26), kind=kLoop, calls=%fused_computation.17 | loop fusion | flops 1966080 | bytes 3407872 | tf_op jit(solution)/shard_map/convert_element_type | solution.py:337
  67.1 3.4 %collective-permute-start.18 = (bf16[1024,128]{1,0:T(8,128)(2,1)}, bf16[1024,128]{1,0:T(8,128)(2,1)S(1)}, u32[]{:S(2)}, u32[]{:S(2)}) collective-permute-start(bf16[1024,128]{1,0:T(8,128)(2,1)} %get-tuple-element.55), channel_id=1, source_target_pairs={{0,24},{4,28},{8,16},{12,20},{16,8},{20,12},{24,0},{28,4},{1,25},{... | collective-permute-start | bytes 786440 | tf_op jit(solution)/shard_map/ppermute | solution.py:315
  71.2 1.3 add_convert_fusion.3
  72.5 9.5 %shard_map.104 = (bf16[4,448,512]{2,1,0:T(8,128)(2,1)}, bf16[4,448,512]{2,1,0:T(8,128)(2,1)}, f32[1024,128]{1,0:T(8,128)}) custom-call(s32[2]{0:T(128)} %pad_add_fusion.my_ref, bf16[512,1024]{1,0:T(8,128)(2,1)} %get-tuple-element.25.left_ref, bf16[1024,3584]{1,0:T(8,128)(2,1)} %right_ref.1, ...), custom_call_target="tpu_custom_call", output_to_operand_aliasing={{2}: (5, {})} | custom-call | tf_op jit(solution)/shard_map/pallas_call | solution.py:499
  83.8 2.2 %shard_map.105 = (bf16[1024,128]{1,0:T(8,128)(2,1)}, bf16[1024,128]{1,0:T(8,128)(2,1)}, bf16[4,448,512]{2,1,0:T(8,128)(2,1)}) custom-call(f32[1024,128]{1,0:T(8,128)} %get-tuple-element.31.refs_0_, bf16[1024,128]{1,0:T(8,128)(2,1)} %copy-done.35, bf16[1024,128]{1,0:T(8,128)(2,1)} %copy-done.33, ...), custom_call_target="tpu_custom_call", output_to_operand_aliasing={{2}: (4, {})} | custom-call | tf_op jit(solution)/shard_map/pallas_call | solution.py:359
  86.0 1.8 %collective-permute-start.20 = (bf16[1024,128]{1,0:T(8,128)(2,1)S(1)}, bf16[1024,128]{1,0:T(8,128)(2,1)S(1)}, u32[]{:S(2)}, u32[]{:S(2)}) collective-permute-start(bf16[1024,128]{1,0:T(8,128)(2,1)S(1)} %copy-done.9), channel_id=1, source_target_pairs={{0,8},{4,12},{8,0},{12,4},{16,24},{20,28},{24,16},{28,20},{1,9},{5... | collective-permute-start | bytes 786440 | tf_op jit(solution)/shard_map/ppermute | solution.py:315
  88.1 1.4 collective-permute-start.21
  89.5 2.6 %collective-permute-start.23 = (bf16[1024,128]{1,0:T(8,128)(2,1)}, bf16[1024,128]{1,0:T(8,128)(2,1)S(1)}, u32[]{:S(2)}, u32[]{:S(2)}) collective-permute-start(bf16[1024,128]{1,0:T(8,128)(2,1)} %get-tuple-element.34), channel_id=1, source_target_pairs={{0,2},{1,3},{2,0},{3,1},{4,6},{5,7},{6,4},{7,5},{8,10},{9,11},{10,... | collective-permute-start | bytes 786440 | tf_op jit(solution)/shard_map/ppermute | solution.py:302
  92.1 1.6 %add_convert_fusion = (bf16[1,448,512]{2,1,0:T(8,128)(2,1)S(1)}, bf16[1,448,512]{2,1,0:T(8,128)(2,1)S(1)}, f32[1,448,512]{2,1,0:T(8,128)}, bf16[1,448,512]{2,1,0:T(8,128)(2,1)}) fusion(bf16[4,448,512]{2,1,0:T(8,128)(2,1)S(1)} %collective-permute-done.19, bf16[4,448,512]{2,1,0:T(8,128)(2,1)S(1)} %copy-done.2), kind=kLoop, calls=%fused_computation.1 | loop fusion | flops 3440640 | bytes 5963776 | tf_op jit(solution)/shard_map/convert_element_type | solution.py:337
  93.7 1.6 %collective-permute-start.27 = (bf16[1024,128]{1,0:T(8,128)(2,1)}, bf16[1024,128]{1,0:T(8,128)(2,1)S(1)}, u32[]{:S(2)}, u32[]{:S(2)}) collective-permute-start(bf16[1024,128]{1,0:T(8,128)(2,1)} %shard_map.109.refs_0_), channel_id=1, source_target_pairs={{0,1},{1,0},{2,3},{3,2},{4,5},{5,4},{6,7},{7,6},{8,9},{9,8},{10,11... | collective-permute-start | bytes 786440 | tf_op jit(solution)/shard_map/ppermute | solution.py:302
  95.3 4.4 %shard_map.106.refs_6_ = bf16[1024,512]{1,0:T(8,128)(2,1)} custom-call(f32[512,1024]{1,0:T(8,128)} %get-tuple-element.24.grad_ref, f32[1024,128]{1,0:T(8,128)} %get-tuple-element.59.cos_ref.refs_4_, f32[1024,128]{1,0:T(8,128)} %get-tuple-element.39.sin_ref.refs_5_, bf16[1,448,512]{2,1,0:T(8,128)(2,1)} %get-tuple-element.50.refs_0_.refs_1_), custom_call_target="tpu_custom_call" | custom-call | tf_op jit(solution)/shard_map/pallas_call | solution.py:434
  100.7 1.6 %collective-permute-done.21.refs_2_ = bf16[1024,128]{1,0:T(8,128)(2,1)S(1)} collective-permute-done((bf16[1024,128]{1,0:T(8,128)(2,1)}, bf16[1024,128]{1,0:T(8,128)(2,1)S(1)}, u32[]{:S(2)}, u32[]{:S(2)}) %collective-permute-start.21) | collective-permute-done | bytes 262176 | tf_op jit(solution)/shard_map/ppermute | solution.py:315
  102.3 1.9 %collective-permute-done.23.refs_7_ = bf16[1024,128]{1,0:T(8,128)(2,1)S(1)} collective-permute-done((bf16[1024,128]{1,0:T(8,128)(2,1)}, bf16[1024,128]{1,0:T(8,128)(2,1)S(1)}, u32[]{:S(2)}, u32[]{:S(2)}) %collective-permute-start.23) | collective-permute-done | bytes 262176 | tf_op jit(solution)/shard_map/ppermute | solution.py:302
  104.9 2.6 %shard_map.107 = (bf16[1024,128]{1,0:T(8,128)(2,1)}, bf16[1024,128]{1,0:T(8,128)(2,1)}) custom-call(f32[1024,128]{1,0:T(8,128)} %get-tuple-element.53.refs_0_, bf16[1024,128]{1,0:T(8,128)(2,1)} %copy-done.14, bf16[1024,128]{1,0:T(8,128)(2,1)} %copy-done.16, bf16[1024,128]{1,0:T(8,128)(2,1)} %copy-done.15, ...), custom_call_target="tpu_custom_call", output_to_operand_aliasing={{1}: (7, {})} | custom-call | tf_op jit(solution)/shard_map/pallas_call | solution.py:359
  108.2 3.3 %collective-permute-start.25 = (bf16[1024,128]{1,0:T(8,128)(2,1)}, bf16[1024,128]{1,0:T(8,128)(2,1)S(1)}, u32[]{:S(2)}, u32[]{:S(2)}) collective-permute-start(bf16[1024,128]{1,0:T(8,128)(2,1)} %get-tuple-element.35.refs_0_), channel_id=1, source_target_pairs={{0,2},{1,3},{2,0},{3,1},{4,6},{5,7},{6,4},{7,5},{8,10},{9,11},{10,... | collective-permute-start | bytes 786440 | tf_op jit(solution)/shard_map/ppermute | solution.py:302
  111.5 2.0 %collective-permute-start.31 = (bf16[1,448,512]{2,1,0:T(8,128)(2,1)S(1)}, bf16[1,448,512]{2,1,0:T(8,128)(2,1)S(1)}, u32[]{:S(2)}, u32[]{:S(2)}) collective-permute-start(bf16[1,448,512]{2,1,0:T(8,128)(2,1)S(1)} %get-tuple-element.47), channel_id=1, source_target_pairs={{0,24},{4,28},{8,16},{12,20},{16,8},{20,12},{24,0},{28,4},{1,25},{... | collective-permute-start | bytes 1376264 | tf_op jit(solution)/shard_map/ppermute | solution.py:315
  115.1 5.2 %collective-permute-done.28.refs_3_ = bf16[1024,128]{1,0:T(8,128)(2,1)S(1)} collective-permute-done((bf16[1024,128]{1,0:T(8,128)(2,1)}, bf16[1024,128]{1,0:T(8,128)(2,1)S(1)}, u32[]{:S(2)}, u32[]{:S(2)}) %collective-permute-start.28) | collective-permute-done | bytes 262176 | tf_op jit(solution)/shard_map/ppermute | solution.py:302
  120.3 3.4 %collective-permute-done.25.refs_2_.refs_5_ = bf16[1024,128]{1,0:T(8,128)(2,1)S(1)} collective-permute-done((bf16[1024,128]{1,0:T(8,128)(2,1)}, bf16[1024,128]{1,0:T(8,128)(2,1)S(1)}, u32[]{:S(2)}, u32[]{:S(2)}) %collective-permute-start.25) | collective-permute-done | bytes 262176 | tf_op jit(solution)/shard_map/ppermute | solution.py:302
  123.9 2.2 %shard_map.110.refs_6_ = bf16[1024,512]{1,0:T(8,128)(2,1)} custom-call(s32[1]{0:T(128)} %bitcast.7.my_ref, bf16[1024,128]{1,0:T(8,128)(2,1)} %shard_map.109.refs_0_, bf16[1024,128]{1,0:T(8,128)(2,1)} %copy-done.28, bf16[1024,128]{1,0:T(8,128)(2,1)} %get-tuple-element.37.refs_2_, bf16[1024,128]{1,0:T(8,128)(2,1)} %copy-done.34), custom_call_target="tpu_custom_call" | custom-call | tf_op jit(solution)/shard_map/pallas_call | solution.py:289
  126.1 3.5 %collective-permute-done.24.refs_1_.refs_4_ = bf16[1024,128]{1,0:T(8,128)(2,1)S(1)} collective-permute-done((bf16[1024,128]{1,0:T(8,128)(2,1)}, bf16[1024,128]{1,0:T(8,128)(2,1)S(1)}, u32[]{:S(2)}, u32[]{:S(2)}) %collective-permute-start.24) | collective-permute-done | bytes 262176 | tf_op jit(solution)/shard_map/ppermute | solution.py:302
  129.7 4.4 %collective-permute-done.30.refs_2_ = bf16[1,448,512]{2,1,0:T(8,128)(2,1)S(1)} collective-permute-done((bf16[1,448,512]{2,1,0:T(8,128)(2,1)S(1)}, bf16[1,448,512]{2,1,0:T(8,128)(2,1)S(1)}, u32[]{:S(2)}, u32[]{:S(2)}) %collective-permute-start.30) | collective-permute-done | bytes 458784 | tf_op jit(solution)/shard_map/ppermute | solution.py:315
  135.1 2.7 %shard_map.111 = f32[448,512]{1,0:T(8,128)} custom-call(f32[1,448,512]{2,1,0:T(8,128)} %get-tuple-element.49.refs_0_, bf16[1,448,512]{2,1,0:T(8,128)(2,1)} %copy-done.13, bf16[1,448,512]{2,1,0:T(8,128)(2,1)} %copy-done.12, bf16[1,448,512]{2,1,0:T(8,128)(2,1)} %copy-done.11, bf16[1024,128]{1,0:T(8,128)(2,1)} %copy-done.6, bf16[1024,128]{1,0:T(8,128)(2,1)} %copy-done.5, ...), custom_call_target="tpu_custom_call" | custom-call | tf_op jit(solution)/shard_map/pallas_call | solution.py:528
  138.5 2.2 %shard_map.108 = bf16[1024,512]{1,0:T(8,128)(2,1)} custom-call(s32[1]{0:T(128)} %bitcast.7.my_ref, bf16[1024,128]{1,0:T(8,128)(2,1)} %get-tuple-element.35.refs_0_, bf16[1024,128]{1,0:T(8,128)(2,1)} %copy-done.6, bf16[1024,128]{1,0:T(8,128)(2,1)} %copy-done.5, bf16[1024,128]{1,0:T(8,128)(2,1)} %copy-done.36), custom_call_target="tpu_custom_call" | custom-call | tf_op jit(solution)/shard_map/pallas_call | solution.py:289
  (149 shorter events, 25.2 us)
Async XLA Ops:
  1.9 23.9 %collective-permute-start.12 = (bf16[1024,128]{1,0:T(8,128)(2,1)S(1)}, bf16[1024,128]{1,0:T(8,128)(2,1)S(1)}, u32[]{:S(2)}, u32[]{:S(2)}) collective-permute-start(bf16[1024,128]{1,0:T(8,128)(2,1)S(1)} %constant_dynamic-slice_fusion.refs_8_), channel_id=1, source_target_pairs={{0,24},{4,28},{8,16},{12,20},{16,8},{20,12},{24,0},{28,4},{1,25},{... | collective-permute-start | bytes 786440 | tf_op jit(solution)/shard_map/ppermute | solution.py:315
  5.9 20.5 %collective-permute-start.10 = (bf16[1024,128]{1,0:T(8,128)(2,1)S(1)}, bf16[1024,128]{1,0:T(8,128)(2,1)S(1)}, u32[]{:S(2)}, u32[]{:S(2)}) collective-permute-start(bf16[1024,128]{1,0:T(8,128)(2,1)S(1)} %constant_dynamic-slice_fusion.refs_8_), channel_id=1, source_target_pairs={{0,16},{4,20},{8,24},{12,28},{16,0},{20,4},{24,8},{28,12},{1,17},{... | collective-permute-start | bytes 786440 | tf_op jit(solution)/shard_map/ppermute | solution.py:315
  6.4 20.5 %collective-permute-start.8 = (bf16[1024,128]{1,0:T(8,128)(2,1)S(1)}, bf16[1024,128]{1,0:T(8,128)(2,1)S(1)}, u32[]{:S(2)}, u32[]{:S(2)}) collective-permute-start(bf16[1024,128]{1,0:T(8,128)(2,1)S(1)} %constant_dynamic-slice_fusion.refs_8_), channel_id=1, source_target_pairs={{0,8},{4,12},{8,0},{12,4},{16,24},{20,28},{24,16},{28,20},{1,9},{5... | collective-permute-start | bytes 786440 | tf_op jit(solution)/shard_map/ppermute | solution.py:315
  6.5 20.4 %collective-permute-start.7 = (bf16[1024,128]{1,0:T(8,128)(2,1)S(1)}, bf16[1024,128]{1,0:T(8,128)(2,1)S(1)}, u32[]{:S(2)}, u32[]{:S(2)}) collective-permute-start(bf16[1024,128]{1,0:T(8,128)(2,1)S(1)} %constant_dynamic-slice_fusion.refs_8_), channel_id=1, source_target_pairs={{0,4},{4,0},{8,12},{12,8},{16,20},{20,16},{24,28},{28,24},{1,5},{5... | collective-permute-start | bytes 786440 | tf_op jit(solution)/shard_map/ppermute | solution.py:315
  8.6 9.8 %all-to-all-start = ((s32[8,8,128]{2,1,0:T(8,128)}), s32[8,8,128]{2,1,0:T(8,128)S(1)}, u32[]{:S(2)}, u32[]{:S(2)}) async-start(s32[8,8,128]{2,1,0:T(8,128)} %broadcast_in_dim.40), calls=%async_computation | async-start | bytes 65536 | tf_op jit(solution)/shard_map/all_to_all | solution.py:551
  23.4 13.3 %collective-permute-start.5 = (bf16[1024,128]{1,0:T(8,128)(2,1)S(1)}, bf16[1024,128]{1,0:T(8,128)(2,1)S(1)}, u32[]{:S(2)}, u32[]{:S(2)}) collective-permute-start(bf16[1024,128]{1,0:T(8,128)(2,1)S(1)} %get-tuple-element.38.refs_0_), channel_id=1, source_target_pairs={{0,24},{4,28},{8,16},{12,20},{16,8},{20,12},{24,0},{28,4},{1,25},{... | collective-permute-start | bytes 786440 | tf_op jit(solution)/shard_map/ppermute | solution.py:315
  25.8 12.3 %collective-permute-start.3 = (bf16[1024,128]{1,0:T(8,128)(2,1)S(1)}, bf16[1024,128]{1,0:T(8,128)(2,1)S(1)}, u32[]{:S(2)}, u32[]{:S(2)}) collective-permute-start(bf16[1024,128]{1,0:T(8,128)(2,1)S(1)} %get-tuple-element.38.refs_0_), channel_id=1, source_target_pairs={{0,16},{4,20},{8,24},{12,28},{16,0},{20,4},{24,8},{28,12},{1,17},{... | collective-permute-start | bytes 786440 | tf_op jit(solution)/shard_map/ppermute | solution.py:315
  26.4 11.7 %collective-permute-start.1 = (bf16[1024,128]{1,0:T(8,128)(2,1)S(1)}, bf16[1024,128]{1,0:T(8,128)(2,1)S(1)}, u32[]{:S(2)}, u32[]{:S(2)}) collective-permute-start(bf16[1024,128]{1,0:T(8,128)(2,1)S(1)} %get-tuple-element.38.refs_0_), channel_id=1, source_target_pairs={{0,8},{4,12},{8,0},{12,4},{16,24},{20,28},{24,16},{28,20},{1,9},{5... | collective-permute-start | bytes 786440 | tf_op jit(solution)/shard_map/ppermute | solution.py:315
  26.9 11.7 %collective-permute-start = (bf16[1024,128]{1,0:T(8,128)(2,1)S(1)}, bf16[1024,128]{1,0:T(8,128)(2,1)S(1)}, u32[]{:S(2)}, u32[]{:S(2)}) collective-permute-start(bf16[1024,128]{1,0:T(8,128)(2,1)S(1)} %get-tuple-element.38.refs_0_), channel_id=1, source_target_pairs={{0,4},{4,0},{8,12},{12,8},{16,20},{20,16},{24,28},{28,24},{1,5},{5... | collective-permute-start | bytes 786440 | tf_op jit(solution)/shard_map/ppermute | solution.py:315
  26.9 11.8 %collective-permute-start.13 = (bf16[1024,128]{1,0:T(8,128)(2,1)S(1)}, bf16[1024,128]{1,0:T(8,128)(2,1)S(1)}, u32[]{:S(2)}, u32[]{:S(2)}) collective-permute-start(bf16[1024,128]{1,0:T(8,128)(2,1)S(1)} %collective-permute-done.12.refs_14_), channel_id=1, source_target_pairs={{0,4},{4,0},{8,12},{12,8},{16,20},{20,16},{24,28},{28,24},{1,5},{5... | collective-permute-start | bytes 786440 | tf_op jit(solution)/shard_map/ppermute | solution.py:315
  36.7 3.2 %collective-permute-start.11 = (bf16[1024,128]{1,0:T(8,128)(2,1)S(1)}, bf16[1024,128]{1,0:T(8,128)(2,1)S(1)}, u32[]{:S(2)}, u32[]{:S(2)}) collective-permute-start(bf16[1024,128]{1,0:T(8,128)(2,1)S(1)} %collective-permute-done.10.refs_12_), channel_id=1, source_target_pairs={{0,4},{4,0},{8,12},{12,8},{16,20},{20,16},{24,28},{28,24},{1,5},{5... | collective-permute-start | bytes 786440 | tf_op jit(solution)/shard_map/ppermute | solution.py:315
  38.1 1.8 %collective-permute-start.9 = (bf16[1024,128]{1,0:T(8,128)(2,1)S(1)}, bf16[1024,128]{1,0:T(8,128)(2,1)S(1)}, u32[]{:S(2)}, u32[]{:S(2)}) collective-permute-start(bf16[1024,128]{1,0:T(8,128)(2,1)S(1)} %collective-permute-done.8.refs_10_), channel_id=1, source_target_pairs={{0,4},{4,0},{8,12},{12,8},{16,20},{20,16},{24,28},{28,24},{1,5},{5... | collective-permute-start | bytes 786440 | tf_op jit(solution)/shard_map/ppermute | solution.py:315
  38.1 1.9 %collective-permute-start.6 = (bf16[1024,128]{1,0:T(8,128)(2,1)S(1)}, bf16[1024,128]{1,0:T(8,128)(2,1)S(1)}, u32[]{:S(2)}, u32[]{:S(2)}) collective-permute-start(bf16[1024,128]{1,0:T(8,128)(2,1)S(1)} %collective-permute-done.5.refs_6_), channel_id=1, source_target_pairs={{0,4},{4,0},{8,12},{12,8},{16,20},{20,16},{24,28},{28,24},{1,5},{5... | collective-permute-start | bytes 786440 | tf_op jit(solution)/shard_map/ppermute | solution.py:315
  38.7 2.0 %collective-permute-start.2 = (bf16[1024,128]{1,0:T(8,128)(2,1)S(1)}, bf16[1024,128]{1,0:T(8,128)(2,1)S(1)}, u32[]{:S(2)}, u32[]{:S(2)}) collective-permute-start(bf16[1024,128]{1,0:T(8,128)(2,1)S(1)} %collective-permute-done.1.refs_2_), channel_id=1, source_target_pairs={{0,4},{4,0},{8,12},{12,8},{16,20},{20,16},{24,28},{28,24},{1,5},{5... | collective-permute-start | bytes 786440 | tf_op jit(solution)/shard_map/ppermute | solution.py:315
  60.2 4.3 %collective-permute-start.14 = (bf16[4096,128]{1,0:T(8,128)(2,1)}, bf16[4096,128]{1,0:T(8,128)(2,1)}, u32[]{:S(2)}, u32[]{:S(2)}) collective-permute-start(bf16[4096,128]{1,0:T(8,128)(2,1)} %get-tuple-element.27), channel_id=1, source_target_pairs={{0,4},{4,0},{8,12},{12,8},{16,20},{20,16},{24,28},{28,24},{1,5},{5... | collective-permute-start | bytes 3145736 | tf_op jit(solution)/shard_map/ppermute | solution.py:315
  61.2 10.0 %collective-permute-start.15 = (bf16[4096,128]{1,0:T(8,128)(2,1)}, bf16[4096,128]{1,0:T(8,128)(2,1)S(1)}, u32[]{:S(2)}, u32[]{:S(2)}) collective-permute-start(bf16[4096,128]{1,0:T(8,128)(2,1)} %get-tuple-element.29), channel_id=1, source_target_pairs={{0,4},{4,0},{8,12},{12,8},{16,20},{20,16},{24,28},{28,24},{1,5},{5... | collective-permute-start | bytes 3145736 | tf_op jit(solution)/shard_map/ppermute | solution.py:315
  67.1 14.9 %collective-permute-start.18 = (bf16[1024,128]{1,0:T(8,128)(2,1)}, bf16[1024,128]{1,0:T(8,128)(2,1)S(1)}, u32[]{:S(2)}, u32[]{:S(2)}) collective-permute-start(bf16[1024,128]{1,0:T(8,128)(2,1)} %get-tuple-element.55), channel_id=1, source_target_pairs={{0,24},{4,28},{8,16},{12,20},{16,8},{20,12},{24,0},{28,4},{1,25},{... | collective-permute-start | bytes 786440 | tf_op jit(solution)/shard_map/ppermute | solution.py:315
  70.5 12.4 %collective-permute-start.17 = (bf16[1024,128]{1,0:T(8,128)(2,1)}, bf16[1024,128]{1,0:T(8,128)(2,1)S(1)}, u32[]{:S(2)}, u32[]{:S(2)}) collective-permute-start(bf16[1024,128]{1,0:T(8,128)(2,1)} %get-tuple-element.56), channel_id=1, source_target_pairs={{0,16},{4,20},{8,24},{12,28},{16,0},{20,4},{24,8},{28,12},{1,17},{... | collective-permute-start | bytes 786440 | tf_op jit(solution)/shard_map/ppermute | solution.py:315
  70.5 12.4 %collective-permute-start.16 = (bf16[1024,128]{1,0:T(8,128)(2,1)S(1)}, bf16[1024,128]{1,0:T(8,128)(2,1)S(1)}, u32[]{:S(2)}, u32[]{:S(2)}) collective-permute-start(bf16[1024,128]{1,0:T(8,128)(2,1)S(1)} %get-tuple-element.58.refs_0_), channel_id=1, source_target_pairs={{0,8},{4,12},{8,0},{12,4},{16,24},{20,28},{24,16},{28,20},{1,9},{5... | collective-permute-start | bytes 786440 | tf_op jit(solution)/shard_map/ppermute | solution.py:315
  85.9 6.2 %collective-permute-start.19 = (bf16[4,448,512]{2,1,0:T(8,128)(2,1)}, bf16[4,448,512]{2,1,0:T(8,128)(2,1)S(1)}, u32[]{:S(2)}, u32[]{:S(2)}) collective-permute-start(bf16[4,448,512]{2,1,0:T(8,128)(2,1)} %get-tuple-element.33), channel_id=1, source_target_pairs={{0,4},{4,0},{8,12},{12,8},{16,20},{20,16},{24,28},{28,24},{1,5},{5... | collective-permute-start | bytes 5505032 | tf_op jit(solution)/shard_map/ppermute | solution.py:315
  86.0 16.3 %collective-permute-start.20 = (bf16[1024,128]{1,0:T(8,128)(2,1)S(1)}, bf16[1024,128]{1,0:T(8,128)(2,1)S(1)}, u32[]{:S(2)}, u32[]{:S(2)}) collective-permute-start(bf16[1024,128]{1,0:T(8,128)(2,1)S(1)} %copy-done.9), channel_id=1, source_target_pairs={{0,8},{4,12},{8,0},{12,4},{16,24},{20,28},{24,16},{28,20},{1,9},{5... | collective-permute-start | bytes 786440 | tf_op jit(solution)/shard_map/ppermute | solution.py:315
  87.7 13.0 %collective-permute-start.22 = (bf16[1024,128]{1,0:T(8,128)(2,1)}, bf16[1024,128]{1,0:T(8,128)(2,1)S(1)}, u32[]{:S(2)}, u32[]{:S(2)}) collective-permute-start(bf16[1024,128]{1,0:T(8,128)(2,1)} %get-tuple-element.51), channel_id=1, source_target_pairs={{0,24},{4,28},{8,16},{12,20},{16,8},{20,12},{24,0},{28,4},{1,25},{... | collective-permute-start | bytes 786440 | tf_op jit(solution)/shard_map/ppermute | solution.py:315
  88.1 14.1 %collective-permute-start.21 = (bf16[1024,128]{1,0:T(8,128)(2,1)}, bf16[1024,128]{1,0:T(8,128)(2,1)S(1)}, u32[]{:S(2)}, u32[]{:S(2)}) collective-permute-start(bf16[1024,128]{1,0:T(8,128)(2,1)} %get-tuple-element.52), channel_id=1, source_target_pairs={{0,16},{4,20},{8,24},{12,28},{16,0},{20,4},{24,8},{28,12},{1,17},{... | collective-permute-start | bytes 786440 | tf_op jit(solution)/shard_map/ppermute | solution.py:315
  89.5 14.7 %collective-permute-start.23 = (bf16[1024,128]{1,0:T(8,128)(2,1)}, bf16[1024,128]{1,0:T(8,128)(2,1)S(1)}, u32[]{:S(2)}, u32[]{:S(2)}) collective-permute-start(bf16[1024,128]{1,0:T(8,128)(2,1)} %get-tuple-element.34), channel_id=1, source_target_pairs={{0,2},{1,3},{2,0},{3,1},{4,6},{5,7},{6,4},{7,5},{8,10},{9,11},{10,... | collective-permute-start | bytes 786440 | tf_op jit(solution)/shard_map/ppermute | solution.py:302
  93.7 21.0 %collective-permute-start.27 = (bf16[1024,128]{1,0:T(8,128)(2,1)}, bf16[1024,128]{1,0:T(8,128)(2,1)S(1)}, u32[]{:S(2)}, u32[]{:S(2)}) collective-permute-start(bf16[1024,128]{1,0:T(8,128)(2,1)} %shard_map.109.refs_0_), channel_id=1, source_target_pairs={{0,1},{1,0},{2,3},{3,2},{4,5},{5,4},{6,7},{7,6},{8,9},{9,8},{10,11... | collective-permute-start | bytes 786440 | tf_op jit(solution)/shard_map/ppermute | solution.py:302
  107.5 12.8 %collective-permute-start.28 = (bf16[1024,128]{1,0:T(8,128)(2,1)}, bf16[1024,128]{1,0:T(8,128)(2,1)S(1)}, u32[]{:S(2)}, u32[]{:S(2)}) collective-permute-start(bf16[1024,128]{1,0:T(8,128)(2,1)} %get-tuple-element.37.refs_2_), channel_id=1, source_target_pairs={{0,1},{1,0},{2,3},{3,2},{4,5},{5,4},{6,7},{7,6},{8,9},{9,8},{10,11... | collective-permute-start | bytes 786440 | tf_op jit(solution)/shard_map/ppermute | solution.py:302
  108.2 15.5 %collective-permute-start.25 = (bf16[1024,128]{1,0:T(8,128)(2,1)}, bf16[1024,128]{1,0:T(8,128)(2,1)S(1)}, u32[]{:S(2)}, u32[]{:S(2)}) collective-permute-start(bf16[1024,128]{1,0:T(8,128)(2,1)} %get-tuple-element.35.refs_0_), channel_id=1, source_target_pairs={{0,2},{1,3},{2,0},{3,1},{4,6},{5,7},{6,4},{7,5},{8,10},{9,11},{10,... | collective-permute-start | bytes 786440 | tf_op jit(solution)/shard_map/ppermute | solution.py:302
  111.5 18.1 %collective-permute-start.31 = (bf16[1,448,512]{2,1,0:T(8,128)(2,1)S(1)}, bf16[1,448,512]{2,1,0:T(8,128)(2,1)S(1)}, u32[]{:S(2)}, u32[]{:S(2)}) collective-permute-start(bf16[1,448,512]{2,1,0:T(8,128)(2,1)S(1)} %get-tuple-element.47), channel_id=1, source_target_pairs={{0,24},{4,28},{8,16},{12,20},{16,8},{20,12},{24,0},{28,4},{1,25},{... | collective-permute-start | bytes 1376264 | tf_op jit(solution)/shard_map/ppermute | solution.py:315
  113.6 20.5 %collective-permute-start.30 = (bf16[1,448,512]{2,1,0:T(8,128)(2,1)S(1)}, bf16[1,448,512]{2,1,0:T(8,128)(2,1)S(1)}, u32[]{:S(2)}, u32[]{:S(2)}) collective-permute-start(bf16[1,448,512]{2,1,0:T(8,128)(2,1)S(1)} %get-tuple-element.48), channel_id=1, source_target_pairs={{0,16},{4,20},{8,24},{12,28},{16,0},{20,4},{24,8},{28,12},{1,17},{... | collective-permute-start | bytes 1376264 | tf_op jit(solution)/shard_map/ppermute | solution.py:315
  114.7 19.4 %collective-permute-start.29 = (bf16[1,448,512]{2,1,0:T(8,128)(2,1)S(1)}, bf16[1,448,512]{2,1,0:T(8,128)(2,1)S(1)}, u32[]{:S(2)}, u32[]{:S(2)}) collective-permute-start(bf16[1,448,512]{2,1,0:T(8,128)(2,1)S(1)} %copy-done.1), channel_id=1, source_target_pairs={{0,8},{4,12},{8,0},{12,4},{16,24},{20,28},{24,16},{28,20},{1,9},{5... | collective-permute-start | bytes 1376264 | tf_op jit(solution)/shard_map/ppermute | solution.py:315
  120.3 9.3 %collective-permute-start.24 = (bf16[1024,128]{1,0:T(8,128)(2,1)}, bf16[1024,128]{1,0:T(8,128)(2,1)S(1)}, u32[]{:S(2)}, u32[]{:S(2)}) collective-permute-start(bf16[1024,128]{1,0:T(8,128)(2,1)} %get-tuple-element.35.refs_0_), channel_id=1, source_target_pairs={{0,1},{1,0},{2,3},{3,2},{4,5},{5,4},{6,7},{7,6},{8,9},{9,8},{10,11... | collective-permute-start | bytes 786440 | tf_op jit(solution)/shard_map/ppermute | solution.py:302
  123.7 14.1 %collective-permute-start.26 = (bf16[1024,128]{1,0:T(8,128)(2,1)S(1)}, bf16[1024,128]{1,0:T(8,128)(2,1)S(1)}, u32[]{:S(2)}, u32[]{:S(2)}) collective-permute-start(bf16[1024,128]{1,0:T(8,128)(2,1)S(1)} %collective-permute-done.25.refs_2_.refs_5_), channel_id=1, source_target_pairs={{0,1},{1,0},{2,3},{3,2},{4,5},{5,4},{6,7},{7,6},{8,9},{9,8},{10,11... | collective-permute-start | bytes 786440 | tf_op jit(solution)/shard_map/ppermute | solution.py:302
  (39 other events, 191.3 us)

commit v11 on v10

--- a/solution.py
+++ b/solution.py
@@ -82,22 +82,24 @@
 def attend_kernel(
     heads,
     ranks,
-    target_ref,
+    key_target_ref,
+    value_target_ref,
     source_ref,
     run_ref,
     slot_ref,
     need_ref,
-    query_ref,
-    up_ref,
-    up_t_ref,
     place_ref,
+    query_in,
+    up_in,
+    up_t_in,
     *refs,
 ):
     key_parts, refs = refs[:ranks], refs[ranks:]
     value_parts, refs = refs[:ranks], refs[ranks:]
-    gquery_ref, out_ref, *halves = refs[:6]
+    gquery_out, out_out, *halves = refs[:6]
     key_ref, value_ref, gkey_ref, gvalue_ref, key_win, value_win = refs[6:12]
-    score_ref, prob_ref, gscore_ref, load_sems, sems = refs[12:]
+    score_ref, prob_ref, gscore_ref, query_ref, up_ref, up_t_ref = refs[12:18]
+    gquery_ref, out_ref, load_sems, sems = refs[18:]
     rows_each = query_ref.shape[0]
     half_blocks = ranks * RUN_BLOCKS // 2
     scale = 1.0 / math.sqrt(HD)
@@ -111,19 +113,34 @@
             )
             copy.start()
             loads.append(copy)
+    for item, (source, whole) in enumerate(
+        ((query_in, query_ref), (up_in, up_ref), (up_t_in, up_t_ref))
+    ):
+        copy = pltpu.make_async_copy(source, whole, load_sems.at[2, item])
+        copy.start()
+        loads.append(copy)
     for copy in loads:
         copy.wait()
 
     def stores(block, act):
         side = block % 2
-        for step in range(RUN_BLOCKS):
-            target = target_ref[run_ref[block] * RUN_BLOCKS + step]
-            for place in range(2):
-
-                @pl.when(target // half_blocks == place)
-                def one_half():
-                    start = pl.multiple_of(target % half_blocks * ROWBLK, ROWBLK)
-                    for item, source in enumerate((gkey_ref, gvalue_ref)):
+        columns = pl.ds(pl.multiple_of(block * ROWBLK, ROWBLK), ROWBLK)
+        for item, (source, whole) in enumerate(((gquery_ref, gquery_out), (out_ref, out_out))):
+            act(
+                pltpu.make_async_copy(
+                    source.at[side], whole.at[:, columns], sems.at[side, 2, item]
+                )
+            )
+        for item, (source, target_ref) in enumerate(
+            ((gkey_ref, key_target_ref), (gvalue_ref, value_target_ref))
+        ):
+            for step in range(RUN_BLOCKS):
+                target = target_ref[run_ref[block] * RUN_BLOCKS + step]
+                start = pl.multiple_of(target % half_blocks * ROWBLK, ROWBLK)
+                for place in range(2):
+
+                    @pl.when(target // half_blocks == place)
+                    def one_half():
                         act(
                             pltpu.make_async_copy(
                                 source.at[side, pl.ds(step * ROWBLK, ROWBLK)],
@@ -209,8 +226,8 @@
         gvalue = jnp.dot(prob_b, up, preferred_element_type=jnp.float32)
         for head in range(heads):
             part = slice(head * ROWBLK, (head + 1) * ROWBLK)
-            out_ref[columns[head], at_rows] = out_b[:, part]
-            gquery_ref[columns[head], at_rows] = gquery_t[:, part]
+            out_ref[block % 2, columns[head], :] = out_b[:, part]
+            gquery_ref[block % 2, columns[head], :] = gquery_t[:, part]
         gkey = (gkey * scale).astype(jnp.bfloat16)
         gvalue = gvalue.astype(jnp.bfloat16)
         place_at = pl.ds(pl.multiple_of(first * ROWBLK, ROWBLK), rows)
@@ -236,7 +253,7 @@
         stores(block, lambda copy: copy.wait())
 
 
-def attend(tables, query, up, up_t, places, keys, values):
+def attend(tables, places, query, up, up_t, keys, values):
     rows, width = query.shape
     heads = width // HD
     ranks = len(keys)
@@ -255,17 +272,21 @@
             half,
             half,
         ),
-        in_specs=[smem] * 5 + [vmem] * 4 + [hbm] * (2 * ranks),
-        out_specs=(vmem, vmem, hbm, hbm, hbm, hbm),
+        in_specs=[smem] * 6 + [vmem] + [hbm] * (3 + 2 * ranks),
+        out_specs=[hbm] * 6,
         scratch_shapes=[pltpu.VMEM((every, HD), jnp.bfloat16)] * 2
         + [pltpu.VMEM((2, RUN_BLOCKS * ROWBLK, HD), jnp.bfloat16)] * 2
         + [pltpu.VMEM((RUN_BLOCKS * ROWBLK, HD), jnp.bfloat16)] * 2
         + [pltpu.VMEM((RUN_BLOCKS * ROWBLK, heads * ROWBLK), jnp.float32)]
         + [pltpu.VMEM((RUN_BLOCKS * ROWBLK, heads * ROWBLK), jnp.bfloat16)] * 2
-        + [pltpu.SemaphoreType.DMA((2, ranks)), pltpu.SemaphoreType.DMA((2, 2, RUN_BLOCKS))],
+        + [pltpu.VMEM((rows, width), jnp.bfloat16)] * 2
+        + [pltpu.VMEM((width, rows), jnp.bfloat16)]
+        + [pltpu.VMEM((2, width, ROWBLK), jnp.float32)]
+        + [pltpu.VMEM((2, width, ROWBLK), jnp.bfloat16)]
+        + [pltpu.SemaphoreType.DMA((3, ranks)), pltpu.SemaphoreType.DMA((2, 3, RUN_BLOCKS))],
         compiler_params=pltpu.CompilerParams(vmem_limit_bytes=VMEM_BYTES),
         cost_estimate=NO_COST,
-    )(*tables, query, up, up_t, places, *keys, *values)
+    )(*tables, places, query, up, up_t, *keys, *values)
 
 
 def assemble_kernel(lanes, my_ref, *refs):
@@ -341,34 +362,61 @@
     return [swap(item, 2 * at + 2) for at, item in enumerate(sends)]
 
 
-def final_kernel(count, rotary, outs, *refs):
-    total = refs[0][...].astype(jnp.float32)
-    for ref in refs[1 : 1 + count]:
-        total = total + ref[...].astype(jnp.float32)
-    if rotary:
-        total = total * refs[1 + count][...] - pltpu.roll(total, HD // 2, 1) * refs[2 + count][...]
-    for at in outs:
-        refs[at][...] = total.astype(refs[at].dtype)
-
-
-def final_sum(keep, received, tables, after, thru=(), copies=1):
+def place_of(distance, bits):
+    place = distance * 0
+    for bit in bits:
+        place = place * 2 + (distance & bit) // bit
+    return place
+
+
+def halved(keep, received):
+    half = keep.shape[0] // 2
+    send = added(keep[half:], received[half:]).astype(jnp.bfloat16)
+    return added(keep[:half], received[:half]), send
+
+
+def parts_of(array):
+    return [array[: array.shape[0] // 2], array[array.shape[0] // 2 :]]
+
+
+def final_kernel(counts, rotary, outs, *refs):
+    at = 0
+    rows = 0
+    tables = refs[sum(counts) : sum(counts) + 2]
+    for count in counts:
+        span = pl.ds(rows, refs[at].shape[0])
+        rows += refs[at].shape[0]
+        total = refs[at][...].astype(jnp.float32)
+        for ref in refs[at + 1 : at + count]:
+            total = total + ref[...].astype(jnp.float32)
+        at += count
+        if rotary:
+            total = total * tables[0][span, :] - pltpu.roll(total, HD // 2, 1) * tables[1][span, :]
+        for out in outs:
+            refs[out][span, :] = total.astype(refs[out].dtype)
+
+
+def final_sum(parts, tables, after, thru=(), copies=1):
     vmem = pl.BlockSpec(memory_space=pltpu.VMEM)
     hbm = pl.BlockSpec(memory_space=pl.ANY)
-    parts = [keep, *received, *tables]
-    inputs = len(parts) + len(after) + len(thru)
-    results = pl.pallas_call(
+    loaded = [item for part in parts for item in part] + [*tables]
+    rows = sum(part[0].shape[0] for part in parts)
+    inputs = len(loaded) + len(after) + len(thru)
+    return pl.pallas_call(
         partial(
-            final_kernel, len(received), len(tables) > 0, range(inputs, inputs + copies)
+            final_kernel,
+            [len(part) for part in parts],
+            len(tables) > 0,
+            range(inputs, inputs + copies),
         ),
-        out_shape=[jax.ShapeDtypeStruct(keep.shape, jnp.bfloat16)] * copies
+        out_shape=[jax.ShapeDtypeStruct((rows, HD), jnp.bfloat16)] * copies
         + [jax.ShapeDtypeStruct(item.shape, item.dtype) for item in thru],
-        in_specs=[vmem] * len(parts) + [hbm] * (len(after) + len(thru)),
+        in_specs=[vmem] * len(loaded) + [hbm] * (len(after) + len(thru)),
         out_specs=[vmem] * copies + [hbm] * len(thru),
         input_output_aliases={inputs - len(thru) + at: copies + at for at in range(len(thru))},
         compiler_params=pltpu.CompilerParams(vmem_limit_bytes=VMEM_BYTES),
         cost_estimate=NO_COST,
-    )(*parts, *after, *thru)
-    return results
+    )(*loaded, *after, *thru)
 
 
 def prepare_kernel(
@@ -575,7 +623,14 @@
     distance = (plan // block_count) ^ my_rank
     within = plan % block_count
     half_place = (distance & 1) * (rank_count // 2) + distance // 2
+    part_blocks = block_count // 2
+    stage_place = jnp.where(
+        within < part_blocks, place_of(distance, bits[1:]), place_of(distance, bits[:0:-1])
+    )
+    quarter = (distance & 1) * 2 + within // part_blocks
+    key_target = (quarter * (rank_count // 2) + stage_place) * part_blocks + within % part_blocks
     tables = (
+        key_target,
         half_place * block_count + within,
         distance * block_count + within,
         run,
@@ -583,32 +638,44 @@
         need,
     )
     grad_query_t, attn_t, gkey_keep, gkey_send, gvalue_keep, gvalue_send = attend(
-        tables, turned, up, up_t, places, keys, values
+        tables, places, turned, up, up_t, keys, values
     )
     value_keep, value_sends = chip_sum(gvalue_keep, swap(gvalue_send, 1))
     value_received = exchange(value_sends)
-    key_keep, key_sends = chip_sum(gkey_keep, swap(gkey_send, 1))
-    key_received = exchange(key_sends)
-    weight_keep, weight_send, value_keep = product(
-        my_rank, attn_t, grad_out, value_keep, [value_sends[0], key_sends[0]]
-    )
+    key_received = parts_of(swap(gkey_send, 1))
+    key_keeps = parts_of(gkey_keep)
+    for stage in range(len(bits) - 1):
+        key_sums = [halved(keep, item) for keep, item in zip(key_keeps, key_received)]
+        key_keeps = [item[0] for item in key_sums]
+        key_sends = [item[1] for item in key_sums]
+        steps = (bits[1 + stage], bits[len(bits) - 1 - stage])
+        key_received = [swap(item, step) for item, step in zip(key_sends, steps)]
+        if stage == 0:
+            first_received = key_received
+            weight_keep, weight_send, value_keep = product(
+                my_rank, attn_t, grad_out, value_keep, [*value_sends, *key_sends]
+            )
     far = lax.axis_size("tensor") // 2
     value_partial, value_near, weight_send = final_sum(
-        value_keep, value_received, (), (), thru=[weight_send], copies=2
+        [[value_keep, *value_received]], (), first_received, thru=[weight_send], copies=2
     )
     value_far = lane_swap(value_partial, far)
     weight_keep, weight_sends = chip_sum(weight_keep, swap(weight_send, 1))
     weight_received = exchange(weight_sends)
     value_near = hold(value_near, weight_sends[:1])
-    grad_query = turn_back(grad_query_t, cosine, sine, weight_sends[:1])
     key_partial, value_far = final_sum(
-        key_keep, key_received, (cosine, sine), [grad_query], thru=[value_far]
+        [list(part) for part in zip(key_keeps, key_received)], (cosine, sine), weight_sends[:1],
+        thru=[value_far],
     )
     value_all = assemble(my_lane, lane_pieces({0: value_near, far: value_far}, far // 2))
     key_pieces = lane_pieces({0: key_partial}, far)
     key_all = assemble(my_lane, key_pieces)
+    grad_query = turn_back(grad_query_t, cosine, sine, [key_partial])
     weight_grad = weight_final(
-        weight_keep, weight_received, 1.0 / rank_count, [*key_pieces[1:3], value_all]
+        weight_keep,
+        weight_received,
+        1.0 / rank_count,
+        [*key_pieces[1:3], value_all, grad_query],
     )
     lanes_per_key = group // local_heads
 

time: 143 us -> 143 us (level); the launches traced: 141 us -> 142 us
    convert_element_type x0 -> x3, other arithmetic: none -> 3.98 us  [halved(): send = added(keep[half:], received[half:]).astype(jnp.bfloat16)]
    convert_element_type x3 -> x1, other arithmetic: 5.52 us -> 1.59 us  [chip_sum(): return (total[0], [item.astype(keep.dtype) for item in total[1:]])]
    ppermute x26 -> x27, waiting for transfers between devices: 12.7 us -> 15.7 us  [swap(): lax.ppermute(array, 'dp', [(rank, rank ^ bit) for rank in range(ranks)])]
    ppermute x6, waiting for transfers between devices: 14 us -> 12.2 us  [lane_swap(): lax.ppermute(array, 'tensor', [(lane, lane ^ bit) for lane in range(lanes)])]
    ppermute x26 -> x27, starting transfers between devices: 21.9 us -> 22.7 us  [swap(): lax.ppermute(array, 'dp', [(rank, rank ^ bit) for rank in range(ranks)])]
  transfers between devices with their start and end apart: 33 -> 34, of which waited for: 14 -> 13; matrix products, arithmetic and copies ran while one was open for 13% -> 13% of each run, Pallas kernels for 22% -> 21%
where the time goes in v11:
time: 143 us; the launch traced here: 142 us
  Pallas kernels  53 us (37%)
  starting transfers between devices  35.4 us (25%)
  waiting for transfers between devices  29.5 us (21%)
  other arithmetic  17.3 us (12%)
  local copies, waits for them, and re-layouts  6.03 us (4%)
    ppermute x27, starting transfers between devices, swap(): lax.ppermute(array, 'dp', [(rank, rank ^ bit) for rank in range(ranks)])  22.7 us
    pallas_call x1, Pallas kernels, attend(): pl.pallas_call(partial(attend_kernel, heads, ranks), out_shape=(jax.Shape...  18 us
    ppermute x27, waiting for transfers between devices, swap(): lax.ppermute(array, 'dp', [(rank, rank ^ bit) for rank in range(ranks)])  15.7 us
    ppermute x6, waiting for transfers between devices, lane_swap(): lax.ppermute(array, 'tensor', [(lane, lane ^ bit) for lane in range(lanes)])  12.2 us
    pallas_call x1, Pallas kernels, product(): pl.pallas_call(product_kernel, grid_spec=pltpu.PrefetchScalarGridSpec(num...  9.52 us
    pallas_call x1, Pallas kernels, prepare(): pl.pallas_call(prepare_kernel, grid=(steps,), out_shape=[jax.ShapeDtypeSt...  9.22 us
    ppermute x6, starting transfers between devices, lane_swap(): lax.ppermute(array, 'tensor', [(lane, lane ^ bit) for lane in range(lanes)])  8.53 us
    pallas_call x2, Pallas kernels, final_sum(): pl.pallas_call(partial(final_kernel, [len(part) for part in parts], len(t...  4.74 us
  transfers between devices with their start and end apart: 34, of which 13 were waited for; matrix products, arithmetic and copies ran while one was open for 13% of the time, Pallas kernels for 21%

profile of v11, /device:TPU:0, one launch (start us, length us, event | category | flops | bytes accessed | tf_op | source)
XLA Modules:
  0.0 142.4 jit_solution(12056504897357696736)
XLA Ops:
  1.9 4.0 %collective-permute-start.12 = (bf16[1024,128]{1,0:T(8,128)(2,1)S(1)}, bf16[1024,128]{1,0:T(8,128)(2,1)S(1)}, u32[]{:S(2)}, u32[]{:S(2)}) collective-permute-start(bf16[1024,128]{1,0:T(8,128)(2,1)S(1)} %constant_dynamic-slice_fusion.refs_8_), channel_id=1, source_target_pairs={{0,24},{4,28},{8,16},{12,20},{16,8},{20,12},{24,0},{28,4},{1,25},{... | collective-permute-start | bytes 786440 | tf_op jit(solution)/shard_map/ppermute | solution.py:336
  8.6 4.2 %all-to-all-start = ((s32[8,8,128]{2,1,0:T(8,128)}), s32[8,8,128]{2,1,0:T(8,128)S(1)}, u32[]{:S(2)}, u32[]{:S(2)}) async-start(s32[8,8,128]{2,1,0:T(8,128)} %broadcast_in_dim.40), calls=%async_computation | async-start | bytes 65536 | tf_op jit(solution)/shard_map/all_to_all | solution.py:599
  16.8 1.6 %all-to-all-done = s32[8,8,128]{2,1,0:T(8,128)S(1)} async-done(((s32[8,8,128]{2,1,0:T(8,128)}), s32[8,8,128]{2,1,0:T(8,128)S(1)}, u32[]{:S(2)}, u32[]{:S(2)}) %all-to-all-start) | async-done | bytes 32800 | tf_op jit(solution)/shard_map/all_to_all | solution.py:599
  19.0 1.9 %fusion.6 = (f32[1024,64]{1,0:T(8,128)S(1)}, f32[1024,64]{1,0:T(8,128)S(1)}, f32[1024,64]{1,0:T(8,128)S(1)}) fusion(f32[64]{0:T(128)S(1)} %multiply_add_fusion.1, f32[1024]{0:T(1024)S(1)} %get-tuple-element.40), kind=kLoop, calls=%fused_computation.29 | loop fusion | flops 262144 | bytes 790784 | tf_op jit(solution)/shard_map/neg | solution.py:69
  21.0 2.4 %fusion.3 = (bf16[1024,128]{1,0:T(8,128)(2,1)S(1)}, f32[1024,128]{1,0:T(8,128)}, f32[1024,128]{1,0:T(8,128)}) fusion(f32[1024,64]{1,0:T(8,128)S(1)} %get-tuple-element.65, f32[1024,64]{1,0:T(8,128)S(1)} %get-tuple-element.64, bf16[1024,512]{1,0:T(8,128)(2,1)} %param.8, s32[]{:T(128)S(6)} %select_n.103, f32[1024,64]{1,0:T(8,128)S(1)} %get-tuple-element.68, ...), kind=kLoop, calls=%fused_computation.13 | loop fusion | flops 1048576 | bytes 2883588 | tf_op jit(solution)/shard_map/convert_element_type | solution.py:619
  23.4 2.4 %collective-permute-start.5 = (bf16[1024,128]{1,0:T(8,128)(2,1)S(1)}, bf16[1024,128]{1,0:T(8,128)(2,1)S(1)}, u32[]{:S(2)}, u32[]{:S(2)}) collective-permute-start(bf16[1024,128]{1,0:T(8,128)(2,1)S(1)} %get-tuple-element.38.refs_0_), channel_id=1, source_target_pairs={{0,24},{4,28},{8,16},{12,20},{16,8},{20,12},{24,0},{28,4},{1,25},{... | collective-permute-start | bytes 786440 | tf_op jit(solution)/shard_map/ppermute | solution.py:336
  27.4 9.2 %shard_map.102 = (bf16[1024,512]{1,0:T(8,128)(2,1)}, bf16[512,1024]{1,0:T(8,128)(2,1)}, bf16[1024,512]{1,0:T(8,128)(2,1)}) custom-call(bf16[1024,3584]{1,0:T(8,128)(2,1)} %right_ref.1, bf16[3584,512]{1,0:T(8,128)(2,1)} %weight_ref.1, bf16[1024,512]{1,0:T(8,128)(2,1)} %query_ref.1, f32[1024,128]{1,0:T(8,128)} %get-tuple-element.63.cos_ref.refs_4_, ...), custom_call_target="tpu_custom_call" | custom-call | flops 3758096384 | bytes 7340032 | tf_op jit(solution)/shard_map/pallas_call | solution.py:441
  36.8 1.3 collective-permute-done.3.refs_4_
  41.5 18.0 %shard_map.103 = (f32[512,1024]{1,0:T(8,128)}, bf16[512,1024]{1,0:T(8,128)(2,1)}, bf16[4096,128]{1,0:T(8,128)(2,1)}, bf16[4096,128]{1,0:T(8,128)(2,1)}, bf16[409...) custom-call(s32[64]{0:T(128)} %get-tuple-element.70.key_target_ref, s32[64]{0:T(128)} %get-tuple-element.69.value_target_ref, ...), custom_call_target="tpu_custom_call" | custom-call | tf_op jit(solution)/shard_map/pallas_call | solution.py:265
  60.8 2.4 %collective-permute-done.14 = bf16[4096,128]{1,0:T(8,128)(2,1)S(1)} collective-permute-done((bf16[4096,128]{1,0:T(8,128)(2,1)}, bf16[4096,128]{1,0:T(8,128)(2,1)S(1)}, u32[]{:S(2)}, u32[]{:S(2)}) %collective-permute-start.14) | collective-permute-done | bytes 1048608 | tf_op jit(solution)/shard_map/ppermute | solution.py:336
  63.2 1.5 %add_convert_fusion.6 = (bf16[1024,128]{1,0:T(8,128)(2,1)S(1)}, f32[1024,128]{1,0:T(8,128)S(1)}, bf16[1024,128]{1,0:T(8,128)(2,1)S(1)}, f32[1024,128]{1,0:T(8,128)S(1)}) fusion(bf16[4096,128]{1,0:T(8,128)(2,1)S(1)} %collective-permute-done.14, bf16[4096,128]{1,0:T(8,128)(2,1)} %get-tuple-element.25), kind=kLoop, calls=%fused_computation.18 | loop fusion | flops 1835008 | bytes 3670016 | tf_op jit(solution)/shard_map/convert_element_type | solution.py:374
  68.0 1.4 %collective-permute-start.22 = (bf16[1024,128]{1,0:T(8,128)(2,1)}, bf16[1024,128]{1,0:T(8,128)(2,1)}, u32[]{:S(2)}, u32[]{:S(2)}) collective-permute-start(bf16[1024,128]{1,0:T(8,128)(2,1)} %get-tuple-element.52.refs_2_), channel_id=1, source_target_pairs={{0,24},{4,28},{8,16},{12,20},{16,8},{20,12},{24,0},{28,4},{1,25},{... | collective-permute-start | bytes 786440 | tf_op jit(solution)/shard_map/ppermute | solution.py:336
  72.2 9.5 %shard_map.104 = (bf16[4,448,512]{2,1,0:T(8,128)(2,1)}, bf16[4,448,512]{2,1,0:T(8,128)(2,1)}, f32[1024,128]{1,0:T(8,128)}) custom-call(s32[2]{0:T(128)} %pad_add_fusion.my_ref, bf16[512,1024]{1,0:T(8,128)(2,1)} %get-tuple-element.27.left_ref, bf16[1024,3584]{1,0:T(8,128)(2,1)} %right_ref.1, ...), custom_call_target="tpu_custom_call", output_to_operand_aliasing={{2}: (8, {})} | custom-call | tf_op jit(solution)/shard_map/pallas_call | solution.py:547
  81.7 3.0 %collective-permute-done.21.refs_2_ = bf16[1024,128]{1,0:T(8,128)(2,1)} collective-permute-done((bf16[1024,128]{1,0:T(8,128)(2,1)}, bf16[1024,128]{1,0:T(8,128)(2,1)}, u32[]{:S(2)}, u32[]{:S(2)}) %collective-permute-start.21) | collective-permute-done | bytes 262176 | tf_op jit(solution)/shard_map/ppermute | solution.py:336
  85.4 2.3 %shard_map.105 = (bf16[1024,128]{1,0:T(8,128)(2,1)}, bf16[1024,128]{1,0:T(8,128)(2,1)}, bf16[4,448,512]{2,1,0:T(8,128)(2,1)}) custom-call(f32[1024,128]{1,0:T(8,128)} %get-tuple-element.31.refs_0_, bf16[1024,128]{1,0:T(8,128)(2,1)} %collective-permute-done.20.refs_1_, ...), custom_call_target="tpu_custom_call", output_to_operand_aliasing={{2}: (6, {})} | custom-call | tf_op jit(solution)/shard_map/pallas_call | solution.py:405
  87.8 1.7 %fusion.4 = (bf16[512,128]{1,0:T(8,128)(2,1)S(1)}, f32[512,128]{1,0:T(8,128)}) fusion(f32[1024,128]{1,0:T(8,128)S(1)} %get-tuple-element.56, bf16[1024,128]{1,0:T(8,128)(2,1)} %copy-done.7), kind=kLoop, calls=%fused_computation.23 | loop fusion | flops 327680 | bytes 1179648 | tf_op jit(solution)/shard_map/convert_element_type | solution.py:374
  90.6 2.6 %collective-permute-start.24 = (bf16[1024,128]{1,0:T(8,128)(2,1)}, bf16[1024,128]{1,0:T(8,128)(2,1)S(1)}, u32[]{:S(2)}, u32[]{:S(2)}) collective-permute-start(bf16[1024,128]{1,0:T(8,128)(2,1)} %get-tuple-element.34), channel_id=1, source_target_pairs={{0,2},{1,3},{2,0},{3,1},{4,6},{5,7},{6,4},{7,5},{8,10},{9,11},{10,... | collective-permute-start | bytes 786440 | tf_op jit(solution)/shard_map/ppermute | solution.py:323
  93.3 1.6 %add_convert_fusion = (bf16[1,448,512]{2,1,0:T(8,128)(2,1)S(1)}, bf16[1,448,512]{2,1,0:T(8,128)(2,1)S(1)}, f32[1,448,512]{2,1,0:T(8,128)}, bf16[1,448,512]{2,1,0:T(8,128)(2,1)}) fusion(bf16[4,448,512]{2,1,0:T(8,128)(2,1)S(1)} %collective-permute-done.23, bf16[4,448,512]{2,1,0:T(8,128)(2,1)S(1)} %copy-done.2), kind=kLoop, calls=%fused_computation.1 | loop fusion | flops 3440640 | bytes 5963776 | tf_op jit(solution)/shard_map/convert_element_type | solution.py:358
  94.9 1.6 %collective-permute-start.28 = (bf16[1024,128]{1,0:T(8,128)(2,1)}, bf16[1024,128]{1,0:T(8,128)(2,1)S(1)}, u32[]{:S(2)}, u32[]{:S(2)}) collective-permute-start(bf16[1024,128]{1,0:T(8,128)(2,1)} %shard_map.109.refs_0_), channel_id=1, source_target_pairs={{0,1},{1,0},{2,3},{3,2},{4,5},{5,4},{6,7},{7,6},{8,9},{9,8},{10,11... | collective-permute-start | bytes 786440 | tf_op jit(solution)/shard_map/ppermute | solution.py:323
  97.2 1.3 collective-permute-start.16
  98.5 3.8 %collective-permute-done.16.refs_1_ = bf16[512,128]{1,0:T(8,128)(2,1)S(1)} collective-permute-done((bf16[512,128]{1,0:T(8,128)(2,1)S(1)}, bf16[512,128]{1,0:T(8,128)(2,1)S(1)}, u32[]{:S(2)}, u32[]{:S(2)}) %collective-permute-start.16) | collective-permute-done | bytes 131104 | tf_op jit(solution)/shard_map/ppermute | solution.py:336
  102.3 3.6 %collective-permute-done.24.refs_7_ = bf16[1024,128]{1,0:T(8,128)(2,1)S(1)} collective-permute-done((bf16[1024,128]{1,0:T(8,128)(2,1)}, bf16[1024,128]{1,0:T(8,128)(2,1)S(1)}, u32[]{:S(2)}, u32[]{:S(2)}) %collective-permute-start.24) | collective-permute-done | bytes 262176 | tf_op jit(solution)/shard_map/ppermute | solution.py:323
  106.6 2.4 %shard_map.106 = (bf16[1024,128]{1,0:T(8,128)(2,1)}, bf16[1024,128]{1,0:T(8,128)(2,1)}) custom-call(f32[512,128]{1,0:T(8,128)} %get-tuple-element.62.refs_0_, bf16[512,128]{1,0:T(8,128)(2,1)} %copy-done.36, f32[512,128]{1,0:T(8,128)} %get-tuple-element.60.refs_2_, bf16[512,128]{1,0:T(8,128)(2,1)} %copy-done.35, ...), custom_call_target="tpu_custom_call", output_to_operand_aliasing={{1}: (7, {})} | custom-call | tf_op jit(solution)/shard_map/pallas_call | solution.py:405
  109.8 3.3 %collective-permute-start.26 = (bf16[1024,128]{1,0:T(8,128)(2,1)}, bf16[1024,128]{1,0:T(8,128)(2,1)S(1)}, u32[]{:S(2)}, u32[]{:S(2)}) collective-permute-start(bf16[1024,128]{1,0:T(8,128)(2,1)} %get-tuple-element.35.refs_0_), channel_id=1, source_target_pairs={{0,2},{1,3},{2,0},{3,1},{4,6},{5,7},{6,4},{7,5},{8,10},{9,11},{10,... | collective-permute-start | bytes 786440 | tf_op jit(solution)/shard_map/ppermute | solution.py:323
  113.1 1.4 %collective-permute-start.32 = (bf16[1,448,512]{2,1,0:T(8,128)(2,1)S(1)}, bf16[1,448,512]{2,1,0:T(8,128)(2,1)S(1)}, u32[]{:S(2)}, u32[]{:S(2)}) collective-permute-start(bf16[1,448,512]{2,1,0:T(8,128)(2,1)S(1)} %get-tuple-element.47), channel_id=1, source_target_pairs={{0,24},{4,28},{8,16},{12,20},{16,8},{20,12},{24,0},{28,4},{1,25},{... | collective-permute-start | bytes 1376264 | tf_op jit(solution)/shard_map/ppermute | solution.py:336
  116.7 5.5 %collective-permute-done.29.refs_3_ = bf16[1024,128]{1,0:T(8,128)(2,1)S(1)} collective-permute-done((bf16[1024,128]{1,0:T(8,128)(2,1)}, bf16[1024,128]{1,0:T(8,128)(2,1)S(1)}, u32[]{:S(2)}, u32[]{:S(2)}) %collective-permute-start.29) | collective-permute-done | bytes 262176 | tf_op jit(solution)/shard_map/ppermute | solution.py:323
  122.2 3.1 %collective-permute-done.26.refs_2_.refs_5_ = bf16[1024,128]{1,0:T(8,128)(2,1)S(1)} collective-permute-done((bf16[1024,128]{1,0:T(8,128)(2,1)}, bf16[1024,128]{1,0:T(8,128)(2,1)S(1)}, u32[]{:S(2)}, u32[]{:S(2)}) %collective-permute-start.26) | collective-permute-done | bytes 262176 | tf_op jit(solution)/shard_map/ppermute | solution.py:323
  125.5 4.4 %shard_map.107.refs_7_ = bf16[1024,512]{1,0:T(8,128)(2,1)} custom-call(f32[512,1024]{1,0:T(8,128)} %get-tuple-element.24.grad_ref, f32[1024,128]{1,0:T(8,128)} %get-tuple-element.63.cos_ref.refs_4_, f32[1024,128]{1,0:T(8,128)} %get-tuple-element.39.sin_ref.refs_5_, bf16[1024,128]{1,0:T(8,128)(2,1)} %get-tuple-element.35.refs_0_), custom_call_target="tpu_custom_call" | custom-call | tf_op jit(solution)/shard_map/pallas_call | solution.py:482
  129.9 2.2 %shard_map.110.refs_6_ = bf16[1024,512]{1,0:T(8,128)(2,1)} custom-call(s32[1]{0:T(128)} %bitcast.7.my_ref, bf16[1024,128]{1,0:T(8,128)(2,1)} %shard_map.109.refs_0_, bf16[1024,128]{1,0:T(8,128)(2,1)} %copy-done.28, bf16[1024,128]{1,0:T(8,128)(2,1)} %get-tuple-element.37.refs_2_, bf16[1024,128]{1,0:T(8,128)(2,1)} %copy-done.33), custom_call_target="tpu_custom_call" | custom-call | tf_op jit(solution)/shard_map/pallas_call | solution.py:310
  132.2 3.5 %collective-permute-done.31.refs_2_ = bf16[1,448,512]{2,1,0:T(8,128)(2,1)S(1)} collective-permute-done((bf16[1,448,512]{2,1,0:T(8,128)(2,1)S(1)}, bf16[1,448,512]{2,1,0:T(8,128)(2,1)S(1)}, u32[]{:S(2)}, u32[]{:S(2)}) %collective-permute-start.31) | collective-permute-done | bytes 458784 | tf_op jit(solution)/shard_map/ppermute | solution.py:336
  136.6 2.7 %shard_map.111 = f32[448,512]{1,0:T(8,128)} custom-call(f32[1,448,512]{2,1,0:T(8,128)} %get-tuple-element.49.refs_0_, bf16[1,448,512]{2,1,0:T(8,128)(2,1)} %copy-done.17, bf16[1,448,512]{2,1,0:T(8,128)(2,1)} %copy-done.16, bf16[1,448,512]{2,1,0:T(8,128)(2,1)} %copy-done.15, bf16[1024,128]{1,0:T(8,128)(2,1)} %copy-done.11, bf16[1024,128]{1,0:T(8,128)(2,1)} %copy-done.9, ...), custom_call_target="tpu_custom_call" | custom-call | tf_op jit(solution)/shard_map/pallas_call | solution.py:576
  140.1 2.2 %shard_map.108 = bf16[1024,512]{1,0:T(8,128)(2,1)} custom-call(s32[1]{0:T(128)} %bitcast.7.my_ref, bf16[1024,128]{1,0:T(8,128)(2,1)} %get-tuple-element.35.refs_0_, bf16[1024,128]{1,0:T(8,128)(2,1)} %copy-done.11, bf16[1024,128]{1,0:T(8,128)(2,1)} %copy-done.9, bf16[1024,128]{1,0:T(8,128)(2,1)} %copy-done.34), custom_call_target="tpu_custom_call" | custom-call | tf_op jit(solution)/shard_map/pallas_call | solution.py:310
  (153 shorter events, 29.0 us)
Async XLA Ops:
  1.9 23.9 %collective-permute-start.12 = (bf16[1024,128]{1,0:T(8,128)(2,1)S(1)}, bf16[1024,128]{1,0:T(8,128)(2,1)S(1)}, u32[]{:S(2)}, u32[]{:S(2)}) collective-permute-start(bf16[1024,128]{1,0:T(8,128)(2,1)S(1)} %constant_dynamic-slice_fusion.refs_8_), channel_id=1, source_target_pairs={{0,24},{4,28},{8,16},{12,20},{16,8},{20,12},{24,0},{28,4},{1,25},{... | collective-permute-start | bytes 786440 | tf_op jit(solution)/shard_map/ppermute | solution.py:336
  5.9 20.5 %collective-permute-start.10 = (bf16[1024,128]{1,0:T(8,128)(2,1)S(1)}, bf16[1024,128]{1,0:T(8,128)(2,1)S(1)}, u32[]{:S(2)}, u32[]{:S(2)}) collective-permute-start(bf16[1024,128]{1,0:T(8,128)(2,1)S(1)} %constant_dynamic-slice_fusion.refs_8_), channel_id=1, source_target_pairs={{0,16},{4,20},{8,24},{12,28},{16,0},{20,4},{24,8},{28,12},{1,17},{... | collective-permute-start | bytes 786440 | tf_op jit(solution)/shard_map/ppermute | solution.py:336
  6.4 20.5 %collective-permute-start.8 = (bf16[1024,128]{1,0:T(8,128)(2,1)S(1)}, bf16[1024,128]{1,0:T(8,128)(2,1)S(1)}, u32[]{:S(2)}, u32[]{:S(2)}) collective-permute-start(bf16[1024,128]{1,0:T(8,128)(2,1)S(1)} %constant_dynamic-slice_fusion.refs_8_), channel_id=1, source_target_pairs={{0,8},{4,12},{8,0},{12,4},{16,24},{20,28},{24,16},{28,20},{1,9},{5... | collective-permute-start | bytes 786440 | tf_op jit(solution)/shard_map/ppermute | solution.py:336
  6.5 20.4 %collective-permute-start.7 = (bf16[1024,128]{1,0:T(8,128)(2,1)S(1)}, bf16[1024,128]{1,0:T(8,128)(2,1)S(1)}, u32[]{:S(2)}, u32[]{:S(2)}) collective-permute-start(bf16[1024,128]{1,0:T(8,128)(2,1)S(1)} %constant_dynamic-slice_fusion.refs_8_), channel_id=1, source_target_pairs={{0,4},{4,0},{8,12},{12,8},{16,20},{20,16},{24,28},{28,24},{1,5},{5... | collective-permute-start | bytes 786440 | tf_op jit(solution)/shard_map/ppermute | solution.py:336
  8.6 9.8 %all-to-all-start = ((s32[8,8,128]{2,1,0:T(8,128)}), s32[8,8,128]{2,1,0:T(8,128)S(1)}, u32[]{:S(2)}, u32[]{:S(2)}) async-start(s32[8,8,128]{2,1,0:T(8,128)} %broadcast_in_dim.40), calls=%async_computation | async-start | bytes 65536 | tf_op jit(solution)/shard_map/all_to_all | solution.py:599
  23.4 13.3 %collective-permute-start.5 = (bf16[1024,128]{1,0:T(8,128)(2,1)S(1)}, bf16[1024,128]{1,0:T(8,128)(2,1)S(1)}, u32[]{:S(2)}, u32[]{:S(2)}) collective-permute-start(bf16[1024,128]{1,0:T(8,128)(2,1)S(1)} %get-tuple-element.38.refs_0_), channel_id=1, source_target_pairs={{0,24},{4,28},{8,16},{12,20},{16,8},{20,12},{24,0},{28,4},{1,25},{... | collective-permute-start | bytes 786440 | tf_op jit(solution)/shard_map/ppermute | solution.py:336
  25.8 12.3 %collective-permute-start.3 = (bf16[1024,128]{1,0:T(8,128)(2,1)S(1)}, bf16[1024,128]{1,0:T(8,128)(2,1)S(1)}, u32[]{:S(2)}, u32[]{:S(2)}) collective-permute-start(bf16[1024,128]{1,0:T(8,128)(2,1)S(1)} %get-tuple-element.38.refs_0_), channel_id=1, source_target_pairs={{0,16},{4,20},{8,24},{12,28},{16,0},{20,4},{24,8},{28,12},{1,17},{... | collective-permute-start | bytes 786440 | tf_op jit(solution)/shard_map/ppermute | solution.py:336
  26.4 11.7 %collective-permute-start.1 = (bf16[1024,128]{1,0:T(8,128)(2,1)S(1)}, bf16[1024,128]{1,0:T(8,128)(2,1)S(1)}, u32[]{:S(2)}, u32[]{:S(2)}) collective-permute-start(bf16[1024,128]{1,0:T(8,128)(2,1)S(1)} %get-tuple-element.38.refs_0_), channel_id=1, source_target_pairs={{0,8},{4,12},{8,0},{12,4},{16,24},{20,28},{24,16},{28,20},{1,9},{5... | collective-permute-start | bytes 786440 | tf_op jit(solution)/shard_map/ppermute | solution.py:336
  26.9 11.7 %collective-permute-start = (bf16[1024,128]{1,0:T(8,128)(2,1)S(1)}, bf16[1024,128]{1,0:T(8,128)(2,1)S(1)}, u32[]{:S(2)}, u32[]{:S(2)}) collective-permute-start(bf16[1024,128]{1,0:T(8,128)(2,1)S(1)} %get-tuple-element.38.refs_0_), channel_id=1, source_target_pairs={{0,4},{4,0},{8,12},{12,8},{16,20},{20,16},{24,28},{28,24},{1,5},{5... | collective-permute-start | bytes 786440 | tf_op jit(solution)/shard_map/ppermute | solution.py:336
  26.9 11.8 %collective-permute-start.13 = (bf16[1024,128]{1,0:T(8,128)(2,1)S(1)}, bf16[1024,128]{1,0:T(8,128)(2,1)S(1)}, u32[]{:S(2)}, u32[]{:S(2)}) collective-permute-start(bf16[1024,128]{1,0:T(8,128)(2,1)S(1)} %collective-permute-done.12.refs_14_), channel_id=1, source_target_pairs={{0,4},{4,0},{8,12},{12,8},{16,20},{20,16},{24,28},{28,24},{1,5},{5... | collective-permute-start | bytes 786440 | tf_op jit(solution)/shard_map/ppermute | solution.py:336
  36.7 3.2 %collective-permute-start.11 = (bf16[1024,128]{1,0:T(8,128)(2,1)S(1)}, bf16[1024,128]{1,0:T(8,128)(2,1)S(1)}, u32[]{:S(2)}, u32[]{:S(2)}) collective-permute-start(bf16[1024,128]{1,0:T(8,128)(2,1)S(1)} %collective-permute-done.10.refs_12_), channel_id=1, source_target_pairs={{0,4},{4,0},{8,12},{12,8},{16,20},{20,16},{24,28},{28,24},{1,5},{5... | collective-permute-start | bytes 786440 | tf_op jit(solution)/shard_map/ppermute | solution.py:336
  38.1 1.9 %collective-permute-start.6 = (bf16[1024,128]{1,0:T(8,128)(2,1)S(1)}, bf16[1024,128]{1,0:T(8,128)(2,1)S(1)}, u32[]{:S(2)}, u32[]{:S(2)}) collective-permute-start(bf16[1024,128]{1,0:T(8,128)(2,1)S(1)} %collective-permute-done.5.refs_6_), channel_id=1, source_target_pairs={{0,4},{4,0},{8,12},{12,8},{16,20},{20,16},{24,28},{28,24},{1,5},{5... | collective-permute-start | bytes 786440 | tf_op jit(solution)/shard_map/ppermute | solution.py:336
  38.7 2.0 %collective-permute-start.2 = (bf16[1024,128]{1,0:T(8,128)(2,1)S(1)}, bf16[1024,128]{1,0:T(8,128)(2,1)S(1)}, u32[]{:S(2)}, u32[]{:S(2)}) collective-permute-start(bf16[1024,128]{1,0:T(8,128)(2,1)S(1)} %collective-permute-done.1.refs_2_), channel_id=1, source_target_pairs={{0,4},{4,0},{8,12},{12,8},{16,20},{20,16},{24,28},{28,24},{1,5},{5... | collective-permute-start | bytes 786440 | tf_op jit(solution)/shard_map/ppermute | solution.py:336
  59.5 3.8 %collective-permute-start.14 = (bf16[4096,128]{1,0:T(8,128)(2,1)}, bf16[4096,128]{1,0:T(8,128)(2,1)S(1)}, u32[]{:S(2)}, u32[]{:S(2)}) collective-permute-start(bf16[4096,128]{1,0:T(8,128)(2,1)} %get-tuple-element.26), channel_id=1, source_target_pairs={{0,4},{4,0},{8,12},{12,8},{16,20},{20,16},{24,28},{28,24},{1,5},{5... | collective-permute-start | bytes 3145736 | tf_op jit(solution)/shard_map/ppermute | solution.py:336
  60.7 6.2 %collective-permute-start.19 = (bf16[4096,128]{1,0:T(8,128)(2,1)}, bf16[4096,128]{1,0:T(8,128)(2,1)S(1)}, u32[]{:S(2)}, u32[]{:S(2)}) collective-permute-start(bf16[4096,128]{1,0:T(8,128)(2,1)} %get-tuple-element.29), channel_id=1, source_target_pairs={{0,4},{4,0},{8,12},{12,8},{16,20},{20,16},{24,28},{28,24},{1,5},{5... | collective-permute-start | bytes 3145736 | tf_op jit(solution)/shard_map/ppermute | solution.py:336
  64.8 16.9 %collective-permute-start.17 = (bf16[1024,128]{1,0:T(8,128)(2,1)S(1)}, bf16[1024,128]{1,0:T(8,128)(2,1)S(1)}, u32[]{:S(2)}, u32[]{:S(2)}) collective-permute-start(bf16[1024,128]{1,0:T(8,128)(2,1)S(1)} %get-tuple-element.55.refs_4_), channel_id=1, source_target_pairs={{0,16},{4,20},{8,24},{12,28},{16,0},{20,4},{24,8},{28,12},{1,17},{... | collective-permute-start | bytes 786440 | tf_op jit(solution)/shard_map/ppermute | solution.py:336
  65.8 15.9 %collective-permute-start.15 = (bf16[1024,128]{1,0:T(8,128)(2,1)S(1)}, bf16[1024,128]{1,0:T(8,128)(2,1)S(1)}, u32[]{:S(2)}, u32[]{:S(2)}) collective-permute-start(bf16[1024,128]{1,0:T(8,128)(2,1)S(1)} %get-tuple-element.57.refs_3_), channel_id=1, source_target_pairs={{0,8},{4,12},{8,0},{12,4},{16,24},{20,28},{24,16},{28,20},{1,9},{5... | collective-permute-start | bytes 786440 | tf_op jit(solution)/shard_map/ppermute | solution.py:336
  68.0 13.7 %collective-permute-start.22 = (bf16[1024,128]{1,0:T(8,128)(2,1)}, bf16[1024,128]{1,0:T(8,128)(2,1)}, u32[]{:S(2)}, u32[]{:S(2)}) collective-permute-start(bf16[1024,128]{1,0:T(8,128)(2,1)} %get-tuple-element.52.refs_2_), channel_id=1, source_target_pairs={{0,24},{4,28},{8,16},{12,20},{16,8},{20,12},{24,0},{28,4},{1,25},{... | collective-permute-start | bytes 786440 | tf_op jit(solution)/shard_map/ppermute | solution.py:336
  69.5 15.3 %collective-permute-start.21 = (bf16[1024,128]{1,0:T(8,128)(2,1)}, bf16[1024,128]{1,0:T(8,128)(2,1)}, u32[]{:S(2)}, u32[]{:S(2)}) collective-permute-start(bf16[1024,128]{1,0:T(8,128)(2,1)} %get-tuple-element.53.refs_1_), channel_id=1, source_target_pairs={{0,16},{4,20},{8,24},{12,28},{16,0},{20,4},{24,8},{28,12},{1,17},{... | collective-permute-start | bytes 786440 | tf_op jit(solution)/shard_map/ppermute | solution.py:336
  70.4 15.1 %collective-permute-start.20 = (bf16[1024,128]{1,0:T(8,128)(2,1)S(1)}, bf16[1024,128]{1,0:T(8,128)(2,1)}, u32[]{:S(2)}, u32[]{:S(2)}) collective-permute-start(bf16[1024,128]{1,0:T(8,128)(2,1)S(1)} %get-tuple-element.54.refs_0_), channel_id=1, source_target_pairs={{0,8},{4,12},{8,0},{12,4},{16,24},{20,28},{24,16},{28,20},{1,9},{5... | collective-permute-start | bytes 786440 | tf_op jit(solution)/shard_map/ppermute | solution.py:336
  87.8 5.5 %collective-permute-start.23 = (bf16[4,448,512]{2,1,0:T(8,128)(2,1)}, bf16[4,448,512]{2,1,0:T(8,128)(2,1)S(1)}, u32[]{:S(2)}, u32[]{:S(2)}) collective-permute-start(bf16[4,448,512]{2,1,0:T(8,128)(2,1)} %get-tuple-element.33), channel_id=1, source_target_pairs={{0,4},{4,0},{8,12},{12,8},{16,20},{20,16},{24,28},{28,24},{1,5},{5... | collective-permute-start | bytes 5505032 | tf_op jit(solution)/shard_map/ppermute | solution.py:336
  89.5 9.0 %collective-permute-start.18 = (bf16[512,128]{1,0:T(8,128)(2,1)S(1)}, bf16[512,128]{1,0:T(8,128)(2,1)S(1)}, u32[]{:S(2)}, u32[]{:S(2)}) collective-permute-start(bf16[512,128]{1,0:T(8,128)(2,1)S(1)} %get-tuple-element.59), channel_id=1, source_target_pairs={{0,8},{4,12},{8,0},{12,4},{16,24},{20,28},{24,16},{28,20},{1,9},{5... | collective-permute-start | bytes 393224 | tf_op jit(solution)/shard_map/ppermute | solution.py:336
  90.6 15.3 %collective-permute-start.24 = (bf16[1024,128]{1,0:T(8,128)(2,1)}, bf16[1024,128]{1,0:T(8,128)(2,1)S(1)}, u32[]{:S(2)}, u32[]{:S(2)}) collective-permute-start(bf16[1024,128]{1,0:T(8,128)(2,1)} %get-tuple-element.34), channel_id=1, source_target_pairs={{0,2},{1,3},{2,0},{3,1},{4,6},{5,7},{6,4},{7,5},{8,10},{9,11},{10,... | collective-permute-start | bytes 786440 | tf_op jit(solution)/shard_map/ppermute | solution.py:323
  94.9 20.5 %collective-permute-start.28 = (bf16[1024,128]{1,0:T(8,128)(2,1)}, bf16[1024,128]{1,0:T(8,128)(2,1)S(1)}, u32[]{:S(2)}, u32[]{:S(2)}) collective-permute-start(bf16[1024,128]{1,0:T(8,128)(2,1)} %shard_map.109.refs_0_), channel_id=1, source_target_pairs={{0,1},{1,0},{2,3},{3,2},{4,5},{5,4},{6,7},{7,6},{8,9},{9,8},{10,11... | collective-permute-start | bytes 786440 | tf_op jit(solution)/shard_map/ppermute | solution.py:323
  97.2 5.1 %collective-permute-start.16 = (bf16[512,128]{1,0:T(8,128)(2,1)S(1)}, bf16[512,128]{1,0:T(8,128)(2,1)S(1)}, u32[]{:S(2)}, u32[]{:S(2)}) collective-permute-start(bf16[512,128]{1,0:T(8,128)(2,1)S(1)} %get-tuple-element.61), channel_id=1, source_target_pairs={{0,16},{4,20},{8,24},{12,28},{16,0},{20,4},{24,8},{28,12},{1,17},{... | collective-permute-start | bytes 393224 | tf_op jit(solution)/shard_map/ppermute | solution.py:336
  109.0 13.2 %collective-permute-start.29 = (bf16[1024,128]{1,0:T(8,128)(2,1)}, bf16[1024,128]{1,0:T(8,128)(2,1)S(1)}, u32[]{:S(2)}, u32[]{:S(2)}) collective-permute-start(bf16[1024,128]{1,0:T(8,128)(2,1)} %get-tuple-element.37.refs_2_), channel_id=1, source_target_pairs={{0,1},{1,0},{2,3},{3,2},{4,5},{5,4},{6,7},{7,6},{8,9},{9,8},{10,11... | collective-permute-start | bytes 786440 | tf_op jit(solution)/shard_map/ppermute | solution.py:323
  109.8 15.5 %collective-permute-start.26 = (bf16[1024,128]{1,0:T(8,128)(2,1)}, bf16[1024,128]{1,0:T(8,128)(2,1)S(1)}, u32[]{:S(2)}, u32[]{:S(2)}) collective-permute-start(bf16[1024,128]{1,0:T(8,128)(2,1)} %get-tuple-element.35.refs_0_), channel_id=1, source_target_pairs={{0,2},{1,3},{2,0},{3,1},{4,6},{5,7},{6,4},{7,5},{8,10},{9,11},{10,... | collective-permute-start | bytes 786440 | tf_op jit(solution)/shard_map/ppermute | solution.py:323
  113.1 19.0 %collective-permute-start.32 = (bf16[1,448,512]{2,1,0:T(8,128)(2,1)S(1)}, bf16[1,448,512]{2,1,0:T(8,128)(2,1)S(1)}, u32[]{:S(2)}, u32[]{:S(2)}) collective-permute-start(bf16[1,448,512]{2,1,0:T(8,128)(2,1)S(1)} %get-tuple-element.47), channel_id=1, source_target_pairs={{0,24},{4,28},{8,16},{12,20},{16,8},{20,12},{24,0},{28,4},{1,25},{... | collective-permute-start | bytes 1376264 | tf_op jit(solution)/shard_map/ppermute | solution.py:336
  114.6 21.1 %collective-permute-start.31 = (bf16[1,448,512]{2,1,0:T(8,128)(2,1)S(1)}, bf16[1,448,512]{2,1,0:T(8,128)(2,1)S(1)}, u32[]{:S(2)}, u32[]{:S(2)}) collective-permute-start(bf16[1,448,512]{2,1,0:T(8,128)(2,1)S(1)} %get-tuple-element.48), channel_id=1, source_target_pairs={{0,16},{4,20},{8,24},{12,28},{16,0},{20,4},{24,8},{28,12},{1,17},{... | collective-permute-start | bytes 1376264 | tf_op jit(solution)/shard_map/ppermute | solution.py:336
  115.4 20.3 %collective-permute-start.30 = (bf16[1,448,512]{2,1,0:T(8,128)(2,1)S(1)}, bf16[1,448,512]{2,1,0:T(8,128)(2,1)S(1)}, u32[]{:S(2)}, u32[]{:S(2)}) collective-permute-start(bf16[1,448,512]{2,1,0:T(8,128)(2,1)S(1)} %copy-done.1), channel_id=1, source_target_pairs={{0,8},{4,12},{8,0},{12,4},{16,24},{20,28},{24,16},{28,20},{1,9},{5... | collective-permute-start | bytes 1376264 | tf_op jit(solution)/shard_map/ppermute | solution.py:336
  122.2 9.9 %collective-permute-start.25 = (bf16[1024,128]{1,0:T(8,128)(2,1)}, bf16[1024,128]{1,0:T(8,128)(2,1)S(1)}, u32[]{:S(2)}, u32[]{:S(2)}) collective-permute-start(bf16[1024,128]{1,0:T(8,128)(2,1)} %get-tuple-element.35.refs_0_), channel_id=1, source_target_pairs={{0,1},{1,0},{2,3},{3,2},{4,5},{5,4},{6,7},{7,6},{8,9},{9,8},{10,11... | collective-permute-start | bytes 786440 | tf_op jit(solution)/shard_map/ppermute | solution.py:323
  125.3 14.1 %collective-permute-start.27 = (bf16[1024,128]{1,0:T(8,128)(2,1)S(1)}, bf16[1024,128]{1,0:T(8,128)(2,1)S(1)}, u32[]{:S(2)}, u32[]{:S(2)}) collective-permute-start(bf16[1024,128]{1,0:T(8,128)(2,1)S(1)} %collective-permute-done.26.refs_2_.refs_5_), channel_id=1, source_target_pairs={{0,1},{1,0},{2,3},{3,2},{4,5},{5,4},{6,7},{7,6},{8,9},{9,8},{10,11... | collective-permute-start | bytes 786440 | tf_op jit(solution)/shard_map/ppermute | solution.py:323
  (40 other events, 216.1 us)

commit v12 on v10

--- a/solution.py
+++ b/solution.py
@@ -59,20 +59,53 @@
     return row_index - seg_start
 
 
-def rope_tables(places, head_size):
-    angles = places.astype(jnp.float32)[:, None] * yarn_frequencies(head_size)[None, :]
+def rope_kernel(at_ref, dest_ref, places_ref, freq_ref, key_ref, *refs):
+    cos_ref, sin_ref, turned_ref, own_ref = refs
     factor = 0.1 * math.log(yarn_factor) + 1.0
-    cosine = jnp.cos(angles) * factor
-    sine = jnp.sin(angles) * factor
-    return (
-        jnp.concatenate([cosine, cosine], axis=1),
-        jnp.concatenate([-sine, sine], axis=1),
-    )
-
-
-def swap_halves(values):
-    half = values.shape[-1] // 2
-    return jnp.concatenate([values[..., half:], values[..., :half]], axis=-1)
+    half = lax.broadcasted_iota(jnp.int32, (ROWBLK, HD), 1) < HD // 2
+    for block in range(own_ref.shape[0]):
+        rows = pl.ds(block * ROWBLK, ROWBLK)
+        place = places_ref[pl.ds(dest_ref[block], 1), :]
+        own_ref[pl.ds(block, 1), :] = place
+        spread_out = jnp.broadcast_to(place.astype(jnp.float32), (ROWBLK, HD)).T
+        angles = spread_out * freq_ref[...]
+        cosine = jnp.cos(angles) * factor
+        sine = jnp.sin(angles) * factor
+        sine = jnp.where(half, -sine, sine)
+        cos_ref[rows, :] = cosine
+        sin_ref[rows, :] = sine
+        raw = key_ref[rows, :].astype(jnp.float32)
+        turned = raw * cosine + pltpu.roll(raw, HD // 2, 1) * sine
+        turned_ref[rows, :] = turned.astype(turned_ref.dtype)
+
+
+def rope(kv_head, dest, places_all, key):
+    rows = key.shape[0]
+    blocks = rows // ROWBLK
+    freq = yarn_frequencies(HD)
+    freq = jnp.concatenate([freq, freq]).reshape(1, HD)
+    whole = lambda shape: pl.BlockSpec(shape, lambda step, *refs: (0,) * len(shape))
+    table = jax.ShapeDtypeStruct((rows, HD), jnp.float32)
+    return pl.pallas_call(
+        rope_kernel,
+        grid_spec=pltpu.PrefetchScalarGridSpec(
+            num_scalar_prefetch=2,
+            grid=(1,),
+            in_specs=[
+                whole(places_all.shape),
+                whole((1, HD)),
+                pl.BlockSpec((rows, HD), lambda step, at_ref, dest_ref: (0, at_ref[0])),
+            ],
+            out_specs=[whole((rows, HD))] * 3 + [whole((blocks, ROWBLK))],
+        ),
+        out_shape=[
+            table,
+            table,
+            jax.ShapeDtypeStruct((rows, HD), key.dtype),
+            jax.ShapeDtypeStruct((blocks, ROWBLK), jnp.int32),
+        ],
+        cost_estimate=NO_COST,
+    )(kv_head.reshape(1), dest, places_all, freq, key)
 
 
 NT = (((1,), (1,)), ((), ()))
@@ -545,7 +578,6 @@
     group = HEADS // KV
     bits = [1 << at for at in range(rank_count.bit_length() - 1)]
     kv_head = my_lane * local_heads // group
-    own_key = lax.dynamic_slice_in_dim(key, kv_head * HD, HD, 1)
     own_value = lax.dynamic_slice_in_dim(value, kv_head * HD, HD, 1)
     own_places = positions_of(segments).reshape(1, block_count, ROWBLK)
     places_all = lax.all_to_all(
@@ -564,11 +596,8 @@
     )
     run = dest // RUN_BLOCKS
     slot = dest % RUN_BLOCKS
-    places = jnp.take(places_all, dest, axis=0)
+    cosine, sine, rot_key, places = rope(kv_head, dest, places_all, key)
     need = slot - (slot * ROWBLK - places[:, 0]) // ROWBLK + 1
-    cosine, sine = rope_tables(places.reshape(row_count), HD)
-    key_f = own_key.astype(jnp.float32)
-    rot_key = (key_f * cosine + swap_halves(key_f) * sine).astype(jnp.bfloat16)
     keys = spread(rot_key)
     up, up_t, turned = prepare(grad_out, out_weight, query, cosine, sine, [rot_key])
 
@@ -601,10 +630,12 @@
     weight_received = exchange(weight_sends)
     value_near = hold(value_near, weight_sends[:1])
     grad_query = turn_back(grad_query_t, cosine, sine, weight_sends[:1])
-    key_partial, value_far = final_sum(
-        key_keep, key_received, (cosine, sine), [grad_query], thru=[value_far]
-    )
-    value_all = assemble(my_lane, lane_pieces({0: value_near, far: value_far}, far // 2))
+    value_far = hold(value_far, [grad_query])
+    value_pieces = lane_pieces({0: value_near, far: value_far}, far // 2)
+    value_all = assemble(my_lane, value_pieces)
+    (key_partial,) = final_sum(
+        key_keep, key_received, (cosine, sine), [grad_query, value_pieces[1]]
+    )
     key_pieces = lane_pieces({0: key_partial}, far)
     key_all = assemble(my_lane, key_pieces)
     weight_grad = weight_final(

time: 143 us -> 143 us (level); the launches traced: 141 us -> 144 us
  Pallas kernels: 53.7 us -> 60.4 us
  other arithmetic: 16.1 us -> 11.6 us
    pallas_call x0 -> x1, Pallas kernels: none -> 4.81 us  [rope(): pl.pallas_call(rope_kernel, grid_spec=pltpu.PrefetchScalarGridSpec(num_sc...]
    convert_element_type x3 -> x0, other arithmetic: 3.47 us -> none  [the longest x1 2.41 us: local(): rot_key = (key_f * cosine + swap_halves(key_f) * sine).astype(jnp.bfloat16)]
    neg x1 -> x0, other arithmetic: 1.93 us -> none  [rope_tables(): -sine]
    pallas_call x1, Pallas kernels: 18.7 us -> 20.5 us  [attend(): pl.pallas_call(partial(attend_kernel, heads, ranks), out_shape=(jax.Shape...]
    unnamed x76 -> x78, local copies, waits for them, and re-layouts: 5.08 us -> 6.39 us
  transfers between devices with their start and end apart: 33 -> 33, of which waited for: 14 -> 12; matrix products, arithmetic and copies ran while one was open for 13% -> 9% of each run, Pallas kernels for 22% -> 25%
where the time goes in v12:
time: 143 us; the launch traced here: 144 us
  Pallas kernels  60.4 us (42%)
  starting transfers between devices  34.4 us (24%)
  waiting for transfers between devices  28.6 us (20%)
  other arithmetic  11.6 us (8%)
  local copies, waits for them, and re-layouts  7.35 us (5%)
    ppermute x26, starting transfers between devices, swap(): lax.ppermute(array, 'dp', [(rank, rank ^ bit) for rank in range(ranks)])  21.4 us
    pallas_call x1, Pallas kernels, attend(): pl.pallas_call(partial(attend_kernel, heads, ranks), out_shape=(jax.Shape...  20.5 us
    ppermute x26, waiting for transfers between devices, swap(): lax.ppermute(array, 'dp', [(rank, rank ^ bit) for rank in range(ranks)])  14.1 us
    ppermute x6, waiting for transfers between devices, lane_swap(): lax.ppermute(array, 'tensor', [(lane, lane ^ bit) for lane in range(lanes)])  12.7 us
    pallas_call x1, Pallas kernels, product(): pl.pallas_call(product_kernel, grid_spec=pltpu.PrefetchScalarGridSpec(num...  9.53 us
    pallas_call x1, Pallas kernels, prepare(): pl.pallas_call(prepare_kernel, grid=(steps,), out_shape=[jax.ShapeDtypeSt...  9.22 us
    ppermute x6, starting transfers between devices, lane_swap(): lax.ppermute(array, 'tensor', [(lane, lane ^ bit) for lane in range(lanes)])  8.76 us
    unnamed x78, local copies, waits for them, and re-layouts  6.39 us
  transfers between devices with their start and end apart: 33, of which 12 were waited for; matrix products, arithmetic and copies ran while one was open for 9% of the time, Pallas kernels for 25%

profile of v12, /device:TPU:0, one launch (start us, length us, event | category | flops | bytes accessed | tf_op | source)
XLA Modules:
  0.0 143.5 jit_solution(10263245303826772543)
XLA Ops:
  1.9 4.0 %collective-permute-start.12 = (bf16[1024,128]{1,0:T(8,128)(2,1)S(1)}, bf16[1024,128]{1,0:T(8,128)(2,1)S(1)}, u32[]{:S(2)}, u32[]{:S(2)}) collective-permute-start(bf16[1024,128]{1,0:T(8,128)(2,1)S(1)} %constant_dynamic-slice_fusion.refs_8_), channel_id=1, source_target_pairs={{0,24},{4,28},{8,16},{12,20},{16,8},{20,12},{24,0},{28,4},{1,25},{... | collective-permute-start | bytes 786440 | tf_op jit(solution)/shard_map/ppermute | solution.py:348
  8.6 4.2 %all-to-all-start = ((s32[8,8,128]{2,1,0:T(8,128)}), s32[8,8,128]{2,1,0:T(8,128)S(1)}, u32[]{:S(2)}, u32[]{:S(2)}) async-start(s32[8,8,128]{2,1,0:T(8,128)} %broadcast_in_dim.27), calls=%async_computation | async-start | bytes 65536 | tf_op jit(solution)/shard_map/all_to_all | solution.py:583
  12.9 1.3 multiply_add_fusion.2
  14.6 1.3 select_reduce_fusion.dest_ref
  16.6 1.8 %all-to-all-done = s32[8,8,128]{2,1,0:T(8,128)S(1)} async-done(((s32[8,8,128]{2,1,0:T(8,128)}), s32[8,8,128]{2,1,0:T(8,128)S(1)}, u32[]{:S(2)}, u32[]{:S(2)}) %all-to-all-start) | async-done | bytes 32800 | tf_op jit(solution)/shard_map/all_to_all | solution.py:583
  19.0 4.8 %shard_map.102 = (f32[1024,128]{1,0:T(8,128)}, f32[1024,128]{1,0:T(8,128)}, bf16[1024,128]{1,0:T(8,128)(2,1)}, s32[8,128]{1,0:T(8,128)}) custom-call(s32[1]{0:T(128)} %bitcast.at_ref, s32[8]{0:T(128)} %select_reduce_fusion.dest_ref, s32[64,128]{1,0:T(8,128)} %bitcast.11, f32[1,128]{1,0:T(1,128)} %maximum_bitcast_fusion.freq_ref, bf16[1024,512]{1,0:T(8,128)(2,1)} %key_ref.1), custom_call_target="tpu_custom_call" | custom-call | tf_op jit(solution)/shard_map/pallas_call | solution.py:89
  23.8 2.4 %collective-permute-start.5 = (bf16[1024,128]{1,0:T(8,128)(2,1)}, bf16[1024,128]{1,0:T(8,128)(2,1)S(1)}, u32[]{:S(2)}, u32[]{:S(2)}) collective-permute-start(bf16[1024,128]{1,0:T(8,128)(2,1)} %get-tuple-element.26.refs_0_), channel_id=1, source_target_pairs={{0,24},{4,28},{8,16},{12,20},{16,8},{20,12},{24,0},{28,4},{1,25},{... | collective-permute-start | bytes 786440 | tf_op jit(solution)/shard_map/ppermute | solution.py:348
  27.8 9.2 %shard_map.103 = (bf16[1024,512]{1,0:T(8,128)(2,1)}, bf16[512,1024]{1,0:T(8,128)(2,1)}, bf16[1024,512]{1,0:T(8,128)(2,1)}) custom-call(bf16[1024,3584]{1,0:T(8,128)(2,1)} %right_ref.1, bf16[3584,512]{1,0:T(8,128)(2,1)} %weight_ref.1, bf16[1024,512]{1,0:T(8,128)(2,1)} %query_ref.1, f32[1024,128]{1,0:T(8,128)} %get-tuple-element.24.cos_ref.refs_4_, ...), custom_call_target="tpu_custom_call" | custom-call | flops 3758096384 | bytes 7340032 | tf_op jit(solution)/shard_map/pallas_call | solution.py:426
  37.3 1.5 %collective-permute-done.3.refs_4_ = bf16[1024,128]{1,0:T(8,128)(2,1)S(1)} collective-permute-done((bf16[1024,128]{1,0:T(8,128)(2,1)}, bf16[1024,128]{1,0:T(8,128)(2,1)S(1)}, u32[]{:S(2)}, u32[]{:S(2)}) %collective-permute-start.3) | collective-permute-done | bytes 262176 | tf_op jit(solution)/shard_map/ppermute | solution.py:348
  42.1 20.5 %shard_map.104 = (f32[512,1024]{1,0:T(8,128)}, bf16[512,1024]{1,0:T(8,128)(2,1)}, bf16[4096,128]{1,0:T(8,128)(2,1)}, bf16[4096,128]{1,0:T(8,128)(2,1)}, bf16[409...) custom-call(s32[64]{0:T(128)} %multiply_add_fusion.3.target_ref, s32[64]{0:T(128)} %get-tuple-element.44.source_ref, ...), custom_call_target="tpu_custom_call" | custom-call | tf_op jit(solution)/shard_map/pallas_call | solution.py:281
  63.8 2.6 %collective-permute-done.14 = bf16[4096,128]{1,0:T(8,128)(2,1)} collective-permute-done((bf16[4096,128]{1,0:T(8,128)(2,1)}, bf16[4096,128]{1,0:T(8,128)(2,1)}, u32[]{:S(2)}, u32[]{:S(2)}) %collective-permute-start.14) | collective-permute-done | bytes 1048608 | tf_op jit(solution)/shard_map/ppermute | solution.py:348
  66.4 2.6 %add_convert_fusion.5 = (bf16[1024,128]{1,0:T(8,128)(2,1)}, bf16[1024,128]{1,0:T(8,128)(2,1)}, f32[1024,128]{1,0:T(8,128)}, bf16[1024,128]{1,0:T(8,128)(2,1)S(1)}) fusion(bf16[4096,128]{1,0:T(8,128)(2,1)} %collective-permute-done.14, bf16[4096,128]{1,0:T(8,128)(2,1)} %get-tuple-element.32), kind=kLoop, calls=%fused_computation.7 | loop fusion | flops 1966080 | bytes 3407872 | tf_op jit(solution)/shard_map/convert_element_type | solution.py:370
  69.0 2.7 %collective-permute-start.17 = (bf16[1024,128]{1,0:T(8,128)(2,1)}, bf16[1024,128]{1,0:T(8,128)(2,1)S(1)}, u32[]{:S(2)}, u32[]{:S(2)}) collective-permute-start(bf16[1024,128]{1,0:T(8,128)(2,1)} %get-tuple-element.56), channel_id=1, source_target_pairs={{0,16},{4,20},{8,24},{12,28},{16,0},{20,4},{24,8},{28,12},{1,17},{... | collective-permute-start | bytes 786440 | tf_op jit(solution)/shard_map/ppermute | solution.py:348
  71.7 1.4 collective-permute-start.16
  73.1 1.3 add_convert_fusion.3
  74.4 9.5 %shard_map.105 = (bf16[4,448,512]{2,1,0:T(8,128)(2,1)}, bf16[4,448,512]{2,1,0:T(8,128)(2,1)}, f32[1024,128]{1,0:T(8,128)}) custom-call(s32[2]{0:T(128)} %pad_add_fusion.my_ref, bf16[512,1024]{1,0:T(8,128)(2,1)} %get-tuple-element.31.left_ref, bf16[1024,3584]{1,0:T(8,128)(2,1)} %right_ref.1, ...), custom_call_target="tpu_custom_call", output_to_operand_aliasing={{2}: (5, {})} | custom-call | tf_op jit(solution)/shard_map/pallas_call | solution.py:532
  84.1 1.2 collective-permute-done.16.refs_1_
  86.0 2.2 %shard_map.106 = (bf16[1024,128]{1,0:T(8,128)(2,1)}, bf16[1024,128]{1,0:T(8,128)(2,1)}, bf16[4,448,512]{2,1,0:T(8,128)(2,1)}) custom-call(f32[1024,128]{1,0:T(8,128)} %get-tuple-element.37.refs_0_, bf16[1024,128]{1,0:T(8,128)(2,1)} %copy-done.31, bf16[1024,128]{1,0:T(8,128)(2,1)} %copy-done.30, ...), custom_call_target="tpu_custom_call", output_to_operand_aliasing={{2}: (4, {})} | custom-call | tf_op jit(solution)/shard_map/pallas_call | solution.py:392
  88.5 2.1 %collective-permute-start.22 = (bf16[1024,128]{1,0:T(8,128)(2,1)}, bf16[1024,128]{1,0:T(8,128)(2,1)S(1)}, u32[]{:S(2)}, u32[]{:S(2)}) collective-permute-start(bf16[1024,128]{1,0:T(8,128)(2,1)} %get-tuple-element.51), channel_id=1, source_target_pairs={{0,24},{4,28},{8,16},{12,20},{16,8},{20,12},{24,0},{28,4},{1,25},{... | collective-permute-start | bytes 786440 | tf_op jit(solution)/shard_map/ppermute | solution.py:348
  91.7 2.6 %collective-permute-start.27 = (bf16[1024,128]{1,0:T(8,128)(2,1)}, bf16[1024,128]{1,0:T(8,128)(2,1)S(1)}, u32[]{:S(2)}, u32[]{:S(2)}) collective-permute-start(bf16[1024,128]{1,0:T(8,128)(2,1)} %get-tuple-element.41), channel_id=1, source_target_pairs={{0,2},{1,3},{2,0},{3,1},{4,6},{5,7},{6,4},{7,5},{8,10},{9,11},{10,... | collective-permute-start | bytes 786440 | tf_op jit(solution)/shard_map/ppermute | solution.py:335
  94.3 1.6 %add_convert_fusion = (bf16[1,448,512]{2,1,0:T(8,128)(2,1)S(1)}, bf16[1,448,512]{2,1,0:T(8,128)(2,1)S(1)}, f32[1,448,512]{2,1,0:T(8,128)}, bf16[1,448,512]{2,1,0:T(8,128)(2,1)}) fusion(bf16[4,448,512]{2,1,0:T(8,128)(2,1)S(1)} %collective-permute-done.19, bf16[4,448,512]{2,1,0:T(8,128)(2,1)S(1)} %copy-done.2), kind=kLoop, calls=%fused_computation | loop fusion | flops 3440640 | bytes 5963776 | tf_op jit(solution)/shard_map/convert_element_type | solution.py:370
  95.9 1.6 %collective-permute-start.23 = (bf16[1024,128]{1,0:T(8,128)(2,1)}, bf16[1024,128]{1,0:T(8,128)(2,1)S(1)}, u32[]{:S(2)}, u32[]{:S(2)}) collective-permute-start(bf16[1024,128]{1,0:T(8,128)(2,1)} %shard_map.108.refs_0_), channel_id=1, source_target_pairs={{0,1},{1,0},{2,3},{3,2},{4,5},{5,4},{6,7},{7,6},{8,9},{9,8},{10,11... | collective-permute-start | bytes 786440 | tf_op jit(solution)/shard_map/ppermute | solution.py:335
  97.5 4.4 %shard_map.107.refs_6_.refs_1_ = bf16[1024,512]{1,0:T(8,128)(2,1)} custom-call(f32[512,1024]{1,0:T(8,128)} %get-tuple-element.30.grad_ref, f32[1024,128]{1,0:T(8,128)} %get-tuple-element.24.cos_ref.refs_4_, f32[1024,128]{1,0:T(8,128)} %get-tuple-element.25.sin_ref.refs_5_, bf16[1,448,512]{2,1,0:T(8,128)(2,1)} %get-tuple-element.50.refs_0_.refs_1_), custom_call_target="tpu_custom_call" | custom-call | tf_op jit(solution)/shard_map/pallas_call | solution.py:467
  101.9 4.4 %collective-permute-done.27.refs_0_ = bf16[1024,128]{1,0:T(8,128)(2,1)S(1)} collective-permute-done((bf16[1024,128]{1,0:T(8,128)(2,1)}, bf16[1024,128]{1,0:T(8,128)(2,1)S(1)}, u32[]{:S(2)}, u32[]{:S(2)}) %collective-permute-start.27) | collective-permute-done | bytes 262176 | tf_op jit(solution)/shard_map/ppermute | solution.py:335
  108.9 2.6 %shard_map.109.refs_0_ = bf16[1024,128]{1,0:T(8,128)(2,1)} custom-call(f32[1024,128]{1,0:T(8,128)} %get-tuple-element.53.refs_0_, bf16[1024,128]{1,0:T(8,128)(2,1)} %copy-done.34, bf16[1024,128]{1,0:T(8,128)(2,1)} %collective-permute-done.21.refs_2_, bf16[1024,128]{1,0:T(8,128)(2,1)} %copy-done.35, f32[1024,128]{1,0:T(8,128)} %get-tuple-element.24.cos_ref.refs_4_, ...), custom_call_target="tpu_custom_call" | custom-call | tf_op jit(solution)/shard_map/pallas_call | solution.py:392
  111.5 3.2 %collective-permute-start.25 = (bf16[1024,128]{1,0:T(8,128)(2,1)}, bf16[1024,128]{1,0:T(8,128)(2,1)S(1)}, u32[]{:S(2)}, u32[]{:S(2)}) collective-permute-start(bf16[1024,128]{1,0:T(8,128)(2,1)} %shard_map.109.refs_0_), channel_id=1, source_target_pairs={{0,2},{1,3},{2,0},{3,1},{4,6},{5,7},{6,4},{7,5},{8,10},{9,11},{10,... | collective-permute-start | bytes 786440 | tf_op jit(solution)/shard_map/ppermute | solution.py:335
  116.4 1.7 %collective-permute-start.29 = (bf16[1,448,512]{2,1,0:T(8,128)(2,1)S(1)}, bf16[1,448,512]{2,1,0:T(8,128)(2,1)S(1)}, u32[]{:S(2)}, u32[]{:S(2)}) collective-permute-start(bf16[1,448,512]{2,1,0:T(8,128)(2,1)S(1)} %copy-done.1), channel_id=1, source_target_pairs={{0,8},{4,12},{8,0},{12,4},{16,24},{20,28},{24,16},{28,20},{1,9},{5... | collective-permute-start | bytes 1376264 | tf_op jit(solution)/shard_map/ppermute | solution.py:348
  118.8 7.9 %collective-permute-done.25.refs_2_.refs_5_ = bf16[1024,128]{1,0:T(8,128)(2,1)S(1)} collective-permute-done((bf16[1024,128]{1,0:T(8,128)(2,1)}, bf16[1024,128]{1,0:T(8,128)(2,1)S(1)}, u32[]{:S(2)}, u32[]{:S(2)}) %collective-permute-start.25) | collective-permute-done | bytes 262176 | tf_op jit(solution)/shard_map/ppermute | solution.py:335
  126.7 2.3 %shard_map.112.refs_6_ = bf16[1024,512]{1,0:T(8,128)(2,1)} custom-call(s32[1]{0:T(128)} %bitcast.6.my_ref, bf16[1024,128]{1,0:T(8,128)(2,1)} %shard_map.108.refs_0_, bf16[1024,128]{1,0:T(8,128)(2,1)} %copy-done.10, bf16[1024,128]{1,0:T(8,128)(2,1)} %shard_map.111.refs_2_, bf16[1024,128]{1,0:T(8,128)(2,1)} %copy-done.27), custom_call_target="tpu_custom_call" | custom-call | tf_op jit(solution)/shard_map/pallas_call | solution.py:322
  129.0 7.6 %collective-permute-done.30.refs_2_ = bf16[1,448,512]{2,1,0:T(8,128)(2,1)S(1)} collective-permute-done((bf16[1,448,512]{2,1,0:T(8,128)(2,1)S(1)}, bf16[1,448,512]{2,1,0:T(8,128)(2,1)S(1)}, u32[]{:S(2)}, u32[]{:S(2)}) %collective-permute-start.30) | collective-permute-done | bytes 458784 | tf_op jit(solution)/shard_map/ppermute | solution.py:348
  137.7 2.7 %shard_map.113 = f32[448,512]{1,0:T(8,128)} custom-call(f32[1,448,512]{2,1,0:T(8,128)} %get-tuple-element.49.refs_0_, bf16[1,448,512]{2,1,0:T(8,128)(2,1)} %copy-done.13, bf16[1,448,512]{2,1,0:T(8,128)(2,1)} %copy-done.12, bf16[1,448,512]{2,1,0:T(8,128)(2,1)} %copy-done.11, bf16[1024,128]{1,0:T(8,128)(2,1)} %copy-done.4, bf16[1024,128]{1,0:T(8,128)(2,1)} %copy-done.3, ...), custom_call_target="tpu_custom_call" | custom-call | tf_op jit(solution)/shard_map/pallas_call | solution.py:561
  141.1 2.2 %shard_map.110 = bf16[1024,512]{1,0:T(8,128)(2,1)} custom-call(s32[1]{0:T(128)} %bitcast.6.my_ref, bf16[1024,128]{1,0:T(8,128)(2,1)} %shard_map.109.refs_0_, bf16[1024,128]{1,0:T(8,128)(2,1)} %copy-done.4, bf16[1024,128]{1,0:T(8,128)(2,1)} %copy-done.3, bf16[1024,128]{1,0:T(8,128)(2,1)} %copy-done.32), custom_call_target="tpu_custom_call" | custom-call | tf_op jit(solution)/shard_map/pallas_call | solution.py:322
  (145 shorter events, 21.0 us)
Async XLA Ops:
  1.9 24.3 %collective-permute-start.12 = (bf16[1024,128]{1,0:T(8,128)(2,1)S(1)}, bf16[1024,128]{1,0:T(8,128)(2,1)S(1)}, u32[]{:S(2)}, u32[]{:S(2)}) collective-permute-start(bf16[1024,128]{1,0:T(8,128)(2,1)S(1)} %constant_dynamic-slice_fusion.refs_8_), channel_id=1, source_target_pairs={{0,24},{4,28},{8,16},{12,20},{16,8},{20,12},{24,0},{28,4},{1,25},{... | collective-permute-start | bytes 786440 | tf_op jit(solution)/shard_map/ppermute | solution.py:348
  5.9 21.0 %collective-permute-start.10 = (bf16[1024,128]{1,0:T(8,128)(2,1)S(1)}, bf16[1024,128]{1,0:T(8,128)(2,1)S(1)}, u32[]{:S(2)}, u32[]{:S(2)}) collective-permute-start(bf16[1024,128]{1,0:T(8,128)(2,1)S(1)} %constant_dynamic-slice_fusion.refs_8_), channel_id=1, source_target_pairs={{0,16},{4,20},{8,24},{12,28},{16,0},{20,4},{24,8},{28,12},{1,17},{... | collective-permute-start | bytes 786440 | tf_op jit(solution)/shard_map/ppermute | solution.py:348
  6.4 20.9 %collective-permute-start.8 = (bf16[1024,128]{1,0:T(8,128)(2,1)S(1)}, bf16[1024,128]{1,0:T(8,128)(2,1)S(1)}, u32[]{:S(2)}, u32[]{:S(2)}) collective-permute-start(bf16[1024,128]{1,0:T(8,128)(2,1)S(1)} %constant_dynamic-slice_fusion.refs_8_), channel_id=1, source_target_pairs={{0,8},{4,12},{8,0},{12,4},{16,24},{20,28},{24,16},{28,20},{1,9},{5... | collective-permute-start | bytes 786440 | tf_op jit(solution)/shard_map/ppermute | solution.py:348
  6.5 20.8 %collective-permute-start.7 = (bf16[1024,128]{1,0:T(8,128)(2,1)S(1)}, bf16[1024,128]{1,0:T(8,128)(2,1)S(1)}, u32[]{:S(2)}, u32[]{:S(2)}) collective-permute-start(bf16[1024,128]{1,0:T(8,128)(2,1)S(1)} %constant_dynamic-slice_fusion.refs_8_), channel_id=1, source_target_pairs={{0,4},{4,0},{8,12},{12,8},{16,20},{20,16},{24,28},{28,24},{1,5},{5... | collective-permute-start | bytes 786440 | tf_op jit(solution)/shard_map/ppermute | solution.py:348
  8.6 9.8 %all-to-all-start = ((s32[8,8,128]{2,1,0:T(8,128)}), s32[8,8,128]{2,1,0:T(8,128)S(1)}, u32[]{:S(2)}, u32[]{:S(2)}) async-start(s32[8,8,128]{2,1,0:T(8,128)} %broadcast_in_dim.27), calls=%async_computation | async-start | bytes 65536 | tf_op jit(solution)/shard_map/all_to_all | solution.py:583
  23.8 13.3 %collective-permute-start.5 = (bf16[1024,128]{1,0:T(8,128)(2,1)}, bf16[1024,128]{1,0:T(8,128)(2,1)S(1)}, u32[]{:S(2)}, u32[]{:S(2)}) collective-permute-start(bf16[1024,128]{1,0:T(8,128)(2,1)} %get-tuple-element.26.refs_0_), channel_id=1, source_target_pairs={{0,24},{4,28},{8,16},{12,20},{16,8},{20,12},{24,0},{28,4},{1,25},{... | collective-permute-start | bytes 786440 | tf_op jit(solution)/shard_map/ppermute | solution.py:348
  26.2 12.5 %collective-permute-start.3 = (bf16[1024,128]{1,0:T(8,128)(2,1)}, bf16[1024,128]{1,0:T(8,128)(2,1)S(1)}, u32[]{:S(2)}, u32[]{:S(2)}) collective-permute-start(bf16[1024,128]{1,0:T(8,128)(2,1)} %get-tuple-element.26.refs_0_), channel_id=1, source_target_pairs={{0,16},{4,20},{8,24},{12,28},{16,0},{20,4},{24,8},{28,12},{1,17},{... | collective-permute-start | bytes 786440 | tf_op jit(solution)/shard_map/ppermute | solution.py:348
  26.8 12.0 %collective-permute-start.1 = (bf16[1024,128]{1,0:T(8,128)(2,1)}, bf16[1024,128]{1,0:T(8,128)(2,1)S(1)}, u32[]{:S(2)}, u32[]{:S(2)}) collective-permute-start(bf16[1024,128]{1,0:T(8,128)(2,1)} %get-tuple-element.26.refs_0_), channel_id=1, source_target_pairs={{0,8},{4,12},{8,0},{12,4},{16,24},{20,28},{24,16},{28,20},{1,9},{5... | collective-permute-start | bytes 786440 | tf_op jit(solution)/shard_map/ppermute | solution.py:348
  27.3 11.9 %collective-permute-start = (bf16[1024,128]{1,0:T(8,128)(2,1)}, bf16[1024,128]{1,0:T(8,128)(2,1)S(1)}, u32[]{:S(2)}, u32[]{:S(2)}) collective-permute-start(bf16[1024,128]{1,0:T(8,128)(2,1)} %get-tuple-element.26.refs_0_), channel_id=1, source_target_pairs={{0,4},{4,0},{8,12},{12,8},{16,20},{20,16},{24,28},{28,24},{1,5},{5... | collective-permute-start | bytes 786440 | tf_op jit(solution)/shard_map/ppermute | solution.py:348
  27.3 12.0 %collective-permute-start.13 = (bf16[1024,128]{1,0:T(8,128)(2,1)S(1)}, bf16[1024,128]{1,0:T(8,128)(2,1)S(1)}, u32[]{:S(2)}, u32[]{:S(2)}) collective-permute-start(bf16[1024,128]{1,0:T(8,128)(2,1)S(1)} %collective-permute-done.12.refs_14_), channel_id=1, source_target_pairs={{0,4},{4,0},{8,12},{12,8},{16,20},{20,16},{24,28},{28,24},{1,5},{5... | collective-permute-start | bytes 786440 | tf_op jit(solution)/shard_map/ppermute | solution.py:348
  37.1 3.3 %collective-permute-start.11 = (bf16[1024,128]{1,0:T(8,128)(2,1)S(1)}, bf16[1024,128]{1,0:T(8,128)(2,1)S(1)}, u32[]{:S(2)}, u32[]{:S(2)}) collective-permute-start(bf16[1024,128]{1,0:T(8,128)(2,1)S(1)} %collective-permute-done.10.refs_12_), channel_id=1, source_target_pairs={{0,4},{4,0},{8,12},{12,8},{16,20},{20,16},{24,28},{28,24},{1,5},{5... | collective-permute-start | bytes 786440 | tf_op jit(solution)/shard_map/ppermute | solution.py:348
  38.8 1.9 %collective-permute-start.6 = (bf16[1024,128]{1,0:T(8,128)(2,1)S(1)}, bf16[1024,128]{1,0:T(8,128)(2,1)S(1)}, u32[]{:S(2)}, u32[]{:S(2)}) collective-permute-start(bf16[1024,128]{1,0:T(8,128)(2,1)S(1)} %collective-permute-done.5.refs_6_), channel_id=1, source_target_pairs={{0,4},{4,0},{8,12},{12,8},{16,20},{20,16},{24,28},{28,24},{1,5},{5... | collective-permute-start | bytes 786440 | tf_op jit(solution)/shard_map/ppermute | solution.py:348
  39.3 1.8 %collective-permute-start.4 = (bf16[1024,128]{1,0:T(8,128)(2,1)S(1)}, bf16[1024,128]{1,0:T(8,128)(2,1)S(1)}, u32[]{:S(2)}, u32[]{:S(2)}) collective-permute-start(bf16[1024,128]{1,0:T(8,128)(2,1)S(1)} %collective-permute-done.3.refs_4_), channel_id=1, source_target_pairs={{0,4},{4,0},{8,12},{12,8},{16,20},{20,16},{24,28},{28,24},{1,5},{5... | collective-permute-start | bytes 786440 | tf_op jit(solution)/shard_map/ppermute | solution.py:348
  39.4 2.0 %collective-permute-start.2 = (bf16[1024,128]{1,0:T(8,128)(2,1)S(1)}, bf16[1024,128]{1,0:T(8,128)(2,1)S(1)}, u32[]{:S(2)}, u32[]{:S(2)}) collective-permute-start(bf16[1024,128]{1,0:T(8,128)(2,1)S(1)} %collective-permute-done.1.refs_2_), channel_id=1, source_target_pairs={{0,4},{4,0},{8,12},{12,8},{16,20},{20,16},{24,28},{28,24},{1,5},{5... | collective-permute-start | bytes 786440 | tf_op jit(solution)/shard_map/ppermute | solution.py:348
  62.6 3.8 %collective-permute-start.14 = (bf16[4096,128]{1,0:T(8,128)(2,1)}, bf16[4096,128]{1,0:T(8,128)(2,1)}, u32[]{:S(2)}, u32[]{:S(2)}) collective-permute-start(bf16[4096,128]{1,0:T(8,128)(2,1)} %get-tuple-element.33), channel_id=1, source_target_pairs={{0,4},{4,0},{8,12},{12,8},{16,20},{20,16},{24,28},{28,24},{1,5},{5... | collective-permute-start | bytes 3145736 | tf_op jit(solution)/shard_map/ppermute | solution.py:348
  62.7 10.4 %collective-permute-start.15 = (bf16[4096,128]{1,0:T(8,128)(2,1)}, bf16[4096,128]{1,0:T(8,128)(2,1)S(1)}, u32[]{:S(2)}, u32[]{:S(2)}) collective-permute-start(bf16[4096,128]{1,0:T(8,128)(2,1)} %get-tuple-element.35), channel_id=1, source_target_pairs={{0,4},{4,0},{8,12},{12,8},{16,20},{20,16},{24,28},{28,24},{1,5},{5... | collective-permute-start | bytes 3145736 | tf_op jit(solution)/shard_map/ppermute | solution.py:348
  69.0 14.9 %collective-permute-start.18 = (bf16[1024,128]{1,0:T(8,128)(2,1)}, bf16[1024,128]{1,0:T(8,128)(2,1)S(1)}, u32[]{:S(2)}, u32[]{:S(2)}) collective-permute-start(bf16[1024,128]{1,0:T(8,128)(2,1)} %get-tuple-element.55), channel_id=1, source_target_pairs={{0,24},{4,28},{8,16},{12,20},{16,8},{20,12},{24,0},{28,4},{1,25},{... | collective-permute-start | bytes 786440 | tf_op jit(solution)/shard_map/ppermute | solution.py:348
  69.0 15.1 %collective-permute-start.17 = (bf16[1024,128]{1,0:T(8,128)(2,1)}, bf16[1024,128]{1,0:T(8,128)(2,1)S(1)}, u32[]{:S(2)}, u32[]{:S(2)}) collective-permute-start(bf16[1024,128]{1,0:T(8,128)(2,1)} %get-tuple-element.56), channel_id=1, source_target_pairs={{0,16},{4,20},{8,24},{12,28},{16,0},{20,4},{24,8},{28,12},{1,17},{... | collective-permute-start | bytes 786440 | tf_op jit(solution)/shard_map/ppermute | solution.py:348
  71.7 13.6 %collective-permute-start.16 = (bf16[1024,128]{1,0:T(8,128)(2,1)S(1)}, bf16[1024,128]{1,0:T(8,128)(2,1)S(1)}, u32[]{:S(2)}, u32[]{:S(2)}) collective-permute-start(bf16[1024,128]{1,0:T(8,128)(2,1)S(1)} %get-tuple-element.58.refs_0_), channel_id=1, source_target_pairs={{0,8},{4,12},{8,0},{12,4},{16,24},{20,28},{24,16},{28,20},{1,9},{5... | collective-permute-start | bytes 786440 | tf_op jit(solution)/shard_map/ppermute | solution.py:348
  88.2 6.2 %collective-permute-start.19 = (bf16[4,448,512]{2,1,0:T(8,128)(2,1)}, bf16[4,448,512]{2,1,0:T(8,128)(2,1)S(1)}, u32[]{:S(2)}, u32[]{:S(2)}) collective-permute-start(bf16[4,448,512]{2,1,0:T(8,128)(2,1)} %get-tuple-element.39), channel_id=1, source_target_pairs={{0,4},{4,0},{8,12},{12,8},{16,20},{20,16},{24,28},{28,24},{1,5},{5... | collective-permute-start | bytes 5505032 | tf_op jit(solution)/shard_map/ppermute | solution.py:348
  88.2 19.7 %collective-permute-start.20 = (bf16[1024,128]{1,0:T(8,128)(2,1)S(1)}, bf16[1024,128]{1,0:T(8,128)(2,1)S(1)}, u32[]{:S(2)}, u32[]{:S(2)}) collective-permute-start(bf16[1024,128]{1,0:T(8,128)(2,1)S(1)} %copy-done.8), channel_id=1, source_target_pairs={{0,8},{4,12},{8,0},{12,4},{16,24},{20,28},{24,16},{28,20},{1,9},{5... | collective-permute-start | bytes 786440 | tf_op jit(solution)/shard_map/ppermute | solution.py:348
  88.5 19.3 %collective-permute-start.22 = (bf16[1024,128]{1,0:T(8,128)(2,1)}, bf16[1024,128]{1,0:T(8,128)(2,1)S(1)}, u32[]{:S(2)}, u32[]{:S(2)}) collective-permute-start(bf16[1024,128]{1,0:T(8,128)(2,1)} %get-tuple-element.51), channel_id=1, source_target_pairs={{0,24},{4,28},{8,16},{12,20},{16,8},{20,12},{24,0},{28,4},{1,25},{... | collective-permute-start | bytes 786440 | tf_op jit(solution)/shard_map/ppermute | solution.py:348
  90.6 17.2 %collective-permute-start.21 = (bf16[1024,128]{1,0:T(8,128)(2,1)S(1)}, bf16[1024,128]{1,0:T(8,128)(2,1)}, u32[]{:S(2)}, u32[]{:S(2)}) collective-permute-start(bf16[1024,128]{1,0:T(8,128)(2,1)S(1)} %copy-done.33), channel_id=1, source_target_pairs={{0,16},{4,20},{8,24},{12,28},{16,0},{20,4},{24,8},{28,12},{1,17},{... | collective-permute-start | bytes 786440 | tf_op jit(solution)/shard_map/ppermute | solution.py:348
  91.7 14.7 %collective-permute-start.27 = (bf16[1024,128]{1,0:T(8,128)(2,1)}, bf16[1024,128]{1,0:T(8,128)(2,1)S(1)}, u32[]{:S(2)}, u32[]{:S(2)}) collective-permute-start(bf16[1024,128]{1,0:T(8,128)(2,1)} %get-tuple-element.41), channel_id=1, source_target_pairs={{0,2},{1,3},{2,0},{3,1},{4,6},{5,7},{6,4},{7,5},{8,10},{9,11},{10,... | collective-permute-start | bytes 786440 | tf_op jit(solution)/shard_map/ppermute | solution.py:335
  95.9 12.3 %collective-permute-start.23 = (bf16[1024,128]{1,0:T(8,128)(2,1)}, bf16[1024,128]{1,0:T(8,128)(2,1)S(1)}, u32[]{:S(2)}, u32[]{:S(2)}) collective-permute-start(bf16[1024,128]{1,0:T(8,128)(2,1)} %shard_map.108.refs_0_), channel_id=1, source_target_pairs={{0,1},{1,0},{2,3},{3,2},{4,5},{5,4},{6,7},{7,6},{8,9},{9,8},{10,11... | collective-permute-start | bytes 786440 | tf_op jit(solution)/shard_map/ppermute | solution.py:335
  107.1 11.0 %collective-permute-start.28 = (bf16[1024,128]{1,0:T(8,128)(2,1)}, bf16[1024,128]{1,0:T(8,128)(2,1)S(1)}, u32[]{:S(2)}, u32[]{:S(2)}) collective-permute-start(bf16[1024,128]{1,0:T(8,128)(2,1)} %shard_map.111.refs_2_), channel_id=1, source_target_pairs={{0,1},{1,0},{2,3},{3,2},{4,5},{5,4},{6,7},{7,6},{8,9},{9,8},{10,11... | collective-permute-start | bytes 786440 | tf_op jit(solution)/shard_map/ppermute | solution.py:335
  111.5 15.3 %collective-permute-start.25 = (bf16[1024,128]{1,0:T(8,128)(2,1)}, bf16[1024,128]{1,0:T(8,128)(2,1)S(1)}, u32[]{:S(2)}, u32[]{:S(2)}) collective-permute-start(bf16[1024,128]{1,0:T(8,128)(2,1)} %shard_map.109.refs_0_), channel_id=1, source_target_pairs={{0,2},{1,3},{2,0},{3,1},{4,6},{5,7},{6,4},{7,5},{8,10},{9,11},{10,... | collective-permute-start | bytes 786440 | tf_op jit(solution)/shard_map/ppermute | solution.py:335
  114.6 14.4 %collective-permute-start.31 = (bf16[1,448,512]{2,1,0:T(8,128)(2,1)S(1)}, bf16[1,448,512]{2,1,0:T(8,128)(2,1)S(1)}, u32[]{:S(2)}, u32[]{:S(2)}) collective-permute-start(bf16[1,448,512]{2,1,0:T(8,128)(2,1)S(1)} %get-tuple-element.47), channel_id=1, source_target_pairs={{0,24},{4,28},{8,16},{12,20},{16,8},{20,12},{24,0},{28,4},{1,25},{... | collective-permute-start | bytes 1376264 | tf_op jit(solution)/shard_map/ppermute | solution.py:348
  115.3 21.4 %collective-permute-start.30 = (bf16[1,448,512]{2,1,0:T(8,128)(2,1)S(1)}, bf16[1,448,512]{2,1,0:T(8,128)(2,1)S(1)}, u32[]{:S(2)}, u32[]{:S(2)}) collective-permute-start(bf16[1,448,512]{2,1,0:T(8,128)(2,1)S(1)} %get-tuple-element.48), channel_id=1, source_target_pairs={{0,16},{4,20},{8,24},{12,28},{16,0},{20,4},{24,8},{28,12},{1,17},{... | collective-permute-start | bytes 1376264 | tf_op jit(solution)/shard_map/ppermute | solution.py:348
  116.4 20.3 %collective-permute-start.29 = (bf16[1,448,512]{2,1,0:T(8,128)(2,1)S(1)}, bf16[1,448,512]{2,1,0:T(8,128)(2,1)S(1)}, u32[]{:S(2)}, u32[]{:S(2)}) collective-permute-start(bf16[1,448,512]{2,1,0:T(8,128)(2,1)S(1)} %copy-done.1), channel_id=1, source_target_pairs={{0,8},{4,12},{8,0},{12,4},{16,24},{20,28},{24,16},{28,20},{1,9},{5... | collective-permute-start | bytes 1376264 | tf_op jit(solution)/shard_map/ppermute | solution.py:348
  118.1 18.6 %collective-permute-start.24 = (bf16[1024,128]{1,0:T(8,128)(2,1)}, bf16[1024,128]{1,0:T(8,128)(2,1)S(1)}, u32[]{:S(2)}, u32[]{:S(2)}) collective-permute-start(bf16[1024,128]{1,0:T(8,128)(2,1)} %shard_map.109.refs_0_), channel_id=1, source_target_pairs={{0,1},{1,0},{2,3},{3,2},{4,5},{5,4},{6,7},{7,6},{8,9},{9,8},{10,11... | collective-permute-start | bytes 786440 | tf_op jit(solution)/shard_map/ppermute | solution.py:335
  126.7 13.7 %collective-permute-start.26 = (bf16[1024,128]{1,0:T(8,128)(2,1)S(1)}, bf16[1024,128]{1,0:T(8,128)(2,1)S(1)}, u32[]{:S(2)}, u32[]{:S(2)}) collective-permute-start(bf16[1024,128]{1,0:T(8,128)(2,1)S(1)} %collective-permute-done.25.refs_2_.refs_5_), channel_id=1, source_target_pairs={{0,1},{1,0},{2,3},{3,2},{4,5},{5,4},{6,7},{7,6},{8,9},{9,8},{10,11... | collective-permute-start | bytes 786440 | tf_op jit(solution)/shard_map/ppermute | solution.py:335
  (40 other events, 203.8 us)

commit v13 on v12

--- a/solution.py
+++ b/solution.py
@@ -634,12 +634,12 @@
     value_pieces = lane_pieces({0: value_near, far: value_far}, far // 2)
     value_all = assemble(my_lane, value_pieces)
     (key_partial,) = final_sum(
-        key_keep, key_received, (cosine, sine), [grad_query, value_pieces[1]]
-    )
-    key_pieces = lane_pieces({0: key_partial}, far)
-    key_all = assemble(my_lane, key_pieces)
+        key_keep, key_received, (cosine, sine), [grad_query, value_far, value_pieces[1]]
+    )
+    key_far = hold(lane_swap(key_partial, far), weight_received)
+    key_all = assemble(my_lane, lane_pieces({0: key_partial, far: key_far}, far // 2))
     weight_grad = weight_final(
-        weight_keep, weight_received, 1.0 / rank_count, [*key_pieces[1:3], value_all]
+        weight_keep, weight_received, 1.0 / rank_count, [key_far, value_all]
     )
     lanes_per_key = group // local_heads
 

time: 143 us -> 144 us (level)
  starting transfers between devices: 34.4 us -> 37.8 us
  Pallas kernels: 60.4 us -> 58.7 us
  waiting for transfers between devices: 28.6 us -> 27 us
    ppermute x6, waiting for transfers between devices: 12.7 us -> 7 us  [lane_swap(): lax.ppermute(array, 'tensor', [(lane, lane ^ bit) for lane in range(lanes)])]
    ppermute x26, waiting for transfers between devices: 14.1 us -> 18.2 us  [swap(): lax.ppermute(array, 'dp', [(rank, rank ^ bit) for rank in range(ranks)])]
    ppermute x26, starting transfers between devices: 21.4 us -> 24.1 us  [swap(): lax.ppermute(array, 'dp', [(rank, rank ^ bit) for rank in range(ranks)])]
    add x0 -> x1, other arithmetic: none -> 1.76 us  [added(): return left.astype(jnp.float32) + right.astype(jnp.float32)]
    convert_element_type x3 -> x2, other arithmetic: 5.51 us -> 3.92 us  [chip_sum(): return (total[0], [item.astype(keep.dtype) for item in total[1:]])]
    pallas_call x1, Pallas kernels: 20.5 us -> 18.9 us  [attend(): pl.pallas_call(partial(attend_kernel, heads, ranks), out_shape=(jax.Shape...]
    unnamed x78 -> x82, local copies, waits for them, and re-layouts: 6.39 us -> 7.53 us
  transfers between devices with their start and end apart: 33 -> 33, of which waited for: 12 -> 12; matrix products, arithmetic and copies ran while one was open for 9% -> 9% of each run, Pallas kernels for 25% -> 24%
where the time goes in v13:
time: 144 us; the launch traced here: 145 us
  Pallas kernels  58.7 us (41%)
  starting transfers between devices  37.8 us (26%)
  waiting for transfers between devices  27 us (19%)
  other arithmetic  11.8 us (8%)
  local copies, waits for them, and re-layouts  8.49 us (6%)
    ppermute x26, starting transfers between devices, swap(): lax.ppermute(array, 'dp', [(rank, rank ^ bit) for rank in range(ranks)])  24.1 us
    pallas_call x1, Pallas kernels, attend(): pl.pallas_call(partial(attend_kernel, heads, ranks), out_shape=(jax.Shape...  18.9 us
    ppermute x26, waiting for transfers between devices, swap(): lax.ppermute(array, 'dp', [(rank, rank ^ bit) for rank in range(ranks)])  18.2 us
    pallas_call x1, Pallas kernels, product(): pl.pallas_call(product_kernel, grid_spec=pltpu.PrefetchScalarGridSpec(num...  9.54 us
    ppermute x6, starting transfers between devices, lane_swap(): lax.ppermute(array, 'tensor', [(lane, lane ^ bit) for lane in range(lanes)])  9.5 us
    pallas_call x1, Pallas kernels, prepare(): pl.pallas_call(prepare_kernel, grid=(steps,), out_shape=[jax.ShapeDtypeSt...  9.22 us
    unnamed x82, local copies, waits for them, and re-layouts  7.53 us
    ppermute x6, waiting for transfers between devices, lane_swap(): lax.ppermute(array, 'tensor', [(lane, lane ^ bit) for lane in range(lanes)])  7 us
  transfers between devices with their start and end apart: 33, of which 12 were waited for; matrix products, arithmetic and copies ran while one was open for 9% of the time, Pallas kernels for 24%

profile of v13, /device:TPU:0, one launch (start us, length us, event | category | flops | bytes accessed | tf_op | source)
XLA Modules:
  0.0 145.0 jit_solution(6079334942422459370)
XLA Ops:
  1.9 4.0 %collective-permute-start.12 = (bf16[1024,128]{1,0:T(8,128)(2,1)S(1)}, bf16[1024,128]{1,0:T(8,128)(2,1)S(1)}, u32[]{:S(2)}, u32[]{:S(2)}) collective-permute-start(bf16[1024,128]{1,0:T(8,128)(2,1)S(1)} %constant_dynamic-slice_fusion.refs_8_), channel_id=1, source_target_pairs={{0,24},{4,28},{8,16},{12,20},{16,8},{20,12},{24,0},{28,4},{1,25},{... | collective-permute-start | bytes 786440 | tf_op jit(solution)/shard_map/ppermute | solution.py:348
  8.6 4.2 %all-to-all-start = ((s32[8,8,128]{2,1,0:T(8,128)}), s32[8,8,128]{2,1,0:T(8,128)S(1)}, u32[]{:S(2)}, u32[]{:S(2)}) async-start(s32[8,8,128]{2,1,0:T(8,128)} %broadcast_in_dim.27), calls=%async_computation | async-start | bytes 65536 | tf_op jit(solution)/shard_map/all_to_all | solution.py:583
  16.6 1.8 %all-to-all-done = s32[8,8,128]{2,1,0:T(8,128)S(1)} async-done(((s32[8,8,128]{2,1,0:T(8,128)}), s32[8,8,128]{2,1,0:T(8,128)S(1)}, u32[]{:S(2)}, u32[]{:S(2)}) %all-to-all-start) | async-done | bytes 32800 | tf_op jit(solution)/shard_map/all_to_all | solution.py:583
  19.0 4.8 %shard_map.102 = (f32[1024,128]{1,0:T(8,128)}, f32[1024,128]{1,0:T(8,128)}, bf16[1024,128]{1,0:T(8,128)(2,1)}, s32[8,128]{1,0:T(8,128)}) custom-call(s32[1]{0:T(128)} %bitcast.at_ref, s32[8]{0:T(128)} %select_reduce_fusion.dest_ref, s32[64,128]{1,0:T(8,128)} %bitcast.11, f32[1,128]{1,0:T(1,128)} %maximum_bitcast_fusion.freq_ref, bf16[1024,512]{1,0:T(8,128)(2,1)} %key_ref.1), custom_call_target="tpu_custom_call" | custom-call | tf_op jit(solution)/shard_map/pallas_call | solution.py:89
  23.8 2.4 %collective-permute-start.5 = (bf16[1024,128]{1,0:T(8,128)(2,1)}, bf16[1024,128]{1,0:T(8,128)(2,1)S(1)}, u32[]{:S(2)}, u32[]{:S(2)}) collective-permute-start(bf16[1024,128]{1,0:T(8,128)(2,1)} %get-tuple-element.26.refs_0_), channel_id=1, source_target_pairs={{0,24},{4,28},{8,16},{12,20},{16,8},{20,12},{24,0},{28,4},{1,25},{... | collective-permute-start | bytes 786440 | tf_op jit(solution)/shard_map/ppermute | solution.py:348
  27.8 9.2 %shard_map.103 = (bf16[1024,512]{1,0:T(8,128)(2,1)}, bf16[512,1024]{1,0:T(8,128)(2,1)}, bf16[1024,512]{1,0:T(8,128)(2,1)}) custom-call(bf16[1024,3584]{1,0:T(8,128)(2,1)} %right_ref.1, bf16[3584,512]{1,0:T(8,128)(2,1)} %weight_ref.1, bf16[1024,512]{1,0:T(8,128)(2,1)} %query_ref.1, f32[1024,128]{1,0:T(8,128)} %get-tuple-element.24.cos_ref.refs_4_, ...), custom_call_target="tpu_custom_call" | custom-call | flops 3758096384 | bytes 7340032 | tf_op jit(solution)/shard_map/pallas_call | solution.py:426
  37.3 1.5 %collective-permute-done.3.refs_4_ = bf16[1024,128]{1,0:T(8,128)(2,1)S(1)} collective-permute-done((bf16[1024,128]{1,0:T(8,128)(2,1)}, bf16[1024,128]{1,0:T(8,128)(2,1)S(1)}, u32[]{:S(2)}, u32[]{:S(2)}) %collective-permute-start.3) | collective-permute-done | bytes 262176 | tf_op jit(solution)/shard_map/ppermute | solution.py:348
  42.1 18.9 %shard_map.104 = (f32[512,1024]{1,0:T(8,128)}, bf16[512,1024]{1,0:T(8,128)(2,1)}, bf16[4096,128]{1,0:T(8,128)(2,1)}, bf16[4096,128]{1,0:T(8,128)(2,1)}, bf16[409...) custom-call(s32[64]{0:T(128)} %multiply_add_fusion.3.target_ref, s32[64]{0:T(128)} %get-tuple-element.44.source_ref, ...), custom_call_target="tpu_custom_call" | custom-call | tf_op jit(solution)/shard_map/pallas_call | solution.py:281
  61.0 2.0 %collective-permute-start.14 = (bf16[4096,128]{1,0:T(8,128)(2,1)}, bf16[4096,128]{1,0:T(8,128)(2,1)}, u32[]{:S(2)}, u32[]{:S(2)}) collective-permute-start(bf16[4096,128]{1,0:T(8,128)(2,1)} %get-tuple-element.33), channel_id=1, source_target_pairs={{0,4},{4,0},{8,12},{12,8},{16,20},{20,16},{24,28},{28,24},{1,5},{5... | collective-permute-start | bytes 3145736 | tf_op jit(solution)/shard_map/ppermute | solution.py:348
  63.7 2.7 %collective-permute-done.14 = bf16[4096,128]{1,0:T(8,128)(2,1)} collective-permute-done((bf16[4096,128]{1,0:T(8,128)(2,1)}, bf16[4096,128]{1,0:T(8,128)(2,1)}, u32[]{:S(2)}, u32[]{:S(2)}) %collective-permute-start.14) | collective-permute-done | bytes 1048608 | tf_op jit(solution)/shard_map/ppermute | solution.py:348
  66.4 2.6 %add_convert_fusion.5 = (bf16[1024,128]{1,0:T(8,128)(2,1)}, bf16[1024,128]{1,0:T(8,128)(2,1)}, f32[1024,128]{1,0:T(8,128)}, bf16[1024,128]{1,0:T(8,128)(2,1)S(1)}) fusion(bf16[4096,128]{1,0:T(8,128)(2,1)} %collective-permute-done.14, bf16[4096,128]{1,0:T(8,128)(2,1)} %get-tuple-element.32), kind=kLoop, calls=%fused_computation.7 | loop fusion | flops 1966080 | bytes 3407872 | tf_op jit(solution)/shard_map/convert_element_type | solution.py:370
  69.0 3.4 %collective-permute-start.18 = (bf16[1024,128]{1,0:T(8,128)(2,1)}, bf16[1024,128]{1,0:T(8,128)(2,1)S(1)}, u32[]{:S(2)}, u32[]{:S(2)}) collective-permute-start(bf16[1024,128]{1,0:T(8,128)(2,1)} %get-tuple-element.55), channel_id=1, source_target_pairs={{0,24},{4,28},{8,16},{12,20},{16,8},{20,12},{24,0},{28,4},{1,25},{... | collective-permute-start | bytes 786440 | tf_op jit(solution)/shard_map/ppermute | solution.py:348
  72.8 1.4 collective-permute-start.16
  75.5 9.5 %shard_map.105 = (bf16[4,448,512]{2,1,0:T(8,128)(2,1)}, bf16[4,448,512]{2,1,0:T(8,128)(2,1)}, f32[1024,128]{1,0:T(8,128)}) custom-call(s32[2]{0:T(128)} %pad_add_fusion.my_ref, bf16[512,1024]{1,0:T(8,128)(2,1)} %get-tuple-element.31.left_ref, bf16[1024,3584]{1,0:T(8,128)(2,1)} %right_ref.1, ...), custom_call_target="tpu_custom_call", output_to_operand_aliasing={{2}: (5, {})} | custom-call | tf_op jit(solution)/shard_map/pallas_call | solution.py:532
  85.1 1.5 %collective-permute-done.16.refs_1_ = bf16[1024,128]{1,0:T(8,128)(2,1)S(1)} collective-permute-done((bf16[1024,128]{1,0:T(8,128)(2,1)S(1)}, bf16[1024,128]{1,0:T(8,128)(2,1)S(1)}, u32[]{:S(2)}, u32[]{:S(2)}) %collective-permute-start.16) | collective-permute-done | bytes 262176 | tf_op jit(solution)/shard_map/ppermute | solution.py:348
  87.3 2.2 %shard_map.106 = (bf16[1024,128]{1,0:T(8,128)(2,1)}, bf16[1024,128]{1,0:T(8,128)(2,1)}, bf16[4,448,512]{2,1,0:T(8,128)(2,1)}) custom-call(f32[1024,128]{1,0:T(8,128)} %get-tuple-element.37.refs_0_, bf16[1024,128]{1,0:T(8,128)(2,1)} %copy-done.33, bf16[1024,128]{1,0:T(8,128)(2,1)} %copy-done.31, ...), custom_call_target="tpu_custom_call", output_to_operand_aliasing={{2}: (4, {})} | custom-call | tf_op jit(solution)/shard_map/pallas_call | solution.py:392
  89.9 1.9 %collective-permute-start.22 = (bf16[1024,128]{1,0:T(8,128)(2,1)S(1)}, bf16[1024,128]{1,0:T(8,128)(2,1)S(1)}, u32[]{:S(2)}, u32[]{:S(2)}) collective-permute-start(bf16[1024,128]{1,0:T(8,128)(2,1)S(1)} %copy-done.37), channel_id=1, source_target_pairs={{0,24},{4,28},{8,16},{12,20},{16,8},{20,12},{24,0},{28,4},{1,25},{... | collective-permute-start | bytes 786440 | tf_op jit(solution)/shard_map/ppermute | solution.py:348
  93.1 2.6 %collective-permute-start.23 = (bf16[1024,128]{1,0:T(8,128)(2,1)}, bf16[1024,128]{1,0:T(8,128)(2,1)S(1)}, u32[]{:S(2)}, u32[]{:S(2)}) collective-permute-start(bf16[1024,128]{1,0:T(8,128)(2,1)} %get-tuple-element.40), channel_id=1, source_target_pairs={{0,2},{1,3},{2,0},{3,1},{4,6},{5,7},{6,4},{7,5},{8,10},{9,11},{10,... | collective-permute-start | bytes 786440 | tf_op jit(solution)/shard_map/ppermute | solution.py:335
  95.7 1.8 %convert_add_fusion = (f32[1,448,512]{2,1,0:T(8,128)}, bf16[1,448,512]{2,1,0:T(8,128)(2,1)}, bf16[1,448,512]{2,1,0:T(8,128)(2,1)}, bf16[1,448,512]{2,1,0:T(8,128)(2,1)}) fusion(bf16[4,448,512]{2,1,0:T(8,128)(2,1)S(1)} %collective-permute-done.19, bf16[4,448,512]{2,1,0:T(8,128)(2,1)S(1)} %copy-done.7), kind=kLoop, calls=%fused_computation | loop fusion | flops 3440640 | bytes 5963776 | tf_op jit(solution)/shard_map/add | solution.py:360
  97.5 1.6 %collective-permute-start.24 = (bf16[1024,128]{1,0:T(8,128)(2,1)}, bf16[1024,128]{1,0:T(8,128)(2,1)S(1)}, u32[]{:S(2)}, u32[]{:S(2)}) collective-permute-start(bf16[1024,128]{1,0:T(8,128)(2,1)} %shard_map.109.refs_0_), channel_id=1, source_target_pairs={{0,1},{1,0},{2,3},{3,2},{4,5},{5,4},{6,7},{7,6},{8,9},{9,8},{10,11... | collective-permute-start | bytes 786440 | tf_op jit(solution)/shard_map/ppermute | solution.py:335
  99.0 5.2 %collective-permute-done.22.refs_3_ = bf16[1024,128]{1,0:T(8,128)(2,1)S(1)} collective-permute-done((bf16[1024,128]{1,0:T(8,128)(2,1)S(1)}, bf16[1024,128]{1,0:T(8,128)(2,1)S(1)}, u32[]{:S(2)}, u32[]{:S(2)}) %collective-permute-start.22) | collective-permute-done | bytes 262176 | tf_op jit(solution)/shard_map/ppermute | solution.py:348
  106.6 1.4 collective-permute-start.28
  109.1 4.4 %shard_map.107.refs_1_.refs_6_ = bf16[1024,512]{1,0:T(8,128)(2,1)} custom-call(f32[512,1024]{1,0:T(8,128)} %get-tuple-element.30.grad_ref, f32[1024,128]{1,0:T(8,128)} %get-tuple-element.24.cos_ref.refs_4_, f32[1024,128]{1,0:T(8,128)} %get-tuple-element.25.sin_ref.refs_5_, bf16[1,448,512]{2,1,0:T(8,128)(2,1)} %get-tuple-element.50.refs_0_.refs_1_), custom_call_target="tpu_custom_call" | custom-call | tf_op jit(solution)/shard_map/pallas_call | solution.py:467
  114.4 2.6 %shard_map.110.refs_0_ = bf16[1024,128]{1,0:T(8,128)(2,1)} custom-call(f32[1024,128]{1,0:T(8,128)} %get-tuple-element.53.refs_0_, bf16[1024,128]{1,0:T(8,128)(2,1)} %copy-done.24, bf16[1024,128]{1,0:T(8,128)(2,1)} %copy-done.27, bf16[1024,128]{1,0:T(8,128)(2,1)} %copy-done.25, f32[1024,128]{1,0:T(8,128)} %get-tuple-element.24.cos_ref.refs_4_, ...), custom_call_target="tpu_custom_call" | custom-call | tf_op jit(solution)/shard_map/pallas_call | solution.py:392
  116.9 2.6 %collective-permute-start.26 = (bf16[1024,128]{1,0:T(8,128)(2,1)}, bf16[1024,128]{1,0:T(8,128)(2,1)S(1)}, u32[]{:S(2)}, u32[]{:S(2)}) collective-permute-start(bf16[1024,128]{1,0:T(8,128)(2,1)} %shard_map.110.refs_0_), channel_id=1, source_target_pairs={{0,2},{1,3},{2,0},{3,1},{4,6},{5,7},{6,4},{7,5},{8,10},{9,11},{10,... | collective-permute-start | bytes 786440 | tf_op jit(solution)/shard_map/ppermute | solution.py:335
  119.5 1.6 %collective-permute-start.31 = (bf16[1024,128]{1,0:T(8,128)(2,1)S(1)}, bf16[1024,128]{1,0:T(8,128)(2,1)S(1)}, u32[]{:S(2)}, u32[]{:S(2)}) collective-permute-start(bf16[1024,128]{1,0:T(8,128)(2,1)S(1)} %copy-done.2), channel_id=1, source_target_pairs={{0,1},{1,0},{2,3},{3,2},{4,5},{5,4},{6,7},{7,6},{8,9},{9,8},{10,11... | collective-permute-start | bytes 786440 | tf_op jit(solution)/shard_map/ppermute | solution.py:335
  121.6 6.3 %collective-permute-done.28.refs_2_ = bf16[1,448,512]{2,1,0:T(8,128)(2,1)S(1)} collective-permute-done((bf16[1,448,512]{2,1,0:T(8,128)(2,1)}, bf16[1,448,512]{2,1,0:T(8,128)(2,1)S(1)}, u32[]{:S(2)}, u32[]{:S(2)}) %collective-permute-start.28) | collective-permute-done | bytes 458784 | tf_op jit(solution)/shard_map/ppermute | solution.py:348
  127.9 2.8 %collective-permute-done.26.refs_0_ = bf16[1024,128]{1,0:T(8,128)(2,1)S(1)} collective-permute-done((bf16[1024,128]{1,0:T(8,128)(2,1)}, bf16[1024,128]{1,0:T(8,128)(2,1)S(1)}, u32[]{:S(2)}, u32[]{:S(2)}) %collective-permute-start.26) | collective-permute-done | bytes 262176 | tf_op jit(solution)/shard_map/ppermute | solution.py:335
  134.0 2.2 %shard_map.113.refs_5_ = bf16[1024,512]{1,0:T(8,128)(2,1)} custom-call(s32[1]{0:T(128)} %bitcast.6.my_ref, bf16[1024,128]{1,0:T(8,128)(2,1)} %shard_map.109.refs_0_, bf16[1024,128]{1,0:T(8,128)(2,1)} %copy-done.8, bf16[1024,128]{1,0:T(8,128)(2,1)} %shard_map.108.refs_7_.refs_2_, bf16[1024,128]{1,0:T(8,128)(2,1)} %copy-done.34), custom_call_target="tpu_custom_call" | custom-call | tf_op jit(solution)/shard_map/pallas_call | solution.py:322
  136.2 2.7 %shard_map.114 = f32[448,512]{1,0:T(8,128)} custom-call(f32[1,448,512]{2,1,0:T(8,128)} %get-tuple-element.47.refs_0_, bf16[1,448,512]{2,1,0:T(8,128)(2,1)} %copy-done.6, bf16[1,448,512]{2,1,0:T(8,128)(2,1)} %copy-done.5, bf16[1,448,512]{2,1,0:T(8,128)(2,1)} %copy-done.4, bf16[1024,128]{1,0:T(8,128)(2,1)} %shard_map.111.refs_2_.refs_4_, ...), custom_call_target="tpu_custom_call" | custom-call | tf_op jit(solution)/shard_map/pallas_call | solution.py:561
  138.9 3.1 %collective-permute-done.30.refs_3_ = bf16[1024,128]{1,0:T(8,128)(2,1)S(1)} collective-permute-done((bf16[1024,128]{1,0:T(8,128)(2,1)}, bf16[1024,128]{1,0:T(8,128)(2,1)S(1)}, u32[]{:S(2)}, u32[]{:S(2)}) %collective-permute-start.30) | collective-permute-done | bytes 262176 | tf_op jit(solution)/shard_map/ppermute | solution.py:335
  142.6 2.2 %shard_map.112 = bf16[1024,512]{1,0:T(8,128)(2,1)} custom-call(s32[1]{0:T(128)} %bitcast.6.my_ref, bf16[1024,128]{1,0:T(8,128)(2,1)} %shard_map.110.refs_0_, bf16[1024,128]{1,0:T(8,128)(2,1)} %copy-done.32, bf16[1024,128]{1,0:T(8,128)(2,1)} %shard_map.111.refs_2_.refs_4_, bf16[1024,128]{1,0:T(8,128)(2,1)} %copy-done.35), custom_call_target="tpu_custom_call" | custom-call | tf_op jit(solution)/shard_map/pallas_call | solution.py:322
  (150 shorter events, 26.7 us)
Async XLA Ops:
  1.9 24.3 %collective-permute-start.12 = (bf16[1024,128]{1,0:T(8,128)(2,1)S(1)}, bf16[1024,128]{1,0:T(8,128)(2,1)S(1)}, u32[]{:S(2)}, u32[]{:S(2)}) collective-permute-start(bf16[1024,128]{1,0:T(8,128)(2,1)S(1)} %constant_dynamic-slice_fusion.refs_8_), channel_id=1, source_target_pairs={{0,24},{4,28},{8,16},{12,20},{16,8},{20,12},{24,0},{28,4},{1,25},{... | collective-permute-start | bytes 786440 | tf_op jit(solution)/shard_map/ppermute | solution.py:348
  5.9 21.0 %collective-permute-start.10 = (bf16[1024,128]{1,0:T(8,128)(2,1)S(1)}, bf16[1024,128]{1,0:T(8,128)(2,1)S(1)}, u32[]{:S(2)}, u32[]{:S(2)}) collective-permute-start(bf16[1024,128]{1,0:T(8,128)(2,1)S(1)} %constant_dynamic-slice_fusion.refs_8_), channel_id=1, source_target_pairs={{0,16},{4,20},{8,24},{12,28},{16,0},{20,4},{24,8},{28,12},{1,17},{... | collective-permute-start | bytes 786440 | tf_op jit(solution)/shard_map/ppermute | solution.py:348
  6.4 20.9 %collective-permute-start.8 = (bf16[1024,128]{1,0:T(8,128)(2,1)S(1)}, bf16[1024,128]{1,0:T(8,128)(2,1)S(1)}, u32[]{:S(2)}, u32[]{:S(2)}) collective-permute-start(bf16[1024,128]{1,0:T(8,128)(2,1)S(1)} %constant_dynamic-slice_fusion.refs_8_), channel_id=1, source_target_pairs={{0,8},{4,12},{8,0},{12,4},{16,24},{20,28},{24,16},{28,20},{1,9},{5... | collective-permute-start | bytes 786440 | tf_op jit(solution)/shard_map/ppermute | solution.py:348
  6.5 20.8 %collective-permute-start.7 = (bf16[1024,128]{1,0:T(8,128)(2,1)S(1)}, bf16[1024,128]{1,0:T(8,128)(2,1)S(1)}, u32[]{:S(2)}, u32[]{:S(2)}) collective-permute-start(bf16[1024,128]{1,0:T(8,128)(2,1)S(1)} %constant_dynamic-slice_fusion.refs_8_), channel_id=1, source_target_pairs={{0,4},{4,0},{8,12},{12,8},{16,20},{20,16},{24,28},{28,24},{1,5},{5... | collective-permute-start | bytes 786440 | tf_op jit(solution)/shard_map/ppermute | solution.py:348
  8.6 9.8 %all-to-all-start = ((s32[8,8,128]{2,1,0:T(8,128)}), s32[8,8,128]{2,1,0:T(8,128)S(1)}, u32[]{:S(2)}, u32[]{:S(2)}) async-start(s32[8,8,128]{2,1,0:T(8,128)} %broadcast_in_dim.27), calls=%async_computation | async-start | bytes 65536 | tf_op jit(solution)/shard_map/all_to_all | solution.py:583
  23.8 13.3 %collective-permute-start.5 = (bf16[1024,128]{1,0:T(8,128)(2,1)}, bf16[1024,128]{1,0:T(8,128)(2,1)S(1)}, u32[]{:S(2)}, u32[]{:S(2)}) collective-permute-start(bf16[1024,128]{1,0:T(8,128)(2,1)} %get-tuple-element.26.refs_0_), channel_id=1, source_target_pairs={{0,24},{4,28},{8,16},{12,20},{16,8},{20,12},{24,0},{28,4},{1,25},{... | collective-permute-start | bytes 786440 | tf_op jit(solution)/shard_map/ppermute | solution.py:348
  26.2 12.5 %collective-permute-start.3 = (bf16[1024,128]{1,0:T(8,128)(2,1)}, bf16[1024,128]{1,0:T(8,128)(2,1)S(1)}, u32[]{:S(2)}, u32[]{:S(2)}) collective-permute-start(bf16[1024,128]{1,0:T(8,128)(2,1)} %get-tuple-element.26.refs_0_), channel_id=1, source_target_pairs={{0,16},{4,20},{8,24},{12,28},{16,0},{20,4},{24,8},{28,12},{1,17},{... | collective-permute-start | bytes 786440 | tf_op jit(solution)/shard_map/ppermute | solution.py:348
  26.8 12.0 %collective-permute-start.1 = (bf16[1024,128]{1,0:T(8,128)(2,1)}, bf16[1024,128]{1,0:T(8,128)(2,1)S(1)}, u32[]{:S(2)}, u32[]{:S(2)}) collective-permute-start(bf16[1024,128]{1,0:T(8,128)(2,1)} %get-tuple-element.26.refs_0_), channel_id=1, source_target_pairs={{0,8},{4,12},{8,0},{12,4},{16,24},{20,28},{24,16},{28,20},{1,9},{5... | collective-permute-start | bytes 786440 | tf_op jit(solution)/shard_map/ppermute | solution.py:348
  27.3 11.9 %collective-permute-start = (bf16[1024,128]{1,0:T(8,128)(2,1)}, bf16[1024,128]{1,0:T(8,128)(2,1)S(1)}, u32[]{:S(2)}, u32[]{:S(2)}) collective-permute-start(bf16[1024,128]{1,0:T(8,128)(2,1)} %get-tuple-element.26.refs_0_), channel_id=1, source_target_pairs={{0,4},{4,0},{8,12},{12,8},{16,20},{20,16},{24,28},{28,24},{1,5},{5... | collective-permute-start | bytes 786440 | tf_op jit(solution)/shard_map/ppermute | solution.py:348
  27.4 12.0 %collective-permute-start.13 = (bf16[1024,128]{1,0:T(8,128)(2,1)S(1)}, bf16[1024,128]{1,0:T(8,128)(2,1)S(1)}, u32[]{:S(2)}, u32[]{:S(2)}) collective-permute-start(bf16[1024,128]{1,0:T(8,128)(2,1)S(1)} %collective-permute-done.12.refs_14_), channel_id=1, source_target_pairs={{0,4},{4,0},{8,12},{12,8},{16,20},{20,16},{24,28},{28,24},{1,5},{5... | collective-permute-start | bytes 786440 | tf_op jit(solution)/shard_map/ppermute | solution.py:348
  37.1 3.3 %collective-permute-start.11 = (bf16[1024,128]{1,0:T(8,128)(2,1)S(1)}, bf16[1024,128]{1,0:T(8,128)(2,1)S(1)}, u32[]{:S(2)}, u32[]{:S(2)}) collective-permute-start(bf16[1024,128]{1,0:T(8,128)(2,1)S(1)} %collective-permute-done.10.refs_12_), channel_id=1, source_target_pairs={{0,4},{4,0},{8,12},{12,8},{16,20},{20,16},{24,28},{28,24},{1,5},{5... | collective-permute-start | bytes 786440 | tf_op jit(solution)/shard_map/ppermute | solution.py:348
  38.8 1.9 %collective-permute-start.6 = (bf16[1024,128]{1,0:T(8,128)(2,1)S(1)}, bf16[1024,128]{1,0:T(8,128)(2,1)S(1)}, u32[]{:S(2)}, u32[]{:S(2)}) collective-permute-start(bf16[1024,128]{1,0:T(8,128)(2,1)S(1)} %collective-permute-done.5.refs_6_), channel_id=1, source_target_pairs={{0,4},{4,0},{8,12},{12,8},{16,20},{20,16},{24,28},{28,24},{1,5},{5... | collective-permute-start | bytes 786440 | tf_op jit(solution)/shard_map/ppermute | solution.py:348
  39.3 1.8 %collective-permute-start.4 = (bf16[1024,128]{1,0:T(8,128)(2,1)S(1)}, bf16[1024,128]{1,0:T(8,128)(2,1)S(1)}, u32[]{:S(2)}, u32[]{:S(2)}) collective-permute-start(bf16[1024,128]{1,0:T(8,128)(2,1)S(1)} %collective-permute-done.3.refs_4_), channel_id=1, source_target_pairs={{0,4},{4,0},{8,12},{12,8},{16,20},{20,16},{24,28},{28,24},{1,5},{5... | collective-permute-start | bytes 786440 | tf_op jit(solution)/shard_map/ppermute | solution.py:348
  39.4 2.0 %collective-permute-start.2 = (bf16[1024,128]{1,0:T(8,128)(2,1)S(1)}, bf16[1024,128]{1,0:T(8,128)(2,1)S(1)}, u32[]{:S(2)}, u32[]{:S(2)}) collective-permute-start(bf16[1024,128]{1,0:T(8,128)(2,1)S(1)} %collective-permute-done.1.refs_2_), channel_id=1, source_target_pairs={{0,4},{4,0},{8,12},{12,8},{16,20},{20,16},{24,28},{28,24},{1,5},{5... | collective-permute-start | bytes 786440 | tf_op jit(solution)/shard_map/ppermute | solution.py:348
  61.0 5.3 %collective-permute-start.14 = (bf16[4096,128]{1,0:T(8,128)(2,1)}, bf16[4096,128]{1,0:T(8,128)(2,1)}, u32[]{:S(2)}, u32[]{:S(2)}) collective-permute-start(bf16[4096,128]{1,0:T(8,128)(2,1)} %get-tuple-element.33), channel_id=1, source_target_pairs={{0,4},{4,0},{8,12},{12,8},{16,20},{20,16},{24,28},{28,24},{1,5},{5... | collective-permute-start | bytes 3145736 | tf_op jit(solution)/shard_map/ppermute | solution.py:348
  63.0 11.2 %collective-permute-start.15 = (bf16[4096,128]{1,0:T(8,128)(2,1)}, bf16[4096,128]{1,0:T(8,128)(2,1)S(1)}, u32[]{:S(2)}, u32[]{:S(2)}) collective-permute-start(bf16[4096,128]{1,0:T(8,128)(2,1)} %get-tuple-element.35), channel_id=1, source_target_pairs={{0,4},{4,0},{8,12},{12,8},{16,20},{20,16},{24,28},{28,24},{1,5},{5... | collective-permute-start | bytes 3145736 | tf_op jit(solution)/shard_map/ppermute | solution.py:348
  69.0 16.1 %collective-permute-start.18 = (bf16[1024,128]{1,0:T(8,128)(2,1)}, bf16[1024,128]{1,0:T(8,128)(2,1)S(1)}, u32[]{:S(2)}, u32[]{:S(2)}) collective-permute-start(bf16[1024,128]{1,0:T(8,128)(2,1)} %get-tuple-element.55), channel_id=1, source_target_pairs={{0,24},{4,28},{8,16},{12,20},{16,8},{20,12},{24,0},{28,4},{1,25},{... | collective-permute-start | bytes 786440 | tf_op jit(solution)/shard_map/ppermute | solution.py:348
  72.4 12.7 %collective-permute-start.17 = (bf16[1024,128]{1,0:T(8,128)(2,1)}, bf16[1024,128]{1,0:T(8,128)(2,1)S(1)}, u32[]{:S(2)}, u32[]{:S(2)}) collective-permute-start(bf16[1024,128]{1,0:T(8,128)(2,1)} %get-tuple-element.56), channel_id=1, source_target_pairs={{0,16},{4,20},{8,24},{12,28},{16,0},{20,4},{24,8},{28,12},{1,17},{... | collective-permute-start | bytes 786440 | tf_op jit(solution)/shard_map/ppermute | solution.py:348
  72.8 13.8 %collective-permute-start.16 = (bf16[1024,128]{1,0:T(8,128)(2,1)S(1)}, bf16[1024,128]{1,0:T(8,128)(2,1)S(1)}, u32[]{:S(2)}, u32[]{:S(2)}) collective-permute-start(bf16[1024,128]{1,0:T(8,128)(2,1)S(1)} %get-tuple-element.58.refs_0_), channel_id=1, source_target_pairs={{0,8},{4,12},{8,0},{12,4},{16,24},{20,28},{24,16},{28,20},{1,9},{5... | collective-permute-start | bytes 786440 | tf_op jit(solution)/shard_map/ppermute | solution.py:348
  89.5 6.2 %collective-permute-start.19 = (bf16[4,448,512]{2,1,0:T(8,128)(2,1)}, bf16[4,448,512]{2,1,0:T(8,128)(2,1)S(1)}, u32[]{:S(2)}, u32[]{:S(2)}) collective-permute-start(bf16[4,448,512]{2,1,0:T(8,128)(2,1)} %get-tuple-element.39), channel_id=1, source_target_pairs={{0,4},{4,0},{8,12},{12,8},{16,20},{20,16},{24,28},{28,24},{1,5},{5... | collective-permute-start | bytes 5505032 | tf_op jit(solution)/shard_map/ppermute | solution.py:348
  89.5 24.0 %collective-permute-start.20 = (bf16[1024,128]{1,0:T(8,128)(2,1)S(1)}, bf16[1024,128]{1,0:T(8,128)(2,1)S(1)}, u32[]{:S(2)}, u32[]{:S(2)}) collective-permute-start(bf16[1024,128]{1,0:T(8,128)(2,1)S(1)} %copy-done.11), channel_id=1, source_target_pairs={{0,8},{4,12},{8,0},{12,4},{16,24},{20,28},{24,16},{28,20},{1,9},{5... | collective-permute-start | bytes 786440 | tf_op jit(solution)/shard_map/ppermute | solution.py:348
  89.9 14.3 %collective-permute-start.22 = (bf16[1024,128]{1,0:T(8,128)(2,1)S(1)}, bf16[1024,128]{1,0:T(8,128)(2,1)S(1)}, u32[]{:S(2)}, u32[]{:S(2)}) collective-permute-start(bf16[1024,128]{1,0:T(8,128)(2,1)S(1)} %copy-done.37), channel_id=1, source_target_pairs={{0,24},{4,28},{8,16},{12,20},{16,8},{20,12},{24,0},{28,4},{1,25},{... | collective-permute-start | bytes 786440 | tf_op jit(solution)/shard_map/ppermute | solution.py:348
  91.9 14.0 %collective-permute-start.21 = (bf16[1024,128]{1,0:T(8,128)(2,1)S(1)}, bf16[1024,128]{1,0:T(8,128)(2,1)S(1)}, u32[]{:S(2)}, u32[]{:S(2)}) collective-permute-start(bf16[1024,128]{1,0:T(8,128)(2,1)S(1)} %copy-done.36), channel_id=1, source_target_pairs={{0,16},{4,20},{8,24},{12,28},{16,0},{20,4},{24,8},{28,12},{1,17},{... | collective-permute-start | bytes 786440 | tf_op jit(solution)/shard_map/ppermute | solution.py:348
  93.1 15.0 %collective-permute-start.23 = (bf16[1024,128]{1,0:T(8,128)(2,1)}, bf16[1024,128]{1,0:T(8,128)(2,1)S(1)}, u32[]{:S(2)}, u32[]{:S(2)}) collective-permute-start(bf16[1024,128]{1,0:T(8,128)(2,1)} %get-tuple-element.40), channel_id=1, source_target_pairs={{0,2},{1,3},{2,0},{3,1},{4,6},{5,7},{6,4},{7,5},{8,10},{9,11},{10,... | collective-permute-start | bytes 786440 | tf_op jit(solution)/shard_map/ppermute | solution.py:335
  97.5 16.1 %collective-permute-start.24 = (bf16[1024,128]{1,0:T(8,128)(2,1)}, bf16[1024,128]{1,0:T(8,128)(2,1)S(1)}, u32[]{:S(2)}, u32[]{:S(2)}) collective-permute-start(bf16[1024,128]{1,0:T(8,128)(2,1)} %shard_map.109.refs_0_), channel_id=1, source_target_pairs={{0,1},{1,0},{2,3},{3,2},{4,5},{5,4},{6,7},{7,6},{8,9},{9,8},{10,11... | collective-permute-start | bytes 786440 | tf_op jit(solution)/shard_map/ppermute | solution.py:335
  104.9 16.2 %collective-permute-start.29 = (bf16[1,448,512]{2,1,0:T(8,128)(2,1)}, bf16[1,448,512]{2,1,0:T(8,128)(2,1)S(1)}, u32[]{:S(2)}, u32[]{:S(2)}) collective-permute-start(bf16[1,448,512]{2,1,0:T(8,128)(2,1)} %get-tuple-element.48), channel_id=1, source_target_pairs={{0,24},{4,28},{8,16},{12,20},{16,8},{20,12},{24,0},{28,4},{1,25},{... | collective-permute-start | bytes 1376264 | tf_op jit(solution)/shard_map/ppermute | solution.py:348
  106.6 21.3 %collective-permute-start.28 = (bf16[1,448,512]{2,1,0:T(8,128)(2,1)}, bf16[1,448,512]{2,1,0:T(8,128)(2,1)S(1)}, u32[]{:S(2)}, u32[]{:S(2)}) collective-permute-start(bf16[1,448,512]{2,1,0:T(8,128)(2,1)} %get-tuple-element.49), channel_id=1, source_target_pairs={{0,16},{4,20},{8,24},{12,28},{16,0},{20,4},{24,8},{28,12},{1,17},{... | collective-permute-start | bytes 1376264 | tf_op jit(solution)/shard_map/ppermute | solution.py:348
  108.1 19.8 %collective-permute-start.27 = (bf16[1,448,512]{2,1,0:T(8,128)(2,1)}, bf16[1,448,512]{2,1,0:T(8,128)(2,1)S(1)}, u32[]{:S(2)}, u32[]{:S(2)}) collective-permute-start(bf16[1,448,512]{2,1,0:T(8,128)(2,1)} %get-tuple-element.50.refs_0_.refs_1_), channel_id=1, source_target_pairs={{0,8},{4,12},{8,0},{12,4},{16,24},{20,28},{24,16},{28,20},{1,9},{5... | collective-permute-start | bytes 1376264 | tf_op jit(solution)/shard_map/ppermute | solution.py:348
  116.9 13.8 %collective-permute-start.26 = (bf16[1024,128]{1,0:T(8,128)(2,1)}, bf16[1024,128]{1,0:T(8,128)(2,1)S(1)}, u32[]{:S(2)}, u32[]{:S(2)}) collective-permute-start(bf16[1024,128]{1,0:T(8,128)(2,1)} %shard_map.110.refs_0_), channel_id=1, source_target_pairs={{0,2},{1,3},{2,0},{3,1},{4,6},{5,7},{6,4},{7,5},{8,10},{9,11},{10,... | collective-permute-start | bytes 786440 | tf_op jit(solution)/shard_map/ppermute | solution.py:335
  119.5 13.7 %collective-permute-start.31 = (bf16[1024,128]{1,0:T(8,128)(2,1)S(1)}, bf16[1024,128]{1,0:T(8,128)(2,1)S(1)}, u32[]{:S(2)}, u32[]{:S(2)}) collective-permute-start(bf16[1024,128]{1,0:T(8,128)(2,1)S(1)} %copy-done.2), channel_id=1, source_target_pairs={{0,1},{1,0},{2,3},{3,2},{4,5},{5,4},{6,7},{7,6},{8,9},{9,8},{10,11... | collective-permute-start | bytes 786440 | tf_op jit(solution)/shard_map/ppermute | solution.py:335
  121.1 17.8 %collective-permute-start.25 = (bf16[1024,128]{1,0:T(8,128)(2,1)}, bf16[1024,128]{1,0:T(8,128)(2,1)S(1)}, u32[]{:S(2)}, u32[]{:S(2)}) collective-permute-start(bf16[1024,128]{1,0:T(8,128)(2,1)} %shard_map.110.refs_0_), channel_id=1, source_target_pairs={{0,1},{1,0},{2,3},{3,2},{4,5},{5,4},{6,7},{7,6},{8,9},{9,8},{10,11... | collective-permute-start | bytes 786440 | tf_op jit(solution)/shard_map/ppermute | solution.py:335
  131.4 10.5 %collective-permute-start.30 = (bf16[1024,128]{1,0:T(8,128)(2,1)}, bf16[1024,128]{1,0:T(8,128)(2,1)S(1)}, u32[]{:S(2)}, u32[]{:S(2)}) collective-permute-start(bf16[1024,128]{1,0:T(8,128)(2,1)} %shard_map.111.refs_2_.refs_4_), channel_id=1, source_target_pairs={{0,1},{1,0},{2,3},{3,2},{4,5},{5,4},{6,7},{7,6},{8,9},{9,8},{10,11... | collective-permute-start | bytes 786440 | tf_op jit(solution)/shard_map/ppermute | solution.py:335
  (42 other events, 207.4 us)

commit v14 on v13

--- a/solution.py
+++ b/solution.py
@@ -63,8 +63,10 @@
     cos_ref, sin_ref, turned_ref, own_ref = refs
     factor = 0.1 * math.log(yarn_factor) + 1.0
     half = lax.broadcasted_iota(jnp.int32, (ROWBLK, HD), 1) < HD // 2
-    for block in range(own_ref.shape[0]):
-        rows = pl.ds(block * ROWBLK, ROWBLK)
+    each = key_ref.shape[0] // ROWBLK
+    for item in range(each):
+        block = pl.program_id(0) * each + item
+        rows = pl.ds(item * ROWBLK, ROWBLK)
         place = places_ref[pl.ds(dest_ref[block], 1), :]
         own_ref[pl.ds(block, 1), :] = place
         spread_out = jnp.broadcast_to(place.astype(jnp.float32), (ROWBLK, HD)).T
@@ -82,6 +84,7 @@
 def rope(kv_head, dest, places_all, key):
     rows = key.shape[0]
     blocks = rows // ROWBLK
+    steps = 4
     freq = yarn_frequencies(HD)
     freq = jnp.concatenate([freq, freq]).reshape(1, HD)
     whole = lambda shape: pl.BlockSpec(shape, lambda step, *refs: (0,) * len(shape))
@@ -90,13 +93,14 @@
         rope_kernel,
         grid_spec=pltpu.PrefetchScalarGridSpec(
             num_scalar_prefetch=2,
-            grid=(1,),
+            grid=(steps,),
             in_specs=[
                 whole(places_all.shape),
                 whole((1, HD)),
-                pl.BlockSpec((rows, HD), lambda step, at_ref, dest_ref: (0, at_ref[0])),
+                pl.BlockSpec((rows // steps, HD), lambda step, at_ref, dest_ref: (step, at_ref[0])),
             ],
-            out_specs=[whole((rows, HD))] * 3 + [whole((blocks, ROWBLK))],
+            out_specs=[pl.BlockSpec((rows // steps, HD), lambda step, *refs: (step, 0))] * 3
+            + [whole((blocks, ROWBLK))],
         ),
         out_shape=[
             table,
@@ -115,11 +119,7 @@
 def attend_kernel(
     heads,
     ranks,
-    target_ref,
-    source_ref,
-    run_ref,
-    slot_ref,
-    need_ref,
+    table_ref,
     query_ref,
     up_ref,
     up_t_ref,
@@ -132,6 +132,12 @@
     key_ref, value_ref, gkey_ref, gvalue_ref, key_win, value_win = refs[6:12]
     score_ref, prob_ref, gscore_ref, load_sems, sems = refs[12:]
     rows_each = query_ref.shape[0]
+    total_blocks = ranks * RUN_BLOCKS
+    target_ref = table_ref.at[pl.ds(0, total_blocks)]
+    source_ref = table_ref.at[pl.ds(total_blocks, total_blocks)]
+    run_ref, slot_ref, need_ref = (
+        table_ref.at[pl.ds(2 * total_blocks + at * RUN_BLOCKS, RUN_BLOCKS)] for at in range(3)
+    )
     half_blocks = ranks * RUN_BLOCKS // 2
     scale = 1.0 / math.sqrt(HD)
     to_exp2 = scale * math.log2(math.e)
@@ -288,7 +294,7 @@
             half,
             half,
         ),
-        in_specs=[smem] * 5 + [vmem] * 4 + [hbm] * (2 * ranks),
+        in_specs=[smem] + [vmem] * 4 + [hbm] * (2 * ranks),
         out_specs=(vmem, vmem, hbm, hbm, hbm, hbm),
         scratch_shapes=[pltpu.VMEM((every, HD), jnp.bfloat16)] * 2
         + [pltpu.VMEM((2, RUN_BLOCKS * ROWBLK, HD), jnp.bfloat16)] * 2
@@ -298,7 +304,7 @@
         + [pltpu.SemaphoreType.DMA((2, ranks)), pltpu.SemaphoreType.DMA((2, 2, RUN_BLOCKS))],
         compiler_params=pltpu.CompilerParams(vmem_limit_bytes=VMEM_BYTES),
         cost_estimate=NO_COST,
-    )(*tables, query, up, up_t, places, *keys, *values)
+    )(jnp.concatenate(tables), query, up, up_t, places, *keys, *values)
 
 
 def assemble_kernel(lanes, my_ref, *refs):
@@ -629,14 +635,14 @@
     weight_keep, weight_sends = chip_sum(weight_keep, swap(weight_send, 1))
     weight_received = exchange(weight_sends)
     value_near = hold(value_near, weight_sends[:1])
-    grad_query = turn_back(grad_query_t, cosine, sine, weight_sends[:1])
-    value_far = hold(value_far, [grad_query])
+    value_far = hold(value_far, weight_sends[:1])
     value_pieces = lane_pieces({0: value_near, far: value_far}, far // 2)
     value_all = assemble(my_lane, value_pieces)
     (key_partial,) = final_sum(
-        key_keep, key_received, (cosine, sine), [grad_query, value_far, value_pieces[1]]
-    )
-    key_far = hold(lane_swap(key_partial, far), weight_received)
+        key_keep, key_received, (cosine, sine), [value_far, value_pieces[1]]
+    )
+    grad_query = turn_back(grad_query_t, cosine, sine, [key_partial])
+    key_far = hold(lane_swap(key_partial, far), [*weight_received, grad_query])
     key_all = assemble(my_lane, lane_pieces({0: key_partial, far: key_far}, far // 2))
     weight_grad = weight_final(
         weight_keep, weight_received, 1.0 / rank_count, [key_far, value_all]

time: 144 us -> 148 us (1.028); the launches traced: 145 us -> 147 us
  starting transfers between devices: 37.8 us -> 35.1 us
  Pallas kernels: 58.7 us -> 60.9 us
  waiting for transfers between devices: 27 us -> 28.9 us
    ppermute x26, waiting for transfers between devices: 18.2 us -> 22.8 us  [swap(): lax.ppermute(array, 'dp', [(rank, rank ^ bit) for rank in range(ranks)])]
    ppermute x6, waiting for transfers between devices: 7 us -> 3.24 us  [lane_swap(): lax.ppermute(array, 'tensor', [(lane, lane ^ bit) for lane in range(lanes)])]
    ppermute x26, starting transfers between devices: 24.1 us -> 21.1 us  [swap(): lax.ppermute(array, 'dp', [(rank, rank ^ bit) for rank in range(ranks)])]
    pallas_call x1, Pallas kernels: 18.9 us -> 21 us  [attend(): pl.pallas_call(partial(attend_kernel, heads, ranks), out_shape=(jax.Shape...]
    unnamed x82 -> x74, local copies, waits for them, and re-layouts: 7.53 us -> 7.47 us
  transfers between devices with their start and end apart: 33 -> 33, of which waited for: 12 -> 9; matrix products, arithmetic and copies ran while one was open for 9% -> 9% of each run, Pallas kernels for 24% -> 24%
where the time goes in v14:
time: 148 us; the launch traced here: 147 us
  Pallas kernels  60.9 us (41%)
  starting transfers between devices  35.1 us (24%)
  waiting for transfers between devices  28.9 us (20%)
  other arithmetic  10.9 us (7%)
  local copies, waits for them, and re-layouts  9.79 us (7%)
    ppermute x26, waiting for transfers between devices, swap(): lax.ppermute(array, 'dp', [(rank, rank ^ bit) for rank in range(ranks)])  22.8 us
    ppermute x26, starting transfers between devices, swap(): lax.ppermute(array, 'dp', [(rank, rank ^ bit) for rank in range(ranks)])  21.1 us
    pallas_call x1, Pallas kernels, attend(): pl.pallas_call(partial(attend_kernel, heads, ranks), out_shape=(jax.Shape...  21 us
    ppermute x6, starting transfers between devices, lane_swap(): lax.ppermute(array, 'tensor', [(lane, lane ^ bit) for lane in range(lanes)])  9.74 us
    pallas_call x1, Pallas kernels, product(): pl.pallas_call(product_kernel, grid_spec=pltpu.PrefetchScalarGridSpec(num...  9.51 us
    pallas_call x1, Pallas kernels, prepare(): pl.pallas_call(prepare_kernel, grid=(steps,), out_shape=[jax.ShapeDtypeSt...  9.21 us
    unnamed x74, local copies, waits for them, and re-layouts  7.47 us
    pallas_call x1, Pallas kernels, rope(): pl.pallas_call(rope_kernel, grid_spec=pltpu.PrefetchScalarGridSpec(num_sc...  4.96 us
  transfers between devices with their start and end apart: 33, of which 9 were waited for; matrix products, arithmetic and copies ran while one was open for 9% of the time, Pallas kernels for 24%

profile of v14, /device:TPU:0, one launch (start us, length us, event | category | flops | bytes accessed | tf_op | source)
XLA Modules:
  0.0 146.7 jit_solution(5517276667747083677)
XLA Ops:
  1.9 4.0 %collective-permute-start.12 = (bf16[1024,128]{1,0:T(8,128)(2,1)S(1)}, bf16[1024,128]{1,0:T(8,128)(2,1)S(1)}, u32[]{:S(2)}, u32[]{:S(2)}) collective-permute-start(bf16[1024,128]{1,0:T(8,128)(2,1)S(1)} %constant_dynamic-slice_fusion.refs_8_), channel_id=1, source_target_pairs={{0,24},{4,28},{8,16},{12,20},{16,8},{20,12},{24,0},{28,4},{1,25},{... | collective-permute-start | bytes 786440 | tf_op jit(solution)/shard_map/ppermute | solution.py:354
  8.6 4.2 %all-to-all-start = ((s32[8,8,128]{2,1,0:T(8,128)}), s32[8,8,128]{2,1,0:T(8,128)S(1)}, u32[]{:S(2)}, u32[]{:S(2)}) async-start(s32[8,8,128]{2,1,0:T(8,128)} %broadcast_in_dim.27), calls=%async_computation | async-start | bytes 65536 | tf_op jit(solution)/shard_map/all_to_all | solution.py:589
  13.6 1.3 select_reduce_fusion.dest_ref
  15.6 2.8 %all-to-all-done = s32[8,8,128]{2,1,0:T(8,128)S(1)} async-done(((s32[8,8,128]{2,1,0:T(8,128)}), s32[8,8,128]{2,1,0:T(8,128)S(1)}, u32[]{:S(2)}, u32[]{:S(2)}) %all-to-all-start) | async-done | bytes 32800 | tf_op jit(solution)/shard_map/all_to_all | solution.py:589
  19.0 5.0 %shard_map.102 = (f32[1024,128]{1,0:T(8,128)}, f32[1024,128]{1,0:T(8,128)}, bf16[1024,128]{1,0:T(8,128)(2,1)}, s32[8,128]{1,0:T(8,128)}) custom-call(s32[1]{0:T(128)} %bitcast.at_ref, s32[8]{0:T(128)} %select_reduce_fusion.dest_ref, s32[64,128]{1,0:T(8,128)} %bitcast.11, f32[1,128]{1,0:T(1,128)} %maximum_bitcast_fusion.freq_ref, bf16[1024,512]{1,0:T(8,128)(2,1)} %key_ref.1), custom_call_target="tpu_custom_call" | custom-call | tf_op jit(solution)/shard_map/pallas_call | solution.py:92
  24.0 2.4 %collective-permute-start.5 = (bf16[1024,128]{1,0:T(8,128)(2,1)}, bf16[1024,128]{1,0:T(8,128)(2,1)S(1)}, u32[]{:S(2)}, u32[]{:S(2)}) collective-permute-start(bf16[1024,128]{1,0:T(8,128)(2,1)} %get-tuple-element.26.refs_0_), channel_id=1, source_target_pairs={{0,24},{4,28},{8,16},{12,20},{16,8},{20,12},{24,0},{28,4},{1,25},{... | collective-permute-start | bytes 786440 | tf_op jit(solution)/shard_map/ppermute | solution.py:354
  30.1 4.2 %collective-permute-done.5.refs_6_ = bf16[1024,128]{1,0:T(8,128)(2,1)S(1)} collective-permute-done((bf16[1024,128]{1,0:T(8,128)(2,1)}, bf16[1024,128]{1,0:T(8,128)(2,1)S(1)}, u32[]{:S(2)}, u32[]{:S(2)}) %collective-permute-start.5) | collective-permute-done | bytes 262176 | tf_op jit(solution)/shard_map/ppermute | solution.py:354
  34.3 4.6 %collective-permute-done.3.refs_4_ = bf16[1024,128]{1,0:T(8,128)(2,1)S(1)} collective-permute-done((bf16[1024,128]{1,0:T(8,128)(2,1)}, bf16[1024,128]{1,0:T(8,128)(2,1)S(1)}, u32[]{:S(2)}, u32[]{:S(2)}) %collective-permute-start.3) | collective-permute-done | bytes 262176 | tf_op jit(solution)/shard_map/ppermute | solution.py:354
  39.9 9.2 %shard_map.103 = (bf16[1024,512]{1,0:T(8,128)(2,1)}, bf16[512,1024]{1,0:T(8,128)(2,1)}, bf16[1024,512]{1,0:T(8,128)(2,1)}) custom-call(bf16[1024,3584]{1,0:T(8,128)(2,1)} %right_ref.1, bf16[3584,512]{1,0:T(8,128)(2,1)} %weight_ref.1, bf16[1024,512]{1,0:T(8,128)(2,1)} %query_ref.1, f32[1024,128]{1,0:T(8,128)} %get-tuple-element.24.cos_ref.refs_4_, ...), custom_call_target="tpu_custom_call" | custom-call | flops 3758096384 | bytes 7340032 | tf_op jit(solution)/shard_map/pallas_call | solution.py:432
  50.3 21.0 %shard_map.104 = (f32[512,1024]{1,0:T(8,128)}, bf16[512,1024]{1,0:T(8,128)(2,1)}, bf16[4096,128]{1,0:T(8,128)(2,1)}, bf16[4096,128]{1,0:T(8,128)(2,1)}, bf16[409...) custom-call(s32[152]{0:T(256)} %concatenate.14.table_ref, bf16[1024,512]{1,0:T(8,128)(2,1)} %get-tuple-element.27.query_ref, ...), custom_call_target="tpu_custom_call" | custom-call | tf_op jit(solution)/shard_map/pallas_call | solution.py:287
  72.5 2.6 %collective-permute-done.18 = bf16[4096,128]{1,0:T(8,128)(2,1)} collective-permute-done((bf16[4096,128]{1,0:T(8,128)(2,1)}, bf16[4096,128]{1,0:T(8,128)(2,1)}, u32[]{:S(2)}, u32[]{:S(2)}) %collective-permute-start.18) | collective-permute-done | bytes 1048608 | tf_op jit(solution)/shard_map/ppermute | solution.py:354
  75.1 2.6 %add_convert_fusion.3 = (bf16[1024,128]{1,0:T(8,128)(2,1)}, bf16[1024,128]{1,0:T(8,128)(2,1)}, f32[1024,128]{1,0:T(8,128)}, bf16[1024,128]{1,0:T(8,128)(2,1)S(1)}) fusion(bf16[4096,128]{1,0:T(8,128)(2,1)} %collective-permute-done.18, bf16[4096,128]{1,0:T(8,128)(2,1)} %get-tuple-element.34), kind=kLoop, calls=%fused_computation.4 | loop fusion | flops 1966080 | bytes 3407872 | tf_op jit(solution)/shard_map/convert_element_type | solution.py:376
  79.7 1.5 %collective-permute-start.19 = (bf16[1024,128]{1,0:T(8,128)(2,1)S(1)}, bf16[1024,128]{1,0:T(8,128)(2,1)S(1)}, u32[]{:S(2)}, u32[]{:S(2)}) collective-permute-start(bf16[1024,128]{1,0:T(8,128)(2,1)S(1)} %get-tuple-element.54.refs_0_), channel_id=1, source_target_pairs={{0,8},{4,12},{8,0},{12,4},{16,24},{20,28},{24,16},{28,20},{1,9},{5... | collective-permute-start | bytes 786440 | tf_op jit(solution)/shard_map/ppermute | solution.py:354
  82.4 9.5 %shard_map.105 = (bf16[4,448,512]{2,1,0:T(8,128)(2,1)}, bf16[4,448,512]{2,1,0:T(8,128)(2,1)}, f32[1024,128]{1,0:T(8,128)}) custom-call(s32[2]{0:T(128)} %pad_add_fusion.my_ref, bf16[512,1024]{1,0:T(8,128)(2,1)} %get-tuple-element.33.left_ref, bf16[1024,3584]{1,0:T(8,128)(2,1)} %right_ref.1, ...), custom_call_target="tpu_custom_call", output_to_operand_aliasing={{2}: (5, {})} | custom-call | tf_op jit(solution)/shard_map/pallas_call | solution.py:538
  93.4 2.2 %shard_map.106 = (bf16[1024,128]{1,0:T(8,128)(2,1)}, bf16[1024,128]{1,0:T(8,128)(2,1)}, bf16[4,448,512]{2,1,0:T(8,128)(2,1)}) custom-call(f32[1024,128]{1,0:T(8,128)} %get-tuple-element.36.refs_0_, bf16[1024,128]{1,0:T(8,128)(2,1)} %copy-done.33, bf16[1024,128]{1,0:T(8,128)(2,1)} %copy-done.31, ...), custom_call_target="tpu_custom_call", output_to_operand_aliasing={{2}: (4, {})} | custom-call | tf_op jit(solution)/shard_map/pallas_call | solution.py:398
  97.8 1.4 collective-permute-start.16
  99.2 2.6 %collective-permute-start.22 = (bf16[1024,128]{1,0:T(8,128)(2,1)}, bf16[1024,128]{1,0:T(8,128)(2,1)S(1)}, u32[]{:S(2)}, u32[]{:S(2)}) collective-permute-start(bf16[1024,128]{1,0:T(8,128)(2,1)} %get-tuple-element.38), channel_id=1, source_target_pairs={{0,2},{1,3},{2,0},{3,1},{4,6},{5,7},{6,4},{7,5},{8,10},{9,11},{10,... | collective-permute-start | bytes 786440 | tf_op jit(solution)/shard_map/ppermute | solution.py:341
  101.8 1.7 %convert_add_fusion = (f32[1,448,512]{2,1,0:T(8,128)}, bf16[1,448,512]{2,1,0:T(8,128)(2,1)}, bf16[1,448,512]{2,1,0:T(8,128)(2,1)}, bf16[1,448,512]{2,1,0:T(8,128)(2,1)}) fusion(bf16[4,448,512]{2,1,0:T(8,128)(2,1)S(1)} %collective-permute-done.23, bf16[4,448,512]{2,1,0:T(8,128)(2,1)S(1)} %copy-done.8), kind=kLoop, calls=%fused_computation | loop fusion | flops 3440640 | bytes 5963776 | tf_op jit(solution)/shard_map/add | solution.py:366
  103.5 1.6 %collective-permute-start.24 = (bf16[1024,128]{1,0:T(8,128)(2,1)}, bf16[1024,128]{1,0:T(8,128)(2,1)S(1)}, u32[]{:S(2)}, u32[]{:S(2)}) collective-permute-start(bf16[1024,128]{1,0:T(8,128)(2,1)} %shard_map.108.refs_0_), channel_id=1, source_target_pairs={{0,1},{1,0},{2,3},{3,2},{4,5},{5,4},{6,7},{7,6},{8,9},{9,8},{10,11... | collective-permute-start | bytes 786440 | tf_op jit(solution)/shard_map/ppermute | solution.py:341
  105.1 5.1 %collective-permute-done.17.refs_3_ = bf16[1024,128]{1,0:T(8,128)(2,1)S(1)} collective-permute-done((bf16[1024,128]{1,0:T(8,128)(2,1)S(1)}, bf16[1024,128]{1,0:T(8,128)(2,1)S(1)}, u32[]{:S(2)}, u32[]{:S(2)}) %collective-permute-start.17) | collective-permute-done | bytes 262176 | tf_op jit(solution)/shard_map/ppermute | solution.py:354
  110.2 1.7 %collective-permute-start.29 = (bf16[1,448,512]{2,1,0:T(8,128)(2,1)}, bf16[1,448,512]{2,1,0:T(8,128)(2,1)S(1)}, u32[]{:S(2)}, u32[]{:S(2)}) collective-permute-start(bf16[1,448,512]{2,1,0:T(8,128)(2,1)} %get-tuple-element.48), channel_id=1, source_target_pairs={{0,24},{4,28},{8,16},{12,20},{16,8},{20,12},{24,0},{28,4},{1,25},{... | collective-permute-start | bytes 1376264 | tf_op jit(solution)/shard_map/ppermute | solution.py:354
  112.6 1.2 collective-permute-start.28
  116.5 2.5 %shard_map.109.refs_0_ = bf16[1024,128]{1,0:T(8,128)(2,1)} custom-call(f32[1024,128]{1,0:T(8,128)} %get-tuple-element.58.refs_0_, bf16[1024,128]{1,0:T(8,128)(2,1)} %copy-done.23, bf16[1024,128]{1,0:T(8,128)(2,1)} %copy-done.26, bf16[1024,128]{1,0:T(8,128)(2,1)} %copy-done.24, f32[1024,128]{1,0:T(8,128)} %get-tuple-element.24.cos_ref.refs_4_, ...), custom_call_target="tpu_custom_call" | custom-call | tf_op jit(solution)/shard_map/pallas_call | solution.py:398
  119.0 1.6 %collective-permute-start.26 = (bf16[1024,128]{1,0:T(8,128)(2,1)}, bf16[1024,128]{1,0:T(8,128)(2,1)S(1)}, u32[]{:S(2)}, u32[]{:S(2)}) collective-permute-start(bf16[1024,128]{1,0:T(8,128)(2,1)} %shard_map.109.refs_0_), channel_id=1, source_target_pairs={{0,2},{1,3},{2,0},{3,1},{4,6},{5,7},{6,4},{7,5},{8,10},{9,11},{10,... | collective-permute-start | bytes 786440 | tf_op jit(solution)/shard_map/ppermute | solution.py:341
  120.5 2.3 %collective-permute-start.31 = (bf16[1024,128]{1,0:T(8,128)(2,1)S(1)}, bf16[1024,128]{1,0:T(8,128)(2,1)}, u32[]{:S(2)}, u32[]{:S(2)}) collective-permute-start(bf16[1024,128]{1,0:T(8,128)(2,1)S(1)} %copy-done.4), channel_id=1, source_target_pairs={{0,1},{1,0},{2,3},{3,2},{4,5},{5,4},{6,7},{7,6},{8,9},{9,8},{10,11... | collective-permute-start | bytes 786440 | tf_op jit(solution)/shard_map/ppermute | solution.py:341
  122.9 4.5 %shard_map.110.refs_4_ = bf16[1024,512]{1,0:T(8,128)(2,1)} custom-call(f32[512,1024]{1,0:T(8,128)} %get-tuple-element.30.grad_ref, f32[1024,128]{1,0:T(8,128)} %get-tuple-element.24.cos_ref.refs_4_, f32[1024,128]{1,0:T(8,128)} %get-tuple-element.25.sin_ref.refs_5_, bf16[1024,128]{1,0:T(8,128)(2,1)} %shard_map.109.refs_0_), custom_call_target="tpu_custom_call" | custom-call | tf_op jit(solution)/shard_map/pallas_call | solution.py:473
  127.4 5.7 %collective-permute-done.28.refs_2_ = bf16[1,448,512]{2,1,0:T(8,128)(2,1)S(1)} collective-permute-done((bf16[1,448,512]{2,1,0:T(8,128)(2,1)}, bf16[1,448,512]{2,1,0:T(8,128)(2,1)S(1)}, u32[]{:S(2)}, u32[]{:S(2)}) %collective-permute-start.28) | collective-permute-done | bytes 458784 | tf_op jit(solution)/shard_map/ppermute | solution.py:354
  134.8 1.6 %collective-permute-start.30 = (bf16[1024,128]{1,0:T(8,128)(2,1)}, bf16[1024,128]{1,0:T(8,128)(2,1)S(1)}, u32[]{:S(2)}, u32[]{:S(2)}) collective-permute-start(bf16[1024,128]{1,0:T(8,128)(2,1)} %shard_map.111.refs_2_.refs_4_), channel_id=1, source_target_pairs={{0,1},{1,0},{2,3},{3,2},{4,5},{5,4},{6,7},{7,6},{8,9},{9,8},{10,11... | collective-permute-start | bytes 786440 | tf_op jit(solution)/shard_map/ppermute | solution.py:341
  136.4 2.2 %shard_map.113.refs_5_ = bf16[1024,512]{1,0:T(8,128)(2,1)} custom-call(s32[1]{0:T(128)} %bitcast.6.my_ref, bf16[1024,128]{1,0:T(8,128)(2,1)} %shard_map.108.refs_0_, bf16[1024,128]{1,0:T(8,128)(2,1)} %copy-done.9, bf16[1024,128]{1,0:T(8,128)(2,1)} %shard_map.107.refs_6_.refs_2_, bf16[1024,128]{1,0:T(8,128)(2,1)} %collective-permute-done.31.refs_3_), custom_call_target="tpu_custom_call" | custom-call | tf_op jit(solution)/shard_map/pallas_call | solution.py:328
  138.6 2.7 %shard_map.114 = f32[448,512]{1,0:T(8,128)} custom-call(f32[1,448,512]{2,1,0:T(8,128)} %get-tuple-element.47.refs_0_, bf16[1,448,512]{2,1,0:T(8,128)(2,1)} %copy-done.7, bf16[1,448,512]{2,1,0:T(8,128)(2,1)} %copy-done.6, bf16[1,448,512]{2,1,0:T(8,128)(2,1)} %copy-done.5, bf16[1024,128]{1,0:T(8,128)(2,1)} %shard_map.111.refs_2_.refs_4_, ...), custom_call_target="tpu_custom_call" | custom-call | tf_op jit(solution)/shard_map/pallas_call | solution.py:567
  141.3 2.3 %collective-permute-done.30.refs_3_ = bf16[1024,128]{1,0:T(8,128)(2,1)S(1)} collective-permute-done((bf16[1024,128]{1,0:T(8,128)(2,1)}, bf16[1024,128]{1,0:T(8,128)(2,1)S(1)}, u32[]{:S(2)}, u32[]{:S(2)}) %collective-permute-start.30) | collective-permute-done | bytes 262176 | tf_op jit(solution)/shard_map/ppermute | solution.py:341
  144.3 2.2 %shard_map.112 = bf16[1024,512]{1,0:T(8,128)(2,1)} custom-call(s32[1]{0:T(128)} %bitcast.6.my_ref, bf16[1024,128]{1,0:T(8,128)(2,1)} %shard_map.109.refs_0_, bf16[1024,128]{1,0:T(8,128)(2,1)} %copy-done.32, bf16[1024,128]{1,0:T(8,128)(2,1)} %shard_map.111.refs_2_.refs_4_, bf16[1024,128]{1,0:T(8,128)(2,1)} %copy-done.34), custom_call_target="tpu_custom_call" | custom-call | tf_op jit(solution)/shard_map/pallas_call | solution.py:328
  (143 shorter events, 25.6 us)
Async XLA Ops:
  1.9 24.5 %collective-permute-start.12 = (bf16[1024,128]{1,0:T(8,128)(2,1)S(1)}, bf16[1024,128]{1,0:T(8,128)(2,1)S(1)}, u32[]{:S(2)}, u32[]{:S(2)}) collective-permute-start(bf16[1024,128]{1,0:T(8,128)(2,1)S(1)} %constant_dynamic-slice_fusion.refs_8_), channel_id=1, source_target_pairs={{0,24},{4,28},{8,16},{12,20},{16,8},{20,12},{24,0},{28,4},{1,25},{... | collective-permute-start | bytes 786440 | tf_op jit(solution)/shard_map/ppermute | solution.py:354
  5.9 21.1 %collective-permute-start.10 = (bf16[1024,128]{1,0:T(8,128)(2,1)S(1)}, bf16[1024,128]{1,0:T(8,128)(2,1)S(1)}, u32[]{:S(2)}, u32[]{:S(2)}) collective-permute-start(bf16[1024,128]{1,0:T(8,128)(2,1)S(1)} %constant_dynamic-slice_fusion.refs_8_), channel_id=1, source_target_pairs={{0,16},{4,20},{8,24},{12,28},{16,0},{20,4},{24,8},{28,12},{1,17},{... | collective-permute-start | bytes 786440 | tf_op jit(solution)/shard_map/ppermute | solution.py:354
  6.4 21.1 %collective-permute-start.8 = (bf16[1024,128]{1,0:T(8,128)(2,1)S(1)}, bf16[1024,128]{1,0:T(8,128)(2,1)S(1)}, u32[]{:S(2)}, u32[]{:S(2)}) collective-permute-start(bf16[1024,128]{1,0:T(8,128)(2,1)S(1)} %constant_dynamic-slice_fusion.refs_8_), channel_id=1, source_target_pairs={{0,8},{4,12},{8,0},{12,4},{16,24},{20,28},{24,16},{28,20},{1,9},{5... | collective-permute-start | bytes 786440 | tf_op jit(solution)/shard_map/ppermute | solution.py:354
  6.5 21.0 %collective-permute-start.7 = (bf16[1024,128]{1,0:T(8,128)(2,1)S(1)}, bf16[1024,128]{1,0:T(8,128)(2,1)S(1)}, u32[]{:S(2)}, u32[]{:S(2)}) collective-permute-start(bf16[1024,128]{1,0:T(8,128)(2,1)S(1)} %constant_dynamic-slice_fusion.refs_8_), channel_id=1, source_target_pairs={{0,4},{4,0},{8,12},{12,8},{16,20},{20,16},{24,28},{28,24},{1,5},{5... | collective-permute-start | bytes 786440 | tf_op jit(solution)/shard_map/ppermute | solution.py:354
  8.6 9.8 %all-to-all-start = ((s32[8,8,128]{2,1,0:T(8,128)}), s32[8,8,128]{2,1,0:T(8,128)S(1)}, u32[]{:S(2)}, u32[]{:S(2)}) async-start(s32[8,8,128]{2,1,0:T(8,128)} %broadcast_in_dim.27), calls=%async_computation | async-start | bytes 65536 | tf_op jit(solution)/shard_map/all_to_all | solution.py:589
  24.0 10.3 %collective-permute-start.5 = (bf16[1024,128]{1,0:T(8,128)(2,1)}, bf16[1024,128]{1,0:T(8,128)(2,1)S(1)}, u32[]{:S(2)}, u32[]{:S(2)}) collective-permute-start(bf16[1024,128]{1,0:T(8,128)(2,1)} %get-tuple-element.26.refs_0_), channel_id=1, source_target_pairs={{0,24},{4,28},{8,16},{12,20},{16,8},{20,12},{24,0},{28,4},{1,25},{... | collective-permute-start | bytes 786440 | tf_op jit(solution)/shard_map/ppermute | solution.py:354
  26.4 12.5 %collective-permute-start.3 = (bf16[1024,128]{1,0:T(8,128)(2,1)}, bf16[1024,128]{1,0:T(8,128)(2,1)S(1)}, u32[]{:S(2)}, u32[]{:S(2)}) collective-permute-start(bf16[1024,128]{1,0:T(8,128)(2,1)} %get-tuple-element.26.refs_0_), channel_id=1, source_target_pairs={{0,16},{4,20},{8,24},{12,28},{16,0},{20,4},{24,8},{28,12},{1,17},{... | collective-permute-start | bytes 786440 | tf_op jit(solution)/shard_map/ppermute | solution.py:354
  27.0 12.0 %collective-permute-start.1 = (bf16[1024,128]{1,0:T(8,128)(2,1)}, bf16[1024,128]{1,0:T(8,128)(2,1)S(1)}, u32[]{:S(2)}, u32[]{:S(2)}) collective-permute-start(bf16[1024,128]{1,0:T(8,128)(2,1)} %get-tuple-element.26.refs_0_), channel_id=1, source_target_pairs={{0,8},{4,12},{8,0},{12,4},{16,24},{20,28},{24,16},{28,20},{1,9},{5... | collective-permute-start | bytes 786440 | tf_op jit(solution)/shard_map/ppermute | solution.py:354
  27.5 11.9 %collective-permute-start = (bf16[1024,128]{1,0:T(8,128)(2,1)}, bf16[1024,128]{1,0:T(8,128)(2,1)S(1)}, u32[]{:S(2)}, u32[]{:S(2)}) collective-permute-start(bf16[1024,128]{1,0:T(8,128)(2,1)} %get-tuple-element.26.refs_0_), channel_id=1, source_target_pairs={{0,4},{4,0},{8,12},{12,8},{16,20},{20,16},{24,28},{28,24},{1,5},{5... | collective-permute-start | bytes 786440 | tf_op jit(solution)/shard_map/ppermute | solution.py:354
  27.5 12.0 %collective-permute-start.13 = (bf16[1024,128]{1,0:T(8,128)(2,1)S(1)}, bf16[1024,128]{1,0:T(8,128)(2,1)}, u32[]{:S(2)}, u32[]{:S(2)}) collective-permute-start(bf16[1024,128]{1,0:T(8,128)(2,1)S(1)} %collective-permute-done.12.refs_14_), channel_id=1, source_target_pairs={{0,4},{4,0},{8,12},{12,8},{16,20},{20,16},{24,28},{28,24},{1,5},{5... | collective-permute-start | bytes 786440 | tf_op jit(solution)/shard_map/ppermute | solution.py:354
  34.3 14.9 %collective-permute-start.11 = (bf16[1024,128]{1,0:T(8,128)(2,1)S(1)}, bf16[1024,128]{1,0:T(8,128)(2,1)S(1)}, u32[]{:S(2)}, u32[]{:S(2)}) collective-permute-start(bf16[1024,128]{1,0:T(8,128)(2,1)S(1)} %collective-permute-done.10.refs_12_), channel_id=1, source_target_pairs={{0,4},{4,0},{8,12},{12,8},{16,20},{20,16},{24,28},{28,24},{1,5},{5... | collective-permute-start | bytes 786440 | tf_op jit(solution)/shard_map/ppermute | solution.py:354
  38.9 10.4 %collective-permute-start.9 = (bf16[1024,128]{1,0:T(8,128)(2,1)S(1)}, bf16[1024,128]{1,0:T(8,128)(2,1)S(1)}, u32[]{:S(2)}, u32[]{:S(2)}) collective-permute-start(bf16[1024,128]{1,0:T(8,128)(2,1)S(1)} %collective-permute-done.8.refs_10_), channel_id=1, source_target_pairs={{0,4},{4,0},{8,12},{12,8},{16,20},{20,16},{24,28},{28,24},{1,5},{5... | collective-permute-start | bytes 786440 | tf_op jit(solution)/shard_map/ppermute | solution.py:354
  38.9 10.3 %collective-permute-start.6 = (bf16[1024,128]{1,0:T(8,128)(2,1)S(1)}, bf16[1024,128]{1,0:T(8,128)(2,1)S(1)}, u32[]{:S(2)}, u32[]{:S(2)}) collective-permute-start(bf16[1024,128]{1,0:T(8,128)(2,1)S(1)} %collective-permute-done.5.refs_6_), channel_id=1, source_target_pairs={{0,4},{4,0},{8,12},{12,8},{16,20},{20,16},{24,28},{28,24},{1,5},{5... | collective-permute-start | bytes 786440 | tf_op jit(solution)/shard_map/ppermute | solution.py:354
  39.4 9.9 %collective-permute-start.4 = (bf16[1024,128]{1,0:T(8,128)(2,1)S(1)}, bf16[1024,128]{1,0:T(8,128)(2,1)S(1)}, u32[]{:S(2)}, u32[]{:S(2)}) collective-permute-start(bf16[1024,128]{1,0:T(8,128)(2,1)S(1)} %collective-permute-done.3.refs_4_), channel_id=1, source_target_pairs={{0,4},{4,0},{8,12},{12,8},{16,20},{20,16},{24,28},{28,24},{1,5},{5... | collective-permute-start | bytes 786440 | tf_op jit(solution)/shard_map/ppermute | solution.py:354
  39.5 9.8 %collective-permute-start.2 = (bf16[1024,128]{1,0:T(8,128)(2,1)S(1)}, bf16[1024,128]{1,0:T(8,128)(2,1)S(1)}, u32[]{:S(2)}, u32[]{:S(2)}) collective-permute-start(bf16[1024,128]{1,0:T(8,128)(2,1)S(1)} %collective-permute-done.1.refs_2_), channel_id=1, source_target_pairs={{0,4},{4,0},{8,12},{12,8},{16,20},{20,16},{24,28},{28,24},{1,5},{5... | collective-permute-start | bytes 786440 | tf_op jit(solution)/shard_map/ppermute | solution.py:354
  71.4 9.8 %collective-permute-start.14 = (bf16[4096,128]{1,0:T(8,128)(2,1)}, bf16[4096,128]{1,0:T(8,128)(2,1)S(1)}, u32[]{:S(2)}, u32[]{:S(2)}) collective-permute-start(bf16[4096,128]{1,0:T(8,128)(2,1)} %get-tuple-element.32), channel_id=1, source_target_pairs={{0,4},{4,0},{8,12},{12,8},{16,20},{20,16},{24,28},{28,24},{1,5},{5... | collective-permute-start | bytes 3145736 | tf_op jit(solution)/shard_map/ppermute | solution.py:354
  77.7 14.2 %collective-permute-start.21 = (bf16[1024,128]{1,0:T(8,128)(2,1)}, bf16[1024,128]{1,0:T(8,128)(2,1)S(1)}, u32[]{:S(2)}, u32[]{:S(2)}) collective-permute-start(bf16[1024,128]{1,0:T(8,128)(2,1)} %get-tuple-element.51), channel_id=1, source_target_pairs={{0,24},{4,28},{8,16},{12,20},{16,8},{20,12},{24,0},{28,4},{1,25},{... | collective-permute-start | bytes 786440 | tf_op jit(solution)/shard_map/ppermute | solution.py:354
  78.7 13.9 %collective-permute-start.20 = (bf16[1024,128]{1,0:T(8,128)(2,1)}, bf16[1024,128]{1,0:T(8,128)(2,1)S(1)}, u32[]{:S(2)}, u32[]{:S(2)}) collective-permute-start(bf16[1024,128]{1,0:T(8,128)(2,1)} %get-tuple-element.52), channel_id=1, source_target_pairs={{0,16},{4,20},{8,24},{12,28},{16,0},{20,4},{24,8},{28,12},{1,17},{... | collective-permute-start | bytes 786440 | tf_op jit(solution)/shard_map/ppermute | solution.py:354
  79.7 12.9 %collective-permute-start.19 = (bf16[1024,128]{1,0:T(8,128)(2,1)S(1)}, bf16[1024,128]{1,0:T(8,128)(2,1)S(1)}, u32[]{:S(2)}, u32[]{:S(2)}) collective-permute-start(bf16[1024,128]{1,0:T(8,128)(2,1)S(1)} %get-tuple-element.54.refs_0_), channel_id=1, source_target_pairs={{0,8},{4,12},{8,0},{12,4},{16,24},{20,28},{24,16},{28,20},{1,9},{5... | collective-permute-start | bytes 786440 | tf_op jit(solution)/shard_map/ppermute | solution.py:354
  95.6 6.2 %collective-permute-start.23 = (bf16[4,448,512]{2,1,0:T(8,128)(2,1)}, bf16[4,448,512]{2,1,0:T(8,128)(2,1)S(1)}, u32[]{:S(2)}, u32[]{:S(2)}) collective-permute-start(bf16[4,448,512]{2,1,0:T(8,128)(2,1)} %get-tuple-element.40), channel_id=1, source_target_pairs={{0,4},{4,0},{8,12},{12,8},{16,20},{20,16},{24,28},{28,24},{1,5},{5... | collective-permute-start | bytes 5505032 | tf_op jit(solution)/shard_map/ppermute | solution.py:354
  95.6 19.2 %collective-permute-start.15 = (bf16[1024,128]{1,0:T(8,128)(2,1)S(1)}, bf16[1024,128]{1,0:T(8,128)(2,1)S(1)}, u32[]{:S(2)}, u32[]{:S(2)}) collective-permute-start(bf16[1024,128]{1,0:T(8,128)(2,1)S(1)} %copy-done.12), channel_id=1, source_target_pairs={{0,8},{4,12},{8,0},{12,4},{16,24},{20,28},{24,16},{28,20},{1,9},{5... | collective-permute-start | bytes 786440 | tf_op jit(solution)/shard_map/ppermute | solution.py:354
  96.6 13.6 %collective-permute-start.17 = (bf16[1024,128]{1,0:T(8,128)(2,1)S(1)}, bf16[1024,128]{1,0:T(8,128)(2,1)S(1)}, u32[]{:S(2)}, u32[]{:S(2)}) collective-permute-start(bf16[1024,128]{1,0:T(8,128)(2,1)S(1)} %copy-done.35), channel_id=1, source_target_pairs={{0,24},{4,28},{8,16},{12,20},{16,8},{20,12},{24,0},{28,4},{1,25},{... | collective-permute-start | bytes 786440 | tf_op jit(solution)/shard_map/ppermute | solution.py:354
  97.8 14.0 %collective-permute-start.16 = (bf16[1024,128]{1,0:T(8,128)(2,1)}, bf16[1024,128]{1,0:T(8,128)(2,1)S(1)}, u32[]{:S(2)}, u32[]{:S(2)}) collective-permute-start(bf16[1024,128]{1,0:T(8,128)(2,1)} %get-tuple-element.56), channel_id=1, source_target_pairs={{0,16},{4,20},{8,24},{12,28},{16,0},{20,4},{24,8},{28,12},{1,17},{... | collective-permute-start | bytes 786440 | tf_op jit(solution)/shard_map/ppermute | solution.py:354
  99.2 14.7 %collective-permute-start.22 = (bf16[1024,128]{1,0:T(8,128)(2,1)}, bf16[1024,128]{1,0:T(8,128)(2,1)S(1)}, u32[]{:S(2)}, u32[]{:S(2)}) collective-permute-start(bf16[1024,128]{1,0:T(8,128)(2,1)} %get-tuple-element.38), channel_id=1, source_target_pairs={{0,2},{1,3},{2,0},{3,1},{4,6},{5,7},{6,4},{7,5},{8,10},{9,11},{10,... | collective-permute-start | bytes 786440 | tf_op jit(solution)/shard_map/ppermute | solution.py:341
  103.5 12.2 %collective-permute-start.24 = (bf16[1024,128]{1,0:T(8,128)(2,1)}, bf16[1024,128]{1,0:T(8,128)(2,1)S(1)}, u32[]{:S(2)}, u32[]{:S(2)}) collective-permute-start(bf16[1024,128]{1,0:T(8,128)(2,1)} %shard_map.108.refs_0_), channel_id=1, source_target_pairs={{0,1},{1,0},{2,3},{3,2},{4,5},{5,4},{6,7},{7,6},{8,9},{9,8},{10,11... | collective-permute-start | bytes 786440 | tf_op jit(solution)/shard_map/ppermute | solution.py:341
  110.2 17.2 %collective-permute-start.29 = (bf16[1,448,512]{2,1,0:T(8,128)(2,1)}, bf16[1,448,512]{2,1,0:T(8,128)(2,1)S(1)}, u32[]{:S(2)}, u32[]{:S(2)}) collective-permute-start(bf16[1,448,512]{2,1,0:T(8,128)(2,1)} %get-tuple-element.48), channel_id=1, source_target_pairs={{0,24},{4,28},{8,16},{12,20},{16,8},{20,12},{24,0},{28,4},{1,25},{... | collective-permute-start | bytes 1376264 | tf_op jit(solution)/shard_map/ppermute | solution.py:354
  112.6 20.6 %collective-permute-start.28 = (bf16[1,448,512]{2,1,0:T(8,128)(2,1)}, bf16[1,448,512]{2,1,0:T(8,128)(2,1)S(1)}, u32[]{:S(2)}, u32[]{:S(2)}) collective-permute-start(bf16[1,448,512]{2,1,0:T(8,128)(2,1)} %get-tuple-element.49), channel_id=1, source_target_pairs={{0,16},{4,20},{8,24},{12,28},{16,0},{20,4},{24,8},{28,12},{1,17},{... | collective-permute-start | bytes 1376264 | tf_op jit(solution)/shard_map/ppermute | solution.py:354
  113.8 19.3 %collective-permute-start.27 = (bf16[1,448,512]{2,1,0:T(8,128)(2,1)}, bf16[1,448,512]{2,1,0:T(8,128)(2,1)S(1)}, u32[]{:S(2)}, u32[]{:S(2)}) collective-permute-start(bf16[1,448,512]{2,1,0:T(8,128)(2,1)} %get-tuple-element.50.refs_1_), channel_id=1, source_target_pairs={{0,8},{4,12},{8,0},{12,4},{16,24},{20,28},{24,16},{28,20},{1,9},{5... | collective-permute-start | bytes 1376264 | tf_op jit(solution)/shard_map/ppermute | solution.py:354
  119.0 14.1 %collective-permute-start.26 = (bf16[1024,128]{1,0:T(8,128)(2,1)}, bf16[1024,128]{1,0:T(8,128)(2,1)S(1)}, u32[]{:S(2)}, u32[]{:S(2)}) collective-permute-start(bf16[1024,128]{1,0:T(8,128)(2,1)} %shard_map.109.refs_0_), channel_id=1, source_target_pairs={{0,2},{1,3},{2,0},{3,1},{4,6},{5,7},{6,4},{7,5},{8,10},{9,11},{10,... | collective-permute-start | bytes 786440 | tf_op jit(solution)/shard_map/ppermute | solution.py:341
  120.5 15.8 %collective-permute-start.31 = (bf16[1024,128]{1,0:T(8,128)(2,1)S(1)}, bf16[1024,128]{1,0:T(8,128)(2,1)}, u32[]{:S(2)}, u32[]{:S(2)}) collective-permute-start(bf16[1024,128]{1,0:T(8,128)(2,1)S(1)} %copy-done.4), channel_id=1, source_target_pairs={{0,1},{1,0},{2,3},{3,2},{4,5},{5,4},{6,7},{7,6},{8,9},{9,8},{10,11... | collective-permute-start | bytes 786440 | tf_op jit(solution)/shard_map/ppermute | solution.py:341
  127.3 13.9 %collective-permute-start.25 = (bf16[1024,128]{1,0:T(8,128)(2,1)S(1)}, bf16[1024,128]{1,0:T(8,128)(2,1)S(1)}, u32[]{:S(2)}, u32[]{:S(2)}) collective-permute-start(bf16[1024,128]{1,0:T(8,128)(2,1)S(1)} %copy-done.1), channel_id=1, source_target_pairs={{0,1},{1,0},{2,3},{3,2},{4,5},{5,4},{6,7},{7,6},{8,9},{9,8},{10,11... | collective-permute-start | bytes 786440 | tf_op jit(solution)/shard_map/ppermute | solution.py:341
  134.8 8.8 %collective-permute-start.30 = (bf16[1024,128]{1,0:T(8,128)(2,1)}, bf16[1024,128]{1,0:T(8,128)(2,1)S(1)}, u32[]{:S(2)}, u32[]{:S(2)}) collective-permute-start(bf16[1024,128]{1,0:T(8,128)(2,1)} %shard_map.111.refs_2_.refs_4_), channel_id=1, source_target_pairs={{0,1},{1,0},{2,3},{3,2},{4,5},{5,4},{6,7},{7,6},{8,9},{9,8},{10,11... | collective-permute-start | bytes 786440 | tf_op jit(solution)/shard_map/ppermute | solution.py:341
  (38 other events, 254.3 us)

commit v15 on v13

--- a/solution.py
+++ b/solution.py
@@ -629,14 +629,14 @@
     weight_keep, weight_sends = chip_sum(weight_keep, swap(weight_send, 1))
     weight_received = exchange(weight_sends)
     value_near = hold(value_near, weight_sends[:1])
-    grad_query = turn_back(grad_query_t, cosine, sine, weight_sends[:1])
-    value_far = hold(value_far, [grad_query])
+    value_far = hold(value_far, weight_sends[:1])
     value_pieces = lane_pieces({0: value_near, far: value_far}, far // 2)
     value_all = assemble(my_lane, value_pieces)
     (key_partial,) = final_sum(
-        key_keep, key_received, (cosine, sine), [grad_query, value_far, value_pieces[1]]
-    )
-    key_far = hold(lane_swap(key_partial, far), weight_received)
+        key_keep, key_received, (cosine, sine), [value_far, value_pieces[1]]
+    )
+    grad_query = turn_back(grad_query_t, cosine, sine, [key_partial])
+    key_far = hold(lane_swap(key_partial, far), [*weight_received, grad_query])
     key_all = assemble(my_lane, lane_pieces({0: key_partial, far: key_far}, far // 2))
     weight_grad = weight_final(
         weight_keep, weight_received, 1.0 / rank_count, [key_far, value_all]

time: 144 us -> 139 us (0.965); the launches traced: 145 us -> 138 us
  waiting for transfers between devices: 27 us -> 20.6 us
    ppermute x6, waiting for transfers between devices: 7 us -> 2.23 us  [lane_swap(): lax.ppermute(array, 'tensor', [(lane, lane ^ bit) for lane in range(lanes)])]
    ppermute x26, waiting for transfers between devices: 18.2 us -> 16.5 us  [swap(): lax.ppermute(array, 'dp', [(rank, rank ^ bit) for rank in range(ranks)])]
    unnamed x82 -> x80, local copies, waits for them, and re-layouts: 7.53 us -> 7.06 us
  transfers between devices with their start and end apart: 33 -> 33, of which waited for: 12 -> 11; matrix products, arithmetic and copies ran while one was open for 9% -> 9% of each run, Pallas kernels for 24% -> 26%
where the time goes in v15:
time: 139 us; the launch traced here: 138 us
  Pallas kernels  58.5 us (42%)
  starting transfers between devices  38.5 us (28%)
  waiting for transfers between devices  20.6 us (15%)
  other arithmetic  11.7 us (8%)
  local copies, waits for them, and re-layouts  8.02 us (6%)
    ppermute x26, starting transfers between devices, swap(): lax.ppermute(array, 'dp', [(rank, rank ^ bit) for rank in range(ranks)])  23.9 us
    pallas_call x1, Pallas kernels, attend(): pl.pallas_call(partial(attend_kernel, heads, ranks), out_shape=(jax.Shape...  18.7 us
    ppermute x26, waiting for transfers between devices, swap(): lax.ppermute(array, 'dp', [(rank, rank ^ bit) for rank in range(ranks)])  16.5 us
    ppermute x6, starting transfers between devices, lane_swap(): lax.ppermute(array, 'tensor', [(lane, lane ^ bit) for lane in range(lanes)])  10.4 us
    pallas_call x1, Pallas kernels, product(): pl.pallas_call(product_kernel, grid_spec=pltpu.PrefetchScalarGridSpec(num...  9.51 us
    pallas_call x1, Pallas kernels, prepare(): pl.pallas_call(prepare_kernel, grid=(steps,), out_shape=[jax.ShapeDtypeSt...  9.22 us
    unnamed x80, local copies, waits for them, and re-layouts  7.06 us
    pallas_call x1, Pallas kernels, rope(): pl.pallas_call(rope_kernel, grid_spec=pltpu.PrefetchScalarGridSpec(num_sc...  4.8 us
  transfers between devices with their start and end apart: 33, of which 11 were waited for; matrix products, arithmetic and copies ran while one was open for 9% of the time, Pallas kernels for 26%

profile of v15, /device:TPU:0, one launch (start us, length us, event | category | flops | bytes accessed | tf_op | source)
XLA Modules:
  0.0 138.4 jit_solution(14230768114285015819)
XLA Ops:
  1.9 4.0 %collective-permute-start.12 = (bf16[1024,128]{1,0:T(8,128)(2,1)S(1)}, bf16[1024,128]{1,0:T(8,128)(2,1)S(1)}, u32[]{:S(2)}, u32[]{:S(2)}) collective-permute-start(bf16[1024,128]{1,0:T(8,128)(2,1)S(1)} %constant_dynamic-slice_fusion.refs_8_), channel_id=1, source_target_pairs={{0,24},{4,28},{8,16},{12,20},{16,8},{20,12},{24,0},{28,4},{1,25},{... | collective-permute-start | bytes 786440 | tf_op jit(solution)/shard_map/ppermute | solution.py:348
  8.6 4.2 %all-to-all-start = ((s32[8,8,128]{2,1,0:T(8,128)}), s32[8,8,128]{2,1,0:T(8,128)S(1)}, u32[]{:S(2)}, u32[]{:S(2)}) async-start(s32[8,8,128]{2,1,0:T(8,128)} %broadcast_in_dim.27), calls=%async_computation | async-start | bytes 65536 | tf_op jit(solution)/shard_map/all_to_all | solution.py:583
  14.6 1.4 select_reduce_fusion.dest_ref
  16.6 1.8 %all-to-all-done = s32[8,8,128]{2,1,0:T(8,128)S(1)} async-done(((s32[8,8,128]{2,1,0:T(8,128)}), s32[8,8,128]{2,1,0:T(8,128)S(1)}, u32[]{:S(2)}, u32[]{:S(2)}) %all-to-all-start) | async-done | bytes 32800 | tf_op jit(solution)/shard_map/all_to_all | solution.py:583
  19.0 4.8 %shard_map.102 = (f32[1024,128]{1,0:T(8,128)}, f32[1024,128]{1,0:T(8,128)}, bf16[1024,128]{1,0:T(8,128)(2,1)}, s32[8,128]{1,0:T(8,128)}) custom-call(s32[1]{0:T(128)} %bitcast.at_ref, s32[8]{0:T(128)} %select_reduce_fusion.dest_ref, s32[64,128]{1,0:T(8,128)} %bitcast.11, f32[1,128]{1,0:T(1,128)} %maximum_bitcast_fusion.freq_ref, bf16[1024,512]{1,0:T(8,128)(2,1)} %key_ref.1), custom_call_target="tpu_custom_call" | custom-call | tf_op jit(solution)/shard_map/pallas_call | solution.py:89
  23.8 2.4 %collective-permute-start.5 = (bf16[1024,128]{1,0:T(8,128)(2,1)}, bf16[1024,128]{1,0:T(8,128)(2,1)S(1)}, u32[]{:S(2)}, u32[]{:S(2)}) collective-permute-start(bf16[1024,128]{1,0:T(8,128)(2,1)} %get-tuple-element.26.refs_0_), channel_id=1, source_target_pairs={{0,24},{4,28},{8,16},{12,20},{16,8},{20,12},{24,0},{28,4},{1,25},{... | collective-permute-start | bytes 786440 | tf_op jit(solution)/shard_map/ppermute | solution.py:348
  27.8 9.2 %shard_map.103 = (bf16[1024,512]{1,0:T(8,128)(2,1)}, bf16[512,1024]{1,0:T(8,128)(2,1)}, bf16[1024,512]{1,0:T(8,128)(2,1)}) custom-call(bf16[1024,3584]{1,0:T(8,128)(2,1)} %right_ref.1, bf16[3584,512]{1,0:T(8,128)(2,1)} %weight_ref.1, bf16[1024,512]{1,0:T(8,128)(2,1)} %query_ref.1, f32[1024,128]{1,0:T(8,128)} %get-tuple-element.24.cos_ref.refs_4_, ...), custom_call_target="tpu_custom_call" | custom-call | flops 3758096384 | bytes 7340032 | tf_op jit(solution)/shard_map/pallas_call | solution.py:426
  37.3 1.5 %collective-permute-done.3.refs_4_ = bf16[1024,128]{1,0:T(8,128)(2,1)S(1)} collective-permute-done((bf16[1024,128]{1,0:T(8,128)(2,1)}, bf16[1024,128]{1,0:T(8,128)(2,1)S(1)}, u32[]{:S(2)}, u32[]{:S(2)}) %collective-permute-start.3) | collective-permute-done | bytes 262176 | tf_op jit(solution)/shard_map/ppermute | solution.py:348
  42.1 18.7 %shard_map.104 = (f32[512,1024]{1,0:T(8,128)}, bf16[512,1024]{1,0:T(8,128)(2,1)}, bf16[4096,128]{1,0:T(8,128)(2,1)}, bf16[4096,128]{1,0:T(8,128)(2,1)}, bf16[409...) custom-call(s32[64]{0:T(128)} %multiply_add_fusion.3.target_ref, s32[64]{0:T(128)} %get-tuple-element.44.source_ref, ...), custom_call_target="tpu_custom_call" | custom-call | tf_op jit(solution)/shard_map/pallas_call | solution.py:281
  62.0 2.6 %collective-permute-done.18 = bf16[4096,128]{1,0:T(8,128)(2,1)} collective-permute-done((bf16[4096,128]{1,0:T(8,128)(2,1)}, bf16[4096,128]{1,0:T(8,128)(2,1)}, u32[]{:S(2)}, u32[]{:S(2)}) %collective-permute-start.18) | collective-permute-done | bytes 1048608 | tf_op jit(solution)/shard_map/ppermute | solution.py:348
  64.6 2.6 %add_convert_fusion.3 = (bf16[1024,128]{1,0:T(8,128)(2,1)}, bf16[1024,128]{1,0:T(8,128)(2,1)}, f32[1024,128]{1,0:T(8,128)}, bf16[1024,128]{1,0:T(8,128)(2,1)S(1)}) fusion(bf16[4096,128]{1,0:T(8,128)(2,1)} %collective-permute-done.18, bf16[4096,128]{1,0:T(8,128)(2,1)} %get-tuple-element.34), kind=kLoop, calls=%fused_computation.4 | loop fusion | flops 1966080 | bytes 3407872 | tf_op jit(solution)/shard_map/convert_element_type | solution.py:370
  67.2 4.5 %collective-permute-start.21 = (bf16[1024,128]{1,0:T(8,128)(2,1)}, bf16[1024,128]{1,0:T(8,128)(2,1)S(1)}, u32[]{:S(2)}, u32[]{:S(2)}) collective-permute-start(bf16[1024,128]{1,0:T(8,128)(2,1)} %get-tuple-element.51), channel_id=1, source_target_pairs={{0,24},{4,28},{8,16},{12,20},{16,8},{20,12},{24,0},{28,4},{1,25},{... | collective-permute-start | bytes 786440 | tf_op jit(solution)/shard_map/ppermute | solution.py:348
  71.7 1.3 collective-permute-start.20
  73.0 1.2 add_convert_fusion.6
  74.2 9.5 %shard_map.105 = (bf16[4,448,512]{2,1,0:T(8,128)(2,1)}, bf16[4,448,512]{2,1,0:T(8,128)(2,1)}, f32[1024,128]{1,0:T(8,128)}) custom-call(s32[2]{0:T(128)} %pad_add_fusion.my_ref, bf16[512,1024]{1,0:T(8,128)(2,1)} %get-tuple-element.33.left_ref, bf16[1024,3584]{1,0:T(8,128)(2,1)} %right_ref.1, ...), custom_call_target="tpu_custom_call", output_to_operand_aliasing={{2}: (5, {})} | custom-call | tf_op jit(solution)/shard_map/pallas_call | solution.py:532
  85.2 2.2 %shard_map.106 = (bf16[1024,128]{1,0:T(8,128)(2,1)}, bf16[1024,128]{1,0:T(8,128)(2,1)}, bf16[4,448,512]{2,1,0:T(8,128)(2,1)}) custom-call(f32[1024,128]{1,0:T(8,128)} %get-tuple-element.36.refs_0_, bf16[1024,128]{1,0:T(8,128)(2,1)} %copy-done.34, bf16[1024,128]{1,0:T(8,128)(2,1)} %copy-done.32, ...), custom_call_target="tpu_custom_call", output_to_operand_aliasing={{2}: (4, {})} | custom-call | tf_op jit(solution)/shard_map/pallas_call | solution.py:392
  87.4 1.7 %collective-permute-start.15 = (bf16[1024,128]{1,0:T(8,128)(2,1)S(1)}, bf16[1024,128]{1,0:T(8,128)(2,1)S(1)}, u32[]{:S(2)}, u32[]{:S(2)}) collective-permute-start(bf16[1024,128]{1,0:T(8,128)(2,1)S(1)} %copy-done.12), channel_id=1, source_target_pairs={{0,8},{4,12},{8,0},{12,4},{16,24},{20,28},{24,16},{28,20},{1,9},{5... | collective-permute-start | bytes 786440 | tf_op jit(solution)/shard_map/ppermute | solution.py:348
  90.9 2.6 %collective-permute-start.22 = (bf16[1024,128]{1,0:T(8,128)(2,1)}, bf16[1024,128]{1,0:T(8,128)(2,1)S(1)}, u32[]{:S(2)}, u32[]{:S(2)}) collective-permute-start(bf16[1024,128]{1,0:T(8,128)(2,1)} %get-tuple-element.38), channel_id=1, source_target_pairs={{0,2},{1,3},{2,0},{3,1},{4,6},{5,7},{6,4},{7,5},{8,10},{9,11},{10,... | collective-permute-start | bytes 786440 | tf_op jit(solution)/shard_map/ppermute | solution.py:335
  93.6 1.7 %convert_add_fusion = (f32[1,448,512]{2,1,0:T(8,128)}, bf16[1,448,512]{2,1,0:T(8,128)(2,1)}, bf16[1,448,512]{2,1,0:T(8,128)(2,1)}, bf16[1,448,512]{2,1,0:T(8,128)(2,1)}) fusion(bf16[4,448,512]{2,1,0:T(8,128)(2,1)S(1)} %collective-permute-done.23, bf16[4,448,512]{2,1,0:T(8,128)(2,1)S(1)} %copy-done.8), kind=kLoop, calls=%fused_computation | loop fusion | flops 3440640 | bytes 5963776 | tf_op jit(solution)/shard_map/add | solution.py:360
  95.3 1.6 %collective-permute-start.24 = (bf16[1024,128]{1,0:T(8,128)(2,1)}, bf16[1024,128]{1,0:T(8,128)(2,1)S(1)}, u32[]{:S(2)}, u32[]{:S(2)}) collective-permute-start(bf16[1024,128]{1,0:T(8,128)(2,1)} %shard_map.108.refs_0_), channel_id=1, source_target_pairs={{0,1},{1,0},{2,3},{3,2},{4,5},{5,4},{6,7},{7,6},{8,9},{9,8},{10,11... | collective-permute-start | bytes 786440 | tf_op jit(solution)/shard_map/ppermute | solution.py:335
  96.8 5.4 %collective-permute-done.17.refs_3_ = bf16[1024,128]{1,0:T(8,128)(2,1)S(1)} collective-permute-done((bf16[1024,128]{1,0:T(8,128)(2,1)S(1)}, bf16[1024,128]{1,0:T(8,128)(2,1)S(1)}, u32[]{:S(2)}, u32[]{:S(2)}) %collective-permute-start.17) | collective-permute-done | bytes 262176 | tf_op jit(solution)/shard_map/ppermute | solution.py:348
  102.3 2.1 %collective-permute-start.29 = (bf16[1,448,512]{2,1,0:T(8,128)(2,1)}, bf16[1,448,512]{2,1,0:T(8,128)(2,1)S(1)}, u32[]{:S(2)}, u32[]{:S(2)}) collective-permute-start(bf16[1,448,512]{2,1,0:T(8,128)(2,1)} %get-tuple-element.48), channel_id=1, source_target_pairs={{0,24},{4,28},{8,16},{12,20},{16,8},{20,12},{24,0},{28,4},{1,25},{... | collective-permute-start | bytes 1376264 | tf_op jit(solution)/shard_map/ppermute | solution.py:348
  108.2 2.5 %shard_map.109.refs_0_ = bf16[1024,128]{1,0:T(8,128)(2,1)} custom-call(f32[1024,128]{1,0:T(8,128)} %get-tuple-element.58.refs_0_, bf16[1024,128]{1,0:T(8,128)(2,1)} %copy-done.25, bf16[1024,128]{1,0:T(8,128)(2,1)} %copy-done.28, bf16[1024,128]{1,0:T(8,128)(2,1)} %copy-done.27, f32[1024,128]{1,0:T(8,128)} %get-tuple-element.24.cos_ref.refs_4_, ...), custom_call_target="tpu_custom_call" | custom-call | tf_op jit(solution)/shard_map/pallas_call | solution.py:392
  110.7 2.5 %collective-permute-start.26 = (bf16[1024,128]{1,0:T(8,128)(2,1)}, bf16[1024,128]{1,0:T(8,128)(2,1)S(1)}, u32[]{:S(2)}, u32[]{:S(2)}) collective-permute-start(bf16[1024,128]{1,0:T(8,128)(2,1)} %shard_map.109.refs_0_), channel_id=1, source_target_pairs={{0,2},{1,3},{2,0},{3,1},{4,6},{5,7},{6,4},{7,5},{8,10},{9,11},{10,... | collective-permute-start | bytes 786440 | tf_op jit(solution)/shard_map/ppermute | solution.py:335
  113.2 1.6 %collective-permute-start.31 = (bf16[1024,128]{1,0:T(8,128)(2,1)S(1)}, bf16[1024,128]{1,0:T(8,128)(2,1)}, u32[]{:S(2)}, u32[]{:S(2)}) collective-permute-start(bf16[1024,128]{1,0:T(8,128)(2,1)S(1)} %copy-done.4), channel_id=1, source_target_pairs={{0,1},{1,0},{2,3},{3,2},{4,5},{5,4},{6,7},{7,6},{8,9},{9,8},{10,11... | collective-permute-start | bytes 786440 | tf_op jit(solution)/shard_map/ppermute | solution.py:335
  114.8 4.5 %shard_map.110.refs_4_ = bf16[1024,512]{1,0:T(8,128)(2,1)} custom-call(f32[512,1024]{1,0:T(8,128)} %get-tuple-element.30.grad_ref, f32[1024,128]{1,0:T(8,128)} %get-tuple-element.24.cos_ref.refs_4_, f32[1024,128]{1,0:T(8,128)} %get-tuple-element.25.sin_ref.refs_5_, bf16[1024,128]{1,0:T(8,128)(2,1)} %shard_map.109.refs_0_), custom_call_target="tpu_custom_call" | custom-call | tf_op jit(solution)/shard_map/pallas_call | solution.py:467
  119.8 5.4 %collective-permute-done.28.refs_2_ = bf16[1,448,512]{2,1,0:T(8,128)(2,1)S(1)} collective-permute-done((bf16[1,448,512]{2,1,0:T(8,128)(2,1)}, bf16[1,448,512]{2,1,0:T(8,128)(2,1)S(1)}, u32[]{:S(2)}, u32[]{:S(2)}) %collective-permute-start.28) | collective-permute-done | bytes 458784 | tf_op jit(solution)/shard_map/ppermute | solution.py:348
  126.9 1.6 %collective-permute-start.30 = (bf16[1024,128]{1,0:T(8,128)(2,1)}, bf16[1024,128]{1,0:T(8,128)(2,1)S(1)}, u32[]{:S(2)}, u32[]{:S(2)}) collective-permute-start(bf16[1024,128]{1,0:T(8,128)(2,1)} %shard_map.111.refs_2_.refs_4_), channel_id=1, source_target_pairs={{0,1},{1,0},{2,3},{3,2},{4,5},{5,4},{6,7},{7,6},{8,9},{9,8},{10,11... | collective-permute-start | bytes 786440 | tf_op jit(solution)/shard_map/ppermute | solution.py:335
  128.4 2.2 %shard_map.113.refs_5_ = bf16[1024,512]{1,0:T(8,128)(2,1)} custom-call(s32[1]{0:T(128)} %bitcast.6.my_ref, bf16[1024,128]{1,0:T(8,128)(2,1)} %shard_map.108.refs_0_, bf16[1024,128]{1,0:T(8,128)(2,1)} %copy-done.9, bf16[1024,128]{1,0:T(8,128)(2,1)} %shard_map.107.refs_6_.refs_2_, bf16[1024,128]{1,0:T(8,128)(2,1)} %collective-permute-done.31.refs_3_), custom_call_target="tpu_custom_call" | custom-call | tf_op jit(solution)/shard_map/pallas_call | solution.py:322
  130.6 2.7 %shard_map.114 = f32[448,512]{1,0:T(8,128)} custom-call(f32[1,448,512]{2,1,0:T(8,128)} %get-tuple-element.47.refs_0_, bf16[1,448,512]{2,1,0:T(8,128)(2,1)} %copy-done.7, bf16[1,448,512]{2,1,0:T(8,128)(2,1)} %copy-done.6, bf16[1,448,512]{2,1,0:T(8,128)(2,1)} %copy-done.5, bf16[1024,128]{1,0:T(8,128)(2,1)} %shard_map.111.refs_2_.refs_4_, ...), custom_call_target="tpu_custom_call" | custom-call | tf_op jit(solution)/shard_map/pallas_call | solution.py:561
  133.3 2.0 %collective-permute-done.30.refs_3_ = bf16[1024,128]{1,0:T(8,128)(2,1)S(1)} collective-permute-done((bf16[1024,128]{1,0:T(8,128)(2,1)}, bf16[1024,128]{1,0:T(8,128)(2,1)S(1)}, u32[]{:S(2)}, u32[]{:S(2)}) %collective-permute-start.30) | collective-permute-done | bytes 262176 | tf_op jit(solution)/shard_map/ppermute | solution.py:335
  136.1 2.2 %shard_map.112 = bf16[1024,512]{1,0:T(8,128)(2,1)} custom-call(s32[1]{0:T(128)} %bitcast.6.my_ref, bf16[1024,128]{1,0:T(8,128)(2,1)} %shard_map.109.refs_0_, bf16[1024,128]{1,0:T(8,128)(2,1)} %copy-done.33, bf16[1024,128]{1,0:T(8,128)(2,1)} %shard_map.111.refs_2_.refs_4_, bf16[1024,128]{1,0:T(8,128)(2,1)} %copy-done.35), custom_call_target="tpu_custom_call" | custom-call | tf_op jit(solution)/shard_map/pallas_call | solution.py:322
  (148 shorter events, 23.1 us)
Async XLA Ops:
  1.9 24.3 %collective-permute-start.12 = (bf16[1024,128]{1,0:T(8,128)(2,1)S(1)}, bf16[1024,128]{1,0:T(8,128)(2,1)S(1)}, u32[]{:S(2)}, u32[]{:S(2)}) collective-permute-start(bf16[1024,128]{1,0:T(8,128)(2,1)S(1)} %constant_dynamic-slice_fusion.refs_8_), channel_id=1, source_target_pairs={{0,24},{4,28},{8,16},{12,20},{16,8},{20,12},{24,0},{28,4},{1,25},{... | collective-permute-start | bytes 786440 | tf_op jit(solution)/shard_map/ppermute | solution.py:348
  5.9 20.9 %collective-permute-start.10 = (bf16[1024,128]{1,0:T(8,128)(2,1)S(1)}, bf16[1024,128]{1,0:T(8,128)(2,1)S(1)}, u32[]{:S(2)}, u32[]{:S(2)}) collective-permute-start(bf16[1024,128]{1,0:T(8,128)(2,1)S(1)} %constant_dynamic-slice_fusion.refs_8_), channel_id=1, source_target_pairs={{0,16},{4,20},{8,24},{12,28},{16,0},{20,4},{24,8},{28,12},{1,17},{... | collective-permute-start | bytes 786440 | tf_op jit(solution)/shard_map/ppermute | solution.py:348
  6.4 20.9 %collective-permute-start.8 = (bf16[1024,128]{1,0:T(8,128)(2,1)S(1)}, bf16[1024,128]{1,0:T(8,128)(2,1)S(1)}, u32[]{:S(2)}, u32[]{:S(2)}) collective-permute-start(bf16[1024,128]{1,0:T(8,128)(2,1)S(1)} %constant_dynamic-slice_fusion.refs_8_), channel_id=1, source_target_pairs={{0,8},{4,12},{8,0},{12,4},{16,24},{20,28},{24,16},{28,20},{1,9},{5... | collective-permute-start | bytes 786440 | tf_op jit(solution)/shard_map/ppermute | solution.py:348
  6.5 20.8 %collective-permute-start.7 = (bf16[1024,128]{1,0:T(8,128)(2,1)S(1)}, bf16[1024,128]{1,0:T(8,128)(2,1)S(1)}, u32[]{:S(2)}, u32[]{:S(2)}) collective-permute-start(bf16[1024,128]{1,0:T(8,128)(2,1)S(1)} %constant_dynamic-slice_fusion.refs_8_), channel_id=1, source_target_pairs={{0,4},{4,0},{8,12},{12,8},{16,20},{20,16},{24,28},{28,24},{1,5},{5... | collective-permute-start | bytes 786440 | tf_op jit(solution)/shard_map/ppermute | solution.py:348
  8.6 9.8 %all-to-all-start = ((s32[8,8,128]{2,1,0:T(8,128)}), s32[8,8,128]{2,1,0:T(8,128)S(1)}, u32[]{:S(2)}, u32[]{:S(2)}) async-start(s32[8,8,128]{2,1,0:T(8,128)} %broadcast_in_dim.27), calls=%async_computation | async-start | bytes 65536 | tf_op jit(solution)/shard_map/all_to_all | solution.py:583
  23.8 13.3 %collective-permute-start.5 = (bf16[1024,128]{1,0:T(8,128)(2,1)}, bf16[1024,128]{1,0:T(8,128)(2,1)S(1)}, u32[]{:S(2)}, u32[]{:S(2)}) collective-permute-start(bf16[1024,128]{1,0:T(8,128)(2,1)} %get-tuple-element.26.refs_0_), channel_id=1, source_target_pairs={{0,24},{4,28},{8,16},{12,20},{16,8},{20,12},{24,0},{28,4},{1,25},{... | collective-permute-start | bytes 786440 | tf_op jit(solution)/shard_map/ppermute | solution.py:348
  26.2 12.5 %collective-permute-start.3 = (bf16[1024,128]{1,0:T(8,128)(2,1)}, bf16[1024,128]{1,0:T(8,128)(2,1)S(1)}, u32[]{:S(2)}, u32[]{:S(2)}) collective-permute-start(bf16[1024,128]{1,0:T(8,128)(2,1)} %get-tuple-element.26.refs_0_), channel_id=1, source_target_pairs={{0,16},{4,20},{8,24},{12,28},{16,0},{20,4},{24,8},{28,12},{1,17},{... | collective-permute-start | bytes 786440 | tf_op jit(solution)/shard_map/ppermute | solution.py:348
  26.8 12.0 %collective-permute-start.1 = (bf16[1024,128]{1,0:T(8,128)(2,1)}, bf16[1024,128]{1,0:T(8,128)(2,1)S(1)}, u32[]{:S(2)}, u32[]{:S(2)}) collective-permute-start(bf16[1024,128]{1,0:T(8,128)(2,1)} %get-tuple-element.26.refs_0_), channel_id=1, source_target_pairs={{0,8},{4,12},{8,0},{12,4},{16,24},{20,28},{24,16},{28,20},{1,9},{5... | collective-permute-start | bytes 786440 | tf_op jit(solution)/shard_map/ppermute | solution.py:348
  27.3 11.9 %collective-permute-start = (bf16[1024,128]{1,0:T(8,128)(2,1)}, bf16[1024,128]{1,0:T(8,128)(2,1)S(1)}, u32[]{:S(2)}, u32[]{:S(2)}) collective-permute-start(bf16[1024,128]{1,0:T(8,128)(2,1)} %get-tuple-element.26.refs_0_), channel_id=1, source_target_pairs={{0,4},{4,0},{8,12},{12,8},{16,20},{20,16},{24,28},{28,24},{1,5},{5... | collective-permute-start | bytes 786440 | tf_op jit(solution)/shard_map/ppermute | solution.py:348
  27.3 12.0 %collective-permute-start.13 = (bf16[1024,128]{1,0:T(8,128)(2,1)S(1)}, bf16[1024,128]{1,0:T(8,128)(2,1)S(1)}, u32[]{:S(2)}, u32[]{:S(2)}) collective-permute-start(bf16[1024,128]{1,0:T(8,128)(2,1)S(1)} %collective-permute-done.12.refs_14_), channel_id=1, source_target_pairs={{0,4},{4,0},{8,12},{12,8},{16,20},{20,16},{24,28},{28,24},{1,5},{5... | collective-permute-start | bytes 786440 | tf_op jit(solution)/shard_map/ppermute | solution.py:348
  37.1 3.4 %collective-permute-start.11 = (bf16[1024,128]{1,0:T(8,128)(2,1)S(1)}, bf16[1024,128]{1,0:T(8,128)(2,1)S(1)}, u32[]{:S(2)}, u32[]{:S(2)}) collective-permute-start(bf16[1024,128]{1,0:T(8,128)(2,1)S(1)} %collective-permute-done.10.refs_12_), channel_id=1, source_target_pairs={{0,4},{4,0},{8,12},{12,8},{16,20},{20,16},{24,28},{28,24},{1,5},{5... | collective-permute-start | bytes 786440 | tf_op jit(solution)/shard_map/ppermute | solution.py:348
  38.8 1.9 %collective-permute-start.6 = (bf16[1024,128]{1,0:T(8,128)(2,1)S(1)}, bf16[1024,128]{1,0:T(8,128)(2,1)S(1)}, u32[]{:S(2)}, u32[]{:S(2)}) collective-permute-start(bf16[1024,128]{1,0:T(8,128)(2,1)S(1)} %collective-permute-done.5.refs_6_), channel_id=1, source_target_pairs={{0,4},{4,0},{8,12},{12,8},{16,20},{20,16},{24,28},{28,24},{1,5},{5... | collective-permute-start | bytes 786440 | tf_op jit(solution)/shard_map/ppermute | solution.py:348
  39.3 1.8 %collective-permute-start.4 = (bf16[1024,128]{1,0:T(8,128)(2,1)S(1)}, bf16[1024,128]{1,0:T(8,128)(2,1)S(1)}, u32[]{:S(2)}, u32[]{:S(2)}) collective-permute-start(bf16[1024,128]{1,0:T(8,128)(2,1)S(1)} %collective-permute-done.3.refs_4_), channel_id=1, source_target_pairs={{0,4},{4,0},{8,12},{12,8},{16,20},{20,16},{24,28},{28,24},{1,5},{5... | collective-permute-start | bytes 786440 | tf_op jit(solution)/shard_map/ppermute | solution.py:348
  39.3 2.0 %collective-permute-start.2 = (bf16[1024,128]{1,0:T(8,128)(2,1)S(1)}, bf16[1024,128]{1,0:T(8,128)(2,1)S(1)}, u32[]{:S(2)}, u32[]{:S(2)}) collective-permute-start(bf16[1024,128]{1,0:T(8,128)(2,1)S(1)} %collective-permute-done.1.refs_2_), channel_id=1, source_target_pairs={{0,4},{4,0},{8,12},{12,8},{16,20},{20,16},{24,28},{28,24},{1,5},{5... | collective-permute-start | bytes 786440 | tf_op jit(solution)/shard_map/ppermute | solution.py:348
  60.8 3.8 %collective-permute-start.18 = (bf16[4096,128]{1,0:T(8,128)(2,1)}, bf16[4096,128]{1,0:T(8,128)(2,1)}, u32[]{:S(2)}, u32[]{:S(2)}) collective-permute-start(bf16[4096,128]{1,0:T(8,128)(2,1)} %get-tuple-element.35), channel_id=1, source_target_pairs={{0,4},{4,0},{8,12},{12,8},{16,20},{20,16},{24,28},{28,24},{1,5},{5... | collective-permute-start | bytes 3145736 | tf_op jit(solution)/shard_map/ppermute | solution.py:348
  60.9 12.1 %collective-permute-start.14 = (bf16[4096,128]{1,0:T(8,128)(2,1)}, bf16[4096,128]{1,0:T(8,128)(2,1)S(1)}, u32[]{:S(2)}, u32[]{:S(2)}) collective-permute-start(bf16[4096,128]{1,0:T(8,128)(2,1)} %get-tuple-element.32), channel_id=1, source_target_pairs={{0,4},{4,0},{8,12},{12,8},{16,20},{20,16},{24,28},{28,24},{1,5},{5... | collective-permute-start | bytes 3145736 | tf_op jit(solution)/shard_map/ppermute | solution.py:348
  67.2 16.5 %collective-permute-start.21 = (bf16[1024,128]{1,0:T(8,128)(2,1)}, bf16[1024,128]{1,0:T(8,128)(2,1)S(1)}, u32[]{:S(2)}, u32[]{:S(2)}) collective-permute-start(bf16[1024,128]{1,0:T(8,128)(2,1)} %get-tuple-element.51), channel_id=1, source_target_pairs={{0,24},{4,28},{8,16},{12,20},{16,8},{20,12},{24,0},{28,4},{1,25},{... | collective-permute-start | bytes 786440 | tf_op jit(solution)/shard_map/ppermute | solution.py:348
  71.7 12.7 %collective-permute-start.20 = (bf16[1024,128]{1,0:T(8,128)(2,1)}, bf16[1024,128]{1,0:T(8,128)(2,1)S(1)}, u32[]{:S(2)}, u32[]{:S(2)}) collective-permute-start(bf16[1024,128]{1,0:T(8,128)(2,1)} %get-tuple-element.52), channel_id=1, source_target_pairs={{0,16},{4,20},{8,24},{12,28},{16,0},{20,4},{24,8},{28,12},{1,17},{... | collective-permute-start | bytes 786440 | tf_op jit(solution)/shard_map/ppermute | solution.py:348
  73.0 11.4 %collective-permute-start.19 = (bf16[1024,128]{1,0:T(8,128)(2,1)S(1)}, bf16[1024,128]{1,0:T(8,128)(2,1)S(1)}, u32[]{:S(2)}, u32[]{:S(2)}) collective-permute-start(bf16[1024,128]{1,0:T(8,128)(2,1)S(1)} %get-tuple-element.54.refs_0_), channel_id=1, source_target_pairs={{0,8},{4,12},{8,0},{12,4},{16,24},{20,28},{24,16},{28,20},{1,9},{5... | collective-permute-start | bytes 786440 | tf_op jit(solution)/shard_map/ppermute | solution.py:348
  87.4 6.2 %collective-permute-start.23 = (bf16[4,448,512]{2,1,0:T(8,128)(2,1)}, bf16[4,448,512]{2,1,0:T(8,128)(2,1)S(1)}, u32[]{:S(2)}, u32[]{:S(2)}) collective-permute-start(bf16[4,448,512]{2,1,0:T(8,128)(2,1)} %get-tuple-element.40), channel_id=1, source_target_pairs={{0,4},{4,0},{8,12},{12,8},{16,20},{20,16},{24,28},{28,24},{1,5},{5... | collective-permute-start | bytes 5505032 | tf_op jit(solution)/shard_map/ppermute | solution.py:348
  87.4 19.9 %collective-permute-start.15 = (bf16[1024,128]{1,0:T(8,128)(2,1)S(1)}, bf16[1024,128]{1,0:T(8,128)(2,1)S(1)}, u32[]{:S(2)}, u32[]{:S(2)}) collective-permute-start(bf16[1024,128]{1,0:T(8,128)(2,1)S(1)} %copy-done.12), channel_id=1, source_target_pairs={{0,8},{4,12},{8,0},{12,4},{16,24},{20,28},{24,16},{28,20},{1,9},{5... | collective-permute-start | bytes 786440 | tf_op jit(solution)/shard_map/ppermute | solution.py:348
  89.1 13.2 %collective-permute-start.17 = (bf16[1024,128]{1,0:T(8,128)(2,1)S(1)}, bf16[1024,128]{1,0:T(8,128)(2,1)S(1)}, u32[]{:S(2)}, u32[]{:S(2)}) collective-permute-start(bf16[1024,128]{1,0:T(8,128)(2,1)S(1)} %copy-done.36), channel_id=1, source_target_pairs={{0,24},{4,28},{8,16},{12,20},{16,8},{20,12},{24,0},{28,4},{1,25},{... | collective-permute-start | bytes 786440 | tf_op jit(solution)/shard_map/ppermute | solution.py:348
  89.9 14.4 %collective-permute-start.16 = (bf16[1024,128]{1,0:T(8,128)(2,1)}, bf16[1024,128]{1,0:T(8,128)(2,1)S(1)}, u32[]{:S(2)}, u32[]{:S(2)}) collective-permute-start(bf16[1024,128]{1,0:T(8,128)(2,1)} %get-tuple-element.56), channel_id=1, source_target_pairs={{0,16},{4,20},{8,24},{12,28},{16,0},{20,4},{24,8},{28,12},{1,17},{... | collective-permute-start | bytes 786440 | tf_op jit(solution)/shard_map/ppermute | solution.py:348
  90.9 15.2 %collective-permute-start.22 = (bf16[1024,128]{1,0:T(8,128)(2,1)}, bf16[1024,128]{1,0:T(8,128)(2,1)S(1)}, u32[]{:S(2)}, u32[]{:S(2)}) collective-permute-start(bf16[1024,128]{1,0:T(8,128)(2,1)} %get-tuple-element.38), channel_id=1, source_target_pairs={{0,2},{1,3},{2,0},{3,1},{4,6},{5,7},{6,4},{7,5},{8,10},{9,11},{10,... | collective-permute-start | bytes 786440 | tf_op jit(solution)/shard_map/ppermute | solution.py:335
  95.3 12.2 %collective-permute-start.24 = (bf16[1024,128]{1,0:T(8,128)(2,1)}, bf16[1024,128]{1,0:T(8,128)(2,1)S(1)}, u32[]{:S(2)}, u32[]{:S(2)}) collective-permute-start(bf16[1024,128]{1,0:T(8,128)(2,1)} %shard_map.108.refs_0_), channel_id=1, source_target_pairs={{0,1},{1,0},{2,3},{3,2},{4,5},{5,4},{6,7},{7,6},{8,9},{9,8},{10,11... | collective-permute-start | bytes 786440 | tf_op jit(solution)/shard_map/ppermute | solution.py:335
  102.3 17.0 %collective-permute-start.29 = (bf16[1,448,512]{2,1,0:T(8,128)(2,1)}, bf16[1,448,512]{2,1,0:T(8,128)(2,1)S(1)}, u32[]{:S(2)}, u32[]{:S(2)}) collective-permute-start(bf16[1,448,512]{2,1,0:T(8,128)(2,1)} %get-tuple-element.48), channel_id=1, source_target_pairs={{0,24},{4,28},{8,16},{12,20},{16,8},{20,12},{24,0},{28,4},{1,25},{... | collective-permute-start | bytes 1376264 | tf_op jit(solution)/shard_map/ppermute | solution.py:348
  105.1 20.2 %collective-permute-start.28 = (bf16[1,448,512]{2,1,0:T(8,128)(2,1)}, bf16[1,448,512]{2,1,0:T(8,128)(2,1)S(1)}, u32[]{:S(2)}, u32[]{:S(2)}) collective-permute-start(bf16[1,448,512]{2,1,0:T(8,128)(2,1)} %get-tuple-element.49), channel_id=1, source_target_pairs={{0,16},{4,20},{8,24},{12,28},{16,0},{20,4},{24,8},{28,12},{1,17},{... | collective-permute-start | bytes 1376264 | tf_op jit(solution)/shard_map/ppermute | solution.py:348
  106.1 19.1 %collective-permute-start.27 = (bf16[1,448,512]{2,1,0:T(8,128)(2,1)}, bf16[1,448,512]{2,1,0:T(8,128)(2,1)S(1)}, u32[]{:S(2)}, u32[]{:S(2)}) collective-permute-start(bf16[1,448,512]{2,1,0:T(8,128)(2,1)} %get-tuple-element.50.refs_1_), channel_id=1, source_target_pairs={{0,8},{4,12},{8,0},{12,4},{16,24},{20,28},{24,16},{28,20},{1,9},{5... | collective-permute-start | bytes 1376264 | tf_op jit(solution)/shard_map/ppermute | solution.py:348
  110.7 14.5 %collective-permute-start.26 = (bf16[1024,128]{1,0:T(8,128)(2,1)}, bf16[1024,128]{1,0:T(8,128)(2,1)S(1)}, u32[]{:S(2)}, u32[]{:S(2)}) collective-permute-start(bf16[1024,128]{1,0:T(8,128)(2,1)} %shard_map.109.refs_0_), channel_id=1, source_target_pairs={{0,2},{1,3},{2,0},{3,1},{4,6},{5,7},{6,4},{7,5},{8,10},{9,11},{10,... | collective-permute-start | bytes 786440 | tf_op jit(solution)/shard_map/ppermute | solution.py:335
  113.2 15.2 %collective-permute-start.31 = (bf16[1024,128]{1,0:T(8,128)(2,1)S(1)}, bf16[1024,128]{1,0:T(8,128)(2,1)}, u32[]{:S(2)}, u32[]{:S(2)}) collective-permute-start(bf16[1024,128]{1,0:T(8,128)(2,1)S(1)} %copy-done.4), channel_id=1, source_target_pairs={{0,1},{1,0},{2,3},{3,2},{4,5},{5,4},{6,7},{7,6},{8,9},{9,8},{10,11... | collective-permute-start | bytes 786440 | tf_op jit(solution)/shard_map/ppermute | solution.py:335
  119.3 14.1 %collective-permute-start.25 = (bf16[1024,128]{1,0:T(8,128)(2,1)S(1)}, bf16[1024,128]{1,0:T(8,128)(2,1)S(1)}, u32[]{:S(2)}, u32[]{:S(2)}) collective-permute-start(bf16[1024,128]{1,0:T(8,128)(2,1)S(1)} %copy-done.1), channel_id=1, source_target_pairs={{0,1},{1,0},{2,3},{3,2},{4,5},{5,4},{6,7},{7,6},{8,9},{9,8},{10,11... | collective-permute-start | bytes 786440 | tf_op jit(solution)/shard_map/ppermute | solution.py:335
  126.9 8.5 %collective-permute-start.30 = (bf16[1024,128]{1,0:T(8,128)(2,1)}, bf16[1024,128]{1,0:T(8,128)(2,1)S(1)}, u32[]{:S(2)}, u32[]{:S(2)}) collective-permute-start(bf16[1024,128]{1,0:T(8,128)(2,1)} %shard_map.111.refs_2_.refs_4_), channel_id=1, source_target_pairs={{0,1},{1,0},{2,3},{3,2},{4,5},{5,4},{6,7},{7,6},{8,9},{9,8},{10,11... | collective-permute-start | bytes 786440 | tf_op jit(solution)/shard_map/ppermute | solution.py:335
  (41 other events, 191.9 us)

commit v16 on v15

--- a/solution.py
+++ b/solution.py
@@ -146,6 +146,21 @@
             loads.append(copy)
     for copy in loads:
         copy.wait()
+
+    if ranks > rows_each // ROWBLK:
+        gkey_ref[0] = jnp.zeros(gkey_ref.shape[1:], jnp.bfloat16)
+        fills = []
+        for item, whole in enumerate(halves):
+            for part in range(ranks // 2):
+                copy = pltpu.make_async_copy(
+                    gkey_ref.at[0],
+                    whole.at[pl.ds(part * rows_each, rows_each)],
+                    load_sems.at[item // 2, item % 2 * (ranks // 2) + part],
+                )
+                copy.start()
+                fills.append(copy)
+        for copy in fills:
+            copy.wait()
 
     def stores(block, act):
         side = block % 2

time: 139 us -> 139 us (level)
  starting transfers between devices: 38.5 us -> 33.9 us
  Pallas kernels: 58.5 us -> 61.3 us
  waiting for transfers between devices: 20.6 us -> 22.3 us
    ppermute x26, starting transfers between devices: 23.9 us -> 19.9 us  [swap(): lax.ppermute(array, 'dp', [(rank, rank ^ bit) for rank in range(ranks)])]
    pallas_call x1, Pallas kernels: 18.7 us -> 21.4 us  [attend(): pl.pallas_call(partial(attend_kernel, heads, ranks), out_shape=(jax.Shape...]
where the time goes in v16:
time: 139 us; the launch traced here: 138 us
  Pallas kernels  61.3 us (44%)
  starting transfers between devices  33.9 us (24%)
  waiting for transfers between devices  22.3 us (16%)
  other arithmetic  11.7 us (8%)
  local copies, waits for them, and re-layouts  8.06 us (6%)
    pallas_call x1, Pallas kernels, attend(): pl.pallas_call(partial(attend_kernel, heads, ranks), out_shape=(jax.Shape...  21.4 us
    ppermute x26, starting transfers between devices, swap(): lax.ppermute(array, 'dp', [(rank, rank ^ bit) for rank in range(ranks)])  19.9 us
    ppermute x26, waiting for transfers between devices, swap(): lax.ppermute(array, 'dp', [(rank, rank ^ bit) for rank in range(ranks)])  17.7 us
    ppermute x6, starting transfers between devices, lane_swap(): lax.ppermute(array, 'tensor', [(lane, lane ^ bit) for lane in range(lanes)])  9.81 us
    pallas_call x1, Pallas kernels, product(): pl.pallas_call(product_kernel, grid_spec=pltpu.PrefetchScalarGridSpec(num...  9.51 us
    pallas_call x1, Pallas kernels, prepare(): pl.pallas_call(prepare_kernel, grid=(steps,), out_shape=[jax.ShapeDtypeSt...  9.22 us
    unnamed x80, local copies, waits for them, and re-layouts  7.09 us
    pallas_call x1, Pallas kernels, rope(): pl.pallas_call(rope_kernel, grid_spec=pltpu.PrefetchScalarGridSpec(num_sc...  4.8 us
  transfers between devices with their start and end apart: 33, of which 11 were waited for; matrix products, arithmetic and copies ran while one was open for 9% of the time, Pallas kernels for 26%

profile of v16, /device:TPU:0, one launch (start us, length us, event | category | flops | bytes accessed | tf_op | source)
XLA Modules:
  0.0 138.5 jit_solution(14230768114285015819)
XLA Ops:
  0.7 1.2 copy-done
  1.9 4.0 %collective-permute-start.12 = (bf16[1024,128]{1,0:T(8,128)(2,1)S(1)}, bf16[1024,128]{1,0:T(8,128)(2,1)S(1)}, u32[]{:S(2)}, u32[]{:S(2)}) collective-permute-start(bf16[1024,128]{1,0:T(8,128)(2,1)S(1)} %constant_dynamic-slice_fusion.refs_8_), channel_id=1, source_target_pairs={{0,24},{4,28},{8,16},{12,20},{16,8},{20,12},{24,0},{28,4},{1,25},{... | collective-permute-start | bytes 786440 | tf_op jit(solution)/shard_map/ppermute | solution.py:363
  8.6 4.2 %all-to-all-start = ((s32[8,8,128]{2,1,0:T(8,128)}), s32[8,8,128]{2,1,0:T(8,128)S(1)}, u32[]{:S(2)}, u32[]{:S(2)}) async-start(s32[8,8,128]{2,1,0:T(8,128)} %broadcast_in_dim.27), calls=%async_computation | async-start | bytes 65536 | tf_op jit(solution)/shard_map/all_to_all | solution.py:598
  12.9 1.2 multiply_add_fusion.2
  14.6 1.4 select_reduce_fusion.dest_ref
  16.6 1.8 %all-to-all-done = s32[8,8,128]{2,1,0:T(8,128)S(1)} async-done(((s32[8,8,128]{2,1,0:T(8,128)}), s32[8,8,128]{2,1,0:T(8,128)S(1)}, u32[]{:S(2)}, u32[]{:S(2)}) %all-to-all-start) | async-done | bytes 32800 | tf_op jit(solution)/shard_map/all_to_all | solution.py:598
  19.0 4.8 %shard_map.102 = (f32[1024,128]{1,0:T(8,128)}, f32[1024,128]{1,0:T(8,128)}, bf16[1024,128]{1,0:T(8,128)(2,1)}, s32[8,128]{1,0:T(8,128)}) custom-call(s32[1]{0:T(128)} %bitcast.at_ref, s32[8]{0:T(128)} %select_reduce_fusion.dest_ref, s32[64,128]{1,0:T(8,128)} %bitcast.11, f32[1,128]{1,0:T(1,128)} %maximum_bitcast_fusion.freq_ref, bf16[1024,512]{1,0:T(8,128)(2,1)} %key_ref.1), custom_call_target="tpu_custom_call" | custom-call | tf_op jit(solution)/shard_map/pallas_call | solution.py:89
  23.8 2.4 %collective-permute-start.5 = (bf16[1024,128]{1,0:T(8,128)(2,1)}, bf16[1024,128]{1,0:T(8,128)(2,1)S(1)}, u32[]{:S(2)}, u32[]{:S(2)}) collective-permute-start(bf16[1024,128]{1,0:T(8,128)(2,1)} %get-tuple-element.26.refs_0_), channel_id=1, source_target_pairs={{0,24},{4,28},{8,16},{12,20},{16,8},{20,12},{24,0},{28,4},{1,25},{... | collective-permute-start | bytes 786440 | tf_op jit(solution)/shard_map/ppermute | solution.py:363
  27.8 9.2 %shard_map.103 = (bf16[1024,512]{1,0:T(8,128)(2,1)}, bf16[512,1024]{1,0:T(8,128)(2,1)}, bf16[1024,512]{1,0:T(8,128)(2,1)}) custom-call(bf16[1024,3584]{1,0:T(8,128)(2,1)} %right_ref.1, bf16[3584,512]{1,0:T(8,128)(2,1)} %weight_ref.1, bf16[1024,512]{1,0:T(8,128)(2,1)} %query_ref.1, f32[1024,128]{1,0:T(8,128)} %get-tuple-element.24.cos_ref.refs_4_, ...), custom_call_target="tpu_custom_call" | custom-call | flops 3758096384 | bytes 7340032 | tf_op jit(solution)/shard_map/pallas_call | solution.py:441
  37.3 1.5 %collective-permute-done.3.refs_4_ = bf16[1024,128]{1,0:T(8,128)(2,1)S(1)} collective-permute-done((bf16[1024,128]{1,0:T(8,128)(2,1)}, bf16[1024,128]{1,0:T(8,128)(2,1)S(1)}, u32[]{:S(2)}, u32[]{:S(2)}) %collective-permute-start.3) | collective-permute-done | bytes 262176 | tf_op jit(solution)/shard_map/ppermute | solution.py:363
  42.1 21.4 %shard_map.104 = (f32[512,1024]{1,0:T(8,128)}, bf16[512,1024]{1,0:T(8,128)(2,1)}, bf16[4096,128]{1,0:T(8,128)(2,1)}, bf16[4096,128]{1,0:T(8,128)(2,1)}, bf16[409...) custom-call(s32[64]{0:T(128)} %multiply_add_fusion.3.target_ref, s32[64]{0:T(128)} %get-tuple-element.44.source_ref, ...), custom_call_target="tpu_custom_call" | custom-call | tf_op jit(solution)/shard_map/pallas_call | solution.py:296
  64.7 2.6 %collective-permute-done.18 = bf16[4096,128]{1,0:T(8,128)(2,1)} collective-permute-done((bf16[4096,128]{1,0:T(8,128)(2,1)}, bf16[4096,128]{1,0:T(8,128)(2,1)}, u32[]{:S(2)}, u32[]{:S(2)}) %collective-permute-start.18) | collective-permute-done | bytes 1048608 | tf_op jit(solution)/shard_map/ppermute | solution.py:363
  67.3 2.6 %add_convert_fusion.3 = (bf16[1024,128]{1,0:T(8,128)(2,1)}, bf16[1024,128]{1,0:T(8,128)(2,1)}, f32[1024,128]{1,0:T(8,128)}, bf16[1024,128]{1,0:T(8,128)(2,1)S(1)}) fusion(bf16[4096,128]{1,0:T(8,128)(2,1)} %collective-permute-done.18, bf16[4096,128]{1,0:T(8,128)(2,1)} %get-tuple-element.34), kind=kLoop, calls=%fused_computation.4 | loop fusion | flops 1966080 | bytes 3407872 | tf_op jit(solution)/shard_map/convert_element_type | solution.py:385
  70.7 2.7 %collective-permute-start.19 = (bf16[1024,128]{1,0:T(8,128)(2,1)S(1)}, bf16[1024,128]{1,0:T(8,128)(2,1)S(1)}, u32[]{:S(2)}, u32[]{:S(2)}) collective-permute-start(bf16[1024,128]{1,0:T(8,128)(2,1)S(1)} %get-tuple-element.54.refs_0_), channel_id=1, source_target_pairs={{0,8},{4,12},{8,0},{12,4},{16,24},{20,28},{24,16},{28,20},{1,9},{5... | collective-permute-start | bytes 786440 | tf_op jit(solution)/shard_map/ppermute | solution.py:363
  73.4 1.2 add_convert_fusion.6
  74.7 9.5 %shard_map.105 = (bf16[4,448,512]{2,1,0:T(8,128)(2,1)}, bf16[4,448,512]{2,1,0:T(8,128)(2,1)}, f32[1024,128]{1,0:T(8,128)}) custom-call(s32[2]{0:T(128)} %pad_add_fusion.my_ref, bf16[512,1024]{1,0:T(8,128)(2,1)} %get-tuple-element.33.left_ref, bf16[1024,3584]{1,0:T(8,128)(2,1)} %right_ref.1, ...), custom_call_target="tpu_custom_call", output_to_operand_aliasing={{2}: (5, {})} | custom-call | tf_op jit(solution)/shard_map/pallas_call | solution.py:547
  85.1 2.3 %shard_map.106 = (bf16[1024,128]{1,0:T(8,128)(2,1)}, bf16[1024,128]{1,0:T(8,128)(2,1)}, bf16[4,448,512]{2,1,0:T(8,128)(2,1)}) custom-call(f32[1024,128]{1,0:T(8,128)} %get-tuple-element.36.refs_0_, bf16[1024,128]{1,0:T(8,128)(2,1)} %copy-done.34, bf16[1024,128]{1,0:T(8,128)(2,1)} %copy-done.32, ...), custom_call_target="tpu_custom_call", output_to_operand_aliasing={{2}: (4, {})} | custom-call | tf_op jit(solution)/shard_map/pallas_call | solution.py:407
  87.4 2.6 %collective-permute-start.17 = (bf16[1024,128]{1,0:T(8,128)(2,1)S(1)}, bf16[1024,128]{1,0:T(8,128)(2,1)S(1)}, u32[]{:S(2)}, u32[]{:S(2)}) collective-permute-start(bf16[1024,128]{1,0:T(8,128)(2,1)S(1)} %copy-done.36), channel_id=1, source_target_pairs={{0,24},{4,28},{8,16},{12,20},{16,8},{20,12},{24,0},{28,4},{1,25},{... | collective-permute-start | bytes 786440 | tf_op jit(solution)/shard_map/ppermute | solution.py:363
  90.9 2.6 %collective-permute-start.22 = (bf16[1024,128]{1,0:T(8,128)(2,1)}, bf16[1024,128]{1,0:T(8,128)(2,1)S(1)}, u32[]{:S(2)}, u32[]{:S(2)}) collective-permute-start(bf16[1024,128]{1,0:T(8,128)(2,1)} %get-tuple-element.38), channel_id=1, source_target_pairs={{0,2},{1,3},{2,0},{3,1},{4,6},{5,7},{6,4},{7,5},{8,10},{9,11},{10,... | collective-permute-start | bytes 786440 | tf_op jit(solution)/shard_map/ppermute | solution.py:350
  93.5 1.7 %convert_add_fusion = (f32[1,448,512]{2,1,0:T(8,128)}, bf16[1,448,512]{2,1,0:T(8,128)(2,1)}, bf16[1,448,512]{2,1,0:T(8,128)(2,1)}, bf16[1,448,512]{2,1,0:T(8,128)(2,1)}) fusion(bf16[4,448,512]{2,1,0:T(8,128)(2,1)S(1)} %collective-permute-done.23, bf16[4,448,512]{2,1,0:T(8,128)(2,1)S(1)} %copy-done.8), kind=kLoop, calls=%fused_computation | loop fusion | flops 3440640 | bytes 5963776 | tf_op jit(solution)/shard_map/add | solution.py:375
  95.3 1.6 %collective-permute-start.24 = (bf16[1024,128]{1,0:T(8,128)(2,1)}, bf16[1024,128]{1,0:T(8,128)(2,1)S(1)}, u32[]{:S(2)}, u32[]{:S(2)}) collective-permute-start(bf16[1024,128]{1,0:T(8,128)(2,1)} %shard_map.108.refs_0_), channel_id=1, source_target_pairs={{0,1},{1,0},{2,3},{3,2},{4,5},{5,4},{6,7},{7,6},{8,9},{9,8},{10,11... | collective-permute-start | bytes 786440 | tf_op jit(solution)/shard_map/ppermute | solution.py:350
  96.8 5.6 %collective-permute-done.17.refs_3_ = bf16[1024,128]{1,0:T(8,128)(2,1)S(1)} collective-permute-done((bf16[1024,128]{1,0:T(8,128)(2,1)S(1)}, bf16[1024,128]{1,0:T(8,128)(2,1)S(1)}, u32[]{:S(2)}, u32[]{:S(2)}) %collective-permute-start.17) | collective-permute-done | bytes 262176 | tf_op jit(solution)/shard_map/ppermute | solution.py:363
  108.2 2.5 %shard_map.109.refs_0_ = bf16[1024,128]{1,0:T(8,128)(2,1)} custom-call(f32[1024,128]{1,0:T(8,128)} %get-tuple-element.58.refs_0_, bf16[1024,128]{1,0:T(8,128)(2,1)} %copy-done.25, bf16[1024,128]{1,0:T(8,128)(2,1)} %copy-done.28, bf16[1024,128]{1,0:T(8,128)(2,1)} %copy-done.27, f32[1024,128]{1,0:T(8,128)} %get-tuple-element.24.cos_ref.refs_4_, ...), custom_call_target="tpu_custom_call" | custom-call | tf_op jit(solution)/shard_map/pallas_call | solution.py:407
  110.7 1.9 %collective-permute-start.26 = (bf16[1024,128]{1,0:T(8,128)(2,1)}, bf16[1024,128]{1,0:T(8,128)(2,1)S(1)}, u32[]{:S(2)}, u32[]{:S(2)}) collective-permute-start(bf16[1024,128]{1,0:T(8,128)(2,1)} %shard_map.109.refs_0_), channel_id=1, source_target_pairs={{0,2},{1,3},{2,0},{3,1},{4,6},{5,7},{6,4},{7,5},{8,10},{9,11},{10,... | collective-permute-start | bytes 786440 | tf_op jit(solution)/shard_map/ppermute | solution.py:350
  112.6 2.0 %collective-permute-start.31 = (bf16[1024,128]{1,0:T(8,128)(2,1)S(1)}, bf16[1024,128]{1,0:T(8,128)(2,1)}, u32[]{:S(2)}, u32[]{:S(2)}) collective-permute-start(bf16[1024,128]{1,0:T(8,128)(2,1)S(1)} %copy-done.4), channel_id=1, source_target_pairs={{0,1},{1,0},{2,3},{3,2},{4,5},{5,4},{6,7},{7,6},{8,9},{9,8},{10,11... | collective-permute-start | bytes 786440 | tf_op jit(solution)/shard_map/ppermute | solution.py:350
  114.6 4.5 %shard_map.110.refs_4_ = bf16[1024,512]{1,0:T(8,128)(2,1)} custom-call(f32[512,1024]{1,0:T(8,128)} %get-tuple-element.30.grad_ref, f32[1024,128]{1,0:T(8,128)} %get-tuple-element.24.cos_ref.refs_4_, f32[1024,128]{1,0:T(8,128)} %get-tuple-element.25.sin_ref.refs_5_, bf16[1024,128]{1,0:T(8,128)(2,1)} %shard_map.109.refs_0_), custom_call_target="tpu_custom_call" | custom-call | tf_op jit(solution)/shard_map/pallas_call | solution.py:482
  119.2 6.2 %collective-permute-done.28.refs_2_ = bf16[1,448,512]{2,1,0:T(8,128)(2,1)S(1)} collective-permute-done((bf16[1,448,512]{2,1,0:T(8,128)(2,1)}, bf16[1,448,512]{2,1,0:T(8,128)(2,1)S(1)}, u32[]{:S(2)}, u32[]{:S(2)}) %collective-permute-start.28) | collective-permute-done | bytes 458784 | tf_op jit(solution)/shard_map/ppermute | solution.py:363
  127.0 1.6 %collective-permute-start.30 = (bf16[1024,128]{1,0:T(8,128)(2,1)}, bf16[1024,128]{1,0:T(8,128)(2,1)S(1)}, u32[]{:S(2)}, u32[]{:S(2)}) collective-permute-start(bf16[1024,128]{1,0:T(8,128)(2,1)} %shard_map.111.refs_2_.refs_4_), channel_id=1, source_target_pairs={{0,1},{1,0},{2,3},{3,2},{4,5},{5,4},{6,7},{7,6},{8,9},{9,8},{10,11... | collective-permute-start | bytes 786440 | tf_op jit(solution)/shard_map/ppermute | solution.py:350
  128.6 2.2 %shard_map.113.refs_5_ = bf16[1024,512]{1,0:T(8,128)(2,1)} custom-call(s32[1]{0:T(128)} %bitcast.6.my_ref, bf16[1024,128]{1,0:T(8,128)(2,1)} %shard_map.108.refs_0_, bf16[1024,128]{1,0:T(8,128)(2,1)} %copy-done.9, bf16[1024,128]{1,0:T(8,128)(2,1)} %shard_map.107.refs_6_.refs_2_, bf16[1024,128]{1,0:T(8,128)(2,1)} %collective-permute-done.31.refs_3_), custom_call_target="tpu_custom_call" | custom-call | tf_op jit(solution)/shard_map/pallas_call | solution.py:337
  130.8 2.7 %shard_map.114 = f32[448,512]{1,0:T(8,128)} custom-call(f32[1,448,512]{2,1,0:T(8,128)} %get-tuple-element.47.refs_0_, bf16[1,448,512]{2,1,0:T(8,128)(2,1)} %copy-done.7, bf16[1,448,512]{2,1,0:T(8,128)(2,1)} %copy-done.6, bf16[1,448,512]{2,1,0:T(8,128)(2,1)} %copy-done.5, bf16[1024,128]{1,0:T(8,128)(2,1)} %shard_map.111.refs_2_.refs_4_, ...), custom_call_target="tpu_custom_call" | custom-call | tf_op jit(solution)/shard_map/pallas_call | solution.py:576
  133.5 1.9 %collective-permute-done.30.refs_3_ = bf16[1024,128]{1,0:T(8,128)(2,1)S(1)} collective-permute-done((bf16[1024,128]{1,0:T(8,128)(2,1)}, bf16[1024,128]{1,0:T(8,128)(2,1)S(1)}, u32[]{:S(2)}, u32[]{:S(2)}) %collective-permute-start.30) | collective-permute-done | bytes 262176 | tf_op jit(solution)/shard_map/ppermute | solution.py:350
  136.1 2.2 %shard_map.112 = bf16[1024,512]{1,0:T(8,128)(2,1)} custom-call(s32[1]{0:T(128)} %bitcast.6.my_ref, bf16[1024,128]{1,0:T(8,128)(2,1)} %shard_map.109.refs_0_, bf16[1024,128]{1,0:T(8,128)(2,1)} %copy-done.33, bf16[1024,128]{1,0:T(8,128)(2,1)} %shard_map.111.refs_2_.refs_4_, bf16[1024,128]{1,0:T(8,128)(2,1)} %copy-done.35), custom_call_target="tpu_custom_call" | custom-call | tf_op jit(solution)/shard_map/pallas_call | solution.py:337
  (148 shorter events, 21.6 us)
Async XLA Ops:
  1.9 24.3 %collective-permute-start.12 = (bf16[1024,128]{1,0:T(8,128)(2,1)S(1)}, bf16[1024,128]{1,0:T(8,128)(2,1)S(1)}, u32[]{:S(2)}, u32[]{:S(2)}) collective-permute-start(bf16[1024,128]{1,0:T(8,128)(2,1)S(1)} %constant_dynamic-slice_fusion.refs_8_), channel_id=1, source_target_pairs={{0,24},{4,28},{8,16},{12,20},{16,8},{20,12},{24,0},{28,4},{1,25},{... | collective-permute-start | bytes 786440 | tf_op jit(solution)/shard_map/ppermute | solution.py:363
  5.9 20.9 %collective-permute-start.10 = (bf16[1024,128]{1,0:T(8,128)(2,1)S(1)}, bf16[1024,128]{1,0:T(8,128)(2,1)S(1)}, u32[]{:S(2)}, u32[]{:S(2)}) collective-permute-start(bf16[1024,128]{1,0:T(8,128)(2,1)S(1)} %constant_dynamic-slice_fusion.refs_8_), channel_id=1, source_target_pairs={{0,16},{4,20},{8,24},{12,28},{16,0},{20,4},{24,8},{28,12},{1,17},{... | collective-permute-start | bytes 786440 | tf_op jit(solution)/shard_map/ppermute | solution.py:363
  6.4 20.9 %collective-permute-start.8 = (bf16[1024,128]{1,0:T(8,128)(2,1)S(1)}, bf16[1024,128]{1,0:T(8,128)(2,1)S(1)}, u32[]{:S(2)}, u32[]{:S(2)}) collective-permute-start(bf16[1024,128]{1,0:T(8,128)(2,1)S(1)} %constant_dynamic-slice_fusion.refs_8_), channel_id=1, source_target_pairs={{0,8},{4,12},{8,0},{12,4},{16,24},{20,28},{24,16},{28,20},{1,9},{5... | collective-permute-start | bytes 786440 | tf_op jit(solution)/shard_map/ppermute | solution.py:363
  6.5 20.8 %collective-permute-start.7 = (bf16[1024,128]{1,0:T(8,128)(2,1)S(1)}, bf16[1024,128]{1,0:T(8,128)(2,1)S(1)}, u32[]{:S(2)}, u32[]{:S(2)}) collective-permute-start(bf16[1024,128]{1,0:T(8,128)(2,1)S(1)} %constant_dynamic-slice_fusion.refs_8_), channel_id=1, source_target_pairs={{0,4},{4,0},{8,12},{12,8},{16,20},{20,16},{24,28},{28,24},{1,5},{5... | collective-permute-start | bytes 786440 | tf_op jit(solution)/shard_map/ppermute | solution.py:363
  8.6 9.8 %all-to-all-start = ((s32[8,8,128]{2,1,0:T(8,128)}), s32[8,8,128]{2,1,0:T(8,128)S(1)}, u32[]{:S(2)}, u32[]{:S(2)}) async-start(s32[8,8,128]{2,1,0:T(8,128)} %broadcast_in_dim.27), calls=%async_computation | async-start | bytes 65536 | tf_op jit(solution)/shard_map/all_to_all | solution.py:598
  23.8 13.3 %collective-permute-start.5 = (bf16[1024,128]{1,0:T(8,128)(2,1)}, bf16[1024,128]{1,0:T(8,128)(2,1)S(1)}, u32[]{:S(2)}, u32[]{:S(2)}) collective-permute-start(bf16[1024,128]{1,0:T(8,128)(2,1)} %get-tuple-element.26.refs_0_), channel_id=1, source_target_pairs={{0,24},{4,28},{8,16},{12,20},{16,8},{20,12},{24,0},{28,4},{1,25},{... | collective-permute-start | bytes 786440 | tf_op jit(solution)/shard_map/ppermute | solution.py:363
  26.2 12.5 %collective-permute-start.3 = (bf16[1024,128]{1,0:T(8,128)(2,1)}, bf16[1024,128]{1,0:T(8,128)(2,1)S(1)}, u32[]{:S(2)}, u32[]{:S(2)}) collective-permute-start(bf16[1024,128]{1,0:T(8,128)(2,1)} %get-tuple-element.26.refs_0_), channel_id=1, source_target_pairs={{0,16},{4,20},{8,24},{12,28},{16,0},{20,4},{24,8},{28,12},{1,17},{... | collective-permute-start | bytes 786440 | tf_op jit(solution)/shard_map/ppermute | solution.py:363
  26.8 12.0 %collective-permute-start.1 = (bf16[1024,128]{1,0:T(8,128)(2,1)}, bf16[1024,128]{1,0:T(8,128)(2,1)S(1)}, u32[]{:S(2)}, u32[]{:S(2)}) collective-permute-start(bf16[1024,128]{1,0:T(8,128)(2,1)} %get-tuple-element.26.refs_0_), channel_id=1, source_target_pairs={{0,8},{4,12},{8,0},{12,4},{16,24},{20,28},{24,16},{28,20},{1,9},{5... | collective-permute-start | bytes 786440 | tf_op jit(solution)/shard_map/ppermute | solution.py:363
  27.3 11.9 %collective-permute-start = (bf16[1024,128]{1,0:T(8,128)(2,1)}, bf16[1024,128]{1,0:T(8,128)(2,1)S(1)}, u32[]{:S(2)}, u32[]{:S(2)}) collective-permute-start(bf16[1024,128]{1,0:T(8,128)(2,1)} %get-tuple-element.26.refs_0_), channel_id=1, source_target_pairs={{0,4},{4,0},{8,12},{12,8},{16,20},{20,16},{24,28},{28,24},{1,5},{5... | collective-permute-start | bytes 786440 | tf_op jit(solution)/shard_map/ppermute | solution.py:363
  27.3 12.0 %collective-permute-start.13 = (bf16[1024,128]{1,0:T(8,128)(2,1)S(1)}, bf16[1024,128]{1,0:T(8,128)(2,1)S(1)}, u32[]{:S(2)}, u32[]{:S(2)}) collective-permute-start(bf16[1024,128]{1,0:T(8,128)(2,1)S(1)} %collective-permute-done.12.refs_14_), channel_id=1, source_target_pairs={{0,4},{4,0},{8,12},{12,8},{16,20},{20,16},{24,28},{28,24},{1,5},{5... | collective-permute-start | bytes 786440 | tf_op jit(solution)/shard_map/ppermute | solution.py:363
  37.1 3.4 %collective-permute-start.11 = (bf16[1024,128]{1,0:T(8,128)(2,1)S(1)}, bf16[1024,128]{1,0:T(8,128)(2,1)S(1)}, u32[]{:S(2)}, u32[]{:S(2)}) collective-permute-start(bf16[1024,128]{1,0:T(8,128)(2,1)S(1)} %collective-permute-done.10.refs_12_), channel_id=1, source_target_pairs={{0,4},{4,0},{8,12},{12,8},{16,20},{20,16},{24,28},{28,24},{1,5},{5... | collective-permute-start | bytes 786440 | tf_op jit(solution)/shard_map/ppermute | solution.py:363
  38.8 1.9 %collective-permute-start.6 = (bf16[1024,128]{1,0:T(8,128)(2,1)S(1)}, bf16[1024,128]{1,0:T(8,128)(2,1)S(1)}, u32[]{:S(2)}, u32[]{:S(2)}) collective-permute-start(bf16[1024,128]{1,0:T(8,128)(2,1)S(1)} %collective-permute-done.5.refs_6_), channel_id=1, source_target_pairs={{0,4},{4,0},{8,12},{12,8},{16,20},{20,16},{24,28},{28,24},{1,5},{5... | collective-permute-start | bytes 786440 | tf_op jit(solution)/shard_map/ppermute | solution.py:363
  39.3 1.8 %collective-permute-start.4 = (bf16[1024,128]{1,0:T(8,128)(2,1)S(1)}, bf16[1024,128]{1,0:T(8,128)(2,1)S(1)}, u32[]{:S(2)}, u32[]{:S(2)}) collective-permute-start(bf16[1024,128]{1,0:T(8,128)(2,1)S(1)} %collective-permute-done.3.refs_4_), channel_id=1, source_target_pairs={{0,4},{4,0},{8,12},{12,8},{16,20},{20,16},{24,28},{28,24},{1,5},{5... | collective-permute-start | bytes 786440 | tf_op jit(solution)/shard_map/ppermute | solution.py:363
  39.3 2.0 %collective-permute-start.2 = (bf16[1024,128]{1,0:T(8,128)(2,1)S(1)}, bf16[1024,128]{1,0:T(8,128)(2,1)S(1)}, u32[]{:S(2)}, u32[]{:S(2)}) collective-permute-start(bf16[1024,128]{1,0:T(8,128)(2,1)S(1)} %collective-permute-done.1.refs_2_), channel_id=1, source_target_pairs={{0,4},{4,0},{8,12},{12,8},{16,20},{20,16},{24,28},{28,24},{1,5},{5... | collective-permute-start | bytes 786440 | tf_op jit(solution)/shard_map/ppermute | solution.py:363
  63.5 3.8 %collective-permute-start.18 = (bf16[4096,128]{1,0:T(8,128)(2,1)}, bf16[4096,128]{1,0:T(8,128)(2,1)}, u32[]{:S(2)}, u32[]{:S(2)}) collective-permute-start(bf16[4096,128]{1,0:T(8,128)(2,1)} %get-tuple-element.35), channel_id=1, source_target_pairs={{0,4},{4,0},{8,12},{12,8},{16,20},{20,16},{24,28},{28,24},{1,5},{5... | collective-permute-start | bytes 3145736 | tf_op jit(solution)/shard_map/ppermute | solution.py:363
  63.6 9.8 %collective-permute-start.14 = (bf16[4096,128]{1,0:T(8,128)(2,1)}, bf16[4096,128]{1,0:T(8,128)(2,1)S(1)}, u32[]{:S(2)}, u32[]{:S(2)}) collective-permute-start(bf16[4096,128]{1,0:T(8,128)(2,1)} %get-tuple-element.32), channel_id=1, source_target_pairs={{0,4},{4,0},{8,12},{12,8},{16,20},{20,16},{24,28},{28,24},{1,5},{5... | collective-permute-start | bytes 3145736 | tf_op jit(solution)/shard_map/ppermute | solution.py:363
  69.9 14.2 %collective-permute-start.21 = (bf16[1024,128]{1,0:T(8,128)(2,1)}, bf16[1024,128]{1,0:T(8,128)(2,1)S(1)}, u32[]{:S(2)}, u32[]{:S(2)}) collective-permute-start(bf16[1024,128]{1,0:T(8,128)(2,1)} %get-tuple-element.51), channel_id=1, source_target_pairs={{0,24},{4,28},{8,16},{12,20},{16,8},{20,12},{24,0},{28,4},{1,25},{... | collective-permute-start | bytes 786440 | tf_op jit(solution)/shard_map/ppermute | solution.py:363
  70.2 14.0 %collective-permute-start.20 = (bf16[1024,128]{1,0:T(8,128)(2,1)}, bf16[1024,128]{1,0:T(8,128)(2,1)S(1)}, u32[]{:S(2)}, u32[]{:S(2)}) collective-permute-start(bf16[1024,128]{1,0:T(8,128)(2,1)} %get-tuple-element.52), channel_id=1, source_target_pairs={{0,16},{4,20},{8,24},{12,28},{16,0},{20,4},{24,8},{28,12},{1,17},{... | collective-permute-start | bytes 786440 | tf_op jit(solution)/shard_map/ppermute | solution.py:363
  70.7 13.5 %collective-permute-start.19 = (bf16[1024,128]{1,0:T(8,128)(2,1)S(1)}, bf16[1024,128]{1,0:T(8,128)(2,1)S(1)}, u32[]{:S(2)}, u32[]{:S(2)}) collective-permute-start(bf16[1024,128]{1,0:T(8,128)(2,1)S(1)} %get-tuple-element.54.refs_0_), channel_id=1, source_target_pairs={{0,8},{4,12},{8,0},{12,4},{16,24},{20,28},{24,16},{28,20},{1,9},{5... | collective-permute-start | bytes 786440 | tf_op jit(solution)/shard_map/ppermute | solution.py:363
  87.3 6.2 %collective-permute-start.23 = (bf16[4,448,512]{2,1,0:T(8,128)(2,1)}, bf16[4,448,512]{2,1,0:T(8,128)(2,1)S(1)}, u32[]{:S(2)}, u32[]{:S(2)}) collective-permute-start(bf16[4,448,512]{2,1,0:T(8,128)(2,1)} %get-tuple-element.40), channel_id=1, source_target_pairs={{0,4},{4,0},{8,12},{12,8},{16,20},{20,16},{24,28},{28,24},{1,5},{5... | collective-permute-start | bytes 5505032 | tf_op jit(solution)/shard_map/ppermute | solution.py:363
  87.4 19.3 %collective-permute-start.15 = (bf16[1024,128]{1,0:T(8,128)(2,1)S(1)}, bf16[1024,128]{1,0:T(8,128)(2,1)S(1)}, u32[]{:S(2)}, u32[]{:S(2)}) collective-permute-start(bf16[1024,128]{1,0:T(8,128)(2,1)S(1)} %copy-done.12), channel_id=1, source_target_pairs={{0,8},{4,12},{8,0},{12,4},{16,24},{20,28},{24,16},{28,20},{1,9},{5... | collective-permute-start | bytes 786440 | tf_op jit(solution)/shard_map/ppermute | solution.py:363
  87.4 14.9 %collective-permute-start.17 = (bf16[1024,128]{1,0:T(8,128)(2,1)S(1)}, bf16[1024,128]{1,0:T(8,128)(2,1)S(1)}, u32[]{:S(2)}, u32[]{:S(2)}) collective-permute-start(bf16[1024,128]{1,0:T(8,128)(2,1)S(1)} %copy-done.36), channel_id=1, source_target_pairs={{0,24},{4,28},{8,16},{12,20},{16,8},{20,12},{24,0},{28,4},{1,25},{... | collective-permute-start | bytes 786440 | tf_op jit(solution)/shard_map/ppermute | solution.py:363
  90.0 13.9 %collective-permute-start.16 = (bf16[1024,128]{1,0:T(8,128)(2,1)}, bf16[1024,128]{1,0:T(8,128)(2,1)S(1)}, u32[]{:S(2)}, u32[]{:S(2)}) collective-permute-start(bf16[1024,128]{1,0:T(8,128)(2,1)} %get-tuple-element.56), channel_id=1, source_target_pairs={{0,16},{4,20},{8,24},{12,28},{16,0},{20,4},{24,8},{28,12},{1,17},{... | collective-permute-start | bytes 786440 | tf_op jit(solution)/shard_map/ppermute | solution.py:363
  90.9 14.7 %collective-permute-start.22 = (bf16[1024,128]{1,0:T(8,128)(2,1)}, bf16[1024,128]{1,0:T(8,128)(2,1)S(1)}, u32[]{:S(2)}, u32[]{:S(2)}) collective-permute-start(bf16[1024,128]{1,0:T(8,128)(2,1)} %get-tuple-element.38), channel_id=1, source_target_pairs={{0,2},{1,3},{2,0},{3,1},{4,6},{5,7},{6,4},{7,5},{8,10},{9,11},{10,... | collective-permute-start | bytes 786440 | tf_op jit(solution)/shard_map/ppermute | solution.py:350
  95.3 12.2 %collective-permute-start.24 = (bf16[1024,128]{1,0:T(8,128)(2,1)}, bf16[1024,128]{1,0:T(8,128)(2,1)S(1)}, u32[]{:S(2)}, u32[]{:S(2)}) collective-permute-start(bf16[1024,128]{1,0:T(8,128)(2,1)} %shard_map.108.refs_0_), channel_id=1, source_target_pairs={{0,1},{1,0},{2,3},{3,2},{4,5},{5,4},{6,7},{7,6},{8,9},{9,8},{10,11... | collective-permute-start | bytes 786440 | tf_op jit(solution)/shard_map/ppermute | solution.py:350
  102.4 16.7 %collective-permute-start.29 = (bf16[1,448,512]{2,1,0:T(8,128)(2,1)}, bf16[1,448,512]{2,1,0:T(8,128)(2,1)S(1)}, u32[]{:S(2)}, u32[]{:S(2)}) collective-permute-start(bf16[1,448,512]{2,1,0:T(8,128)(2,1)} %get-tuple-element.48), channel_id=1, source_target_pairs={{0,24},{4,28},{8,16},{12,20},{16,8},{20,12},{24,0},{28,4},{1,25},{... | collective-permute-start | bytes 1376264 | tf_op jit(solution)/shard_map/ppermute | solution.py:363
  104.7 20.7 %collective-permute-start.28 = (bf16[1,448,512]{2,1,0:T(8,128)(2,1)}, bf16[1,448,512]{2,1,0:T(8,128)(2,1)S(1)}, u32[]{:S(2)}, u32[]{:S(2)}) collective-permute-start(bf16[1,448,512]{2,1,0:T(8,128)(2,1)} %get-tuple-element.49), channel_id=1, source_target_pairs={{0,16},{4,20},{8,24},{12,28},{16,0},{20,4},{24,8},{28,12},{1,17},{... | collective-permute-start | bytes 1376264 | tf_op jit(solution)/shard_map/ppermute | solution.py:363
  105.6 19.8 %collective-permute-start.27 = (bf16[1,448,512]{2,1,0:T(8,128)(2,1)}, bf16[1,448,512]{2,1,0:T(8,128)(2,1)S(1)}, u32[]{:S(2)}, u32[]{:S(2)}) collective-permute-start(bf16[1,448,512]{2,1,0:T(8,128)(2,1)} %get-tuple-element.50.refs_1_), channel_id=1, source_target_pairs={{0,8},{4,12},{8,0},{12,4},{16,24},{20,28},{24,16},{28,20},{1,9},{5... | collective-permute-start | bytes 1376264 | tf_op jit(solution)/shard_map/ppermute | solution.py:363
  110.7 14.7 %collective-permute-start.26 = (bf16[1024,128]{1,0:T(8,128)(2,1)}, bf16[1024,128]{1,0:T(8,128)(2,1)S(1)}, u32[]{:S(2)}, u32[]{:S(2)}) collective-permute-start(bf16[1024,128]{1,0:T(8,128)(2,1)} %shard_map.109.refs_0_), channel_id=1, source_target_pairs={{0,2},{1,3},{2,0},{3,1},{4,6},{5,7},{6,4},{7,5},{8,10},{9,11},{10,... | collective-permute-start | bytes 786440 | tf_op jit(solution)/shard_map/ppermute | solution.py:350
  112.6 16.0 %collective-permute-start.31 = (bf16[1024,128]{1,0:T(8,128)(2,1)S(1)}, bf16[1024,128]{1,0:T(8,128)(2,1)}, u32[]{:S(2)}, u32[]{:S(2)}) collective-permute-start(bf16[1024,128]{1,0:T(8,128)(2,1)S(1)} %copy-done.4), channel_id=1, source_target_pairs={{0,1},{1,0},{2,3},{3,2},{4,5},{5,4},{6,7},{7,6},{8,9},{9,8},{10,11... | collective-permute-start | bytes 786440 | tf_op jit(solution)/shard_map/ppermute | solution.py:350
  119.1 14.4 %collective-permute-start.25 = (bf16[1024,128]{1,0:T(8,128)(2,1)S(1)}, bf16[1024,128]{1,0:T(8,128)(2,1)S(1)}, u32[]{:S(2)}, u32[]{:S(2)}) collective-permute-start(bf16[1024,128]{1,0:T(8,128)(2,1)S(1)} %copy-done.1), channel_id=1, source_target_pairs={{0,1},{1,0},{2,3},{3,2},{4,5},{5,4},{6,7},{7,6},{8,9},{9,8},{10,11... | collective-permute-start | bytes 786440 | tf_op jit(solution)/shard_map/ppermute | solution.py:350
  127.0 8.4 %collective-permute-start.30 = (bf16[1024,128]{1,0:T(8,128)(2,1)}, bf16[1024,128]{1,0:T(8,128)(2,1)S(1)}, u32[]{:S(2)}, u32[]{:S(2)}) collective-permute-start(bf16[1024,128]{1,0:T(8,128)(2,1)} %shard_map.111.refs_2_.refs_4_), channel_id=1, source_target_pairs={{0,1},{1,0},{2,3},{3,2},{4,5},{5,4},{6,7},{7,6},{8,9},{9,8},{10,11... | collective-permute-start | bytes 786440 | tf_op jit(solution)/shard_map/ppermute | solution.py:350
  (41 other events, 184.0 us)
